TPU v7x, 32 devices: a whole 2x2x4 slice. The times are simulated.
32 devices in a mesh: row: 8 (over z, y), col: 4 (over x, core).
Axes of the slice: x: 2, y: 2, z: 4, core: 2. Of those that a mesh axis runs over, the one named last changes fastest.
Arguments:
- right_side: float32 [8, 4, 1024, 256], P('row', 'col'), may hold values from -4 to 4
- local_operator: bfloat16 [8, 4, 1536, 1536], P('row', 'col'), may hold values from -1 to 4
- local_inverse: bfloat16 [8, 4, 1536, 1536], P('row', 'col'), may hold values from -1 to 1
- coarse_basis: bfloat16 [8, 4, 1536, 32], P('row', 'col'), may hold values from -1 to 1
- coarse_inverse: bfloat16 [8, 128, 1024], P(None, 'col', 'row'), may hold values from -1 to 1
- send_rows: int32 [8, 4, 4, 128], P('row', 'col'), may hold values from 0 to 1023, as said below
- send_count: int32 [8, 4, 4], P('row', 'col'), may hold values from 0 to 128, as said below
Outputs:
- solution: float32 [8, 4, 1024, 256], P('row', 'col')
Inputs may be any that keep to these rules, and one draw needn't show every extreme that they name: `send_rows`: within one subdomain and direction the entries are distinct owned rows; entries at or past that direction's count are ignored. `send_count`: 0 exactly where the neighbour in that direction lies outside the grid of subdomains; otherwise from 128 // 4 to 128, and 128 is reached.
All inputs are finite; a program needn't handle non-finite values.
Results may differ from a plain program's by a relative error of at most 0.023.
Values may be sent and summed in bfloat16 or wider, within the bound.
No kernel may reach another device: no remote copies, remote signals or barrier semaphores. Data moves between devices by JAX's collectives and lax.ppermute only.
A program may use at most 64 MiB of HBM per device.

v0:
```python
import jax
import jax.numpy as jnp
from jax import lax
from jax.sharding import PartitionSpec as P

ITERS = 3


DAMPING = 0.5


def passed_along(shard, axis, by):
    devices = lax.axis_size(axis)
    pairs = [(i, i + by) for i in range(devices) if 0 <= i + by < devices]
    return lax.ppermute(shard, axis, pairs)


def ghost_trade(buffer):
    arrived = []
    for offset, source in ((1, 1), (-1, 0)):
        arrived.append(passed_along(buffer[source], "row", offset))
    for offset, source in ((1, 3), (-1, 2)):
        arrived.append(passed_along(buffer[source], "col", offset))
    return jnp.stack(arrived)


def per_device(
    right_side, local_operator, local_inverse, coarse_basis, coarse_inverse, send_rows, send_count
):
    target = right_side[0, 0]
    operator = local_operator[0, 0]
    inverse = local_inverse[0, 0]
    prolong = coarse_basis[0, 0]
    rows_list = send_rows[0, 0]
    counts = send_count[0, 0]
    own_rows, columns = target.shape
    tile_rows = rows_list.shape[1]
    live_mask = (lax.broadcasted_iota(jnp.int32, rows_list.shape, 1) < counts[:, None]).astype(
        jnp.float32
    )
    live_half = live_mask[..., None].astype(jnp.bfloat16)
    flat_rows = rows_list.reshape(-1)
    coarse_rows = coarse_inverse.reshape(-1, coarse_inverse.shape[2])

    def with_ghosts(values_half):
        packed = values_half[flat_rows].reshape(4, tile_rows, columns) * live_half
        ghosts = ghost_trade(packed)
        return jnp.concatenate([values_half, ghosts.reshape(4 * tile_rows, columns)], axis=0)

    def owner_sum(local_terms):
        rim_half = local_terms[own_rows:].astype(jnp.bfloat16).reshape(4, tile_rows, columns)
        returned = ghost_trade(rim_half)
        weighted = returned.astype(jnp.float32) * live_mask[..., None]
        summed = (
            jnp.zeros((own_rows, columns), jnp.float32)
            .at[flat_rows]
            .add(weighted.reshape(-1, columns))
        )
        return local_terms[:own_rows] + summed

    solution = jnp.zeros((own_rows, columns), jnp.float32)
    for sweep in range(ITERS):
        if sweep == 0:
            residual_half = target.astype(jnp.bfloat16)
        else:
            solution_half = solution.astype(jnp.bfloat16)
            image = owner_sum(
                jnp.dot(operator, with_ghosts(solution_half), preferred_element_type=jnp.float32)
            )
            residual_half = (target - image).astype(jnp.bfloat16)
        residual_local = with_ghosts(residual_half)
        local_part = jnp.dot(inverse, residual_local, preferred_element_type=jnp.float32)
        restricted = lax.dot_general(
            prolong, residual_local, (((0,), (0,)), ((), ())), preferred_element_type=jnp.float32
        )
        restricted = restricted.astype(jnp.bfloat16)
        block_rows = lax.all_gather(restricted, "col", axis=0, tiled=True)
        solved = lax.psum_scatter(
            jnp.dot(coarse_rows, block_rows, preferred_element_type=jnp.float32).astype(
                jnp.bfloat16
            ),
            "row",
            scatter_dimension=0,
            tiled=True,
        )
        update = owner_sum(
            local_part + jnp.dot(prolong, solved, preferred_element_type=jnp.float32)
        )
        solution = solution + DAMPING * update
    return solution[None, None]


def solution(mesh):
    return jax.shard_map(
        per_device,
        mesh=mesh,
        in_specs=(
            P("row", "col", None, None),
            P("row", "col", None, None),
            P("row", "col", None, None),
            P("row", "col", None, None),
            P(None, "col", "row"),
            P("row", "col", None, None),
            P("row", "col", None),
        ),
        out_specs=P("row", "col", None, None),
        check_vma=False,
    )
```

profile of v0, /device:TPU:0, one launch (start us, length us, event | category | flops | bytes accessed | tf_op | source)
XLA Modules:
  0.0 427.5 jit_solution(5946464651022154692)
XLA Ops:
  11.4 4.9 %collective-permute-start = (bf16[128,256]{1,0:T(8,128)(2,1)S(1)}, bf16[128,256]{1,0:T(8,128)(2,1)S(1)}, u32[]{:S(2)}, u32[]{:S(2)}) collective-permute-start(bf16[128,256]{1,0:T(8,128)(2,1)S(1)} %get-tuple-element.41), channel_id=1, source_target_pairs={{0,4},{4,8},{8,12},{12,16},{16,20},{20,24},{24,28},{1,5},{5,9},{9,... | collective-permute-start | bytes 196616 | tf_op jit(solution)/shard_map/ppermute | solution.py:15
  17.6 3.0 collective-permute-start.2
  22.0 5.4 %collective-permute-done.1 = bf16[128,256]{1,0:T(8,128)(2,1)S(1)} collective-permute-done((bf16[128,256]{1,0:T(8,128)(2,1)S(1)}, bf16[128,256]{1,0:T(8,128)(2,1)S(1)}, u32[]{:S(2)}, u32[]{:S(2)}) %collective-permute-start.1) | collective-permute-done | bytes 65568 | tf_op jit(solution)/shard_map/ppermute | solution.py:15
  27.6 5.2 %all_gather.9 = bf16[128,256]{1,0:T(8,128)(2,1)S(1)} all-gather(bf16[32,256]{1,0:T(8,128)(2,1)S(1)} %fusion.22), channel_id=1, replica_groups=mesh['row'=8,'col'=4] {'col'}, dimensions={0}, use_global_device_ids=true | all-gather | bytes 81920 | tf_op jit(solution)/shard_map/all_gather | solution.py:77
  33.9 3.8 fusion.8
  37.7 58.2 %reduce-scatter.10.cloned.1.call-done = bf16[32,256]{1,0:T(8,128)(2,1)} async-done(((bf16[256,256]{1,0:T(8,128)(2,1)}), bf16[32,256]{1,0:T(8,128)(2,1)}) %reduce-scatter.10.cloned.1.call-update) | async-done | bytes 16400
  97.1 3.3 collective-permute-start.4
  101.7 3.0 collective-permute-start.6
  106.5 5.0 %collective-permute-done.5 = bf16[128,256]{0,1:T(8,128)(2,1)S(1)} collective-permute-done((bf16[128,256]{0,1:T(8,128)(2,1)S(1)}, bf16[128,256]{0,1:T(8,128)(2,1)S(1)}, u32[]{:S(2)}, u32[]{:S(2)}) %collective-permute-start.5) | collective-permute-done | bytes 65568 | tf_op jit(solution)/shard_map/ppermute | solution.py:15
  111.9 3.7 scatter_fusion
  117.9 4.2 collective-permute-start.8
  123.4 3.0 collective-permute-start.10
  127.7 5.4 %collective-permute-done.9 = bf16[128,256]{1,0:T(8,128)(2,1)S(1)} collective-permute-done((bf16[128,256]{1,0:T(8,128)(2,1)S(1)}, bf16[128,256]{1,0:T(8,128)(2,1)S(1)}, u32[]{:S(2)}, u32[]{:S(2)}) %collective-permute-start.9) | collective-permute-done | bytes 65568 | tf_op jit(solution)/shard_map/ppermute | solution.py:15
  133.2 3.8 fusion.54
  137.0 3.4 collective-permute-start.12
  141.8 3.0 collective-permute-start.14
  148.8 2.8 collective-permute-done.13
  152.0 3.9 scatter_fusion.1
  159.4 3.4 collective-permute-start.16
  164.1 3.0 collective-permute-start.18
  168.4 5.4 %collective-permute-done.17 = bf16[128,256]{1,0:T(8,128)(2,1)S(1)} collective-permute-done((bf16[128,256]{1,0:T(8,128)(2,1)S(1)}, bf16[128,256]{1,0:T(8,128)(2,1)S(1)}, u32[]{:S(2)}, u32[]{:S(2)}) %collective-permute-start.17) | collective-permute-done | bytes 65568 | tf_op jit(solution)/shard_map/ppermute | solution.py:15
  174.6 5.2 %all_gather.10 = bf16[128,256]{1,0:T(8,128)(2,1)S(1)} all-gather(bf16[32,256]{1,0:T(8,128)(2,1)S(1)} %fusion.23), channel_id=1, replica_groups=mesh['row'=8,'col'=4] {'col'}, dimensions={0}, use_global_device_ids=true | all-gather | bytes 81920 | tf_op jit(solution)/shard_map/all_gather | solution.py:77
  180.9 3.9 fusion.6
  184.8 55.0 %reduce-scatter.12.cloned.1.call-done = bf16[32,256]{1,0:T(8,128)(2,1)} async-done(((bf16[256,256]{1,0:T(8,128)(2,1)}), bf16[32,256]{1,0:T(8,128)(2,1)}) %reduce-scatter.12.cloned.1.call-update) | async-done | bytes 16400
  241.6 3.3 collective-permute-start.20
  246.2 3.0 collective-permute-start.22
  251.0 5.3 %collective-permute-done.21 = bf16[128,256]{0,1:T(8,128)(2,1)} collective-permute-done((bf16[128,256]{0,1:T(8,128)(2,1)}, bf16[128,256]{0,1:T(8,128)(2,1)}, u32[]{:S(2)}, u32[]{:S(2)}) %collective-permute-start.21) | collective-permute-done | bytes 65568 | tf_op jit(solution)/shard_map/ppermute | solution.py:15
  257.5 3.7 scatter_fusion.2
  263.5 4.2 collective-permute-start.24
  269.1 3.0 collective-permute-start.26
  273.5 5.4 %collective-permute-done.25 = bf16[128,256]{1,0:T(8,128)(2,1)S(1)} collective-permute-done((bf16[128,256]{1,0:T(8,128)(2,1)S(1)}, bf16[128,256]{1,0:T(8,128)(2,1)S(1)}, u32[]{:S(2)}, u32[]{:S(2)}) %collective-permute-start.25) | collective-permute-done | bytes 65568 | tf_op jit(solution)/shard_map/ppermute | solution.py:15
  278.9 3.8 fusion.56
  283.4 3.4 collective-permute-start.28
  288.2 3.3 collective-permute-start.30
  295.4 3.1 collective-permute-done.29
  304.2 4.2 scatter_fusion.3
  308.4 2.1 fusion.26
  310.5 2.7 gather_fusion.4
  313.4 3.4 collective-permute-start.32
  318.2 3.0 collective-permute-start.34
  322.5 5.4 %collective-permute-done.33 = bf16[128,256]{1,0:T(8,128)(2,1)S(1)} collective-permute-done((bf16[128,256]{1,0:T(8,128)(2,1)S(1)}, bf16[128,256]{1,0:T(8,128)(2,1)S(1)}, u32[]{:S(2)}, u32[]{:S(2)}) %collective-permute-start.33) | collective-permute-done | bytes 65568 | tf_op jit(solution)/shard_map/ppermute | solution.py:15
  328.3 5.2 %all_gather.11 = bf16[128,256]{1,0:T(8,128)(2,1)S(1)} all-gather(bf16[32,256]{1,0:T(8,128)(2,1)S(1)} %fusion.24), channel_id=1, replica_groups=mesh['row'=8,'col'=4] {'col'}, dimensions={0}, use_global_device_ids=true | all-gather | bytes 81920 | tf_op jit(solution)/shard_map/all_gather | solution.py:77
  334.5 5.0 %fusion.4 = f32[256,1536]{1,0:T(8,128)} fusion(bf16[1,1,1536,1536]{3,2,1,0:T(8,128)(2,1)} %param.9, bf16[512,256]{1,0:T(8,128)(2,1)S(1)} %bitcast.202, bf16[1024,256]{1,0:T(8,128)(2,1)S(1)} %copy-done.1), kind=kOutput, calls=%fused_computation.14 | convolution fusion | flops 1209532416 | bytes 7077888 | tf_op jit(solution)/shard_map/dot_general | solution.py:72
  339.4 54.2 %reduce-scatter.14.cloned.1.call-done = bf16[32,256]{1,0:T(8,128)(2,1)} async-done(((bf16[256,256]{1,0:T(8,128)(2,1)}), bf16[32,256]{1,0:T(8,128)(2,1)}) %reduce-scatter.14.cloned.1.call-update) | async-done | bytes 16400
  396.2 3.3 collective-permute-start.36
  400.8 3.0 collective-permute-start.38
  407.8 3.0 collective-permute-done.37
  415.6 4.2 scatter_fusion.4
  (133 shorter events, 71.8 us)
Async XLA Ops:
  6.5 20.9 %copy-start = (bf16[1,1,1536,32]{2,3,1,0:T(8,128)(2,1)S(1)}, bf16[1,1,1536,32]{2,3,1,0:T(8,128)(2,1)}, u32[]{:S(2)}) copy-start(bf16[1,1,1536,32]{2,3,1,0:T(8,128)(2,1)} %param.10) | copy-start | bytes 294916
  6.5 89.4 %reduce-scatter.10.cloned.1.call-start = ((), (), s32[]{:S(2)}) async-start(), calls=%async_computation.3 | async-start | bytes 147456
  11.2 21.7 %copy-start.2 = (bf16[8,32,128]{2,1,0:T(8,128)(2,1)S(1)}, bf16[8,32,128]{2,1,0:T(8,128)(2,1)}, u32[]{:S(2)}) copy-start(bf16[8,32,128]{2,1,0:T(8,128)(2,1)} %param.11) | copy-start | bytes 196612
  11.4 10.5 %collective-permute-start = (bf16[128,256]{1,0:T(8,128)(2,1)S(1)}, bf16[128,256]{1,0:T(8,128)(2,1)S(1)}, u32[]{:S(2)}, u32[]{:S(2)}) collective-permute-start(bf16[128,256]{1,0:T(8,128)(2,1)S(1)} %get-tuple-element.41), channel_id=1, source_target_pairs={{0,4},{4,8},{8,12},{12,16},{16,20},{20,24},{24,28},{1,5},{5,9},{9,... | collective-permute-start | bytes 196616 | tf_op jit(solution)/shard_map/ppermute | solution.py:15
  16.3 5.7 %collective-permute-start.3 = (bf16[128,256]{1,0:T(8,128)(2,1)S(1)}, bf16[128,256]{1,0:T(8,128)(2,1)S(1)}, u32[]{:S(2)}, u32[]{:S(2)}) collective-permute-start(bf16[128,256]{1,0:T(8,128)(2,1)S(1)} %get-tuple-element.42), channel_id=1, source_target_pairs={{1,0},{2,1},{3,2},{5,4},{6,5},{7,6},{9,8},{10,9},{11,10},{13,12},{... | collective-permute-start | bytes 196616 | tf_op jit(solution)/shard_map/ppermute | solution.py:15
  17.6 4.4 %collective-permute-start.2 = (bf16[128,256]{1,0:T(8,128)(2,1)S(1)}, bf16[128,256]{1,0:T(8,128)(2,1)S(1)}, u32[]{:S(2)}, u32[]{:S(2)}) collective-permute-start(bf16[128,256]{1,0:T(8,128)(2,1)S(1)} %get-tuple-element.43), channel_id=1, source_target_pairs={{0,1},{1,2},{2,3},{4,5},{5,6},{6,7},{8,9},{9,10},{10,11},{12,13},{... | collective-permute-start | bytes 196616 | tf_op jit(solution)/shard_map/ppermute | solution.py:15
  20.6 6.7 %collective-permute-start.1 = (bf16[128,256]{1,0:T(8,128)(2,1)S(1)}, bf16[128,256]{1,0:T(8,128)(2,1)S(1)}, u32[]{:S(2)}, u32[]{:S(2)}) collective-permute-start(bf16[128,256]{1,0:T(8,128)(2,1)S(1)} %get-tuple-element.44), channel_id=1, source_target_pairs={{4,0},{8,4},{12,8},{16,12},{20,16},{24,20},{28,24},{5,1},{9,5},{13... | collective-permute-start | bytes 196616 | tf_op jit(solution)/shard_map/ppermute | solution.py:15
  33.9 205.9 %reduce-scatter.12.cloned.1.call-start = ((), (), s32[]{:S(2)}) async-start(), calls=%async_computation.4 | async-start | bytes 147456
  97.1 9.4 %collective-permute-start.4 = (bf16[128,256]{0,1:T(8,128)(2,1)S(1)}, bf16[128,256]{0,1:T(8,128)(2,1)S(1)}, u32[]{:S(2)}, u32[]{:S(2)}) collective-permute-start(bf16[128,256]{0,1:T(8,128)(2,1)S(1)} %get-tuple-element.21), channel_id=1, source_target_pairs={{0,4},{4,8},{8,12},{12,16},{16,20},{20,24},{24,28},{1,5},{5,9},{9,... | collective-permute-start | bytes 196616 | tf_op jit(solution)/shard_map/ppermute | solution.py:15
  100.4 6.1 %collective-permute-start.7 = (bf16[128,256]{0,1:T(8,128)(2,1)S(1)}, bf16[128,256]{0,1:T(8,128)(2,1)S(1)}, u32[]{:S(2)}, u32[]{:S(2)}) collective-permute-start(bf16[128,256]{0,1:T(8,128)(2,1)S(1)} %get-tuple-element.22), channel_id=1, source_target_pairs={{1,0},{2,1},{3,2},{5,4},{6,5},{7,6},{9,8},{10,9},{11,10},{13,12},{... | collective-permute-start | bytes 196616 | tf_op jit(solution)/shard_map/ppermute | solution.py:15
  101.7 4.8 %collective-permute-start.6 = (bf16[128,256]{0,1:T(8,128)(2,1)S(1)}, bf16[128,256]{0,1:T(8,128)(2,1)S(1)}, u32[]{:S(2)}, u32[]{:S(2)}) collective-permute-start(bf16[128,256]{0,1:T(8,128)(2,1)S(1)} %get-tuple-element.23), channel_id=1, source_target_pairs={{0,1},{1,2},{2,3},{4,5},{5,6},{6,7},{8,9},{9,10},{10,11},{12,13},{... | collective-permute-start | bytes 196616 | tf_op jit(solution)/shard_map/ppermute | solution.py:15
  104.8 6.7 %collective-permute-start.5 = (bf16[128,256]{0,1:T(8,128)(2,1)S(1)}, bf16[128,256]{0,1:T(8,128)(2,1)S(1)}, u32[]{:S(2)}, u32[]{:S(2)}) collective-permute-start(bf16[128,256]{0,1:T(8,128)(2,1)S(1)} %get-tuple-element.24), channel_id=1, source_target_pairs={{4,0},{8,4},{12,8},{16,12},{20,16},{24,20},{28,24},{5,1},{9,5},{13... | collective-permute-start | bytes 196616 | tf_op jit(solution)/shard_map/ppermute | solution.py:15
  117.9 9.8 %collective-permute-start.8 = (bf16[128,256]{1,0:T(8,128)(2,1)S(1)}, bf16[128,256]{1,0:T(8,128)(2,1)S(1)}, u32[]{:S(2)}, u32[]{:S(2)}) collective-permute-start(bf16[128,256]{1,0:T(8,128)(2,1)S(1)} %get-tuple-element.37), channel_id=1, source_target_pairs={{0,4},{4,8},{8,12},{12,16},{16,20},{20,24},{24,28},{1,5},{5,9},{9,... | collective-permute-start | bytes 196616 | tf_op jit(solution)/shard_map/ppermute | solution.py:15
  122.1 5.7 %collective-permute-start.11 = (bf16[128,256]{1,0:T(8,128)(2,1)S(1)}, bf16[128,256]{1,0:T(8,128)(2,1)S(1)}, u32[]{:S(2)}, u32[]{:S(2)}) collective-permute-start(bf16[128,256]{1,0:T(8,128)(2,1)S(1)} %get-tuple-element.38), channel_id=1, source_target_pairs={{1,0},{2,1},{3,2},{5,4},{6,5},{7,6},{9,8},{10,9},{11,10},{13,12},{... | collective-permute-start | bytes 196616 | tf_op jit(solution)/shard_map/ppermute | solution.py:15
  123.4 4.4 %collective-permute-start.10 = (bf16[128,256]{1,0:T(8,128)(2,1)S(1)}, bf16[128,256]{1,0:T(8,128)(2,1)S(1)}, u32[]{:S(2)}, u32[]{:S(2)}) collective-permute-start(bf16[128,256]{1,0:T(8,128)(2,1)S(1)} %get-tuple-element.39), channel_id=1, source_target_pairs={{0,1},{1,2},{2,3},{4,5},{5,6},{6,7},{8,9},{9,10},{10,11},{12,13},{... | collective-permute-start | bytes 196616 | tf_op jit(solution)/shard_map/ppermute | solution.py:15
  126.4 6.8 %collective-permute-start.9 = (bf16[128,256]{1,0:T(8,128)(2,1)S(1)}, bf16[128,256]{1,0:T(8,128)(2,1)S(1)}, u32[]{:S(2)}, u32[]{:S(2)}) collective-permute-start(bf16[128,256]{1,0:T(8,128)(2,1)S(1)} %get-tuple-element.40), channel_id=1, source_target_pairs={{4,0},{8,4},{12,8},{16,12},{20,16},{24,20},{28,24},{5,1},{9,5},{13... | collective-permute-start | bytes 196616 | tf_op jit(solution)/shard_map/ppermute | solution.py:15
  137.0 11.7 %collective-permute-start.12 = (bf16[128,256]{0,1:T(8,128)(2,1)S(1)}, bf16[128,256]{0,1:T(8,128)(2,1)S(1)}, u32[]{:S(2)}, u32[]{:S(2)}) collective-permute-start(bf16[128,256]{0,1:T(8,128)(2,1)S(1)} %get-tuple-element.17), channel_id=1, source_target_pairs={{0,4},{4,8},{8,12},{12,16},{16,20},{20,24},{24,28},{1,5},{5,9},{9,... | collective-permute-start | bytes 196616 | tf_op jit(solution)/shard_map/ppermute | solution.py:15
  140.5 8.3 %collective-permute-start.15 = (bf16[128,256]{0,1:T(8,128)(2,1)S(1)}, bf16[128,256]{0,1:T(8,128)(2,1)S(1)}, u32[]{:S(2)}, u32[]{:S(2)}) collective-permute-start(bf16[128,256]{0,1:T(8,128)(2,1)S(1)} %get-tuple-element.18), channel_id=1, source_target_pairs={{1,0},{2,1},{3,2},{5,4},{6,5},{7,6},{9,8},{10,9},{11,10},{13,12},{... | collective-permute-start | bytes 196616 | tf_op jit(solution)/shard_map/ppermute | solution.py:15
  141.8 7.0 %collective-permute-start.14 = (bf16[128,256]{0,1:T(8,128)(2,1)S(1)}, bf16[128,256]{0,1:T(8,128)(2,1)S(1)}, u32[]{:S(2)}, u32[]{:S(2)}) collective-permute-start(bf16[128,256]{0,1:T(8,128)(2,1)S(1)} %get-tuple-element.19), channel_id=1, source_target_pairs={{0,1},{1,2},{2,3},{4,5},{5,6},{6,7},{8,9},{9,10},{10,11},{12,13},{... | collective-permute-start | bytes 196616 | tf_op jit(solution)/shard_map/ppermute | solution.py:15
  144.8 6.8 %collective-permute-start.13 = (bf16[128,256]{0,1:T(8,128)(2,1)S(1)}, bf16[128,256]{0,1:T(8,128)(2,1)S(1)}, u32[]{:S(2)}, u32[]{:S(2)}) collective-permute-start(bf16[128,256]{0,1:T(8,128)(2,1)S(1)} %get-tuple-element.20), channel_id=1, source_target_pairs={{4,0},{8,4},{12,8},{16,12},{20,16},{24,20},{28,24},{5,1},{9,5},{13... | collective-permute-start | bytes 196616 | tf_op jit(solution)/shard_map/ppermute | solution.py:15
  159.4 9.1 %collective-permute-start.16 = (bf16[128,256]{1,0:T(8,128)(2,1)S(1)}, bf16[128,256]{1,0:T(8,128)(2,1)S(1)}, u32[]{:S(2)}, u32[]{:S(2)}) collective-permute-start(bf16[128,256]{1,0:T(8,128)(2,1)S(1)} %get-tuple-element.33), channel_id=1, source_target_pairs={{0,4},{4,8},{8,12},{12,16},{16,20},{20,24},{24,28},{1,5},{5,9},{9,... | collective-permute-start | bytes 196616 | tf_op jit(solution)/shard_map/ppermute | solution.py:15
  162.8 5.7 %collective-permute-start.19 = (bf16[128,256]{1,0:T(8,128)(2,1)S(1)}, bf16[128,256]{1,0:T(8,128)(2,1)S(1)}, u32[]{:S(2)}, u32[]{:S(2)}) collective-permute-start(bf16[128,256]{1,0:T(8,128)(2,1)S(1)} %get-tuple-element.34), channel_id=1, source_target_pairs={{1,0},{2,1},{3,2},{5,4},{6,5},{7,6},{9,8},{10,9},{11,10},{13,12},{... | collective-permute-start | bytes 196616 | tf_op jit(solution)/shard_map/ppermute | solution.py:15
  164.1 4.4 %collective-permute-start.18 = (bf16[128,256]{1,0:T(8,128)(2,1)S(1)}, bf16[128,256]{1,0:T(8,128)(2,1)S(1)}, u32[]{:S(2)}, u32[]{:S(2)}) collective-permute-start(bf16[128,256]{1,0:T(8,128)(2,1)S(1)} %get-tuple-element.35), channel_id=1, source_target_pairs={{0,1},{1,2},{2,3},{4,5},{5,6},{6,7},{8,9},{9,10},{10,11},{12,13},{... | collective-permute-start | bytes 196616 | tf_op jit(solution)/shard_map/ppermute | solution.py:15
  167.1 6.8 %collective-permute-start.17 = (bf16[128,256]{1,0:T(8,128)(2,1)S(1)}, bf16[128,256]{1,0:T(8,128)(2,1)S(1)}, u32[]{:S(2)}, u32[]{:S(2)}) collective-permute-start(bf16[128,256]{1,0:T(8,128)(2,1)S(1)} %get-tuple-element.36), channel_id=1, source_target_pairs={{4,0},{8,4},{12,8},{16,12},{20,16},{24,20},{28,24},{5,1},{9,5},{13... | collective-permute-start | bytes 196616 | tf_op jit(solution)/shard_map/ppermute | solution.py:15
  173.9 0.7 copy-start.3
  180.8 212.8 %reduce-scatter.14.cloned.1.call-start = ((), (), s32[]{:S(2)}) async-start(), calls=%async_computation.5 | async-start | bytes 147456
  241.6 9.4 %collective-permute-start.20 = (bf16[128,256]{0,1:T(8,128)(2,1)}, bf16[128,256]{0,1:T(8,128)(2,1)S(1)}, u32[]{:S(2)}, u32[]{:S(2)}) collective-permute-start(bf16[128,256]{0,1:T(8,128)(2,1)} %get-tuple-element.13), channel_id=1, source_target_pairs={{0,4},{4,8},{8,12},{12,16},{16,20},{20,24},{24,28},{1,5},{5,9},{9,... | collective-permute-start | bytes 196616 | tf_op jit(solution)/shard_map/ppermute | solution.py:15
  244.9 6.1 %collective-permute-start.23 = (bf16[128,256]{0,1:T(8,128)(2,1)}, bf16[128,256]{0,1:T(8,128)(2,1)S(1)}, u32[]{:S(2)}, u32[]{:S(2)}) collective-permute-start(bf16[128,256]{0,1:T(8,128)(2,1)} %get-tuple-element.14), channel_id=1, source_target_pairs={{1,0},{2,1},{3,2},{5,4},{6,5},{7,6},{9,8},{10,9},{11,10},{13,12},{... | collective-permute-start | bytes 196616 | tf_op jit(solution)/shard_map/ppermute | solution.py:15
  246.2 4.8 %collective-permute-start.22 = (bf16[128,256]{0,1:T(8,128)(2,1)}, bf16[128,256]{0,1:T(8,128)(2,1)S(1)}, u32[]{:S(2)}, u32[]{:S(2)}) collective-permute-start(bf16[128,256]{0,1:T(8,128)(2,1)} %get-tuple-element.15), channel_id=1, source_target_pairs={{0,1},{1,2},{2,3},{4,5},{5,6},{6,7},{8,9},{9,10},{10,11},{12,13},{... | collective-permute-start | bytes 196616 | tf_op jit(solution)/shard_map/ppermute | solution.py:15
  249.3 7.0 %collective-permute-start.21 = (bf16[128,256]{0,1:T(8,128)(2,1)}, bf16[128,256]{0,1:T(8,128)(2,1)}, u32[]{:S(2)}, u32[]{:S(2)}) collective-permute-start(bf16[128,256]{0,1:T(8,128)(2,1)} %get-tuple-element.16), channel_id=1, source_target_pairs={{4,0},{8,4},{12,8},{16,12},{20,16},{24,20},{28,24},{5,1},{9,5},{13... | collective-permute-start | bytes 196616 | tf_op jit(solution)/shard_map/ppermute | solution.py:15
  263.5 9.9 %collective-permute-start.24 = (bf16[128,256]{1,0:T(8,128)(2,1)S(1)}, bf16[128,256]{1,0:T(8,128)(2,1)S(1)}, u32[]{:S(2)}, u32[]{:S(2)}) collective-permute-start(bf16[128,256]{1,0:T(8,128)(2,1)S(1)} %get-tuple-element.29), channel_id=1, source_target_pairs={{0,4},{4,8},{8,12},{12,16},{16,20},{20,24},{24,28},{1,5},{5,9},{9,... | collective-permute-start | bytes 196616 | tf_op jit(solution)/shard_map/ppermute | solution.py:15
  267.8 5.7 %collective-permute-start.27 = (bf16[128,256]{1,0:T(8,128)(2,1)S(1)}, bf16[128,256]{1,0:T(8,128)(2,1)S(1)}, u32[]{:S(2)}, u32[]{:S(2)}) collective-permute-start(bf16[128,256]{1,0:T(8,128)(2,1)S(1)} %get-tuple-element.30), channel_id=1, source_target_pairs={{1,0},{2,1},{3,2},{5,4},{6,5},{7,6},{9,8},{10,9},{11,10},{13,12},{... | collective-permute-start | bytes 196616 | tf_op jit(solution)/shard_map/ppermute | solution.py:15
  269.1 4.4 %collective-permute-start.26 = (bf16[128,256]{1,0:T(8,128)(2,1)S(1)}, bf16[128,256]{1,0:T(8,128)(2,1)S(1)}, u32[]{:S(2)}, u32[]{:S(2)}) collective-permute-start(bf16[128,256]{1,0:T(8,128)(2,1)S(1)} %get-tuple-element.31), channel_id=1, source_target_pairs={{0,1},{1,2},{2,3},{4,5},{5,6},{6,7},{8,9},{9,10},{10,11},{12,13},{... | collective-permute-start | bytes 196616 | tf_op jit(solution)/shard_map/ppermute | solution.py:15
  272.1 6.8 %collective-permute-start.25 = (bf16[128,256]{1,0:T(8,128)(2,1)S(1)}, bf16[128,256]{1,0:T(8,128)(2,1)S(1)}, u32[]{:S(2)}, u32[]{:S(2)}) collective-permute-start(bf16[128,256]{1,0:T(8,128)(2,1)S(1)} %get-tuple-element.32), channel_id=1, source_target_pairs={{4,0},{8,4},{12,8},{16,12},{20,16},{24,20},{28,24},{5,1},{9,5},{13... | collective-permute-start | bytes 196616 | tf_op jit(solution)/shard_map/ppermute | solution.py:15
  283.4 11.9 %collective-permute-start.28 = (bf16[128,256]{0,1:T(8,128)(2,1)}, bf16[128,256]{0,1:T(8,128)(2,1)S(1)}, u32[]{:S(2)}, u32[]{:S(2)}) collective-permute-start(bf16[128,256]{0,1:T(8,128)(2,1)} %get-tuple-element.9), channel_id=1, source_target_pairs={{0,4},{4,8},{8,12},{12,16},{16,20},{20,24},{24,28},{1,5},{5,9},{9,... | collective-permute-start | bytes 196616 | tf_op jit(solution)/shard_map/ppermute | solution.py:15
  286.9 8.5 %collective-permute-start.31 = (bf16[128,256]{0,1:T(8,128)(2,1)}, bf16[128,256]{0,1:T(8,128)(2,1)S(1)}, u32[]{:S(2)}, u32[]{:S(2)}) collective-permute-start(bf16[128,256]{0,1:T(8,128)(2,1)} %get-tuple-element.10), channel_id=1, source_target_pairs={{1,0},{2,1},{3,2},{5,4},{6,5},{7,6},{9,8},{10,9},{11,10},{13,12},{... | collective-permute-start | bytes 196616 | tf_op jit(solution)/shard_map/ppermute | solution.py:15
  288.2 7.2 %collective-permute-start.30 = (bf16[128,256]{0,1:T(8,128)(2,1)}, bf16[128,256]{0,1:T(8,128)(2,1)S(1)}, u32[]{:S(2)}, u32[]{:S(2)}) collective-permute-start(bf16[128,256]{0,1:T(8,128)(2,1)} %get-tuple-element.11), channel_id=1, source_target_pairs={{0,1},{1,2},{2,3},{4,5},{5,6},{6,7},{8,9},{9,10},{10,11},{12,13},{... | collective-permute-start | bytes 196616 | tf_op jit(solution)/shard_map/ppermute | solution.py:15
  291.4 7.1 %collective-permute-start.29 = (bf16[128,256]{0,1:T(8,128)(2,1)}, bf16[128,256]{0,1:T(8,128)(2,1)}, u32[]{:S(2)}, u32[]{:S(2)}) collective-permute-start(bf16[128,256]{0,1:T(8,128)(2,1)} %get-tuple-element.12), channel_id=1, source_target_pairs={{4,0},{8,4},{12,8},{16,12},{20,16},{24,20},{28,24},{5,1},{9,5},{13... | collective-permute-start | bytes 196616 | tf_op jit(solution)/shard_map/ppermute | solution.py:15
  310.5 17.5 %copy-start.1 = (bf16[1024,256]{1,0:T(8,128)(2,1)S(1)}, bf16[1024,256]{1,0:T(8,128)(2,1)}, u32[]{:S(2)}) copy-start(bf16[1024,256]{1,0:T(8,128)(2,1)} %fusion.26) | copy-start | bytes 1572868
  313.4 9.1 %collective-permute-start.32 = (bf16[128,256]{1,0:T(8,128)(2,1)S(1)}, bf16[128,256]{1,0:T(8,128)(2,1)S(1)}, u32[]{:S(2)}, u32[]{:S(2)}) collective-permute-start(bf16[128,256]{1,0:T(8,128)(2,1)S(1)} %get-tuple-element.25), channel_id=1, source_target_pairs={{0,4},{4,8},{8,12},{12,16},{16,20},{20,24},{24,28},{1,5},{5,9},{9,... | collective-permute-start | bytes 196616 | tf_op jit(solution)/shard_map/ppermute | solution.py:15
  316.9 5.7 %collective-permute-start.35 = (bf16[128,256]{1,0:T(8,128)(2,1)S(1)}, bf16[128,256]{1,0:T(8,128)(2,1)S(1)}, u32[]{:S(2)}, u32[]{:S(2)}) collective-permute-start(bf16[128,256]{1,0:T(8,128)(2,1)S(1)} %get-tuple-element.26), channel_id=1, source_target_pairs={{1,0},{2,1},{3,2},{5,4},{6,5},{7,6},{9,8},{10,9},{11,10},{13,12},{... | collective-permute-start | bytes 196616 | tf_op jit(solution)/shard_map/ppermute | solution.py:15
  318.2 4.4 %collective-permute-start.34 = (bf16[128,256]{1,0:T(8,128)(2,1)S(1)}, bf16[128,256]{1,0:T(8,128)(2,1)S(1)}, u32[]{:S(2)}, u32[]{:S(2)}) collective-permute-start(bf16[128,256]{1,0:T(8,128)(2,1)S(1)} %get-tuple-element.27), channel_id=1, source_target_pairs={{0,1},{1,2},{2,3},{4,5},{5,6},{6,7},{8,9},{9,10},{10,11},{12,13},{... | collective-permute-start | bytes 196616 | tf_op jit(solution)/shard_map/ppermute | solution.py:15
  321.2 6.8 %collective-permute-start.33 = (bf16[128,256]{1,0:T(8,128)(2,1)S(1)}, bf16[128,256]{1,0:T(8,128)(2,1)S(1)}, u32[]{:S(2)}, u32[]{:S(2)}) collective-permute-start(bf16[128,256]{1,0:T(8,128)(2,1)S(1)} %get-tuple-element.28), channel_id=1, source_target_pairs={{4,0},{8,4},{12,8},{16,12},{20,16},{24,20},{28,24},{5,1},{9,5},{13... | collective-permute-start | bytes 196616 | tf_op jit(solution)/shard_map/ppermute | solution.py:15
  396.2 11.6 %collective-permute-start.36 = (bf16[128,256]{0,1:T(8,128)(2,1)}, bf16[128,256]{0,1:T(8,128)(2,1)S(1)}, u32[]{:S(2)}, u32[]{:S(2)}) collective-permute-start(bf16[128,256]{0,1:T(8,128)(2,1)} %get-tuple-element.5), channel_id=1, source_target_pairs={{0,4},{4,8},{8,12},{12,16},{16,20},{20,24},{24,28},{1,5},{5,9},{9,... | collective-permute-start | bytes 196616 | tf_op jit(solution)/shard_map/ppermute | solution.py:15
  399.5 8.3 %collective-permute-start.39 = (bf16[128,256]{0,1:T(8,128)(2,1)}, bf16[128,256]{0,1:T(8,128)(2,1)S(1)}, u32[]{:S(2)}, u32[]{:S(2)}) collective-permute-start(bf16[128,256]{0,1:T(8,128)(2,1)} %get-tuple-element.6), channel_id=1, source_target_pairs={{1,0},{2,1},{3,2},{5,4},{6,5},{7,6},{9,8},{10,9},{11,10},{13,12},{... | collective-permute-start | bytes 196616 | tf_op jit(solution)/shard_map/ppermute | solution.py:15
  400.8 7.0 %collective-permute-start.38 = (bf16[128,256]{0,1:T(8,128)(2,1)}, bf16[128,256]{0,1:T(8,128)(2,1)S(1)}, u32[]{:S(2)}, u32[]{:S(2)}) collective-permute-start(bf16[128,256]{0,1:T(8,128)(2,1)} %get-tuple-element.7), channel_id=1, source_target_pairs={{0,1},{1,2},{2,3},{4,5},{5,6},{6,7},{8,9},{9,10},{10,11},{12,13},{... | collective-permute-start | bytes 196616 | tf_op jit(solution)/shard_map/ppermute | solution.py:15
  403.8 7.0 %collective-permute-start.37 = (bf16[128,256]{0,1:T(8,128)(2,1)}, bf16[128,256]{0,1:T(8,128)(2,1)S(1)}, u32[]{:S(2)}, u32[]{:S(2)}) collective-permute-start(bf16[128,256]{0,1:T(8,128)(2,1)} %get-tuple-element.8), channel_id=1, source_target_pairs={{4,0},{8,4},{12,8},{16,12},{20,16},{24,20},{28,24},{5,1},{9,5},{13... | collective-permute-start | bytes 196616 | tf_op jit(solution)/shard_map/ppermute | solution.py:15
Sparse Core Ops, SparseCore 0:
  34.0 61.8 reduce-scatter.9
  181.0 58.7 reduce-scatter.11
  334.6 58.9 reduce-scatter.13
where the time goes:
time: 430 us; the launch traced here: 428 us
  waiting for transfers between devices  214 us (50%)
  starting transfers between devices  93.4 us (22%)
  other arithmetic  36.1 us (8%)
  local copies, waits for them, and re-layouts  29 us (7%)
  matrix products  25.5 us (6%)
  blocking collectives  15.7 us (4%)
  between operations  14.1 us (3%)
    unnamed x6, waiting for transfers between devices  167 us
    ppermute x40, starting transfers between devices, passed_along(): return lax.ppermute(shard, axis, pairs)  93.3 us
    ppermute x40, waiting for transfers between devices, passed_along(): return lax.ppermute(shard, axis, pairs)  46.4 us
    scatter-add x5, other arithmetic, owner_sum(): summed = jnp.zeros((own_rows, columns), jnp.float32).at[flat_rows].add(we...  19.7 us
    all_gather x3, blocking collectives, per_device(): block_rows = lax.all_gather(restricted, 'col', axis=0, tiled=True)  15.7 us
    dot_general x3, matrix products, per_device(): jnp.dot(inverse, residual_local, preferred_element_type=jnp.float32)  12.6 us
    gather x5, local copies, waits for them, and re-layouts, with_ghosts(): packed = values_half[flat_rows].reshape(4, tile_rows, columns) * live_half  10.6 us
    slice x10, local copies, waits for them, and re-layouts, owner_sum(): return local_terms[:own_rows] + summed  8.67 us
  transfers between devices with their start and end apart: 43, of which 13 were waited for; matrix products, arithmetic and copies ran while one was open for 5% of the time, Pallas kernels for 0%

commit v1 on v0

v1 whole, which is shorter than its diff:
```python
import jax
import jax.numpy as jnp
from jax import lax
from jax.experimental import pallas as pl
from jax.experimental.pallas import tpu as pltpu
from jax.sharding import PartitionSpec as P

ITERS = 3
DAMPING = 0.5
HALF = jnp.bfloat16
FULL = jnp.float32


def product(left, right):
    return jnp.dot(left, right, preferred_element_type=FULL)


def turned_product(left, right):
    return lax.dot_general(left, right, (((0,), (0,)), ((), ())), preferred_element_type=FULL)


def call(body, name, outs, *args, flops=0):
    here = pl.BlockSpec(memory_space=pltpu.VMEM)
    size = sum(a.size * a.dtype.itemsize for a in args)
    return pl.pallas_call(
        body,
        out_shape=tuple(pltpu.VMEM(shape, dtype) for shape, dtype in outs),
        in_specs=[here] * len(args),
        out_specs=tuple(here for _ in outs),
        compiler_params=pltpu.CompilerParams(vmem_limit_bytes=24 * 1024 * 1024),
        cost_estimate=pl.CostEstimate(flops=flops, bytes_accessed=size, transcendentals=0),
        name=name,
    )(*(pltpu.with_memory_space_constraint(a, pltpu.VMEM) for a in args))


def select_kernel(target, rows, counts, half, pick, spread, *tiles):
    own = target.shape[0]
    tile = rows.shape[1]
    half[...] = target[...].astype(HALF)
    for d in range(4):
        here = jnp.where(
            lax.broadcasted_iota(jnp.int32, (1, tile), 1) < counts[d : d + 1, :],
            rows[d : d + 1, :],
            -1,
        )
        wide = jnp.broadcast_to(here, (own, tile))
        spread[:, d * tile : (d + 1) * tile] = (
            lax.broadcasted_iota(jnp.int32, (own, tile), 0) == wide
        ).astype(FULL).astype(HALF)
        down = jnp.transpose(jnp.broadcast_to(here, (tile, tile)))[:, :1]
        pick[d * tile : (d + 1) * tile, :] = (
            lax.broadcasted_iota(jnp.int32, (tile, own), 1) == down
        ).astype(FULL).astype(HALF)
    for d in range(4):
        tiles[d][...] = product(pick[d * tile : (d + 1) * tile, :], half[...]).astype(HALF)


def own_columns_kernel(matrix, owned, out):
    own = owned.shape[0]
    out[...] = product(matrix[:, :own], owned[...])


def restrict_kernel(basis, owned, g0, g1, g2, g3, out):
    own, tile = owned.shape[0], g0.shape[0]
    total = turned_product(basis[:own, :], owned[...])
    for d, ghost in enumerate((g0, g1, g2, g3)):
        total += turned_product(basis[own + d * tile : own + (d + 1) * tile, :], ghost[...])
    out[...] = total.astype(HALF)


def stacked(g0, g1, g2, g3):
    return jnp.concatenate([g0[...], g1[...], g2[...], g3[...]], axis=0)


def margin_columns_kernel(matrix, partial, g0, g1, g2, g3, out):
    own = matrix.shape[1] - 4 * g0.shape[0]
    out[...] = partial[...] + product(matrix[:, own:], stacked(g0, g1, g2, g3))


def coarse_kernel(coarse_rows, gathered, basis, local, level, *tiles):
    tile = tiles[0].shape[0]
    own = local.shape[0] - 4 * tile
    level[...] = product(coarse_rows[...], gathered[...]).astype(HALF)
    for d in range(4):
        at = slice(own + d * tile, own + (d + 1) * tile)
        tiles[d][...] = (local[at, :] + product(basis[at, :], level[...])).astype(HALF)


def rim_kernel(matrix, partial, g0, g1, g2, g3, *tiles):
    tile = g0.shape[0]
    own = matrix.shape[1] - 4 * tile
    ghosts = stacked(g0, g1, g2, g3)
    for d in range(4):
        at = slice(own + d * tile, own + (d + 1) * tile)
        tiles[d][...] = (partial[at, :] + product(matrix[at, own:], ghosts)).astype(HALF)


def inner_kernel(matrix, partial, g0, g1, g2, g3, out):
    own = matrix.shape[1] - 4 * g0.shape[0]
    out[...] = partial[:own, :] + product(matrix[:own, own:], stacked(g0, g1, g2, g3))


def update_kernel(first, last):
    def body(*refs):
        refs = list(refs)
        before = None if first else refs.pop(0)
        local, level, basis, pick, spread, r0, r1, r2, r3, after, *rest = refs
        own = after.shape[0]
        update = (
            local[:own, :]
            + product(basis[:own, :], level[...])
            + product(spread[...], stacked(r0, r1, r2, r3))
        )
        after[...] = DAMPING * update if first else before[...] + DAMPING * update
        if last:
            return
        half, *tiles = rest
        tile = tiles[0].shape[0]
        half[...] = after[...].astype(HALF)
        for d in range(4):
            tiles[d][...] = product(pick[d * tile : (d + 1) * tile, :], half[...]).astype(HALF)

    return body


def residual_kernel(target, image, pick, spread, r0, r1, r2, r3, half, *tiles):
    tile = tiles[0].shape[0]
    half[...] = (
        target[...] - (image[...] + product(spread[...], stacked(r0, r1, r2, r3)))
    ).astype(HALF)
    for d in range(4):
        tiles[d][...] = product(pick[d * tile : (d + 1) * tile, :], half[...]).astype(HALF)


def passed_along(shard, axis, by):
    devices = lax.axis_size(axis)
    pairs = [(i, i + by) for i in range(devices) if 0 <= i + by < devices]
    return lax.ppermute(shard, axis, pairs)


def traded(tiles):
    return (
        passed_along(tiles[1], "row", 1),
        passed_along(tiles[0], "row", -1),
        passed_along(tiles[3], "col", 1),
        passed_along(tiles[2], "col", -1),
    )


def per_device(
    right_side, local_operator, local_inverse, coarse_basis, coarse_inverse, send_rows, send_count
):
    target = right_side[0, 0]
    operator = local_operator[0, 0]
    inverse = local_inverse[0, 0]
    basis = coarse_basis[0, 0]
    rows_list = send_rows[0, 0]
    own, columns = target.shape
    local = operator.shape[0]
    tile = rows_list.shape[1]
    margin = 4 * tile
    coarse = basis.shape[1]
    counts = jnp.broadcast_to(send_count[0, 0][:, None], rows_list.shape)
    coarse_rows = lax.all_to_all(coarse_inverse, "row", 0, 2, tiled=True)[0]

    four_tiles = [((tile, columns), HALF)] * 4
    owned_half = ((own, columns), HALF)
    residual, pick, spread, *tiles = call(
        select_kernel,
        "select",
        [owned_half, ((margin, own), HALF), ((own, margin), HALF)] + four_tiles,
        target,
        rows_list,
        counts,
        flops=2 * margin * own * columns,
    )
    solution = None
    for sweep in range(ITERS):
        if sweep:
            ghosts = traded(tiles)
            (partial,) = call(
                own_columns_kernel,
                "operator_own",
                [((local, columns), FULL)],
                operator,
                solution_half,
                flops=2 * local * own * columns,
            )
            tiles = call(
                rim_kernel,
                "operator_rim",
                four_tiles,
                operator,
                partial,
                *ghosts,
                flops=2 * margin * margin * columns,
            )
            returned = traded(tiles)
            (image,) = call(
                inner_kernel,
                "operator_inner",
                [((own, columns), FULL)],
                operator,
                partial,
                *ghosts,
                flops=2 * own * margin * columns,
            )
            residual, *tiles = call(
                residual_kernel,
                "residual",
                [owned_half] + four_tiles,
                target,
                image,
                pick,
                spread,
                *returned,
                flops=4 * margin * own * columns,
            )
        ghosts = traded(tiles)
        (partial,) = call(
            own_columns_kernel,
            "inverse_own",
            [((local, columns), FULL)],
            inverse,
            residual,
            flops=2 * local * own * columns,
        )
        (restricted,) = call(
            restrict_kernel,
            "restrict",
            [((coarse, columns), HALF)],
            basis,
            residual,
            *ghosts,
            flops=2 * local * coarse * columns,
        )
        gathered = lax.all_gather(restricted, ("row", "col"), axis=0, tiled=True)
        (correction,) = call(
            margin_columns_kernel,
            "inverse_margin",
            [((local, columns), FULL)],
            inverse,
            partial,
            *ghosts,
            flops=2 * local * margin * columns,
        )
        level, *tiles = call(
            coarse_kernel,
            "coarse",
            [((coarse, columns), HALF)] + four_tiles,
            coarse_rows,
            gathered,
            basis,
            correction,
            flops=2 * coarse * (coarse_rows.shape[1] + margin) * columns,
        )
        returned = traded(tiles)
        first, last = sweep == 0, sweep == ITERS - 1
        before = [] if first else [solution]
        outs = [((own, columns), FULL)] + ([] if last else [owned_half] + four_tiles)
        solution, *rest = call(
            update_kernel(first, last),
            "update",
            outs,
            *before,
            correction,
            level,
            basis,
            pick,
            spread,
            *returned,
            flops=4 * margin * own * columns,
        )
        if not last:
            solution_half, *tiles = rest
    return solution[None, None]


def solution(mesh):
    return jax.shard_map(
        per_device,
        mesh=mesh,
        in_specs=(
            P("row", "col", None, None),
            P("row", "col", None, None),
            P("row", "col", None, None),
            P("row", "col", None, None),
            P(None, "col", "row"),
            P("row", "col", None, None),
            P("row", "col", None),
        ),
        out_specs=P("row", "col", None, None),
        check_vma=False,
    )
```

time: 430 us -> 285 us (0.66)
  waiting for transfers between devices: 214 us -> 12 us
  blocking collectives: 15.7 us -> 132 us
  other arithmetic: 36.1 us -> 0.01 us
  matrix products: 25.5 us -> 0 us
  Pallas kernels: 0 us -> 19.9 us
  local copies, waits for them, and re-layouts: 29 us -> 15.2 us
  between operations: 14.1 us -> 0.79 us
  starting transfers between devices: 93.4 us -> 101 us
    unnamed x6 -> x0, waiting for transfers between devices: 167 us -> none
    all_gather x3, blocking collectives: 15.7 us -> 132 us  [per_device(): gathered = lax.all_gather(restricted, ('row', 'col'), axis=0, tiled=True)]
    ppermute x40, waiting for transfers between devices: 46.4 us -> 12 us  [passed_along(): return lax.ppermute(shard, axis, pairs)]
    dot_general x14 -> x0, matrix products: 25.5 us -> none  [the longest x3 12.6 us: per_device(): jnp.dot(inverse, residual_local, preferred_element_type=jnp.float32)]
    pallas_call x0 -> x24, Pallas kernels: none -> 19.9 us  [call(): pl.pallas_call(body, out_shape=tuple((pltpu.VMEM(shape, dtype) for shape,...]
    scatter-add x5 -> x0, other arithmetic: 19.7 us -> none  [owner_sum(): summed = jnp.zeros((own_rows, columns), jnp.float32).at[flat_rows].add(we...]
    slice x15 -> x0, local copies, waits for them, and re-layouts: 10.9 us -> none  [the longest x10 8.67 us: owner_sum(): return local_terms[:own_rows] + summed]
    unnamed x11 -> x31, local copies, waits for them, and re-layouts: 2.74 us -> 13.6 us
  transfers between devices with their start and end apart: 43 -> 41, of which waited for: 13 -> 12; matrix products, arithmetic and copies ran while one was open for 5% -> 1% of each run, Pallas kernels for 0% -> 4%
where the time goes in v1:
time: 285 us; the launch traced here: 281 us
  blocking collectives  132 us (46%)
  starting transfers between devices  101 us (35%)
  Pallas kernels  19.9 us (7%)
  local copies, waits for them, and re-layouts  15.2 us (5%)
  waiting for transfers between devices  12 us (4%)
    all_gather x3, blocking collectives, per_device(): gathered = lax.all_gather(restricted, ('row', 'col'), axis=0, tiled=True)  132 us
    ppermute x40, starting transfers between devices, passed_along(): return lax.ppermute(shard, axis, pairs)  94 us
    pallas_call x24, Pallas kernels, call(): pl.pallas_call(body, out_shape=tuple((pltpu.VMEM(shape, dtype) for shape,...  19.9 us
    unnamed x31, local copies, waits for them, and re-layouts  13.6 us
    ppermute x40, waiting for transfers between devices, passed_along(): return lax.ppermute(shard, axis, pairs)  12 us
    all_to_all x1, starting transfers between devices, per_device(): coarse_rows = lax.all_to_all(coarse_inverse, 'row', 0, 2, tiled=True)[0]  7.28 us
  transfers between devices with their start and end apart: 41, of which 12 were waited for; matrix products, arithmetic and copies ran while one was open for 1% of the time, Pallas kernels for 4%

profile of v1, /device:TPU:0, one launch (start us, length us, event | category | flops | bytes accessed | tf_op | source)
XLA Modules:
  0.0 281.4 jit_solution(14255225428657488411)
XLA Ops:
  0.0 7.3 %all-to-all-start = ((bf16[8,32,128]{2,1,0:T(8,128)(2,1)}), bf16[8,32,128]{2,1,0:T(8,128)(2,1)}, u32[]{:S(2)}, u32[]{:S(2)}) async-start(bf16[8,32,128]{2,1,0:T(8,128)(2,1)} %param.11), calls=%async_computation | async-start | bytes 131072 | tf_op jit(solution)/shard_map/all_to_all | solution.py:164
  9.9 1.7 select.1
  11.6 4.5 %collective-permute-start = (bf16[128,256]{1,0:T(8,128)(2,1)}, bf16[128,256]{1,0:T(8,128)(2,1)}, u32[]{:S(2)}, u32[]{:S(2)}) collective-permute-start(bf16[128,256]{1,0:T(8,128)(2,1)} %get-tuple-element.58), channel_id=1, source_target_pairs={{0,4},{4,8},{8,12},{12,16},{16,20},{20,24},{24,28},{1,5},{5,9},{9,... | collective-permute-start | bytes 196616 | tf_op jit(solution)/shard_map/ppermute | solution.py:138
  17.4 1.9 collective-permute-start.2
  21.7 2.3 copy-done.2
  25.1 1.4 restrict.3
  26.5 46.4 %all_gather.9.gathered = bf16[1024,256]{1,0:T(8,128)(2,1)S(1)} all-gather(bf16[32,256]{1,0:T(8,128)(2,1)S(1)} %restrict.3), channel_id=1, replica_groups=mesh['row'=8,'col'=4] {'row','col'}, dimensions={0}, use_global_device_ids=true | all-gather | bytes 540672 | tf_op jit(solution)/shard_map/all_gather | solution.py:237
  72.9 1.5 inverse_margin.3.local.refs_0_
  76.5 1.4 copy-done.4
  78.4 1.3 collective-permute-start.4
  79.7 1.3 collective-permute-start.5
  81.0 2.3 collective-permute-start.6
  83.3 1.3 collective-permute-start.7
  84.6 1.4 collective-permute-done.5.refs_6_
  86.4 1.4 update.3
  87.8 4.3 %collective-permute-start.8 = (bf16[128,256]{1,0:T(8,128)(2,1)S(1)}, bf16[128,256]{1,0:T(8,128)(2,1)S(1)}, u32[]{:S(2)}, u32[]{:S(2)}) collective-permute-start(bf16[128,256]{1,0:T(8,128)(2,1)S(1)} %get-tuple-element.71), channel_id=1, source_target_pairs={{0,4},{4,8},{8,12},{12,16},{16,20},{20,24},{24,28},{1,5},{5,9},{9,... | collective-permute-start | bytes 196616 | tf_op jit(solution)/shard_map/ppermute | solution.py:138
  92.1 1.3 collective-permute-start.9
  93.4 4.1 %collective-permute-start.10 = (bf16[128,256]{1,0:T(8,128)(2,1)S(1)}, bf16[128,256]{1,0:T(8,128)(2,1)S(1)}, u32[]{:S(2)}, u32[]{:S(2)}) collective-permute-start(bf16[128,256]{1,0:T(8,128)(2,1)S(1)} %get-tuple-element.73), channel_id=1, source_target_pairs={{0,1},{1,2},{2,3},{4,5},{5,6},{6,7},{8,9},{9,10},{10,11},{12,13},{... | collective-permute-start | bytes 196616 | tf_op jit(solution)/shard_map/ppermute | solution.py:138
  97.4 1.3 collective-permute-start.11
  98.8 2.3 copy-done
  102.1 2.3 copy-done.1
  104.8 4.3 %collective-permute-start.12 = (bf16[128,256]{1,0:T(8,128)(2,1)S(1)}, bf16[128,256]{1,0:T(8,128)(2,1)S(1)}, u32[]{:S(2)}, u32[]{:S(2)}) collective-permute-start(bf16[128,256]{1,0:T(8,128)(2,1)S(1)} %get-tuple-element.75), channel_id=1, source_target_pairs={{0,4},{4,8},{8,12},{12,16},{16,20},{20,24},{24,28},{1,5},{5,9},{9,... | collective-permute-start | bytes 196616 | tf_op jit(solution)/shard_map/ppermute | solution.py:138
  109.0 1.3 collective-permute-start.13
  110.3 3.1 %collective-permute-start.14 = (bf16[128,256]{1,0:T(8,128)(2,1)S(1)}, bf16[128,256]{1,0:T(8,128)(2,1)S(1)}, u32[]{:S(2)}, u32[]{:S(2)}) collective-permute-start(bf16[128,256]{1,0:T(8,128)(2,1)S(1)} %get-tuple-element.77), channel_id=1, source_target_pairs={{0,1},{1,2},{2,3},{4,5},{5,6},{6,7},{8,9},{9,10},{10,11},{12,13},{... | collective-permute-start | bytes 196616 | tf_op jit(solution)/shard_map/ppermute | solution.py:138
  113.4 1.6 collective-permute-start.15
  115.7 2.5 collective-permute-done.15.r3
  119.5 4.5 %collective-permute-start.16 = (bf16[128,256]{1,0:T(8,128)(2,1)S(1)}, bf16[128,256]{1,0:T(8,128)(2,1)S(1)}, u32[]{:S(2)}, u32[]{:S(2)}) collective-permute-start(bf16[128,256]{1,0:T(8,128)(2,1)S(1)} %get-tuple-element.80), channel_id=1, source_target_pairs={{0,4},{4,8},{8,12},{12,16},{16,20},{20,24},{24,28},{1,5},{5,9},{9,... | collective-permute-start | bytes 196616 | tf_op jit(solution)/shard_map/ppermute | solution.py:138
  124.1 1.3 collective-permute-start.17
  125.4 4.4 %collective-permute-start.18 = (bf16[128,256]{1,0:T(8,128)(2,1)S(1)}, bf16[128,256]{1,0:T(8,128)(2,1)S(1)}, u32[]{:S(2)}, u32[]{:S(2)}) collective-permute-start(bf16[128,256]{1,0:T(8,128)(2,1)S(1)} %get-tuple-element.82), channel_id=1, source_target_pairs={{0,1},{1,2},{2,3},{4,5},{5,6},{6,7},{8,9},{9,10},{10,11},{12,13},{... | collective-permute-start | bytes 196616 | tf_op jit(solution)/shard_map/ppermute | solution.py:138
  133.2 43.0 %all_gather.10.gathered = bf16[1024,256]{1,0:T(8,128)(2,1)S(1)} all-gather(bf16[32,256]{1,0:T(8,128)(2,1)S(1)} %restrict.4), channel_id=1, replica_groups=mesh['row'=8,'col'=4] {'row','col'}, dimensions={0}, use_global_device_ids=true | all-gather | bytes 540672 | tf_op jit(solution)/shard_map/all_gather | solution.py:237
  177.2 1.3 collective-permute-start.20
  179.8 2.3 collective-permute-start.22
  183.4 1.4 collective-permute-done.21.refs_7_
  185.3 1.4 update.4
  186.6 4.3 %collective-permute-start.24 = (bf16[128,256]{1,0:T(8,128)(2,1)S(1)}, bf16[128,256]{1,0:T(8,128)(2,1)S(1)}, u32[]{:S(2)}, u32[]{:S(2)}) collective-permute-start(bf16[128,256]{1,0:T(8,128)(2,1)S(1)} %get-tuple-element.91), channel_id=1, source_target_pairs={{0,4},{4,8},{8,12},{12,16},{16,20},{20,24},{24,28},{1,5},{5,9},{9,... | collective-permute-start | bytes 196616 | tf_op jit(solution)/shard_map/ppermute | solution.py:138
  192.2 4.1 %collective-permute-start.26 = (bf16[128,256]{1,0:T(8,128)(2,1)S(1)}, bf16[128,256]{1,0:T(8,128)(2,1)S(1)}, u32[]{:S(2)}, u32[]{:S(2)}) collective-permute-start(bf16[128,256]{1,0:T(8,128)(2,1)S(1)} %get-tuple-element.93), channel_id=1, source_target_pairs={{0,1},{1,2},{2,3},{4,5},{5,6},{6,7},{8,9},{9,10},{10,11},{12,13},{... | collective-permute-start | bytes 196616 | tf_op jit(solution)/shard_map/ppermute | solution.py:138
  196.3 1.5 collective-permute-start.27
  199.8 4.3 %collective-permute-start.28 = (bf16[128,256]{1,0:T(8,128)(2,1)S(1)}, bf16[128,256]{1,0:T(8,128)(2,1)S(1)}, u32[]{:S(2)}, u32[]{:S(2)}) collective-permute-start(bf16[128,256]{1,0:T(8,128)(2,1)S(1)} %get-tuple-element.95), channel_id=1, source_target_pairs={{0,4},{4,8},{8,12},{12,16},{16,20},{20,24},{24,28},{1,5},{5,9},{9,... | collective-permute-start | bytes 196616 | tf_op jit(solution)/shard_map/ppermute | solution.py:138
  204.1 1.3 collective-permute-start.29
  205.4 4.6 %collective-permute-start.30 = (bf16[128,256]{1,0:T(8,128)(2,1)S(1)}, bf16[128,256]{1,0:T(8,128)(2,1)S(1)}, u32[]{:S(2)}, u32[]{:S(2)}) collective-permute-start(bf16[128,256]{1,0:T(8,128)(2,1)S(1)} %get-tuple-element.97), channel_id=1, source_target_pairs={{0,1},{1,2},{2,3},{4,5},{5,6},{6,7},{8,9},{9,10},{10,11},{12,13},{... | collective-permute-start | bytes 196616 | tf_op jit(solution)/shard_map/ppermute | solution.py:138
  211.7 1.4 collective-permute-done.31.r3
  214.3 4.3 %collective-permute-start.32 = (bf16[128,256]{1,0:T(8,128)(2,1)S(1)}, bf16[128,256]{1,0:T(8,128)(2,1)S(1)}, u32[]{:S(2)}, u32[]{:S(2)}) collective-permute-start(bf16[128,256]{1,0:T(8,128)(2,1)S(1)} %get-tuple-element.100), channel_id=1, source_target_pairs={{0,4},{4,8},{8,12},{12,16},{16,20},{20,24},{24,28},{1,5},{5,9},{9,... | collective-permute-start | bytes 196616 | tf_op jit(solution)/shard_map/ppermute | solution.py:138
  218.6 1.3 collective-permute-start.33
  219.9 4.6 %collective-permute-start.34 = (bf16[128,256]{1,0:T(8,128)(2,1)S(1)}, bf16[128,256]{1,0:T(8,128)(2,1)S(1)}, u32[]{:S(2)}, u32[]{:S(2)}) collective-permute-start(bf16[128,256]{1,0:T(8,128)(2,1)S(1)} %get-tuple-element.102), channel_id=1, source_target_pairs={{0,1},{1,2},{2,3},{4,5},{5,6},{6,7},{8,9},{9,10},{10,11},{12,13},{... | collective-permute-start | bytes 196616 | tf_op jit(solution)/shard_map/ppermute | solution.py:138
  227.9 42.9 %all_gather.11.gathered = bf16[1024,256]{1,0:T(8,128)(2,1)S(1)} all-gather(bf16[32,256]{1,0:T(8,128)(2,1)S(1)} %restrict.5), channel_id=1, replica_groups=mesh['row'=8,'col'=4] {'row','col'}, dimensions={0}, use_global_device_ids=true | all-gather | bytes 540672 | tf_op jit(solution)/shard_map/all_gather | solution.py:237
  271.8 1.3 collective-permute-start.36
  274.4 2.3 collective-permute-start.38
  278.0 1.4 collective-permute-done.37.refs_7_
  (97 shorter events, 36.3 us)
Async XLA Ops:
  0.0 75.6 %all-to-all-start = ((bf16[8,32,128]{2,1,0:T(8,128)(2,1)}), bf16[8,32,128]{2,1,0:T(8,128)(2,1)}, u32[]{:S(2)}, u32[]{:S(2)}) async-start(bf16[8,32,128]{2,1,0:T(8,128)(2,1)} %param.11), calls=%async_computation | async-start | bytes 131072 | tf_op jit(solution)/shard_map/all_to_all | solution.py:164
  9.9 63.0 %slice-start.2 = ((s8[4718592]{0:T(1024)(128)(4,1)}), s8[524288]{0:T(1024)(128)(4,1)S(1)}, s32[]{:S(2)}) async-start(s8[4718592]{0:T(1024)(128)(4,1)} %bitcast.25), calls=%async_computation.3 | async-start | bytes 1048576
  11.6 13.5 %collective-permute-start = (bf16[128,256]{1,0:T(8,128)(2,1)}, bf16[128,256]{1,0:T(8,128)(2,1)}, u32[]{:S(2)}, u32[]{:S(2)}) collective-permute-start(bf16[128,256]{1,0:T(8,128)(2,1)} %get-tuple-element.58), channel_id=1, source_target_pairs={{0,4},{4,8},{8,12},{12,16},{16,20},{20,24},{24,28},{1,5},{5,9},{9,... | collective-permute-start | bytes 196616 | tf_op jit(solution)/shard_map/ppermute | solution.py:138
  16.1 9.0 %collective-permute-start.1 = (bf16[128,256]{1,0:T(8,128)(2,1)}, bf16[128,256]{1,0:T(8,128)(2,1)}, u32[]{:S(2)}, u32[]{:S(2)}) collective-permute-start(bf16[128,256]{1,0:T(8,128)(2,1)} %get-tuple-element.59), channel_id=1, source_target_pairs={{4,0},{8,4},{12,8},{16,12},{20,16},{24,20},{28,24},{5,1},{9,5},{13... | collective-permute-start | bytes 196616 | tf_op jit(solution)/shard_map/ppermute | solution.py:138
  17.4 7.7 %collective-permute-start.2 = (bf16[128,256]{1,0:T(8,128)(2,1)}, bf16[128,256]{1,0:T(8,128)(2,1)}, u32[]{:S(2)}, u32[]{:S(2)}) collective-permute-start(bf16[128,256]{1,0:T(8,128)(2,1)} %get-tuple-element.60), channel_id=1, source_target_pairs={{0,1},{1,2},{2,3},{4,5},{5,6},{6,7},{8,9},{9,10},{10,11},{12,13},{... | collective-permute-start | bytes 196616 | tf_op jit(solution)/shard_map/ppermute | solution.py:138
  19.3 5.8 %collective-permute-start.3 = (bf16[128,256]{1,0:T(8,128)(2,1)}, bf16[128,256]{1,0:T(8,128)(2,1)}, u32[]{:S(2)}, u32[]{:S(2)}) collective-permute-start(bf16[128,256]{1,0:T(8,128)(2,1)} %get-tuple-element.61), channel_id=1, source_target_pairs={{1,0},{2,1},{3,2},{5,4},{6,5},{7,6},{9,8},{10,9},{11,10},{13,12},{... | collective-permute-start | bytes 196616 | tf_op jit(solution)/shard_map/ppermute | solution.py:138
  24.1 48.8 %slice-start.3 = ((s8[4718592]{0:T(1024)(128)(4,1)}), s8[4194304]{0:T(1024)(128)(4,1)S(1)}, s32[]{:S(2)}) async-start(s8[4718592]{0:T(1024)(128)(4,1)} %bitcast.25), calls=%async_computation.4 | async-start | bytes 8388608
  78.4 6.2 %collective-permute-start.4 = (bf16[128,256]{1,0:T(8,128)(2,1)S(1)}, bf16[128,256]{1,0:T(8,128)(2,1)S(1)}, u32[]{:S(2)}, u32[]{:S(2)}) collective-permute-start(bf16[128,256]{1,0:T(8,128)(2,1)S(1)} %get-tuple-element.65), channel_id=1, source_target_pairs={{0,4},{4,8},{8,12},{12,16},{16,20},{20,24},{24,28},{1,5},{5,9},{9,... | collective-permute-start | bytes 196616 | tf_op jit(solution)/shard_map/ppermute | solution.py:138
  79.7 6.2 %collective-permute-start.5 = (bf16[128,256]{1,0:T(8,128)(2,1)S(1)}, bf16[128,256]{1,0:T(8,128)(2,1)S(1)}, u32[]{:S(2)}, u32[]{:S(2)}) collective-permute-start(bf16[128,256]{1,0:T(8,128)(2,1)S(1)} %get-tuple-element.66), channel_id=1, source_target_pairs={{4,0},{8,4},{12,8},{16,12},{20,16},{24,20},{28,24},{5,1},{9,5},{13... | collective-permute-start | bytes 196616 | tf_op jit(solution)/shard_map/ppermute | solution.py:138
  81.0 4.9 %collective-permute-start.6 = (bf16[128,256]{1,0:T(8,128)(2,1)S(1)}, bf16[128,256]{1,0:T(8,128)(2,1)S(1)}, u32[]{:S(2)}, u32[]{:S(2)}) collective-permute-start(bf16[128,256]{1,0:T(8,128)(2,1)S(1)} %get-tuple-element.67), channel_id=1, source_target_pairs={{0,1},{1,2},{2,3},{4,5},{5,6},{6,7},{8,9},{9,10},{10,11},{12,13},{... | collective-permute-start | bytes 196616 | tf_op jit(solution)/shard_map/ppermute | solution.py:138
  83.3 3.1 %collective-permute-start.7 = (bf16[128,256]{1,0:T(8,128)(2,1)S(1)}, bf16[128,256]{1,0:T(8,128)(2,1)S(1)}, u32[]{:S(2)}, u32[]{:S(2)}) collective-permute-start(bf16[128,256]{1,0:T(8,128)(2,1)S(1)} %get-tuple-element.68), channel_id=1, source_target_pairs={{1,0},{2,1},{3,2},{5,4},{6,5},{7,6},{9,8},{10,9},{11,10},{13,12},{... | collective-permute-start | bytes 196616 | tf_op jit(solution)/shard_map/ppermute | solution.py:138
  87.8 14.3 %collective-permute-start.8 = (bf16[128,256]{1,0:T(8,128)(2,1)S(1)}, bf16[128,256]{1,0:T(8,128)(2,1)S(1)}, u32[]{:S(2)}, u32[]{:S(2)}) collective-permute-start(bf16[128,256]{1,0:T(8,128)(2,1)S(1)} %get-tuple-element.71), channel_id=1, source_target_pairs={{0,4},{4,8},{8,12},{12,16},{16,20},{20,24},{24,28},{1,5},{5,9},{9,... | collective-permute-start | bytes 196616 | tf_op jit(solution)/shard_map/ppermute | solution.py:138
  92.1 10.0 %collective-permute-start.9 = (bf16[128,256]{1,0:T(8,128)(2,1)S(1)}, bf16[128,256]{1,0:T(8,128)(2,1)S(1)}, u32[]{:S(2)}, u32[]{:S(2)}) collective-permute-start(bf16[128,256]{1,0:T(8,128)(2,1)S(1)} %get-tuple-element.72), channel_id=1, source_target_pairs={{4,0},{8,4},{12,8},{16,12},{20,16},{24,20},{28,24},{5,1},{9,5},{13... | collective-permute-start | bytes 196616 | tf_op jit(solution)/shard_map/ppermute | solution.py:138
  93.4 8.7 %collective-permute-start.10 = (bf16[128,256]{1,0:T(8,128)(2,1)S(1)}, bf16[128,256]{1,0:T(8,128)(2,1)S(1)}, u32[]{:S(2)}, u32[]{:S(2)}) collective-permute-start(bf16[128,256]{1,0:T(8,128)(2,1)S(1)} %get-tuple-element.73), channel_id=1, source_target_pairs={{0,1},{1,2},{2,3},{4,5},{5,6},{6,7},{8,9},{9,10},{10,11},{12,13},{... | collective-permute-start | bytes 196616 | tf_op jit(solution)/shard_map/ppermute | solution.py:138
  97.4 4.7 %collective-permute-start.11 = (bf16[128,256]{1,0:T(8,128)(2,1)S(1)}, bf16[128,256]{1,0:T(8,128)(2,1)S(1)}, u32[]{:S(2)}, u32[]{:S(2)}) collective-permute-start(bf16[128,256]{1,0:T(8,128)(2,1)S(1)} %get-tuple-element.74), channel_id=1, source_target_pairs={{1,0},{2,1},{3,2},{5,4},{6,5},{7,6},{9,8},{10,9},{11,10},{13,12},{... | collective-permute-start | bytes 196616 | tf_op jit(solution)/shard_map/ppermute | solution.py:138
  104.8 10.7 %collective-permute-start.12 = (bf16[128,256]{1,0:T(8,128)(2,1)S(1)}, bf16[128,256]{1,0:T(8,128)(2,1)S(1)}, u32[]{:S(2)}, u32[]{:S(2)}) collective-permute-start(bf16[128,256]{1,0:T(8,128)(2,1)S(1)} %get-tuple-element.75), channel_id=1, source_target_pairs={{0,4},{4,8},{8,12},{12,16},{16,20},{20,24},{24,28},{1,5},{5,9},{9,... | collective-permute-start | bytes 196616 | tf_op jit(solution)/shard_map/ppermute | solution.py:138
  109.0 6.7 %collective-permute-start.13 = (bf16[128,256]{1,0:T(8,128)(2,1)S(1)}, bf16[128,256]{1,0:T(8,128)(2,1)S(1)}, u32[]{:S(2)}, u32[]{:S(2)}) collective-permute-start(bf16[128,256]{1,0:T(8,128)(2,1)S(1)} %get-tuple-element.76), channel_id=1, source_target_pairs={{4,0},{8,4},{12,8},{16,12},{20,16},{24,20},{28,24},{5,1},{9,5},{13... | collective-permute-start | bytes 196616 | tf_op jit(solution)/shard_map/ppermute | solution.py:138
  110.3 5.4 %collective-permute-start.14 = (bf16[128,256]{1,0:T(8,128)(2,1)S(1)}, bf16[128,256]{1,0:T(8,128)(2,1)S(1)}, u32[]{:S(2)}, u32[]{:S(2)}) collective-permute-start(bf16[128,256]{1,0:T(8,128)(2,1)S(1)} %get-tuple-element.77), channel_id=1, source_target_pairs={{0,1},{1,2},{2,3},{4,5},{5,6},{6,7},{8,9},{9,10},{10,11},{12,13},{... | collective-permute-start | bytes 196616 | tf_op jit(solution)/shard_map/ppermute | solution.py:138
  113.4 17.7 %slice-start.4 = ((s8[4718592]{0:T(1024)(128)(4,1)}), s8[4194304]{0:T(1024)(128)(4,1)S(1)}, s32[]{:S(2)}) async-start(s8[4718592]{0:T(1024)(128)(4,1)} %bitcast.28), calls=%async_computation.5 | async-start | bytes 8388608
  113.4 4.8 %copy-start.6 = (f32[1,1,1024,256]{3,2,1,0:T(8,128)S(1)}, f32[1,1,1024,256]{3,2,1,0:T(8,128)}, u32[]{:S(2)}) copy-start(f32[1,1,1024,256]{3,2,1,0:T(8,128)} %param.7) | copy-start | bytes 3145732
  113.4 17.7 %slice-start.5 = ((s8[4718592]{0:T(1024)(128)(4,1)}), s8[524288]{0:T(1024)(128)(4,1)S(1)}, s32[]{:S(2)}) async-start(s8[4718592]{0:T(1024)(128)(4,1)} %bitcast.28), calls=%async_computation.6 | async-start | bytes 1048576
  113.4 4.8 %collective-permute-start.15 = (bf16[128,256]{1,0:T(8,128)(2,1)S(1)}, bf16[128,256]{1,0:T(8,128)(2,1)S(1)}, u32[]{:S(2)}, u32[]{:S(2)}) collective-permute-start(bf16[128,256]{1,0:T(8,128)(2,1)S(1)} %get-tuple-element.78), channel_id=1, source_target_pairs={{1,0},{2,1},{3,2},{5,4},{6,5},{7,6},{9,8},{10,9},{11,10},{13,12},{... | collective-permute-start | bytes 196616 | tf_op jit(solution)/shard_map/ppermute | solution.py:138
  119.5 12.6 %collective-permute-start.16 = (bf16[128,256]{1,0:T(8,128)(2,1)S(1)}, bf16[128,256]{1,0:T(8,128)(2,1)S(1)}, u32[]{:S(2)}, u32[]{:S(2)}) collective-permute-start(bf16[128,256]{1,0:T(8,128)(2,1)S(1)} %get-tuple-element.80), channel_id=1, source_target_pairs={{0,4},{4,8},{8,12},{12,16},{16,20},{20,24},{24,28},{1,5},{5,9},{9,... | collective-permute-start | bytes 196616 | tf_op jit(solution)/shard_map/ppermute | solution.py:138
  124.1 8.1 %collective-permute-start.17 = (bf16[128,256]{1,0:T(8,128)(2,1)S(1)}, bf16[128,256]{1,0:T(8,128)(2,1)S(1)}, u32[]{:S(2)}, u32[]{:S(2)}) collective-permute-start(bf16[128,256]{1,0:T(8,128)(2,1)S(1)} %get-tuple-element.81), channel_id=1, source_target_pairs={{4,0},{8,4},{12,8},{16,12},{20,16},{24,20},{28,24},{5,1},{9,5},{13... | collective-permute-start | bytes 196616 | tf_op jit(solution)/shard_map/ppermute | solution.py:138
  125.4 6.8 %collective-permute-start.18 = (bf16[128,256]{1,0:T(8,128)(2,1)S(1)}, bf16[128,256]{1,0:T(8,128)(2,1)S(1)}, u32[]{:S(2)}, u32[]{:S(2)}) collective-permute-start(bf16[128,256]{1,0:T(8,128)(2,1)S(1)} %get-tuple-element.82), channel_id=1, source_target_pairs={{0,1},{1,2},{2,3},{4,5},{5,6},{6,7},{8,9},{9,10},{10,11},{12,13},{... | collective-permute-start | bytes 196616 | tf_op jit(solution)/shard_map/ppermute | solution.py:138
  129.8 3.1 %collective-permute-start.19 = (bf16[128,256]{1,0:T(8,128)(2,1)S(1)}, bf16[128,256]{1,0:T(8,128)(2,1)S(1)}, u32[]{:S(2)}, u32[]{:S(2)}) collective-permute-start(bf16[128,256]{1,0:T(8,128)(2,1)S(1)} %get-tuple-element.83), channel_id=1, source_target_pairs={{1,0},{2,1},{3,2},{5,4},{6,5},{7,6},{9,8},{10,9},{11,10},{13,12},{... | collective-permute-start | bytes 196616 | tf_op jit(solution)/shard_map/ppermute | solution.py:138
  132.9 64.8 %slice-start = ((s8[4718592]{0:T(1024)(128)(4,1)}), s8[4194304]{0:T(1024)(128)(4,1)S(1)}, s32[]{:S(2)}) async-start(s8[4718592]{0:T(1024)(128)(4,1)} %bitcast.19), calls=%async_computation.1 | async-start | bytes 8388608
  176.2 21.6 %slice-start.1 = ((s8[4718592]{0:T(1024)(128)(4,1)}), s8[524288]{0:T(1024)(128)(4,1)S(1)}, s32[]{:S(2)}) async-start(s8[4718592]{0:T(1024)(128)(4,1)} %bitcast.19), calls=%async_computation.2 | async-start | bytes 1048576
  177.2 6.2 %collective-permute-start.20 = (bf16[128,256]{1,0:T(8,128)(2,1)S(1)}, bf16[128,256]{1,0:T(8,128)(2,1)S(1)}, u32[]{:S(2)}, u32[]{:S(2)}) collective-permute-start(bf16[128,256]{1,0:T(8,128)(2,1)S(1)} %get-tuple-element.85), channel_id=1, source_target_pairs={{0,4},{4,8},{8,12},{12,16},{16,20},{20,24},{24,28},{1,5},{5,9},{9,... | collective-permute-start | bytes 196616 | tf_op jit(solution)/shard_map/ppermute | solution.py:138
  178.5 6.2 %collective-permute-start.21 = (bf16[128,256]{1,0:T(8,128)(2,1)S(1)}, bf16[128,256]{1,0:T(8,128)(2,1)S(1)}, u32[]{:S(2)}, u32[]{:S(2)}) collective-permute-start(bf16[128,256]{1,0:T(8,128)(2,1)S(1)} %get-tuple-element.86), channel_id=1, source_target_pairs={{4,0},{8,4},{12,8},{16,12},{20,16},{24,20},{28,24},{5,1},{9,5},{13... | collective-permute-start | bytes 196616 | tf_op jit(solution)/shard_map/ppermute | solution.py:138
  179.8 4.9 %collective-permute-start.22 = (bf16[128,256]{1,0:T(8,128)(2,1)S(1)}, bf16[128,256]{1,0:T(8,128)(2,1)S(1)}, u32[]{:S(2)}, u32[]{:S(2)}) collective-permute-start(bf16[128,256]{1,0:T(8,128)(2,1)S(1)} %get-tuple-element.87), channel_id=1, source_target_pairs={{0,1},{1,2},{2,3},{4,5},{5,6},{6,7},{8,9},{9,10},{10,11},{12,13},{... | collective-permute-start | bytes 196616 | tf_op jit(solution)/shard_map/ppermute | solution.py:138
  182.1 3.1 %collective-permute-start.23 = (bf16[128,256]{1,0:T(8,128)(2,1)S(1)}, bf16[128,256]{1,0:T(8,128)(2,1)S(1)}, u32[]{:S(2)}, u32[]{:S(2)}) collective-permute-start(bf16[128,256]{1,0:T(8,128)(2,1)S(1)} %get-tuple-element.88), channel_id=1, source_target_pairs={{1,0},{2,1},{3,2},{5,4},{6,5},{7,6},{9,8},{10,9},{11,10},{13,12},{... | collective-permute-start | bytes 196616 | tf_op jit(solution)/shard_map/ppermute | solution.py:138
  186.6 12.2 %collective-permute-start.24 = (bf16[128,256]{1,0:T(8,128)(2,1)S(1)}, bf16[128,256]{1,0:T(8,128)(2,1)S(1)}, u32[]{:S(2)}, u32[]{:S(2)}) collective-permute-start(bf16[128,256]{1,0:T(8,128)(2,1)S(1)} %get-tuple-element.91), channel_id=1, source_target_pairs={{0,4},{4,8},{8,12},{12,16},{16,20},{20,24},{24,28},{1,5},{5,9},{9,... | collective-permute-start | bytes 196616 | tf_op jit(solution)/shard_map/ppermute | solution.py:138
  190.9 7.9 %collective-permute-start.25 = (bf16[128,256]{1,0:T(8,128)(2,1)S(1)}, bf16[128,256]{1,0:T(8,128)(2,1)S(1)}, u32[]{:S(2)}, u32[]{:S(2)}) collective-permute-start(bf16[128,256]{1,0:T(8,128)(2,1)S(1)} %get-tuple-element.92), channel_id=1, source_target_pairs={{4,0},{8,4},{12,8},{16,12},{20,16},{24,20},{28,24},{5,1},{9,5},{13... | collective-permute-start | bytes 196616 | tf_op jit(solution)/shard_map/ppermute | solution.py:138
  192.2 6.6 %collective-permute-start.26 = (bf16[128,256]{1,0:T(8,128)(2,1)S(1)}, bf16[128,256]{1,0:T(8,128)(2,1)S(1)}, u32[]{:S(2)}, u32[]{:S(2)}) collective-permute-start(bf16[128,256]{1,0:T(8,128)(2,1)S(1)} %get-tuple-element.93), channel_id=1, source_target_pairs={{0,1},{1,2},{2,3},{4,5},{5,6},{6,7},{8,9},{9,10},{10,11},{12,13},{... | collective-permute-start | bytes 196616 | tf_op jit(solution)/shard_map/ppermute | solution.py:138
  196.3 3.1 %collective-permute-start.27 = (bf16[128,256]{1,0:T(8,128)(2,1)S(1)}, bf16[128,256]{1,0:T(8,128)(2,1)S(1)}, u32[]{:S(2)}, u32[]{:S(2)}) collective-permute-start(bf16[128,256]{1,0:T(8,128)(2,1)S(1)} %get-tuple-element.94), channel_id=1, source_target_pairs={{1,0},{2,1},{3,2},{5,4},{6,5},{7,6},{9,8},{10,9},{11,10},{13,12},{... | collective-permute-start | bytes 196616 | tf_op jit(solution)/shard_map/ppermute | solution.py:138
  199.8 11.9 %collective-permute-start.28 = (bf16[128,256]{1,0:T(8,128)(2,1)S(1)}, bf16[128,256]{1,0:T(8,128)(2,1)S(1)}, u32[]{:S(2)}, u32[]{:S(2)}) collective-permute-start(bf16[128,256]{1,0:T(8,128)(2,1)S(1)} %get-tuple-element.95), channel_id=1, source_target_pairs={{0,4},{4,8},{8,12},{12,16},{16,20},{20,24},{24,28},{1,5},{5,9},{9,... | collective-permute-start | bytes 196616 | tf_op jit(solution)/shard_map/ppermute | solution.py:138
  204.1 7.6 %collective-permute-start.29 = (bf16[128,256]{1,0:T(8,128)(2,1)S(1)}, bf16[128,256]{1,0:T(8,128)(2,1)S(1)}, u32[]{:S(2)}, u32[]{:S(2)}) collective-permute-start(bf16[128,256]{1,0:T(8,128)(2,1)S(1)} %get-tuple-element.96), channel_id=1, source_target_pairs={{4,0},{8,4},{12,8},{16,12},{20,16},{24,20},{28,24},{5,1},{9,5},{13... | collective-permute-start | bytes 196616 | tf_op jit(solution)/shard_map/ppermute | solution.py:138
  205.4 6.3 %collective-permute-start.30 = (bf16[128,256]{1,0:T(8,128)(2,1)S(1)}, bf16[128,256]{1,0:T(8,128)(2,1)S(1)}, u32[]{:S(2)}, u32[]{:S(2)}) collective-permute-start(bf16[128,256]{1,0:T(8,128)(2,1)S(1)} %get-tuple-element.97), channel_id=1, source_target_pairs={{0,1},{1,2},{2,3},{4,5},{5,6},{6,7},{8,9},{9,10},{10,11},{12,13},{... | collective-permute-start | bytes 196616 | tf_op jit(solution)/shard_map/ppermute | solution.py:138
  209.9 3.1 %collective-permute-start.31 = (bf16[128,256]{1,0:T(8,128)(2,1)S(1)}, bf16[128,256]{1,0:T(8,128)(2,1)S(1)}, u32[]{:S(2)}, u32[]{:S(2)}) collective-permute-start(bf16[128,256]{1,0:T(8,128)(2,1)S(1)} %get-tuple-element.98), channel_id=1, source_target_pairs={{1,0},{2,1},{3,2},{5,4},{6,5},{7,6},{9,8},{10,9},{11,10},{13,12},{... | collective-permute-start | bytes 196616 | tf_op jit(solution)/shard_map/ppermute | solution.py:138
  214.3 12.5 %collective-permute-start.32 = (bf16[128,256]{1,0:T(8,128)(2,1)S(1)}, bf16[128,256]{1,0:T(8,128)(2,1)S(1)}, u32[]{:S(2)}, u32[]{:S(2)}) collective-permute-start(bf16[128,256]{1,0:T(8,128)(2,1)S(1)} %get-tuple-element.100), channel_id=1, source_target_pairs={{0,4},{4,8},{8,12},{12,16},{16,20},{20,24},{24,28},{1,5},{5,9},{9,... | collective-permute-start | bytes 196616 | tf_op jit(solution)/shard_map/ppermute | solution.py:138
  218.6 8.2 %collective-permute-start.33 = (bf16[128,256]{1,0:T(8,128)(2,1)S(1)}, bf16[128,256]{1,0:T(8,128)(2,1)S(1)}, u32[]{:S(2)}, u32[]{:S(2)}) collective-permute-start(bf16[128,256]{1,0:T(8,128)(2,1)S(1)} %get-tuple-element.101), channel_id=1, source_target_pairs={{4,0},{8,4},{12,8},{16,12},{20,16},{24,20},{28,24},{5,1},{9,5},{13... | collective-permute-start | bytes 196616 | tf_op jit(solution)/shard_map/ppermute | solution.py:138
  219.9 6.9 %collective-permute-start.34 = (bf16[128,256]{1,0:T(8,128)(2,1)S(1)}, bf16[128,256]{1,0:T(8,128)(2,1)S(1)}, u32[]{:S(2)}, u32[]{:S(2)}) collective-permute-start(bf16[128,256]{1,0:T(8,128)(2,1)S(1)} %get-tuple-element.102), channel_id=1, source_target_pairs={{0,1},{1,2},{2,3},{4,5},{5,6},{6,7},{8,9},{9,10},{10,11},{12,13},{... | collective-permute-start | bytes 196616 | tf_op jit(solution)/shard_map/ppermute | solution.py:138
  224.5 3.1 %collective-permute-start.35 = (bf16[128,256]{1,0:T(8,128)(2,1)S(1)}, bf16[128,256]{1,0:T(8,128)(2,1)S(1)}, u32[]{:S(2)}, u32[]{:S(2)}) collective-permute-start(bf16[128,256]{1,0:T(8,128)(2,1)S(1)} %get-tuple-element.103), channel_id=1, source_target_pairs={{1,0},{2,1},{3,2},{5,4},{6,5},{7,6},{9,8},{10,9},{11,10},{13,12},{... | collective-permute-start | bytes 196616 | tf_op jit(solution)/shard_map/ppermute | solution.py:138
  271.8 6.2 %collective-permute-start.36 = (bf16[128,256]{1,0:T(8,128)(2,1)S(1)}, bf16[128,256]{1,0:T(8,128)(2,1)S(1)}, u32[]{:S(2)}, u32[]{:S(2)}) collective-permute-start(bf16[128,256]{1,0:T(8,128)(2,1)S(1)} %get-tuple-element.105), channel_id=1, source_target_pairs={{0,4},{4,8},{8,12},{12,16},{16,20},{20,24},{24,28},{1,5},{5,9},{9,... | collective-permute-start | bytes 196616 | tf_op jit(solution)/shard_map/ppermute | solution.py:138
  273.1 6.2 %collective-permute-start.37 = (bf16[128,256]{1,0:T(8,128)(2,1)S(1)}, bf16[128,256]{1,0:T(8,128)(2,1)S(1)}, u32[]{:S(2)}, u32[]{:S(2)}) collective-permute-start(bf16[128,256]{1,0:T(8,128)(2,1)S(1)} %get-tuple-element.106), channel_id=1, source_target_pairs={{4,0},{8,4},{12,8},{16,12},{20,16},{24,20},{28,24},{5,1},{9,5},{13... | collective-permute-start | bytes 196616 | tf_op jit(solution)/shard_map/ppermute | solution.py:138
  274.4 4.9 %collective-permute-start.38 = (bf16[128,256]{1,0:T(8,128)(2,1)S(1)}, bf16[128,256]{1,0:T(8,128)(2,1)S(1)}, u32[]{:S(2)}, u32[]{:S(2)}) collective-permute-start(bf16[128,256]{1,0:T(8,128)(2,1)S(1)} %get-tuple-element.107), channel_id=1, source_target_pairs={{0,1},{1,2},{2,3},{4,5},{5,6},{6,7},{8,9},{9,10},{10,11},{12,13},{... | collective-permute-start | bytes 196616 | tf_op jit(solution)/shard_map/ppermute | solution.py:138
  276.7 3.1 %collective-permute-start.39 = (bf16[128,256]{1,0:T(8,128)(2,1)S(1)}, bf16[128,256]{1,0:T(8,128)(2,1)S(1)}, u32[]{:S(2)}, u32[]{:S(2)}) collective-permute-start(bf16[128,256]{1,0:T(8,128)(2,1)S(1)} %get-tuple-element.108), channel_id=1, source_target_pairs={{1,0},{2,1},{3,2},{5,4},{6,5},{7,6},{9,8},{10,9},{11,10},{13,12},{... | collective-permute-start | bytes 196616 | tf_op jit(solution)/shard_map/ppermute | solution.py:138
  (7 other events, 11.5 us)

commit v2 on v1

--- a/solution.py
+++ b/solution.py
@@ -19,29 +19,39 @@
     return lax.dot_general(left, right, (((0,), (0,)), ((), ())), preferred_element_type=FULL)
 
 
-def call(body, name, outs, *args, flops=0):
+def call(body, name, outs, *args, far=0, away=False, scratch=(), flops=0):
     here = pl.BlockSpec(memory_space=pltpu.VMEM)
+    there = pl.BlockSpec(memory_space=pltpu.HBM)
     size = sum(a.size * a.dtype.itemsize for a in args)
+    distant = [pltpu.with_memory_space_constraint(a, pltpu.HBM) for a in args[:far]]
+    near = [pltpu.with_memory_space_constraint(a, pltpu.VMEM) for a in args[far:]]
     return pl.pallas_call(
         body,
-        out_shape=tuple(pltpu.VMEM(shape, dtype) for shape, dtype in outs),
-        in_specs=[here] * len(args),
-        out_specs=tuple(here for _ in outs),
+        out_shape=tuple((pltpu.HBM if away else pltpu.VMEM)(*out) for out in outs),
+        in_specs=[there] * far + [here] * len(near),
+        out_specs=tuple(there if away else here for _ in outs),
+        scratch_shapes=list(scratch),
         compiler_params=pltpu.CompilerParams(vmem_limit_bytes=24 * 1024 * 1024),
         cost_estimate=pl.CostEstimate(flops=flops, bytes_accessed=size, transcendentals=0),
         name=name,
-    )(*(pltpu.with_memory_space_constraint(a, pltpu.VMEM) for a in args))
-
-
-def select_kernel(target, rows, counts, half, pick, spread, *tiles):
+    )(*distant, *near)
+
+
+def select_kernel(far_target, far_rows, far_counts, target, half, pick, spread, *rest):
+    *tiles, rows, counts, sems = rest
     own = target.shape[0]
     tile = rows.shape[1]
-    half[...] = target[...].astype(HALF)
+    loads = [
+        pltpu.make_async_copy(far, near, sems.at[i])
+        for i, (far, near) in enumerate(((far_rows, rows), (far_counts, counts), (far_target, target)))
+    ]
+    for load in loads:
+        load.start()
+    loads[0].wait()
+    loads[1].wait()
     for d in range(4):
         here = jnp.where(
-            lax.broadcasted_iota(jnp.int32, (1, tile), 1) < counts[d : d + 1, :],
-            rows[d : d + 1, :],
-            -1,
+            lax.broadcasted_iota(jnp.int32, (1, tile), 1) < counts[0, d], rows[d : d + 1, :], -1
         )
         wide = jnp.broadcast_to(here, (own, tile))
         spread[:, d * tile : (d + 1) * tile] = (
@@ -51,8 +61,25 @@
         pick[d * tile : (d + 1) * tile, :] = (
             lax.broadcasted_iota(jnp.int32, (tile, own), 1) == down
         ).astype(FULL).astype(HALF)
+    loads[2].wait()
+    half[...] = target[...].astype(HALF)
     for d in range(4):
         tiles[d][...] = product(pick[d * tile : (d + 1) * tile, :], half[...]).astype(HALF)
+
+
+def resident_kernel(far, owned, matrix, out, sems):
+    own = owned.shape[0]
+    pieces = sems.shape[0]
+    height = far.shape[0] // pieces
+    spans = [slice(i * height, (i + 1) * height) for i in range(pieces)]
+    loads = [
+        pltpu.make_async_copy(far.at[at], matrix.at[at], sems.at[i]) for i, at in enumerate(spans)
+    ]
+    for load in loads:
+        load.start()
+    for load, at in zip(loads, spans):
+        load.wait()
+        out[at, :] = product(matrix[at, :own], owned[...])
 
 
 def own_columns_kernel(matrix, owned, out):
@@ -62,9 +89,9 @@
 
 def restrict_kernel(basis, owned, g0, g1, g2, g3, out):
     own, tile = owned.shape[0], g0.shape[0]
-    total = turned_product(basis[:own, :], owned[...])
+    total = product(basis[:, :own], owned[...])
     for d, ghost in enumerate((g0, g1, g2, g3)):
-        total += turned_product(basis[own + d * tile : own + (d + 1) * tile, :], ghost[...])
+        total += product(basis[:, own + d * tile : own + (d + 1) * tile], ghost[...])
     out[...] = total.astype(HALF)
 
 
@@ -77,13 +104,21 @@
     out[...] = partial[...] + product(matrix[:, own:], stacked(g0, g1, g2, g3))
 
 
-def coarse_kernel(coarse_rows, gathered, basis, local, level, *tiles):
+def partial_kernel(inverse, gathered, out):
+    for i in range(inverse.shape[0]):
+        out[i, :, :] = product(inverse[i, :, :], gathered[...]).astype(HALF)
+
+
+def coarse_kernel(parts, basis, local, level, *tiles):
     tile = tiles[0].shape[0]
     own = local.shape[0] - 4 * tile
-    level[...] = product(coarse_rows[...], gathered[...]).astype(HALF)
+    total = parts[0, :, :].astype(FULL)
+    for i in range(1, parts.shape[0]):
+        total += parts[i, :, :].astype(FULL)
+    level[...] = total.astype(HALF)
     for d in range(4):
         at = slice(own + d * tile, own + (d + 1) * tile)
-        tiles[d][...] = (local[at, :] + product(basis[at, :], level[...])).astype(HALF)
+        tiles[d][...] = (local[at, :] + turned_product(basis[:, at], level[...])).astype(HALF)
 
 
 def rim_kernel(matrix, partial, g0, g1, g2, g3, *tiles):
@@ -100,27 +135,43 @@
     out[...] = partial[:own, :] + product(matrix[:own, own:], stacked(g0, g1, g2, g3))
 
 
-def update_kernel(first, last):
+def update_kernel(first):
     def body(*refs):
         refs = list(refs)
         before = None if first else refs.pop(0)
-        local, level, basis, pick, spread, r0, r1, r2, r3, after, *rest = refs
+        local, level, basis, pick, spread, r0, r1, r2, r3, after, half, *tiles = refs
         own = after.shape[0]
         update = (
             local[:own, :]
-            + product(basis[:own, :], level[...])
+            + turned_product(basis[:, :own], level[...])
             + product(spread[...], stacked(r0, r1, r2, r3))
         )
         after[...] = DAMPING * update if first else before[...] + DAMPING * update
-        if last:
-            return
-        half, *tiles = rest
         tile = tiles[0].shape[0]
         half[...] = after[...].astype(HALF)
         for d in range(4):
             tiles[d][...] = product(pick[d * tile : (d + 1) * tile, :], half[...]).astype(HALF)
 
     return body
+
+
+def last_update_kernel(before, local, level, basis, spread, r0, r1, r2, r3, far, after, sems):
+    pieces = sems.shape[0]
+    height = after.shape[0] // pieces
+    returned = stacked(r0, r1, r2, r3)
+    stores = []
+    for i in range(pieces):
+        at = slice(i * height, (i + 1) * height)
+        update = (
+            local[at, :]
+            + turned_product(basis[:, at], level[...])
+            + product(spread[at, :], returned)
+        )
+        after[at, :] = before[at, :] + DAMPING * update
+        stores.append(pltpu.make_async_copy(after.at[at], far.at[at], sems.at[i]))
+        stores[-1].start()
+    for store in stores:
+        store.wait()
 
 
 def residual_kernel(target, image, pick, spread, r0, r1, r2, r3, half, *tiles):
@@ -130,6 +181,24 @@
     ).astype(HALF)
     for d in range(4):
         tiles[d][...] = product(pick[d * tile : (d + 1) * tile, :], half[...]).astype(HALF)
+
+
+def own_product(matrix, owned, arriving, name):
+    local = matrix.shape[0]
+    out = ((local, owned.shape[1]), FULL)
+    flops = 2 * local * owned.size
+    if arriving:
+        return call(
+            resident_kernel,
+            name,
+            [(matrix.shape, HALF), out],
+            matrix,
+            owned,
+            far=1,
+            scratch=(pltpu.SemaphoreType.DMA((6,)),),
+            flops=flops,
+        )
+    return matrix, call(own_columns_kernel, name, [out], matrix, owned, flops=flops)[0]
 
 
 def passed_along(shard, axis, by):
@@ -153,39 +222,37 @@
     target = right_side[0, 0]
     operator = local_operator[0, 0]
     inverse = local_inverse[0, 0]
-    basis = coarse_basis[0, 0]
+    basis = jnp.swapaxes(coarse_basis[0, 0], 0, 1)
     rows_list = send_rows[0, 0]
     own, columns = target.shape
     local = operator.shape[0]
     tile = rows_list.shape[1]
     margin = 4 * tile
-    coarse = basis.shape[1]
-    counts = jnp.broadcast_to(send_count[0, 0][:, None], rows_list.shape)
-    coarse_rows = lax.all_to_all(coarse_inverse, "row", 0, 2, tiled=True)[0]
-
+    coarse = basis.shape[0]
+    groups = coarse_inverse.shape[0]
     four_tiles = [((tile, columns), HALF)] * 4
     owned_half = ((own, columns), HALF)
-    residual, pick, spread, *tiles = call(
+    target, residual, pick, spread, *tiles = call(
         select_kernel,
         "select",
-        [owned_half, ((margin, own), HALF), ((own, margin), HALF)] + four_tiles,
+        [((own, columns), FULL), owned_half, ((margin, own), HALF), ((own, margin), HALF)]
+        + four_tiles,
         target,
         rows_list,
-        counts,
+        send_count[0],
+        far=3,
+        scratch=(
+            pltpu.VMEM(rows_list.shape, jnp.int32),
+            pltpu.SMEM((1, 4), jnp.int32),
+            pltpu.SemaphoreType.DMA((3,)),
+        ),
         flops=2 * margin * own * columns,
     )
     solution = None
     for sweep in range(ITERS):
         if sweep:
             ghosts = traded(tiles)
-            (partial,) = call(
-                own_columns_kernel,
-                "operator_own",
-                [((local, columns), FULL)],
-                operator,
-                solution_half,
-                flops=2 * local * own * columns,
-            )
+            operator, partial = own_product(operator, solution_half, sweep == 1, "operator_own")
             tiles = call(
                 rim_kernel,
                 "operator_rim",
@@ -217,14 +284,7 @@
                 flops=4 * margin * own * columns,
             )
         ghosts = traded(tiles)
-        (partial,) = call(
-            own_columns_kernel,
-            "inverse_own",
-            [((local, columns), FULL)],
-            inverse,
-            residual,
-            flops=2 * local * own * columns,
-        )
+        inverse, partial = own_product(inverse, residual, sweep == 0, "inverse_own")
         (restricted,) = call(
             restrict_kernel,
             "restrict",
@@ -234,7 +294,16 @@
             *ghosts,
             flops=2 * local * coarse * columns,
         )
-        gathered = lax.all_gather(restricted, ("row", "col"), axis=0, tiled=True)
+        gathered = lax.all_gather(restricted, "col", axis=0, tiled=True)
+        (parts,) = call(
+            partial_kernel,
+            "coarse_part",
+            [((groups, coarse, columns), HALF)],
+            coarse_inverse,
+            gathered,
+            flops=2 * coarse_inverse.size * columns,
+        )
+        parts = lax.all_to_all(parts, "row", 0, 0, tiled=True)
         (correction,) = call(
             margin_columns_kernel,
             "inverse_margin",
@@ -248,20 +317,19 @@
             coarse_kernel,
             "coarse",
             [((coarse, columns), HALF)] + four_tiles,
-            coarse_rows,
-            gathered,
+            parts,
             basis,
             correction,
-            flops=2 * coarse * (coarse_rows.shape[1] + margin) * columns,
+            flops=2 * coarse * margin * columns,
         )
         returned = traded(tiles)
-        first, last = sweep == 0, sweep == ITERS - 1
-        before = [] if first else [solution]
-        outs = [((own, columns), FULL)] + ([] if last else [owned_half] + four_tiles)
-        solution, *rest = call(
-            update_kernel(first, last),
+        if sweep == ITERS - 1:
+            break
+        before = [solution] if sweep else []
+        solution, solution_half, *tiles = call(
+            update_kernel(not sweep),
             "update",
-            outs,
+            [((own, columns), FULL), owned_half] + four_tiles,
             *before,
             correction,
             level,
@@ -271,8 +339,20 @@
             *returned,
             flops=4 * margin * own * columns,
         )
-        if not last:
-            solution_half, *tiles = rest
+    (solution,) = call(
+        last_update_kernel,
+        "last_update",
+        [((own, columns), FULL)],
+        solution,
+        correction,
+        level,
+        basis,
+        spread,
+        *returned,
+        away=True,
+        scratch=(pltpu.VMEM((own, columns), FULL), pltpu.SemaphoreType.DMA((4,))),
+        flops=2 * margin * own * columns,
+    )
     return solution[None, None]
 
 

time: 285 us -> 219 us (0.77)
  the two profiles are of different devices: /device:TPU:0 before, /device:TPU:9 now
where the time goes in v2:
time: 219 us; the launch traced here: 217 us
  starting transfers between devices  132 us (60%)
  waiting for transfers between devices  29 us (13%)
  Pallas kernels  26.1 us (12%)
  local copies, waits for them, and re-layouts  17.2 us (8%)
  blocking collectives  12.3 us (6%)
    ppermute x40, starting transfers between devices, passed_along(): return lax.ppermute(shard, axis, pairs)  118 us
    ppermute x40, waiting for transfers between devices, passed_along(): return lax.ppermute(shard, axis, pairs)  28.3 us
    pallas_call x27, Pallas kernels, call(): pl.pallas_call(body, out_shape=tuple(((pltpu.HBM if away else pltpu.VMEM)...  26.1 us
    unnamed x38, local copies, waits for them, and re-layouts  17.2 us
    all_to_all x3, starting transfers between devices, per_device(): parts = lax.all_to_all(parts, 'row', 0, 0, tiled=True)  13.5 us
    all_gather x3, blocking collectives, per_device(): gathered = lax.all_gather(restricted, 'col', axis=0, tiled=True)  12.3 us
  transfers between devices with their start and end apart: 43, of which 10 were waited for; matrix products, arithmetic and copies ran while one was open for 0% of the time, Pallas kernels for 6%

profile of v2, /device:TPU:9, one launch (start us, length us, event | category | flops | bytes accessed | tf_op | source)
XLA Modules:
  0.0 217.3 jit_solution(2107331537746840514)
XLA Ops:
  3.0 3.1 %collective-permute-start = (bf16[128,256]{1,0:T(8,128)(2,1)S(1)}, bf16[128,256]{1,0:T(8,128)(2,1)S(1)}, u32[]{:S(2)}, u32[]{:S(2)}) collective-permute-start(bf16[128,256]{1,0:T(8,128)(2,1)S(1)} %get-tuple-element.65), channel_id=1, source_target_pairs={{0,4},{4,8},{8,12},{12,16},{16,20},{20,24},{24,28},{1,5},{5,9},{9,... | collective-permute-start | bytes 196616 | tf_op jit(solution)/shard_map/ppermute | solution.py:207
  6.1 3.0 %collective-permute-start.1 = (bf16[128,256]{1,0:T(8,128)(2,1)S(1)}, bf16[128,256]{1,0:T(8,128)(2,1)S(1)}, u32[]{:S(2)}, u32[]{:S(2)}) collective-permute-start(bf16[128,256]{1,0:T(8,128)(2,1)S(1)} %get-tuple-element.66), channel_id=1, source_target_pairs={{4,0},{8,4},{12,8},{16,12},{20,16},{24,20},{28,24},{5,1},{9,5},{13... | collective-permute-start | bytes 196616 | tf_op jit(solution)/shard_map/ppermute | solution.py:207
  9.2 4.2 %collective-permute-start.2 = (bf16[128,256]{1,0:T(8,128)(2,1)S(1)}, bf16[128,256]{1,0:T(8,128)(2,1)S(1)}, u32[]{:S(2)}, u32[]{:S(2)}) collective-permute-start(bf16[128,256]{1,0:T(8,128)(2,1)S(1)} %get-tuple-element.67), channel_id=1, source_target_pairs={{0,1},{1,2},{2,3},{4,5},{5,6},{6,7},{8,9},{9,10},{10,11},{12,13},{... | collective-permute-start | bytes 196616 | tf_op jit(solution)/shard_map/ppermute | solution.py:207
  15.4 3.6 %collective-permute-done.3.g3 = bf16[128,256]{1,0:T(8,128)(2,1)S(1)} collective-permute-done((bf16[128,256]{1,0:T(8,128)(2,1)S(1)}, bf16[128,256]{1,0:T(8,128)(2,1)S(1)}, u32[]{:S(2)}, u32[]{:S(2)}) %collective-permute-start.3) | collective-permute-done | bytes 65568 | tf_op jit(solution)/shard_map/ppermute | solution.py:207
  20.1 4.1 %all_gather.9.gathered = bf16[128,256]{1,0:T(8,128)(2,1)S(1)} all-gather(bf16[32,256]{1,0:T(8,128)(2,1)S(1)} %restrict.3), channel_id=1, replica_groups=mesh['row'=8,'col'=4] {'col'}, dimensions={0}, use_global_device_ids=true | all-gather | bytes 81920 | tf_op jit(solution)/shard_map/all_gather | solution.py:297
  25.1 4.8 %all-to-all-start = ((bf16[8,32,256]{2,1,0:T(8,128)(2,1)}), bf16[8,32,256]{2,1,0:T(8,128)(2,1)S(1)}, u32[]{:S(2)}, u32[]{:S(2)}) async-start(bf16[8,32,256]{2,1,0:T(8,128)(2,1)} %coarse_part.3), calls=%async_computation | async-start | bytes 262144 | tf_op jit(solution)/shard_map/all_to_all | solution.py:306
  29.9 3.7 %inverse_own.3 = (bf16[1536,1536]{1,0:T(8,128)(2,1)S(1)}, f32[1536,256]{1,0:T(8,128)S(1)}) custom-call(bf16[1536,1536]{1,0:T(8,128)(2,1)} %bitcast.18, bf16[1024,256]{1,0:T(8,128)(2,1)S(1)} %get-tuple-element.62.owned), custom_call_target="tpu_custom_call" | custom-call | flops 805306368 | bytes 5242880 | tf_op jit(solution)/shard_map/inverse_own/pallas_call | solution.py:28
  34.2 2.1 copy-done
  39.2 3.1 %collective-permute-start.4 = (bf16[128,256]{1,0:T(8,128)(2,1)S(1)}, bf16[128,256]{1,0:T(8,128)(2,1)S(1)}, u32[]{:S(2)}, u32[]{:S(2)}) collective-permute-start(bf16[128,256]{1,0:T(8,128)(2,1)S(1)} %get-tuple-element.72), channel_id=1, source_target_pairs={{0,4},{4,8},{8,12},{12,16},{16,20},{20,24},{24,28},{1,5},{5,9},{9,... | collective-permute-start | bytes 196616 | tf_op jit(solution)/shard_map/ppermute | solution.py:207
  42.3 3.1 %collective-permute-start.5 = (bf16[128,256]{1,0:T(8,128)(2,1)S(1)}, bf16[128,256]{1,0:T(8,128)(2,1)S(1)}, u32[]{:S(2)}, u32[]{:S(2)}) collective-permute-start(bf16[128,256]{1,0:T(8,128)(2,1)S(1)} %get-tuple-element.73), channel_id=1, source_target_pairs={{4,0},{8,4},{12,8},{16,12},{20,16},{24,20},{28,24},{5,1},{9,5},{13... | collective-permute-start | bytes 196616 | tf_op jit(solution)/shard_map/ppermute | solution.py:207
  45.4 4.3 %collective-permute-start.6 = (bf16[128,256]{1,0:T(8,128)(2,1)S(1)}, bf16[128,256]{1,0:T(8,128)(2,1)S(1)}, u32[]{:S(2)}, u32[]{:S(2)}) collective-permute-start(bf16[128,256]{1,0:T(8,128)(2,1)S(1)} %get-tuple-element.74), channel_id=1, source_target_pairs={{0,1},{1,2},{2,3},{4,5},{5,6},{6,7},{8,9},{9,10},{10,11},{12,13},{... | collective-permute-start | bytes 196616 | tf_op jit(solution)/shard_map/ppermute | solution.py:207
  51.6 3.6 %collective-permute-done.7.refs_8_ = bf16[128,256]{1,0:T(8,128)(2,1)S(1)} collective-permute-done((bf16[128,256]{1,0:T(8,128)(2,1)S(1)}, bf16[128,256]{1,0:T(8,128)(2,1)S(1)}, u32[]{:S(2)}, u32[]{:S(2)}) %collective-permute-start.7) | collective-permute-done | bytes 65568 | tf_op jit(solution)/shard_map/ppermute | solution.py:207
  56.7 2.2 %collective-permute-start.8 = (bf16[128,256]{1,0:T(8,128)(2,1)S(1)}, bf16[128,256]{1,0:T(8,128)(2,1)S(1)}, u32[]{:S(2)}, u32[]{:S(2)}) collective-permute-start(bf16[128,256]{1,0:T(8,128)(2,1)S(1)} %get-tuple-element.81), channel_id=1, source_target_pairs={{0,4},{4,8},{8,12},{12,16},{16,20},{20,24},{24,28},{1,5},{5,9},{9,... | collective-permute-start | bytes 196616 | tf_op jit(solution)/shard_map/ppermute | solution.py:207
  58.9 4.0 %collective-permute-start.9 = (bf16[128,256]{1,0:T(8,128)(2,1)S(1)}, bf16[128,256]{1,0:T(8,128)(2,1)S(1)}, u32[]{:S(2)}, u32[]{:S(2)}) collective-permute-start(bf16[128,256]{1,0:T(8,128)(2,1)S(1)} %get-tuple-element.82), channel_id=1, source_target_pairs={{4,0},{8,4},{12,8},{16,12},{20,16},{24,20},{28,24},{5,1},{9,5},{13... | collective-permute-start | bytes 196616 | tf_op jit(solution)/shard_map/ppermute | solution.py:207
  62.9 2.4 %collective-permute-start.10 = (bf16[128,256]{1,0:T(8,128)(2,1)S(1)}, bf16[128,256]{1,0:T(8,128)(2,1)S(1)}, u32[]{:S(2)}, u32[]{:S(2)}) collective-permute-start(bf16[128,256]{1,0:T(8,128)(2,1)S(1)} %get-tuple-element.83), channel_id=1, source_target_pairs={{0,1},{1,2},{2,3},{4,5},{5,6},{6,7},{8,9},{9,10},{10,11},{12,13},{... | collective-permute-start | bytes 196616 | tf_op jit(solution)/shard_map/ppermute | solution.py:207
  67.2 3.7 %operator_own.2 = (bf16[1536,1536]{1,0:T(8,128)(2,1)S(1)}, f32[1536,256]{1,0:T(8,128)S(1)}) custom-call(bf16[1536,1536]{1,0:T(8,128)(2,1)} %bitcast.19, bf16[1024,256]{1,0:T(8,128)(2,1)S(1)} %get-tuple-element.78.owned), custom_call_target="tpu_custom_call" | custom-call | flops 805306368 | bytes 5242880 | tf_op jit(solution)/shard_map/operator_own/pallas_call | solution.py:28
  73.2 4.3 %collective-permute-start.13 = (bf16[128,256]{1,0:T(8,128)(2,1)S(1)}, bf16[128,256]{1,0:T(8,128)(2,1)S(1)}, u32[]{:S(2)}, u32[]{:S(2)}) collective-permute-start(bf16[128,256]{1,0:T(8,128)(2,1)S(1)} %get-tuple-element.86), channel_id=1, source_target_pairs={{4,0},{8,4},{12,8},{16,12},{20,16},{24,20},{28,24},{5,1},{9,5},{13... | collective-permute-start | bytes 196616 | tf_op jit(solution)/shard_map/ppermute | solution.py:207
  77.5 4.2 %collective-permute-start.14 = (bf16[128,256]{1,0:T(8,128)(2,1)S(1)}, bf16[128,256]{1,0:T(8,128)(2,1)S(1)}, u32[]{:S(2)}, u32[]{:S(2)}) collective-permute-start(bf16[128,256]{1,0:T(8,128)(2,1)S(1)} %get-tuple-element.87), channel_id=1, source_target_pairs={{0,1},{1,2},{2,3},{4,5},{5,6},{6,7},{8,9},{9,10},{10,11},{12,13},{... | collective-permute-start | bytes 196616 | tf_op jit(solution)/shard_map/ppermute | solution.py:207
  81.7 2.1 collective-permute-start.15
  84.3 3.2 %collective-permute-done.15.r3 = bf16[128,256]{1,0:T(8,128)(2,1)S(1)} collective-permute-done((bf16[128,256]{1,0:T(8,128)(2,1)S(1)}, bf16[128,256]{1,0:T(8,128)(2,1)S(1)}, u32[]{:S(2)}, u32[]{:S(2)}) %collective-permute-start.15) | collective-permute-done | bytes 65568 | tf_op jit(solution)/shard_map/ppermute | solution.py:207
  90.6 4.3 %collective-permute-start.17 = (bf16[128,256]{1,0:T(8,128)(2,1)S(1)}, bf16[128,256]{1,0:T(8,128)(2,1)S(1)}, u32[]{:S(2)}, u32[]{:S(2)}) collective-permute-start(bf16[128,256]{1,0:T(8,128)(2,1)S(1)} %get-tuple-element.91), channel_id=1, source_target_pairs={{4,0},{8,4},{12,8},{16,12},{20,16},{24,20},{28,24},{5,1},{9,5},{13... | collective-permute-start | bytes 196616 | tf_op jit(solution)/shard_map/ppermute | solution.py:207
  94.9 2.4 %collective-permute-start.18 = (bf16[128,256]{1,0:T(8,128)(2,1)S(1)}, bf16[128,256]{1,0:T(8,128)(2,1)S(1)}, u32[]{:S(2)}, u32[]{:S(2)}) collective-permute-start(bf16[128,256]{1,0:T(8,128)(2,1)S(1)} %get-tuple-element.92), channel_id=1, source_target_pairs={{0,1},{1,2},{2,3},{4,5},{5,6},{6,7},{8,9},{9,10},{10,11},{12,13},{... | collective-permute-start | bytes 196616 | tf_op jit(solution)/shard_map/ppermute | solution.py:207
  99.3 3.6 %collective-permute-done.19.g3 = bf16[128,256]{1,0:T(8,128)(2,1)S(1)} collective-permute-done((bf16[128,256]{1,0:T(8,128)(2,1)S(1)}, bf16[128,256]{1,0:T(8,128)(2,1)S(1)}, u32[]{:S(2)}, u32[]{:S(2)}) %collective-permute-start.19) | collective-permute-done | bytes 65568 | tf_op jit(solution)/shard_map/ppermute | solution.py:207
  103.2 4.1 %all_gather.10.gathered = bf16[128,256]{1,0:T(8,128)(2,1)S(1)} all-gather(bf16[32,256]{1,0:T(8,128)(2,1)S(1)} %restrict.4), channel_id=1, replica_groups=mesh['row'=8,'col'=4] {'col'}, dimensions={0}, use_global_device_ids=true | all-gather | bytes 81920 | tf_op jit(solution)/shard_map/all_gather | solution.py:297
  108.1 4.5 %all-to-all-start.1 = ((bf16[8,32,256]{2,1,0:T(8,128)(2,1)}), bf16[8,32,256]{2,1,0:T(8,128)(2,1)S(1)}, u32[]{:S(2)}, u32[]{:S(2)}) async-start(bf16[8,32,256]{2,1,0:T(8,128)(2,1)} %coarse_part.4), calls=%async_computation.1 | async-start | bytes 262144 | tf_op jit(solution)/shard_map/all_to_all | solution.py:306
  112.7 2.3 %copy-done.1 = bf16[1536,1536]{1,0:T(8,128)(2,1)S(1)} copy-done((bf16[1536,1536]{1,0:T(8,128)(2,1)S(1)}, bf16[1536,1536]{1,0:T(8,128)(2,1)}, u32[]{:S(2)}) %copy-start.1) | copy-done | bytes 4718616
  119.4 3.2 %collective-permute-start.20 = (bf16[128,256]{1,0:T(8,128)(2,1)S(1)}, bf16[128,256]{1,0:T(8,128)(2,1)S(1)}, u32[]{:S(2)}, u32[]{:S(2)}) collective-permute-start(bf16[128,256]{1,0:T(8,128)(2,1)S(1)} %get-tuple-element.95), channel_id=1, source_target_pairs={{0,4},{4,8},{8,12},{12,16},{16,20},{20,24},{24,28},{1,5},{5,9},{9,... | collective-permute-start | bytes 196616 | tf_op jit(solution)/shard_map/ppermute | solution.py:207
  122.6 3.1 %collective-permute-start.21 = (bf16[128,256]{1,0:T(8,128)(2,1)S(1)}, bf16[128,256]{1,0:T(8,128)(2,1)S(1)}, u32[]{:S(2)}, u32[]{:S(2)}) collective-permute-start(bf16[128,256]{1,0:T(8,128)(2,1)S(1)} %get-tuple-element.96), channel_id=1, source_target_pairs={{4,0},{8,4},{12,8},{16,12},{20,16},{24,20},{28,24},{5,1},{9,5},{13... | collective-permute-start | bytes 196616 | tf_op jit(solution)/shard_map/ppermute | solution.py:207
  125.7 4.7 %collective-permute-start.22 = (bf16[128,256]{1,0:T(8,128)(2,1)S(1)}, bf16[128,256]{1,0:T(8,128)(2,1)S(1)}, u32[]{:S(2)}, u32[]{:S(2)}) collective-permute-start(bf16[128,256]{1,0:T(8,128)(2,1)S(1)} %get-tuple-element.97), channel_id=1, source_target_pairs={{0,1},{1,2},{2,3},{4,5},{5,6},{6,7},{8,9},{9,10},{10,11},{12,13},{... | collective-permute-start | bytes 196616 | tf_op jit(solution)/shard_map/ppermute | solution.py:207
  132.4 3.6 %collective-permute-done.23.refs_9_ = bf16[128,256]{1,0:T(8,128)(2,1)S(1)} collective-permute-done((bf16[128,256]{1,0:T(8,128)(2,1)S(1)}, bf16[128,256]{1,0:T(8,128)(2,1)S(1)}, u32[]{:S(2)}, u32[]{:S(2)}) %collective-permute-start.23) | collective-permute-done | bytes 65568 | tf_op jit(solution)/shard_map/ppermute | solution.py:207
  140.4 4.2 %collective-permute-start.25 = (bf16[128,256]{1,0:T(8,128)(2,1)S(1)}, bf16[128,256]{1,0:T(8,128)(2,1)S(1)}, u32[]{:S(2)}, u32[]{:S(2)}) collective-permute-start(bf16[128,256]{1,0:T(8,128)(2,1)S(1)} %get-tuple-element.102), channel_id=1, source_target_pairs={{4,0},{8,4},{12,8},{16,12},{20,16},{24,20},{28,24},{5,1},{9,5},{13... | collective-permute-start | bytes 196616 | tf_op jit(solution)/shard_map/ppermute | solution.py:207
  144.6 2.4 %collective-permute-start.26 = (bf16[128,256]{1,0:T(8,128)(2,1)S(1)}, bf16[128,256]{1,0:T(8,128)(2,1)S(1)}, u32[]{:S(2)}, u32[]{:S(2)}) collective-permute-start(bf16[128,256]{1,0:T(8,128)(2,1)S(1)} %get-tuple-element.103), channel_id=1, source_target_pairs={{0,1},{1,2},{2,3},{4,5},{5,6},{6,7},{8,9},{9,10},{10,11},{12,13},{... | collective-permute-start | bytes 196616 | tf_op jit(solution)/shard_map/ppermute | solution.py:207
  147.0 2.1 collective-permute-start.27
  149.1 2.3 %copy-done.4 = bf16[1536,1536]{1,0:T(8,128)(2,1)S(1)} copy-done((bf16[1536,1536]{1,0:T(8,128)(2,1)S(1)}, bf16[1536,1536]{1,0:T(8,128)(2,1)}, u32[]{:S(2)}) %copy-start.4) | copy-done | bytes 4718616
  154.8 4.3 %collective-permute-start.29 = (bf16[128,256]{1,0:T(8,128)(2,1)S(1)}, bf16[128,256]{1,0:T(8,128)(2,1)S(1)}, u32[]{:S(2)}, u32[]{:S(2)}) collective-permute-start(bf16[128,256]{1,0:T(8,128)(2,1)S(1)} %get-tuple-element.106), channel_id=1, source_target_pairs={{4,0},{8,4},{12,8},{16,12},{20,16},{24,20},{28,24},{5,1},{9,5},{13... | collective-permute-start | bytes 196616 | tf_op jit(solution)/shard_map/ppermute | solution.py:207
  159.1 4.1 %collective-permute-start.30 = (bf16[128,256]{1,0:T(8,128)(2,1)S(1)}, bf16[128,256]{1,0:T(8,128)(2,1)S(1)}, u32[]{:S(2)}, u32[]{:S(2)}) collective-permute-start(bf16[128,256]{1,0:T(8,128)(2,1)S(1)} %get-tuple-element.107), channel_id=1, source_target_pairs={{0,1},{1,2},{2,3},{4,5},{5,6},{6,7},{8,9},{9,10},{10,11},{12,13},{... | collective-permute-start | bytes 196616 | tf_op jit(solution)/shard_map/ppermute | solution.py:207
  163.2 2.1 collective-permute-start.31
  165.8 3.2 %collective-permute-done.31.r3 = bf16[128,256]{1,0:T(8,128)(2,1)S(1)} collective-permute-done((bf16[128,256]{1,0:T(8,128)(2,1)S(1)}, bf16[128,256]{1,0:T(8,128)(2,1)S(1)}, u32[]{:S(2)}, u32[]{:S(2)}) %collective-permute-start.31) | collective-permute-done | bytes 65568 | tf_op jit(solution)/shard_map/ppermute | solution.py:207
  172.1 4.3 %collective-permute-start.33 = (bf16[128,256]{1,0:T(8,128)(2,1)S(1)}, bf16[128,256]{1,0:T(8,128)(2,1)S(1)}, u32[]{:S(2)}, u32[]{:S(2)}) collective-permute-start(bf16[128,256]{1,0:T(8,128)(2,1)S(1)} %get-tuple-element.111), channel_id=1, source_target_pairs={{4,0},{8,4},{12,8},{16,12},{20,16},{24,20},{28,24},{5,1},{9,5},{13... | collective-permute-start | bytes 196616 | tf_op jit(solution)/shard_map/ppermute | solution.py:207
  176.4 2.4 %collective-permute-start.34 = (bf16[128,256]{1,0:T(8,128)(2,1)S(1)}, bf16[128,256]{1,0:T(8,128)(2,1)S(1)}, u32[]{:S(2)}, u32[]{:S(2)}) collective-permute-start(bf16[128,256]{1,0:T(8,128)(2,1)S(1)} %get-tuple-element.112), channel_id=1, source_target_pairs={{0,1},{1,2},{2,3},{4,5},{5,6},{6,7},{8,9},{9,10},{10,11},{12,13},{... | collective-permute-start | bytes 196616 | tf_op jit(solution)/shard_map/ppermute | solution.py:207
  180.8 3.6 %collective-permute-done.35.g3 = bf16[128,256]{1,0:T(8,128)(2,1)S(1)} collective-permute-done((bf16[128,256]{1,0:T(8,128)(2,1)S(1)}, bf16[128,256]{1,0:T(8,128)(2,1)S(1)}, u32[]{:S(2)}, u32[]{:S(2)}) %collective-permute-start.35) | collective-permute-done | bytes 65568 | tf_op jit(solution)/shard_map/ppermute | solution.py:207
  184.6 4.1 %all_gather.11.gathered = bf16[128,256]{1,0:T(8,128)(2,1)S(1)} all-gather(bf16[32,256]{1,0:T(8,128)(2,1)S(1)} %restrict.5), channel_id=1, replica_groups=mesh['row'=8,'col'=4] {'col'}, dimensions={0}, use_global_device_ids=true | all-gather | bytes 81920 | tf_op jit(solution)/shard_map/all_gather | solution.py:297
  189.6 4.1 %all-to-all-start.2 = ((bf16[8,32,256]{2,1,0:T(8,128)(2,1)}), bf16[8,32,256]{2,1,0:T(8,128)(2,1)S(1)}, u32[]{:S(2)}, u32[]{:S(2)}) async-start(bf16[8,32,256]{2,1,0:T(8,128)(2,1)} %coarse_part.5), calls=%async_computation.2 | async-start | bytes 262144 | tf_op jit(solution)/shard_map/all_to_all | solution.py:306
  193.7 2.3 %copy-done.2 = bf16[1536,1536]{1,0:T(8,128)(2,1)S(1)} copy-done((bf16[1536,1536]{1,0:T(8,128)(2,1)S(1)}, bf16[1536,1536]{1,0:T(8,128)(2,1)}, u32[]{:S(2)}) %copy-start.2) | copy-done | bytes 4718616
  198.6 2.9 %collective-permute-start.36 = (bf16[128,256]{1,0:T(8,128)(2,1)S(1)}, bf16[128,256]{1,0:T(8,128)(2,1)S(1)}, u32[]{:S(2)}, u32[]{:S(2)}) collective-permute-start(bf16[128,256]{1,0:T(8,128)(2,1)S(1)} %get-tuple-element.115), channel_id=1, source_target_pairs={{0,4},{4,8},{8,12},{12,16},{16,20},{20,24},{24,28},{1,5},{5,9},{9,... | collective-permute-start | bytes 196616 | tf_op jit(solution)/shard_map/ppermute | solution.py:207
  201.5 3.4 %collective-permute-start.37 = (bf16[128,256]{1,0:T(8,128)(2,1)S(1)}, bf16[128,256]{1,0:T(8,128)(2,1)S(1)}, u32[]{:S(2)}, u32[]{:S(2)}) collective-permute-start(bf16[128,256]{1,0:T(8,128)(2,1)S(1)} %get-tuple-element.116), channel_id=1, source_target_pairs={{4,0},{8,4},{12,8},{16,12},{20,16},{24,20},{28,24},{5,1},{9,5},{13... | collective-permute-start | bytes 196616 | tf_op jit(solution)/shard_map/ppermute | solution.py:207
  204.9 5.2 %collective-permute-start.38 = (bf16[128,256]{1,0:T(8,128)(2,1)S(1)}, bf16[128,256]{1,0:T(8,128)(2,1)S(1)}, u32[]{:S(2)}, u32[]{:S(2)}) collective-permute-start(bf16[128,256]{1,0:T(8,128)(2,1)S(1)} %get-tuple-element.117), channel_id=1, source_target_pairs={{0,1},{1,2},{2,3},{4,5},{5,6},{6,7},{8,9},{9,10},{10,11},{12,13},{... | collective-permute-start | bytes 196616 | tf_op jit(solution)/shard_map/ppermute | solution.py:207
  212.0 3.6 %collective-permute-done.39.r3 = bf16[128,256]{1,0:T(8,128)(2,1)S(1)} collective-permute-done((bf16[128,256]{1,0:T(8,128)(2,1)S(1)}, bf16[128,256]{1,0:T(8,128)(2,1)S(1)}, u32[]{:S(2)}, u32[]{:S(2)}) %collective-permute-start.39) | collective-permute-done | bytes 65568 | tf_op jit(solution)/shard_map/ppermute | solution.py:207
  (106 shorter events, 50.8 us)
Async XLA Ops:
  0.0 24.2 %copy-start.18 = (bf16[8,32,128]{2,1,0:T(8,128)(2,1)S(1)}, bf16[8,32,128]{2,1,0:T(8,128)(2,1)}, u32[]{:S(2)}) copy-start(bf16[8,32,128]{2,1,0:T(8,128)(2,1)} %inverse.5) | copy-start | bytes 196612
  3.0 12.4 %collective-permute-start = (bf16[128,256]{1,0:T(8,128)(2,1)S(1)}, bf16[128,256]{1,0:T(8,128)(2,1)S(1)}, u32[]{:S(2)}, u32[]{:S(2)}) collective-permute-start(bf16[128,256]{1,0:T(8,128)(2,1)S(1)} %get-tuple-element.65), channel_id=1, source_target_pairs={{0,4},{4,8},{8,12},{12,16},{16,20},{20,24},{24,28},{1,5},{5,9},{9,... | collective-permute-start | bytes 196616 | tf_op jit(solution)/shard_map/ppermute | solution.py:207
  6.1 9.2 %collective-permute-start.1 = (bf16[128,256]{1,0:T(8,128)(2,1)S(1)}, bf16[128,256]{1,0:T(8,128)(2,1)S(1)}, u32[]{:S(2)}, u32[]{:S(2)}) collective-permute-start(bf16[128,256]{1,0:T(8,128)(2,1)S(1)} %get-tuple-element.66), channel_id=1, source_target_pairs={{4,0},{8,4},{12,8},{16,12},{20,16},{24,20},{28,24},{5,1},{9,5},{13... | collective-permute-start | bytes 196616 | tf_op jit(solution)/shard_map/ppermute | solution.py:207
  9.2 6.2 %collective-permute-start.2 = (bf16[128,256]{1,0:T(8,128)(2,1)S(1)}, bf16[128,256]{1,0:T(8,128)(2,1)S(1)}, u32[]{:S(2)}, u32[]{:S(2)}) collective-permute-start(bf16[128,256]{1,0:T(8,128)(2,1)S(1)} %get-tuple-element.67), channel_id=1, source_target_pairs={{0,1},{1,2},{2,3},{4,5},{5,6},{6,7},{8,9},{9,10},{10,11},{12,13},{... | collective-permute-start | bytes 196616 | tf_op jit(solution)/shard_map/ppermute | solution.py:207
  13.4 5.6 %collective-permute-start.3 = (bf16[128,256]{1,0:T(8,128)(2,1)S(1)}, bf16[128,256]{1,0:T(8,128)(2,1)S(1)}, u32[]{:S(2)}, u32[]{:S(2)}) collective-permute-start(bf16[128,256]{1,0:T(8,128)(2,1)S(1)} %get-tuple-element.68), channel_id=1, source_target_pairs={{1,0},{2,1},{3,2},{5,4},{6,5},{7,6},{9,8},{10,9},{11,10},{13,12},{... | collective-permute-start | bytes 196616 | tf_op jit(solution)/shard_map/ppermute | solution.py:207
  25.1 12.5 %all-to-all-start = ((bf16[8,32,256]{2,1,0:T(8,128)(2,1)}), bf16[8,32,256]{2,1,0:T(8,128)(2,1)S(1)}, u32[]{:S(2)}, u32[]{:S(2)}) async-start(bf16[8,32,256]{2,1,0:T(8,128)(2,1)} %coarse_part.3), calls=%async_computation | async-start | bytes 262144 | tf_op jit(solution)/shard_map/all_to_all | solution.py:306
  39.2 12.4 %collective-permute-start.4 = (bf16[128,256]{1,0:T(8,128)(2,1)S(1)}, bf16[128,256]{1,0:T(8,128)(2,1)S(1)}, u32[]{:S(2)}, u32[]{:S(2)}) collective-permute-start(bf16[128,256]{1,0:T(8,128)(2,1)S(1)} %get-tuple-element.72), channel_id=1, source_target_pairs={{0,4},{4,8},{8,12},{12,16},{16,20},{20,24},{24,28},{1,5},{5,9},{9,... | collective-permute-start | bytes 196616 | tf_op jit(solution)/shard_map/ppermute | solution.py:207
  42.3 9.3 %collective-permute-start.5 = (bf16[128,256]{1,0:T(8,128)(2,1)S(1)}, bf16[128,256]{1,0:T(8,128)(2,1)S(1)}, u32[]{:S(2)}, u32[]{:S(2)}) collective-permute-start(bf16[128,256]{1,0:T(8,128)(2,1)S(1)} %get-tuple-element.73), channel_id=1, source_target_pairs={{4,0},{8,4},{12,8},{16,12},{20,16},{24,20},{28,24},{5,1},{9,5},{13... | collective-permute-start | bytes 196616 | tf_op jit(solution)/shard_map/ppermute | solution.py:207
  45.4 6.2 %collective-permute-start.6 = (bf16[128,256]{1,0:T(8,128)(2,1)S(1)}, bf16[128,256]{1,0:T(8,128)(2,1)S(1)}, u32[]{:S(2)}, u32[]{:S(2)}) collective-permute-start(bf16[128,256]{1,0:T(8,128)(2,1)S(1)} %get-tuple-element.74), channel_id=1, source_target_pairs={{0,1},{1,2},{2,3},{4,5},{5,6},{6,7},{8,9},{9,10},{10,11},{12,13},{... | collective-permute-start | bytes 196616 | tf_op jit(solution)/shard_map/ppermute | solution.py:207
  49.6 5.6 %collective-permute-start.7 = (bf16[128,256]{1,0:T(8,128)(2,1)S(1)}, bf16[128,256]{1,0:T(8,128)(2,1)S(1)}, u32[]{:S(2)}, u32[]{:S(2)}) collective-permute-start(bf16[128,256]{1,0:T(8,128)(2,1)S(1)} %get-tuple-element.75), channel_id=1, source_target_pairs={{1,0},{2,1},{3,2},{5,4},{6,5},{7,6},{9,8},{10,9},{11,10},{13,12},{... | collective-permute-start | bytes 196616 | tf_op jit(solution)/shard_map/ppermute | solution.py:207
  56.7 14.3 %copy-start.14 = (f32[1024,256]{1,0:T(8,128)}, f32[1024,256]{1,0:T(8,128)S(1)}, u32[]{:S(2)}) copy-start(f32[1024,256]{1,0:T(8,128)S(1)} %get-tuple-element.76.refs_0_) | copy-start | bytes 3145732
  56.7 14.3 %collective-permute-start.8 = (bf16[128,256]{1,0:T(8,128)(2,1)S(1)}, bf16[128,256]{1,0:T(8,128)(2,1)S(1)}, u32[]{:S(2)}, u32[]{:S(2)}) collective-permute-start(bf16[128,256]{1,0:T(8,128)(2,1)S(1)} %get-tuple-element.81), channel_id=1, source_target_pairs={{0,4},{4,8},{8,12},{12,16},{16,20},{20,24},{24,28},{1,5},{5,9},{9,... | collective-permute-start | bytes 196616 | tf_op jit(solution)/shard_map/ppermute | solution.py:207
  58.9 12.1 %collective-permute-start.9 = (bf16[128,256]{1,0:T(8,128)(2,1)S(1)}, bf16[128,256]{1,0:T(8,128)(2,1)S(1)}, u32[]{:S(2)}, u32[]{:S(2)}) collective-permute-start(bf16[128,256]{1,0:T(8,128)(2,1)S(1)} %get-tuple-element.82), channel_id=1, source_target_pairs={{4,0},{8,4},{12,8},{16,12},{20,16},{24,20},{28,24},{5,1},{9,5},{13... | collective-permute-start | bytes 196616 | tf_op jit(solution)/shard_map/ppermute | solution.py:207
  62.9 8.1 %collective-permute-start.10 = (bf16[128,256]{1,0:T(8,128)(2,1)S(1)}, bf16[128,256]{1,0:T(8,128)(2,1)S(1)}, u32[]{:S(2)}, u32[]{:S(2)}) collective-permute-start(bf16[128,256]{1,0:T(8,128)(2,1)S(1)} %get-tuple-element.83), channel_id=1, source_target_pairs={{0,1},{1,2},{2,3},{4,5},{5,6},{6,7},{8,9},{9,10},{10,11},{12,13},{... | collective-permute-start | bytes 196616 | tf_op jit(solution)/shard_map/ppermute | solution.py:207
  65.3 5.7 %collective-permute-start.11 = (bf16[128,256]{1,0:T(8,128)(2,1)S(1)}, bf16[128,256]{1,0:T(8,128)(2,1)S(1)}, u32[]{:S(2)}, u32[]{:S(2)}) collective-permute-start(bf16[128,256]{1,0:T(8,128)(2,1)S(1)} %get-tuple-element.84), channel_id=1, source_target_pairs={{1,0},{2,1},{3,2},{5,4},{6,5},{7,6},{9,8},{10,9},{11,10},{13,12},{... | collective-permute-start | bytes 196616 | tf_op jit(solution)/shard_map/ppermute | solution.py:207
  71.0 12.8 %copy-start.3 = (bf16[1536,1536]{1,0:T(8,128)(2,1)}, bf16[1536,1536]{1,0:T(8,128)(2,1)S(1)}, u32[]{:S(2)}) copy-start(bf16[1536,1536]{1,0:T(8,128)(2,1)S(1)} %get-tuple-element.79.matrix) | copy-start | bytes 14155780
  71.3 12.9 %collective-permute-start.12 = (bf16[128,256]{1,0:T(8,128)(2,1)S(1)}, bf16[128,256]{1,0:T(8,128)(2,1)S(1)}, u32[]{:S(2)}, u32[]{:S(2)}) collective-permute-start(bf16[128,256]{1,0:T(8,128)(2,1)S(1)} %get-tuple-element.85), channel_id=1, source_target_pairs={{0,4},{4,8},{8,12},{12,16},{16,20},{20,24},{24,28},{1,5},{5,9},{9,... | collective-permute-start | bytes 196616 | tf_op jit(solution)/shard_map/ppermute | solution.py:207
  73.2 11.0 %collective-permute-start.13 = (bf16[128,256]{1,0:T(8,128)(2,1)S(1)}, bf16[128,256]{1,0:T(8,128)(2,1)S(1)}, u32[]{:S(2)}, u32[]{:S(2)}) collective-permute-start(bf16[128,256]{1,0:T(8,128)(2,1)S(1)} %get-tuple-element.86), channel_id=1, source_target_pairs={{4,0},{8,4},{12,8},{16,12},{20,16},{24,20},{28,24},{5,1},{9,5},{13... | collective-permute-start | bytes 196616 | tf_op jit(solution)/shard_map/ppermute | solution.py:207
  77.5 6.8 %collective-permute-start.14 = (bf16[128,256]{1,0:T(8,128)(2,1)S(1)}, bf16[128,256]{1,0:T(8,128)(2,1)S(1)}, u32[]{:S(2)}, u32[]{:S(2)}) collective-permute-start(bf16[128,256]{1,0:T(8,128)(2,1)S(1)} %get-tuple-element.87), channel_id=1, source_target_pairs={{0,1},{1,2},{2,3},{4,5},{5,6},{6,7},{8,9},{9,10},{10,11},{12,13},{... | collective-permute-start | bytes 196616 | tf_op jit(solution)/shard_map/ppermute | solution.py:207
  81.7 5.7 %collective-permute-start.15 = (bf16[128,256]{1,0:T(8,128)(2,1)S(1)}, bf16[128,256]{1,0:T(8,128)(2,1)S(1)}, u32[]{:S(2)}, u32[]{:S(2)}) collective-permute-start(bf16[128,256]{1,0:T(8,128)(2,1)S(1)} %get-tuple-element.88), channel_id=1, source_target_pairs={{1,0},{2,1},{3,2},{5,4},{6,5},{7,6},{9,8},{10,9},{11,10},{13,12},{... | collective-permute-start | bytes 196616 | tf_op jit(solution)/shard_map/ppermute | solution.py:207
  88.7 10.6 %collective-permute-start.16 = (bf16[128,256]{1,0:T(8,128)(2,1)S(1)}, bf16[128,256]{1,0:T(8,128)(2,1)S(1)}, u32[]{:S(2)}, u32[]{:S(2)}) collective-permute-start(bf16[128,256]{1,0:T(8,128)(2,1)S(1)} %get-tuple-element.90), channel_id=1, source_target_pairs={{0,4},{4,8},{8,12},{12,16},{16,20},{20,24},{24,28},{1,5},{5,9},{9,... | collective-permute-start | bytes 196616 | tf_op jit(solution)/shard_map/ppermute | solution.py:207
  90.6 8.6 %collective-permute-start.17 = (bf16[128,256]{1,0:T(8,128)(2,1)S(1)}, bf16[128,256]{1,0:T(8,128)(2,1)S(1)}, u32[]{:S(2)}, u32[]{:S(2)}) collective-permute-start(bf16[128,256]{1,0:T(8,128)(2,1)S(1)} %get-tuple-element.91), channel_id=1, source_target_pairs={{4,0},{8,4},{12,8},{16,12},{20,16},{24,20},{28,24},{5,1},{9,5},{13... | collective-permute-start | bytes 196616 | tf_op jit(solution)/shard_map/ppermute | solution.py:207
  94.9 4.4 %collective-permute-start.18 = (bf16[128,256]{1,0:T(8,128)(2,1)S(1)}, bf16[128,256]{1,0:T(8,128)(2,1)S(1)}, u32[]{:S(2)}, u32[]{:S(2)}) collective-permute-start(bf16[128,256]{1,0:T(8,128)(2,1)S(1)} %get-tuple-element.92), channel_id=1, source_target_pairs={{0,1},{1,2},{2,3},{4,5},{5,6},{6,7},{8,9},{9,10},{10,11},{12,13},{... | collective-permute-start | bytes 196616 | tf_op jit(solution)/shard_map/ppermute | solution.py:207
  97.3 5.6 %collective-permute-start.19 = (bf16[128,256]{1,0:T(8,128)(2,1)S(1)}, bf16[128,256]{1,0:T(8,128)(2,1)S(1)}, u32[]{:S(2)}, u32[]{:S(2)}) collective-permute-start(bf16[128,256]{1,0:T(8,128)(2,1)S(1)} %get-tuple-element.93), channel_id=1, source_target_pairs={{1,0},{2,1},{3,2},{5,4},{6,5},{7,6},{9,8},{10,9},{11,10},{13,12},{... | collective-permute-start | bytes 196616 | tf_op jit(solution)/shard_map/ppermute | solution.py:207
  108.1 9.6 %all-to-all-start.1 = ((bf16[8,32,256]{2,1,0:T(8,128)(2,1)}), bf16[8,32,256]{2,1,0:T(8,128)(2,1)S(1)}, u32[]{:S(2)}, u32[]{:S(2)}) async-start(bf16[8,32,256]{2,1,0:T(8,128)(2,1)} %coarse_part.4), calls=%async_computation.1 | async-start | bytes 262144 | tf_op jit(solution)/shard_map/all_to_all | solution.py:306
  119.1 16.9 %copy-start.15 = (f32[1024,256]{1,0:T(8,128)S(1)}, f32[1024,256]{1,0:T(8,128)}, u32[]{:S(2)}) copy-start(f32[1024,256]{1,0:T(8,128)} %copy-done.14) | copy-start | bytes 3145732
  119.4 13.0 %collective-permute-start.20 = (bf16[128,256]{1,0:T(8,128)(2,1)S(1)}, bf16[128,256]{1,0:T(8,128)(2,1)S(1)}, u32[]{:S(2)}, u32[]{:S(2)}) collective-permute-start(bf16[128,256]{1,0:T(8,128)(2,1)S(1)} %get-tuple-element.95), channel_id=1, source_target_pairs={{0,4},{4,8},{8,12},{12,16},{16,20},{20,24},{24,28},{1,5},{5,9},{9,... | collective-permute-start | bytes 196616 | tf_op jit(solution)/shard_map/ppermute | solution.py:207
  122.6 9.8 %collective-permute-start.21 = (bf16[128,256]{1,0:T(8,128)(2,1)S(1)}, bf16[128,256]{1,0:T(8,128)(2,1)S(1)}, u32[]{:S(2)}, u32[]{:S(2)}) collective-permute-start(bf16[128,256]{1,0:T(8,128)(2,1)S(1)} %get-tuple-element.96), channel_id=1, source_target_pairs={{4,0},{8,4},{12,8},{16,12},{20,16},{24,20},{28,24},{5,1},{9,5},{13... | collective-permute-start | bytes 196616 | tf_op jit(solution)/shard_map/ppermute | solution.py:207
  125.7 6.7 %collective-permute-start.22 = (bf16[128,256]{1,0:T(8,128)(2,1)S(1)}, bf16[128,256]{1,0:T(8,128)(2,1)S(1)}, u32[]{:S(2)}, u32[]{:S(2)}) collective-permute-start(bf16[128,256]{1,0:T(8,128)(2,1)S(1)} %get-tuple-element.97), channel_id=1, source_target_pairs={{0,1},{1,2},{2,3},{4,5},{5,6},{6,7},{8,9},{9,10},{10,11},{12,13},{... | collective-permute-start | bytes 196616 | tf_op jit(solution)/shard_map/ppermute | solution.py:207
  130.4 5.6 %collective-permute-start.23 = (bf16[128,256]{1,0:T(8,128)(2,1)S(1)}, bf16[128,256]{1,0:T(8,128)(2,1)S(1)}, u32[]{:S(2)}, u32[]{:S(2)}) collective-permute-start(bf16[128,256]{1,0:T(8,128)(2,1)S(1)} %get-tuple-element.98), channel_id=1, source_target_pairs={{1,0},{2,1},{3,2},{5,4},{6,5},{7,6},{9,8},{10,9},{11,10},{13,12},{... | collective-permute-start | bytes 196616 | tf_op jit(solution)/shard_map/ppermute | solution.py:207
  138.4 14.1 %collective-permute-start.24 = (bf16[128,256]{1,0:T(8,128)(2,1)S(1)}, bf16[128,256]{1,0:T(8,128)(2,1)S(1)}, u32[]{:S(2)}, u32[]{:S(2)}) collective-permute-start(bf16[128,256]{1,0:T(8,128)(2,1)S(1)} %get-tuple-element.101), channel_id=1, source_target_pairs={{0,4},{4,8},{8,12},{12,16},{16,20},{20,24},{24,28},{1,5},{5,9},{9,... | collective-permute-start | bytes 196616 | tf_op jit(solution)/shard_map/ppermute | solution.py:207
  140.4 12.1 %collective-permute-start.25 = (bf16[128,256]{1,0:T(8,128)(2,1)S(1)}, bf16[128,256]{1,0:T(8,128)(2,1)S(1)}, u32[]{:S(2)}, u32[]{:S(2)}) collective-permute-start(bf16[128,256]{1,0:T(8,128)(2,1)S(1)} %get-tuple-element.102), channel_id=1, source_target_pairs={{4,0},{8,4},{12,8},{16,12},{20,16},{24,20},{28,24},{5,1},{9,5},{13... | collective-permute-start | bytes 196616 | tf_op jit(solution)/shard_map/ppermute | solution.py:207
  144.6 7.9 %collective-permute-start.26 = (bf16[128,256]{1,0:T(8,128)(2,1)S(1)}, bf16[128,256]{1,0:T(8,128)(2,1)S(1)}, u32[]{:S(2)}, u32[]{:S(2)}) collective-permute-start(bf16[128,256]{1,0:T(8,128)(2,1)S(1)} %get-tuple-element.103), channel_id=1, source_target_pairs={{0,1},{1,2},{2,3},{4,5},{5,6},{6,7},{8,9},{9,10},{10,11},{12,13},{... | collective-permute-start | bytes 196616 | tf_op jit(solution)/shard_map/ppermute | solution.py:207
  147.0 5.6 %collective-permute-start.27 = (bf16[128,256]{1,0:T(8,128)(2,1)S(1)}, bf16[128,256]{1,0:T(8,128)(2,1)S(1)}, u32[]{:S(2)}, u32[]{:S(2)}) collective-permute-start(bf16[128,256]{1,0:T(8,128)(2,1)S(1)} %get-tuple-element.104), channel_id=1, source_target_pairs={{1,0},{2,1},{3,2},{5,4},{6,5},{7,6},{9,8},{10,9},{11,10},{13,12},{... | collective-permute-start | bytes 196616 | tf_op jit(solution)/shard_map/ppermute | solution.py:207
  152.9 12.8 %collective-permute-start.28 = (bf16[128,256]{1,0:T(8,128)(2,1)S(1)}, bf16[128,256]{1,0:T(8,128)(2,1)S(1)}, u32[]{:S(2)}, u32[]{:S(2)}) collective-permute-start(bf16[128,256]{1,0:T(8,128)(2,1)S(1)} %get-tuple-element.105), channel_id=1, source_target_pairs={{0,4},{4,8},{8,12},{12,16},{16,20},{20,24},{24,28},{1,5},{5,9},{9,... | collective-permute-start | bytes 196616 | tf_op jit(solution)/shard_map/ppermute | solution.py:207
  154.8 10.9 %collective-permute-start.29 = (bf16[128,256]{1,0:T(8,128)(2,1)S(1)}, bf16[128,256]{1,0:T(8,128)(2,1)S(1)}, u32[]{:S(2)}, u32[]{:S(2)}) collective-permute-start(bf16[128,256]{1,0:T(8,128)(2,1)S(1)} %get-tuple-element.106), channel_id=1, source_target_pairs={{4,0},{8,4},{12,8},{16,12},{20,16},{24,20},{28,24},{5,1},{9,5},{13... | collective-permute-start | bytes 196616 | tf_op jit(solution)/shard_map/ppermute | solution.py:207
  159.1 6.6 %collective-permute-start.30 = (bf16[128,256]{1,0:T(8,128)(2,1)S(1)}, bf16[128,256]{1,0:T(8,128)(2,1)S(1)}, u32[]{:S(2)}, u32[]{:S(2)}) collective-permute-start(bf16[128,256]{1,0:T(8,128)(2,1)S(1)} %get-tuple-element.107), channel_id=1, source_target_pairs={{0,1},{1,2},{2,3},{4,5},{5,6},{6,7},{8,9},{9,10},{10,11},{12,13},{... | collective-permute-start | bytes 196616 | tf_op jit(solution)/shard_map/ppermute | solution.py:207
  163.2 5.7 %collective-permute-start.31 = (bf16[128,256]{1,0:T(8,128)(2,1)S(1)}, bf16[128,256]{1,0:T(8,128)(2,1)S(1)}, u32[]{:S(2)}, u32[]{:S(2)}) collective-permute-start(bf16[128,256]{1,0:T(8,128)(2,1)S(1)} %get-tuple-element.108), channel_id=1, source_target_pairs={{1,0},{2,1},{3,2},{5,4},{6,5},{7,6},{9,8},{10,9},{11,10},{13,12},{... | collective-permute-start | bytes 196616 | tf_op jit(solution)/shard_map/ppermute | solution.py:207
  170.2 10.6 %collective-permute-start.32 = (bf16[128,256]{1,0:T(8,128)(2,1)S(1)}, bf16[128,256]{1,0:T(8,128)(2,1)S(1)}, u32[]{:S(2)}, u32[]{:S(2)}) collective-permute-start(bf16[128,256]{1,0:T(8,128)(2,1)S(1)} %get-tuple-element.110), channel_id=1, source_target_pairs={{0,4},{4,8},{8,12},{12,16},{16,20},{20,24},{24,28},{1,5},{5,9},{9,... | collective-permute-start | bytes 196616 | tf_op jit(solution)/shard_map/ppermute | solution.py:207
  172.1 8.6 %collective-permute-start.33 = (bf16[128,256]{1,0:T(8,128)(2,1)S(1)}, bf16[128,256]{1,0:T(8,128)(2,1)S(1)}, u32[]{:S(2)}, u32[]{:S(2)}) collective-permute-start(bf16[128,256]{1,0:T(8,128)(2,1)S(1)} %get-tuple-element.111), channel_id=1, source_target_pairs={{4,0},{8,4},{12,8},{16,12},{20,16},{24,20},{28,24},{5,1},{9,5},{13... | collective-permute-start | bytes 196616 | tf_op jit(solution)/shard_map/ppermute | solution.py:207
  176.4 4.4 %collective-permute-start.34 = (bf16[128,256]{1,0:T(8,128)(2,1)S(1)}, bf16[128,256]{1,0:T(8,128)(2,1)S(1)}, u32[]{:S(2)}, u32[]{:S(2)}) collective-permute-start(bf16[128,256]{1,0:T(8,128)(2,1)S(1)} %get-tuple-element.112), channel_id=1, source_target_pairs={{0,1},{1,2},{2,3},{4,5},{5,6},{6,7},{8,9},{9,10},{10,11},{12,13},{... | collective-permute-start | bytes 196616 | tf_op jit(solution)/shard_map/ppermute | solution.py:207
  178.8 5.6 %collective-permute-start.35 = (bf16[128,256]{1,0:T(8,128)(2,1)S(1)}, bf16[128,256]{1,0:T(8,128)(2,1)S(1)}, u32[]{:S(2)}, u32[]{:S(2)}) collective-permute-start(bf16[128,256]{1,0:T(8,128)(2,1)S(1)} %get-tuple-element.113), channel_id=1, source_target_pairs={{1,0},{2,1},{3,2},{5,4},{6,5},{7,6},{9,8},{10,9},{11,10},{13,12},{... | collective-permute-start | bytes 196616 | tf_op jit(solution)/shard_map/ppermute | solution.py:207
  189.6 8.7 %all-to-all-start.2 = ((bf16[8,32,256]{2,1,0:T(8,128)(2,1)}), bf16[8,32,256]{2,1,0:T(8,128)(2,1)S(1)}, u32[]{:S(2)}, u32[]{:S(2)}) async-start(bf16[8,32,256]{2,1,0:T(8,128)(2,1)} %coarse_part.5), calls=%async_computation.2 | async-start | bytes 262144 | tf_op jit(solution)/shard_map/all_to_all | solution.py:306
  198.3 17.4 %copy-start.17 = (f32[1024,256]{1,0:T(8,128)S(1)}, f32[1024,256]{1,0:T(8,128)}, u32[]{:S(2)}) copy-start(f32[1024,256]{1,0:T(8,128)} %copy-done.16) | copy-start | bytes 3145732
  198.6 13.4 %collective-permute-start.36 = (bf16[128,256]{1,0:T(8,128)(2,1)S(1)}, bf16[128,256]{1,0:T(8,128)(2,1)S(1)}, u32[]{:S(2)}, u32[]{:S(2)}) collective-permute-start(bf16[128,256]{1,0:T(8,128)(2,1)S(1)} %get-tuple-element.115), channel_id=1, source_target_pairs={{0,4},{4,8},{8,12},{12,16},{16,20},{20,24},{24,28},{1,5},{5,9},{9,... | collective-permute-start | bytes 196616 | tf_op jit(solution)/shard_map/ppermute | solution.py:207
  201.5 10.5 %collective-permute-start.37 = (bf16[128,256]{1,0:T(8,128)(2,1)S(1)}, bf16[128,256]{1,0:T(8,128)(2,1)S(1)}, u32[]{:S(2)}, u32[]{:S(2)}) collective-permute-start(bf16[128,256]{1,0:T(8,128)(2,1)S(1)} %get-tuple-element.116), channel_id=1, source_target_pairs={{4,0},{8,4},{12,8},{16,12},{20,16},{24,20},{28,24},{5,1},{9,5},{13... | collective-permute-start | bytes 196616 | tf_op jit(solution)/shard_map/ppermute | solution.py:207
  204.9 7.1 %collective-permute-start.38 = (bf16[128,256]{1,0:T(8,128)(2,1)S(1)}, bf16[128,256]{1,0:T(8,128)(2,1)S(1)}, u32[]{:S(2)}, u32[]{:S(2)}) collective-permute-start(bf16[128,256]{1,0:T(8,128)(2,1)S(1)} %get-tuple-element.117), channel_id=1, source_target_pairs={{0,1},{1,2},{2,3},{4,5},{5,6},{6,7},{8,9},{9,10},{10,11},{12,13},{... | collective-permute-start | bytes 196616 | tf_op jit(solution)/shard_map/ppermute | solution.py:207
  210.1 5.6 %collective-permute-start.39 = (bf16[128,256]{1,0:T(8,128)(2,1)S(1)}, bf16[128,256]{1,0:T(8,128)(2,1)S(1)}, u32[]{:S(2)}, u32[]{:S(2)}) collective-permute-start(bf16[128,256]{1,0:T(8,128)(2,1)S(1)} %get-tuple-element.118), channel_id=1, source_target_pairs={{1,0},{2,1},{3,2},{5,4},{6,5},{7,6},{9,8},{10,9},{11,10},{13,12},{... | collective-permute-start | bytes 196616 | tf_op jit(solution)/shard_map/ppermute | solution.py:207
  (14 other events, 32.6 us)

commit v3 on v2

--- a/solution.py
+++ b/solution.py
@@ -104,17 +104,13 @@
     out[...] = partial[...] + product(matrix[:, own:], stacked(g0, g1, g2, g3))
 
 
-def partial_kernel(inverse, gathered, out):
-    for i in range(inverse.shape[0]):
-        out[i, :, :] = product(inverse[i, :, :], gathered[...]).astype(HALF)
-
-
-def coarse_kernel(parts, basis, local, level, *tiles):
+def coarse_kernel(coarse_rows, gathered, basis, local, level, *tiles):
     tile = tiles[0].shape[0]
     own = local.shape[0] - 4 * tile
-    total = parts[0, :, :].astype(FULL)
-    for i in range(1, parts.shape[0]):
-        total += parts[i, :, :].astype(FULL)
+    width = coarse_rows.shape[2]
+    total = product(coarse_rows[0, :, :], gathered[:width, :])
+    for i in range(1, coarse_rows.shape[0]):
+        total += product(coarse_rows[i, :, :], gathered[i * width : (i + 1) * width, :])
     level[...] = total.astype(HALF)
     for d in range(4):
         at = slice(own + d * tile, own + (d + 1) * tile)
@@ -229,7 +225,9 @@
     tile = rows_list.shape[1]
     margin = 4 * tile
     coarse = basis.shape[0]
-    groups = coarse_inverse.shape[0]
+    coarse_rows = lax.all_to_all(coarse_inverse, "row", 0, 0, tiled=True)
+    coarse_rows, rows_list = lax.optimization_barrier((coarse_rows, rows_list))
+
     four_tiles = [((tile, columns), HALF)] * 4
     owned_half = ((own, columns), HALF)
     target, residual, pick, spread, *tiles = call(
@@ -295,15 +293,7 @@
             flops=2 * local * coarse * columns,
         )
         gathered = lax.all_gather(restricted, "col", axis=0, tiled=True)
-        (parts,) = call(
-            partial_kernel,
-            "coarse_part",
-            [((groups, coarse, columns), HALF)],
-            coarse_inverse,
-            gathered,
-            flops=2 * coarse_inverse.size * columns,
-        )
-        parts = lax.all_to_all(parts, "row", 0, 0, tiled=True)
+        gathered = lax.all_gather(gathered, "row", axis=0, tiled=True)
         (correction,) = call(
             margin_columns_kernel,
             "inverse_margin",
@@ -317,10 +307,11 @@
             coarse_kernel,
             "coarse",
             [((coarse, columns), HALF)] + four_tiles,
-            parts,
+            coarse_rows,
+            gathered,
             basis,
             correction,
-            flops=2 * coarse * margin * columns,
+            flops=2 * (coarse_rows.size + coarse * margin) * columns,
         )
         returned = traded(tiles)
         if sweep == ITERS - 1:

time: 219 us -> 275 us (1.26)
  the two profiles are of different devices: /device:TPU:9 before, /device:TPU:0 now
where the time goes in v3:
time: 275 us; the launch traced here: 270 us
  blocking collectives  137 us (50%)
  starting transfers between devices  90.7 us (33%)
  Pallas kernels  24.4 us (9%)
  waiting for transfers between devices  17.2 us (6%)
    all_gather x3, blocking collectives, per_device(): gathered = lax.all_gather(gathered, 'row', axis=0, tiled=True)  102 us
    ppermute x40, starting transfers between devices, passed_along(): return lax.ppermute(shard, axis, pairs)  90.7 us
    pallas_call x24, Pallas kernels, call(): pl.pallas_call(body, out_shape=tuple(((pltpu.HBM if away else pltpu.VMEM)...  24.4 us
    all_gather x3, blocking collectives, per_device(): gathered = lax.all_gather(restricted, 'col', axis=0, tiled=True)  20.9 us
    ppermute x40, waiting for transfers between devices, passed_along(): return lax.ppermute(shard, axis, pairs)  17.2 us
    all_to_all x1, blocking collectives, per_device(): coarse_rows = lax.all_to_all(coarse_inverse, 'row', 0, 0, tiled=True)  14.2 us
  transfers between devices with their start and end apart: 40, of which 12 were waited for; matrix products, arithmetic and copies ran while one was open for 0% of the time, Pallas kernels for 4%

profile of v3, /device:TPU:0, one launch (start us, length us, event | category | flops | bytes accessed | tf_op | source)
XLA Modules:
  0.0 270.2 jit_solution(4088934708804265240)
XLA Ops:
  0.0 14.2 %all_to_all.5.coarse_rows = bf16[8,32,128]{2,1,0:T(8,128)(2,1)S(1)} all-to-all(bf16[8,32,128]{2,1,0:T(8,128)(2,1)} %param.11), channel_id=1, replica_groups=mesh['row'=8,'col'=4] {'row'}, dimensions={0} | all-to-all | bytes 131072 | tf_op jit(solution)/shard_map/all_to_all | solution.py:228
  14.2 1.9 select.1
  16.1 2.3 collective-permute-start
  18.4 1.3 collective-permute-start.1
  19.7 1.3 collective-permute-start.2
  21.0 1.3 collective-permute-start.3
  22.4 3.7 %inverse_own.3 = (bf16[1536,1536]{1,0:T(8,128)(2,1)S(1)}, f32[1536,256]{1,0:T(8,128)S(1)}) custom-call(bf16[1536,1536]{1,0:T(8,128)(2,1)} %bitcast.18, bf16[1024,256]{1,0:T(8,128)(2,1)S(1)} %get-tuple-element.65.owned), custom_call_target="tpu_custom_call" | custom-call | flops 805306368 | bytes 5242880 | tf_op jit(solution)/shard_map/inverse_own/pallas_call | solution.py:28
  26.4 7.7 %all_gather.18 = bf16[128,256]{1,0:T(8,128)(2,1)S(1)} all-gather(bf16[32,256]{1,0:T(8,128)(2,1)S(1)} %restrict.3), channel_id=1, replica_groups=mesh['row'=8,'col'=4] {'col'}, dimensions={0}, use_global_device_ids=true | all-gather | bytes 81920 | tf_op jit(solution)/shard_map/all_gather | solution.py:295
  34.1 31.9 %all_gather.19.gathered = bf16[1024,256]{1,0:T(8,128)(2,1)S(1)} all-gather(bf16[128,256]{1,0:T(8,128)(2,1)S(1)} %all_gather.18), channel_id=1, replica_groups=mesh['row'=8,'col'=4] {'row'}, dimensions={0}, use_global_device_ids=true | all-gather | bytes 589824 | tf_op jit(solution)/shard_map/all_gather | solution.py:296
  67.0 1.7 collective-permute-start.4
  68.7 1.3 collective-permute-start.5
  70.0 1.3 collective-permute-start.6
  71.3 1.3 collective-permute-start.7
  72.6 2.2 collective-permute-done.5.refs_6_
  74.9 1.8 collective-permute-done.7.refs_8_
  76.7 1.4 update.2
  78.1 4.5 %collective-permute-start.8 = (bf16[128,256]{1,0:T(8,128)(2,1)S(1)}, bf16[128,256]{1,0:T(8,128)(2,1)S(1)}, u32[]{:S(2)}, u32[]{:S(2)}) collective-permute-start(bf16[128,256]{1,0:T(8,128)(2,1)S(1)} %get-tuple-element.85), channel_id=1, source_target_pairs={{0,4},{4,8},{8,12},{12,16},{16,20},{20,24},{24,28},{1,5},{5,9},{9,... | collective-permute-start | bytes 196616 | tf_op jit(solution)/shard_map/ppermute | solution.py:203
  82.7 1.3 collective-permute-start.9
  84.0 4.6 %collective-permute-start.10 = (bf16[128,256]{1,0:T(8,128)(2,1)S(1)}, bf16[128,256]{1,0:T(8,128)(2,1)S(1)}, u32[]{:S(2)}, u32[]{:S(2)}) collective-permute-start(bf16[128,256]{1,0:T(8,128)(2,1)S(1)} %get-tuple-element.87), channel_id=1, source_target_pairs={{0,1},{1,2},{2,3},{4,5},{5,6},{6,7},{8,9},{9,10},{10,11},{12,13},{... | collective-permute-start | bytes 196616 | tf_op jit(solution)/shard_map/ppermute | solution.py:203
  88.6 1.3 collective-permute-start.11
  89.9 3.7 %operator_own.2 = (bf16[1536,1536]{1,0:T(8,128)(2,1)S(1)}, f32[1536,256]{1,0:T(8,128)S(1)}) custom-call(bf16[1536,1536]{1,0:T(8,128)(2,1)} %bitcast.19, bf16[1024,256]{1,0:T(8,128)(2,1)S(1)} %get-tuple-element.82.owned), custom_call_target="tpu_custom_call" | custom-call | flops 805306368 | bytes 5242880 | tf_op jit(solution)/shard_map/operator_own/pallas_call | solution.py:28
  93.9 4.3 %collective-permute-start.12 = (bf16[128,256]{1,0:T(8,128)(2,1)S(1)}, bf16[128,256]{1,0:T(8,128)(2,1)S(1)}, u32[]{:S(2)}, u32[]{:S(2)}) collective-permute-start(bf16[128,256]{1,0:T(8,128)(2,1)S(1)} %get-tuple-element.89), channel_id=1, source_target_pairs={{0,4},{4,8},{8,12},{12,16},{16,20},{20,24},{24,28},{1,5},{5,9},{9,... | collective-permute-start | bytes 196616 | tf_op jit(solution)/shard_map/ppermute | solution.py:203
  99.5 2.8 %collective-permute-start.14 = (bf16[128,256]{1,0:T(8,128)(2,1)S(1)}, bf16[128,256]{1,0:T(8,128)(2,1)S(1)}, u32[]{:S(2)}, u32[]{:S(2)}) collective-permute-start(bf16[128,256]{1,0:T(8,128)(2,1)S(1)} %get-tuple-element.91), channel_id=1, source_target_pairs={{0,1},{1,2},{2,3},{4,5},{5,6},{6,7},{8,9},{9,10},{10,11},{12,13},{... | collective-permute-start | bytes 196616 | tf_op jit(solution)/shard_map/ppermute | solution.py:203
  105.1 1.8 collective-permute-done.15.r3
  108.2 4.8 %collective-permute-start.16 = (bf16[128,256]{1,0:T(8,128)(2,1)S(1)}, bf16[128,256]{1,0:T(8,128)(2,1)S(1)}, u32[]{:S(2)}, u32[]{:S(2)}) collective-permute-start(bf16[128,256]{1,0:T(8,128)(2,1)S(1)} %get-tuple-element.94), channel_id=1, source_target_pairs={{0,4},{4,8},{8,12},{12,16},{16,20},{20,24},{24,28},{1,5},{5,9},{9,... | collective-permute-start | bytes 196616 | tf_op jit(solution)/shard_map/ppermute | solution.py:203
  114.3 4.6 %collective-permute-start.18 = (bf16[128,256]{1,0:T(8,128)(2,1)S(1)}, bf16[128,256]{1,0:T(8,128)(2,1)S(1)}, u32[]{:S(2)}, u32[]{:S(2)}) collective-permute-start(bf16[128,256]{1,0:T(8,128)(2,1)S(1)} %get-tuple-element.96), channel_id=1, source_target_pairs={{0,1},{1,2},{2,3},{4,5},{5,6},{6,7},{8,9},{9,10},{10,11},{12,13},{... | collective-permute-start | bytes 196616 | tf_op jit(solution)/shard_map/ppermute | solution.py:203
  122.3 6.6 %all_gather.20 = bf16[128,256]{1,0:T(8,128)(2,1)S(1)} all-gather(bf16[32,256]{1,0:T(8,128)(2,1)S(1)} %restrict.4), channel_id=1, replica_groups=mesh['row'=8,'col'=4] {'col'}, dimensions={0}, use_global_device_ids=true | all-gather | bytes 81920 | tf_op jit(solution)/shard_map/all_gather | solution.py:295
  128.9 35.0 %all_gather.21.gathered = bf16[1024,256]{1,0:T(8,128)(2,1)S(1)} all-gather(bf16[128,256]{1,0:T(8,128)(2,1)S(1)} %all_gather.20), channel_id=1, replica_groups=mesh['row'=8,'col'=4] {'row'}, dimensions={0}, use_global_device_ids=true | all-gather | bytes 589824 | tf_op jit(solution)/shard_map/all_gather | solution.py:296
  165.0 1.3 collective-permute-start.20
  167.6 1.3 collective-permute-start.22
  170.2 2.2 collective-permute-done.21.refs_7_
  173.4 1.4 update.3
  174.8 4.5 %collective-permute-start.24 = (bf16[128,256]{1,0:T(8,128)(2,1)S(1)}, bf16[128,256]{1,0:T(8,128)(2,1)S(1)}, u32[]{:S(2)}, u32[]{:S(2)}) collective-permute-start(bf16[128,256]{1,0:T(8,128)(2,1)S(1)} %get-tuple-element.105), channel_id=1, source_target_pairs={{0,4},{4,8},{8,12},{12,16},{16,20},{20,24},{24,28},{1,5},{5,9},{9,... | collective-permute-start | bytes 196616 | tf_op jit(solution)/shard_map/ppermute | solution.py:203
  180.7 4.6 %collective-permute-start.26 = (bf16[128,256]{1,0:T(8,128)(2,1)S(1)}, bf16[128,256]{1,0:T(8,128)(2,1)S(1)}, u32[]{:S(2)}, u32[]{:S(2)}) collective-permute-start(bf16[128,256]{1,0:T(8,128)(2,1)S(1)} %get-tuple-element.107), channel_id=1, source_target_pairs={{0,1},{1,2},{2,3},{4,5},{5,6},{6,7},{8,9},{9,10},{10,11},{12,13},{... | collective-permute-start | bytes 196616 | tf_op jit(solution)/shard_map/ppermute | solution.py:203
  185.3 1.5 collective-permute-start.27
  188.7 4.3 %collective-permute-start.28 = (bf16[128,256]{1,0:T(8,128)(2,1)S(1)}, bf16[128,256]{1,0:T(8,128)(2,1)S(1)}, u32[]{:S(2)}, u32[]{:S(2)}) collective-permute-start(bf16[128,256]{1,0:T(8,128)(2,1)S(1)} %get-tuple-element.109), channel_id=1, source_target_pairs={{0,4},{4,8},{8,12},{12,16},{16,20},{20,24},{24,28},{1,5},{5,9},{9,... | collective-permute-start | bytes 196616 | tf_op jit(solution)/shard_map/ppermute | solution.py:203
  193.0 1.3 collective-permute-start.29
  194.3 4.6 %collective-permute-start.30 = (bf16[128,256]{1,0:T(8,128)(2,1)S(1)}, bf16[128,256]{1,0:T(8,128)(2,1)S(1)}, u32[]{:S(2)}, u32[]{:S(2)}) collective-permute-start(bf16[128,256]{1,0:T(8,128)(2,1)S(1)} %get-tuple-element.111), channel_id=1, source_target_pairs={{0,1},{1,2},{2,3},{4,5},{5,6},{6,7},{8,9},{9,10},{10,11},{12,13},{... | collective-permute-start | bytes 196616 | tf_op jit(solution)/shard_map/ppermute | solution.py:203
  200.7 1.4 collective-permute-done.31.r3
  203.3 5.2 %collective-permute-start.32 = (bf16[128,256]{1,0:T(8,128)(2,1)S(1)}, bf16[128,256]{1,0:T(8,128)(2,1)S(1)}, u32[]{:S(2)}, u32[]{:S(2)}) collective-permute-start(bf16[128,256]{1,0:T(8,128)(2,1)S(1)} %get-tuple-element.114), channel_id=1, source_target_pairs={{0,4},{4,8},{8,12},{12,16},{16,20},{20,24},{24,28},{1,5},{5,9},{9,... | collective-permute-start | bytes 196616 | tf_op jit(solution)/shard_map/ppermute | solution.py:203
  209.8 4.3 %collective-permute-start.34 = (bf16[128,256]{1,0:T(8,128)(2,1)S(1)}, bf16[128,256]{1,0:T(8,128)(2,1)S(1)}, u32[]{:S(2)}, u32[]{:S(2)}) collective-permute-start(bf16[128,256]{1,0:T(8,128)(2,1)S(1)} %get-tuple-element.116), channel_id=1, source_target_pairs={{0,1},{1,2},{2,3},{4,5},{5,6},{6,7},{8,9},{9,10},{10,11},{12,13},{... | collective-permute-start | bytes 196616 | tf_op jit(solution)/shard_map/ppermute | solution.py:203
  217.5 6.6 %all_gather.22 = bf16[128,256]{1,0:T(8,128)(2,1)S(1)} all-gather(bf16[32,256]{1,0:T(8,128)(2,1)S(1)} %restrict.5), channel_id=1, replica_groups=mesh['row'=8,'col'=4] {'col'}, dimensions={0}, use_global_device_ids=true | all-gather | bytes 81920 | tf_op jit(solution)/shard_map/all_gather | solution.py:295
  224.1 35.0 %all_gather.23.gathered = bf16[1024,256]{1,0:T(8,128)(2,1)S(1)} all-gather(bf16[128,256]{1,0:T(8,128)(2,1)S(1)} %all_gather.22), channel_id=1, replica_groups=mesh['row'=8,'col'=4] {'row'}, dimensions={0}, use_global_device_ids=true | all-gather | bytes 589824 | tf_op jit(solution)/shard_map/all_gather | solution.py:296
  260.2 1.3 collective-permute-start.36
  261.5 1.3 collective-permute-start.37
  262.8 1.3 collective-permute-start.38
  265.4 2.2 collective-permute-done.37.r1
  268.6 1.4 last_update.1
  (65 shorter events, 30.4 us)
Async XLA Ops:
  16.1 10.0 %collective-permute-start = (bf16[128,256]{1,0:T(8,128)(2,1)S(1)}, bf16[128,256]{1,0:T(8,128)(2,1)S(1)}, u32[]{:S(2)}, u32[]{:S(2)}) collective-permute-start(bf16[128,256]{1,0:T(8,128)(2,1)S(1)} %get-tuple-element.68), channel_id=1, source_target_pairs={{0,4},{4,8},{8,12},{12,16},{16,20},{20,24},{24,28},{1,5},{5,9},{9,... | collective-permute-start | bytes 196616 | tf_op jit(solution)/shard_map/ppermute | solution.py:203
  18.4 7.7 %collective-permute-start.1 = (bf16[128,256]{1,0:T(8,128)(2,1)S(1)}, bf16[128,256]{1,0:T(8,128)(2,1)S(1)}, u32[]{:S(2)}, u32[]{:S(2)}) collective-permute-start(bf16[128,256]{1,0:T(8,128)(2,1)S(1)} %get-tuple-element.69), channel_id=1, source_target_pairs={{4,0},{8,4},{12,8},{16,12},{20,16},{24,20},{28,24},{5,1},{9,5},{13... | collective-permute-start | bytes 196616 | tf_op jit(solution)/shard_map/ppermute | solution.py:203
  19.7 6.4 %collective-permute-start.2 = (bf16[128,256]{1,0:T(8,128)(2,1)S(1)}, bf16[128,256]{1,0:T(8,128)(2,1)S(1)}, u32[]{:S(2)}, u32[]{:S(2)}) collective-permute-start(bf16[128,256]{1,0:T(8,128)(2,1)S(1)} %get-tuple-element.70), channel_id=1, source_target_pairs={{0,1},{1,2},{2,3},{4,5},{5,6},{6,7},{8,9},{9,10},{10,11},{12,13},{... | collective-permute-start | bytes 196616 | tf_op jit(solution)/shard_map/ppermute | solution.py:203
  21.0 5.1 %collective-permute-start.3 = (bf16[128,256]{1,0:T(8,128)(2,1)S(1)}, bf16[128,256]{1,0:T(8,128)(2,1)S(1)}, u32[]{:S(2)}, u32[]{:S(2)}) collective-permute-start(bf16[128,256]{1,0:T(8,128)(2,1)S(1)} %get-tuple-element.71), channel_id=1, source_target_pairs={{1,0},{2,1},{3,2},{5,4},{6,5},{7,6},{9,8},{10,9},{11,10},{13,12},{... | collective-permute-start | bytes 196616 | tf_op jit(solution)/shard_map/ppermute | solution.py:203
  22.3 3.8 %copy-start = (bf16[1,1,1536,32]{2,3,1,0:T(8,128)(2,1)S(1)}, bf16[1,1,1536,32]{2,3,1,0:T(8,128)(2,1)}, u32[]{:S(2)}) copy-start(bf16[1,1,1536,32]{2,3,1,0:T(8,128)(2,1)} %param.10) | copy-start | bytes 294916
  67.0 5.6 %collective-permute-start.4 = (bf16[128,256]{1,0:T(8,128)(2,1)S(1)}, bf16[128,256]{1,0:T(8,128)(2,1)S(1)}, u32[]{:S(2)}, u32[]{:S(2)}) collective-permute-start(bf16[128,256]{1,0:T(8,128)(2,1)S(1)} %get-tuple-element.76), channel_id=1, source_target_pairs={{0,4},{4,8},{8,12},{12,16},{16,20},{20,24},{24,28},{1,5},{5,9},{9,... | collective-permute-start | bytes 196616 | tf_op jit(solution)/shard_map/ppermute | solution.py:203
  68.7 6.2 %collective-permute-start.5 = (bf16[128,256]{1,0:T(8,128)(2,1)S(1)}, bf16[128,256]{1,0:T(8,128)(2,1)S(1)}, u32[]{:S(2)}, u32[]{:S(2)}) collective-permute-start(bf16[128,256]{1,0:T(8,128)(2,1)S(1)} %get-tuple-element.77), channel_id=1, source_target_pairs={{4,0},{8,4},{12,8},{16,12},{20,16},{24,20},{28,24},{5,1},{9,5},{13... | collective-permute-start | bytes 196616 | tf_op jit(solution)/shard_map/ppermute | solution.py:203
  70.0 4.9 %collective-permute-start.6 = (bf16[128,256]{1,0:T(8,128)(2,1)S(1)}, bf16[128,256]{1,0:T(8,128)(2,1)S(1)}, u32[]{:S(2)}, u32[]{:S(2)}) collective-permute-start(bf16[128,256]{1,0:T(8,128)(2,1)S(1)} %get-tuple-element.78), channel_id=1, source_target_pairs={{0,1},{1,2},{2,3},{4,5},{5,6},{6,7},{8,9},{9,10},{10,11},{12,13},{... | collective-permute-start | bytes 196616 | tf_op jit(solution)/shard_map/ppermute | solution.py:203
  71.3 5.4 %collective-permute-start.7 = (bf16[128,256]{1,0:T(8,128)(2,1)S(1)}, bf16[128,256]{1,0:T(8,128)(2,1)S(1)}, u32[]{:S(2)}, u32[]{:S(2)}) collective-permute-start(bf16[128,256]{1,0:T(8,128)(2,1)S(1)} %get-tuple-element.79), channel_id=1, source_target_pairs={{1,0},{2,1},{3,2},{5,4},{6,5},{7,6},{9,8},{10,9},{11,10},{13,12},{... | collective-permute-start | bytes 196616 | tf_op jit(solution)/shard_map/ppermute | solution.py:203
  78.1 15.4 %collective-permute-start.8 = (bf16[128,256]{1,0:T(8,128)(2,1)S(1)}, bf16[128,256]{1,0:T(8,128)(2,1)S(1)}, u32[]{:S(2)}, u32[]{:S(2)}) collective-permute-start(bf16[128,256]{1,0:T(8,128)(2,1)S(1)} %get-tuple-element.85), channel_id=1, source_target_pairs={{0,4},{4,8},{8,12},{12,16},{16,20},{20,24},{24,28},{1,5},{5,9},{9,... | collective-permute-start | bytes 196616 | tf_op jit(solution)/shard_map/ppermute | solution.py:203
  82.7 10.9 %collective-permute-start.9 = (bf16[128,256]{1,0:T(8,128)(2,1)S(1)}, bf16[128,256]{1,0:T(8,128)(2,1)S(1)}, u32[]{:S(2)}, u32[]{:S(2)}) collective-permute-start(bf16[128,256]{1,0:T(8,128)(2,1)S(1)} %get-tuple-element.86), channel_id=1, source_target_pairs={{4,0},{8,4},{12,8},{16,12},{20,16},{24,20},{28,24},{5,1},{9,5},{13... | collective-permute-start | bytes 196616 | tf_op jit(solution)/shard_map/ppermute | solution.py:203
  84.0 9.6 %collective-permute-start.10 = (bf16[128,256]{1,0:T(8,128)(2,1)S(1)}, bf16[128,256]{1,0:T(8,128)(2,1)S(1)}, u32[]{:S(2)}, u32[]{:S(2)}) collective-permute-start(bf16[128,256]{1,0:T(8,128)(2,1)S(1)} %get-tuple-element.87), channel_id=1, source_target_pairs={{0,1},{1,2},{2,3},{4,5},{5,6},{6,7},{8,9},{9,10},{10,11},{12,13},{... | collective-permute-start | bytes 196616 | tf_op jit(solution)/shard_map/ppermute | solution.py:203
  88.6 5.0 %collective-permute-start.11 = (bf16[128,256]{1,0:T(8,128)(2,1)S(1)}, bf16[128,256]{1,0:T(8,128)(2,1)S(1)}, u32[]{:S(2)}, u32[]{:S(2)}) collective-permute-start(bf16[128,256]{1,0:T(8,128)(2,1)S(1)} %get-tuple-element.88), channel_id=1, source_target_pairs={{1,0},{2,1},{3,2},{5,4},{6,5},{7,6},{9,8},{10,9},{11,10},{13,12},{... | collective-permute-start | bytes 196616 | tf_op jit(solution)/shard_map/ppermute | solution.py:203
  93.9 10.1 %collective-permute-start.12 = (bf16[128,256]{1,0:T(8,128)(2,1)S(1)}, bf16[128,256]{1,0:T(8,128)(2,1)S(1)}, u32[]{:S(2)}, u32[]{:S(2)}) collective-permute-start(bf16[128,256]{1,0:T(8,128)(2,1)S(1)} %get-tuple-element.89), channel_id=1, source_target_pairs={{0,4},{4,8},{8,12},{12,16},{16,20},{20,24},{24,28},{1,5},{5,9},{9,... | collective-permute-start | bytes 196616 | tf_op jit(solution)/shard_map/ppermute | solution.py:203
  98.2 6.9 %collective-permute-start.13 = (bf16[128,256]{1,0:T(8,128)(2,1)S(1)}, bf16[128,256]{1,0:T(8,128)(2,1)S(1)}, u32[]{:S(2)}, u32[]{:S(2)}) collective-permute-start(bf16[128,256]{1,0:T(8,128)(2,1)S(1)} %get-tuple-element.90), channel_id=1, source_target_pairs={{4,0},{8,4},{12,8},{16,12},{20,16},{24,20},{28,24},{5,1},{9,5},{13... | collective-permute-start | bytes 196616 | tf_op jit(solution)/shard_map/ppermute | solution.py:203
  99.5 5.6 %collective-permute-start.14 = (bf16[128,256]{1,0:T(8,128)(2,1)S(1)}, bf16[128,256]{1,0:T(8,128)(2,1)S(1)}, u32[]{:S(2)}, u32[]{:S(2)}) collective-permute-start(bf16[128,256]{1,0:T(8,128)(2,1)S(1)} %get-tuple-element.91), channel_id=1, source_target_pairs={{0,1},{1,2},{2,3},{4,5},{5,6},{6,7},{8,9},{9,10},{10,11},{12,13},{... | collective-permute-start | bytes 196616 | tf_op jit(solution)/shard_map/ppermute | solution.py:203
  102.3 4.7 %collective-permute-start.15 = (bf16[128,256]{1,0:T(8,128)(2,1)S(1)}, bf16[128,256]{1,0:T(8,128)(2,1)S(1)}, u32[]{:S(2)}, u32[]{:S(2)}) collective-permute-start(bf16[128,256]{1,0:T(8,128)(2,1)S(1)} %get-tuple-element.92), channel_id=1, source_target_pairs={{1,0},{2,1},{3,2},{5,4},{6,5},{7,6},{9,8},{10,9},{11,10},{13,12},{... | collective-permute-start | bytes 196616 | tf_op jit(solution)/shard_map/ppermute | solution.py:203
  108.2 13.0 %collective-permute-start.16 = (bf16[128,256]{1,0:T(8,128)(2,1)S(1)}, bf16[128,256]{1,0:T(8,128)(2,1)S(1)}, u32[]{:S(2)}, u32[]{:S(2)}) collective-permute-start(bf16[128,256]{1,0:T(8,128)(2,1)S(1)} %get-tuple-element.94), channel_id=1, source_target_pairs={{0,4},{4,8},{8,12},{12,16},{16,20},{20,24},{24,28},{1,5},{5,9},{9,... | collective-permute-start | bytes 196616 | tf_op jit(solution)/shard_map/ppermute | solution.py:203
  113.0 8.2 %collective-permute-start.17 = (bf16[128,256]{1,0:T(8,128)(2,1)S(1)}, bf16[128,256]{1,0:T(8,128)(2,1)S(1)}, u32[]{:S(2)}, u32[]{:S(2)}) collective-permute-start(bf16[128,256]{1,0:T(8,128)(2,1)S(1)} %get-tuple-element.95), channel_id=1, source_target_pairs={{4,0},{8,4},{12,8},{16,12},{20,16},{24,20},{28,24},{5,1},{9,5},{13... | collective-permute-start | bytes 196616 | tf_op jit(solution)/shard_map/ppermute | solution.py:203
  114.3 6.9 %collective-permute-start.18 = (bf16[128,256]{1,0:T(8,128)(2,1)S(1)}, bf16[128,256]{1,0:T(8,128)(2,1)S(1)}, u32[]{:S(2)}, u32[]{:S(2)}) collective-permute-start(bf16[128,256]{1,0:T(8,128)(2,1)S(1)} %get-tuple-element.96), channel_id=1, source_target_pairs={{0,1},{1,2},{2,3},{4,5},{5,6},{6,7},{8,9},{9,10},{10,11},{12,13},{... | collective-permute-start | bytes 196616 | tf_op jit(solution)/shard_map/ppermute | solution.py:203
  118.9 3.1 %collective-permute-start.19 = (bf16[128,256]{1,0:T(8,128)(2,1)S(1)}, bf16[128,256]{1,0:T(8,128)(2,1)S(1)}, u32[]{:S(2)}, u32[]{:S(2)}) collective-permute-start(bf16[128,256]{1,0:T(8,128)(2,1)S(1)} %get-tuple-element.97), channel_id=1, source_target_pairs={{1,0},{2,1},{3,2},{5,4},{6,5},{7,6},{9,8},{10,9},{11,10},{13,12},{... | collective-permute-start | bytes 196616 | tf_op jit(solution)/shard_map/ppermute | solution.py:203
  165.0 5.2 %collective-permute-start.20 = (bf16[128,256]{1,0:T(8,128)(2,1)S(1)}, bf16[128,256]{1,0:T(8,128)(2,1)S(1)}, u32[]{:S(2)}, u32[]{:S(2)}) collective-permute-start(bf16[128,256]{1,0:T(8,128)(2,1)S(1)} %get-tuple-element.99), channel_id=1, source_target_pairs={{0,4},{4,8},{8,12},{12,16},{16,20},{20,24},{24,28},{1,5},{5,9},{9,... | collective-permute-start | bytes 196616 | tf_op jit(solution)/shard_map/ppermute | solution.py:203
  166.3 6.2 %collective-permute-start.21 = (bf16[128,256]{1,0:T(8,128)(2,1)S(1)}, bf16[128,256]{1,0:T(8,128)(2,1)S(1)}, u32[]{:S(2)}, u32[]{:S(2)}) collective-permute-start(bf16[128,256]{1,0:T(8,128)(2,1)S(1)} %get-tuple-element.100), channel_id=1, source_target_pairs={{4,0},{8,4},{12,8},{16,12},{20,16},{24,20},{28,24},{5,1},{9,5},{13... | collective-permute-start | bytes 196616 | tf_op jit(solution)/shard_map/ppermute | solution.py:203
  167.6 4.9 %collective-permute-start.22 = (bf16[128,256]{1,0:T(8,128)(2,1)S(1)}, bf16[128,256]{1,0:T(8,128)(2,1)S(1)}, u32[]{:S(2)}, u32[]{:S(2)}) collective-permute-start(bf16[128,256]{1,0:T(8,128)(2,1)S(1)} %get-tuple-element.101), channel_id=1, source_target_pairs={{0,1},{1,2},{2,3},{4,5},{5,6},{6,7},{8,9},{9,10},{10,11},{12,13},{... | collective-permute-start | bytes 196616 | tf_op jit(solution)/shard_map/ppermute | solution.py:203
  168.9 4.5 %collective-permute-start.23 = (bf16[128,256]{1,0:T(8,128)(2,1)S(1)}, bf16[128,256]{1,0:T(8,128)(2,1)S(1)}, u32[]{:S(2)}, u32[]{:S(2)}) collective-permute-start(bf16[128,256]{1,0:T(8,128)(2,1)S(1)} %get-tuple-element.102), channel_id=1, source_target_pairs={{1,0},{2,1},{3,2},{5,4},{6,5},{7,6},{9,8},{10,9},{11,10},{13,12},{... | collective-permute-start | bytes 196616 | tf_op jit(solution)/shard_map/ppermute | solution.py:203
  174.8 12.9 %collective-permute-start.24 = (bf16[128,256]{1,0:T(8,128)(2,1)S(1)}, bf16[128,256]{1,0:T(8,128)(2,1)S(1)}, u32[]{:S(2)}, u32[]{:S(2)}) collective-permute-start(bf16[128,256]{1,0:T(8,128)(2,1)S(1)} %get-tuple-element.105), channel_id=1, source_target_pairs={{0,4},{4,8},{8,12},{12,16},{16,20},{20,24},{24,28},{1,5},{5,9},{9,... | collective-permute-start | bytes 196616 | tf_op jit(solution)/shard_map/ppermute | solution.py:203
  179.4 8.4 %collective-permute-start.25 = (bf16[128,256]{1,0:T(8,128)(2,1)S(1)}, bf16[128,256]{1,0:T(8,128)(2,1)S(1)}, u32[]{:S(2)}, u32[]{:S(2)}) collective-permute-start(bf16[128,256]{1,0:T(8,128)(2,1)S(1)} %get-tuple-element.106), channel_id=1, source_target_pairs={{4,0},{8,4},{12,8},{16,12},{20,16},{24,20},{28,24},{5,1},{9,5},{13... | collective-permute-start | bytes 196616 | tf_op jit(solution)/shard_map/ppermute | solution.py:203
  180.7 7.1 %collective-permute-start.26 = (bf16[128,256]{1,0:T(8,128)(2,1)S(1)}, bf16[128,256]{1,0:T(8,128)(2,1)S(1)}, u32[]{:S(2)}, u32[]{:S(2)}) collective-permute-start(bf16[128,256]{1,0:T(8,128)(2,1)S(1)} %get-tuple-element.107), channel_id=1, source_target_pairs={{0,1},{1,2},{2,3},{4,5},{5,6},{6,7},{8,9},{9,10},{10,11},{12,13},{... | collective-permute-start | bytes 196616 | tf_op jit(solution)/shard_map/ppermute | solution.py:203
  185.3 3.1 %collective-permute-start.27 = (bf16[128,256]{1,0:T(8,128)(2,1)S(1)}, bf16[128,256]{1,0:T(8,128)(2,1)S(1)}, u32[]{:S(2)}, u32[]{:S(2)}) collective-permute-start(bf16[128,256]{1,0:T(8,128)(2,1)S(1)} %get-tuple-element.108), channel_id=1, source_target_pairs={{1,0},{2,1},{3,2},{5,4},{6,5},{7,6},{9,8},{10,9},{11,10},{13,12},{... | collective-permute-start | bytes 196616 | tf_op jit(solution)/shard_map/ppermute | solution.py:203
  188.7 11.9 %collective-permute-start.28 = (bf16[128,256]{1,0:T(8,128)(2,1)S(1)}, bf16[128,256]{1,0:T(8,128)(2,1)S(1)}, u32[]{:S(2)}, u32[]{:S(2)}) collective-permute-start(bf16[128,256]{1,0:T(8,128)(2,1)S(1)} %get-tuple-element.109), channel_id=1, source_target_pairs={{0,4},{4,8},{8,12},{12,16},{16,20},{20,24},{24,28},{1,5},{5,9},{9,... | collective-permute-start | bytes 196616 | tf_op jit(solution)/shard_map/ppermute | solution.py:203
  193.0 7.6 %collective-permute-start.29 = (bf16[128,256]{1,0:T(8,128)(2,1)S(1)}, bf16[128,256]{1,0:T(8,128)(2,1)S(1)}, u32[]{:S(2)}, u32[]{:S(2)}) collective-permute-start(bf16[128,256]{1,0:T(8,128)(2,1)S(1)} %get-tuple-element.110), channel_id=1, source_target_pairs={{4,0},{8,4},{12,8},{16,12},{20,16},{24,20},{28,24},{5,1},{9,5},{13... | collective-permute-start | bytes 196616 | tf_op jit(solution)/shard_map/ppermute | solution.py:203
  194.3 6.3 %collective-permute-start.30 = (bf16[128,256]{1,0:T(8,128)(2,1)S(1)}, bf16[128,256]{1,0:T(8,128)(2,1)S(1)}, u32[]{:S(2)}, u32[]{:S(2)}) collective-permute-start(bf16[128,256]{1,0:T(8,128)(2,1)S(1)} %get-tuple-element.111), channel_id=1, source_target_pairs={{0,1},{1,2},{2,3},{4,5},{5,6},{6,7},{8,9},{9,10},{10,11},{12,13},{... | collective-permute-start | bytes 196616 | tf_op jit(solution)/shard_map/ppermute | solution.py:203
  198.9 3.1 %collective-permute-start.31 = (bf16[128,256]{1,0:T(8,128)(2,1)S(1)}, bf16[128,256]{1,0:T(8,128)(2,1)S(1)}, u32[]{:S(2)}, u32[]{:S(2)}) collective-permute-start(bf16[128,256]{1,0:T(8,128)(2,1)S(1)} %get-tuple-element.112), channel_id=1, source_target_pairs={{1,0},{2,1},{3,2},{5,4},{6,5},{7,6},{9,8},{10,9},{11,10},{13,12},{... | collective-permute-start | bytes 196616 | tf_op jit(solution)/shard_map/ppermute | solution.py:203
  203.3 13.1 %collective-permute-start.32 = (bf16[128,256]{1,0:T(8,128)(2,1)S(1)}, bf16[128,256]{1,0:T(8,128)(2,1)S(1)}, u32[]{:S(2)}, u32[]{:S(2)}) collective-permute-start(bf16[128,256]{1,0:T(8,128)(2,1)S(1)} %get-tuple-element.114), channel_id=1, source_target_pairs={{0,4},{4,8},{8,12},{12,16},{16,20},{20,24},{24,28},{1,5},{5,9},{9,... | collective-permute-start | bytes 196616 | tf_op jit(solution)/shard_map/ppermute | solution.py:203
  208.5 7.9 %collective-permute-start.33 = (bf16[128,256]{1,0:T(8,128)(2,1)S(1)}, bf16[128,256]{1,0:T(8,128)(2,1)S(1)}, u32[]{:S(2)}, u32[]{:S(2)}) collective-permute-start(bf16[128,256]{1,0:T(8,128)(2,1)S(1)} %get-tuple-element.115), channel_id=1, source_target_pairs={{4,0},{8,4},{12,8},{16,12},{20,16},{24,20},{28,24},{5,1},{9,5},{13... | collective-permute-start | bytes 196616 | tf_op jit(solution)/shard_map/ppermute | solution.py:203
  209.8 6.6 %collective-permute-start.34 = (bf16[128,256]{1,0:T(8,128)(2,1)S(1)}, bf16[128,256]{1,0:T(8,128)(2,1)S(1)}, u32[]{:S(2)}, u32[]{:S(2)}) collective-permute-start(bf16[128,256]{1,0:T(8,128)(2,1)S(1)} %get-tuple-element.116), channel_id=1, source_target_pairs={{0,1},{1,2},{2,3},{4,5},{5,6},{6,7},{8,9},{9,10},{10,11},{12,13},{... | collective-permute-start | bytes 196616 | tf_op jit(solution)/shard_map/ppermute | solution.py:203
  214.1 3.1 %collective-permute-start.35 = (bf16[128,256]{1,0:T(8,128)(2,1)S(1)}, bf16[128,256]{1,0:T(8,128)(2,1)S(1)}, u32[]{:S(2)}, u32[]{:S(2)}) collective-permute-start(bf16[128,256]{1,0:T(8,128)(2,1)S(1)} %get-tuple-element.117), channel_id=1, source_target_pairs={{1,0},{2,1},{3,2},{5,4},{6,5},{7,6},{9,8},{10,9},{11,10},{13,12},{... | collective-permute-start | bytes 196616 | tf_op jit(solution)/shard_map/ppermute | solution.py:203
  260.2 5.2 %collective-permute-start.36 = (bf16[128,256]{1,0:T(8,128)(2,1)S(1)}, bf16[128,256]{1,0:T(8,128)(2,1)S(1)}, u32[]{:S(2)}, u32[]{:S(2)}) collective-permute-start(bf16[128,256]{1,0:T(8,128)(2,1)S(1)} %get-tuple-element.119), channel_id=1, source_target_pairs={{0,4},{4,8},{8,12},{12,16},{16,20},{20,24},{24,28},{1,5},{5,9},{9,... | collective-permute-start | bytes 196616 | tf_op jit(solution)/shard_map/ppermute | solution.py:203
  261.5 6.2 %collective-permute-start.37 = (bf16[128,256]{1,0:T(8,128)(2,1)S(1)}, bf16[128,256]{1,0:T(8,128)(2,1)S(1)}, u32[]{:S(2)}, u32[]{:S(2)}) collective-permute-start(bf16[128,256]{1,0:T(8,128)(2,1)S(1)} %get-tuple-element.120), channel_id=1, source_target_pairs={{4,0},{8,4},{12,8},{16,12},{20,16},{24,20},{28,24},{5,1},{9,5},{13... | collective-permute-start | bytes 196616 | tf_op jit(solution)/shard_map/ppermute | solution.py:203
  262.8 4.9 %collective-permute-start.38 = (bf16[128,256]{1,0:T(8,128)(2,1)S(1)}, bf16[128,256]{1,0:T(8,128)(2,1)S(1)}, u32[]{:S(2)}, u32[]{:S(2)}) collective-permute-start(bf16[128,256]{1,0:T(8,128)(2,1)S(1)} %get-tuple-element.121), channel_id=1, source_target_pairs={{0,1},{1,2},{2,3},{4,5},{5,6},{6,7},{8,9},{9,10},{10,11},{12,13},{... | collective-permute-start | bytes 196616 | tf_op jit(solution)/shard_map/ppermute | solution.py:203
  264.1 4.6 %collective-permute-start.39 = (bf16[128,256]{1,0:T(8,128)(2,1)S(1)}, bf16[128,256]{1,0:T(8,128)(2,1)S(1)}, u32[]{:S(2)}, u32[]{:S(2)}) collective-permute-start(bf16[128,256]{1,0:T(8,128)(2,1)S(1)} %get-tuple-element.122), channel_id=1, source_target_pairs={{1,0},{2,1},{3,2},{5,4},{6,5},{7,6},{9,8},{10,9},{11,10},{13,12},{... | collective-permute-start | bytes 196616 | tf_op jit(solution)/shard_map/ppermute | solution.py:203

commit v4 on v2

--- a/solution.py
+++ b/solution.py
@@ -37,8 +37,8 @@
     )(*distant, *near)
 
 
-def select_kernel(far_target, far_rows, far_counts, target, half, pick, spread, *rest):
-    *tiles, rows, counts, sems = rest
+def select_kernel(far_target, far_rows, far_counts, half, pick, spread, *rest):
+    *tiles, target, rows, counts, sems = rest
     own = target.shape[0]
     tile = rows.shape[1]
     loads = [
@@ -82,26 +82,35 @@
         out[at, :] = product(matrix[at, :own], owned[...])
 
 
+def load_kernel(far, near, sems):
+    pieces = sems.shape[0]
+    height = far.shape[0] // pieces
+    loads = []
+    for i in range(pieces):
+        at = slice(i * height, (i + 1) * height)
+        loads.append(pltpu.make_async_copy(far.at[at], near.at[at], sems.at[i]))
+        loads[-1].start()
+    for load in loads:
+        load.wait()
+
+
 def own_columns_kernel(matrix, owned, out):
     own = owned.shape[0]
     out[...] = product(matrix[:, :own], owned[...])
 
 
-def restrict_kernel(basis, owned, g0, g1, g2, g3, out):
-    own, tile = owned.shape[0], g0.shape[0]
-    total = product(basis[:, :own], owned[...])
-    for d, ghost in enumerate((g0, g1, g2, g3)):
-        total += product(basis[:, own + d * tile : own + (d + 1) * tile], ghost[...])
-    out[...] = total.astype(HALF)
-
-
 def stacked(g0, g1, g2, g3):
     return jnp.concatenate([g0[...], g1[...], g2[...], g3[...]], axis=0)
 
 
-def margin_columns_kernel(matrix, partial, g0, g1, g2, g3, out):
-    own = matrix.shape[1] - 4 * g0.shape[0]
-    out[...] = partial[...] + product(matrix[:, own:], stacked(g0, g1, g2, g3))
+def solve_kernel(matrix, partial, basis, owned, g0, g1, g2, g3, restricted, rim, inner):
+    own = owned.shape[0]
+    ghosts = stacked(g0, g1, g2, g3)
+    total = product(basis[:, :own], owned[...]) + product(basis[:, own:], ghosts)
+    for i in range(restricted.shape[0]):
+        restricted[i, :, :] = total.astype(HALF)
+    rim[...] = partial[own:, :] + product(matrix[own:, own:], ghosts)
+    inner[...] = partial[:own, :] + product(matrix[:own, own:], ghosts)
 
 
 def partial_kernel(inverse, gathered, out):
@@ -109,16 +118,17 @@
         out[i, :, :] = product(inverse[i, :, :], gathered[...]).astype(HALF)
 
 
-def coarse_kernel(parts, basis, local, level, *tiles):
+def coarse_kernel(parts, basis, rim, level, *tiles):
     tile = tiles[0].shape[0]
-    own = local.shape[0] - 4 * tile
+    own = basis.shape[1] - 4 * tile
     total = parts[0, :, :].astype(FULL)
     for i in range(1, parts.shape[0]):
         total += parts[i, :, :].astype(FULL)
     level[...] = total.astype(HALF)
     for d in range(4):
-        at = slice(own + d * tile, own + (d + 1) * tile)
-        tiles[d][...] = (local[at, :] + turned_product(basis[:, at], level[...])).astype(HALF)
+        here = slice(d * tile, (d + 1) * tile)
+        there = slice(own + d * tile, own + (d + 1) * tile)
+        tiles[d][...] = (rim[here, :] + turned_product(basis[:, there], level[...])).astype(HALF)
 
 
 def rim_kernel(matrix, partial, g0, g1, g2, g3, *tiles):
@@ -142,7 +152,7 @@
         local, level, basis, pick, spread, r0, r1, r2, r3, after, half, *tiles = refs
         own = after.shape[0]
         update = (
-            local[:own, :]
+            local[...]
             + turned_product(basis[:, :own], level[...])
             + product(spread[...], stacked(r0, r1, r2, r3))
         )
@@ -174,31 +184,29 @@
         store.wait()
 
 
-def residual_kernel(target, image, pick, spread, r0, r1, r2, r3, half, *tiles):
+def residual_kernel(far, image, pick, spread, r0, r1, r2, r3, half, *rest):
+    *tiles, target, sem = rest
     tile = tiles[0].shape[0]
-    half[...] = (
-        target[...] - (image[...] + product(spread[...], stacked(r0, r1, r2, r3)))
-    ).astype(HALF)
+    load = pltpu.make_async_copy(far, target, sem)
+    load.start()
+    image_sum = image[...] + product(spread[...], stacked(r0, r1, r2, r3))
+    load.wait()
+    half[...] = (target[...] - image_sum).astype(HALF)
     for d in range(4):
         tiles[d][...] = product(pick[d * tile : (d + 1) * tile, :], half[...]).astype(HALF)
 
 
-def own_product(matrix, owned, arriving, name):
-    local = matrix.shape[0]
-    out = ((local, owned.shape[1]), FULL)
-    flops = 2 * local * owned.size
-    if arriving:
-        return call(
-            resident_kernel,
-            name,
-            [(matrix.shape, HALF), out],
-            matrix,
-            owned,
-            far=1,
-            scratch=(pltpu.SemaphoreType.DMA((6,)),),
-            flops=flops,
-        )
-    return matrix, call(own_columns_kernel, name, [out], matrix, owned, flops=flops)[0]
+def brought(matrix, tiles, name):
+    matrix, tiles = lax.optimization_barrier((matrix, tuple(tiles)))
+    (near,) = call(
+        load_kernel,
+        name,
+        [(matrix.shape, HALF)],
+        matrix,
+        far=1,
+        scratch=(pltpu.SemaphoreType.DMA((8,)),),
+    )
+    return near, tiles
 
 
 def passed_along(shard, axis, by):
@@ -230,18 +238,22 @@
     margin = 4 * tile
     coarse = basis.shape[0]
     groups = coarse_inverse.shape[0]
+    across = lax.axis_size("col")
+
     four_tiles = [((tile, columns), HALF)] * 4
     owned_half = ((own, columns), HALF)
-    target, residual, pick, spread, *tiles = call(
+    owned_full = ((own, columns), FULL)
+    local_full = ((local, columns), FULL)
+    residual, pick, spread, *tiles = call(
         select_kernel,
         "select",
-        [((own, columns), FULL), owned_half, ((margin, own), HALF), ((own, margin), HALF)]
-        + four_tiles,
+        [owned_half, ((margin, own), HALF), ((own, margin), HALF)] + four_tiles,
         target,
         rows_list,
         send_count[0],
         far=3,
         scratch=(
+            pltpu.VMEM((own, columns), FULL),
             pltpu.VMEM(rows_list.shape, jnp.int32),
             pltpu.SMEM((1, 4), jnp.int32),
             pltpu.SemaphoreType.DMA((3,)),
@@ -252,22 +264,30 @@
     for sweep in range(ITERS):
         if sweep:
             ghosts = traded(tiles)
-            operator, partial = own_product(operator, solution_half, sweep == 1, "operator_own")
+            (partial,) = call(
+                own_columns_kernel,
+                "operator_own",
+                [local_full],
+                near_operator,
+                solution_half,
+                flops=2 * local * own * columns,
+            )
             tiles = call(
                 rim_kernel,
                 "operator_rim",
                 four_tiles,
-                operator,
+                near_operator,
                 partial,
                 *ghosts,
                 flops=2 * margin * margin * columns,
             )
+            near_inverse, tiles = brought(inverse, tiles, "inverse_load")
             returned = traded(tiles)
             (image,) = call(
                 inner_kernel,
                 "operator_inner",
-                [((own, columns), FULL)],
-                operator,
+                [owned_full],
+                near_operator,
                 partial,
                 *ghosts,
                 flops=2 * own * margin * columns,
@@ -281,47 +301,63 @@
                 pick,
                 spread,
                 *returned,
+                far=1,
+                scratch=(pltpu.VMEM((own, columns), FULL), pltpu.SemaphoreType.DMA),
                 flops=4 * margin * own * columns,
             )
-        ghosts = traded(tiles)
-        inverse, partial = own_product(inverse, residual, sweep == 0, "inverse_own")
-        (restricted,) = call(
-            restrict_kernel,
-            "restrict",
-            [((coarse, columns), HALF)],
+            ghosts = traded(tiles)
+            (partial,) = call(
+                own_columns_kernel,
+                "inverse_own",
+                [local_full],
+                near_inverse,
+                residual,
+                flops=2 * local * own * columns,
+            )
+        else:
+            ghosts = traded(tiles)
+            near_inverse, partial = call(
+                resident_kernel,
+                "inverse_own",
+                [(inverse.shape, HALF), local_full],
+                inverse,
+                residual,
+                far=1,
+                scratch=(pltpu.SemaphoreType.DMA((6,)),),
+                flops=2 * local * own * columns,
+            )
+        restricted, rim, inner = call(
+            solve_kernel,
+            "inverse_margin",
+            [((across, coarse, columns), HALF), ((margin, columns), FULL), owned_full],
+            near_inverse,
+            partial,
             basis,
             residual,
             *ghosts,
-            flops=2 * local * coarse * columns,
-        )
-        gathered = lax.all_gather(restricted, "col", axis=0, tiled=True)
+            flops=2 * local * (margin + coarse) * columns,
+        )
+        gathered = lax.all_to_all(restricted, "col", 0, 0, tiled=True)
         (parts,) = call(
             partial_kernel,
             "coarse_part",
             [((groups, coarse, columns), HALF)],
             coarse_inverse,
-            gathered,
+            gathered.reshape(across * coarse, columns),
             flops=2 * coarse_inverse.size * columns,
         )
         parts = lax.all_to_all(parts, "row", 0, 0, tiled=True)
-        (correction,) = call(
-            margin_columns_kernel,
-            "inverse_margin",
-            [((local, columns), FULL)],
-            inverse,
-            partial,
-            *ghosts,
-            flops=2 * local * margin * columns,
-        )
         level, *tiles = call(
             coarse_kernel,
             "coarse",
             [((coarse, columns), HALF)] + four_tiles,
             parts,
             basis,
-            correction,
+            rim,
             flops=2 * coarse * margin * columns,
         )
+        if sweep < ITERS - 1:
+            near_operator, tiles = brought(operator, tiles, "operator_load")
         returned = traded(tiles)
         if sweep == ITERS - 1:
             break
@@ -329,9 +365,9 @@
         solution, solution_half, *tiles = call(
             update_kernel(not sweep),
             "update",
-            [((own, columns), FULL), owned_half] + four_tiles,
+            [owned_full, owned_half] + four_tiles,
             *before,
-            correction,
+            inner,
             level,
             basis,
             pick,
@@ -342,9 +378,9 @@
     (solution,) = call(
         last_update_kernel,
         "last_update",
-        [((own, columns), FULL)],
+        [owned_full],
         solution,
-        correction,
+        inner,
         level,
         basis,
         spread,

time: 219 us -> 210 us (0.959)
  blocking collectives: 12.3 us -> 40.1 us
  local copies, waits for them, and re-layouts: 17.2 us -> 0.01 us
  starting transfers between devices: 132 us -> 118 us
  waiting for transfers between devices: 29 us -> 18.1 us
  Pallas kernels: 26.1 us -> 32.1 us
    all_to_all x0 -> x6, blocking collectives: none -> 40.1 us  [the longest x3 24 us: per_device(): parts = lax.all_to_all(parts, 'row', 0, 0, tiled=True)]
    unnamed x38 -> x4, local copies, waits for them, and re-layouts: 17.2 us -> 0.01 us
    all_to_all x3 -> x0, starting transfers between devices: 13.5 us -> none  [per_device(): parts = lax.all_to_all(parts, 'row', 0, 0, tiled=True)]
    all_gather x3 -> x0, blocking collectives: 12.3 us -> none  [per_device(): gathered = lax.all_gather(restricted, 'col', axis=0, tiled=True)]
    ppermute x40, waiting for transfers between devices: 28.3 us -> 18.1 us  [passed_along(): return lax.ppermute(shard, axis, pairs)]
    pallas_call x27 -> x28, Pallas kernels: 26.1 us -> 32.1 us  [call(): pl.pallas_call(body, out_shape=tuple(((pltpu.HBM if away else pltpu.VMEM)...]
  transfers between devices with their start and end apart: 43 -> 40, of which waited for: 10 -> 9; matrix products, arithmetic and copies ran while one was open for 0% -> 0% of each run, Pallas kernels for 6% -> 9%
where the time goes in v4:
time: 210 us; the launch traced here: 209 us
  starting transfers between devices  118 us (56%)
  blocking collectives  40.1 us (19%)
  Pallas kernels  32.1 us (15%)
  waiting for transfers between devices  18.1 us (9%)
    ppermute x40, starting transfers between devices, passed_along(): return lax.ppermute(shard, axis, pairs)  118 us
    pallas_call x28, Pallas kernels, call(): pl.pallas_call(body, out_shape=tuple(((pltpu.HBM if away else pltpu.VMEM)...  32.1 us
    all_to_all x3, blocking collectives, per_device(): parts = lax.all_to_all(parts, 'row', 0, 0, tiled=True)  24 us
    ppermute x40, waiting for transfers between devices, passed_along(): return lax.ppermute(shard, axis, pairs)  18.1 us
    all_to_all x3, blocking collectives, per_device(): gathered = lax.all_to_all(restricted, 'col', 0, 0, tiled=True)  16.1 us
  transfers between devices with their start and end apart: 40, of which 9 were waited for; matrix products, arithmetic and copies ran while one was open for 0% of the time, Pallas kernels for 9%

profile of v4, /device:TPU:9, one launch (start us, length us, event | category | flops | bytes accessed | tf_op | source)
XLA Modules:
  0.0 208.9 jit_solution(15467668177826334239)
XLA Ops:
  0.0 1.9 select.1
  2.0 3.1 %collective-permute-start = (bf16[128,256]{1,0:T(8,128)(2,1)S(1)}, bf16[128,256]{1,0:T(8,128)(2,1)S(1)}, u32[]{:S(2)}, u32[]{:S(2)}) collective-permute-start(bf16[128,256]{1,0:T(8,128)(2,1)S(1)} %get-tuple-element.91), channel_id=1, source_target_pairs={{0,4},{4,8},{8,12},{12,16},{16,20},{20,24},{24,28},{1,5},{5,9},{9,... | collective-permute-start | bytes 196616 | tf_op jit(solution)/shard_map/ppermute | solution.py:215
  5.1 3.0 %collective-permute-start.1 = (bf16[128,256]{1,0:T(8,128)(2,1)S(1)}, bf16[128,256]{1,0:T(8,128)(2,1)S(1)}, u32[]{:S(2)}, u32[]{:S(2)}) collective-permute-start(bf16[128,256]{1,0:T(8,128)(2,1)S(1)} %get-tuple-element.92), channel_id=1, source_target_pairs={{4,0},{8,4},{12,8},{16,12},{20,16},{24,20},{28,24},{5,1},{9,5},{13... | collective-permute-start | bytes 196616 | tf_op jit(solution)/shard_map/ppermute | solution.py:215
  8.2 4.2 %collective-permute-start.2 = (bf16[128,256]{1,0:T(8,128)(2,1)S(1)}, bf16[128,256]{1,0:T(8,128)(2,1)S(1)}, u32[]{:S(2)}, u32[]{:S(2)}) collective-permute-start(bf16[128,256]{1,0:T(8,128)(2,1)S(1)} %get-tuple-element.93), channel_id=1, source_target_pairs={{0,1},{1,2},{2,3},{4,5},{5,6},{6,7},{8,9},{9,10},{10,11},{12,13},{... | collective-permute-start | bytes 196616 | tf_op jit(solution)/shard_map/ppermute | solution.py:215
  14.3 3.7 %inverse_own.3 = (bf16[1536,1536]{1,0:T(8,128)(2,1)S(1)}, f32[1536,256]{1,0:T(8,128)S(1)}) custom-call(bf16[1536,1536]{1,0:T(8,128)(2,1)} %bitcast.24, bf16[1024,256]{1,0:T(8,128)(2,1)S(1)} %get-tuple-element.88.owned), custom_call_target="tpu_custom_call" | custom-call | flops 805306368 | bytes 5242880 | tf_op jit(solution)/shard_map/inverse_own/pallas_call | solution.py:28
  18.8 6.5 %all_to_all.30 = bf16[4,32,256]{2,1,0:T(8,128)(2,1)S(1)} all-to-all(bf16[4,32,256]{2,1,0:T(8,128)(2,1)S(1)} %get-tuple-element.96), channel_id=1, replica_groups=mesh['row'=8,'col'=4] {'col'}, dimensions={0} | all-to-all | bytes 131072 | tf_op jit(solution)/shard_map/all_to_all | solution.py:340
  25.4 8.9 %all_to_all.31.parts = bf16[8,32,256]{2,1,0:T(8,128)(2,1)S(1)} all-to-all(bf16[8,32,256]{2,1,0:T(8,128)(2,1)S(1)} %coarse_part.3), channel_id=1, replica_groups=mesh['row'=8,'col'=4] {'row'}, dimensions={0} | all-to-all | bytes 262144 | tf_op jit(solution)/shard_map/all_to_all | solution.py:349
  34.6 3.3 %collective-permute-start.4 = (bf16[128,256]{1,0:T(8,128)(2,1)S(1)}, bf16[128,256]{1,0:T(8,128)(2,1)S(1)}, u32[]{:S(2)}, u32[]{:S(2)}) collective-permute-start(bf16[128,256]{1,0:T(8,128)(2,1)S(1)} %get-tuple-element.105), channel_id=1, source_target_pairs={{0,4},{4,8},{8,12},{12,16},{16,20},{20,24},{24,28},{1,5},{5,9},{9,... | collective-permute-start | bytes 196616 | tf_op jit(solution)/shard_map/ppermute | solution.py:215
  38.0 2.8 %collective-permute-start.5 = (bf16[128,256]{1,0:T(8,128)(2,1)S(1)}, bf16[128,256]{1,0:T(8,128)(2,1)S(1)}, u32[]{:S(2)}, u32[]{:S(2)}) collective-permute-start(bf16[128,256]{1,0:T(8,128)(2,1)S(1)} %get-tuple-element.106), channel_id=1, source_target_pairs={{4,0},{8,4},{12,8},{16,12},{20,16},{24,20},{28,24},{5,1},{9,5},{13... | collective-permute-start | bytes 196616 | tf_op jit(solution)/shard_map/ppermute | solution.py:215
  40.8 4.6 %collective-permute-start.6 = (bf16[128,256]{1,0:T(8,128)(2,1)S(1)}, bf16[128,256]{1,0:T(8,128)(2,1)S(1)}, u32[]{:S(2)}, u32[]{:S(2)}) collective-permute-start(bf16[128,256]{1,0:T(8,128)(2,1)S(1)} %get-tuple-element.107), channel_id=1, source_target_pairs={{0,1},{1,2},{2,3},{4,5},{5,6},{6,7},{8,9},{9,10},{10,11},{12,13},{... | collective-permute-start | bytes 196616 | tf_op jit(solution)/shard_map/ppermute | solution.py:215
  47.4 2.4 %operator_load.2.matrix = bf16[1536,1536]{1,0:T(8,128)(2,1)S(1)} custom-call(bf16[1536,1536]{1,0:T(8,128)(2,1)} %bitcast.27), custom_call_target="tpu_custom_call" | custom-call | bytes 4718592 | tf_op jit(solution)/shard_map/operator_load/pallas_call | solution.py:28
  52.5 2.1 collective-permute-start.8
  54.5 4.1 %collective-permute-start.9 = (bf16[128,256]{1,0:T(8,128)(2,1)S(1)}, bf16[128,256]{1,0:T(8,128)(2,1)S(1)}, u32[]{:S(2)}, u32[]{:S(2)}) collective-permute-start(bf16[128,256]{1,0:T(8,128)(2,1)S(1)} %get-tuple-element.113), channel_id=1, source_target_pairs={{4,0},{8,4},{12,8},{16,12},{20,16},{24,20},{28,24},{5,1},{9,5},{13... | collective-permute-start | bytes 196616 | tf_op jit(solution)/shard_map/ppermute | solution.py:215
  58.7 3.0 %collective-permute-start.10 = (bf16[128,256]{1,0:T(8,128)(2,1)S(1)}, bf16[128,256]{1,0:T(8,128)(2,1)S(1)}, u32[]{:S(2)}, u32[]{:S(2)}) collective-permute-start(bf16[128,256]{1,0:T(8,128)(2,1)S(1)} %get-tuple-element.114), channel_id=1, source_target_pairs={{0,1},{1,2},{2,3},{4,5},{5,6},{6,7},{8,9},{9,10},{10,11},{12,13},{... | collective-permute-start | bytes 196616 | tf_op jit(solution)/shard_map/ppermute | solution.py:215
  64.6 2.6 %collective-permute-done.11.g3 = bf16[128,256]{1,0:T(8,128)(2,1)S(1)} collective-permute-done((bf16[128,256]{1,0:T(8,128)(2,1)S(1)}, bf16[128,256]{1,0:T(8,128)(2,1)S(1)}, u32[]{:S(2)}, u32[]{:S(2)}) %collective-permute-start.11) | collective-permute-done | bytes 65568 | tf_op jit(solution)/shard_map/ppermute | solution.py:215
  69.5 4.3 %collective-permute-start.13 = (bf16[128,256]{1,0:T(8,128)(2,1)S(1)}, bf16[128,256]{1,0:T(8,128)(2,1)S(1)}, u32[]{:S(2)}, u32[]{:S(2)}) collective-permute-start(bf16[128,256]{1,0:T(8,128)(2,1)S(1)} %get-tuple-element.122), channel_id=1, source_target_pairs={{4,0},{8,4},{12,8},{16,12},{20,16},{24,20},{28,24},{5,1},{9,5},{13... | collective-permute-start | bytes 196616 | tf_op jit(solution)/shard_map/ppermute | solution.py:215
  73.7 2.4 %collective-permute-start.14 = (bf16[128,256]{1,0:T(8,128)(2,1)S(1)}, bf16[128,256]{1,0:T(8,128)(2,1)S(1)}, u32[]{:S(2)}, u32[]{:S(2)}) collective-permute-start(bf16[128,256]{1,0:T(8,128)(2,1)S(1)} %get-tuple-element.123), channel_id=1, source_target_pairs={{0,1},{1,2},{2,3},{4,5},{5,6},{6,7},{8,9},{9,10},{10,11},{12,13},{... | collective-permute-start | bytes 196616 | tf_op jit(solution)/shard_map/ppermute | solution.py:215
  76.2 1.9 collective-permute-start.15
  78.1 2.4 %inverse_load.2.matrix = bf16[1536,1536]{1,0:T(8,128)(2,1)S(1)} custom-call(bf16[1536,1536]{1,0:T(8,128)(2,1)} %bitcast.25), custom_call_target="tpu_custom_call" | custom-call | bytes 4718592 | tf_op jit(solution)/shard_map/inverse_load/pallas_call | solution.py:28
  81.8 2.0 residual.2
  85.7 4.3 %collective-permute-start.17 = (bf16[128,256]{1,0:T(8,128)(2,1)S(1)}, bf16[128,256]{1,0:T(8,128)(2,1)S(1)}, u32[]{:S(2)}, u32[]{:S(2)}) collective-permute-start(bf16[128,256]{1,0:T(8,128)(2,1)S(1)} %get-tuple-element.127), channel_id=1, source_target_pairs={{4,0},{8,4},{12,8},{16,12},{20,16},{24,20},{28,24},{5,1},{9,5},{13... | collective-permute-start | bytes 196616 | tf_op jit(solution)/shard_map/ppermute | solution.py:215
  90.0 3.4 %collective-permute-start.18 = (bf16[128,256]{1,0:T(8,128)(2,1)S(1)}, bf16[128,256]{1,0:T(8,128)(2,1)S(1)}, u32[]{:S(2)}, u32[]{:S(2)}) collective-permute-start(bf16[128,256]{1,0:T(8,128)(2,1)S(1)} %get-tuple-element.128), channel_id=1, source_target_pairs={{0,1},{1,2},{2,3},{4,5},{5,6},{6,7},{8,9},{9,10},{10,11},{12,13},{... | collective-permute-start | bytes 196616 | tf_op jit(solution)/shard_map/ppermute | solution.py:215
  93.4 1.9 collective-permute-start.19
  96.3 2.6 %collective-permute-done.19.g3 = bf16[128,256]{1,0:T(8,128)(2,1)S(1)} collective-permute-done((bf16[128,256]{1,0:T(8,128)(2,1)S(1)}, bf16[128,256]{1,0:T(8,128)(2,1)S(1)}, u32[]{:S(2)}, u32[]{:S(2)}) %collective-permute-start.19) | collective-permute-done | bytes 65568 | tf_op jit(solution)/shard_map/ppermute | solution.py:215
  99.6 4.8 %all_to_all.32 = bf16[4,32,256]{2,1,0:T(8,128)(2,1)S(1)} all-to-all(bf16[4,32,256]{2,1,0:T(8,128)(2,1)S(1)} %get-tuple-element.131), channel_id=1, replica_groups=mesh['row'=8,'col'=4] {'col'}, dimensions={0} | all-to-all | bytes 131072 | tf_op jit(solution)/shard_map/all_to_all | solution.py:340
  104.7 7.5 %all_to_all.33.parts = bf16[8,32,256]{2,1,0:T(8,128)(2,1)S(1)} all-to-all(bf16[8,32,256]{2,1,0:T(8,128)(2,1)S(1)} %coarse_part.4), channel_id=1, replica_groups=mesh['row'=8,'col'=4] {'row'}, dimensions={0} | all-to-all | bytes 262144 | tf_op jit(solution)/shard_map/all_to_all | solution.py:349
  112.4 3.4 %collective-permute-start.20 = (bf16[128,256]{1,0:T(8,128)(2,1)S(1)}, bf16[128,256]{1,0:T(8,128)(2,1)S(1)}, u32[]{:S(2)}, u32[]{:S(2)}) collective-permute-start(bf16[128,256]{1,0:T(8,128)(2,1)S(1)} %get-tuple-element.138), channel_id=1, source_target_pairs={{0,4},{4,8},{8,12},{12,16},{16,20},{20,24},{24,28},{1,5},{5,9},{9,... | collective-permute-start | bytes 196616 | tf_op jit(solution)/shard_map/ppermute | solution.py:215
  115.8 2.8 %collective-permute-start.21 = (bf16[128,256]{1,0:T(8,128)(2,1)S(1)}, bf16[128,256]{1,0:T(8,128)(2,1)S(1)}, u32[]{:S(2)}, u32[]{:S(2)}) collective-permute-start(bf16[128,256]{1,0:T(8,128)(2,1)S(1)} %get-tuple-element.139), channel_id=1, source_target_pairs={{4,0},{8,4},{12,8},{16,12},{20,16},{24,20},{28,24},{5,1},{9,5},{13... | collective-permute-start | bytes 196616 | tf_op jit(solution)/shard_map/ppermute | solution.py:215
  118.6 5.0 %collective-permute-start.22 = (bf16[128,256]{1,0:T(8,128)(2,1)S(1)}, bf16[128,256]{1,0:T(8,128)(2,1)S(1)}, u32[]{:S(2)}, u32[]{:S(2)}) collective-permute-start(bf16[128,256]{1,0:T(8,128)(2,1)S(1)} %get-tuple-element.140), channel_id=1, source_target_pairs={{0,1},{1,2},{2,3},{4,5},{5,6},{6,7},{8,9},{9,10},{10,11},{12,13},{... | collective-permute-start | bytes 196616 | tf_op jit(solution)/shard_map/ppermute | solution.py:215
  125.5 2.4 %operator_load.3.matrix = bf16[1536,1536]{1,0:T(8,128)(2,1)S(1)} custom-call(bf16[1536,1536]{1,0:T(8,128)(2,1)} %bitcast.28), custom_call_target="tpu_custom_call" | custom-call | bytes 4718592 | tf_op jit(solution)/shard_map/operator_load/pallas_call | solution.py:28
  130.6 2.0 collective-permute-start.24
  132.6 4.2 %collective-permute-start.25 = (bf16[128,256]{1,0:T(8,128)(2,1)S(1)}, bf16[128,256]{1,0:T(8,128)(2,1)S(1)}, u32[]{:S(2)}, u32[]{:S(2)}) collective-permute-start(bf16[128,256]{1,0:T(8,128)(2,1)S(1)} %get-tuple-element.146), channel_id=1, source_target_pairs={{4,0},{8,4},{12,8},{16,12},{20,16},{24,20},{28,24},{5,1},{9,5},{13... | collective-permute-start | bytes 196616 | tf_op jit(solution)/shard_map/ppermute | solution.py:215
  136.8 3.0 %collective-permute-start.26 = (bf16[128,256]{1,0:T(8,128)(2,1)S(1)}, bf16[128,256]{1,0:T(8,128)(2,1)S(1)}, u32[]{:S(2)}, u32[]{:S(2)}) collective-permute-start(bf16[128,256]{1,0:T(8,128)(2,1)S(1)} %get-tuple-element.147), channel_id=1, source_target_pairs={{0,1},{1,2},{2,3},{4,5},{5,6},{6,7},{8,9},{9,10},{10,11},{12,13},{... | collective-permute-start | bytes 196616 | tf_op jit(solution)/shard_map/ppermute | solution.py:215
  139.7 2.1 %collective-permute-start.27 = (bf16[128,256]{1,0:T(8,128)(2,1)S(1)}, bf16[128,256]{1,0:T(8,128)(2,1)S(1)}, u32[]{:S(2)}, u32[]{:S(2)}) collective-permute-start(bf16[128,256]{1,0:T(8,128)(2,1)S(1)} %get-tuple-element.148), channel_id=1, source_target_pairs={{1,0},{2,1},{3,2},{5,4},{6,5},{7,6},{9,8},{10,9},{11,10},{13,12},{... | collective-permute-start | bytes 196616 | tf_op jit(solution)/shard_map/ppermute | solution.py:215
  142.9 2.5 %collective-permute-done.27.g3 = bf16[128,256]{1,0:T(8,128)(2,1)S(1)} collective-permute-done((bf16[128,256]{1,0:T(8,128)(2,1)S(1)}, bf16[128,256]{1,0:T(8,128)(2,1)S(1)}, u32[]{:S(2)}, u32[]{:S(2)}) %collective-permute-start.27) | collective-permute-done | bytes 65568 | tf_op jit(solution)/shard_map/ppermute | solution.py:215
  147.6 4.3 %collective-permute-start.29 = (bf16[128,256]{1,0:T(8,128)(2,1)S(1)}, bf16[128,256]{1,0:T(8,128)(2,1)S(1)}, u32[]{:S(2)}, u32[]{:S(2)}) collective-permute-start(bf16[128,256]{1,0:T(8,128)(2,1)S(1)} %get-tuple-element.155), channel_id=1, source_target_pairs={{4,0},{8,4},{12,8},{16,12},{20,16},{24,20},{28,24},{5,1},{9,5},{13... | collective-permute-start | bytes 196616 | tf_op jit(solution)/shard_map/ppermute | solution.py:215
  151.8 2.4 %collective-permute-start.30 = (bf16[128,256]{1,0:T(8,128)(2,1)S(1)}, bf16[128,256]{1,0:T(8,128)(2,1)S(1)}, u32[]{:S(2)}, u32[]{:S(2)}) collective-permute-start(bf16[128,256]{1,0:T(8,128)(2,1)S(1)} %get-tuple-element.156), channel_id=1, source_target_pairs={{0,1},{1,2},{2,3},{4,5},{5,6},{6,7},{8,9},{9,10},{10,11},{12,13},{... | collective-permute-start | bytes 196616 | tf_op jit(solution)/shard_map/ppermute | solution.py:215
  156.2 2.4 %inverse_load.3.matrix = bf16[1536,1536]{1,0:T(8,128)(2,1)S(1)} custom-call(bf16[1536,1536]{1,0:T(8,128)(2,1)} %bitcast.26), custom_call_target="tpu_custom_call" | custom-call | bytes 4718592 | tf_op jit(solution)/shard_map/inverse_load/pallas_call | solution.py:28
  159.9 2.0 residual.3
  163.8 4.3 %collective-permute-start.33 = (bf16[128,256]{1,0:T(8,128)(2,1)S(1)}, bf16[128,256]{1,0:T(8,128)(2,1)S(1)}, u32[]{:S(2)}, u32[]{:S(2)}) collective-permute-start(bf16[128,256]{1,0:T(8,128)(2,1)S(1)} %get-tuple-element.160), channel_id=1, source_target_pairs={{4,0},{8,4},{12,8},{16,12},{20,16},{24,20},{28,24},{5,1},{9,5},{13... | collective-permute-start | bytes 196616 | tf_op jit(solution)/shard_map/ppermute | solution.py:215
  168.0 3.4 %collective-permute-start.34 = (bf16[128,256]{1,0:T(8,128)(2,1)S(1)}, bf16[128,256]{1,0:T(8,128)(2,1)S(1)}, u32[]{:S(2)}, u32[]{:S(2)}) collective-permute-start(bf16[128,256]{1,0:T(8,128)(2,1)S(1)} %get-tuple-element.161), channel_id=1, source_target_pairs={{0,1},{1,2},{2,3},{4,5},{5,6},{6,7},{8,9},{9,10},{10,11},{12,13},{... | collective-permute-start | bytes 196616 | tf_op jit(solution)/shard_map/ppermute | solution.py:215
  174.4 2.6 %collective-permute-done.35.g3 = bf16[128,256]{1,0:T(8,128)(2,1)S(1)} collective-permute-done((bf16[128,256]{1,0:T(8,128)(2,1)S(1)}, bf16[128,256]{1,0:T(8,128)(2,1)S(1)}, u32[]{:S(2)}, u32[]{:S(2)}) %collective-permute-start.35) | collective-permute-done | bytes 65568 | tf_op jit(solution)/shard_map/ppermute | solution.py:215
  177.7 4.8 %all_to_all.34 = bf16[4,32,256]{2,1,0:T(8,128)(2,1)S(1)} all-to-all(bf16[4,32,256]{2,1,0:T(8,128)(2,1)S(1)} %get-tuple-element.164), channel_id=1, replica_groups=mesh['row'=8,'col'=4] {'col'}, dimensions={0} | all-to-all | bytes 131072 | tf_op jit(solution)/shard_map/all_to_all | solution.py:340
  182.8 7.6 %all_to_all.35.parts = bf16[8,32,256]{2,1,0:T(8,128)(2,1)S(1)} all-to-all(bf16[8,32,256]{2,1,0:T(8,128)(2,1)S(1)} %coarse_part.5), channel_id=1, replica_groups=mesh['row'=8,'col'=4] {'row'}, dimensions={0} | all-to-all | bytes 262144 | tf_op jit(solution)/shard_map/all_to_all | solution.py:349
  190.6 3.4 %collective-permute-start.36 = (bf16[128,256]{1,0:T(8,128)(2,1)S(1)}, bf16[128,256]{1,0:T(8,128)(2,1)S(1)}, u32[]{:S(2)}, u32[]{:S(2)}) collective-permute-start(bf16[128,256]{1,0:T(8,128)(2,1)S(1)} %get-tuple-element.167), channel_id=1, source_target_pairs={{0,4},{4,8},{8,12},{12,16},{16,20},{20,24},{24,28},{1,5},{5,9},{9,... | collective-permute-start | bytes 196616 | tf_op jit(solution)/shard_map/ppermute | solution.py:215
  194.0 2.8 %collective-permute-start.37 = (bf16[128,256]{1,0:T(8,128)(2,1)S(1)}, bf16[128,256]{1,0:T(8,128)(2,1)S(1)}, u32[]{:S(2)}, u32[]{:S(2)}) collective-permute-start(bf16[128,256]{1,0:T(8,128)(2,1)S(1)} %get-tuple-element.168), channel_id=1, source_target_pairs={{4,0},{8,4},{12,8},{16,12},{20,16},{24,20},{28,24},{5,1},{9,5},{13... | collective-permute-start | bytes 196616 | tf_op jit(solution)/shard_map/ppermute | solution.py:215
  196.8 4.9 %collective-permute-start.38 = (bf16[128,256]{1,0:T(8,128)(2,1)S(1)}, bf16[128,256]{1,0:T(8,128)(2,1)S(1)}, u32[]{:S(2)}, u32[]{:S(2)}) collective-permute-start(bf16[128,256]{1,0:T(8,128)(2,1)S(1)} %get-tuple-element.169), channel_id=1, source_target_pairs={{0,1},{1,2},{2,3},{4,5},{5,6},{6,7},{8,9},{9,10},{10,11},{12,13},{... | collective-permute-start | bytes 196616 | tf_op jit(solution)/shard_map/ppermute | solution.py:215
  203.7 3.6 %collective-permute-done.39.r3 = bf16[128,256]{1,0:T(8,128)(2,1)S(1)} collective-permute-done((bf16[128,256]{1,0:T(8,128)(2,1)S(1)}, bf16[128,256]{1,0:T(8,128)(2,1)S(1)}, u32[]{:S(2)}, u32[]{:S(2)}) %collective-permute-start.39) | collective-permute-done | bytes 65568 | tf_op jit(solution)/shard_map/ppermute | solution.py:215
  (70 shorter events, 38.3 us)
Async XLA Ops:
  0.0 18.1 %copy-start = (bf16[1,1,1536,32]{2,3,1,0:T(8,128)(2,1)S(1)}, bf16[1,1,1536,32]{2,3,1,0:T(8,128)(2,1)}, u32[]{:S(2)}) copy-start(bf16[1,1,1536,32]{2,3,1,0:T(8,128)(2,1)} %param.10) | copy-start | bytes 294916
  2.0 16.1 %collective-permute-start = (bf16[128,256]{1,0:T(8,128)(2,1)S(1)}, bf16[128,256]{1,0:T(8,128)(2,1)S(1)}, u32[]{:S(2)}, u32[]{:S(2)}) collective-permute-start(bf16[128,256]{1,0:T(8,128)(2,1)S(1)} %get-tuple-element.91), channel_id=1, source_target_pairs={{0,4},{4,8},{8,12},{12,16},{16,20},{20,24},{24,28},{1,5},{5,9},{9,... | collective-permute-start | bytes 196616 | tf_op jit(solution)/shard_map/ppermute | solution.py:215
  5.1 13.0 %collective-permute-start.1 = (bf16[128,256]{1,0:T(8,128)(2,1)S(1)}, bf16[128,256]{1,0:T(8,128)(2,1)S(1)}, u32[]{:S(2)}, u32[]{:S(2)}) collective-permute-start(bf16[128,256]{1,0:T(8,128)(2,1)S(1)} %get-tuple-element.92), channel_id=1, source_target_pairs={{4,0},{8,4},{12,8},{16,12},{20,16},{24,20},{28,24},{5,1},{9,5},{13... | collective-permute-start | bytes 196616 | tf_op jit(solution)/shard_map/ppermute | solution.py:215
  8.2 9.9 %collective-permute-start.2 = (bf16[128,256]{1,0:T(8,128)(2,1)S(1)}, bf16[128,256]{1,0:T(8,128)(2,1)S(1)}, u32[]{:S(2)}, u32[]{:S(2)}) collective-permute-start(bf16[128,256]{1,0:T(8,128)(2,1)S(1)} %get-tuple-element.93), channel_id=1, source_target_pairs={{0,1},{1,2},{2,3},{4,5},{5,6},{6,7},{8,9},{9,10},{10,11},{12,13},{... | collective-permute-start | bytes 196616 | tf_op jit(solution)/shard_map/ppermute | solution.py:215
  12.4 5.7 %collective-permute-start.3 = (bf16[128,256]{1,0:T(8,128)(2,1)S(1)}, bf16[128,256]{1,0:T(8,128)(2,1)S(1)}, u32[]{:S(2)}, u32[]{:S(2)}) collective-permute-start(bf16[128,256]{1,0:T(8,128)(2,1)S(1)} %get-tuple-element.94), channel_id=1, source_target_pairs={{1,0},{2,1},{3,2},{5,4},{6,5},{7,6},{9,8},{10,9},{11,10},{13,12},{... | collective-permute-start | bytes 196616 | tf_op jit(solution)/shard_map/ppermute | solution.py:215
  18.0 7.2 %copy-start.1 = (bf16[8,32,128]{2,1,0:T(8,128)(2,1)S(1)}, bf16[8,32,128]{2,1,0:T(8,128)(2,1)}, u32[]{:S(2)}) copy-start(bf16[8,32,128]{2,1,0:T(8,128)(2,1)} %inverse.5) | copy-start | bytes 196612
  34.6 15.2 %collective-permute-start.4 = (bf16[128,256]{1,0:T(8,128)(2,1)S(1)}, bf16[128,256]{1,0:T(8,128)(2,1)S(1)}, u32[]{:S(2)}, u32[]{:S(2)}) collective-permute-start(bf16[128,256]{1,0:T(8,128)(2,1)S(1)} %get-tuple-element.105), channel_id=1, source_target_pairs={{0,4},{4,8},{8,12},{12,16},{16,20},{20,24},{24,28},{1,5},{5,9},{9,... | collective-permute-start | bytes 196616 | tf_op jit(solution)/shard_map/ppermute | solution.py:215
  38.0 11.8 %collective-permute-start.5 = (bf16[128,256]{1,0:T(8,128)(2,1)S(1)}, bf16[128,256]{1,0:T(8,128)(2,1)S(1)}, u32[]{:S(2)}, u32[]{:S(2)}) collective-permute-start(bf16[128,256]{1,0:T(8,128)(2,1)S(1)} %get-tuple-element.106), channel_id=1, source_target_pairs={{4,0},{8,4},{12,8},{16,12},{20,16},{24,20},{28,24},{5,1},{9,5},{13... | collective-permute-start | bytes 196616 | tf_op jit(solution)/shard_map/ppermute | solution.py:215
  40.8 9.0 %collective-permute-start.6 = (bf16[128,256]{1,0:T(8,128)(2,1)S(1)}, bf16[128,256]{1,0:T(8,128)(2,1)S(1)}, u32[]{:S(2)}, u32[]{:S(2)}) collective-permute-start(bf16[128,256]{1,0:T(8,128)(2,1)S(1)} %get-tuple-element.107), channel_id=1, source_target_pairs={{0,1},{1,2},{2,3},{4,5},{5,6},{6,7},{8,9},{9,10},{10,11},{12,13},{... | collective-permute-start | bytes 196616 | tf_op jit(solution)/shard_map/ppermute | solution.py:215
  45.5 5.6 %collective-permute-start.7 = (bf16[128,256]{1,0:T(8,128)(2,1)S(1)}, bf16[128,256]{1,0:T(8,128)(2,1)S(1)}, u32[]{:S(2)}, u32[]{:S(2)}) collective-permute-start(bf16[128,256]{1,0:T(8,128)(2,1)S(1)} %get-tuple-element.108), channel_id=1, source_target_pairs={{1,0},{2,1},{3,2},{5,4},{6,5},{7,6},{9,8},{10,9},{11,10},{13,12},{... | collective-permute-start | bytes 196616 | tf_op jit(solution)/shard_map/ppermute | solution.py:215
  52.5 12.1 %collective-permute-start.8 = (bf16[128,256]{1,0:T(8,128)(2,1)S(1)}, bf16[128,256]{1,0:T(8,128)(2,1)S(1)}, u32[]{:S(2)}, u32[]{:S(2)}) collective-permute-start(bf16[128,256]{1,0:T(8,128)(2,1)S(1)} %get-tuple-element.112), channel_id=1, source_target_pairs={{0,4},{4,8},{8,12},{12,16},{16,20},{20,24},{24,28},{1,5},{5,9},{9,... | collective-permute-start | bytes 196616 | tf_op jit(solution)/shard_map/ppermute | solution.py:215
  54.5 10.0 %collective-permute-start.9 = (bf16[128,256]{1,0:T(8,128)(2,1)S(1)}, bf16[128,256]{1,0:T(8,128)(2,1)S(1)}, u32[]{:S(2)}, u32[]{:S(2)}) collective-permute-start(bf16[128,256]{1,0:T(8,128)(2,1)S(1)} %get-tuple-element.113), channel_id=1, source_target_pairs={{4,0},{8,4},{12,8},{16,12},{20,16},{24,20},{28,24},{5,1},{9,5},{13... | collective-permute-start | bytes 196616 | tf_op jit(solution)/shard_map/ppermute | solution.py:215
  58.7 5.9 %collective-permute-start.10 = (bf16[128,256]{1,0:T(8,128)(2,1)S(1)}, bf16[128,256]{1,0:T(8,128)(2,1)S(1)}, u32[]{:S(2)}, u32[]{:S(2)}) collective-permute-start(bf16[128,256]{1,0:T(8,128)(2,1)S(1)} %get-tuple-element.114), channel_id=1, source_target_pairs={{0,1},{1,2},{2,3},{4,5},{5,6},{6,7},{8,9},{9,10},{10,11},{12,13},{... | collective-permute-start | bytes 196616 | tf_op jit(solution)/shard_map/ppermute | solution.py:215
  61.7 5.6 %collective-permute-start.11 = (bf16[128,256]{1,0:T(8,128)(2,1)S(1)}, bf16[128,256]{1,0:T(8,128)(2,1)S(1)}, u32[]{:S(2)}, u32[]{:S(2)}) collective-permute-start(bf16[128,256]{1,0:T(8,128)(2,1)S(1)} %get-tuple-element.115), channel_id=1, source_target_pairs={{1,0},{2,1},{3,2},{5,4},{6,5},{7,6},{9,8},{10,9},{11,10},{13,12},{... | collective-permute-start | bytes 196616 | tf_op jit(solution)/shard_map/ppermute | solution.py:215
  67.6 13.4 %collective-permute-start.12 = (bf16[128,256]{1,0:T(8,128)(2,1)S(1)}, bf16[128,256]{1,0:T(8,128)(2,1)S(1)}, u32[]{:S(2)}, u32[]{:S(2)}) collective-permute-start(bf16[128,256]{1,0:T(8,128)(2,1)S(1)} %get-tuple-element.121), channel_id=1, source_target_pairs={{0,4},{4,8},{8,12},{12,16},{16,20},{20,24},{24,28},{1,5},{5,9},{9,... | collective-permute-start | bytes 196616 | tf_op jit(solution)/shard_map/ppermute | solution.py:215
  69.5 11.5 %collective-permute-start.13 = (bf16[128,256]{1,0:T(8,128)(2,1)S(1)}, bf16[128,256]{1,0:T(8,128)(2,1)S(1)}, u32[]{:S(2)}, u32[]{:S(2)}) collective-permute-start(bf16[128,256]{1,0:T(8,128)(2,1)S(1)} %get-tuple-element.122), channel_id=1, source_target_pairs={{4,0},{8,4},{12,8},{16,12},{20,16},{24,20},{28,24},{5,1},{9,5},{13... | collective-permute-start | bytes 196616 | tf_op jit(solution)/shard_map/ppermute | solution.py:215
  73.7 7.2 %collective-permute-start.14 = (bf16[128,256]{1,0:T(8,128)(2,1)S(1)}, bf16[128,256]{1,0:T(8,128)(2,1)S(1)}, u32[]{:S(2)}, u32[]{:S(2)}) collective-permute-start(bf16[128,256]{1,0:T(8,128)(2,1)S(1)} %get-tuple-element.123), channel_id=1, source_target_pairs={{0,1},{1,2},{2,3},{4,5},{5,6},{6,7},{8,9},{9,10},{10,11},{12,13},{... | collective-permute-start | bytes 196616 | tf_op jit(solution)/shard_map/ppermute | solution.py:215
  76.2 5.6 %collective-permute-start.15 = (bf16[128,256]{1,0:T(8,128)(2,1)S(1)}, bf16[128,256]{1,0:T(8,128)(2,1)S(1)}, u32[]{:S(2)}, u32[]{:S(2)}) collective-permute-start(bf16[128,256]{1,0:T(8,128)(2,1)S(1)} %get-tuple-element.124), channel_id=1, source_target_pairs={{1,0},{2,1},{3,2},{5,4},{6,5},{7,6},{9,8},{10,9},{11,10},{13,12},{... | collective-permute-start | bytes 196616 | tf_op jit(solution)/shard_map/ppermute | solution.py:215
  83.8 12.5 %collective-permute-start.16 = (bf16[128,256]{1,0:T(8,128)(2,1)S(1)}, bf16[128,256]{1,0:T(8,128)(2,1)S(1)}, u32[]{:S(2)}, u32[]{:S(2)}) collective-permute-start(bf16[128,256]{1,0:T(8,128)(2,1)S(1)} %get-tuple-element.126), channel_id=1, source_target_pairs={{0,4},{4,8},{8,12},{12,16},{16,20},{20,24},{24,28},{1,5},{5,9},{9,... | collective-permute-start | bytes 196616 | tf_op jit(solution)/shard_map/ppermute | solution.py:215
  85.7 10.6 %collective-permute-start.17 = (bf16[128,256]{1,0:T(8,128)(2,1)S(1)}, bf16[128,256]{1,0:T(8,128)(2,1)S(1)}, u32[]{:S(2)}, u32[]{:S(2)}) collective-permute-start(bf16[128,256]{1,0:T(8,128)(2,1)S(1)} %get-tuple-element.127), channel_id=1, source_target_pairs={{4,0},{8,4},{12,8},{16,12},{20,16},{24,20},{28,24},{5,1},{9,5},{13... | collective-permute-start | bytes 196616 | tf_op jit(solution)/shard_map/ppermute | solution.py:215
  90.0 6.4 %collective-permute-start.18 = (bf16[128,256]{1,0:T(8,128)(2,1)S(1)}, bf16[128,256]{1,0:T(8,128)(2,1)S(1)}, u32[]{:S(2)}, u32[]{:S(2)}) collective-permute-start(bf16[128,256]{1,0:T(8,128)(2,1)S(1)} %get-tuple-element.128), channel_id=1, source_target_pairs={{0,1},{1,2},{2,3},{4,5},{5,6},{6,7},{8,9},{9,10},{10,11},{12,13},{... | collective-permute-start | bytes 196616 | tf_op jit(solution)/shard_map/ppermute | solution.py:215
  93.4 5.6 %collective-permute-start.19 = (bf16[128,256]{1,0:T(8,128)(2,1)S(1)}, bf16[128,256]{1,0:T(8,128)(2,1)S(1)}, u32[]{:S(2)}, u32[]{:S(2)}) collective-permute-start(bf16[128,256]{1,0:T(8,128)(2,1)S(1)} %get-tuple-element.129), channel_id=1, source_target_pairs={{1,0},{2,1},{3,2},{5,4},{6,5},{7,6},{9,8},{10,9},{11,10},{13,12},{... | collective-permute-start | bytes 196616 | tf_op jit(solution)/shard_map/ppermute | solution.py:215
  112.4 15.5 %collective-permute-start.20 = (bf16[128,256]{1,0:T(8,128)(2,1)S(1)}, bf16[128,256]{1,0:T(8,128)(2,1)S(1)}, u32[]{:S(2)}, u32[]{:S(2)}) collective-permute-start(bf16[128,256]{1,0:T(8,128)(2,1)S(1)} %get-tuple-element.138), channel_id=1, source_target_pairs={{0,4},{4,8},{8,12},{12,16},{16,20},{20,24},{24,28},{1,5},{5,9},{9,... | collective-permute-start | bytes 196616 | tf_op jit(solution)/shard_map/ppermute | solution.py:215
  115.8 12.1 %collective-permute-start.21 = (bf16[128,256]{1,0:T(8,128)(2,1)S(1)}, bf16[128,256]{1,0:T(8,128)(2,1)S(1)}, u32[]{:S(2)}, u32[]{:S(2)}) collective-permute-start(bf16[128,256]{1,0:T(8,128)(2,1)S(1)} %get-tuple-element.139), channel_id=1, source_target_pairs={{4,0},{8,4},{12,8},{16,12},{20,16},{24,20},{28,24},{5,1},{9,5},{13... | collective-permute-start | bytes 196616 | tf_op jit(solution)/shard_map/ppermute | solution.py:215
  118.6 9.3 %collective-permute-start.22 = (bf16[128,256]{1,0:T(8,128)(2,1)S(1)}, bf16[128,256]{1,0:T(8,128)(2,1)S(1)}, u32[]{:S(2)}, u32[]{:S(2)}) collective-permute-start(bf16[128,256]{1,0:T(8,128)(2,1)S(1)} %get-tuple-element.140), channel_id=1, source_target_pairs={{0,1},{1,2},{2,3},{4,5},{5,6},{6,7},{8,9},{9,10},{10,11},{12,13},{... | collective-permute-start | bytes 196616 | tf_op jit(solution)/shard_map/ppermute | solution.py:215
  123.6 5.6 %collective-permute-start.23 = (bf16[128,256]{1,0:T(8,128)(2,1)S(1)}, bf16[128,256]{1,0:T(8,128)(2,1)S(1)}, u32[]{:S(2)}, u32[]{:S(2)}) collective-permute-start(bf16[128,256]{1,0:T(8,128)(2,1)S(1)} %get-tuple-element.141), channel_id=1, source_target_pairs={{1,0},{2,1},{3,2},{5,4},{6,5},{7,6},{9,8},{10,9},{11,10},{13,12},{... | collective-permute-start | bytes 196616 | tf_op jit(solution)/shard_map/ppermute | solution.py:215
  130.6 12.3 %collective-permute-start.24 = (bf16[128,256]{1,0:T(8,128)(2,1)S(1)}, bf16[128,256]{1,0:T(8,128)(2,1)S(1)}, u32[]{:S(2)}, u32[]{:S(2)}) collective-permute-start(bf16[128,256]{1,0:T(8,128)(2,1)S(1)} %get-tuple-element.145), channel_id=1, source_target_pairs={{0,4},{4,8},{8,12},{12,16},{16,20},{20,24},{24,28},{1,5},{5,9},{9,... | collective-permute-start | bytes 196616 | tf_op jit(solution)/shard_map/ppermute | solution.py:215
  132.6 10.3 %collective-permute-start.25 = (bf16[128,256]{1,0:T(8,128)(2,1)S(1)}, bf16[128,256]{1,0:T(8,128)(2,1)S(1)}, u32[]{:S(2)}, u32[]{:S(2)}) collective-permute-start(bf16[128,256]{1,0:T(8,128)(2,1)S(1)} %get-tuple-element.146), channel_id=1, source_target_pairs={{4,0},{8,4},{12,8},{16,12},{20,16},{24,20},{28,24},{5,1},{9,5},{13... | collective-permute-start | bytes 196616 | tf_op jit(solution)/shard_map/ppermute | solution.py:215
  136.8 6.1 %collective-permute-start.26 = (bf16[128,256]{1,0:T(8,128)(2,1)S(1)}, bf16[128,256]{1,0:T(8,128)(2,1)S(1)}, u32[]{:S(2)}, u32[]{:S(2)}) collective-permute-start(bf16[128,256]{1,0:T(8,128)(2,1)S(1)} %get-tuple-element.147), channel_id=1, source_target_pairs={{0,1},{1,2},{2,3},{4,5},{5,6},{6,7},{8,9},{9,10},{10,11},{12,13},{... | collective-permute-start | bytes 196616 | tf_op jit(solution)/shard_map/ppermute | solution.py:215
  139.7 5.6 %collective-permute-start.27 = (bf16[128,256]{1,0:T(8,128)(2,1)S(1)}, bf16[128,256]{1,0:T(8,128)(2,1)S(1)}, u32[]{:S(2)}, u32[]{:S(2)}) collective-permute-start(bf16[128,256]{1,0:T(8,128)(2,1)S(1)} %get-tuple-element.148), channel_id=1, source_target_pairs={{1,0},{2,1},{3,2},{5,4},{6,5},{7,6},{9,8},{10,9},{11,10},{13,12},{... | collective-permute-start | bytes 196616 | tf_op jit(solution)/shard_map/ppermute | solution.py:215
  145.6 13.4 %collective-permute-start.28 = (bf16[128,256]{1,0:T(8,128)(2,1)S(1)}, bf16[128,256]{1,0:T(8,128)(2,1)S(1)}, u32[]{:S(2)}, u32[]{:S(2)}) collective-permute-start(bf16[128,256]{1,0:T(8,128)(2,1)S(1)} %get-tuple-element.154), channel_id=1, source_target_pairs={{0,4},{4,8},{8,12},{12,16},{16,20},{20,24},{24,28},{1,5},{5,9},{9,... | collective-permute-start | bytes 196616 | tf_op jit(solution)/shard_map/ppermute | solution.py:215
  147.6 11.5 %collective-permute-start.29 = (bf16[128,256]{1,0:T(8,128)(2,1)S(1)}, bf16[128,256]{1,0:T(8,128)(2,1)S(1)}, u32[]{:S(2)}, u32[]{:S(2)}) collective-permute-start(bf16[128,256]{1,0:T(8,128)(2,1)S(1)} %get-tuple-element.155), channel_id=1, source_target_pairs={{4,0},{8,4},{12,8},{16,12},{20,16},{24,20},{28,24},{5,1},{9,5},{13... | collective-permute-start | bytes 196616 | tf_op jit(solution)/shard_map/ppermute | solution.py:215
  151.8 7.2 %collective-permute-start.30 = (bf16[128,256]{1,0:T(8,128)(2,1)S(1)}, bf16[128,256]{1,0:T(8,128)(2,1)S(1)}, u32[]{:S(2)}, u32[]{:S(2)}) collective-permute-start(bf16[128,256]{1,0:T(8,128)(2,1)S(1)} %get-tuple-element.156), channel_id=1, source_target_pairs={{0,1},{1,2},{2,3},{4,5},{5,6},{6,7},{8,9},{9,10},{10,11},{12,13},{... | collective-permute-start | bytes 196616 | tf_op jit(solution)/shard_map/ppermute | solution.py:215
  154.3 5.6 %collective-permute-start.31 = (bf16[128,256]{1,0:T(8,128)(2,1)S(1)}, bf16[128,256]{1,0:T(8,128)(2,1)S(1)}, u32[]{:S(2)}, u32[]{:S(2)}) collective-permute-start(bf16[128,256]{1,0:T(8,128)(2,1)S(1)} %get-tuple-element.157), channel_id=1, source_target_pairs={{1,0},{2,1},{3,2},{5,4},{6,5},{7,6},{9,8},{10,9},{11,10},{13,12},{... | collective-permute-start | bytes 196616 | tf_op jit(solution)/shard_map/ppermute | solution.py:215
  161.8 12.5 %collective-permute-start.32 = (bf16[128,256]{1,0:T(8,128)(2,1)S(1)}, bf16[128,256]{1,0:T(8,128)(2,1)S(1)}, u32[]{:S(2)}, u32[]{:S(2)}) collective-permute-start(bf16[128,256]{1,0:T(8,128)(2,1)S(1)} %get-tuple-element.159), channel_id=1, source_target_pairs={{0,4},{4,8},{8,12},{12,16},{16,20},{20,24},{24,28},{1,5},{5,9},{9,... | collective-permute-start | bytes 196616 | tf_op jit(solution)/shard_map/ppermute | solution.py:215
  163.8 10.6 %collective-permute-start.33 = (bf16[128,256]{1,0:T(8,128)(2,1)S(1)}, bf16[128,256]{1,0:T(8,128)(2,1)S(1)}, u32[]{:S(2)}, u32[]{:S(2)}) collective-permute-start(bf16[128,256]{1,0:T(8,128)(2,1)S(1)} %get-tuple-element.160), channel_id=1, source_target_pairs={{4,0},{8,4},{12,8},{16,12},{20,16},{24,20},{28,24},{5,1},{9,5},{13... | collective-permute-start | bytes 196616 | tf_op jit(solution)/shard_map/ppermute | solution.py:215
  168.0 6.4 %collective-permute-start.34 = (bf16[128,256]{1,0:T(8,128)(2,1)S(1)}, bf16[128,256]{1,0:T(8,128)(2,1)S(1)}, u32[]{:S(2)}, u32[]{:S(2)}) collective-permute-start(bf16[128,256]{1,0:T(8,128)(2,1)S(1)} %get-tuple-element.161), channel_id=1, source_target_pairs={{0,1},{1,2},{2,3},{4,5},{5,6},{6,7},{8,9},{9,10},{10,11},{12,13},{... | collective-permute-start | bytes 196616 | tf_op jit(solution)/shard_map/ppermute | solution.py:215
  171.5 5.6 %collective-permute-start.35 = (bf16[128,256]{1,0:T(8,128)(2,1)S(1)}, bf16[128,256]{1,0:T(8,128)(2,1)S(1)}, u32[]{:S(2)}, u32[]{:S(2)}) collective-permute-start(bf16[128,256]{1,0:T(8,128)(2,1)S(1)} %get-tuple-element.162), channel_id=1, source_target_pairs={{1,0},{2,1},{3,2},{5,4},{6,5},{7,6},{9,8},{10,9},{11,10},{13,12},{... | collective-permute-start | bytes 196616 | tf_op jit(solution)/shard_map/ppermute | solution.py:215
  190.6 13.1 %collective-permute-start.36 = (bf16[128,256]{1,0:T(8,128)(2,1)S(1)}, bf16[128,256]{1,0:T(8,128)(2,1)S(1)}, u32[]{:S(2)}, u32[]{:S(2)}) collective-permute-start(bf16[128,256]{1,0:T(8,128)(2,1)S(1)} %get-tuple-element.167), channel_id=1, source_target_pairs={{0,4},{4,8},{8,12},{12,16},{16,20},{20,24},{24,28},{1,5},{5,9},{9,... | collective-permute-start | bytes 196616 | tf_op jit(solution)/shard_map/ppermute | solution.py:215
  194.0 9.7 %collective-permute-start.37 = (bf16[128,256]{1,0:T(8,128)(2,1)S(1)}, bf16[128,256]{1,0:T(8,128)(2,1)S(1)}, u32[]{:S(2)}, u32[]{:S(2)}) collective-permute-start(bf16[128,256]{1,0:T(8,128)(2,1)S(1)} %get-tuple-element.168), channel_id=1, source_target_pairs={{4,0},{8,4},{12,8},{16,12},{20,16},{24,20},{28,24},{5,1},{9,5},{13... | collective-permute-start | bytes 196616 | tf_op jit(solution)/shard_map/ppermute | solution.py:215
  196.8 6.9 %collective-permute-start.38 = (bf16[128,256]{1,0:T(8,128)(2,1)S(1)}, bf16[128,256]{1,0:T(8,128)(2,1)S(1)}, u32[]{:S(2)}, u32[]{:S(2)}) collective-permute-start(bf16[128,256]{1,0:T(8,128)(2,1)S(1)} %get-tuple-element.169), channel_id=1, source_target_pairs={{0,1},{1,2},{2,3},{4,5},{5,6},{6,7},{8,9},{9,10},{10,11},{12,13},{... | collective-permute-start | bytes 196616 | tf_op jit(solution)/shard_map/ppermute | solution.py:215
  201.8 5.6 %collective-permute-start.39 = (bf16[128,256]{1,0:T(8,128)(2,1)S(1)}, bf16[128,256]{1,0:T(8,128)(2,1)S(1)}, u32[]{:S(2)}, u32[]{:S(2)}) collective-permute-start(bf16[128,256]{1,0:T(8,128)(2,1)S(1)} %get-tuple-element.170), channel_id=1, source_target_pairs={{1,0},{2,1},{3,2},{5,4},{6,5},{7,6},{9,8},{10,9},{11,10},{13,12},{... | collective-permute-start | bytes 196616 | tf_op jit(solution)/shard_map/ppermute | solution.py:215

commit v5 on v4

v5 whole, which is shorter than its diff:
```python
import jax
import jax.numpy as jnp
from jax import lax
from jax.experimental import pallas as pl
from jax.experimental.pallas import tpu as pltpu
from jax.sharding import PartitionSpec as P

ITERS = 3
DAMPING = 0.5
HALF = jnp.bfloat16
FULL = jnp.float32


def product(left, right):
    return jnp.dot(left, right, preferred_element_type=FULL)


def turned_product(left, right):
    return lax.dot_general(left, right, (((0,), (0,)), ((), ())), preferred_element_type=FULL)


def call(body, name, outs, *args, far=0, away=False, scratch=(), flops=0):
    here = pl.BlockSpec(memory_space=pltpu.VMEM)
    there = pl.BlockSpec(memory_space=pltpu.HBM)
    size = sum(a.size * a.dtype.itemsize for a in args)
    distant = [pltpu.with_memory_space_constraint(a, pltpu.HBM) for a in args[:far]]
    near = [pltpu.with_memory_space_constraint(a, pltpu.VMEM) for a in args[far:]]
    return pl.pallas_call(
        body,
        out_shape=tuple((pltpu.HBM if away else pltpu.VMEM)(*out) for out in outs),
        in_specs=[there] * far + [here] * len(near),
        out_specs=tuple(there if away else here for _ in outs),
        scratch_shapes=list(scratch),
        compiler_params=pltpu.CompilerParams(vmem_limit_bytes=24 * 1024 * 1024),
        cost_estimate=pl.CostEstimate(flops=flops, bytes_accessed=size, transcendentals=0),
        name=name,
    )(*distant, *near)


def select_kernel(
    far_target, far_rows, far_counts, far_inverse, target, half, pick, masked, inverse, *rest
):
    *tiles, rows, counts, sems = rest
    own = target.shape[0]
    tile = rows.shape[1]
    pairs = [(far_rows, rows), (far_counts, counts), (far_target, target)]
    pieces = sems.shape[0] - len(pairs)
    height = inverse.shape[0] // pieces
    for i in range(pieces):
        at = slice(i * height, (i + 1) * height)
        pairs.append((far_inverse.at[at], inverse.at[at]))
    loads = [
        pltpu.make_async_copy(far, near, sems.at[i]) for i, (far, near) in enumerate(pairs)
    ]
    for load in loads:
        load.start()
    loads[0].wait()
    loads[1].wait()
    for d in range(4):
        here = jnp.where(
            lax.broadcasted_iota(jnp.int32, (1, tile), 1) < counts[0, d], rows[d : d + 1, :], -1
        )
        masked[d : d + 1, :] = here
        down = jnp.transpose(jnp.broadcast_to(here, (tile, tile)))[:, :1]
        pick[d * tile : (d + 1) * tile, :] = (
            lax.broadcasted_iota(jnp.int32, (tile, own), 1) == down
        ).astype(FULL).astype(HALF)
    loads[2].wait()
    half[...] = target[...].astype(HALF)
    picked(pick, half, tiles)
    for load in loads[3:]:
        load.wait()


def picked(pick, half, tiles):
    tile = tiles[0].shape[0]
    for d in range(4):
        tiles[d][...] = product(pick[d * tile : (d + 1) * tile, :], half[...]).astype(HALF)


def spread_kernel(masked, spread):
    own = spread.shape[0]
    tile = masked.shape[1]
    for d in range(4):
        wide = jnp.broadcast_to(masked[d : d + 1, :], (own, tile))
        spread[:, d * tile : (d + 1) * tile] = (
            lax.broadcasted_iota(jnp.int32, (own, tile), 0) == wide
        ).astype(FULL).astype(HALF)


def load_kernel(far, near, sems):
    pieces = sems.shape[0]
    height = far.shape[0] // pieces
    loads = []
    for i in range(pieces):
        at = slice(i * height, (i + 1) * height)
        loads.append(pltpu.make_async_copy(far.at[at], near.at[at], sems.at[i]))
        loads[-1].start()
    for load in loads:
        load.wait()


def stacked(*parts):
    return jnp.concatenate([part[...] for part in parts], axis=0)


def own_columns_kernel(matrix, owned, out):
    own = owned.shape[0]
    out[...] = product(matrix[:, :own], owned[...])


def near_columns_kernel(matrix, owned, g0, g1, out):
    own = owned.shape[0]
    split = own + 2 * g0.shape[0]
    out[...] = product(matrix[:, :own], owned[...]) + product(matrix[:, own:split], stacked(g0, g1))


def share_kernel(basis, owned, t2, t3, g0, g1, out):
    own, tile, coarse = owned.shape[0], t2.shape[0], basis.shape[0]
    split = own + 2 * tile
    out[:tile, :] = t2[...]
    out[tile : 2 * tile, :] = t3[...]
    out[2 * tile : 2 * tile + coarse, :] = (
        product(basis[:, :own], owned[...]) + product(basis[:, own:split], stacked(g0, g1))
    ).astype(HALF)
    if out.shape[0] > 2 * tile + coarse:
        out[2 * tile + coarse :, : 2 * tile] = basis[:, split:]


def solve_kernel(first, across):
    def body(*refs):
        refs = list(refs)
        rims = None if first else refs.pop(0)
        matrix, partial, gathered, inverse, g0, g1, parts, rim, inner, *rest = refs
        tile, coarse = g0.shape[0], inverse.shape[1]
        own = inner.shape[0]
        stride = gathered.shape[0] // across
        if first:
            (rims,) = rest
            for b in range(across):
                at = b * stride + 2 * tile + coarse
                rims[b * coarse : (b + 1) * coarse, :] = gathered[at : at + coarse, : 2 * tile]
        restricted = []
        for b in range(across):
            here = slice(b * coarse, (b + 1) * coarse)
            at = b * stride + 2 * tile
            total = gathered[at : at + coarse, :].astype(FULL)
            if b > 0:
                at = (b - 1) * stride + tile
                total += product(rims[here, :tile], gathered[at : at + tile, :])
            if b < across - 1:
                at = (b + 1) * stride
                total += product(rims[here, tile:], gathered[at : at + tile, :])
            restricted.append(total.astype(HALF))
        restricted = jnp.concatenate(restricted, axis=0)
        for i in range(parts.shape[0]):
            parts[i, :, :] = product(inverse[i, :, :], restricted).astype(HALF)
        me = lax.axis_index("col")
        at = pl.multiple_of(jnp.maximum(me - 1, 0) * stride + tile, 32)
        lower = gathered[pl.ds(at, tile), :]
        at = pl.multiple_of(jnp.minimum(me + 1, across - 1) * stride, 32)
        upper = gathered[pl.ds(at, tile), :]
        lower = jnp.where(me > 0, lower, jnp.zeros_like(lower))
        upper = jnp.where(me < across - 1, upper, jnp.zeros_like(upper))
        ghosts = jnp.concatenate([g0[...], g1[...], lower, upper], axis=0)
        rim[...] = partial[own:, :] + product(matrix[own:, own:], ghosts)
        inner[...] = partial[:own, :] + product(matrix[:own, own:], ghosts)

    return body


def coarse_kernel(parts, basis, rim, level, *tiles):
    tile = tiles[0].shape[0]
    own = basis.shape[1] - 4 * tile
    total = parts[0, :, :].astype(FULL)
    for i in range(1, parts.shape[0]):
        total += parts[i, :, :].astype(FULL)
    level[...] = total.astype(HALF)
    for d in range(4):
        here = slice(d * tile, (d + 1) * tile)
        there = slice(own + d * tile, own + (d + 1) * tile)
        tiles[d][...] = (rim[here, :] + turned_product(basis[:, there], level[...])).astype(HALF)


def base_kernel(first):
    def body(*refs):
        refs = list(refs)
        before = None if first else refs.pop(0)
        inner, level, basis, spread, r0, r1, out = refs
        own, tile = out.shape[0], r0.shape[0]
        update = (
            inner[...]
            + turned_product(basis[:, :own], level[...])
            + product(spread[:, : 2 * tile], stacked(r0, r1))
        )
        out[...] = DAMPING * update if first else before[...] + DAMPING * update

    return body


def update_kernel(base, pick, spread, r2, r3, after, half, *tiles):
    tile = r2.shape[0]
    after[...] = base[...] + DAMPING * product(spread[:, 2 * tile :], stacked(r2, r3))
    half[...] = after[...].astype(HALF)
    picked(pick, half, tiles)


def last_update_kernel(base, spread, r2, r3, far, after, sems):
    tile = r2.shape[0]
    pieces = sems.shape[0]
    height = after.shape[0] // pieces
    returned = stacked(r2, r3)
    stores = []
    for i in range(pieces):
        at = slice(i * height, (i + 1) * height)
        after[at, :] = base[at, :] + DAMPING * product(spread[at, 2 * tile :], returned)
        stores.append(pltpu.make_async_copy(after.at[at], far.at[at], sems.at[i]))
        stores[-1].start()
    for store in stores:
        store.wait()


def rim_kernel(matrix, partial, g2, g3, *tiles):
    tile = g2.shape[0]
    own = matrix.shape[1] - 4 * tile
    ghosts = stacked(g2, g3)
    for d in range(4):
        at = slice(own + d * tile, own + (d + 1) * tile)
        tiles[d][...] = (partial[at, :] + product(matrix[at, own + 2 * tile :], ghosts)).astype(HALF)


def remainder_kernel(target, matrix, partial, g2, g3, spread, r0, r1, out):
    own, tile = target.shape[0], g2.shape[0]
    image = (
        partial[:own, :]
        + product(matrix[:own, own + 2 * tile :], stacked(g2, g3))
        + product(spread[:, : 2 * tile], stacked(r0, r1))
    )
    out[...] = target[...] - image


def residual_kernel(remainder, pick, spread, r2, r3, half, *tiles):
    tile = r2.shape[0]
    half[...] = (remainder[...] - product(spread[:, 2 * tile :], stacked(r2, r3))).astype(HALF)
    picked(pick, half, tiles)


def brought(matrix, tiles, name):
    matrix, tiles = lax.optimization_barrier((matrix, tuple(tiles)))
    (near,) = call(
        load_kernel,
        name,
        [(matrix.shape, HALF)],
        matrix,
        far=1,
        scratch=(pltpu.SemaphoreType.DMA((8,)),),
    )
    return near, tiles


def passed_along(shard, axis, by):
    devices = lax.axis_size(axis)
    pairs = [(i, i + by) for i in range(devices) if 0 <= i + by < devices]
    return lax.ppermute(shard, axis, pairs)


def traded_over_row(tiles):
    return passed_along(tiles[1], "row", 1), passed_along(tiles[0], "row", -1)


def traded(tiles):
    return (
        *traded_over_row(tiles),
        passed_along(tiles[3], "col", 1),
        passed_along(tiles[2], "col", -1),
    )


def per_device(
    right_side, local_operator, local_inverse, coarse_basis, coarse_inverse, send_rows, send_count
):
    target = right_side[0, 0]
    operator = local_operator[0, 0]
    inverse = local_inverse[0, 0]
    basis = jnp.swapaxes(coarse_basis[0, 0], 0, 1)
    rows_list = send_rows[0, 0]
    own, columns = target.shape
    local = operator.shape[0]
    tile = rows_list.shape[1]
    margin = 4 * tile
    coarse = basis.shape[0]
    groups = coarse_inverse.shape[0]
    across = lax.axis_size("col")

    four_tiles = [((tile, columns), HALF)] * 4
    owned_half = ((own, columns), HALF)
    owned_full = ((own, columns), FULL)
    local_full = ((local, columns), FULL)
    target, residual, pick, masked, inverse, *tiles = call(
        select_kernel,
        "select",
        [
            owned_full,
            owned_half,
            ((margin, own), HALF),
            (rows_list.shape, jnp.int32),
            (inverse.shape, HALF),
        ]
        + four_tiles,
        target,
        rows_list,
        send_count[0],
        inverse,
        far=4,
        scratch=(
            pltpu.VMEM(rows_list.shape, jnp.int32),
            pltpu.SMEM((1, 4), jnp.int32),
            pltpu.SemaphoreType.DMA((3 + 8,)),
        ),
        flops=2 * margin * own * columns,
    )
    rims = spread = solution = None
    for sweep in range(ITERS):
        first, last = sweep == 0, sweep == ITERS - 1
        if sweep:
            g0, g1, g2, g3 = traded(tiles)
            (partial,) = call(
                near_columns_kernel,
                "operator_near",
                [local_full],
                operator,
                solution_half,
                g0,
                g1,
                flops=2 * local * (own + 2 * tile) * columns,
            )
            tiles = call(
                rim_kernel,
                "operator_rim",
                four_tiles,
                operator,
                partial,
                g2,
                g3,
                flops=4 * margin * tile * columns,
            )
            r0, r1, r2, r3 = traded(tiles)
            (remainder,) = call(
                remainder_kernel,
                "remainder",
                [owned_full],
                target,
                operator,
                partial,
                g2,
                g3,
                spread,
                r0,
                r1,
                flops=8 * own * tile * columns,
            )
            residual, *tiles = call(
                residual_kernel,
                "residual",
                [owned_half] + four_tiles,
                remainder,
                pick,
                spread,
                r2,
                r3,
                flops=(2 * margin + 4 * tile) * own * columns,
            )
        g0, g1 = traded_over_row(tiles)
        (partial,) = call(
            own_columns_kernel,
            "inverse_own",
            [local_full],
            inverse,
            residual,
            flops=2 * local * own * columns,
        )
        if first:
            (spread,) = call(spread_kernel, "spread", [((own, margin), HALF)], masked)
        (share,) = call(
            share_kernel,
            "share",
            [((2 * tile + coarse * (2 if first else 1), columns), HALF)],
            basis,
            residual,
            tiles[2],
            tiles[3],
            g0,
            g1,
            flops=2 * local * coarse * columns,
        )
        gathered = lax.all_gather(share, "col", axis=0, tiled=True)
        outs = [((groups, coarse, columns), HALF), ((margin, columns), FULL), owned_full]
        parts, rim, inner, *rest = call(
            solve_kernel(first, across),
            "inverse_margin",
            outs + ([((across * coarse, 2 * tile), HALF)] if first else []),
            *([] if first else [rims]),
            inverse,
            partial,
            gathered,
            coarse_inverse,
            g0,
            g1,
            flops=2 * (local * margin + coarse_inverse.size) * columns,
        )
        if first:
            (rims,) = rest
        parts = lax.all_to_all(parts, "row", 0, 0, tiled=True)
        level, *tiles = call(
            coarse_kernel,
            "coarse",
            [((coarse, columns), HALF)] + four_tiles,
            parts,
            basis,
            rim,
            flops=2 * coarse * margin * columns,
        )
        if first:
            operator, tiles = brought(operator, tiles, "operator_load")
        r0, r1, r2, r3 = traded(tiles)
        (base,) = call(
            base_kernel(first),
            "base",
            [owned_full],
            *([] if first else [solution]),
            inner,
            level,
            basis,
            spread,
            r0,
            r1,
            flops=2 * (2 * tile + coarse) * own * columns,
        )
        if last:
            break
        solution, solution_half, *tiles = call(
            update_kernel,
            "update",
            [owned_full, owned_half] + four_tiles,
            base,
            pick,
            spread,
            r2,
            r3,
            flops=(2 * margin + 4 * tile) * own * columns,
        )
    (solution,) = call(
        last_update_kernel,
        "last_update",
        [owned_full],
        base,
        spread,
        r2,
        r3,
        away=True,
        scratch=(pltpu.VMEM((own, columns), FULL), pltpu.SemaphoreType.DMA((4,))),
        flops=4 * tile * own * columns,
    )
    return solution[None, None]


def solution(mesh):
    return jax.shard_map(
        per_device,
        mesh=mesh,
        in_specs=(
            P("row", "col", None, None),
            P("row", "col", None, None),
            P("row", "col", None, None),
            P("row", "col", None, None),
            P(None, "col", "row"),
            P("row", "col", None, None),
            P("row", "col", None),
        ),
        out_specs=P("row", "col", None, None),
        check_vma=False,
    )
```

time: 210 us -> 197 us (0.938)
  starting transfers between devices: 118 us -> 98.2 us
  blocking collectives: 40.1 us -> 53.4 us
  Pallas kernels: 32.1 us -> 21.9 us
  waiting for transfers between devices: 18.1 us -> 21.8 us
    all_gather x0 -> x3, blocking collectives: none -> 24.9 us  [per_device(): gathered = lax.all_gather(share, 'col', axis=0, tiled=True)]
    ppermute x40 -> x34, starting transfers between devices: 118 us -> 98.2 us  [passed_along(): return lax.ppermute(shard, axis, pairs)]
    all_to_all x3 -> x0, blocking collectives: 16.1 us -> none  [per_device(): gathered = lax.all_to_all(restricted, 'col', 0, 0, tiled=True)]
    pallas_call x28 -> x29, Pallas kernels: 32.1 us -> 21.9 us  [call(): pl.pallas_call(body, out_shape=tuple(((pltpu.HBM if away else pltpu.VMEM)...]
    all_to_all x3, blocking collectives: 24 us -> 28.5 us  [per_device(): parts = lax.all_to_all(parts, 'row', 0, 0, tiled=True)]
    ppermute x40 -> x34, waiting for transfers between devices: 18.1 us -> 21.8 us  [passed_along(): return lax.ppermute(shard, axis, pairs)]
  transfers between devices with their start and end apart: 40 -> 34, of which waited for: 9 -> 10; matrix products, arithmetic and copies ran while one was open for 0% -> 0% of each run, Pallas kernels for 9% -> 5%
where the time goes in v5:
time: 197 us; the launch traced here: 196 us
  starting transfers between devices  98.2 us (50%)
  blocking collectives  53.4 us (27%)
  Pallas kernels  21.9 us (11%)
  waiting for transfers between devices  21.8 us (11%)
    ppermute x34, starting transfers between devices, passed_along(): return lax.ppermute(shard, axis, pairs)  98.2 us
    all_to_all x3, blocking collectives, per_device(): parts = lax.all_to_all(parts, 'row', 0, 0, tiled=True)  28.5 us
    all_gather x3, blocking collectives, per_device(): gathered = lax.all_gather(share, 'col', axis=0, tiled=True)  24.9 us
    pallas_call x29, Pallas kernels, call(): pl.pallas_call(body, out_shape=tuple(((pltpu.HBM if away else pltpu.VMEM)...  21.9 us
    ppermute x34, waiting for transfers between devices, passed_along(): return lax.ppermute(shard, axis, pairs)  21.8 us
  transfers between devices with their start and end apart: 34, of which 10 were waited for; matrix products, arithmetic and copies ran while one was open for 0% of the time, Pallas kernels for 5%

profile of v5, /device:TPU:9, one launch (start us, length us, event | category | flops | bytes accessed | tf_op | source)
XLA Modules:
  0.0 196.2 jit_solution(886224805199946224)
XLA Ops:
  0.0 2.7 %select.1 = (f32[1024,256]{1,0:T(8,128)S(1)}, bf16[1024,256]{1,0:T(8,128)(2,1)S(1)}, bf16[512,1024]{1,0:T(8,128)(2,1)S(1)}, s32[4,128]{1,0:T(4,128)S(1)}, bf16[1...) custom-call(f32[1024,256]{1,0:T(8,128)} %bitcast.20, ...), custom_call_target="tpu_custom_call" | custom-call | flops 268435456 | bytes 5769232 | tf_op jit(solution)/shard_map/select/pallas_call | solution.py:28
  2.7 3.1 %collective-permute-start = (bf16[128,256]{1,0:T(8,128)(2,1)S(1)}, bf16[128,256]{1,0:T(8,128)(2,1)S(1)}, u32[]{:S(2)}, u32[]{:S(2)}) collective-permute-start(bf16[128,256]{1,0:T(8,128)(2,1)S(1)} %get-tuple-element.78), channel_id=1, source_target_pairs={{0,4},{4,8},{8,12},{12,16},{16,20},{20,24},{24,28},{1,5},{5,9},{9,... | collective-permute-start | bytes 196616 | tf_op jit(solution)/shard_map/ppermute | solution.py:264
  5.9 3.0 %collective-permute-start.1 = (bf16[128,256]{1,0:T(8,128)(2,1)S(1)}, bf16[128,256]{1,0:T(8,128)(2,1)S(1)}, u32[]{:S(2)}, u32[]{:S(2)}) collective-permute-start(bf16[128,256]{1,0:T(8,128)(2,1)S(1)} %get-tuple-element.79), channel_id=1, source_target_pairs={{4,0},{8,4},{12,8},{16,12},{20,16},{24,20},{28,24},{5,1},{9,5},{13... | collective-permute-start | bytes 196616 | tf_op jit(solution)/shard_map/ppermute | solution.py:264
  11.1 9.9 %all_gather.9.refs_2_ = bf16[1280,256]{1,0:T(8,128)(2,1)S(1)} all-gather(bf16[320,256]{1,0:T(8,128)(2,1)S(1)} %share.3), channel_id=1, replica_groups=mesh['row'=8,'col'=4] {'col'}, dimensions={0}, use_global_device_ids=true | all-gather | bytes 819200 | tf_op jit(solution)/shard_map/all_gather | solution.py:396
  21.8 10.0 %all_to_all.15.parts = bf16[8,32,256]{2,1,0:T(8,128)(2,1)S(1)} all-to-all(bf16[8,32,256]{2,1,0:T(8,128)(2,1)S(1)} %get-tuple-element.81), channel_id=1, replica_groups=mesh['row'=8,'col'=4] {'row'}, dimensions={0} | all-to-all | bytes 262144 | tf_op jit(solution)/shard_map/all_to_all | solution.py:413
  32.0 3.0 %collective-permute-start.2 = (bf16[128,256]{1,0:T(8,128)(2,1)S(1)}, bf16[128,256]{1,0:T(8,128)(2,1)S(1)}, u32[]{:S(2)}, u32[]{:S(2)}) collective-permute-start(bf16[128,256]{1,0:T(8,128)(2,1)S(1)} %get-tuple-element.89), channel_id=1, source_target_pairs={{0,4},{4,8},{8,12},{12,16},{16,20},{20,24},{24,28},{1,5},{5,9},{9,... | collective-permute-start | bytes 196616 | tf_op jit(solution)/shard_map/ppermute | solution.py:264
  35.0 3.2 %collective-permute-start.3 = (bf16[128,256]{1,0:T(8,128)(2,1)S(1)}, bf16[128,256]{1,0:T(8,128)(2,1)S(1)}, u32[]{:S(2)}, u32[]{:S(2)}) collective-permute-start(bf16[128,256]{1,0:T(8,128)(2,1)S(1)} %get-tuple-element.90), channel_id=1, source_target_pairs={{4,0},{8,4},{12,8},{16,12},{20,16},{24,20},{28,24},{5,1},{9,5},{13... | collective-permute-start | bytes 196616 | tf_op jit(solution)/shard_map/ppermute | solution.py:264
  38.2 4.3 %collective-permute-start.4 = (bf16[128,256]{1,0:T(8,128)(2,1)S(1)}, bf16[128,256]{1,0:T(8,128)(2,1)S(1)}, u32[]{:S(2)}, u32[]{:S(2)}) collective-permute-start(bf16[128,256]{1,0:T(8,128)(2,1)S(1)} %get-tuple-element.92), channel_id=1, source_target_pairs={{0,1},{1,2},{2,3},{4,5},{5,6},{6,7},{8,9},{9,10},{10,11},{12,13},{... | collective-permute-start | bytes 196616 | tf_op jit(solution)/shard_map/ppermute | solution.py:264
  42.5 1.9 collective-permute-start.5
  45.2 2.9 %collective-permute-done.5.r3 = bf16[128,256]{1,0:T(8,128)(2,1)S(1)} collective-permute-done((bf16[128,256]{1,0:T(8,128)(2,1)S(1)}, bf16[128,256]{1,0:T(8,128)(2,1)S(1)}, u32[]{:S(2)}, u32[]{:S(2)}) %collective-permute-start.5) | collective-permute-done | bytes 65568 | tf_op jit(solution)/shard_map/ppermute | solution.py:264
  49.0 2.0 %collective-permute-start.6 = (bf16[128,256]{1,0:T(8,128)(2,1)S(1)}, bf16[128,256]{1,0:T(8,128)(2,1)S(1)}, u32[]{:S(2)}, u32[]{:S(2)}) collective-permute-start(bf16[128,256]{1,0:T(8,128)(2,1)S(1)} %get-tuple-element.99), channel_id=1, source_target_pairs={{0,4},{4,8},{8,12},{12,16},{16,20},{20,24},{24,28},{1,5},{5,9},{9,... | collective-permute-start | bytes 196616 | tf_op jit(solution)/shard_map/ppermute | solution.py:264
  51.0 4.2 %collective-permute-start.7 = (bf16[128,256]{1,0:T(8,128)(2,1)S(1)}, bf16[128,256]{1,0:T(8,128)(2,1)S(1)}, u32[]{:S(2)}, u32[]{:S(2)}) collective-permute-start(bf16[128,256]{1,0:T(8,128)(2,1)S(1)} %get-tuple-element.100), channel_id=1, source_target_pairs={{4,0},{8,4},{12,8},{16,12},{20,16},{24,20},{28,24},{5,1},{9,5},{13... | collective-permute-start | bytes 196616 | tf_op jit(solution)/shard_map/ppermute | solution.py:264
  55.2 2.4 %operator_load.1.matrix = bf16[1536,1536]{1,0:T(8,128)(2,1)S(1)} custom-call(bf16[1536,1536]{1,0:T(8,128)(2,1)} %bitcast.19), custom_call_target="tpu_custom_call" | custom-call | bytes 4718592 | tf_op jit(solution)/shard_map/operator_load/pallas_call | solution.py:28
  57.5 2.4 %collective-permute-start.8 = (bf16[128,256]{1,0:T(8,128)(2,1)S(1)}, bf16[128,256]{1,0:T(8,128)(2,1)S(1)}, u32[]{:S(2)}, u32[]{:S(2)}) collective-permute-start(bf16[128,256]{1,0:T(8,128)(2,1)S(1)} %get-tuple-element.101), channel_id=1, source_target_pairs={{0,1},{1,2},{2,3},{4,5},{5,6},{6,7},{8,9},{9,10},{10,11},{12,13},{... | collective-permute-start | bytes 196616 | tf_op jit(solution)/shard_map/ppermute | solution.py:264
  60.0 1.9 collective-permute-start.9
  63.1 2.4 %collective-permute-done.9.g3 = bf16[128,256]{1,0:T(8,128)(2,1)S(1)} collective-permute-done((bf16[128,256]{1,0:T(8,128)(2,1)S(1)}, bf16[128,256]{1,0:T(8,128)(2,1)S(1)}, u32[]{:S(2)}, u32[]{:S(2)}) %collective-permute-start.9) | collective-permute-done | bytes 65568 | tf_op jit(solution)/shard_map/ppermute | solution.py:264
  65.8 1.9 collective-permute-start.10
  67.7 4.3 %collective-permute-start.11 = (bf16[128,256]{1,0:T(8,128)(2,1)S(1)}, bf16[128,256]{1,0:T(8,128)(2,1)S(1)}, u32[]{:S(2)}, u32[]{:S(2)}) collective-permute-start(bf16[128,256]{1,0:T(8,128)(2,1)S(1)} %get-tuple-element.104), channel_id=1, source_target_pairs={{4,0},{8,4},{12,8},{16,12},{20,16},{24,20},{28,24},{5,1},{9,5},{13... | collective-permute-start | bytes 196616 | tf_op jit(solution)/shard_map/ppermute | solution.py:264
  72.0 2.4 %collective-permute-start.12 = (bf16[128,256]{1,0:T(8,128)(2,1)S(1)}, bf16[128,256]{1,0:T(8,128)(2,1)S(1)}, u32[]{:S(2)}, u32[]{:S(2)}) collective-permute-start(bf16[128,256]{1,0:T(8,128)(2,1)S(1)} %get-tuple-element.105), channel_id=1, source_target_pairs={{0,1},{1,2},{2,3},{4,5},{5,6},{6,7},{8,9},{9,10},{10,11},{12,13},{... | collective-permute-start | bytes 196616 | tf_op jit(solution)/shard_map/ppermute | solution.py:264
  74.4 1.9 collective-permute-start.13
  76.8 3.2 %collective-permute-done.13.r3 = bf16[128,256]{1,0:T(8,128)(2,1)S(1)} collective-permute-done((bf16[128,256]{1,0:T(8,128)(2,1)S(1)}, bf16[128,256]{1,0:T(8,128)(2,1)S(1)}, u32[]{:S(2)}, u32[]{:S(2)}) %collective-permute-start.13) | collective-permute-done | bytes 65568 | tf_op jit(solution)/shard_map/ppermute | solution.py:264
  80.9 1.9 collective-permute-start.14
  82.8 4.3 %collective-permute-start.15 = (bf16[128,256]{1,0:T(8,128)(2,1)S(1)}, bf16[128,256]{1,0:T(8,128)(2,1)S(1)}, u32[]{:S(2)}, u32[]{:S(2)}) collective-permute-start(bf16[128,256]{1,0:T(8,128)(2,1)S(1)} %get-tuple-element.111), channel_id=1, source_target_pairs={{4,0},{8,4},{12,8},{16,12},{20,16},{24,20},{28,24},{5,1},{9,5},{13... | collective-permute-start | bytes 196616 | tf_op jit(solution)/shard_map/ppermute | solution.py:264
  88.6 7.5 %all_gather.10.refs_3_ = bf16[1152,256]{1,0:T(8,128)(2,1)S(1)} all-gather(bf16[288,256]{1,0:T(8,128)(2,1)S(1)} %share.4), channel_id=1, replica_groups=mesh['row'=8,'col'=4] {'col'}, dimensions={0}, use_global_device_ids=true | all-gather | bytes 737280 | tf_op jit(solution)/shard_map/all_gather | solution.py:396
  97.0 9.3 %all_to_all.16.parts = bf16[8,32,256]{2,1,0:T(8,128)(2,1)S(1)} all-to-all(bf16[8,32,256]{2,1,0:T(8,128)(2,1)S(1)} %get-tuple-element.113), channel_id=1, replica_groups=mesh['row'=8,'col'=4] {'row'}, dimensions={0} | all-to-all | bytes 262144 | tf_op jit(solution)/shard_map/all_to_all | solution.py:413
  106.5 3.0 %collective-permute-start.16 = (bf16[128,256]{1,0:T(8,128)(2,1)S(1)}, bf16[128,256]{1,0:T(8,128)(2,1)S(1)}, u32[]{:S(2)}, u32[]{:S(2)}) collective-permute-start(bf16[128,256]{1,0:T(8,128)(2,1)S(1)} %get-tuple-element.116), channel_id=1, source_target_pairs={{0,4},{4,8},{8,12},{12,16},{16,20},{20,24},{24,28},{1,5},{5,9},{9,... | collective-permute-start | bytes 196616 | tf_op jit(solution)/shard_map/ppermute | solution.py:264
  109.5 3.2 %collective-permute-start.17 = (bf16[128,256]{1,0:T(8,128)(2,1)S(1)}, bf16[128,256]{1,0:T(8,128)(2,1)S(1)}, u32[]{:S(2)}, u32[]{:S(2)}) collective-permute-start(bf16[128,256]{1,0:T(8,128)(2,1)S(1)} %get-tuple-element.117), channel_id=1, source_target_pairs={{4,0},{8,4},{12,8},{16,12},{20,16},{24,20},{28,24},{5,1},{9,5},{13... | collective-permute-start | bytes 196616 | tf_op jit(solution)/shard_map/ppermute | solution.py:264
  112.7 4.4 %collective-permute-start.18 = (bf16[128,256]{1,0:T(8,128)(2,1)S(1)}, bf16[128,256]{1,0:T(8,128)(2,1)S(1)}, u32[]{:S(2)}, u32[]{:S(2)}) collective-permute-start(bf16[128,256]{1,0:T(8,128)(2,1)S(1)} %get-tuple-element.118), channel_id=1, source_target_pairs={{0,1},{1,2},{2,3},{4,5},{5,6},{6,7},{8,9},{9,10},{10,11},{12,13},{... | collective-permute-start | bytes 196616 | tf_op jit(solution)/shard_map/ppermute | solution.py:264
  117.1 1.9 collective-permute-start.19
  119.5 3.1 %collective-permute-done.19.r3 = bf16[128,256]{1,0:T(8,128)(2,1)S(1)} collective-permute-done((bf16[128,256]{1,0:T(8,128)(2,1)S(1)}, bf16[128,256]{1,0:T(8,128)(2,1)S(1)}, u32[]{:S(2)}, u32[]{:S(2)}) %collective-permute-start.19) | collective-permute-done | bytes 65568 | tf_op jit(solution)/shard_map/ppermute | solution.py:264
  123.5 2.0 %collective-permute-start.20 = (bf16[128,256]{1,0:T(8,128)(2,1)S(1)}, bf16[128,256]{1,0:T(8,128)(2,1)S(1)}, u32[]{:S(2)}, u32[]{:S(2)}) collective-permute-start(bf16[128,256]{1,0:T(8,128)(2,1)S(1)} %get-tuple-element.122), channel_id=1, source_target_pairs={{0,4},{4,8},{8,12},{12,16},{16,20},{20,24},{24,28},{1,5},{5,9},{9,... | collective-permute-start | bytes 196616 | tf_op jit(solution)/shard_map/ppermute | solution.py:264
  125.5 4.2 %collective-permute-start.21 = (bf16[128,256]{1,0:T(8,128)(2,1)S(1)}, bf16[128,256]{1,0:T(8,128)(2,1)S(1)}, u32[]{:S(2)}, u32[]{:S(2)}) collective-permute-start(bf16[128,256]{1,0:T(8,128)(2,1)S(1)} %get-tuple-element.123), channel_id=1, source_target_pairs={{4,0},{8,4},{12,8},{16,12},{20,16},{24,20},{28,24},{5,1},{9,5},{13... | collective-permute-start | bytes 196616 | tf_op jit(solution)/shard_map/ppermute | solution.py:264
  129.7 2.4 %collective-permute-start.22 = (bf16[128,256]{1,0:T(8,128)(2,1)S(1)}, bf16[128,256]{1,0:T(8,128)(2,1)S(1)}, u32[]{:S(2)}, u32[]{:S(2)}) collective-permute-start(bf16[128,256]{1,0:T(8,128)(2,1)S(1)} %get-tuple-element.124), channel_id=1, source_target_pairs={{0,1},{1,2},{2,3},{4,5},{5,6},{6,7},{8,9},{9,10},{10,11},{12,13},{... | collective-permute-start | bytes 196616 | tf_op jit(solution)/shard_map/ppermute | solution.py:264
  132.2 2.1 %collective-permute-start.23 = (bf16[128,256]{1,0:T(8,128)(2,1)S(1)}, bf16[128,256]{1,0:T(8,128)(2,1)S(1)}, u32[]{:S(2)}, u32[]{:S(2)}) collective-permute-start(bf16[128,256]{1,0:T(8,128)(2,1)S(1)} %get-tuple-element.125), channel_id=1, source_target_pairs={{1,0},{2,1},{3,2},{5,4},{6,5},{7,6},{9,8},{10,9},{11,10},{13,12},{... | collective-permute-start | bytes 196616 | tf_op jit(solution)/shard_map/ppermute | solution.py:264
  135.5 2.3 %collective-permute-done.23.g3 = bf16[128,256]{1,0:T(8,128)(2,1)S(1)} collective-permute-done((bf16[128,256]{1,0:T(8,128)(2,1)S(1)}, bf16[128,256]{1,0:T(8,128)(2,1)S(1)}, u32[]{:S(2)}, u32[]{:S(2)}) %collective-permute-start.23) | collective-permute-done | bytes 65568 | tf_op jit(solution)/shard_map/ppermute | solution.py:264
  138.0 1.9 collective-permute-start.24
  139.9 4.3 %collective-permute-start.25 = (bf16[128,256]{1,0:T(8,128)(2,1)S(1)}, bf16[128,256]{1,0:T(8,128)(2,1)S(1)}, u32[]{:S(2)}, u32[]{:S(2)}) collective-permute-start(bf16[128,256]{1,0:T(8,128)(2,1)S(1)} %get-tuple-element.127), channel_id=1, source_target_pairs={{4,0},{8,4},{12,8},{16,12},{20,16},{24,20},{28,24},{5,1},{9,5},{13... | collective-permute-start | bytes 196616 | tf_op jit(solution)/shard_map/ppermute | solution.py:264
  144.2 2.4 %collective-permute-start.26 = (bf16[128,256]{1,0:T(8,128)(2,1)S(1)}, bf16[128,256]{1,0:T(8,128)(2,1)S(1)}, u32[]{:S(2)}, u32[]{:S(2)}) collective-permute-start(bf16[128,256]{1,0:T(8,128)(2,1)S(1)} %get-tuple-element.128), channel_id=1, source_target_pairs={{0,1},{1,2},{2,3},{4,5},{5,6},{6,7},{8,9},{9,10},{10,11},{12,13},{... | collective-permute-start | bytes 196616 | tf_op jit(solution)/shard_map/ppermute | solution.py:264
  146.6 1.9 collective-permute-start.27
  149.0 3.2 %collective-permute-done.27.r3 = bf16[128,256]{1,0:T(8,128)(2,1)S(1)} collective-permute-done((bf16[128,256]{1,0:T(8,128)(2,1)S(1)}, bf16[128,256]{1,0:T(8,128)(2,1)S(1)}, u32[]{:S(2)}, u32[]{:S(2)}) %collective-permute-start.27) | collective-permute-done | bytes 65568 | tf_op jit(solution)/shard_map/ppermute | solution.py:264
  153.0 1.9 collective-permute-start.28
  155.0 4.3 %collective-permute-start.29 = (bf16[128,256]{1,0:T(8,128)(2,1)S(1)}, bf16[128,256]{1,0:T(8,128)(2,1)S(1)}, u32[]{:S(2)}, u32[]{:S(2)}) collective-permute-start(bf16[128,256]{1,0:T(8,128)(2,1)S(1)} %get-tuple-element.134), channel_id=1, source_target_pairs={{4,0},{8,4},{12,8},{16,12},{20,16},{24,20},{28,24},{5,1},{9,5},{13... | collective-permute-start | bytes 196616 | tf_op jit(solution)/shard_map/ppermute | solution.py:264
  160.8 7.5 %all_gather.11.refs_3_ = bf16[1152,256]{1,0:T(8,128)(2,1)S(1)} all-gather(bf16[288,256]{1,0:T(8,128)(2,1)S(1)} %share.5), channel_id=1, replica_groups=mesh['row'=8,'col'=4] {'col'}, dimensions={0}, use_global_device_ids=true | all-gather | bytes 737280 | tf_op jit(solution)/shard_map/all_gather | solution.py:396
  169.1 9.3 %all_to_all.17.parts = bf16[8,32,256]{2,1,0:T(8,128)(2,1)S(1)} all-to-all(bf16[8,32,256]{2,1,0:T(8,128)(2,1)S(1)} %get-tuple-element.136), channel_id=1, replica_groups=mesh['row'=8,'col'=4] {'row'}, dimensions={0} | all-to-all | bytes 262144 | tf_op jit(solution)/shard_map/all_to_all | solution.py:413
  178.6 3.0 %collective-permute-start.30 = (bf16[128,256]{1,0:T(8,128)(2,1)S(1)}, bf16[128,256]{1,0:T(8,128)(2,1)S(1)}, u32[]{:S(2)}, u32[]{:S(2)}) collective-permute-start(bf16[128,256]{1,0:T(8,128)(2,1)S(1)} %get-tuple-element.139), channel_id=1, source_target_pairs={{0,4},{4,8},{8,12},{12,16},{16,20},{20,24},{24,28},{1,5},{5,9},{9,... | collective-permute-start | bytes 196616 | tf_op jit(solution)/shard_map/ppermute | solution.py:264
  181.6 3.2 %collective-permute-start.31 = (bf16[128,256]{1,0:T(8,128)(2,1)S(1)}, bf16[128,256]{1,0:T(8,128)(2,1)S(1)}, u32[]{:S(2)}, u32[]{:S(2)}) collective-permute-start(bf16[128,256]{1,0:T(8,128)(2,1)S(1)} %get-tuple-element.140), channel_id=1, source_target_pairs={{4,0},{8,4},{12,8},{16,12},{20,16},{24,20},{28,24},{5,1},{9,5},{13... | collective-permute-start | bytes 196616 | tf_op jit(solution)/shard_map/ppermute | solution.py:264
  184.8 4.4 %collective-permute-start.32 = (bf16[128,256]{1,0:T(8,128)(2,1)S(1)}, bf16[128,256]{1,0:T(8,128)(2,1)S(1)}, u32[]{:S(2)}, u32[]{:S(2)}) collective-permute-start(bf16[128,256]{1,0:T(8,128)(2,1)S(1)} %get-tuple-element.141), channel_id=1, source_target_pairs={{0,1},{1,2},{2,3},{4,5},{5,6},{6,7},{8,9},{9,10},{10,11},{12,13},{... | collective-permute-start | bytes 196616 | tf_op jit(solution)/shard_map/ppermute | solution.py:264
  191.7 3.1 %collective-permute-done.33.r3 = bf16[128,256]{1,0:T(8,128)(2,1)S(1)} collective-permute-done((bf16[128,256]{1,0:T(8,128)(2,1)S(1)}, bf16[128,256]{1,0:T(8,128)(2,1)S(1)}, u32[]{:S(2)}, u32[]{:S(2)}) %collective-permute-start.33) | collective-permute-done | bytes 65568 | tf_op jit(solution)/shard_map/ppermute | solution.py:264
  (59 shorter events, 20.4 us)
Async XLA Ops:
  2.7 7.2 %collective-permute-start = (bf16[128,256]{1,0:T(8,128)(2,1)S(1)}, bf16[128,256]{1,0:T(8,128)(2,1)S(1)}, u32[]{:S(2)}, u32[]{:S(2)}) collective-permute-start(bf16[128,256]{1,0:T(8,128)(2,1)S(1)} %get-tuple-element.78), channel_id=1, source_target_pairs={{0,4},{4,8},{8,12},{12,16},{16,20},{20,24},{24,28},{1,5},{5,9},{9,... | collective-permute-start | bytes 196616 | tf_op jit(solution)/shard_map/ppermute | solution.py:264
  5.9 5.0 %collective-permute-start.1 = (bf16[128,256]{1,0:T(8,128)(2,1)S(1)}, bf16[128,256]{1,0:T(8,128)(2,1)S(1)}, u32[]{:S(2)}, u32[]{:S(2)}) collective-permute-start(bf16[128,256]{1,0:T(8,128)(2,1)S(1)} %get-tuple-element.79), channel_id=1, source_target_pairs={{4,0},{8,4},{12,8},{16,12},{20,16},{24,20},{28,24},{5,1},{9,5},{13... | collective-permute-start | bytes 196616 | tf_op jit(solution)/shard_map/ppermute | solution.py:264
  8.9 2.0 %copy-start = (bf16[1,1,1536,32]{2,3,1,0:T(8,128)(2,1)S(1)}, bf16[1,1,1536,32]{2,3,1,0:T(8,128)(2,1)}, u32[]{:S(2)}) copy-start(bf16[1,1,1536,32]{2,3,1,0:T(8,128)(2,1)} %param.10) | copy-start | bytes 294916
  9.9 11.0 %copy-start.1 = (bf16[8,32,128]{2,1,0:T(8,128)(2,1)S(1)}, bf16[8,32,128]{2,1,0:T(8,128)(2,1)}, u32[]{:S(2)}) copy-start(bf16[8,32,128]{2,1,0:T(8,128)(2,1)} %refs_4_.3) | copy-start | bytes 196612
  32.0 12.7 %collective-permute-start.2 = (bf16[128,256]{1,0:T(8,128)(2,1)S(1)}, bf16[128,256]{1,0:T(8,128)(2,1)S(1)}, u32[]{:S(2)}, u32[]{:S(2)}) collective-permute-start(bf16[128,256]{1,0:T(8,128)(2,1)S(1)} %get-tuple-element.89), channel_id=1, source_target_pairs={{0,4},{4,8},{8,12},{12,16},{16,20},{20,24},{24,28},{1,5},{5,9},{9,... | collective-permute-start | bytes 196616 | tf_op jit(solution)/shard_map/ppermute | solution.py:264
  35.0 9.7 %collective-permute-start.3 = (bf16[128,256]{1,0:T(8,128)(2,1)S(1)}, bf16[128,256]{1,0:T(8,128)(2,1)S(1)}, u32[]{:S(2)}, u32[]{:S(2)}) collective-permute-start(bf16[128,256]{1,0:T(8,128)(2,1)S(1)} %get-tuple-element.90), channel_id=1, source_target_pairs={{4,0},{8,4},{12,8},{16,12},{20,16},{24,20},{28,24},{5,1},{9,5},{13... | collective-permute-start | bytes 196616 | tf_op jit(solution)/shard_map/ppermute | solution.py:264
  38.2 7.0 %collective-permute-start.4 = (bf16[128,256]{1,0:T(8,128)(2,1)S(1)}, bf16[128,256]{1,0:T(8,128)(2,1)S(1)}, u32[]{:S(2)}, u32[]{:S(2)}) collective-permute-start(bf16[128,256]{1,0:T(8,128)(2,1)S(1)} %get-tuple-element.92), channel_id=1, source_target_pairs={{0,1},{1,2},{2,3},{4,5},{5,6},{6,7},{8,9},{9,10},{10,11},{12,13},{... | collective-permute-start | bytes 196616 | tf_op jit(solution)/shard_map/ppermute | solution.py:264
  42.5 5.6 %collective-permute-start.5 = (bf16[128,256]{1,0:T(8,128)(2,1)S(1)}, bf16[128,256]{1,0:T(8,128)(2,1)S(1)}, u32[]{:S(2)}, u32[]{:S(2)}) collective-permute-start(bf16[128,256]{1,0:T(8,128)(2,1)S(1)} %get-tuple-element.93), channel_id=1, source_target_pairs={{1,0},{2,1},{3,2},{5,4},{6,5},{7,6},{9,8},{10,9},{11,10},{13,12},{... | collective-permute-start | bytes 196616 | tf_op jit(solution)/shard_map/ppermute | solution.py:264
  49.0 13.0 %collective-permute-start.6 = (bf16[128,256]{1,0:T(8,128)(2,1)S(1)}, bf16[128,256]{1,0:T(8,128)(2,1)S(1)}, u32[]{:S(2)}, u32[]{:S(2)}) collective-permute-start(bf16[128,256]{1,0:T(8,128)(2,1)S(1)} %get-tuple-element.99), channel_id=1, source_target_pairs={{0,4},{4,8},{8,12},{12,16},{16,20},{20,24},{24,28},{1,5},{5,9},{9,... | collective-permute-start | bytes 196616 | tf_op jit(solution)/shard_map/ppermute | solution.py:264
  51.0 11.0 %collective-permute-start.7 = (bf16[128,256]{1,0:T(8,128)(2,1)S(1)}, bf16[128,256]{1,0:T(8,128)(2,1)S(1)}, u32[]{:S(2)}, u32[]{:S(2)}) collective-permute-start(bf16[128,256]{1,0:T(8,128)(2,1)S(1)} %get-tuple-element.100), channel_id=1, source_target_pairs={{4,0},{8,4},{12,8},{16,12},{20,16},{24,20},{28,24},{5,1},{9,5},{13... | collective-permute-start | bytes 196616 | tf_op jit(solution)/shard_map/ppermute | solution.py:264
  57.5 5.6 %collective-permute-start.8 = (bf16[128,256]{1,0:T(8,128)(2,1)S(1)}, bf16[128,256]{1,0:T(8,128)(2,1)S(1)}, u32[]{:S(2)}, u32[]{:S(2)}) collective-permute-start(bf16[128,256]{1,0:T(8,128)(2,1)S(1)} %get-tuple-element.101), channel_id=1, source_target_pairs={{0,1},{1,2},{2,3},{4,5},{5,6},{6,7},{8,9},{9,10},{10,11},{12,13},{... | collective-permute-start | bytes 196616 | tf_op jit(solution)/shard_map/ppermute | solution.py:264
  60.0 5.6 %collective-permute-start.9 = (bf16[128,256]{1,0:T(8,128)(2,1)S(1)}, bf16[128,256]{1,0:T(8,128)(2,1)S(1)}, u32[]{:S(2)}, u32[]{:S(2)}) collective-permute-start(bf16[128,256]{1,0:T(8,128)(2,1)S(1)} %get-tuple-element.102), channel_id=1, source_target_pairs={{1,0},{2,1},{3,2},{5,4},{6,5},{7,6},{9,8},{10,9},{11,10},{13,12},{... | collective-permute-start | bytes 196616 | tf_op jit(solution)/shard_map/ppermute | solution.py:264
  65.8 10.6 %collective-permute-start.10 = (bf16[128,256]{1,0:T(8,128)(2,1)S(1)}, bf16[128,256]{1,0:T(8,128)(2,1)S(1)}, u32[]{:S(2)}, u32[]{:S(2)}) collective-permute-start(bf16[128,256]{1,0:T(8,128)(2,1)S(1)} %get-tuple-element.103), channel_id=1, source_target_pairs={{0,4},{4,8},{8,12},{12,16},{16,20},{20,24},{24,28},{1,5},{5,9},{9,... | collective-permute-start | bytes 196616 | tf_op jit(solution)/shard_map/ppermute | solution.py:264
  67.7 8.6 %collective-permute-start.11 = (bf16[128,256]{1,0:T(8,128)(2,1)S(1)}, bf16[128,256]{1,0:T(8,128)(2,1)S(1)}, u32[]{:S(2)}, u32[]{:S(2)}) collective-permute-start(bf16[128,256]{1,0:T(8,128)(2,1)S(1)} %get-tuple-element.104), channel_id=1, source_target_pairs={{4,0},{8,4},{12,8},{16,12},{20,16},{24,20},{28,24},{5,1},{9,5},{13... | collective-permute-start | bytes 196616 | tf_op jit(solution)/shard_map/ppermute | solution.py:264
  72.0 4.8 %collective-permute-start.12 = (bf16[128,256]{1,0:T(8,128)(2,1)S(1)}, bf16[128,256]{1,0:T(8,128)(2,1)S(1)}, u32[]{:S(2)}, u32[]{:S(2)}) collective-permute-start(bf16[128,256]{1,0:T(8,128)(2,1)S(1)} %get-tuple-element.105), channel_id=1, source_target_pairs={{0,1},{1,2},{2,3},{4,5},{5,6},{6,7},{8,9},{9,10},{10,11},{12,13},{... | collective-permute-start | bytes 196616 | tf_op jit(solution)/shard_map/ppermute | solution.py:264
  74.4 5.6 %collective-permute-start.13 = (bf16[128,256]{1,0:T(8,128)(2,1)S(1)}, bf16[128,256]{1,0:T(8,128)(2,1)S(1)}, u32[]{:S(2)}, u32[]{:S(2)}) collective-permute-start(bf16[128,256]{1,0:T(8,128)(2,1)S(1)} %get-tuple-element.106), channel_id=1, source_target_pairs={{1,0},{2,1},{3,2},{5,4},{6,5},{7,6},{9,8},{10,9},{11,10},{13,12},{... | collective-permute-start | bytes 196616 | tf_op jit(solution)/shard_map/ppermute | solution.py:264
  80.9 7.2 %collective-permute-start.14 = (bf16[128,256]{1,0:T(8,128)(2,1)S(1)}, bf16[128,256]{1,0:T(8,128)(2,1)S(1)}, u32[]{:S(2)}, u32[]{:S(2)}) collective-permute-start(bf16[128,256]{1,0:T(8,128)(2,1)S(1)} %get-tuple-element.110), channel_id=1, source_target_pairs={{0,4},{4,8},{8,12},{12,16},{16,20},{20,24},{24,28},{1,5},{5,9},{9,... | collective-permute-start | bytes 196616 | tf_op jit(solution)/shard_map/ppermute | solution.py:264
  82.8 5.6 %collective-permute-start.15 = (bf16[128,256]{1,0:T(8,128)(2,1)S(1)}, bf16[128,256]{1,0:T(8,128)(2,1)S(1)}, u32[]{:S(2)}, u32[]{:S(2)}) collective-permute-start(bf16[128,256]{1,0:T(8,128)(2,1)S(1)} %get-tuple-element.111), channel_id=1, source_target_pairs={{4,0},{8,4},{12,8},{16,12},{20,16},{24,20},{28,24},{5,1},{9,5},{13... | collective-permute-start | bytes 196616 | tf_op jit(solution)/shard_map/ppermute | solution.py:264
  106.5 12.5 %collective-permute-start.16 = (bf16[128,256]{1,0:T(8,128)(2,1)S(1)}, bf16[128,256]{1,0:T(8,128)(2,1)S(1)}, u32[]{:S(2)}, u32[]{:S(2)}) collective-permute-start(bf16[128,256]{1,0:T(8,128)(2,1)S(1)} %get-tuple-element.116), channel_id=1, source_target_pairs={{0,4},{4,8},{8,12},{12,16},{16,20},{20,24},{24,28},{1,5},{5,9},{9,... | collective-permute-start | bytes 196616 | tf_op jit(solution)/shard_map/ppermute | solution.py:264
  109.5 9.6 %collective-permute-start.17 = (bf16[128,256]{1,0:T(8,128)(2,1)S(1)}, bf16[128,256]{1,0:T(8,128)(2,1)S(1)}, u32[]{:S(2)}, u32[]{:S(2)}) collective-permute-start(bf16[128,256]{1,0:T(8,128)(2,1)S(1)} %get-tuple-element.117), channel_id=1, source_target_pairs={{4,0},{8,4},{12,8},{16,12},{20,16},{24,20},{28,24},{5,1},{9,5},{13... | collective-permute-start | bytes 196616 | tf_op jit(solution)/shard_map/ppermute | solution.py:264
  112.7 6.8 %collective-permute-start.18 = (bf16[128,256]{1,0:T(8,128)(2,1)S(1)}, bf16[128,256]{1,0:T(8,128)(2,1)S(1)}, u32[]{:S(2)}, u32[]{:S(2)}) collective-permute-start(bf16[128,256]{1,0:T(8,128)(2,1)S(1)} %get-tuple-element.118), channel_id=1, source_target_pairs={{0,1},{1,2},{2,3},{4,5},{5,6},{6,7},{8,9},{9,10},{10,11},{12,13},{... | collective-permute-start | bytes 196616 | tf_op jit(solution)/shard_map/ppermute | solution.py:264
  117.1 5.6 %collective-permute-start.19 = (bf16[128,256]{1,0:T(8,128)(2,1)S(1)}, bf16[128,256]{1,0:T(8,128)(2,1)S(1)}, u32[]{:S(2)}, u32[]{:S(2)}) collective-permute-start(bf16[128,256]{1,0:T(8,128)(2,1)S(1)} %get-tuple-element.119), channel_id=1, source_target_pairs={{1,0},{2,1},{3,2},{5,4},{6,5},{7,6},{9,8},{10,9},{11,10},{13,12},{... | collective-permute-start | bytes 196616 | tf_op jit(solution)/shard_map/ppermute | solution.py:264
  123.5 10.7 %collective-permute-start.20 = (bf16[128,256]{1,0:T(8,128)(2,1)S(1)}, bf16[128,256]{1,0:T(8,128)(2,1)S(1)}, u32[]{:S(2)}, u32[]{:S(2)}) collective-permute-start(bf16[128,256]{1,0:T(8,128)(2,1)S(1)} %get-tuple-element.122), channel_id=1, source_target_pairs={{0,4},{4,8},{8,12},{12,16},{16,20},{20,24},{24,28},{1,5},{5,9},{9,... | collective-permute-start | bytes 196616 | tf_op jit(solution)/shard_map/ppermute | solution.py:264
  125.5 8.8 %collective-permute-start.21 = (bf16[128,256]{1,0:T(8,128)(2,1)S(1)}, bf16[128,256]{1,0:T(8,128)(2,1)S(1)}, u32[]{:S(2)}, u32[]{:S(2)}) collective-permute-start(bf16[128,256]{1,0:T(8,128)(2,1)S(1)} %get-tuple-element.123), channel_id=1, source_target_pairs={{4,0},{8,4},{12,8},{16,12},{20,16},{24,20},{28,24},{5,1},{9,5},{13... | collective-permute-start | bytes 196616 | tf_op jit(solution)/shard_map/ppermute | solution.py:264
  129.7 5.8 %collective-permute-start.22 = (bf16[128,256]{1,0:T(8,128)(2,1)S(1)}, bf16[128,256]{1,0:T(8,128)(2,1)S(1)}, u32[]{:S(2)}, u32[]{:S(2)}) collective-permute-start(bf16[128,256]{1,0:T(8,128)(2,1)S(1)} %get-tuple-element.124), channel_id=1, source_target_pairs={{0,1},{1,2},{2,3},{4,5},{5,6},{6,7},{8,9},{9,10},{10,11},{12,13},{... | collective-permute-start | bytes 196616 | tf_op jit(solution)/shard_map/ppermute | solution.py:264
  132.2 5.6 %collective-permute-start.23 = (bf16[128,256]{1,0:T(8,128)(2,1)S(1)}, bf16[128,256]{1,0:T(8,128)(2,1)S(1)}, u32[]{:S(2)}, u32[]{:S(2)}) collective-permute-start(bf16[128,256]{1,0:T(8,128)(2,1)S(1)} %get-tuple-element.125), channel_id=1, source_target_pairs={{1,0},{2,1},{3,2},{5,4},{6,5},{7,6},{9,8},{10,9},{11,10},{13,12},{... | collective-permute-start | bytes 196616 | tf_op jit(solution)/shard_map/ppermute | solution.py:264
  138.0 10.6 %collective-permute-start.24 = (bf16[128,256]{1,0:T(8,128)(2,1)S(1)}, bf16[128,256]{1,0:T(8,128)(2,1)S(1)}, u32[]{:S(2)}, u32[]{:S(2)}) collective-permute-start(bf16[128,256]{1,0:T(8,128)(2,1)S(1)} %get-tuple-element.126), channel_id=1, source_target_pairs={{0,4},{4,8},{8,12},{12,16},{16,20},{20,24},{24,28},{1,5},{5,9},{9,... | collective-permute-start | bytes 196616 | tf_op jit(solution)/shard_map/ppermute | solution.py:264
  139.9 8.6 %collective-permute-start.25 = (bf16[128,256]{1,0:T(8,128)(2,1)S(1)}, bf16[128,256]{1,0:T(8,128)(2,1)S(1)}, u32[]{:S(2)}, u32[]{:S(2)}) collective-permute-start(bf16[128,256]{1,0:T(8,128)(2,1)S(1)} %get-tuple-element.127), channel_id=1, source_target_pairs={{4,0},{8,4},{12,8},{16,12},{20,16},{24,20},{28,24},{5,1},{9,5},{13... | collective-permute-start | bytes 196616 | tf_op jit(solution)/shard_map/ppermute | solution.py:264
  144.2 4.8 %collective-permute-start.26 = (bf16[128,256]{1,0:T(8,128)(2,1)S(1)}, bf16[128,256]{1,0:T(8,128)(2,1)S(1)}, u32[]{:S(2)}, u32[]{:S(2)}) collective-permute-start(bf16[128,256]{1,0:T(8,128)(2,1)S(1)} %get-tuple-element.128), channel_id=1, source_target_pairs={{0,1},{1,2},{2,3},{4,5},{5,6},{6,7},{8,9},{9,10},{10,11},{12,13},{... | collective-permute-start | bytes 196616 | tf_op jit(solution)/shard_map/ppermute | solution.py:264
  146.6 5.6 %collective-permute-start.27 = (bf16[128,256]{1,0:T(8,128)(2,1)S(1)}, bf16[128,256]{1,0:T(8,128)(2,1)S(1)}, u32[]{:S(2)}, u32[]{:S(2)}) collective-permute-start(bf16[128,256]{1,0:T(8,128)(2,1)S(1)} %get-tuple-element.129), channel_id=1, source_target_pairs={{1,0},{2,1},{3,2},{5,4},{6,5},{7,6},{9,8},{10,9},{11,10},{13,12},{... | collective-permute-start | bytes 196616 | tf_op jit(solution)/shard_map/ppermute | solution.py:264
  153.0 7.2 %collective-permute-start.28 = (bf16[128,256]{1,0:T(8,128)(2,1)S(1)}, bf16[128,256]{1,0:T(8,128)(2,1)S(1)}, u32[]{:S(2)}, u32[]{:S(2)}) collective-permute-start(bf16[128,256]{1,0:T(8,128)(2,1)S(1)} %get-tuple-element.133), channel_id=1, source_target_pairs={{0,4},{4,8},{8,12},{12,16},{16,20},{20,24},{24,28},{1,5},{5,9},{9,... | collective-permute-start | bytes 196616 | tf_op jit(solution)/shard_map/ppermute | solution.py:264
  155.0 5.6 %collective-permute-start.29 = (bf16[128,256]{1,0:T(8,128)(2,1)S(1)}, bf16[128,256]{1,0:T(8,128)(2,1)S(1)}, u32[]{:S(2)}, u32[]{:S(2)}) collective-permute-start(bf16[128,256]{1,0:T(8,128)(2,1)S(1)} %get-tuple-element.134), channel_id=1, source_target_pairs={{4,0},{8,4},{12,8},{16,12},{20,16},{24,20},{28,24},{5,1},{9,5},{13... | collective-permute-start | bytes 196616 | tf_op jit(solution)/shard_map/ppermute | solution.py:264
  178.6 12.5 %collective-permute-start.30 = (bf16[128,256]{1,0:T(8,128)(2,1)S(1)}, bf16[128,256]{1,0:T(8,128)(2,1)S(1)}, u32[]{:S(2)}, u32[]{:S(2)}) collective-permute-start(bf16[128,256]{1,0:T(8,128)(2,1)S(1)} %get-tuple-element.139), channel_id=1, source_target_pairs={{0,4},{4,8},{8,12},{12,16},{16,20},{20,24},{24,28},{1,5},{5,9},{9,... | collective-permute-start | bytes 196616 | tf_op jit(solution)/shard_map/ppermute | solution.py:264
  181.6 9.6 %collective-permute-start.31 = (bf16[128,256]{1,0:T(8,128)(2,1)S(1)}, bf16[128,256]{1,0:T(8,128)(2,1)S(1)}, u32[]{:S(2)}, u32[]{:S(2)}) collective-permute-start(bf16[128,256]{1,0:T(8,128)(2,1)S(1)} %get-tuple-element.140), channel_id=1, source_target_pairs={{4,0},{8,4},{12,8},{16,12},{20,16},{24,20},{28,24},{5,1},{9,5},{13... | collective-permute-start | bytes 196616 | tf_op jit(solution)/shard_map/ppermute | solution.py:264
  184.8 6.8 %collective-permute-start.32 = (bf16[128,256]{1,0:T(8,128)(2,1)S(1)}, bf16[128,256]{1,0:T(8,128)(2,1)S(1)}, u32[]{:S(2)}, u32[]{:S(2)}) collective-permute-start(bf16[128,256]{1,0:T(8,128)(2,1)S(1)} %get-tuple-element.141), channel_id=1, source_target_pairs={{0,1},{1,2},{2,3},{4,5},{5,6},{6,7},{8,9},{9,10},{10,11},{12,13},{... | collective-permute-start | bytes 196616 | tf_op jit(solution)/shard_map/ppermute | solution.py:264
  189.2 5.6 %collective-permute-start.33 = (bf16[128,256]{1,0:T(8,128)(2,1)S(1)}, bf16[128,256]{1,0:T(8,128)(2,1)S(1)}, u32[]{:S(2)}, u32[]{:S(2)}) collective-permute-start(bf16[128,256]{1,0:T(8,128)(2,1)S(1)} %get-tuple-element.142), channel_id=1, source_target_pairs={{1,0},{2,1},{3,2},{5,4},{6,5},{7,6},{9,8},{10,9},{11,10},{13,12},{... | collective-permute-start | bytes 196616 | tf_op jit(solution)/shard_map/ppermute | solution.py:264

commit v6 on v5

--- a/solution.py
+++ b/solution.py
@@ -37,32 +37,72 @@
     )(*distant, *near)
 
 
+def parities():
+    return lax.rem(lax.axis_index("row"), 2), lax.rem(lax.axis_index("col"), 2)
+
+
+def directions():
+    row, col = parities()
+    return 1 - row, row, 3 - col, 2 + col
+
+
+def margin_spans(own, tile):
+    return [
+        (pl.ds(pl.multiple_of(own + d * tile, tile), tile), slice(own + i * tile, own + (i + 1) * tile))
+        for i, d in enumerate(directions())
+    ]
+
+
+def matrix_pieces(far, near, own, tile):
+    margins = margin_spans(own, tile)
+    half = own // 2
+    rows = [(slice(0, half), slice(0, half)), (slice(half, own), slice(half, own))] + margins
+    columns = [(slice(0, own), slice(0, own))] + margins
+    return [(far.at[fr, fc], near.at[nr, nc]) for fr, nr in rows for fc, nc in columns]
+
+
+MATRIX_PIECES = 30
+
+
+def started(pairs, sems):
+    loads = [pltpu.make_async_copy(far, near, sems.at[i]) for i, (far, near) in enumerate(pairs)]
+    for load in loads:
+        load.start()
+    return loads
+
+
 def select_kernel(
-    far_target, far_rows, far_counts, far_inverse, target, half, pick, masked, inverse, *rest
+    far_target, far_rows, far_counts, far_basis, far_inverse, target, half, pick, masked, basis, inverse, *rest
 ):
     *tiles, rows, counts, sems = rest
     own = target.shape[0]
     tile = rows.shape[1]
     pairs = [(far_rows, rows), (far_counts, counts), (far_target, target)]
-    pieces = sems.shape[0] - len(pairs)
-    height = inverse.shape[0] // pieces
-    for i in range(pieces):
-        at = slice(i * height, (i + 1) * height)
-        pairs.append((far_inverse.at[at], inverse.at[at]))
-    loads = [
-        pltpu.make_async_copy(far, near, sems.at[i]) for i, (far, near) in enumerate(pairs)
+    pairs += [
+        (far_basis.at[:, far], basis.at[:, near])
+        for far, near in [(slice(0, own), slice(0, own))] + margin_spans(own, tile)
     ]
-    for load in loads:
-        load.start()
+    pairs += matrix_pieces(far_inverse, inverse, own, tile)
+    loads = started(pairs, sems)
     loads[0].wait()
     loads[1].wait()
-    for d in range(4):
-        here = jnp.where(
+    listed = [
+        jnp.where(
             lax.broadcasted_iota(jnp.int32, (1, tile), 1) < counts[0, d], rows[d : d + 1, :], -1
         )
-        masked[d : d + 1, :] = here
+        for d in range(4)
+    ]
+    row, col = parities()
+    ordered = (
+        jnp.where(row == 0, listed[1], listed[0]),
+        jnp.where(row == 0, listed[0], listed[1]),
+        jnp.where(col == 0, listed[3], listed[2]),
+        jnp.where(col == 0, listed[2], listed[3]),
+    )
+    for i, here in enumerate(ordered):
+        masked[i : i + 1, :] = here
         down = jnp.transpose(jnp.broadcast_to(here, (tile, tile)))[:, :1]
-        pick[d * tile : (d + 1) * tile, :] = (
+        pick[i * tile : (i + 1) * tile, :] = (
             lax.broadcasted_iota(jnp.int32, (tile, own), 1) == down
         ).astype(FULL).astype(HALF)
     loads[2].wait()
@@ -78,24 +118,15 @@
         tiles[d][...] = product(pick[d * tile : (d + 1) * tile, :], half[...]).astype(HALF)
 
 
-def spread_kernel(masked, spread):
+def spread_kernel(far, masked, spread, matrix, sems):
     own = spread.shape[0]
     tile = masked.shape[1]
+    loads = started(matrix_pieces(far, matrix, own, tile), sems)
     for d in range(4):
         wide = jnp.broadcast_to(masked[d : d + 1, :], (own, tile))
         spread[:, d * tile : (d + 1) * tile] = (
             lax.broadcasted_iota(jnp.int32, (own, tile), 0) == wide
         ).astype(FULL).astype(HALF)
-
-
-def load_kernel(far, near, sems):
-    pieces = sems.shape[0]
-    height = far.shape[0] // pieces
-    loads = []
-    for i in range(pieces):
-        at = slice(i * height, (i + 1) * height)
-        loads.append(pltpu.make_async_copy(far.at[at], near.at[at], sems.at[i]))
-        loads[-1].start()
     for load in loads:
         load.wait()
 
@@ -145,24 +176,25 @@
             here = slice(b * coarse, (b + 1) * coarse)
             at = b * stride + 2 * tile
             total = gathered[at : at + coarse, :].astype(FULL)
-            if b > 0:
-                at = (b - 1) * stride + tile
-                total += product(rims[here, :tile], gathered[at : at + tile, :])
-            if b < across - 1:
-                at = (b + 1) * stride
-                total += product(rims[here, tile:], gathered[at : at + tile, :])
+            for i in range(2):
+                other = partner(b, i)
+                if 0 <= other < across:
+                    at = other * stride + i * tile
+                    total += product(
+                        rims[here, i * tile : (i + 1) * tile], gathered[at : at + tile, :]
+                    )
             restricted.append(total.astype(HALF))
         restricted = jnp.concatenate(restricted, axis=0)
         for i in range(parts.shape[0]):
             parts[i, :, :] = product(inverse[i, :, :], restricted).astype(HALF)
-        me = lax.axis_index("col")
-        at = pl.multiple_of(jnp.maximum(me - 1, 0) * stride + tile, 32)
-        lower = gathered[pl.ds(at, tile), :]
-        at = pl.multiple_of(jnp.minimum(me + 1, across - 1) * stride, 32)
-        upper = gathered[pl.ds(at, tile), :]
-        lower = jnp.where(me > 0, lower, jnp.zeros_like(lower))
-        upper = jnp.where(me < across - 1, upper, jnp.zeros_like(upper))
-        ghosts = jnp.concatenate([g0[...], g1[...], lower, upper], axis=0)
+        ghosts = [g0[...], g1[...]]
+        for i in range(2):
+            other = partner(lax.axis_index("col"), i)
+            there = (other >= 0) & (other < across)
+            at = pl.multiple_of(jnp.where(there, other, 0) * stride + i * tile, 32)
+            ghost = gathered[pl.ds(at, tile), :]
+            ghosts.append(jnp.where(there, ghost, jnp.zeros_like(ghost)))
+        ghosts = jnp.concatenate(ghosts, axis=0)
         rim[...] = partial[own:, :] + product(matrix[own:, own:], ghosts)
         inner[...] = partial[:own, :] + product(matrix[:own, own:], ghosts)
 
@@ -245,35 +277,23 @@
     picked(pick, half, tiles)
 
 
-def brought(matrix, tiles, name):
-    matrix, tiles = lax.optimization_barrier((matrix, tuple(tiles)))
-    (near,) = call(
-        load_kernel,
-        name,
-        [(matrix.shape, HALF)],
-        matrix,
-        far=1,
-        scratch=(pltpu.SemaphoreType.DMA((8,)),),
-    )
-    return near, tiles
-
-
-def passed_along(shard, axis, by):
+def partner(place, exchange):
+    odd = place % 2 if isinstance(place, int) else lax.rem(place, 2)
+    return place + 1 - 2 * odd if exchange == 0 else place - 1 + 2 * odd
+
+
+def swapped(shard, axis, exchange):
     devices = lax.axis_size(axis)
-    pairs = [(i, i + by) for i in range(devices) if 0 <= i + by < devices]
-    return lax.ppermute(shard, axis, pairs)
+    pairs = [(i, partner(i, exchange)) for i in range(devices)]
+    return lax.ppermute(shard, axis, [(i, j) for i, j in pairs if 0 <= j < devices])
 
 
 def traded_over_row(tiles):
-    return passed_along(tiles[1], "row", 1), passed_along(tiles[0], "row", -1)
+    return tuple(swapped(tiles[i], "row", i) for i in range(2))
 
 
 def traded(tiles):
-    return (
-        *traded_over_row(tiles),
-        passed_along(tiles[3], "col", 1),
-        passed_along(tiles[2], "col", -1),
-    )
+    return traded_over_row(tiles) + tuple(swapped(tiles[2 + i], "col", i) for i in range(2))
 
 
 def per_device(
@@ -296,7 +316,7 @@
     owned_half = ((own, columns), HALF)
     owned_full = ((own, columns), FULL)
     local_full = ((local, columns), FULL)
-    target, residual, pick, masked, inverse, *tiles = call(
+    target, residual, pick, masked, basis, inverse, *tiles = call(
         select_kernel,
         "select",
         [
@@ -304,18 +324,20 @@
             owned_half,
             ((margin, own), HALF),
             (rows_list.shape, jnp.int32),
+            (basis.shape, HALF),
             (inverse.shape, HALF),
         ]
         + four_tiles,
         target,
         rows_list,
         send_count[0],
+        basis,
         inverse,
-        far=4,
+        far=5,
         scratch=(
             pltpu.VMEM(rows_list.shape, jnp.int32),
             pltpu.SMEM((1, 4), jnp.int32),
-            pltpu.SemaphoreType.DMA((3 + 8,)),
+            pltpu.SemaphoreType.DMA((8 + MATRIX_PIECES,)),
         ),
         flops=2 * margin * own * columns,
     )
@@ -379,8 +401,6 @@
             residual,
             flops=2 * local * own * columns,
         )
-        if first:
-            (spread,) = call(spread_kernel, "spread", [((own, margin), HALF)], masked)
         (share,) = call(
             share_kernel,
             "share",
@@ -421,7 +441,16 @@
             flops=2 * coarse * margin * columns,
         )
         if first:
-            operator, tiles = brought(operator, tiles, "operator_load")
+            masked, tiles = lax.optimization_barrier((masked, tuple(tiles)))
+            spread, operator = call(
+                spread_kernel,
+                "spread",
+                [((own, margin), HALF), (operator.shape, HALF)],
+                operator,
+                masked,
+                far=1,
+                scratch=(pltpu.SemaphoreType.DMA((MATRIX_PIECES,)),),
+            )
         r0, r1, r2, r3 = traded(tiles)
         (base,) = call(
             base_kernel(first),

time: 197 us -> 162 us (0.82)
  starting transfers between devices: 98.2 us -> 64.8 us
    ppermute x34, starting transfers between devices: 98.2 us -> 64.8 us  [swapped(): lax.ppermute(shard, axis, [(i, j) for i, j in pairs if 0 <= j < devices])]
    all_to_all x3, blocking collectives: 28.5 us -> 25.1 us  [per_device(): parts = lax.all_to_all(parts, 'row', 0, 0, tiled=True)]
    all_gather x3, blocking collectives: 24.9 us -> 28.2 us  [per_device(): gathered = lax.all_gather(share, 'col', axis=0, tiled=True)]
    pallas_call x29 -> x28, Pallas kernels: 21.9 us -> 22.1 us  [call(): pl.pallas_call(body, out_shape=tuple(((pltpu.HBM if away else pltpu.VMEM)...]
  transfers between devices with their start and end apart: 34 -> 34, of which waited for: 10 -> 13; matrix products, arithmetic and copies ran while one was open for 0% -> 0% of each run, Pallas kernels for 5% -> 6%
where the time goes in v6:
time: 162 us; the launch traced here: 161 us
  starting transfers between devices  64.8 us (40%)
  blocking collectives  53.3 us (33%)
  Pallas kernels  22.1 us (14%)
  waiting for transfers between devices  20.5 us (13%)
    ppermute x34, starting transfers between devices, swapped(): lax.ppermute(shard, axis, [(i, j) for i, j in pairs if 0 <= j < devices])  64.8 us
    all_gather x3, blocking collectives, per_device(): gathered = lax.all_gather(share, 'col', axis=0, tiled=True)  28.2 us
    all_to_all x3, blocking collectives, per_device(): parts = lax.all_to_all(parts, 'row', 0, 0, tiled=True)  25.1 us
    pallas_call x28, Pallas kernels, call(): pl.pallas_call(body, out_shape=tuple(((pltpu.HBM if away else pltpu.VMEM)...  22.1 us
    ppermute x34, waiting for transfers between devices, swapped(): lax.ppermute(shard, axis, [(i, j) for i, j in pairs if 0 <= j < devices])  20.5 us
  transfers between devices with their start and end apart: 34, of which 13 were waited for; matrix products, arithmetic and copies ran while one was open for 0% of the time, Pallas kernels for 6%

profile of v6, /device:TPU:9, one launch (start us, length us, event | category | flops | bytes accessed | tf_op | source)
XLA Modules:
  0.0 161.4 jit_solution(16578430795635059778)
XLA Ops:
  0.0 3.0 %select.1 = (f32[1024,256]{1,0:T(8,128)S(1)}, bf16[1024,256]{1,0:T(8,128)(2,1)S(1)}, bf16[512,1024]{1,0:T(8,128)(2,1)S(1)}, s32[4,128]{1,0:T(4,128)S(1)}, bf16[3...) custom-call(f32[1024,256]{1,0:T(8,128)} %bitcast.11, ...), custom_call_target="tpu_custom_call" | custom-call | flops 268435456 | bytes 5867536 | tf_op jit(solution)/shard_map/select/pallas_call | solution.py:28
  3.1 1.3 collective-permute-start
  4.4 1.9 %collective-permute-start.1 = (bf16[128,256]{1,0:T(8,128)(2,1)S(1)}, bf16[128,256]{1,0:T(8,128)(2,1)S(1)}, u32[]{:S(2)}, u32[]{:S(2)}) collective-permute-start(bf16[128,256]{1,0:T(8,128)(2,1)S(1)} %get-tuple-element.83), channel_id=1, source_target_pairs={{4,8},{8,4},{12,16},{16,12},{20,24},{24,20},{5,9},{9,5},{13,17},{1... | collective-permute-start | bytes 196616 | tf_op jit(solution)/shard_map/ppermute | solution.py:288
  6.3 1.0 inverse_own.3.refs_1_
  7.3 3.0 %collective-permute-done.1.g1.refs_5_ = bf16[128,256]{1,0:T(8,128)(2,1)S(1)} collective-permute-done((bf16[128,256]{1,0:T(8,128)(2,1)S(1)}, bf16[128,256]{1,0:T(8,128)(2,1)S(1)}, u32[]{:S(2)}, u32[]{:S(2)}) %collective-permute-start.1) | collective-permute-done | bytes 65568 | tf_op jit(solution)/shard_map/ppermute | solution.py:288
  10.5 9.8 %all_gather.9.refs_2_ = bf16[1280,256]{1,0:T(8,128)(2,1)S(1)} all-gather(bf16[320,256]{1,0:T(8,128)(2,1)S(1)} %share.3), channel_id=1, replica_groups=mesh['row'=8,'col'=4] {'col'}, dimensions={0}, use_global_device_ids=true | all-gather | bytes 819200 | tf_op jit(solution)/shard_map/all_gather | solution.py:416
  21.2 9.1 %all_to_all.15.parts = bf16[8,32,256]{2,1,0:T(8,128)(2,1)S(1)} all-to-all(bf16[8,32,256]{2,1,0:T(8,128)(2,1)S(1)} %get-tuple-element.85), channel_id=1, replica_groups=mesh['row'=8,'col'=4] {'row'}, dimensions={0} | all-to-all | bytes 262144 | tf_op jit(solution)/shard_map/all_to_all | solution.py:433
  30.5 1.2 collective-permute-start.2
  31.7 3.6 %collective-permute-start.3 = (bf16[128,256]{1,0:T(8,128)(2,1)S(1)}, bf16[128,256]{1,0:T(8,128)(2,1)S(1)}, u32[]{:S(2)}, u32[]{:S(2)}) collective-permute-start(bf16[128,256]{1,0:T(8,128)(2,1)S(1)} %get-tuple-element.96), channel_id=1, source_target_pairs={{4,8},{8,4},{12,16},{16,12},{20,24},{24,20},{5,9},{9,5},{13,17},{1... | collective-permute-start | bytes 196616 | tf_op jit(solution)/shard_map/ppermute | solution.py:288
  35.3 2.4 %collective-permute-start.4 = (bf16[128,256]{1,0:T(8,128)(2,1)S(1)}, bf16[128,256]{1,0:T(8,128)(2,1)S(1)}, u32[]{:S(2)}, u32[]{:S(2)}) collective-permute-start(bf16[128,256]{1,0:T(8,128)(2,1)S(1)} %get-tuple-element.98), channel_id=1, source_target_pairs={{0,1},{1,0},{2,3},{3,2},{4,5},{5,4},{6,7},{7,6},{8,9},{9,8},{10,11... | collective-permute-start | bytes 196616 | tf_op jit(solution)/shard_map/ppermute | solution.py:288
  37.7 2.1 %collective-permute-start.5 = (bf16[128,256]{1,0:T(8,128)(2,1)S(1)}, bf16[128,256]{1,0:T(8,128)(2,1)S(1)}, u32[]{:S(2)}, u32[]{:S(2)}) collective-permute-start(bf16[128,256]{1,0:T(8,128)(2,1)S(1)} %get-tuple-element.99), channel_id=1, source_target_pairs={{1,2},{2,1},{5,6},{6,5},{9,10},{10,9},{13,14},{14,13},{17,18},{18,... | collective-permute-start | bytes 196616 | tf_op jit(solution)/shard_map/ppermute | solution.py:288
  39.8 2.6 %spread.1 = (bf16[1024,512]{1,0:T(8,128)(2,1)S(1)}, bf16[1536,1536]{1,0:T(8,128)(2,1)S(1)}) custom-call(bf16[1536,1536]{1,0:T(8,128)(2,1)} %bitcast.10, s32[4,128]{1,0:T(4,128)S(1)} %get-tuple-element.93.masked), custom_call_target="tpu_custom_call" | custom-call | bytes 4720640 | tf_op jit(solution)/shard_map/spread/pallas_call | solution.py:28
  44.2 2.4 %collective-permute-start.7 = (bf16[128,256]{1,0:T(8,128)(2,1)S(1)}, bf16[128,256]{1,0:T(8,128)(2,1)S(1)}, u32[]{:S(2)}, u32[]{:S(2)}) collective-permute-start(bf16[128,256]{1,0:T(8,128)(2,1)S(1)} %get-tuple-element.106), channel_id=1, source_target_pairs={{4,8},{8,4},{12,16},{16,12},{20,24},{24,20},{5,9},{9,5},{13,17},{1... | collective-permute-start | bytes 196616 | tf_op jit(solution)/shard_map/ppermute | solution.py:288
  46.7 3.4 %collective-permute-start.9 = (bf16[128,256]{1,0:T(8,128)(2,1)S(1)}, bf16[128,256]{1,0:T(8,128)(2,1)S(1)}, u32[]{:S(2)}, u32[]{:S(2)}) collective-permute-start(bf16[128,256]{1,0:T(8,128)(2,1)S(1)} %get-tuple-element.108), channel_id=1, source_target_pairs={{1,2},{2,1},{5,6},{6,5},{9,10},{10,9},{13,14},{14,13},{17,18},{18,... | collective-permute-start | bytes 196616 | tf_op jit(solution)/shard_map/ppermute | solution.py:288
  50.1 1.2 operator_near.2.partial
  52.5 1.3 collective-permute-start.10
  53.8 2.6 %collective-permute-start.11 = (bf16[128,256]{1,0:T(8,128)(2,1)S(1)}, bf16[128,256]{1,0:T(8,128)(2,1)S(1)}, u32[]{:S(2)}, u32[]{:S(2)}) collective-permute-start(bf16[128,256]{1,0:T(8,128)(2,1)S(1)} %get-tuple-element.110), channel_id=1, source_target_pairs={{4,8},{8,4},{12,16},{16,12},{20,24},{24,20},{5,9},{9,5},{13,17},{1... | collective-permute-start | bytes 196616 | tf_op jit(solution)/shard_map/ppermute | solution.py:288
  56.5 3.6 %collective-permute-start.13 = (bf16[128,256]{1,0:T(8,128)(2,1)S(1)}, bf16[128,256]{1,0:T(8,128)(2,1)S(1)}, u32[]{:S(2)}, u32[]{:S(2)}) collective-permute-start(bf16[128,256]{1,0:T(8,128)(2,1)S(1)} %get-tuple-element.112), channel_id=1, source_target_pairs={{1,2},{2,1},{5,6},{6,5},{9,10},{10,9},{13,14},{14,13},{17,18},{18,... | collective-permute-start | bytes 196616 | tf_op jit(solution)/shard_map/ppermute | solution.py:288
  60.6 1.5 collective-permute-done.13.r3
  62.9 1.8 %collective-permute-start.14 = (bf16[128,256]{1,0:T(8,128)(2,1)S(1)}, bf16[128,256]{1,0:T(8,128)(2,1)S(1)}, u32[]{:S(2)}, u32[]{:S(2)}) collective-permute-start(bf16[128,256]{1,0:T(8,128)(2,1)S(1)} %get-tuple-element.116), channel_id=1, source_target_pairs={{0,4},{4,0},{8,12},{12,8},{16,20},{20,16},{24,28},{28,24},{1,5},{5... | collective-permute-start | bytes 196616 | tf_op jit(solution)/shard_map/ppermute | solution.py:288
  64.7 2.9 %collective-permute-start.15 = (bf16[128,256]{1,0:T(8,128)(2,1)S(1)}, bf16[128,256]{1,0:T(8,128)(2,1)S(1)}, u32[]{:S(2)}, u32[]{:S(2)}) collective-permute-start(bf16[128,256]{1,0:T(8,128)(2,1)S(1)} %get-tuple-element.117), channel_id=1, source_target_pairs={{4,8},{8,4},{12,16},{16,12},{20,24},{24,20},{5,9},{9,5},{13,17},{1... | collective-permute-start | bytes 196616 | tf_op jit(solution)/shard_map/ppermute | solution.py:288
  67.6 1.0 inverse_own.4.refs_2_
  68.6 2.0 %collective-permute-done.15.g1.refs_6_ = bf16[128,256]{1,0:T(8,128)(2,1)S(1)} collective-permute-done((bf16[128,256]{1,0:T(8,128)(2,1)S(1)}, bf16[128,256]{1,0:T(8,128)(2,1)S(1)}, u32[]{:S(2)}, u32[]{:S(2)}) %collective-permute-start.15) | collective-permute-done | bytes 65568 | tf_op jit(solution)/shard_map/ppermute | solution.py:288
  70.8 9.5 %all_gather.10.refs_3_ = bf16[1152,256]{1,0:T(8,128)(2,1)S(1)} all-gather(bf16[288,256]{1,0:T(8,128)(2,1)S(1)} %share.4), channel_id=1, replica_groups=mesh['row'=8,'col'=4] {'col'}, dimensions={0}, use_global_device_ids=true | all-gather | bytes 737280 | tf_op jit(solution)/shard_map/all_gather | solution.py:416
  81.1 8.0 %all_to_all.16.parts = bf16[8,32,256]{2,1,0:T(8,128)(2,1)S(1)} all-to-all(bf16[8,32,256]{2,1,0:T(8,128)(2,1)S(1)} %get-tuple-element.119), channel_id=1, replica_groups=mesh['row'=8,'col'=4] {'row'}, dimensions={0} | all-to-all | bytes 262144 | tf_op jit(solution)/shard_map/all_to_all | solution.py:433
  89.3 1.1 collective-permute-start.16
  90.5 3.6 %collective-permute-start.17 = (bf16[128,256]{1,0:T(8,128)(2,1)S(1)}, bf16[128,256]{1,0:T(8,128)(2,1)S(1)}, u32[]{:S(2)}, u32[]{:S(2)}) collective-permute-start(bf16[128,256]{1,0:T(8,128)(2,1)S(1)} %get-tuple-element.123), channel_id=1, source_target_pairs={{4,8},{8,4},{12,16},{16,12},{20,24},{24,20},{5,9},{9,5},{13,17},{1... | collective-permute-start | bytes 196616 | tf_op jit(solution)/shard_map/ppermute | solution.py:288
  94.1 2.4 %collective-permute-start.18 = (bf16[128,256]{1,0:T(8,128)(2,1)S(1)}, bf16[128,256]{1,0:T(8,128)(2,1)S(1)}, u32[]{:S(2)}, u32[]{:S(2)}) collective-permute-start(bf16[128,256]{1,0:T(8,128)(2,1)S(1)} %get-tuple-element.124), channel_id=1, source_target_pairs={{0,1},{1,0},{2,3},{3,2},{4,5},{5,4},{6,7},{7,6},{8,9},{9,8},{10,11... | collective-permute-start | bytes 196616 | tf_op jit(solution)/shard_map/ppermute | solution.py:288
  96.5 2.2 %collective-permute-start.19 = (bf16[128,256]{1,0:T(8,128)(2,1)S(1)}, bf16[128,256]{1,0:T(8,128)(2,1)S(1)}, u32[]{:S(2)}, u32[]{:S(2)}) collective-permute-start(bf16[128,256]{1,0:T(8,128)(2,1)S(1)} %get-tuple-element.125), channel_id=1, source_target_pairs={{1,2},{2,1},{5,6},{6,5},{9,10},{10,9},{13,14},{14,13},{17,18},{18,... | collective-permute-start | bytes 196616 | tf_op jit(solution)/shard_map/ppermute | solution.py:288
  99.2 2.9 %collective-permute-done.19.r3 = bf16[128,256]{1,0:T(8,128)(2,1)S(1)} collective-permute-done((bf16[128,256]{1,0:T(8,128)(2,1)S(1)}, bf16[128,256]{1,0:T(8,128)(2,1)S(1)}, u32[]{:S(2)}, u32[]{:S(2)}) %collective-permute-start.19) | collective-permute-done | bytes 65568 | tf_op jit(solution)/shard_map/ppermute | solution.py:288
  103.0 2.4 %collective-permute-start.21 = (bf16[128,256]{1,0:T(8,128)(2,1)S(1)}, bf16[128,256]{1,0:T(8,128)(2,1)S(1)}, u32[]{:S(2)}, u32[]{:S(2)}) collective-permute-start(bf16[128,256]{1,0:T(8,128)(2,1)S(1)} %get-tuple-element.129), channel_id=1, source_target_pairs={{4,8},{8,4},{12,16},{16,12},{20,24},{24,20},{5,9},{9,5},{13,17},{1... | collective-permute-start | bytes 196616 | tf_op jit(solution)/shard_map/ppermute | solution.py:288
  105.5 2.7 %collective-permute-start.23 = (bf16[128,256]{1,0:T(8,128)(2,1)S(1)}, bf16[128,256]{1,0:T(8,128)(2,1)S(1)}, u32[]{:S(2)}, u32[]{:S(2)}) collective-permute-start(bf16[128,256]{1,0:T(8,128)(2,1)S(1)} %get-tuple-element.131), channel_id=1, source_target_pairs={{1,2},{2,1},{5,6},{6,5},{9,10},{10,9},{13,14},{14,13},{17,18},{18,... | collective-permute-start | bytes 196616 | tf_op jit(solution)/shard_map/ppermute | solution.py:288
  108.9 1.2 operator_near.3.partial
  111.3 1.3 collective-permute-start.24
  112.6 2.6 %collective-permute-start.25 = (bf16[128,256]{1,0:T(8,128)(2,1)S(1)}, bf16[128,256]{1,0:T(8,128)(2,1)S(1)}, u32[]{:S(2)}, u32[]{:S(2)}) collective-permute-start(bf16[128,256]{1,0:T(8,128)(2,1)S(1)} %get-tuple-element.133), channel_id=1, source_target_pairs={{4,8},{8,4},{12,16},{16,12},{20,24},{24,20},{5,9},{9,5},{13,17},{1... | collective-permute-start | bytes 196616 | tf_op jit(solution)/shard_map/ppermute | solution.py:288
  115.3 2.8 %collective-permute-start.27 = (bf16[128,256]{1,0:T(8,128)(2,1)S(1)}, bf16[128,256]{1,0:T(8,128)(2,1)S(1)}, u32[]{:S(2)}, u32[]{:S(2)}) collective-permute-start(bf16[128,256]{1,0:T(8,128)(2,1)S(1)} %get-tuple-element.135), channel_id=1, source_target_pairs={{1,2},{2,1},{5,6},{6,5},{9,10},{10,9},{13,14},{14,13},{17,18},{18,... | collective-permute-start | bytes 196616 | tf_op jit(solution)/shard_map/ppermute | solution.py:288
  118.9 1.9 %collective-permute-done.27.r3 = bf16[128,256]{1,0:T(8,128)(2,1)S(1)} collective-permute-done((bf16[128,256]{1,0:T(8,128)(2,1)S(1)}, bf16[128,256]{1,0:T(8,128)(2,1)S(1)}, u32[]{:S(2)}, u32[]{:S(2)}) %collective-permute-start.27) | collective-permute-done | bytes 65568 | tf_op jit(solution)/shard_map/ppermute | solution.py:288
  121.7 1.5 collective-permute-start.28
  123.2 2.2 %collective-permute-start.29 = (bf16[128,256]{1,0:T(8,128)(2,1)S(1)}, bf16[128,256]{1,0:T(8,128)(2,1)S(1)}, u32[]{:S(2)}, u32[]{:S(2)}) collective-permute-start(bf16[128,256]{1,0:T(8,128)(2,1)S(1)} %get-tuple-element.140), channel_id=1, source_target_pairs={{4,8},{8,4},{12,16},{16,12},{20,24},{24,20},{5,9},{9,5},{13,17},{1... | collective-permute-start | bytes 196616 | tf_op jit(solution)/shard_map/ppermute | solution.py:288
  126.4 2.7 %collective-permute-done.29.g1.refs_6_ = bf16[128,256]{1,0:T(8,128)(2,1)S(1)} collective-permute-done((bf16[128,256]{1,0:T(8,128)(2,1)S(1)}, bf16[128,256]{1,0:T(8,128)(2,1)S(1)}, u32[]{:S(2)}, u32[]{:S(2)}) %collective-permute-start.29) | collective-permute-done | bytes 65568 | tf_op jit(solution)/shard_map/ppermute | solution.py:288
  129.3 8.8 %all_gather.11.refs_3_ = bf16[1152,256]{1,0:T(8,128)(2,1)S(1)} all-gather(bf16[288,256]{1,0:T(8,128)(2,1)S(1)} %share.5), channel_id=1, replica_groups=mesh['row'=8,'col'=4] {'col'}, dimensions={0}, use_global_device_ids=true | all-gather | bytes 737280 | tf_op jit(solution)/shard_map/all_gather | solution.py:416
  139.0 8.0 %all_to_all.17.parts = bf16[8,32,256]{2,1,0:T(8,128)(2,1)S(1)} all-to-all(bf16[8,32,256]{2,1,0:T(8,128)(2,1)S(1)} %get-tuple-element.142), channel_id=1, replica_groups=mesh['row'=8,'col'=4] {'row'}, dimensions={0} | all-to-all | bytes 262144 | tf_op jit(solution)/shard_map/all_to_all | solution.py:433
  147.3 1.1 collective-permute-start.30
  148.4 3.6 %collective-permute-start.31 = (bf16[128,256]{1,0:T(8,128)(2,1)S(1)}, bf16[128,256]{1,0:T(8,128)(2,1)S(1)}, u32[]{:S(2)}, u32[]{:S(2)}) collective-permute-start(bf16[128,256]{1,0:T(8,128)(2,1)S(1)} %get-tuple-element.146), channel_id=1, source_target_pairs={{4,8},{8,4},{12,16},{16,12},{20,24},{24,20},{5,9},{9,5},{13,17},{1... | collective-permute-start | bytes 196616 | tf_op jit(solution)/shard_map/ppermute | solution.py:288
  152.0 2.4 %collective-permute-start.32 = (bf16[128,256]{1,0:T(8,128)(2,1)S(1)}, bf16[128,256]{1,0:T(8,128)(2,1)S(1)}, u32[]{:S(2)}, u32[]{:S(2)}) collective-permute-start(bf16[128,256]{1,0:T(8,128)(2,1)S(1)} %get-tuple-element.147), channel_id=1, source_target_pairs={{0,1},{1,0},{2,3},{3,2},{4,5},{5,4},{6,7},{7,6},{8,9},{9,8},{10,11... | collective-permute-start | bytes 196616 | tf_op jit(solution)/shard_map/ppermute | solution.py:288
  154.4 2.2 %collective-permute-start.33 = (bf16[128,256]{1,0:T(8,128)(2,1)S(1)}, bf16[128,256]{1,0:T(8,128)(2,1)S(1)}, u32[]{:S(2)}, u32[]{:S(2)}) collective-permute-start(bf16[128,256]{1,0:T(8,128)(2,1)S(1)} %get-tuple-element.148), channel_id=1, source_target_pairs={{1,2},{2,1},{5,6},{6,5},{9,10},{10,9},{13,14},{14,13},{17,18},{18,... | collective-permute-start | bytes 196616 | tf_op jit(solution)/shard_map/ppermute | solution.py:288
  157.1 2.9 %collective-permute-done.33.r3 = bf16[128,256]{1,0:T(8,128)(2,1)S(1)} collective-permute-done((bf16[128,256]{1,0:T(8,128)(2,1)S(1)}, bf16[128,256]{1,0:T(8,128)(2,1)S(1)}, u32[]{:S(2)}, u32[]{:S(2)}) %collective-permute-start.33) | collective-permute-done | bytes 65568 | tf_op jit(solution)/shard_map/ppermute | solution.py:288
  160.0 1.2 last_update.1
  (56 shorter events, 15.0 us)
Async XLA Ops:
  3.1 4.2 %collective-permute-start = (bf16[128,256]{1,0:T(8,128)(2,1)S(1)}, bf16[128,256]{1,0:T(8,128)(2,1)S(1)}, u32[]{:S(2)}, u32[]{:S(2)}) collective-permute-start(bf16[128,256]{1,0:T(8,128)(2,1)S(1)} %get-tuple-element.82), channel_id=1, source_target_pairs={{0,4},{4,0},{8,12},{12,8},{16,20},{20,16},{24,28},{28,24},{1,5},{5... | collective-permute-start | bytes 196616 | tf_op jit(solution)/shard_map/ppermute | solution.py:288
  4.4 5.9 %collective-permute-start.1 = (bf16[128,256]{1,0:T(8,128)(2,1)S(1)}, bf16[128,256]{1,0:T(8,128)(2,1)S(1)}, u32[]{:S(2)}, u32[]{:S(2)}) collective-permute-start(bf16[128,256]{1,0:T(8,128)(2,1)S(1)} %get-tuple-element.83), channel_id=1, source_target_pairs={{4,8},{8,4},{12,16},{16,12},{20,24},{24,20},{5,9},{9,5},{13,17},{1... | collective-permute-start | bytes 196616 | tf_op jit(solution)/shard_map/ppermute | solution.py:288
  7.3 13.1 %copy-start = (bf16[8,32,128]{2,1,0:T(8,128)(2,1)S(1)}, bf16[8,32,128]{2,1,0:T(8,128)(2,1)}, u32[]{:S(2)}) copy-start(bf16[8,32,128]{2,1,0:T(8,128)(2,1)} %refs_4_.3) | copy-start | bytes 196612
  30.5 11.8 %collective-permute-start.2 = (bf16[128,256]{1,0:T(8,128)(2,1)S(1)}, bf16[128,256]{1,0:T(8,128)(2,1)S(1)}, u32[]{:S(2)}, u32[]{:S(2)}) collective-permute-start(bf16[128,256]{1,0:T(8,128)(2,1)S(1)} %get-tuple-element.95), channel_id=1, source_target_pairs={{0,4},{4,0},{8,12},{12,8},{16,20},{20,16},{24,28},{28,24},{1,5},{5... | collective-permute-start | bytes 196616 | tf_op jit(solution)/shard_map/ppermute | solution.py:288
  31.7 10.7 %collective-permute-start.3 = (bf16[128,256]{1,0:T(8,128)(2,1)S(1)}, bf16[128,256]{1,0:T(8,128)(2,1)S(1)}, u32[]{:S(2)}, u32[]{:S(2)}) collective-permute-start(bf16[128,256]{1,0:T(8,128)(2,1)S(1)} %get-tuple-element.96), channel_id=1, source_target_pairs={{4,8},{8,4},{12,16},{16,12},{20,24},{24,20},{5,9},{9,5},{13,17},{1... | collective-permute-start | bytes 196616 | tf_op jit(solution)/shard_map/ppermute | solution.py:288
  35.3 7.5 %collective-permute-start.4 = (bf16[128,256]{1,0:T(8,128)(2,1)S(1)}, bf16[128,256]{1,0:T(8,128)(2,1)S(1)}, u32[]{:S(2)}, u32[]{:S(2)}) collective-permute-start(bf16[128,256]{1,0:T(8,128)(2,1)S(1)} %get-tuple-element.98), channel_id=1, source_target_pairs={{0,1},{1,0},{2,3},{3,2},{4,5},{5,4},{6,7},{7,6},{8,9},{9,8},{10,11... | collective-permute-start | bytes 196616 | tf_op jit(solution)/shard_map/ppermute | solution.py:288
  37.7 5.6 %collective-permute-start.5 = (bf16[128,256]{1,0:T(8,128)(2,1)S(1)}, bf16[128,256]{1,0:T(8,128)(2,1)S(1)}, u32[]{:S(2)}, u32[]{:S(2)}) collective-permute-start(bf16[128,256]{1,0:T(8,128)(2,1)S(1)} %get-tuple-element.99), channel_id=1, source_target_pairs={{1,2},{2,1},{5,6},{6,5},{9,10},{10,9},{13,14},{14,13},{17,18},{18,... | collective-permute-start | bytes 196616 | tf_op jit(solution)/shard_map/ppermute | solution.py:288
  44.1 5.9 %collective-permute-start.6 = (bf16[128,256]{1,0:T(8,128)(2,1)S(1)}, bf16[128,256]{1,0:T(8,128)(2,1)S(1)}, u32[]{:S(2)}, u32[]{:S(2)}) collective-permute-start(bf16[128,256]{1,0:T(8,128)(2,1)S(1)} %get-tuple-element.105), channel_id=1, source_target_pairs={{0,4},{4,0},{8,12},{12,8},{16,20},{20,16},{24,28},{28,24},{1,5},{5... | collective-permute-start | bytes 196616 | tf_op jit(solution)/shard_map/ppermute | solution.py:288
  44.2 5.9 %collective-permute-start.7 = (bf16[128,256]{1,0:T(8,128)(2,1)S(1)}, bf16[128,256]{1,0:T(8,128)(2,1)S(1)}, u32[]{:S(2)}, u32[]{:S(2)}) collective-permute-start(bf16[128,256]{1,0:T(8,128)(2,1)S(1)} %get-tuple-element.106), channel_id=1, source_target_pairs={{4,8},{8,4},{12,16},{16,12},{20,24},{24,20},{5,9},{9,5},{13,17},{1... | collective-permute-start | bytes 196616 | tf_op jit(solution)/shard_map/ppermute | solution.py:288
  46.6 4.7 %collective-permute-start.8 = (bf16[128,256]{1,0:T(8,128)(2,1)S(1)}, bf16[128,256]{1,0:T(8,128)(2,1)S(1)}, u32[]{:S(2)}, u32[]{:S(2)}) collective-permute-start(bf16[128,256]{1,0:T(8,128)(2,1)S(1)} %get-tuple-element.107), channel_id=1, source_target_pairs={{0,1},{1,0},{2,3},{3,2},{4,5},{5,4},{6,7},{7,6},{8,9},{9,8},{10,11... | collective-permute-start | bytes 196616 | tf_op jit(solution)/shard_map/ppermute | solution.py:288
  46.7 5.6 %collective-permute-start.9 = (bf16[128,256]{1,0:T(8,128)(2,1)S(1)}, bf16[128,256]{1,0:T(8,128)(2,1)S(1)}, u32[]{:S(2)}, u32[]{:S(2)}) collective-permute-start(bf16[128,256]{1,0:T(8,128)(2,1)S(1)} %get-tuple-element.108), channel_id=1, source_target_pairs={{1,2},{2,1},{5,6},{6,5},{9,10},{10,9},{13,14},{14,13},{17,18},{18,... | collective-permute-start | bytes 196616 | tf_op jit(solution)/shard_map/ppermute | solution.py:288
  52.5 7.6 %collective-permute-start.10 = (bf16[128,256]{1,0:T(8,128)(2,1)S(1)}, bf16[128,256]{1,0:T(8,128)(2,1)S(1)}, u32[]{:S(2)}, u32[]{:S(2)}) collective-permute-start(bf16[128,256]{1,0:T(8,128)(2,1)S(1)} %get-tuple-element.109), channel_id=1, source_target_pairs={{0,4},{4,0},{8,12},{12,8},{16,20},{20,16},{24,28},{28,24},{1,5},{5... | collective-permute-start | bytes 196616 | tf_op jit(solution)/shard_map/ppermute | solution.py:288
  53.8 6.3 %collective-permute-start.11 = (bf16[128,256]{1,0:T(8,128)(2,1)S(1)}, bf16[128,256]{1,0:T(8,128)(2,1)S(1)}, u32[]{:S(2)}, u32[]{:S(2)}) collective-permute-start(bf16[128,256]{1,0:T(8,128)(2,1)S(1)} %get-tuple-element.110), channel_id=1, source_target_pairs={{4,8},{8,4},{12,16},{16,12},{20,24},{24,20},{5,9},{9,5},{13,17},{1... | collective-permute-start | bytes 196616 | tf_op jit(solution)/shard_map/ppermute | solution.py:288
  56.4 4.2 %collective-permute-start.12 = (bf16[128,256]{1,0:T(8,128)(2,1)S(1)}, bf16[128,256]{1,0:T(8,128)(2,1)S(1)}, u32[]{:S(2)}, u32[]{:S(2)}) collective-permute-start(bf16[128,256]{1,0:T(8,128)(2,1)S(1)} %get-tuple-element.111), channel_id=1, source_target_pairs={{0,1},{1,0},{2,3},{3,2},{4,5},{5,4},{6,7},{7,6},{8,9},{9,8},{10,11... | collective-permute-start | bytes 196616 | tf_op jit(solution)/shard_map/ppermute | solution.py:288
  56.5 5.6 %collective-permute-start.13 = (bf16[128,256]{1,0:T(8,128)(2,1)S(1)}, bf16[128,256]{1,0:T(8,128)(2,1)S(1)}, u32[]{:S(2)}, u32[]{:S(2)}) collective-permute-start(bf16[128,256]{1,0:T(8,128)(2,1)S(1)} %get-tuple-element.112), channel_id=1, source_target_pairs={{1,2},{2,1},{5,6},{6,5},{9,10},{10,9},{13,14},{14,13},{17,18},{18,... | collective-permute-start | bytes 196616 | tf_op jit(solution)/shard_map/ppermute | solution.py:288
  62.9 5.7 %collective-permute-start.14 = (bf16[128,256]{1,0:T(8,128)(2,1)S(1)}, bf16[128,256]{1,0:T(8,128)(2,1)S(1)}, u32[]{:S(2)}, u32[]{:S(2)}) collective-permute-start(bf16[128,256]{1,0:T(8,128)(2,1)S(1)} %get-tuple-element.116), channel_id=1, source_target_pairs={{0,4},{4,0},{8,12},{12,8},{16,20},{20,16},{24,28},{28,24},{1,5},{5... | collective-permute-start | bytes 196616 | tf_op jit(solution)/shard_map/ppermute | solution.py:288
  64.7 5.9 %collective-permute-start.15 = (bf16[128,256]{1,0:T(8,128)(2,1)S(1)}, bf16[128,256]{1,0:T(8,128)(2,1)S(1)}, u32[]{:S(2)}, u32[]{:S(2)}) collective-permute-start(bf16[128,256]{1,0:T(8,128)(2,1)S(1)} %get-tuple-element.117), channel_id=1, source_target_pairs={{4,8},{8,4},{12,16},{16,12},{20,24},{24,20},{5,9},{9,5},{13,17},{1... | collective-permute-start | bytes 196616 | tf_op jit(solution)/shard_map/ppermute | solution.py:288
  89.3 9.3 %collective-permute-start.16 = (bf16[128,256]{1,0:T(8,128)(2,1)S(1)}, bf16[128,256]{1,0:T(8,128)(2,1)S(1)}, u32[]{:S(2)}, u32[]{:S(2)}) collective-permute-start(bf16[128,256]{1,0:T(8,128)(2,1)S(1)} %get-tuple-element.122), channel_id=1, source_target_pairs={{0,4},{4,0},{8,12},{12,8},{16,20},{20,16},{24,28},{28,24},{1,5},{5... | collective-permute-start | bytes 196616 | tf_op jit(solution)/shard_map/ppermute | solution.py:288
  90.5 8.2 %collective-permute-start.17 = (bf16[128,256]{1,0:T(8,128)(2,1)S(1)}, bf16[128,256]{1,0:T(8,128)(2,1)S(1)}, u32[]{:S(2)}, u32[]{:S(2)}) collective-permute-start(bf16[128,256]{1,0:T(8,128)(2,1)S(1)} %get-tuple-element.123), channel_id=1, source_target_pairs={{4,8},{8,4},{12,16},{16,12},{20,24},{24,20},{5,9},{9,5},{13,17},{1... | collective-permute-start | bytes 196616 | tf_op jit(solution)/shard_map/ppermute | solution.py:288
  94.1 5.1 %collective-permute-start.18 = (bf16[128,256]{1,0:T(8,128)(2,1)S(1)}, bf16[128,256]{1,0:T(8,128)(2,1)S(1)}, u32[]{:S(2)}, u32[]{:S(2)}) collective-permute-start(bf16[128,256]{1,0:T(8,128)(2,1)S(1)} %get-tuple-element.124), channel_id=1, source_target_pairs={{0,1},{1,0},{2,3},{3,2},{4,5},{5,4},{6,7},{7,6},{8,9},{9,8},{10,11... | collective-permute-start | bytes 196616 | tf_op jit(solution)/shard_map/ppermute | solution.py:288
  96.5 5.6 %collective-permute-start.19 = (bf16[128,256]{1,0:T(8,128)(2,1)S(1)}, bf16[128,256]{1,0:T(8,128)(2,1)S(1)}, u32[]{:S(2)}, u32[]{:S(2)}) collective-permute-start(bf16[128,256]{1,0:T(8,128)(2,1)S(1)} %get-tuple-element.125), channel_id=1, source_target_pairs={{1,2},{2,1},{5,6},{6,5},{9,10},{10,9},{13,14},{14,13},{17,18},{18,... | collective-permute-start | bytes 196616 | tf_op jit(solution)/shard_map/ppermute | solution.py:288
  102.9 5.2 %collective-permute-start.20 = (bf16[128,256]{1,0:T(8,128)(2,1)S(1)}, bf16[128,256]{1,0:T(8,128)(2,1)S(1)}, u32[]{:S(2)}, u32[]{:S(2)}) collective-permute-start(bf16[128,256]{1,0:T(8,128)(2,1)S(1)} %get-tuple-element.128), channel_id=1, source_target_pairs={{0,4},{4,0},{8,12},{12,8},{16,20},{20,16},{24,28},{28,24},{1,5},{5... | collective-permute-start | bytes 196616 | tf_op jit(solution)/shard_map/ppermute | solution.py:288
  103.0 5.9 %collective-permute-start.21 = (bf16[128,256]{1,0:T(8,128)(2,1)S(1)}, bf16[128,256]{1,0:T(8,128)(2,1)S(1)}, u32[]{:S(2)}, u32[]{:S(2)}) collective-permute-start(bf16[128,256]{1,0:T(8,128)(2,1)S(1)} %get-tuple-element.129), channel_id=1, source_target_pairs={{4,8},{8,4},{12,16},{16,12},{20,24},{24,20},{5,9},{9,5},{13,17},{1... | collective-permute-start | bytes 196616 | tf_op jit(solution)/shard_map/ppermute | solution.py:288
  105.4 4.7 %collective-permute-start.22 = (bf16[128,256]{1,0:T(8,128)(2,1)S(1)}, bf16[128,256]{1,0:T(8,128)(2,1)S(1)}, u32[]{:S(2)}, u32[]{:S(2)}) collective-permute-start(bf16[128,256]{1,0:T(8,128)(2,1)S(1)} %get-tuple-element.130), channel_id=1, source_target_pairs={{0,1},{1,0},{2,3},{3,2},{4,5},{5,4},{6,7},{7,6},{8,9},{9,8},{10,11... | collective-permute-start | bytes 196616 | tf_op jit(solution)/shard_map/ppermute | solution.py:288
  105.5 5.6 %collective-permute-start.23 = (bf16[128,256]{1,0:T(8,128)(2,1)S(1)}, bf16[128,256]{1,0:T(8,128)(2,1)S(1)}, u32[]{:S(2)}, u32[]{:S(2)}) collective-permute-start(bf16[128,256]{1,0:T(8,128)(2,1)S(1)} %get-tuple-element.131), channel_id=1, source_target_pairs={{1,2},{2,1},{5,6},{6,5},{9,10},{10,9},{13,14},{14,13},{17,18},{18,... | collective-permute-start | bytes 196616 | tf_op jit(solution)/shard_map/ppermute | solution.py:288
  111.3 6.7 %collective-permute-start.24 = (bf16[128,256]{1,0:T(8,128)(2,1)S(1)}, bf16[128,256]{1,0:T(8,128)(2,1)S(1)}, u32[]{:S(2)}, u32[]{:S(2)}) collective-permute-start(bf16[128,256]{1,0:T(8,128)(2,1)S(1)} %get-tuple-element.132), channel_id=1, source_target_pairs={{0,4},{4,0},{8,12},{12,8},{16,20},{20,16},{24,28},{28,24},{1,5},{5... | collective-permute-start | bytes 196616 | tf_op jit(solution)/shard_map/ppermute | solution.py:288
  112.6 5.9 %collective-permute-start.25 = (bf16[128,256]{1,0:T(8,128)(2,1)S(1)}, bf16[128,256]{1,0:T(8,128)(2,1)S(1)}, u32[]{:S(2)}, u32[]{:S(2)}) collective-permute-start(bf16[128,256]{1,0:T(8,128)(2,1)S(1)} %get-tuple-element.133), channel_id=1, source_target_pairs={{4,8},{8,4},{12,16},{16,12},{20,24},{24,20},{5,9},{9,5},{13,17},{1... | collective-permute-start | bytes 196616 | tf_op jit(solution)/shard_map/ppermute | solution.py:288
  115.2 3.7 %collective-permute-start.26 = (bf16[128,256]{1,0:T(8,128)(2,1)S(1)}, bf16[128,256]{1,0:T(8,128)(2,1)S(1)}, u32[]{:S(2)}, u32[]{:S(2)}) collective-permute-start(bf16[128,256]{1,0:T(8,128)(2,1)S(1)} %get-tuple-element.134), channel_id=1, source_target_pairs={{0,1},{1,0},{2,3},{3,2},{4,5},{5,4},{6,7},{7,6},{8,9},{9,8},{10,11... | collective-permute-start | bytes 196616 | tf_op jit(solution)/shard_map/ppermute | solution.py:288
  115.3 5.6 %collective-permute-start.27 = (bf16[128,256]{1,0:T(8,128)(2,1)S(1)}, bf16[128,256]{1,0:T(8,128)(2,1)S(1)}, u32[]{:S(2)}, u32[]{:S(2)}) collective-permute-start(bf16[128,256]{1,0:T(8,128)(2,1)S(1)} %get-tuple-element.135), channel_id=1, source_target_pairs={{1,2},{2,1},{5,6},{6,5},{9,10},{10,9},{13,14},{14,13},{17,18},{18,... | collective-permute-start | bytes 196616 | tf_op jit(solution)/shard_map/ppermute | solution.py:288
  121.7 4.7 %collective-permute-start.28 = (bf16[128,256]{1,0:T(8,128)(2,1)S(1)}, bf16[128,256]{1,0:T(8,128)(2,1)S(1)}, u32[]{:S(2)}, u32[]{:S(2)}) collective-permute-start(bf16[128,256]{1,0:T(8,128)(2,1)S(1)} %get-tuple-element.139), channel_id=1, source_target_pairs={{0,4},{4,0},{8,12},{12,8},{16,20},{20,16},{24,28},{28,24},{1,5},{5... | collective-permute-start | bytes 196616 | tf_op jit(solution)/shard_map/ppermute | solution.py:288
  123.2 5.9 %collective-permute-start.29 = (bf16[128,256]{1,0:T(8,128)(2,1)S(1)}, bf16[128,256]{1,0:T(8,128)(2,1)S(1)}, u32[]{:S(2)}, u32[]{:S(2)}) collective-permute-start(bf16[128,256]{1,0:T(8,128)(2,1)S(1)} %get-tuple-element.140), channel_id=1, source_target_pairs={{4,8},{8,4},{12,16},{16,12},{20,24},{24,20},{5,9},{9,5},{13,17},{1... | collective-permute-start | bytes 196616 | tf_op jit(solution)/shard_map/ppermute | solution.py:288
  147.3 9.3 %collective-permute-start.30 = (bf16[128,256]{1,0:T(8,128)(2,1)S(1)}, bf16[128,256]{1,0:T(8,128)(2,1)S(1)}, u32[]{:S(2)}, u32[]{:S(2)}) collective-permute-start(bf16[128,256]{1,0:T(8,128)(2,1)S(1)} %get-tuple-element.145), channel_id=1, source_target_pairs={{0,4},{4,0},{8,12},{12,8},{16,20},{20,16},{24,28},{28,24},{1,5},{5... | collective-permute-start | bytes 196616 | tf_op jit(solution)/shard_map/ppermute | solution.py:288
  148.4 8.2 %collective-permute-start.31 = (bf16[128,256]{1,0:T(8,128)(2,1)S(1)}, bf16[128,256]{1,0:T(8,128)(2,1)S(1)}, u32[]{:S(2)}, u32[]{:S(2)}) collective-permute-start(bf16[128,256]{1,0:T(8,128)(2,1)S(1)} %get-tuple-element.146), channel_id=1, source_target_pairs={{4,8},{8,4},{12,16},{16,12},{20,24},{24,20},{5,9},{9,5},{13,17},{1... | collective-permute-start | bytes 196616 | tf_op jit(solution)/shard_map/ppermute | solution.py:288
  152.0 5.1 %collective-permute-start.32 = (bf16[128,256]{1,0:T(8,128)(2,1)S(1)}, bf16[128,256]{1,0:T(8,128)(2,1)S(1)}, u32[]{:S(2)}, u32[]{:S(2)}) collective-permute-start(bf16[128,256]{1,0:T(8,128)(2,1)S(1)} %get-tuple-element.147), channel_id=1, source_target_pairs={{0,1},{1,0},{2,3},{3,2},{4,5},{5,4},{6,7},{7,6},{8,9},{9,8},{10,11... | collective-permute-start | bytes 196616 | tf_op jit(solution)/shard_map/ppermute | solution.py:288
  154.4 5.6 %collective-permute-start.33 = (bf16[128,256]{1,0:T(8,128)(2,1)S(1)}, bf16[128,256]{1,0:T(8,128)(2,1)S(1)}, u32[]{:S(2)}, u32[]{:S(2)}) collective-permute-start(bf16[128,256]{1,0:T(8,128)(2,1)S(1)} %get-tuple-element.148), channel_id=1, source_target_pairs={{1,2},{2,1},{5,6},{6,5},{9,10},{10,9},{13,14},{14,13},{17,18},{18,... | collective-permute-start | bytes 196616 | tf_op jit(solution)/shard_map/ppermute | solution.py:288

commit v7 on v6

--- a/solution.py
+++ b/solution.py
@@ -285,7 +285,7 @@
 def swapped(shard, axis, exchange):
     devices = lax.axis_size(axis)
     pairs = [(i, partner(i, exchange)) for i in range(devices)]
-    return lax.ppermute(shard, axis, [(i, j) for i, j in pairs if 0 <= j < devices])
+    return lax.ppermute(shard, axis, [(i, j if 0 <= j < devices else i) for i, j in pairs])
 
 
 def traded_over_row(tiles):

time: 162 us -> 162 us (level)
  no operation moved by 1% of the time
where the time goes in v7:
time: 162 us; the launch traced here: 161 us
  starting transfers between devices  64.8 us (40%)
  blocking collectives  53.3 us (33%)
  Pallas kernels  22.1 us (14%)
  waiting for transfers between devices  20.5 us (13%)
    ppermute x34, starting transfers between devices, swapped(): lax.ppermute(shard, axis, [(i, j if 0 <= j < devices else i) for i, j in...  64.8 us
    all_gather x3, blocking collectives, per_device(): gathered = lax.all_gather(share, 'col', axis=0, tiled=True)  28.2 us
    all_to_all x3, blocking collectives, per_device(): parts = lax.all_to_all(parts, 'row', 0, 0, tiled=True)  25.1 us
    pallas_call x28, Pallas kernels, call(): pl.pallas_call(body, out_shape=tuple(((pltpu.HBM if away else pltpu.VMEM)...  22.1 us
    ppermute x34, waiting for transfers between devices, swapped(): lax.ppermute(shard, axis, [(i, j if 0 <= j < devices else i) for i, j in...  20.5 us
  transfers between devices with their start and end apart: 34, of which 13 were waited for; matrix products, arithmetic and copies ran while one was open for 0% of the time, Pallas kernels for 6%

profile of v7, /device:TPU:9, one launch (start us, length us, event | category | flops | bytes accessed | tf_op | source)
XLA Modules:
  0.0 161.4 jit_solution(13349437945491934535)
XLA Ops:
  0.0 3.0 %select.1 = (f32[1024,256]{1,0:T(8,128)S(1)}, bf16[1024,256]{1,0:T(8,128)(2,1)S(1)}, bf16[512,1024]{1,0:T(8,128)(2,1)S(1)}, s32[4,128]{1,0:T(4,128)S(1)}, bf16[3...) custom-call(f32[1024,256]{1,0:T(8,128)} %bitcast.11, ...), custom_call_target="tpu_custom_call" | custom-call | flops 268435456 | bytes 5867536 | tf_op jit(solution)/shard_map/select/pallas_call | solution.py:28
  3.1 1.3 collective-permute-start
  4.4 1.9 %collective-permute-start.1 = (bf16[128,256]{1,0:T(8,128)(2,1)S(1)}, bf16[128,256]{1,0:T(8,128)(2,1)S(1)}, u32[]{:S(2)}, u32[]{:S(2)}) collective-permute-start(bf16[128,256]{1,0:T(8,128)(2,1)S(1)} %get-tuple-element.83), channel_id=1, source_target_pairs={{0,0},{4,8},{8,4},{12,16},{16,12},{20,24},{24,20},{28,28},{1,1},{5... | collective-permute-start | bytes 196616 | tf_op jit(solution)/shard_map/ppermute | solution.py:288
  6.3 1.0 inverse_own.3.refs_1_
  7.3 3.0 %collective-permute-done.1.g1.refs_5_ = bf16[128,256]{1,0:T(8,128)(2,1)S(1)} collective-permute-done((bf16[128,256]{1,0:T(8,128)(2,1)S(1)}, bf16[128,256]{1,0:T(8,128)(2,1)S(1)}, u32[]{:S(2)}, u32[]{:S(2)}) %collective-permute-start.1) | collective-permute-done | bytes 65568 | tf_op jit(solution)/shard_map/ppermute | solution.py:288
  10.5 9.8 %all_gather.9.refs_2_ = bf16[1280,256]{1,0:T(8,128)(2,1)S(1)} all-gather(bf16[320,256]{1,0:T(8,128)(2,1)S(1)} %share.3), channel_id=1, replica_groups=mesh['row'=8,'col'=4] {'col'}, dimensions={0}, use_global_device_ids=true | all-gather | bytes 819200 | tf_op jit(solution)/shard_map/all_gather | solution.py:416
  21.2 9.1 %all_to_all.15.parts = bf16[8,32,256]{2,1,0:T(8,128)(2,1)S(1)} all-to-all(bf16[8,32,256]{2,1,0:T(8,128)(2,1)S(1)} %get-tuple-element.85), channel_id=1, replica_groups=mesh['row'=8,'col'=4] {'row'}, dimensions={0} | all-to-all | bytes 262144 | tf_op jit(solution)/shard_map/all_to_all | solution.py:433
  30.5 1.2 collective-permute-start.2
  31.7 3.6 %collective-permute-start.3 = (bf16[128,256]{1,0:T(8,128)(2,1)S(1)}, bf16[128,256]{1,0:T(8,128)(2,1)S(1)}, u32[]{:S(2)}, u32[]{:S(2)}) collective-permute-start(bf16[128,256]{1,0:T(8,128)(2,1)S(1)} %get-tuple-element.96), channel_id=1, source_target_pairs={{0,0},{4,8},{8,4},{12,16},{16,12},{20,24},{24,20},{28,28},{1,1},{5... | collective-permute-start | bytes 196616 | tf_op jit(solution)/shard_map/ppermute | solution.py:288
  35.3 2.4 %collective-permute-start.4 = (bf16[128,256]{1,0:T(8,128)(2,1)S(1)}, bf16[128,256]{1,0:T(8,128)(2,1)S(1)}, u32[]{:S(2)}, u32[]{:S(2)}) collective-permute-start(bf16[128,256]{1,0:T(8,128)(2,1)S(1)} %get-tuple-element.98), channel_id=1, source_target_pairs={{0,1},{1,0},{2,3},{3,2},{4,5},{5,4},{6,7},{7,6},{8,9},{9,8},{10,11... | collective-permute-start | bytes 196616 | tf_op jit(solution)/shard_map/ppermute | solution.py:288
  37.7 2.1 %collective-permute-start.5 = (bf16[128,256]{1,0:T(8,128)(2,1)S(1)}, bf16[128,256]{1,0:T(8,128)(2,1)S(1)}, u32[]{:S(2)}, u32[]{:S(2)}) collective-permute-start(bf16[128,256]{1,0:T(8,128)(2,1)S(1)} %get-tuple-element.99), channel_id=1, source_target_pairs={{0,0},{1,2},{2,1},{3,3},{4,4},{5,6},{6,5},{7,7},{8,8},{9,10},{10,9... | collective-permute-start | bytes 196616 | tf_op jit(solution)/shard_map/ppermute | solution.py:288
  39.8 2.6 %spread.1 = (bf16[1024,512]{1,0:T(8,128)(2,1)S(1)}, bf16[1536,1536]{1,0:T(8,128)(2,1)S(1)}) custom-call(bf16[1536,1536]{1,0:T(8,128)(2,1)} %bitcast.10, s32[4,128]{1,0:T(4,128)S(1)} %get-tuple-element.93.masked), custom_call_target="tpu_custom_call" | custom-call | bytes 4720640 | tf_op jit(solution)/shard_map/spread/pallas_call | solution.py:28
  44.2 2.4 %collective-permute-start.7 = (bf16[128,256]{1,0:T(8,128)(2,1)S(1)}, bf16[128,256]{1,0:T(8,128)(2,1)S(1)}, u32[]{:S(2)}, u32[]{:S(2)}) collective-permute-start(bf16[128,256]{1,0:T(8,128)(2,1)S(1)} %get-tuple-element.106), channel_id=1, source_target_pairs={{0,0},{4,8},{8,4},{12,16},{16,12},{20,24},{24,20},{28,28},{1,1},{5... | collective-permute-start | bytes 196616 | tf_op jit(solution)/shard_map/ppermute | solution.py:288
  46.7 3.4 %collective-permute-start.9 = (bf16[128,256]{1,0:T(8,128)(2,1)S(1)}, bf16[128,256]{1,0:T(8,128)(2,1)S(1)}, u32[]{:S(2)}, u32[]{:S(2)}) collective-permute-start(bf16[128,256]{1,0:T(8,128)(2,1)S(1)} %get-tuple-element.108), channel_id=1, source_target_pairs={{0,0},{1,2},{2,1},{3,3},{4,4},{5,6},{6,5},{7,7},{8,8},{9,10},{10,9... | collective-permute-start | bytes 196616 | tf_op jit(solution)/shard_map/ppermute | solution.py:288
  50.1 1.2 operator_near.2.partial
  52.5 1.3 collective-permute-start.10
  53.8 2.6 %collective-permute-start.11 = (bf16[128,256]{1,0:T(8,128)(2,1)S(1)}, bf16[128,256]{1,0:T(8,128)(2,1)S(1)}, u32[]{:S(2)}, u32[]{:S(2)}) collective-permute-start(bf16[128,256]{1,0:T(8,128)(2,1)S(1)} %get-tuple-element.110), channel_id=1, source_target_pairs={{0,0},{4,8},{8,4},{12,16},{16,12},{20,24},{24,20},{28,28},{1,1},{5... | collective-permute-start | bytes 196616 | tf_op jit(solution)/shard_map/ppermute | solution.py:288
  56.5 3.6 %collective-permute-start.13 = (bf16[128,256]{1,0:T(8,128)(2,1)S(1)}, bf16[128,256]{1,0:T(8,128)(2,1)S(1)}, u32[]{:S(2)}, u32[]{:S(2)}) collective-permute-start(bf16[128,256]{1,0:T(8,128)(2,1)S(1)} %get-tuple-element.112), channel_id=1, source_target_pairs={{0,0},{1,2},{2,1},{3,3},{4,4},{5,6},{6,5},{7,7},{8,8},{9,10},{10,9... | collective-permute-start | bytes 196616 | tf_op jit(solution)/shard_map/ppermute | solution.py:288
  60.6 1.5 collective-permute-done.13.r3
  62.9 1.8 %collective-permute-start.14 = (bf16[128,256]{1,0:T(8,128)(2,1)S(1)}, bf16[128,256]{1,0:T(8,128)(2,1)S(1)}, u32[]{:S(2)}, u32[]{:S(2)}) collective-permute-start(bf16[128,256]{1,0:T(8,128)(2,1)S(1)} %get-tuple-element.116), channel_id=1, source_target_pairs={{0,4},{4,0},{8,12},{12,8},{16,20},{20,16},{24,28},{28,24},{1,5},{5... | collective-permute-start | bytes 196616 | tf_op jit(solution)/shard_map/ppermute | solution.py:288
  64.7 2.9 %collective-permute-start.15 = (bf16[128,256]{1,0:T(8,128)(2,1)S(1)}, bf16[128,256]{1,0:T(8,128)(2,1)S(1)}, u32[]{:S(2)}, u32[]{:S(2)}) collective-permute-start(bf16[128,256]{1,0:T(8,128)(2,1)S(1)} %get-tuple-element.117), channel_id=1, source_target_pairs={{0,0},{4,8},{8,4},{12,16},{16,12},{20,24},{24,20},{28,28},{1,1},{5... | collective-permute-start | bytes 196616 | tf_op jit(solution)/shard_map/ppermute | solution.py:288
  67.6 1.0 inverse_own.4.refs_2_
  68.6 2.0 %collective-permute-done.15.g1.refs_6_ = bf16[128,256]{1,0:T(8,128)(2,1)S(1)} collective-permute-done((bf16[128,256]{1,0:T(8,128)(2,1)S(1)}, bf16[128,256]{1,0:T(8,128)(2,1)S(1)}, u32[]{:S(2)}, u32[]{:S(2)}) %collective-permute-start.15) | collective-permute-done | bytes 65568 | tf_op jit(solution)/shard_map/ppermute | solution.py:288
  70.8 9.5 %all_gather.10.refs_3_ = bf16[1152,256]{1,0:T(8,128)(2,1)S(1)} all-gather(bf16[288,256]{1,0:T(8,128)(2,1)S(1)} %share.4), channel_id=1, replica_groups=mesh['row'=8,'col'=4] {'col'}, dimensions={0}, use_global_device_ids=true | all-gather | bytes 737280 | tf_op jit(solution)/shard_map/all_gather | solution.py:416
  81.1 8.0 %all_to_all.16.parts = bf16[8,32,256]{2,1,0:T(8,128)(2,1)S(1)} all-to-all(bf16[8,32,256]{2,1,0:T(8,128)(2,1)S(1)} %get-tuple-element.119), channel_id=1, replica_groups=mesh['row'=8,'col'=4] {'row'}, dimensions={0} | all-to-all | bytes 262144 | tf_op jit(solution)/shard_map/all_to_all | solution.py:433
  89.3 1.1 collective-permute-start.16
  90.5 3.6 %collective-permute-start.17 = (bf16[128,256]{1,0:T(8,128)(2,1)S(1)}, bf16[128,256]{1,0:T(8,128)(2,1)S(1)}, u32[]{:S(2)}, u32[]{:S(2)}) collective-permute-start(bf16[128,256]{1,0:T(8,128)(2,1)S(1)} %get-tuple-element.123), channel_id=1, source_target_pairs={{0,0},{4,8},{8,4},{12,16},{16,12},{20,24},{24,20},{28,28},{1,1},{5... | collective-permute-start | bytes 196616 | tf_op jit(solution)/shard_map/ppermute | solution.py:288
  94.1 2.4 %collective-permute-start.18 = (bf16[128,256]{1,0:T(8,128)(2,1)S(1)}, bf16[128,256]{1,0:T(8,128)(2,1)S(1)}, u32[]{:S(2)}, u32[]{:S(2)}) collective-permute-start(bf16[128,256]{1,0:T(8,128)(2,1)S(1)} %get-tuple-element.124), channel_id=1, source_target_pairs={{0,1},{1,0},{2,3},{3,2},{4,5},{5,4},{6,7},{7,6},{8,9},{9,8},{10,11... | collective-permute-start | bytes 196616 | tf_op jit(solution)/shard_map/ppermute | solution.py:288
  96.5 2.2 %collective-permute-start.19 = (bf16[128,256]{1,0:T(8,128)(2,1)S(1)}, bf16[128,256]{1,0:T(8,128)(2,1)S(1)}, u32[]{:S(2)}, u32[]{:S(2)}) collective-permute-start(bf16[128,256]{1,0:T(8,128)(2,1)S(1)} %get-tuple-element.125), channel_id=1, source_target_pairs={{0,0},{1,2},{2,1},{3,3},{4,4},{5,6},{6,5},{7,7},{8,8},{9,10},{10,9... | collective-permute-start | bytes 196616 | tf_op jit(solution)/shard_map/ppermute | solution.py:288
  99.2 2.9 %collective-permute-done.19.r3 = bf16[128,256]{1,0:T(8,128)(2,1)S(1)} collective-permute-done((bf16[128,256]{1,0:T(8,128)(2,1)S(1)}, bf16[128,256]{1,0:T(8,128)(2,1)S(1)}, u32[]{:S(2)}, u32[]{:S(2)}) %collective-permute-start.19) | collective-permute-done | bytes 65568 | tf_op jit(solution)/shard_map/ppermute | solution.py:288
  103.0 2.4 %collective-permute-start.21 = (bf16[128,256]{1,0:T(8,128)(2,1)S(1)}, bf16[128,256]{1,0:T(8,128)(2,1)S(1)}, u32[]{:S(2)}, u32[]{:S(2)}) collective-permute-start(bf16[128,256]{1,0:T(8,128)(2,1)S(1)} %get-tuple-element.129), channel_id=1, source_target_pairs={{0,0},{4,8},{8,4},{12,16},{16,12},{20,24},{24,20},{28,28},{1,1},{5... | collective-permute-start | bytes 196616 | tf_op jit(solution)/shard_map/ppermute | solution.py:288
  105.5 2.7 %collective-permute-start.23 = (bf16[128,256]{1,0:T(8,128)(2,1)S(1)}, bf16[128,256]{1,0:T(8,128)(2,1)S(1)}, u32[]{:S(2)}, u32[]{:S(2)}) collective-permute-start(bf16[128,256]{1,0:T(8,128)(2,1)S(1)} %get-tuple-element.131), channel_id=1, source_target_pairs={{0,0},{1,2},{2,1},{3,3},{4,4},{5,6},{6,5},{7,7},{8,8},{9,10},{10,9... | collective-permute-start | bytes 196616 | tf_op jit(solution)/shard_map/ppermute | solution.py:288
  108.9 1.2 operator_near.3.partial
  111.3 1.3 collective-permute-start.24
  112.6 2.6 %collective-permute-start.25 = (bf16[128,256]{1,0:T(8,128)(2,1)S(1)}, bf16[128,256]{1,0:T(8,128)(2,1)S(1)}, u32[]{:S(2)}, u32[]{:S(2)}) collective-permute-start(bf16[128,256]{1,0:T(8,128)(2,1)S(1)} %get-tuple-element.133), channel_id=1, source_target_pairs={{0,0},{4,8},{8,4},{12,16},{16,12},{20,24},{24,20},{28,28},{1,1},{5... | collective-permute-start | bytes 196616 | tf_op jit(solution)/shard_map/ppermute | solution.py:288
  115.3 2.8 %collective-permute-start.27 = (bf16[128,256]{1,0:T(8,128)(2,1)S(1)}, bf16[128,256]{1,0:T(8,128)(2,1)S(1)}, u32[]{:S(2)}, u32[]{:S(2)}) collective-permute-start(bf16[128,256]{1,0:T(8,128)(2,1)S(1)} %get-tuple-element.135), channel_id=1, source_target_pairs={{0,0},{1,2},{2,1},{3,3},{4,4},{5,6},{6,5},{7,7},{8,8},{9,10},{10,9... | collective-permute-start | bytes 196616 | tf_op jit(solution)/shard_map/ppermute | solution.py:288
  118.9 1.9 %collective-permute-done.27.r3 = bf16[128,256]{1,0:T(8,128)(2,1)S(1)} collective-permute-done((bf16[128,256]{1,0:T(8,128)(2,1)S(1)}, bf16[128,256]{1,0:T(8,128)(2,1)S(1)}, u32[]{:S(2)}, u32[]{:S(2)}) %collective-permute-start.27) | collective-permute-done | bytes 65568 | tf_op jit(solution)/shard_map/ppermute | solution.py:288
  121.7 1.5 collective-permute-start.28
  123.2 2.2 %collective-permute-start.29 = (bf16[128,256]{1,0:T(8,128)(2,1)S(1)}, bf16[128,256]{1,0:T(8,128)(2,1)S(1)}, u32[]{:S(2)}, u32[]{:S(2)}) collective-permute-start(bf16[128,256]{1,0:T(8,128)(2,1)S(1)} %get-tuple-element.140), channel_id=1, source_target_pairs={{0,0},{4,8},{8,4},{12,16},{16,12},{20,24},{24,20},{28,28},{1,1},{5... | collective-permute-start | bytes 196616 | tf_op jit(solution)/shard_map/ppermute | solution.py:288
  126.4 2.7 %collective-permute-done.29.g1.refs_6_ = bf16[128,256]{1,0:T(8,128)(2,1)S(1)} collective-permute-done((bf16[128,256]{1,0:T(8,128)(2,1)S(1)}, bf16[128,256]{1,0:T(8,128)(2,1)S(1)}, u32[]{:S(2)}, u32[]{:S(2)}) %collective-permute-start.29) | collective-permute-done | bytes 65568 | tf_op jit(solution)/shard_map/ppermute | solution.py:288
  129.3 8.8 %all_gather.11.refs_3_ = bf16[1152,256]{1,0:T(8,128)(2,1)S(1)} all-gather(bf16[288,256]{1,0:T(8,128)(2,1)S(1)} %share.5), channel_id=1, replica_groups=mesh['row'=8,'col'=4] {'col'}, dimensions={0}, use_global_device_ids=true | all-gather | bytes 737280 | tf_op jit(solution)/shard_map/all_gather | solution.py:416
  139.0 8.0 %all_to_all.17.parts = bf16[8,32,256]{2,1,0:T(8,128)(2,1)S(1)} all-to-all(bf16[8,32,256]{2,1,0:T(8,128)(2,1)S(1)} %get-tuple-element.142), channel_id=1, replica_groups=mesh['row'=8,'col'=4] {'row'}, dimensions={0} | all-to-all | bytes 262144 | tf_op jit(solution)/shard_map/all_to_all | solution.py:433
  147.3 1.1 collective-permute-start.30
  148.4 3.6 %collective-permute-start.31 = (bf16[128,256]{1,0:T(8,128)(2,1)S(1)}, bf16[128,256]{1,0:T(8,128)(2,1)S(1)}, u32[]{:S(2)}, u32[]{:S(2)}) collective-permute-start(bf16[128,256]{1,0:T(8,128)(2,1)S(1)} %get-tuple-element.146), channel_id=1, source_target_pairs={{0,0},{4,8},{8,4},{12,16},{16,12},{20,24},{24,20},{28,28},{1,1},{5... | collective-permute-start | bytes 196616 | tf_op jit(solution)/shard_map/ppermute | solution.py:288
  152.0 2.4 %collective-permute-start.32 = (bf16[128,256]{1,0:T(8,128)(2,1)S(1)}, bf16[128,256]{1,0:T(8,128)(2,1)S(1)}, u32[]{:S(2)}, u32[]{:S(2)}) collective-permute-start(bf16[128,256]{1,0:T(8,128)(2,1)S(1)} %get-tuple-element.147), channel_id=1, source_target_pairs={{0,1},{1,0},{2,3},{3,2},{4,5},{5,4},{6,7},{7,6},{8,9},{9,8},{10,11... | collective-permute-start | bytes 196616 | tf_op jit(solution)/shard_map/ppermute | solution.py:288
  154.4 2.2 %collective-permute-start.33 = (bf16[128,256]{1,0:T(8,128)(2,1)S(1)}, bf16[128,256]{1,0:T(8,128)(2,1)S(1)}, u32[]{:S(2)}, u32[]{:S(2)}) collective-permute-start(bf16[128,256]{1,0:T(8,128)(2,1)S(1)} %get-tuple-element.148), channel_id=1, source_target_pairs={{0,0},{1,2},{2,1},{3,3},{4,4},{5,6},{6,5},{7,7},{8,8},{9,10},{10,9... | collective-permute-start | bytes 196616 | tf_op jit(solution)/shard_map/ppermute | solution.py:288
  157.1 2.9 %collective-permute-done.33.r3 = bf16[128,256]{1,0:T(8,128)(2,1)S(1)} collective-permute-done((bf16[128,256]{1,0:T(8,128)(2,1)S(1)}, bf16[128,256]{1,0:T(8,128)(2,1)S(1)}, u32[]{:S(2)}, u32[]{:S(2)}) %collective-permute-start.33) | collective-permute-done | bytes 65568 | tf_op jit(solution)/shard_map/ppermute | solution.py:288
  160.0 1.2 last_update.1
  (56 shorter events, 15.0 us)
Async XLA Ops:
  3.1 4.2 %collective-permute-start = (bf16[128,256]{1,0:T(8,128)(2,1)S(1)}, bf16[128,256]{1,0:T(8,128)(2,1)S(1)}, u32[]{:S(2)}, u32[]{:S(2)}) collective-permute-start(bf16[128,256]{1,0:T(8,128)(2,1)S(1)} %get-tuple-element.82), channel_id=1, source_target_pairs={{0,4},{4,0},{8,12},{12,8},{16,20},{20,16},{24,28},{28,24},{1,5},{5... | collective-permute-start | bytes 196616 | tf_op jit(solution)/shard_map/ppermute | solution.py:288
  4.4 5.9 %collective-permute-start.1 = (bf16[128,256]{1,0:T(8,128)(2,1)S(1)}, bf16[128,256]{1,0:T(8,128)(2,1)S(1)}, u32[]{:S(2)}, u32[]{:S(2)}) collective-permute-start(bf16[128,256]{1,0:T(8,128)(2,1)S(1)} %get-tuple-element.83), channel_id=1, source_target_pairs={{0,0},{4,8},{8,4},{12,16},{16,12},{20,24},{24,20},{28,28},{1,1},{5... | collective-permute-start | bytes 196616 | tf_op jit(solution)/shard_map/ppermute | solution.py:288
  7.3 13.1 %copy-start = (bf16[8,32,128]{2,1,0:T(8,128)(2,1)S(1)}, bf16[8,32,128]{2,1,0:T(8,128)(2,1)}, u32[]{:S(2)}) copy-start(bf16[8,32,128]{2,1,0:T(8,128)(2,1)} %refs_4_.3) | copy-start | bytes 196612
  30.5 11.8 %collective-permute-start.2 = (bf16[128,256]{1,0:T(8,128)(2,1)S(1)}, bf16[128,256]{1,0:T(8,128)(2,1)S(1)}, u32[]{:S(2)}, u32[]{:S(2)}) collective-permute-start(bf16[128,256]{1,0:T(8,128)(2,1)S(1)} %get-tuple-element.95), channel_id=1, source_target_pairs={{0,4},{4,0},{8,12},{12,8},{16,20},{20,16},{24,28},{28,24},{1,5},{5... | collective-permute-start | bytes 196616 | tf_op jit(solution)/shard_map/ppermute | solution.py:288
  31.7 10.7 %collective-permute-start.3 = (bf16[128,256]{1,0:T(8,128)(2,1)S(1)}, bf16[128,256]{1,0:T(8,128)(2,1)S(1)}, u32[]{:S(2)}, u32[]{:S(2)}) collective-permute-start(bf16[128,256]{1,0:T(8,128)(2,1)S(1)} %get-tuple-element.96), channel_id=1, source_target_pairs={{0,0},{4,8},{8,4},{12,16},{16,12},{20,24},{24,20},{28,28},{1,1},{5... | collective-permute-start | bytes 196616 | tf_op jit(solution)/shard_map/ppermute | solution.py:288
  35.3 7.5 %collective-permute-start.4 = (bf16[128,256]{1,0:T(8,128)(2,1)S(1)}, bf16[128,256]{1,0:T(8,128)(2,1)S(1)}, u32[]{:S(2)}, u32[]{:S(2)}) collective-permute-start(bf16[128,256]{1,0:T(8,128)(2,1)S(1)} %get-tuple-element.98), channel_id=1, source_target_pairs={{0,1},{1,0},{2,3},{3,2},{4,5},{5,4},{6,7},{7,6},{8,9},{9,8},{10,11... | collective-permute-start | bytes 196616 | tf_op jit(solution)/shard_map/ppermute | solution.py:288
  37.7 5.6 %collective-permute-start.5 = (bf16[128,256]{1,0:T(8,128)(2,1)S(1)}, bf16[128,256]{1,0:T(8,128)(2,1)S(1)}, u32[]{:S(2)}, u32[]{:S(2)}) collective-permute-start(bf16[128,256]{1,0:T(8,128)(2,1)S(1)} %get-tuple-element.99), channel_id=1, source_target_pairs={{0,0},{1,2},{2,1},{3,3},{4,4},{5,6},{6,5},{7,7},{8,8},{9,10},{10,9... | collective-permute-start | bytes 196616 | tf_op jit(solution)/shard_map/ppermute | solution.py:288
  44.1 5.9 %collective-permute-start.6 = (bf16[128,256]{1,0:T(8,128)(2,1)S(1)}, bf16[128,256]{1,0:T(8,128)(2,1)S(1)}, u32[]{:S(2)}, u32[]{:S(2)}) collective-permute-start(bf16[128,256]{1,0:T(8,128)(2,1)S(1)} %get-tuple-element.105), channel_id=1, source_target_pairs={{0,4},{4,0},{8,12},{12,8},{16,20},{20,16},{24,28},{28,24},{1,5},{5... | collective-permute-start | bytes 196616 | tf_op jit(solution)/shard_map/ppermute | solution.py:288
  44.2 5.9 %collective-permute-start.7 = (bf16[128,256]{1,0:T(8,128)(2,1)S(1)}, bf16[128,256]{1,0:T(8,128)(2,1)S(1)}, u32[]{:S(2)}, u32[]{:S(2)}) collective-permute-start(bf16[128,256]{1,0:T(8,128)(2,1)S(1)} %get-tuple-element.106), channel_id=1, source_target_pairs={{0,0},{4,8},{8,4},{12,16},{16,12},{20,24},{24,20},{28,28},{1,1},{5... | collective-permute-start | bytes 196616 | tf_op jit(solution)/shard_map/ppermute | solution.py:288
  46.6 4.7 %collective-permute-start.8 = (bf16[128,256]{1,0:T(8,128)(2,1)S(1)}, bf16[128,256]{1,0:T(8,128)(2,1)S(1)}, u32[]{:S(2)}, u32[]{:S(2)}) collective-permute-start(bf16[128,256]{1,0:T(8,128)(2,1)S(1)} %get-tuple-element.107), channel_id=1, source_target_pairs={{0,1},{1,0},{2,3},{3,2},{4,5},{5,4},{6,7},{7,6},{8,9},{9,8},{10,11... | collective-permute-start | bytes 196616 | tf_op jit(solution)/shard_map/ppermute | solution.py:288
  46.7 5.6 %collective-permute-start.9 = (bf16[128,256]{1,0:T(8,128)(2,1)S(1)}, bf16[128,256]{1,0:T(8,128)(2,1)S(1)}, u32[]{:S(2)}, u32[]{:S(2)}) collective-permute-start(bf16[128,256]{1,0:T(8,128)(2,1)S(1)} %get-tuple-element.108), channel_id=1, source_target_pairs={{0,0},{1,2},{2,1},{3,3},{4,4},{5,6},{6,5},{7,7},{8,8},{9,10},{10,9... | collective-permute-start | bytes 196616 | tf_op jit(solution)/shard_map/ppermute | solution.py:288
  52.5 7.6 %collective-permute-start.10 = (bf16[128,256]{1,0:T(8,128)(2,1)S(1)}, bf16[128,256]{1,0:T(8,128)(2,1)S(1)}, u32[]{:S(2)}, u32[]{:S(2)}) collective-permute-start(bf16[128,256]{1,0:T(8,128)(2,1)S(1)} %get-tuple-element.109), channel_id=1, source_target_pairs={{0,4},{4,0},{8,12},{12,8},{16,20},{20,16},{24,28},{28,24},{1,5},{5... | collective-permute-start | bytes 196616 | tf_op jit(solution)/shard_map/ppermute | solution.py:288
  53.8 6.3 %collective-permute-start.11 = (bf16[128,256]{1,0:T(8,128)(2,1)S(1)}, bf16[128,256]{1,0:T(8,128)(2,1)S(1)}, u32[]{:S(2)}, u32[]{:S(2)}) collective-permute-start(bf16[128,256]{1,0:T(8,128)(2,1)S(1)} %get-tuple-element.110), channel_id=1, source_target_pairs={{0,0},{4,8},{8,4},{12,16},{16,12},{20,24},{24,20},{28,28},{1,1},{5... | collective-permute-start | bytes 196616 | tf_op jit(solution)/shard_map/ppermute | solution.py:288
  56.4 4.2 %collective-permute-start.12 = (bf16[128,256]{1,0:T(8,128)(2,1)S(1)}, bf16[128,256]{1,0:T(8,128)(2,1)S(1)}, u32[]{:S(2)}, u32[]{:S(2)}) collective-permute-start(bf16[128,256]{1,0:T(8,128)(2,1)S(1)} %get-tuple-element.111), channel_id=1, source_target_pairs={{0,1},{1,0},{2,3},{3,2},{4,5},{5,4},{6,7},{7,6},{8,9},{9,8},{10,11... | collective-permute-start | bytes 196616 | tf_op jit(solution)/shard_map/ppermute | solution.py:288
  56.5 5.6 %collective-permute-start.13 = (bf16[128,256]{1,0:T(8,128)(2,1)S(1)}, bf16[128,256]{1,0:T(8,128)(2,1)S(1)}, u32[]{:S(2)}, u32[]{:S(2)}) collective-permute-start(bf16[128,256]{1,0:T(8,128)(2,1)S(1)} %get-tuple-element.112), channel_id=1, source_target_pairs={{0,0},{1,2},{2,1},{3,3},{4,4},{5,6},{6,5},{7,7},{8,8},{9,10},{10,9... | collective-permute-start | bytes 196616 | tf_op jit(solution)/shard_map/ppermute | solution.py:288
  62.9 5.7 %collective-permute-start.14 = (bf16[128,256]{1,0:T(8,128)(2,1)S(1)}, bf16[128,256]{1,0:T(8,128)(2,1)S(1)}, u32[]{:S(2)}, u32[]{:S(2)}) collective-permute-start(bf16[128,256]{1,0:T(8,128)(2,1)S(1)} %get-tuple-element.116), channel_id=1, source_target_pairs={{0,4},{4,0},{8,12},{12,8},{16,20},{20,16},{24,28},{28,24},{1,5},{5... | collective-permute-start | bytes 196616 | tf_op jit(solution)/shard_map/ppermute | solution.py:288
  64.7 5.9 %collective-permute-start.15 = (bf16[128,256]{1,0:T(8,128)(2,1)S(1)}, bf16[128,256]{1,0:T(8,128)(2,1)S(1)}, u32[]{:S(2)}, u32[]{:S(2)}) collective-permute-start(bf16[128,256]{1,0:T(8,128)(2,1)S(1)} %get-tuple-element.117), channel_id=1, source_target_pairs={{0,0},{4,8},{8,4},{12,16},{16,12},{20,24},{24,20},{28,28},{1,1},{5... | collective-permute-start | bytes 196616 | tf_op jit(solution)/shard_map/ppermute | solution.py:288
  89.3 9.3 %collective-permute-start.16 = (bf16[128,256]{1,0:T(8,128)(2,1)S(1)}, bf16[128,256]{1,0:T(8,128)(2,1)S(1)}, u32[]{:S(2)}, u32[]{:S(2)}) collective-permute-start(bf16[128,256]{1,0:T(8,128)(2,1)S(1)} %get-tuple-element.122), channel_id=1, source_target_pairs={{0,4},{4,0},{8,12},{12,8},{16,20},{20,16},{24,28},{28,24},{1,5},{5... | collective-permute-start | bytes 196616 | tf_op jit(solution)/shard_map/ppermute | solution.py:288
  90.5 8.2 %collective-permute-start.17 = (bf16[128,256]{1,0:T(8,128)(2,1)S(1)}, bf16[128,256]{1,0:T(8,128)(2,1)S(1)}, u32[]{:S(2)}, u32[]{:S(2)}) collective-permute-start(bf16[128,256]{1,0:T(8,128)(2,1)S(1)} %get-tuple-element.123), channel_id=1, source_target_pairs={{0,0},{4,8},{8,4},{12,16},{16,12},{20,24},{24,20},{28,28},{1,1},{5... | collective-permute-start | bytes 196616 | tf_op jit(solution)/shard_map/ppermute | solution.py:288
  94.1 5.1 %collective-permute-start.18 = (bf16[128,256]{1,0:T(8,128)(2,1)S(1)}, bf16[128,256]{1,0:T(8,128)(2,1)S(1)}, u32[]{:S(2)}, u32[]{:S(2)}) collective-permute-start(bf16[128,256]{1,0:T(8,128)(2,1)S(1)} %get-tuple-element.124), channel_id=1, source_target_pairs={{0,1},{1,0},{2,3},{3,2},{4,5},{5,4},{6,7},{7,6},{8,9},{9,8},{10,11... | collective-permute-start | bytes 196616 | tf_op jit(solution)/shard_map/ppermute | solution.py:288
  96.5 5.6 %collective-permute-start.19 = (bf16[128,256]{1,0:T(8,128)(2,1)S(1)}, bf16[128,256]{1,0:T(8,128)(2,1)S(1)}, u32[]{:S(2)}, u32[]{:S(2)}) collective-permute-start(bf16[128,256]{1,0:T(8,128)(2,1)S(1)} %get-tuple-element.125), channel_id=1, source_target_pairs={{0,0},{1,2},{2,1},{3,3},{4,4},{5,6},{6,5},{7,7},{8,8},{9,10},{10,9... | collective-permute-start | bytes 196616 | tf_op jit(solution)/shard_map/ppermute | solution.py:288
  102.9 5.2 %collective-permute-start.20 = (bf16[128,256]{1,0:T(8,128)(2,1)S(1)}, bf16[128,256]{1,0:T(8,128)(2,1)S(1)}, u32[]{:S(2)}, u32[]{:S(2)}) collective-permute-start(bf16[128,256]{1,0:T(8,128)(2,1)S(1)} %get-tuple-element.128), channel_id=1, source_target_pairs={{0,4},{4,0},{8,12},{12,8},{16,20},{20,16},{24,28},{28,24},{1,5},{5... | collective-permute-start | bytes 196616 | tf_op jit(solution)/shard_map/ppermute | solution.py:288
  103.0 5.9 %collective-permute-start.21 = (bf16[128,256]{1,0:T(8,128)(2,1)S(1)}, bf16[128,256]{1,0:T(8,128)(2,1)S(1)}, u32[]{:S(2)}, u32[]{:S(2)}) collective-permute-start(bf16[128,256]{1,0:T(8,128)(2,1)S(1)} %get-tuple-element.129), channel_id=1, source_target_pairs={{0,0},{4,8},{8,4},{12,16},{16,12},{20,24},{24,20},{28,28},{1,1},{5... | collective-permute-start | bytes 196616 | tf_op jit(solution)/shard_map/ppermute | solution.py:288
  105.4 4.7 %collective-permute-start.22 = (bf16[128,256]{1,0:T(8,128)(2,1)S(1)}, bf16[128,256]{1,0:T(8,128)(2,1)S(1)}, u32[]{:S(2)}, u32[]{:S(2)}) collective-permute-start(bf16[128,256]{1,0:T(8,128)(2,1)S(1)} %get-tuple-element.130), channel_id=1, source_target_pairs={{0,1},{1,0},{2,3},{3,2},{4,5},{5,4},{6,7},{7,6},{8,9},{9,8},{10,11... | collective-permute-start | bytes 196616 | tf_op jit(solution)/shard_map/ppermute | solution.py:288
  105.5 5.6 %collective-permute-start.23 = (bf16[128,256]{1,0:T(8,128)(2,1)S(1)}, bf16[128,256]{1,0:T(8,128)(2,1)S(1)}, u32[]{:S(2)}, u32[]{:S(2)}) collective-permute-start(bf16[128,256]{1,0:T(8,128)(2,1)S(1)} %get-tuple-element.131), channel_id=1, source_target_pairs={{0,0},{1,2},{2,1},{3,3},{4,4},{5,6},{6,5},{7,7},{8,8},{9,10},{10,9... | collective-permute-start | bytes 196616 | tf_op jit(solution)/shard_map/ppermute | solution.py:288
  111.3 6.7 %collective-permute-start.24 = (bf16[128,256]{1,0:T(8,128)(2,1)S(1)}, bf16[128,256]{1,0:T(8,128)(2,1)S(1)}, u32[]{:S(2)}, u32[]{:S(2)}) collective-permute-start(bf16[128,256]{1,0:T(8,128)(2,1)S(1)} %get-tuple-element.132), channel_id=1, source_target_pairs={{0,4},{4,0},{8,12},{12,8},{16,20},{20,16},{24,28},{28,24},{1,5},{5... | collective-permute-start | bytes 196616 | tf_op jit(solution)/shard_map/ppermute | solution.py:288
  112.6 5.9 %collective-permute-start.25 = (bf16[128,256]{1,0:T(8,128)(2,1)S(1)}, bf16[128,256]{1,0:T(8,128)(2,1)S(1)}, u32[]{:S(2)}, u32[]{:S(2)}) collective-permute-start(bf16[128,256]{1,0:T(8,128)(2,1)S(1)} %get-tuple-element.133), channel_id=1, source_target_pairs={{0,0},{4,8},{8,4},{12,16},{16,12},{20,24},{24,20},{28,28},{1,1},{5... | collective-permute-start | bytes 196616 | tf_op jit(solution)/shard_map/ppermute | solution.py:288
  115.2 3.7 %collective-permute-start.26 = (bf16[128,256]{1,0:T(8,128)(2,1)S(1)}, bf16[128,256]{1,0:T(8,128)(2,1)S(1)}, u32[]{:S(2)}, u32[]{:S(2)}) collective-permute-start(bf16[128,256]{1,0:T(8,128)(2,1)S(1)} %get-tuple-element.134), channel_id=1, source_target_pairs={{0,1},{1,0},{2,3},{3,2},{4,5},{5,4},{6,7},{7,6},{8,9},{9,8},{10,11... | collective-permute-start | bytes 196616 | tf_op jit(solution)/shard_map/ppermute | solution.py:288
  115.3 5.6 %collective-permute-start.27 = (bf16[128,256]{1,0:T(8,128)(2,1)S(1)}, bf16[128,256]{1,0:T(8,128)(2,1)S(1)}, u32[]{:S(2)}, u32[]{:S(2)}) collective-permute-start(bf16[128,256]{1,0:T(8,128)(2,1)S(1)} %get-tuple-element.135), channel_id=1, source_target_pairs={{0,0},{1,2},{2,1},{3,3},{4,4},{5,6},{6,5},{7,7},{8,8},{9,10},{10,9... | collective-permute-start | bytes 196616 | tf_op jit(solution)/shard_map/ppermute | solution.py:288
  121.7 4.7 %collective-permute-start.28 = (bf16[128,256]{1,0:T(8,128)(2,1)S(1)}, bf16[128,256]{1,0:T(8,128)(2,1)S(1)}, u32[]{:S(2)}, u32[]{:S(2)}) collective-permute-start(bf16[128,256]{1,0:T(8,128)(2,1)S(1)} %get-tuple-element.139), channel_id=1, source_target_pairs={{0,4},{4,0},{8,12},{12,8},{16,20},{20,16},{24,28},{28,24},{1,5},{5... | collective-permute-start | bytes 196616 | tf_op jit(solution)/shard_map/ppermute | solution.py:288
  123.2 5.9 %collective-permute-start.29 = (bf16[128,256]{1,0:T(8,128)(2,1)S(1)}, bf16[128,256]{1,0:T(8,128)(2,1)S(1)}, u32[]{:S(2)}, u32[]{:S(2)}) collective-permute-start(bf16[128,256]{1,0:T(8,128)(2,1)S(1)} %get-tuple-element.140), channel_id=1, source_target_pairs={{0,0},{4,8},{8,4},{12,16},{16,12},{20,24},{24,20},{28,28},{1,1},{5... | collective-permute-start | bytes 196616 | tf_op jit(solution)/shard_map/ppermute | solution.py:288
  147.3 9.3 %collective-permute-start.30 = (bf16[128,256]{1,0:T(8,128)(2,1)S(1)}, bf16[128,256]{1,0:T(8,128)(2,1)S(1)}, u32[]{:S(2)}, u32[]{:S(2)}) collective-permute-start(bf16[128,256]{1,0:T(8,128)(2,1)S(1)} %get-tuple-element.145), channel_id=1, source_target_pairs={{0,4},{4,0},{8,12},{12,8},{16,20},{20,16},{24,28},{28,24},{1,5},{5... | collective-permute-start | bytes 196616 | tf_op jit(solution)/shard_map/ppermute | solution.py:288
  148.4 8.2 %collective-permute-start.31 = (bf16[128,256]{1,0:T(8,128)(2,1)S(1)}, bf16[128,256]{1,0:T(8,128)(2,1)S(1)}, u32[]{:S(2)}, u32[]{:S(2)}) collective-permute-start(bf16[128,256]{1,0:T(8,128)(2,1)S(1)} %get-tuple-element.146), channel_id=1, source_target_pairs={{0,0},{4,8},{8,4},{12,16},{16,12},{20,24},{24,20},{28,28},{1,1},{5... | collective-permute-start | bytes 196616 | tf_op jit(solution)/shard_map/ppermute | solution.py:288
  152.0 5.1 %collective-permute-start.32 = (bf16[128,256]{1,0:T(8,128)(2,1)S(1)}, bf16[128,256]{1,0:T(8,128)(2,1)S(1)}, u32[]{:S(2)}, u32[]{:S(2)}) collective-permute-start(bf16[128,256]{1,0:T(8,128)(2,1)S(1)} %get-tuple-element.147), channel_id=1, source_target_pairs={{0,1},{1,0},{2,3},{3,2},{4,5},{5,4},{6,7},{7,6},{8,9},{9,8},{10,11... | collective-permute-start | bytes 196616 | tf_op jit(solution)/shard_map/ppermute | solution.py:288
  154.4 5.6 %collective-permute-start.33 = (bf16[128,256]{1,0:T(8,128)(2,1)S(1)}, bf16[128,256]{1,0:T(8,128)(2,1)S(1)}, u32[]{:S(2)}, u32[]{:S(2)}) collective-permute-start(bf16[128,256]{1,0:T(8,128)(2,1)S(1)} %get-tuple-element.148), channel_id=1, source_target_pairs={{0,0},{1,2},{2,1},{3,3},{4,4},{5,6},{6,5},{7,7},{8,8},{9,10},{10,9... | collective-permute-start | bytes 196616 | tf_op jit(solution)/shard_map/ppermute | solution.py:288

commit v8 on v6

--- a/solution.py
+++ b/solution.py
@@ -285,6 +285,8 @@
 def swapped(shard, axis, exchange):
     devices = lax.axis_size(axis)
     pairs = [(i, partner(i, exchange)) for i in range(devices)]
+    if devices % 2 == 0:
+        pairs = [(i, j % devices) for i, j in pairs]
     return lax.ppermute(shard, axis, [(i, j) for i, j in pairs if 0 <= j < devices])
 
 

time: 162 us -> 147 us (0.907)
  the two profiles are of different devices: /device:TPU:9 before, /device:TPU:0 now
where the time goes in v8:
time: 147 us
  blocking collectives  54.5 us (37%)
  waiting for transfers between devices  38.6 us (26%)
  starting transfers between devices  30.8 us (21%)
  Pallas kernels  22.1 us (15%)
    ppermute x34, waiting for transfers between devices, swapped(): lax.ppermute(shard, axis, [(i, j) for i, j in pairs if 0 <= j < devices])  38.6 us
    all_to_all x3, blocking collectives, per_device(): parts = lax.all_to_all(parts, 'row', 0, 0, tiled=True)  32.7 us
    ppermute x34, starting transfers between devices, swapped(): lax.ppermute(shard, axis, [(i, j) for i, j in pairs if 0 <= j < devices])  30.8 us
    pallas_call x28, Pallas kernels, call(): pl.pallas_call(body, out_shape=tuple(((pltpu.HBM if away else pltpu.VMEM)...  22.1 us
    all_gather x3, blocking collectives, per_device(): gathered = lax.all_gather(share, 'col', axis=0, tiled=True)  21.8 us
  transfers between devices with their start and end apart: 34, of which 18 were waited for; matrix products, arithmetic and copies ran while one was open for 0% of the time, Pallas kernels for 7%

profile of v8, /device:TPU:0, one launch (start us, length us, event | category | flops | bytes accessed | tf_op | source)
XLA Modules:
  0.0 146.7 jit_solution(9954383228334847801)
XLA Ops:
  0.0 3.0 %select.1 = (f32[1024,256]{1,0:T(8,128)S(1)}, bf16[1024,256]{1,0:T(8,128)(2,1)S(1)}, bf16[512,1024]{1,0:T(8,128)(2,1)S(1)}, s32[4,128]{1,0:T(4,128)S(1)}, bf16[3...) custom-call(f32[1024,256]{1,0:T(8,128)} %bitcast.11, ...), custom_call_target="tpu_custom_call" | custom-call | flops 268435456 | bytes 5867536 | tf_op jit(solution)/shard_map/select/pallas_call | solution.py:28
  3.1 3.0 %collective-permute-start = (bf16[128,256]{1,0:T(8,128)(2,1)S(1)}, bf16[128,256]{1,0:T(8,128)(2,1)S(1)}, u32[]{:S(2)}, u32[]{:S(2)}) collective-permute-start(bf16[128,256]{1,0:T(8,128)(2,1)S(1)} %get-tuple-element.82), channel_id=1, source_target_pairs={{0,4},{4,0},{8,12},{12,8},{16,20},{20,16},{24,28},{28,24},{1,5},{5... | collective-permute-start | bytes 196616 | tf_op jit(solution)/shard_map/ppermute | solution.py:290
  6.1 3.5 %collective-permute-start.1 = (bf16[128,256]{1,0:T(8,128)(2,1)S(1)}, bf16[128,256]{1,0:T(8,128)(2,1)S(1)}, u32[]{:S(2)}, u32[]{:S(2)}) collective-permute-start(bf16[128,256]{1,0:T(8,128)(2,1)S(1)} %get-tuple-element.83), channel_id=1, source_target_pairs={{0,28},{4,8},{8,4},{12,16},{16,12},{20,24},{24,20},{28,0},{1,29},{... | collective-permute-start | bytes 196616 | tf_op jit(solution)/shard_map/ppermute | solution.py:290
  9.6 1.0 inverse_own.3.refs_1_
  10.6 2.4 %collective-permute-done.1.g1.refs_5_ = bf16[128,256]{1,0:T(8,128)(2,1)S(1)} collective-permute-done((bf16[128,256]{1,0:T(8,128)(2,1)S(1)}, bf16[128,256]{1,0:T(8,128)(2,1)S(1)}, u32[]{:S(2)}, u32[]{:S(2)}) %collective-permute-start.1) | collective-permute-done | bytes 65568 | tf_op jit(solution)/shard_map/ppermute | solution.py:290
  13.3 7.9 %all_gather.9.refs_2_ = bf16[1280,256]{1,0:T(8,128)(2,1)S(1)} all-gather(bf16[320,256]{1,0:T(8,128)(2,1)S(1)} %share.3), channel_id=1, replica_groups=mesh['row'=8,'col'=4] {'col'}, dimensions={0}, use_global_device_ids=true | all-gather | bytes 819200 | tf_op jit(solution)/shard_map/all_gather | solution.py:418
  22.0 12.1 %all_to_all.15.parts = bf16[8,32,256]{2,1,0:T(8,128)(2,1)S(1)} all-to-all(bf16[8,32,256]{2,1,0:T(8,128)(2,1)S(1)} %get-tuple-element.85), channel_id=1, replica_groups=mesh['row'=8,'col'=4] {'row'}, dimensions={0} | all-to-all | bytes 262144 | tf_op jit(solution)/shard_map/all_to_all | solution.py:435
  34.8 1.6 %collective-permute-start.3 = (bf16[128,256]{1,0:T(8,128)(2,1)S(1)}, bf16[128,256]{1,0:T(8,128)(2,1)S(1)}, u32[]{:S(2)}, u32[]{:S(2)}) collective-permute-start(bf16[128,256]{1,0:T(8,128)(2,1)S(1)} %get-tuple-element.96), channel_id=1, source_target_pairs={{0,28},{4,8},{8,4},{12,16},{16,12},{20,24},{24,20},{28,0},{1,29},{... | collective-permute-start | bytes 196616 | tf_op jit(solution)/shard_map/ppermute | solution.py:290
  37.1 2.6 %spread.1 = (bf16[1024,512]{1,0:T(8,128)(2,1)S(1)}, bf16[1536,1536]{1,0:T(8,128)(2,1)S(1)}) custom-call(bf16[1536,1536]{1,0:T(8,128)(2,1)} %bitcast.10, s32[4,128]{1,0:T(4,128)S(1)} %get-tuple-element.93.masked), custom_call_target="tpu_custom_call" | custom-call | bytes 4720640 | tf_op jit(solution)/shard_map/spread/pallas_call | solution.py:28
  39.7 2.1 %collective-permute-done.3.refs_5_ = bf16[128,256]{1,0:T(8,128)(2,1)S(1)} collective-permute-done((bf16[128,256]{1,0:T(8,128)(2,1)S(1)}, bf16[128,256]{1,0:T(8,128)(2,1)S(1)}, u32[]{:S(2)}, u32[]{:S(2)}) %collective-permute-start.3) | collective-permute-done | bytes 65568 | tf_op jit(solution)/shard_map/ppermute | solution.py:290
  43.2 1.7 %collective-permute-start.7 = (bf16[128,256]{1,0:T(8,128)(2,1)S(1)}, bf16[128,256]{1,0:T(8,128)(2,1)S(1)}, u32[]{:S(2)}, u32[]{:S(2)}) collective-permute-start(bf16[128,256]{1,0:T(8,128)(2,1)S(1)} %get-tuple-element.106), channel_id=1, source_target_pairs={{0,28},{4,8},{8,4},{12,16},{16,12},{20,24},{24,20},{28,0},{1,29},{... | collective-permute-start | bytes 196616 | tf_op jit(solution)/shard_map/ppermute | solution.py:290
  44.9 1.0 collective-permute-start.9
  45.9 1.6 %collective-permute-done.6.g0 = bf16[128,256]{1,0:T(8,128)(2,1)S(1)} collective-permute-done((bf16[128,256]{1,0:T(8,128)(2,1)S(1)}, bf16[128,256]{1,0:T(8,128)(2,1)S(1)}, u32[]{:S(2)}, u32[]{:S(2)}) %collective-permute-start.6) | collective-permute-done | bytes 65568 | tf_op jit(solution)/shard_map/ppermute | solution.py:290
  47.5 2.8 %collective-permute-done.7.g1 = bf16[128,256]{1,0:T(8,128)(2,1)S(1)} collective-permute-done((bf16[128,256]{1,0:T(8,128)(2,1)S(1)}, bf16[128,256]{1,0:T(8,128)(2,1)S(1)}, u32[]{:S(2)}, u32[]{:S(2)}) %collective-permute-start.7) | collective-permute-done | bytes 65568 | tf_op jit(solution)/shard_map/ppermute | solution.py:290
  50.3 1.2 operator_near.2.partial
  51.9 1.6 %collective-permute-start.11 = (bf16[128,256]{1,0:T(8,128)(2,1)S(1)}, bf16[128,256]{1,0:T(8,128)(2,1)S(1)}, u32[]{:S(2)}, u32[]{:S(2)}) collective-permute-start(bf16[128,256]{1,0:T(8,128)(2,1)S(1)} %get-tuple-element.110), channel_id=1, source_target_pairs={{0,28},{4,8},{8,4},{12,16},{16,12},{20,24},{24,20},{28,0},{1,29},{... | collective-permute-start | bytes 196616 | tf_op jit(solution)/shard_map/ppermute | solution.py:290
  53.5 1.0 collective-permute-start.13
  54.5 2.0 %collective-permute-done.10.r0 = bf16[128,256]{1,0:T(8,128)(2,1)S(1)} collective-permute-done((bf16[128,256]{1,0:T(8,128)(2,1)S(1)}, bf16[128,256]{1,0:T(8,128)(2,1)S(1)}, u32[]{:S(2)}, u32[]{:S(2)}) %collective-permute-start.10) | collective-permute-done | bytes 65568 | tf_op jit(solution)/shard_map/ppermute | solution.py:290
  56.5 2.4 %collective-permute-done.11.r1 = bf16[128,256]{1,0:T(8,128)(2,1)S(1)} collective-permute-done((bf16[128,256]{1,0:T(8,128)(2,1)S(1)}, bf16[128,256]{1,0:T(8,128)(2,1)S(1)}, u32[]{:S(2)}, u32[]{:S(2)}) %collective-permute-start.11) | collective-permute-done | bytes 65568 | tf_op jit(solution)/shard_map/ppermute | solution.py:290
  60.3 1.6 %collective-permute-start.15 = (bf16[128,256]{1,0:T(8,128)(2,1)S(1)}, bf16[128,256]{1,0:T(8,128)(2,1)S(1)}, u32[]{:S(2)}, u32[]{:S(2)}) collective-permute-start(bf16[128,256]{1,0:T(8,128)(2,1)S(1)} %get-tuple-element.117), channel_id=1, source_target_pairs={{0,28},{4,8},{8,4},{12,16},{16,12},{20,24},{24,20},{28,0},{1,29},{... | collective-permute-start | bytes 196616 | tf_op jit(solution)/shard_map/ppermute | solution.py:290
  62.0 1.0 inverse_own.4.refs_2_
  62.9 2.3 %collective-permute-done.14.g0.refs_5_ = bf16[128,256]{1,0:T(8,128)(2,1)S(1)} collective-permute-done((bf16[128,256]{1,0:T(8,128)(2,1)S(1)}, bf16[128,256]{1,0:T(8,128)(2,1)S(1)}, u32[]{:S(2)}, u32[]{:S(2)}) %collective-permute-start.14) | collective-permute-done | bytes 65568 | tf_op jit(solution)/shard_map/ppermute | solution.py:290
  65.2 2.1 %collective-permute-done.15.g1.refs_6_ = bf16[128,256]{1,0:T(8,128)(2,1)S(1)} collective-permute-done((bf16[128,256]{1,0:T(8,128)(2,1)S(1)}, bf16[128,256]{1,0:T(8,128)(2,1)S(1)}, u32[]{:S(2)}, u32[]{:S(2)}) %collective-permute-start.15) | collective-permute-done | bytes 65568 | tf_op jit(solution)/shard_map/ppermute | solution.py:290
  67.5 6.7 %all_gather.10.refs_3_ = bf16[1152,256]{1,0:T(8,128)(2,1)S(1)} all-gather(bf16[288,256]{1,0:T(8,128)(2,1)S(1)} %share.4), channel_id=1, replica_groups=mesh['row'=8,'col'=4] {'col'}, dimensions={0}, use_global_device_ids=true | all-gather | bytes 737280 | tf_op jit(solution)/shard_map/all_gather | solution.py:418
  75.1 10.4 %all_to_all.16.parts = bf16[8,32,256]{2,1,0:T(8,128)(2,1)S(1)} all-to-all(bf16[8,32,256]{2,1,0:T(8,128)(2,1)S(1)} %get-tuple-element.119), channel_id=1, replica_groups=mesh['row'=8,'col'=4] {'row'}, dimensions={0} | all-to-all | bytes 262144 | tf_op jit(solution)/shard_map/all_to_all | solution.py:435
  86.2 1.6 %collective-permute-start.17 = (bf16[128,256]{1,0:T(8,128)(2,1)S(1)}, bf16[128,256]{1,0:T(8,128)(2,1)S(1)}, u32[]{:S(2)}, u32[]{:S(2)}) collective-permute-start(bf16[128,256]{1,0:T(8,128)(2,1)S(1)} %get-tuple-element.123), channel_id=1, source_target_pairs={{0,28},{4,8},{8,4},{12,16},{16,12},{20,24},{24,20},{28,0},{1,29},{... | collective-permute-start | bytes 196616 | tf_op jit(solution)/shard_map/ppermute | solution.py:290
  87.8 1.2 collective-permute-start.19
  89.1 1.7 %collective-permute-done.16.refs_5_ = bf16[128,256]{1,0:T(8,128)(2,1)S(1)} collective-permute-done((bf16[128,256]{1,0:T(8,128)(2,1)S(1)}, bf16[128,256]{1,0:T(8,128)(2,1)S(1)}, u32[]{:S(2)}, u32[]{:S(2)}) %collective-permute-start.16) | collective-permute-done | bytes 65568 | tf_op jit(solution)/shard_map/ppermute | solution.py:290
  90.8 2.4 %collective-permute-done.17.refs_6_ = bf16[128,256]{1,0:T(8,128)(2,1)S(1)} collective-permute-done((bf16[128,256]{1,0:T(8,128)(2,1)S(1)}, bf16[128,256]{1,0:T(8,128)(2,1)S(1)}, u32[]{:S(2)}, u32[]{:S(2)}) %collective-permute-start.17) | collective-permute-done | bytes 65568 | tf_op jit(solution)/shard_map/ppermute | solution.py:290
  94.6 1.7 %collective-permute-start.21 = (bf16[128,256]{1,0:T(8,128)(2,1)S(1)}, bf16[128,256]{1,0:T(8,128)(2,1)S(1)}, u32[]{:S(2)}, u32[]{:S(2)}) collective-permute-start(bf16[128,256]{1,0:T(8,128)(2,1)S(1)} %get-tuple-element.129), channel_id=1, source_target_pairs={{0,28},{4,8},{8,4},{12,16},{16,12},{20,24},{24,20},{28,0},{1,29},{... | collective-permute-start | bytes 196616 | tf_op jit(solution)/shard_map/ppermute | solution.py:290
  96.3 1.2 collective-permute-start.23
  97.5 1.3 collective-permute-done.20.g0
  98.9 2.8 %collective-permute-done.21.g1 = bf16[128,256]{1,0:T(8,128)(2,1)S(1)} collective-permute-done((bf16[128,256]{1,0:T(8,128)(2,1)S(1)}, bf16[128,256]{1,0:T(8,128)(2,1)S(1)}, u32[]{:S(2)}, u32[]{:S(2)}) %collective-permute-start.21) | collective-permute-done | bytes 65568 | tf_op jit(solution)/shard_map/ppermute | solution.py:290
  101.6 1.2 operator_near.3.partial
  103.3 1.6 %collective-permute-start.25 = (bf16[128,256]{1,0:T(8,128)(2,1)S(1)}, bf16[128,256]{1,0:T(8,128)(2,1)S(1)}, u32[]{:S(2)}, u32[]{:S(2)}) collective-permute-start(bf16[128,256]{1,0:T(8,128)(2,1)S(1)} %get-tuple-element.133), channel_id=1, source_target_pairs={{0,28},{4,8},{8,4},{12,16},{16,12},{20,24},{24,20},{28,0},{1,29},{... | collective-permute-start | bytes 196616 | tf_op jit(solution)/shard_map/ppermute | solution.py:290
  104.9 1.2 collective-permute-start.27
  106.2 1.7 %collective-permute-done.24.r0 = bf16[128,256]{1,0:T(8,128)(2,1)S(1)} collective-permute-done((bf16[128,256]{1,0:T(8,128)(2,1)S(1)}, bf16[128,256]{1,0:T(8,128)(2,1)S(1)}, u32[]{:S(2)}, u32[]{:S(2)}) %collective-permute-start.24) | collective-permute-done | bytes 65568 | tf_op jit(solution)/shard_map/ppermute | solution.py:290
  107.9 2.4 %collective-permute-done.25.r1 = bf16[128,256]{1,0:T(8,128)(2,1)S(1)} collective-permute-done((bf16[128,256]{1,0:T(8,128)(2,1)S(1)}, bf16[128,256]{1,0:T(8,128)(2,1)S(1)}, u32[]{:S(2)}, u32[]{:S(2)}) %collective-permute-start.25) | collective-permute-done | bytes 65568 | tf_op jit(solution)/shard_map/ppermute | solution.py:290
  111.7 1.6 %collective-permute-start.29 = (bf16[128,256]{1,0:T(8,128)(2,1)S(1)}, bf16[128,256]{1,0:T(8,128)(2,1)S(1)}, u32[]{:S(2)}, u32[]{:S(2)}) collective-permute-start(bf16[128,256]{1,0:T(8,128)(2,1)S(1)} %get-tuple-element.140), channel_id=1, source_target_pairs={{0,28},{4,8},{8,4},{12,16},{16,12},{20,24},{24,20},{28,0},{1,29},{... | collective-permute-start | bytes 196616 | tf_op jit(solution)/shard_map/ppermute | solution.py:290
  114.3 2.3 %collective-permute-done.28.g0.refs_5_ = bf16[128,256]{1,0:T(8,128)(2,1)S(1)} collective-permute-done((bf16[128,256]{1,0:T(8,128)(2,1)S(1)}, bf16[128,256]{1,0:T(8,128)(2,1)S(1)}, u32[]{:S(2)}, u32[]{:S(2)}) %collective-permute-start.28) | collective-permute-done | bytes 65568 | tf_op jit(solution)/shard_map/ppermute | solution.py:290
  116.6 2.1 %collective-permute-done.29.g1.refs_6_ = bf16[128,256]{1,0:T(8,128)(2,1)S(1)} collective-permute-done((bf16[128,256]{1,0:T(8,128)(2,1)S(1)}, bf16[128,256]{1,0:T(8,128)(2,1)S(1)}, u32[]{:S(2)}, u32[]{:S(2)}) %collective-permute-start.29) | collective-permute-done | bytes 65568 | tf_op jit(solution)/shard_map/ppermute | solution.py:290
  118.9 7.2 %all_gather.11.refs_3_ = bf16[1152,256]{1,0:T(8,128)(2,1)S(1)} all-gather(bf16[288,256]{1,0:T(8,128)(2,1)S(1)} %share.5), channel_id=1, replica_groups=mesh['row'=8,'col'=4] {'col'}, dimensions={0}, use_global_device_ids=true | all-gather | bytes 737280 | tf_op jit(solution)/shard_map/all_gather | solution.py:418
  126.9 10.2 %all_to_all.17.parts = bf16[8,32,256]{2,1,0:T(8,128)(2,1)S(1)} all-to-all(bf16[8,32,256]{2,1,0:T(8,128)(2,1)S(1)} %get-tuple-element.142), channel_id=1, replica_groups=mesh['row'=8,'col'=4] {'row'}, dimensions={0} | all-to-all | bytes 262144 | tf_op jit(solution)/shard_map/all_to_all | solution.py:435
  137.8 1.6 %collective-permute-start.31 = (bf16[128,256]{1,0:T(8,128)(2,1)S(1)}, bf16[128,256]{1,0:T(8,128)(2,1)S(1)}, u32[]{:S(2)}, u32[]{:S(2)}) collective-permute-start(bf16[128,256]{1,0:T(8,128)(2,1)S(1)} %get-tuple-element.146), channel_id=1, source_target_pairs={{0,28},{4,8},{8,4},{12,16},{16,12},{20,24},{24,20},{28,0},{1,29},{... | collective-permute-start | bytes 196616 | tf_op jit(solution)/shard_map/ppermute | solution.py:290
  139.4 1.0 collective-permute-start.33
  140.4 1.3 collective-permute-done.30.refs_5_
  141.7 3.1 %collective-permute-done.31.refs_6_ = bf16[128,256]{1,0:T(8,128)(2,1)S(1)} collective-permute-done((bf16[128,256]{1,0:T(8,128)(2,1)S(1)}, bf16[128,256]{1,0:T(8,128)(2,1)S(1)}, u32[]{:S(2)}, u32[]{:S(2)}) %collective-permute-start.31) | collective-permute-done | bytes 65568 | tf_op jit(solution)/shard_map/ppermute | solution.py:290
  145.3 1.2 last_update.1
  (56 shorter events, 13.9 us)
Async XLA Ops:
  3.1 7.6 %collective-permute-start = (bf16[128,256]{1,0:T(8,128)(2,1)S(1)}, bf16[128,256]{1,0:T(8,128)(2,1)S(1)}, u32[]{:S(2)}, u32[]{:S(2)}) collective-permute-start(bf16[128,256]{1,0:T(8,128)(2,1)S(1)} %get-tuple-element.82), channel_id=1, source_target_pairs={{0,4},{4,0},{8,12},{12,8},{16,20},{20,16},{24,28},{28,24},{1,5},{5... | collective-permute-start | bytes 196616 | tf_op jit(solution)/shard_map/ppermute | solution.py:290
  6.1 7.0 %collective-permute-start.1 = (bf16[128,256]{1,0:T(8,128)(2,1)S(1)}, bf16[128,256]{1,0:T(8,128)(2,1)S(1)}, u32[]{:S(2)}, u32[]{:S(2)}) collective-permute-start(bf16[128,256]{1,0:T(8,128)(2,1)S(1)} %get-tuple-element.83), channel_id=1, source_target_pairs={{0,28},{4,8},{8,4},{12,16},{16,12},{20,24},{24,20},{28,0},{1,29},{... | collective-permute-start | bytes 196616 | tf_op jit(solution)/shard_map/ppermute | solution.py:290
  10.6 10.5 %copy-start = (bf16[8,32,128]{2,1,0:T(8,128)(2,1)S(1)}, bf16[8,32,128]{2,1,0:T(8,128)(2,1)}, u32[]{:S(2)}) copy-start(bf16[8,32,128]{2,1,0:T(8,128)(2,1)} %refs_4_.3) | copy-start | bytes 196612
  34.4 5.3 %collective-permute-start.2 = (bf16[128,256]{1,0:T(8,128)(2,1)S(1)}, bf16[128,256]{1,0:T(8,128)(2,1)S(1)}, u32[]{:S(2)}, u32[]{:S(2)}) collective-permute-start(bf16[128,256]{1,0:T(8,128)(2,1)S(1)} %get-tuple-element.95), channel_id=1, source_target_pairs={{0,4},{4,0},{8,12},{12,8},{16,20},{20,16},{24,28},{28,24},{1,5},{5... | collective-permute-start | bytes 196616 | tf_op jit(solution)/shard_map/ppermute | solution.py:290
  34.8 7.0 %collective-permute-start.3 = (bf16[128,256]{1,0:T(8,128)(2,1)S(1)}, bf16[128,256]{1,0:T(8,128)(2,1)S(1)}, u32[]{:S(2)}, u32[]{:S(2)}) collective-permute-start(bf16[128,256]{1,0:T(8,128)(2,1)S(1)} %get-tuple-element.96), channel_id=1, source_target_pairs={{0,28},{4,8},{8,4},{12,16},{16,12},{20,24},{24,20},{28,0},{1,29},{... | collective-permute-start | bytes 196616 | tf_op jit(solution)/shard_map/ppermute | solution.py:290
  36.4 5.8 %collective-permute-start.4 = (bf16[128,256]{1,0:T(8,128)(2,1)S(1)}, bf16[128,256]{1,0:T(8,128)(2,1)S(1)}, u32[]{:S(2)}, u32[]{:S(2)}) collective-permute-start(bf16[128,256]{1,0:T(8,128)(2,1)S(1)} %get-tuple-element.98), channel_id=1, source_target_pairs={{0,1},{1,0},{2,3},{3,2},{4,5},{5,4},{6,7},{7,6},{8,9},{9,8},{10,11... | collective-permute-start | bytes 196616 | tf_op jit(solution)/shard_map/ppermute | solution.py:290
  36.4 5.8 %collective-permute-start.5 = (bf16[128,256]{1,0:T(8,128)(2,1)S(1)}, bf16[128,256]{1,0:T(8,128)(2,1)S(1)}, u32[]{:S(2)}, u32[]{:S(2)}) collective-permute-start(bf16[128,256]{1,0:T(8,128)(2,1)S(1)} %get-tuple-element.99), channel_id=1, source_target_pairs={{0,3},{1,2},{2,1},{3,0},{4,7},{5,6},{6,5},{7,4},{8,11},{9,10},{10,... | collective-permute-start | bytes 196616 | tf_op jit(solution)/shard_map/ppermute | solution.py:290
  43.2 4.3 %collective-permute-start.6 = (bf16[128,256]{1,0:T(8,128)(2,1)S(1)}, bf16[128,256]{1,0:T(8,128)(2,1)S(1)}, u32[]{:S(2)}, u32[]{:S(2)}) collective-permute-start(bf16[128,256]{1,0:T(8,128)(2,1)S(1)} %get-tuple-element.105), channel_id=1, source_target_pairs={{0,4},{4,0},{8,12},{12,8},{16,20},{20,16},{24,28},{28,24},{1,5},{5... | collective-permute-start | bytes 196616 | tf_op jit(solution)/shard_map/ppermute | solution.py:290
  43.2 7.0 %collective-permute-start.7 = (bf16[128,256]{1,0:T(8,128)(2,1)S(1)}, bf16[128,256]{1,0:T(8,128)(2,1)S(1)}, u32[]{:S(2)}, u32[]{:S(2)}) collective-permute-start(bf16[128,256]{1,0:T(8,128)(2,1)S(1)} %get-tuple-element.106), channel_id=1, source_target_pairs={{0,28},{4,8},{8,4},{12,16},{16,12},{20,24},{24,20},{28,0},{1,29},{... | collective-permute-start | bytes 196616 | tf_op jit(solution)/shard_map/ppermute | solution.py:290
  44.9 6.5 %collective-permute-start.8 = (bf16[128,256]{1,0:T(8,128)(2,1)S(1)}, bf16[128,256]{1,0:T(8,128)(2,1)S(1)}, u32[]{:S(2)}, u32[]{:S(2)}) collective-permute-start(bf16[128,256]{1,0:T(8,128)(2,1)S(1)} %get-tuple-element.107), channel_id=1, source_target_pairs={{0,1},{1,0},{2,3},{3,2},{4,5},{5,4},{6,7},{7,6},{8,9},{9,8},{10,11... | collective-permute-start | bytes 196616 | tf_op jit(solution)/shard_map/ppermute | solution.py:290
  44.9 6.6 %collective-permute-start.9 = (bf16[128,256]{1,0:T(8,128)(2,1)S(1)}, bf16[128,256]{1,0:T(8,128)(2,1)S(1)}, u32[]{:S(2)}, u32[]{:S(2)}) collective-permute-start(bf16[128,256]{1,0:T(8,128)(2,1)S(1)} %get-tuple-element.108), channel_id=1, source_target_pairs={{0,3},{1,2},{2,1},{3,0},{4,7},{5,6},{6,5},{7,4},{8,11},{9,10},{10,... | collective-permute-start | bytes 196616 | tf_op jit(solution)/shard_map/ppermute | solution.py:290
  51.7 4.8 %collective-permute-start.10 = (bf16[128,256]{1,0:T(8,128)(2,1)S(1)}, bf16[128,256]{1,0:T(8,128)(2,1)S(1)}, u32[]{:S(2)}, u32[]{:S(2)}) collective-permute-start(bf16[128,256]{1,0:T(8,128)(2,1)S(1)} %get-tuple-element.109), channel_id=1, source_target_pairs={{0,4},{4,0},{8,12},{12,8},{16,20},{20,16},{24,28},{28,24},{1,5},{5... | collective-permute-start | bytes 196616 | tf_op jit(solution)/shard_map/ppermute | solution.py:290
  51.9 7.0 %collective-permute-start.11 = (bf16[128,256]{1,0:T(8,128)(2,1)S(1)}, bf16[128,256]{1,0:T(8,128)(2,1)S(1)}, u32[]{:S(2)}, u32[]{:S(2)}) collective-permute-start(bf16[128,256]{1,0:T(8,128)(2,1)S(1)} %get-tuple-element.110), channel_id=1, source_target_pairs={{0,28},{4,8},{8,4},{12,16},{16,12},{20,24},{24,20},{28,0},{1,29},{... | collective-permute-start | bytes 196616 | tf_op jit(solution)/shard_map/ppermute | solution.py:290
  53.5 5.8 %collective-permute-start.12 = (bf16[128,256]{1,0:T(8,128)(2,1)S(1)}, bf16[128,256]{1,0:T(8,128)(2,1)S(1)}, u32[]{:S(2)}, u32[]{:S(2)}) collective-permute-start(bf16[128,256]{1,0:T(8,128)(2,1)S(1)} %get-tuple-element.111), channel_id=1, source_target_pairs={{0,1},{1,0},{2,3},{3,2},{4,5},{5,4},{6,7},{7,6},{8,9},{9,8},{10,11... | collective-permute-start | bytes 196616 | tf_op jit(solution)/shard_map/ppermute | solution.py:290
  53.5 5.8 %collective-permute-start.13 = (bf16[128,256]{1,0:T(8,128)(2,1)S(1)}, bf16[128,256]{1,0:T(8,128)(2,1)S(1)}, u32[]{:S(2)}, u32[]{:S(2)}) collective-permute-start(bf16[128,256]{1,0:T(8,128)(2,1)S(1)} %get-tuple-element.112), channel_id=1, source_target_pairs={{0,3},{1,2},{2,1},{3,0},{4,7},{5,6},{6,5},{7,4},{8,11},{9,10},{10,... | collective-permute-start | bytes 196616 | tf_op jit(solution)/shard_map/ppermute | solution.py:290
  60.2 5.0 %collective-permute-start.14 = (bf16[128,256]{1,0:T(8,128)(2,1)S(1)}, bf16[128,256]{1,0:T(8,128)(2,1)S(1)}, u32[]{:S(2)}, u32[]{:S(2)}) collective-permute-start(bf16[128,256]{1,0:T(8,128)(2,1)S(1)} %get-tuple-element.116), channel_id=1, source_target_pairs={{0,4},{4,0},{8,12},{12,8},{16,20},{20,16},{24,28},{28,24},{1,5},{5... | collective-permute-start | bytes 196616 | tf_op jit(solution)/shard_map/ppermute | solution.py:290
  60.3 7.0 %collective-permute-start.15 = (bf16[128,256]{1,0:T(8,128)(2,1)S(1)}, bf16[128,256]{1,0:T(8,128)(2,1)S(1)}, u32[]{:S(2)}, u32[]{:S(2)}) collective-permute-start(bf16[128,256]{1,0:T(8,128)(2,1)S(1)} %get-tuple-element.117), channel_id=1, source_target_pairs={{0,28},{4,8},{8,4},{12,16},{16,12},{20,24},{24,20},{28,0},{1,29},{... | collective-permute-start | bytes 196616 | tf_op jit(solution)/shard_map/ppermute | solution.py:290
  85.7 5.0 %collective-permute-start.16 = (bf16[128,256]{1,0:T(8,128)(2,1)S(1)}, bf16[128,256]{1,0:T(8,128)(2,1)S(1)}, u32[]{:S(2)}, u32[]{:S(2)}) collective-permute-start(bf16[128,256]{1,0:T(8,128)(2,1)S(1)} %get-tuple-element.122), channel_id=1, source_target_pairs={{0,4},{4,0},{8,12},{12,8},{16,20},{20,16},{24,28},{28,24},{1,5},{5... | collective-permute-start | bytes 196616 | tf_op jit(solution)/shard_map/ppermute | solution.py:290
  86.2 7.0 %collective-permute-start.17 = (bf16[128,256]{1,0:T(8,128)(2,1)S(1)}, bf16[128,256]{1,0:T(8,128)(2,1)S(1)}, u32[]{:S(2)}, u32[]{:S(2)}) collective-permute-start(bf16[128,256]{1,0:T(8,128)(2,1)S(1)} %get-tuple-element.123), channel_id=1, source_target_pairs={{0,28},{4,8},{8,4},{12,16},{16,12},{20,24},{24,20},{28,0},{1,29},{... | collective-permute-start | bytes 196616 | tf_op jit(solution)/shard_map/ppermute | solution.py:290
  87.8 5.8 %collective-permute-start.18 = (bf16[128,256]{1,0:T(8,128)(2,1)S(1)}, bf16[128,256]{1,0:T(8,128)(2,1)S(1)}, u32[]{:S(2)}, u32[]{:S(2)}) collective-permute-start(bf16[128,256]{1,0:T(8,128)(2,1)S(1)} %get-tuple-element.124), channel_id=1, source_target_pairs={{0,1},{1,0},{2,3},{3,2},{4,5},{5,4},{6,7},{7,6},{8,9},{9,8},{10,11... | collective-permute-start | bytes 196616 | tf_op jit(solution)/shard_map/ppermute | solution.py:290
  87.8 5.8 %collective-permute-start.19 = (bf16[128,256]{1,0:T(8,128)(2,1)S(1)}, bf16[128,256]{1,0:T(8,128)(2,1)S(1)}, u32[]{:S(2)}, u32[]{:S(2)}) collective-permute-start(bf16[128,256]{1,0:T(8,128)(2,1)S(1)} %get-tuple-element.125), channel_id=1, source_target_pairs={{0,3},{1,2},{2,1},{3,0},{4,7},{5,6},{6,5},{7,4},{8,11},{9,10},{10,... | collective-permute-start | bytes 196616 | tf_op jit(solution)/shard_map/ppermute | solution.py:290
  94.5 4.3 %collective-permute-start.20 = (bf16[128,256]{1,0:T(8,128)(2,1)S(1)}, bf16[128,256]{1,0:T(8,128)(2,1)S(1)}, u32[]{:S(2)}, u32[]{:S(2)}) collective-permute-start(bf16[128,256]{1,0:T(8,128)(2,1)S(1)} %get-tuple-element.128), channel_id=1, source_target_pairs={{0,4},{4,0},{8,12},{12,8},{16,20},{20,16},{24,28},{28,24},{1,5},{5... | collective-permute-start | bytes 196616 | tf_op jit(solution)/shard_map/ppermute | solution.py:290
  94.6 7.0 %collective-permute-start.21 = (bf16[128,256]{1,0:T(8,128)(2,1)S(1)}, bf16[128,256]{1,0:T(8,128)(2,1)S(1)}, u32[]{:S(2)}, u32[]{:S(2)}) collective-permute-start(bf16[128,256]{1,0:T(8,128)(2,1)S(1)} %get-tuple-element.129), channel_id=1, source_target_pairs={{0,28},{4,8},{8,4},{12,16},{16,12},{20,24},{24,20},{28,0},{1,29},{... | collective-permute-start | bytes 196616 | tf_op jit(solution)/shard_map/ppermute | solution.py:290
  96.3 6.5 %collective-permute-start.22 = (bf16[128,256]{1,0:T(8,128)(2,1)S(1)}, bf16[128,256]{1,0:T(8,128)(2,1)S(1)}, u32[]{:S(2)}, u32[]{:S(2)}) collective-permute-start(bf16[128,256]{1,0:T(8,128)(2,1)S(1)} %get-tuple-element.130), channel_id=1, source_target_pairs={{0,1},{1,0},{2,3},{3,2},{4,5},{5,4},{6,7},{7,6},{8,9},{9,8},{10,11... | collective-permute-start | bytes 196616 | tf_op jit(solution)/shard_map/ppermute | solution.py:290
  96.3 6.6 %collective-permute-start.23 = (bf16[128,256]{1,0:T(8,128)(2,1)S(1)}, bf16[128,256]{1,0:T(8,128)(2,1)S(1)}, u32[]{:S(2)}, u32[]{:S(2)}) collective-permute-start(bf16[128,256]{1,0:T(8,128)(2,1)S(1)} %get-tuple-element.131), channel_id=1, source_target_pairs={{0,3},{1,2},{2,1},{3,0},{4,7},{5,6},{6,5},{7,4},{8,11},{9,10},{10,... | collective-permute-start | bytes 196616 | tf_op jit(solution)/shard_map/ppermute | solution.py:290
  103.1 4.8 %collective-permute-start.24 = (bf16[128,256]{1,0:T(8,128)(2,1)S(1)}, bf16[128,256]{1,0:T(8,128)(2,1)S(1)}, u32[]{:S(2)}, u32[]{:S(2)}) collective-permute-start(bf16[128,256]{1,0:T(8,128)(2,1)S(1)} %get-tuple-element.132), channel_id=1, source_target_pairs={{0,4},{4,0},{8,12},{12,8},{16,20},{20,16},{24,28},{28,24},{1,5},{5... | collective-permute-start | bytes 196616 | tf_op jit(solution)/shard_map/ppermute | solution.py:290
  103.3 7.0 %collective-permute-start.25 = (bf16[128,256]{1,0:T(8,128)(2,1)S(1)}, bf16[128,256]{1,0:T(8,128)(2,1)S(1)}, u32[]{:S(2)}, u32[]{:S(2)}) collective-permute-start(bf16[128,256]{1,0:T(8,128)(2,1)S(1)} %get-tuple-element.133), channel_id=1, source_target_pairs={{0,28},{4,8},{8,4},{12,16},{16,12},{20,24},{24,20},{28,0},{1,29},{... | collective-permute-start | bytes 196616 | tf_op jit(solution)/shard_map/ppermute | solution.py:290
  104.9 5.8 %collective-permute-start.26 = (bf16[128,256]{1,0:T(8,128)(2,1)S(1)}, bf16[128,256]{1,0:T(8,128)(2,1)S(1)}, u32[]{:S(2)}, u32[]{:S(2)}) collective-permute-start(bf16[128,256]{1,0:T(8,128)(2,1)S(1)} %get-tuple-element.134), channel_id=1, source_target_pairs={{0,1},{1,0},{2,3},{3,2},{4,5},{5,4},{6,7},{7,6},{8,9},{9,8},{10,11... | collective-permute-start | bytes 196616 | tf_op jit(solution)/shard_map/ppermute | solution.py:290
  104.9 5.8 %collective-permute-start.27 = (bf16[128,256]{1,0:T(8,128)(2,1)S(1)}, bf16[128,256]{1,0:T(8,128)(2,1)S(1)}, u32[]{:S(2)}, u32[]{:S(2)}) collective-permute-start(bf16[128,256]{1,0:T(8,128)(2,1)S(1)} %get-tuple-element.135), channel_id=1, source_target_pairs={{0,3},{1,2},{2,1},{3,0},{4,7},{5,6},{6,5},{7,4},{8,11},{9,10},{10,... | collective-permute-start | bytes 196616 | tf_op jit(solution)/shard_map/ppermute | solution.py:290
  111.6 5.0 %collective-permute-start.28 = (bf16[128,256]{1,0:T(8,128)(2,1)S(1)}, bf16[128,256]{1,0:T(8,128)(2,1)S(1)}, u32[]{:S(2)}, u32[]{:S(2)}) collective-permute-start(bf16[128,256]{1,0:T(8,128)(2,1)S(1)} %get-tuple-element.139), channel_id=1, source_target_pairs={{0,4},{4,0},{8,12},{12,8},{16,20},{20,16},{24,28},{28,24},{1,5},{5... | collective-permute-start | bytes 196616 | tf_op jit(solution)/shard_map/ppermute | solution.py:290
  111.7 7.0 %collective-permute-start.29 = (bf16[128,256]{1,0:T(8,128)(2,1)S(1)}, bf16[128,256]{1,0:T(8,128)(2,1)S(1)}, u32[]{:S(2)}, u32[]{:S(2)}) collective-permute-start(bf16[128,256]{1,0:T(8,128)(2,1)S(1)} %get-tuple-element.140), channel_id=1, source_target_pairs={{0,28},{4,8},{8,4},{12,16},{16,12},{20,24},{24,20},{28,0},{1,29},{... | collective-permute-start | bytes 196616 | tf_op jit(solution)/shard_map/ppermute | solution.py:290
  137.4 4.3 %collective-permute-start.30 = (bf16[128,256]{1,0:T(8,128)(2,1)S(1)}, bf16[128,256]{1,0:T(8,128)(2,1)S(1)}, u32[]{:S(2)}, u32[]{:S(2)}) collective-permute-start(bf16[128,256]{1,0:T(8,128)(2,1)S(1)} %get-tuple-element.145), channel_id=1, source_target_pairs={{0,4},{4,0},{8,12},{12,8},{16,20},{20,16},{24,28},{28,24},{1,5},{5... | collective-permute-start | bytes 196616 | tf_op jit(solution)/shard_map/ppermute | solution.py:290
  137.8 7.0 %collective-permute-start.31 = (bf16[128,256]{1,0:T(8,128)(2,1)S(1)}, bf16[128,256]{1,0:T(8,128)(2,1)S(1)}, u32[]{:S(2)}, u32[]{:S(2)}) collective-permute-start(bf16[128,256]{1,0:T(8,128)(2,1)S(1)} %get-tuple-element.146), channel_id=1, source_target_pairs={{0,28},{4,8},{8,4},{12,16},{16,12},{20,24},{24,20},{28,0},{1,29},{... | collective-permute-start | bytes 196616 | tf_op jit(solution)/shard_map/ppermute | solution.py:290
  139.4 5.8 %collective-permute-start.32 = (bf16[128,256]{1,0:T(8,128)(2,1)S(1)}, bf16[128,256]{1,0:T(8,128)(2,1)S(1)}, u32[]{:S(2)}, u32[]{:S(2)}) collective-permute-start(bf16[128,256]{1,0:T(8,128)(2,1)S(1)} %get-tuple-element.147), channel_id=1, source_target_pairs={{0,1},{1,0},{2,3},{3,2},{4,5},{5,4},{6,7},{7,6},{8,9},{9,8},{10,11... | collective-permute-start | bytes 196616 | tf_op jit(solution)/shard_map/ppermute | solution.py:290
  139.4 5.8 %collective-permute-start.33 = (bf16[128,256]{1,0:T(8,128)(2,1)S(1)}, bf16[128,256]{1,0:T(8,128)(2,1)S(1)}, u32[]{:S(2)}, u32[]{:S(2)}) collective-permute-start(bf16[128,256]{1,0:T(8,128)(2,1)S(1)} %get-tuple-element.148), channel_id=1, source_target_pairs={{0,3},{1,2},{2,1},{3,0},{4,7},{5,6},{6,5},{7,4},{8,11},{9,10},{10,... | collective-permute-start | bytes 196616 | tf_op jit(solution)/shard_map/ppermute | solution.py:290

commit v9 on v8

--- a/solution.py
+++ b/solution.py
@@ -72,7 +72,7 @@
 
 
 def select_kernel(
-    far_target, far_rows, far_counts, far_basis, far_inverse, target, half, pick, masked, basis, inverse, *rest
+    far_target, far_rows, far_counts, far_basis, target, half, pick, masked, basis, *rest
 ):
     *tiles, rows, counts, sems = rest
     own = target.shape[0]
@@ -82,7 +82,6 @@
         (far_basis.at[:, far], basis.at[:, near])
         for far, near in [(slice(0, own), slice(0, own))] + margin_spans(own, tile)
     ]
-    pairs += matrix_pieces(far_inverse, inverse, own, tile)
     loads = started(pairs, sems)
     loads[0].wait()
     loads[1].wait()
@@ -135,9 +134,11 @@
     return jnp.concatenate([part[...] for part in parts], axis=0)
 
 
-def own_columns_kernel(matrix, owned, out):
+def load_kernel(far, owned, matrix, sems):
     own = owned.shape[0]
-    out[...] = product(matrix[:, :own], owned[...])
+    tile = (matrix.shape[0] - own) // 4
+    for load in started(matrix_pieces(far, matrix, own, tile), sems):
+        load.wait()
 
 
 def near_columns_kernel(matrix, owned, g0, g1, out):
@@ -146,72 +147,70 @@
     out[...] = product(matrix[:, :own], owned[...]) + product(matrix[:, own:split], stacked(g0, g1))
 
 
-def share_kernel(basis, owned, t2, t3, g0, g1, out):
-    own, tile, coarse = owned.shape[0], t2.shape[0], basis.shape[0]
-    split = own + 2 * tile
-    out[:tile, :] = t2[...]
-    out[tile : 2 * tile, :] = t3[...]
-    out[2 * tile : 2 * tile + coarse, :] = (
-        product(basis[:, :own], owned[...]) + product(basis[:, own:split], stacked(g0, g1))
-    ).astype(HALF)
-    if out.shape[0] > 2 * tile + coarse:
-        out[2 * tile + coarse :, : 2 * tile] = basis[:, split:]
-
-
-def solve_kernel(first, across):
+def near_solve_kernel(matrix, basis, owned, g0, g1, out, restricted):
+    own = owned.shape[0]
+    split = own + 2 * g0.shape[0]
+    ghosts = stacked(g0, g1)
+    out[...] = product(matrix[:, :own], owned[...]) + product(matrix[:, own:split], ghosts)
+    restricted[...] = product(basis[:, :own], owned[...]) + product(basis[:, own:split], ghosts)
+
+
+def restrict_kernel(basis, near, g2, g3, out):
+    split = basis.shape[1] - 2 * g2.shape[0]
+    out[...] = (near[...] + product(basis[:, split:], stacked(g2, g3))).astype(HALF)
+
+
+def solve_kernel(matrix, partial, g2, g3, rim, inner):
+    own = inner.shape[0]
+    ghosts = stacked(g2, g3)
+    split = matrix.shape[1] - ghosts.shape[0]
+    rim[...] = partial[own:, :] + product(matrix[own:, split:], ghosts)
+    inner[...] = partial[:own, :] + product(matrix[:own, split:], ghosts)
+
+
+def met(place, turn, devices):
+    if devices & (devices - 1) == 0:
+        return place ^ turn
+    return (turn + devices - place) % devices
+
+
+def meeting(shard, axis, turn):
+    devices = lax.axis_size(axis)
+    pairs = [(i, met(i, turn, devices)) for i in range(devices)]
+    return shard if all(i == j for i, j in pairs) else lax.ppermute(shard, axis, pairs)
+
+
+def parts_kernel(groups, across):
+    def body(inverse, *refs):
+        restricted, parts, gathered = refs[:across], refs[across:-1], refs[-1]
+        coarse = inverse.shape[1]
+        for turn, piece in enumerate(restricted):
+            at = pl.multiple_of(met(lax.axis_index("col"), turn, across) * coarse, coarse)
+            gathered[pl.ds(at, coarse), :] = piece[...]
+        for turn, part in enumerate(parts):
+            other = met(lax.axis_index("row"), turn, groups)
+            part[...] = product(inverse[other], gathered[...]).astype(HALF)
+
+    return body
+
+
+def coarse_kernel(groups):
     def body(*refs):
-        refs = list(refs)
-        rims = None if first else refs.pop(0)
-        matrix, partial, gathered, inverse, g0, g1, parts, rim, inner, *rest = refs
-        tile, coarse = g0.shape[0], inverse.shape[1]
-        own = inner.shape[0]
-        stride = gathered.shape[0] // across
-        if first:
-            (rims,) = rest
-            for b in range(across):
-                at = b * stride + 2 * tile + coarse
-                rims[b * coarse : (b + 1) * coarse, :] = gathered[at : at + coarse, : 2 * tile]
-        restricted = []
-        for b in range(across):
-            here = slice(b * coarse, (b + 1) * coarse)
-            at = b * stride + 2 * tile
-            total = gathered[at : at + coarse, :].astype(FULL)
-            for i in range(2):
-                other = partner(b, i)
-                if 0 <= other < across:
-                    at = other * stride + i * tile
-                    total += product(
-                        rims[here, i * tile : (i + 1) * tile], gathered[at : at + tile, :]
-                    )
-            restricted.append(total.astype(HALF))
-        restricted = jnp.concatenate(restricted, axis=0)
-        for i in range(parts.shape[0]):
-            parts[i, :, :] = product(inverse[i, :, :], restricted).astype(HALF)
-        ghosts = [g0[...], g1[...]]
-        for i in range(2):
-            other = partner(lax.axis_index("col"), i)
-            there = (other >= 0) & (other < across)
-            at = pl.multiple_of(jnp.where(there, other, 0) * stride + i * tile, 32)
-            ghost = gathered[pl.ds(at, tile), :]
-            ghosts.append(jnp.where(there, ghost, jnp.zeros_like(ghost)))
-        ghosts = jnp.concatenate(ghosts, axis=0)
-        rim[...] = partial[own:, :] + product(matrix[own:, own:], ghosts)
-        inner[...] = partial[:own, :] + product(matrix[:own, own:], ghosts)
+        parts, (basis, rim, level, *tiles) = refs[:groups], refs[groups:]
+        tile = tiles[0].shape[0]
+        own = basis.shape[1] - 4 * tile
+        total = parts[0][...].astype(FULL)
+        for part in parts[1:]:
+            total += part[...].astype(FULL)
+        level[...] = total.astype(HALF)
+        for d in range(4):
+            here = slice(d * tile, (d + 1) * tile)
+            there = slice(own + d * tile, own + (d + 1) * tile)
+            tiles[d][...] = (
+                rim[here, :] + turned_product(basis[:, there], level[...])
+            ).astype(HALF)
 
     return body
-
-
-def coarse_kernel(parts, basis, rim, level, *tiles):
-    tile = tiles[0].shape[0]
-    own = basis.shape[1] - 4 * tile
-    total = parts[0, :, :].astype(FULL)
-    for i in range(1, parts.shape[0]):
-        total += parts[i, :, :].astype(FULL)
-    level[...] = total.astype(HALF)
-    for d in range(4):
-        here = slice(d * tile, (d + 1) * tile)
-        there = slice(own + d * tile, own + (d + 1) * tile)
-        tiles[d][...] = (rim[here, :] + turned_product(basis[:, there], level[...])).astype(HALF)
 
 
 def base_kernel(first):
@@ -290,12 +289,8 @@
     return lax.ppermute(shard, axis, [(i, j) for i, j in pairs if 0 <= j < devices])
 
 
-def traded_over_row(tiles):
-    return tuple(swapped(tiles[i], "row", i) for i in range(2))
-
-
 def traded(tiles):
-    return traded_over_row(tiles) + tuple(swapped(tiles[2 + i], "col", i) for i in range(2))
+    return tuple(swapped(tiles[i], "row" if i < 2 else "col", i % 2) for i in range(4))
 
 
 def per_device(
@@ -318,7 +313,7 @@
     owned_half = ((own, columns), HALF)
     owned_full = ((own, columns), FULL)
     local_full = ((local, columns), FULL)
-    target, residual, pick, masked, basis, inverse, *tiles = call(
+    target, residual, pick, masked, basis, *tiles = call(
         select_kernel,
         "select",
         [
@@ -327,23 +322,21 @@
             ((margin, own), HALF),
             (rows_list.shape, jnp.int32),
             (basis.shape, HALF),
-            (inverse.shape, HALF),
         ]
         + four_tiles,
         target,
         rows_list,
         send_count[0],
         basis,
-        inverse,
-        far=5,
+        far=4,
         scratch=(
             pltpu.VMEM(rows_list.shape, jnp.int32),
             pltpu.SMEM((1, 4), jnp.int32),
-            pltpu.SemaphoreType.DMA((8 + MATRIX_PIECES,)),
+            pltpu.SemaphoreType.DMA((8,)),
         ),
         flops=2 * margin * own * columns,
     )
-    rims = spread = solution = None
+    spread = solution = None
     for sweep in range(ITERS):
         first, last = sweep == 0, sweep == ITERS - 1
         if sweep:
@@ -394,50 +387,65 @@
                 r3,
                 flops=(2 * margin + 4 * tile) * own * columns,
             )
-        g0, g1 = traded_over_row(tiles)
-        (partial,) = call(
-            own_columns_kernel,
-            "inverse_own",
-            [local_full],
+        if first:
+            residual, tiles = lax.optimization_barrier((residual, tuple(tiles)))
+            (inverse,) = call(
+                load_kernel,
+                "load",
+                [(inverse.shape, HALF)],
+                inverse,
+                residual,
+                far=1,
+                scratch=(pltpu.SemaphoreType.DMA((MATRIX_PIECES,)),),
+            )
+        g0, g1, g2, g3 = traded(tiles)
+        partial, near = call(
+            near_solve_kernel,
+            "inverse_near",
+            [local_full, ((coarse, columns), FULL)],
             inverse,
-            residual,
-            flops=2 * local * own * columns,
-        )
-        (share,) = call(
-            share_kernel,
-            "share",
-            [((2 * tile + coarse * (2 if first else 1), columns), HALF)],
             basis,
             residual,
-            tiles[2],
-            tiles[3],
             g0,
             g1,
-            flops=2 * local * coarse * columns,
-        )
-        gathered = lax.all_gather(share, "col", axis=0, tiled=True)
-        outs = [((groups, coarse, columns), HALF), ((margin, columns), FULL), owned_full]
-        parts, rim, inner, *rest = call(
-            solve_kernel(first, across),
+            flops=2 * (local + coarse) * (own + 2 * tile) * columns,
+        )
+        (restricted,) = call(
+            restrict_kernel,
+            "restrict",
+            [((coarse, columns), HALF)],
+            basis,
+            near,
+            g2,
+            g3,
+            flops=4 * coarse * tile * columns,
+        )
+        restricted = [meeting(restricted, "col", turn) for turn in reversed(range(across))][::-1]
+        rim, inner = call(
+            solve_kernel,
             "inverse_margin",
-            outs + ([((across * coarse, 2 * tile), HALF)] if first else []),
-            *([] if first else [rims]),
+            [((margin, columns), FULL), owned_full],
             inverse,
             partial,
-            gathered,
+            g2,
+            g3,
+            flops=4 * local * tile * columns,
+        )
+        parts = call(
+            parts_kernel(groups, across),
+            "coarse_part",
+            [((coarse, columns), HALF)] * groups,
             coarse_inverse,
-            g0,
-            g1,
-            flops=2 * (local * margin + coarse_inverse.size) * columns,
-        )
-        if first:
-            (rims,) = rest
-        parts = lax.all_to_all(parts, "row", 0, 0, tiled=True)
+            *restricted,
+            scratch=(pltpu.VMEM((across * coarse, columns), HALF),),
+            flops=2 * coarse_inverse.size * columns,
+        )
+        parts = [meeting(parts[turn], "row", turn) for turn in reversed(range(groups))]
         level, *tiles = call(
-            coarse_kernel,
+            coarse_kernel(groups),
             "coarse",
             [((coarse, columns), HALF)] + four_tiles,
-            parts,
+            *parts,
             basis,
             rim,
             flops=2 * coarse * margin * columns,

time: 147 us -> 149 us (1.014)
  starting transfers between devices: 30.8 us -> 94.2 us
  blocking collectives: 54.5 us -> 0 us
  waiting for transfers between devices: 38.6 us -> 30.7 us
    ppermute x0 -> x30, starting transfers between devices: none -> 39.3 us  [meeting(): lax.ppermute(shard, axis, pairs)]
    all_to_all x3 -> x0, blocking collectives: 32.7 us -> none  [per_device(): parts = lax.all_to_all(parts, 'row', 0, 0, tiled=True)]
    ppermute x34 -> x40, starting transfers between devices: 30.8 us -> 54.9 us  [swapped(): lax.ppermute(shard, axis, [(i, j) for i, j in pairs if 0 <= j < devices])]
    all_gather x3 -> x0, blocking collectives: 21.8 us -> none  [per_device(): gathered = lax.all_gather(share, 'col', axis=0, tiled=True)]
    ppermute x34 -> x40, waiting for transfers between devices: 38.6 us -> 20.5 us  [swapped(): lax.ppermute(shard, axis, [(i, j) for i, j in pairs if 0 <= j < devices])]
    ppermute x0 -> x30, waiting for transfers between devices: none -> 10.1 us  [meeting(): lax.ppermute(shard, axis, pairs)]
    pallas_call x28 -> x32, Pallas kernels: 22.1 us -> 23.5 us  [call(): pl.pallas_call(body, out_shape=tuple(((pltpu.HBM if away else pltpu.VMEM)...]
  transfers between devices with their start and end apart: 34 -> 70, of which waited for: 18 -> 21; matrix products, arithmetic and copies ran while one was open for 0% -> 0% of each run, Pallas kernels for 7% -> 10%
where the time goes in v9:
time: 149 us
  starting transfers between devices  94.2 us (63%)
  waiting for transfers between devices  30.7 us (21%)
  Pallas kernels  23.5 us (16%)
    ppermute x40, starting transfers between devices, swapped(): lax.ppermute(shard, axis, [(i, j) for i, j in pairs if 0 <= j < devices])  54.9 us
    ppermute x30, starting transfers between devices, meeting(): lax.ppermute(shard, axis, pairs)  39.3 us
    pallas_call x32, Pallas kernels, call(): pl.pallas_call(body, out_shape=tuple(((pltpu.HBM if away else pltpu.VMEM)...  23.5 us
    ppermute x40, waiting for transfers between devices, swapped(): lax.ppermute(shard, axis, [(i, j) for i, j in pairs if 0 <= j < devices])  20.5 us
    ppermute x30, waiting for transfers between devices, meeting(): lax.ppermute(shard, axis, pairs)  10.1 us
  transfers between devices with their start and end apart: 70, of which 21 were waited for; matrix products, arithmetic and copies ran while one was open for 0% of the time, Pallas kernels for 10%

profile of v9, /device:TPU:0, one launch (start us, length us, event | category | flops | bytes accessed | tf_op | source)
XLA Modules:
  0.0 149.0 jit_solution(12880422593833383879)
XLA Ops:
  0.0 1.8 %select.1 = (f32[1024,256]{1,0:T(8,128)S(1)}, bf16[1024,256]{1,0:T(8,128)(2,1)S(1)}, bf16[512,1024]{1,0:T(8,128)(2,1)S(1)}, s32[4,128]{1,0:T(4,128)S(1)}, bf16[3...) custom-call(f32[1024,256]{1,0:T(8,128)} %bitcast.11, ...), custom_call_target="tpu_custom_call" | custom-call | flops 268435456 | bytes 1148944 | tf_op jit(solution)/shard_map/select/pallas_call | solution.py:28
  1.8 3.0 %collective-permute-start = (bf16[128,256]{1,0:T(8,128)(2,1)S(1)}, bf16[128,256]{1,0:T(8,128)(2,1)S(1)}, u32[]{:S(2)}, u32[]{:S(2)}) collective-permute-start(bf16[128,256]{1,0:T(8,128)(2,1)S(1)} %get-tuple-element.114), channel_id=1, source_target_pairs={{0,4},{4,0},{8,12},{12,8},{16,20},{20,16},{24,28},{28,24},{1,5},{5... | collective-permute-start | bytes 196616 | tf_op jit(solution)/shard_map/ppermute | solution.py:289
  4.8 3.6 %collective-permute-start.1 = (bf16[128,256]{1,0:T(8,128)(2,1)S(1)}, bf16[128,256]{1,0:T(8,128)(2,1)S(1)}, u32[]{:S(2)}, u32[]{:S(2)}) collective-permute-start(bf16[128,256]{1,0:T(8,128)(2,1)S(1)} %get-tuple-element.115), channel_id=1, source_target_pairs={{0,28},{4,8},{8,4},{12,16},{16,12},{20,24},{24,20},{28,0},{1,29},{... | collective-permute-start | bytes 196616 | tf_op jit(solution)/shard_map/ppermute | solution.py:289
  8.4 1.6 %collective-permute-start.3 = (bf16[128,256]{1,0:T(8,128)(2,1)S(1)}, bf16[128,256]{1,0:T(8,128)(2,1)S(1)}, u32[]{:S(2)}, u32[]{:S(2)}) collective-permute-start(bf16[128,256]{1,0:T(8,128)(2,1)S(1)} %get-tuple-element.118), channel_id=1, source_target_pairs={{0,3},{1,2},{2,1},{3,0},{4,7},{5,6},{6,5},{7,4},{8,11},{9,10},{10,... | collective-permute-start | bytes 196616 | tf_op jit(solution)/shard_map/ppermute | solution.py:289
  10.0 2.6 %load.1.matrix = bf16[1536,1536]{1,0:T(8,128)(2,1)S(1)} custom-call(bf16[1536,1536]{1,0:T(8,128)(2,1)} %bitcast.9, bf16[1024,256]{1,0:T(8,128)(2,1)S(1)} %get-tuple-element.112.owned), custom_call_target="tpu_custom_call" | custom-call | bytes 5242880 | tf_op jit(solution)/shard_map/load/pallas_call | solution.py:28
  14.2 1.5 collective-permute-start.5
  18.1 2.7 %collective-permute-start.7 = (bf16[32,256]{1,0:T(8,128)(2,1)S(1)}, bf16[32,256]{1,0:T(8,128)(2,1)S(1)}, u32[]{:S(2)}, u32[]{:S(2)}) collective-permute-start(bf16[32,256]{1,0:T(8,128)(2,1)S(1)} %get-tuple-element.121), channel_id=1, source_target_pairs={{0,28},{4,24},{8,20},{12,16},{16,12},{20,8},{24,4},{28,0},{1,29},{... | collective-permute-start | bytes 49160 | tf_op jit(solution)/shard_map/ppermute | solution.py:180
  21.0 4.8 %collective-permute-start.10 = (bf16[32,256]{1,0:T(8,128)(2,1)S(1)}, bf16[32,256]{1,0:T(8,128)(2,1)S(1)}, u32[]{:S(2)}, u32[]{:S(2)}) collective-permute-start(bf16[32,256]{1,0:T(8,128)(2,1)S(1)} %get-tuple-element.124), channel_id=1, source_target_pairs={{0,16},{4,20},{8,24},{12,28},{16,0},{20,4},{24,8},{28,12},{1,17},{... | collective-permute-start | bytes 49160 | tf_op jit(solution)/shard_map/ppermute | solution.py:180
  26.8 2.5 %collective-permute-start.13 = (bf16[32,256]{1,0:T(8,128)(2,1)S(1)}, bf16[32,256]{1,0:T(8,128)(2,1)S(1)}, u32[]{:S(2)}, u32[]{:S(2)}) collective-permute-start(bf16[32,256]{1,0:T(8,128)(2,1)S(1)} %get-tuple-element.127), channel_id=1, source_target_pairs={{0,4},{4,0},{8,12},{12,8},{16,20},{20,16},{24,28},{28,24},{1,5},{5... | collective-permute-start | bytes 49160 | tf_op jit(solution)/shard_map/ppermute | solution.py:180
  31.3 2.2 %collective-permute-start.14 = (bf16[128,256]{1,0:T(8,128)(2,1)S(1)}, bf16[128,256]{1,0:T(8,128)(2,1)S(1)}, u32[]{:S(2)}, u32[]{:S(2)}) collective-permute-start(bf16[128,256]{1,0:T(8,128)(2,1)S(1)} %get-tuple-element.138), channel_id=1, source_target_pairs={{0,4},{4,0},{8,12},{12,8},{16,20},{20,16},{24,28},{28,24},{1,5},{5... | collective-permute-start | bytes 196616 | tf_op jit(solution)/shard_map/ppermute | solution.py:289
  33.5 2.6 %collective-permute-start.15 = (bf16[128,256]{1,0:T(8,128)(2,1)S(1)}, bf16[128,256]{1,0:T(8,128)(2,1)S(1)}, u32[]{:S(2)}, u32[]{:S(2)}) collective-permute-start(bf16[128,256]{1,0:T(8,128)(2,1)S(1)} %get-tuple-element.139), channel_id=1, source_target_pairs={{0,28},{4,8},{8,4},{12,16},{16,12},{20,24},{24,20},{28,0},{1,29},{... | collective-permute-start | bytes 196616 | tf_op jit(solution)/shard_map/ppermute | solution.py:289
  36.0 1.7 %collective-permute-start.17 = (bf16[128,256]{1,0:T(8,128)(2,1)S(1)}, bf16[128,256]{1,0:T(8,128)(2,1)S(1)}, u32[]{:S(2)}, u32[]{:S(2)}) collective-permute-start(bf16[128,256]{1,0:T(8,128)(2,1)S(1)} %get-tuple-element.142), channel_id=1, source_target_pairs={{0,3},{1,2},{2,1},{3,0},{4,7},{5,6},{6,5},{7,4},{8,11},{9,10},{10,... | collective-permute-start | bytes 196616 | tf_op jit(solution)/shard_map/ppermute | solution.py:289
  37.8 2.6 %spread.1 = (bf16[1024,512]{1,0:T(8,128)(2,1)S(1)}, bf16[1536,1536]{1,0:T(8,128)(2,1)S(1)}) custom-call(bf16[1536,1536]{1,0:T(8,128)(2,1)} %bitcast.10, s32[4,128]{1,0:T(4,128)S(1)} %get-tuple-element.136.masked), custom_call_target="tpu_custom_call" | custom-call | bytes 4720640 | tf_op jit(solution)/shard_map/spread/pallas_call | solution.py:28
  41.9 2.6 %collective-permute-start.19 = (bf16[128,256]{1,0:T(8,128)(2,1)S(1)}, bf16[128,256]{1,0:T(8,128)(2,1)S(1)}, u32[]{:S(2)}, u32[]{:S(2)}) collective-permute-start(bf16[128,256]{1,0:T(8,128)(2,1)S(1)} %get-tuple-element.148), channel_id=1, source_target_pairs={{0,28},{4,8},{8,4},{12,16},{16,12},{20,24},{24,20},{28,0},{1,29},{... | collective-permute-start | bytes 196616 | tf_op jit(solution)/shard_map/ppermute | solution.py:289
  44.5 1.7 %collective-permute-start.21 = (bf16[128,256]{1,0:T(8,128)(2,1)S(1)}, bf16[128,256]{1,0:T(8,128)(2,1)S(1)}, u32[]{:S(2)}, u32[]{:S(2)}) collective-permute-start(bf16[128,256]{1,0:T(8,128)(2,1)S(1)} %get-tuple-element.150), channel_id=1, source_target_pairs={{0,3},{1,2},{2,1},{3,0},{4,7},{5,6},{6,5},{7,4},{8,11},{9,10},{10,... | collective-permute-start | bytes 196616 | tf_op jit(solution)/shard_map/ppermute | solution.py:289
  46.2 2.7 %collective-permute-done.19.g1 = bf16[128,256]{1,0:T(8,128)(2,1)S(1)} collective-permute-done((bf16[128,256]{1,0:T(8,128)(2,1)S(1)}, bf16[128,256]{1,0:T(8,128)(2,1)S(1)}, u32[]{:S(2)}, u32[]{:S(2)}) %collective-permute-start.19) | collective-permute-done | bytes 65568 | tf_op jit(solution)/shard_map/ppermute | solution.py:289
  50.6 2.6 %collective-permute-start.23 = (bf16[128,256]{1,0:T(8,128)(2,1)S(1)}, bf16[128,256]{1,0:T(8,128)(2,1)S(1)}, u32[]{:S(2)}, u32[]{:S(2)}) collective-permute-start(bf16[128,256]{1,0:T(8,128)(2,1)S(1)} %get-tuple-element.152), channel_id=1, source_target_pairs={{0,28},{4,8},{8,4},{12,16},{16,12},{20,24},{24,20},{28,0},{1,29},{... | collective-permute-start | bytes 196616 | tf_op jit(solution)/shard_map/ppermute | solution.py:289
  53.1 1.7 %collective-permute-start.25 = (bf16[128,256]{1,0:T(8,128)(2,1)S(1)}, bf16[128,256]{1,0:T(8,128)(2,1)S(1)}, u32[]{:S(2)}, u32[]{:S(2)}) collective-permute-start(bf16[128,256]{1,0:T(8,128)(2,1)S(1)} %get-tuple-element.154), channel_id=1, source_target_pairs={{0,3},{1,2},{2,1},{3,0},{4,7},{5,6},{6,5},{7,4},{8,11},{9,10},{10,... | collective-permute-start | bytes 196616 | tf_op jit(solution)/shard_map/ppermute | solution.py:289
  54.9 2.7 %collective-permute-done.23.r1 = bf16[128,256]{1,0:T(8,128)(2,1)S(1)} collective-permute-done((bf16[128,256]{1,0:T(8,128)(2,1)S(1)}, bf16[128,256]{1,0:T(8,128)(2,1)S(1)}, u32[]{:S(2)}, u32[]{:S(2)}) %collective-permute-start.23) | collective-permute-done | bytes 65568 | tf_op jit(solution)/shard_map/ppermute | solution.py:289
  59.0 2.6 %collective-permute-start.27 = (bf16[128,256]{1,0:T(8,128)(2,1)S(1)}, bf16[128,256]{1,0:T(8,128)(2,1)S(1)}, u32[]{:S(2)}, u32[]{:S(2)}) collective-permute-start(bf16[128,256]{1,0:T(8,128)(2,1)S(1)} %get-tuple-element.157), channel_id=1, source_target_pairs={{0,28},{4,8},{8,4},{12,16},{16,12},{20,24},{24,20},{28,0},{1,29},{... | collective-permute-start | bytes 196616 | tf_op jit(solution)/shard_map/ppermute | solution.py:289
  61.6 1.7 %collective-permute-start.29 = (bf16[128,256]{1,0:T(8,128)(2,1)S(1)}, bf16[128,256]{1,0:T(8,128)(2,1)S(1)}, u32[]{:S(2)}, u32[]{:S(2)}) collective-permute-start(bf16[128,256]{1,0:T(8,128)(2,1)S(1)} %get-tuple-element.160), channel_id=1, source_target_pairs={{0,3},{1,2},{2,1},{3,0},{4,7},{5,6},{6,5},{7,4},{8,11},{9,10},{10,... | collective-permute-start | bytes 196616 | tf_op jit(solution)/shard_map/ppermute | solution.py:289
  63.3 2.7 %collective-permute-done.27.g1 = bf16[128,256]{1,0:T(8,128)(2,1)S(1)} collective-permute-done((bf16[128,256]{1,0:T(8,128)(2,1)S(1)}, bf16[128,256]{1,0:T(8,128)(2,1)S(1)}, u32[]{:S(2)}, u32[]{:S(2)}) %collective-permute-start.27) | collective-permute-done | bytes 65568 | tf_op jit(solution)/shard_map/ppermute | solution.py:289
  67.4 1.6 %collective-permute-start.31 = (bf16[32,256]{1,0:T(8,128)(2,1)S(1)}, bf16[32,256]{1,0:T(8,128)(2,1)S(1)}, u32[]{:S(2)}, u32[]{:S(2)}) collective-permute-start(bf16[32,256]{1,0:T(8,128)(2,1)S(1)} %restrict.4.refs_0_), channel_id=1, source_target_pairs={{0,2},{1,3},{2,0},{3,1},{4,6},{5,7},{6,4},{7,5},{8,10},{9,11},{10,... | collective-permute-start | bytes 49160 | tf_op jit(solution)/shard_map/ppermute | solution.py:180
  71.4 2.6 %collective-permute-start.33 = (bf16[32,256]{1,0:T(8,128)(2,1)S(1)}, bf16[32,256]{1,0:T(8,128)(2,1)S(1)}, u32[]{:S(2)}, u32[]{:S(2)}) collective-permute-start(bf16[32,256]{1,0:T(8,128)(2,1)S(1)} %get-tuple-element.163), channel_id=1, source_target_pairs={{0,28},{4,24},{8,20},{12,16},{16,12},{20,8},{24,4},{28,0},{1,29},{... | collective-permute-start | bytes 49160 | tf_op jit(solution)/shard_map/ppermute | solution.py:180
  74.9 4.2 %collective-permute-start.36 = (bf16[32,256]{1,0:T(8,128)(2,1)S(1)}, bf16[32,256]{1,0:T(8,128)(2,1)S(1)}, u32[]{:S(2)}, u32[]{:S(2)}) collective-permute-start(bf16[32,256]{1,0:T(8,128)(2,1)S(1)} %get-tuple-element.166), channel_id=1, source_target_pairs={{0,16},{4,20},{8,24},{12,28},{16,0},{20,4},{24,8},{28,12},{1,17},{... | collective-permute-start | bytes 49160 | tf_op jit(solution)/shard_map/ppermute | solution.py:180
  79.3 1.4 collective-permute-start.38
  80.7 1.9 %collective-permute-start.39 = (bf16[32,256]{1,0:T(8,128)(2,1)S(1)}, bf16[32,256]{1,0:T(8,128)(2,1)S(1)}, u32[]{:S(2)}, u32[]{:S(2)}) collective-permute-start(bf16[32,256]{1,0:T(8,128)(2,1)S(1)} %get-tuple-element.169), channel_id=1, source_target_pairs={{0,4},{4,0},{8,12},{12,8},{16,20},{20,16},{24,28},{28,24},{1,5},{5... | collective-permute-start | bytes 49160 | tf_op jit(solution)/shard_map/ppermute | solution.py:180
  84.7 1.9 %collective-permute-start.40 = (bf16[128,256]{1,0:T(8,128)(2,1)S(1)}, bf16[128,256]{1,0:T(8,128)(2,1)S(1)}, u32[]{:S(2)}, u32[]{:S(2)}) collective-permute-start(bf16[128,256]{1,0:T(8,128)(2,1)S(1)} %get-tuple-element.173), channel_id=1, source_target_pairs={{0,4},{4,0},{8,12},{12,8},{16,20},{20,16},{24,28},{28,24},{1,5},{5... | collective-permute-start | bytes 196616 | tf_op jit(solution)/shard_map/ppermute | solution.py:289
  86.7 2.6 %collective-permute-start.41 = (bf16[128,256]{1,0:T(8,128)(2,1)S(1)}, bf16[128,256]{1,0:T(8,128)(2,1)S(1)}, u32[]{:S(2)}, u32[]{:S(2)}) collective-permute-start(bf16[128,256]{1,0:T(8,128)(2,1)S(1)} %get-tuple-element.174), channel_id=1, source_target_pairs={{0,28},{4,8},{8,4},{12,16},{16,12},{20,24},{24,20},{28,0},{1,29},{... | collective-permute-start | bytes 196616 | tf_op jit(solution)/shard_map/ppermute | solution.py:289
  89.2 1.9 %collective-permute-start.43 = (bf16[128,256]{1,0:T(8,128)(2,1)S(1)}, bf16[128,256]{1,0:T(8,128)(2,1)S(1)}, u32[]{:S(2)}, u32[]{:S(2)}) collective-permute-start(bf16[128,256]{1,0:T(8,128)(2,1)S(1)} %get-tuple-element.176), channel_id=1, source_target_pairs={{0,3},{1,2},{2,1},{3,0},{4,7},{5,6},{6,5},{7,4},{8,11},{9,10},{10,... | collective-permute-start | bytes 196616 | tf_op jit(solution)/shard_map/ppermute | solution.py:289
  91.1 2.5 %collective-permute-done.41.refs_6_ = bf16[128,256]{1,0:T(8,128)(2,1)S(1)} collective-permute-done((bf16[128,256]{1,0:T(8,128)(2,1)S(1)}, bf16[128,256]{1,0:T(8,128)(2,1)S(1)}, u32[]{:S(2)}, u32[]{:S(2)}) %collective-permute-start.41) | collective-permute-done | bytes 65568 | tf_op jit(solution)/shard_map/ppermute | solution.py:289
  95.2 2.6 %collective-permute-start.45 = (bf16[128,256]{1,0:T(8,128)(2,1)S(1)}, bf16[128,256]{1,0:T(8,128)(2,1)S(1)}, u32[]{:S(2)}, u32[]{:S(2)}) collective-permute-start(bf16[128,256]{1,0:T(8,128)(2,1)S(1)} %get-tuple-element.180), channel_id=1, source_target_pairs={{0,28},{4,8},{8,4},{12,16},{16,12},{20,24},{24,20},{28,0},{1,29},{... | collective-permute-start | bytes 196616 | tf_op jit(solution)/shard_map/ppermute | solution.py:289
  97.9 1.9 %collective-permute-start.47 = (bf16[128,256]{1,0:T(8,128)(2,1)S(1)}, bf16[128,256]{1,0:T(8,128)(2,1)S(1)}, u32[]{:S(2)}, u32[]{:S(2)}) collective-permute-start(bf16[128,256]{1,0:T(8,128)(2,1)S(1)} %get-tuple-element.182), channel_id=1, source_target_pairs={{0,3},{1,2},{2,1},{3,0},{4,7},{5,6},{6,5},{7,4},{8,11},{9,10},{10,... | collective-permute-start | bytes 196616 | tf_op jit(solution)/shard_map/ppermute | solution.py:289
  99.8 2.5 %collective-permute-done.45.g1 = bf16[128,256]{1,0:T(8,128)(2,1)S(1)} collective-permute-done((bf16[128,256]{1,0:T(8,128)(2,1)S(1)}, bf16[128,256]{1,0:T(8,128)(2,1)S(1)}, u32[]{:S(2)}, u32[]{:S(2)}) %collective-permute-start.45) | collective-permute-done | bytes 65568 | tf_op jit(solution)/shard_map/ppermute | solution.py:289
  103.9 2.6 %collective-permute-start.49 = (bf16[128,256]{1,0:T(8,128)(2,1)S(1)}, bf16[128,256]{1,0:T(8,128)(2,1)S(1)}, u32[]{:S(2)}, u32[]{:S(2)}) collective-permute-start(bf16[128,256]{1,0:T(8,128)(2,1)S(1)} %get-tuple-element.184), channel_id=1, source_target_pairs={{0,28},{4,8},{8,4},{12,16},{16,12},{20,24},{24,20},{28,0},{1,29},{... | collective-permute-start | bytes 196616 | tf_op jit(solution)/shard_map/ppermute | solution.py:289
  106.5 1.9 %collective-permute-start.51 = (bf16[128,256]{1,0:T(8,128)(2,1)S(1)}, bf16[128,256]{1,0:T(8,128)(2,1)S(1)}, u32[]{:S(2)}, u32[]{:S(2)}) collective-permute-start(bf16[128,256]{1,0:T(8,128)(2,1)S(1)} %get-tuple-element.186), channel_id=1, source_target_pairs={{0,3},{1,2},{2,1},{3,0},{4,7},{5,6},{6,5},{7,4},{8,11},{9,10},{10,... | collective-permute-start | bytes 196616 | tf_op jit(solution)/shard_map/ppermute | solution.py:289
  108.4 2.5 %collective-permute-done.49.r1 = bf16[128,256]{1,0:T(8,128)(2,1)S(1)} collective-permute-done((bf16[128,256]{1,0:T(8,128)(2,1)S(1)}, bf16[128,256]{1,0:T(8,128)(2,1)S(1)}, u32[]{:S(2)}, u32[]{:S(2)}) %collective-permute-start.49) | collective-permute-done | bytes 65568 | tf_op jit(solution)/shard_map/ppermute | solution.py:289
  112.4 2.6 %collective-permute-start.53 = (bf16[128,256]{1,0:T(8,128)(2,1)S(1)}, bf16[128,256]{1,0:T(8,128)(2,1)S(1)}, u32[]{:S(2)}, u32[]{:S(2)}) collective-permute-start(bf16[128,256]{1,0:T(8,128)(2,1)S(1)} %get-tuple-element.189), channel_id=1, source_target_pairs={{0,28},{4,8},{8,4},{12,16},{16,12},{20,24},{24,20},{28,0},{1,29},{... | collective-permute-start | bytes 196616 | tf_op jit(solution)/shard_map/ppermute | solution.py:289
  114.9 1.9 %collective-permute-start.55 = (bf16[128,256]{1,0:T(8,128)(2,1)S(1)}, bf16[128,256]{1,0:T(8,128)(2,1)S(1)}, u32[]{:S(2)}, u32[]{:S(2)}) collective-permute-start(bf16[128,256]{1,0:T(8,128)(2,1)S(1)} %get-tuple-element.192), channel_id=1, source_target_pairs={{0,3},{1,2},{2,1},{3,0},{4,7},{5,6},{6,5},{7,4},{8,11},{9,10},{10,... | collective-permute-start | bytes 196616 | tf_op jit(solution)/shard_map/ppermute | solution.py:289
  116.8 2.5 %collective-permute-done.53.g1 = bf16[128,256]{1,0:T(8,128)(2,1)S(1)} collective-permute-done((bf16[128,256]{1,0:T(8,128)(2,1)S(1)}, bf16[128,256]{1,0:T(8,128)(2,1)S(1)}, u32[]{:S(2)}, u32[]{:S(2)}) %collective-permute-start.53) | collective-permute-done | bytes 65568 | tf_op jit(solution)/shard_map/ppermute | solution.py:289
  120.9 1.6 %collective-permute-start.57 = (bf16[32,256]{1,0:T(8,128)(2,1)S(1)}, bf16[32,256]{1,0:T(8,128)(2,1)S(1)}, u32[]{:S(2)}, u32[]{:S(2)}) collective-permute-start(bf16[32,256]{1,0:T(8,128)(2,1)S(1)} %restrict.5.refs_0_), channel_id=1, source_target_pairs={{0,2},{1,3},{2,0},{3,1},{4,6},{5,7},{6,4},{7,5},{8,10},{9,11},{10,... | collective-permute-start | bytes 49160 | tf_op jit(solution)/shard_map/ppermute | solution.py:180
  124.9 2.5 %collective-permute-start.59 = (bf16[32,256]{1,0:T(8,128)(2,1)S(1)}, bf16[32,256]{1,0:T(8,128)(2,1)S(1)}, u32[]{:S(2)}, u32[]{:S(2)}) collective-permute-start(bf16[32,256]{1,0:T(8,128)(2,1)S(1)} %get-tuple-element.195), channel_id=1, source_target_pairs={{0,28},{4,24},{8,20},{12,16},{16,12},{20,8},{24,4},{28,0},{1,29},{... | collective-permute-start | bytes 49160 | tf_op jit(solution)/shard_map/ppermute | solution.py:180
  128.2 4.4 %collective-permute-start.62 = (bf16[32,256]{1,0:T(8,128)(2,1)S(1)}, bf16[32,256]{1,0:T(8,128)(2,1)S(1)}, u32[]{:S(2)}, u32[]{:S(2)}) collective-permute-start(bf16[32,256]{1,0:T(8,128)(2,1)S(1)} %get-tuple-element.198), channel_id=1, source_target_pairs={{0,16},{4,20},{8,24},{12,28},{16,0},{20,4},{24,8},{28,12},{1,17},{... | collective-permute-start | bytes 49160 | tf_op jit(solution)/shard_map/ppermute | solution.py:180
  134.1 2.0 %collective-permute-start.65 = (bf16[32,256]{1,0:T(8,128)(2,1)S(1)}, bf16[32,256]{1,0:T(8,128)(2,1)S(1)}, u32[]{:S(2)}, u32[]{:S(2)}) collective-permute-start(bf16[32,256]{1,0:T(8,128)(2,1)S(1)} %get-tuple-element.201), channel_id=1, source_target_pairs={{0,4},{4,0},{8,12},{12,8},{16,20},{20,16},{24,28},{28,24},{1,5},{5... | collective-permute-start | bytes 49160 | tf_op jit(solution)/shard_map/ppermute | solution.py:180
  138.1 2.1 %collective-permute-start.66 = (bf16[128,256]{1,0:T(8,128)(2,1)S(1)}, bf16[128,256]{1,0:T(8,128)(2,1)S(1)}, u32[]{:S(2)}, u32[]{:S(2)}) collective-permute-start(bf16[128,256]{1,0:T(8,128)(2,1)S(1)} %get-tuple-element.205), channel_id=1, source_target_pairs={{0,4},{4,0},{8,12},{12,8},{16,20},{20,16},{24,28},{28,24},{1,5},{5... | collective-permute-start | bytes 196616 | tf_op jit(solution)/shard_map/ppermute | solution.py:289
  140.1 2.4 %collective-permute-start.67 = (bf16[128,256]{1,0:T(8,128)(2,1)S(1)}, bf16[128,256]{1,0:T(8,128)(2,1)S(1)}, u32[]{:S(2)}, u32[]{:S(2)}) collective-permute-start(bf16[128,256]{1,0:T(8,128)(2,1)S(1)} %get-tuple-element.206), channel_id=1, source_target_pairs={{0,28},{4,8},{8,4},{12,16},{16,12},{20,24},{24,20},{28,0},{1,29},{... | collective-permute-start | bytes 196616 | tf_op jit(solution)/shard_map/ppermute | solution.py:289
  142.6 2.1 %collective-permute-start.69 = (bf16[128,256]{1,0:T(8,128)(2,1)S(1)}, bf16[128,256]{1,0:T(8,128)(2,1)S(1)}, u32[]{:S(2)}, u32[]{:S(2)}) collective-permute-start(bf16[128,256]{1,0:T(8,128)(2,1)S(1)} %get-tuple-element.208), channel_id=1, source_target_pairs={{0,3},{1,2},{2,1},{3,0},{4,7},{5,6},{6,5},{7,4},{8,11},{9,10},{10,... | collective-permute-start | bytes 196616 | tf_op jit(solution)/shard_map/ppermute | solution.py:289
  144.7 2.4 %collective-permute-done.67.refs_6_ = bf16[128,256]{1,0:T(8,128)(2,1)S(1)} collective-permute-done((bf16[128,256]{1,0:T(8,128)(2,1)S(1)}, bf16[128,256]{1,0:T(8,128)(2,1)S(1)}, u32[]{:S(2)}, u32[]{:S(2)}) %collective-permute-start.67) | collective-permute-done | bytes 65568 | tf_op jit(solution)/shard_map/ppermute | solution.py:289
  (126 shorter events, 33.2 us)
Async XLA Ops:
  1.8 10.8 %collective-permute-start = (bf16[128,256]{1,0:T(8,128)(2,1)S(1)}, bf16[128,256]{1,0:T(8,128)(2,1)S(1)}, u32[]{:S(2)}, u32[]{:S(2)}) collective-permute-start(bf16[128,256]{1,0:T(8,128)(2,1)S(1)} %get-tuple-element.114), channel_id=1, source_target_pairs={{0,4},{4,0},{8,12},{12,8},{16,20},{20,16},{24,28},{28,24},{1,5},{5... | collective-permute-start | bytes 196616 | tf_op jit(solution)/shard_map/ppermute | solution.py:289
  4.8 7.7 %collective-permute-start.1 = (bf16[128,256]{1,0:T(8,128)(2,1)S(1)}, bf16[128,256]{1,0:T(8,128)(2,1)S(1)}, u32[]{:S(2)}, u32[]{:S(2)}) collective-permute-start(bf16[128,256]{1,0:T(8,128)(2,1)S(1)} %get-tuple-element.115), channel_id=1, source_target_pairs={{0,28},{4,8},{8,4},{12,16},{16,12},{20,24},{24,20},{28,0},{1,29},{... | collective-permute-start | bytes 196616 | tf_op jit(solution)/shard_map/ppermute | solution.py:289
  8.4 5.5 %collective-permute-start.2 = (bf16[128,256]{1,0:T(8,128)(2,1)S(1)}, bf16[128,256]{1,0:T(8,128)(2,1)S(1)}, u32[]{:S(2)}, u32[]{:S(2)}) collective-permute-start(bf16[128,256]{1,0:T(8,128)(2,1)S(1)} %get-tuple-element.117), channel_id=1, source_target_pairs={{0,1},{1,0},{2,3},{3,2},{4,5},{5,4},{6,7},{7,6},{8,9},{9,8},{10,11... | collective-permute-start | bytes 196616 | tf_op jit(solution)/shard_map/ppermute | solution.py:289
  8.4 5.5 %collective-permute-start.3 = (bf16[128,256]{1,0:T(8,128)(2,1)S(1)}, bf16[128,256]{1,0:T(8,128)(2,1)S(1)}, u32[]{:S(2)}, u32[]{:S(2)}) collective-permute-start(bf16[128,256]{1,0:T(8,128)(2,1)S(1)} %get-tuple-element.118), channel_id=1, source_target_pairs={{0,3},{1,2},{2,1},{3,0},{4,7},{5,6},{6,5},{7,4},{8,11},{9,10},{10,... | collective-permute-start | bytes 196616 | tf_op jit(solution)/shard_map/ppermute | solution.py:289
  18.1 8.0 %collective-permute-start.7 = (bf16[32,256]{1,0:T(8,128)(2,1)S(1)}, bf16[32,256]{1,0:T(8,128)(2,1)S(1)}, u32[]{:S(2)}, u32[]{:S(2)}) collective-permute-start(bf16[32,256]{1,0:T(8,128)(2,1)S(1)} %get-tuple-element.121), channel_id=1, source_target_pairs={{0,28},{4,24},{8,20},{12,16},{16,12},{20,8},{24,4},{28,0},{1,29},{... | collective-permute-start | bytes 49160 | tf_op jit(solution)/shard_map/ppermute | solution.py:180
  20.8 6.0 %collective-permute-start.8 = (bf16[32,256]{1,0:T(8,128)(2,1)S(1)}, bf16[32,256]{1,0:T(8,128)(2,1)S(1)}, u32[]{:S(2)}, u32[]{:S(2)}) collective-permute-start(bf16[32,256]{1,0:T(8,128)(2,1)S(1)} %get-tuple-element.122), channel_id=1, source_target_pairs={{0,24},{4,28},{8,16},{12,20},{16,8},{20,12},{24,0},{28,4},{1,25},{... | collective-permute-start | bytes 49160 | tf_op jit(solution)/shard_map/ppermute | solution.py:180
  20.9 8.8 %collective-permute-start.9 = (bf16[32,256]{1,0:T(8,128)(2,1)S(1)}, bf16[32,256]{1,0:T(8,128)(2,1)S(1)}, u32[]{:S(2)}, u32[]{:S(2)}) collective-permute-start(bf16[32,256]{1,0:T(8,128)(2,1)S(1)} %get-tuple-element.123), channel_id=1, source_target_pairs={{0,20},{4,16},{8,28},{12,24},{16,4},{20,0},{24,12},{28,8},{1,21},{... | collective-permute-start | bytes 49160 | tf_op jit(solution)/shard_map/ppermute | solution.py:180
  21.0 8.7 %collective-permute-start.10 = (bf16[32,256]{1,0:T(8,128)(2,1)S(1)}, bf16[32,256]{1,0:T(8,128)(2,1)S(1)}, u32[]{:S(2)}, u32[]{:S(2)}) collective-permute-start(bf16[32,256]{1,0:T(8,128)(2,1)S(1)} %get-tuple-element.124), channel_id=1, source_target_pairs={{0,16},{4,20},{8,24},{12,28},{16,0},{20,4},{24,8},{28,12},{1,17},{... | collective-permute-start | bytes 49160 | tf_op jit(solution)/shard_map/ppermute | solution.py:180
  25.8 4.6 %collective-permute-start.11 = (bf16[32,256]{1,0:T(8,128)(2,1)S(1)}, bf16[32,256]{1,0:T(8,128)(2,1)S(1)}, u32[]{:S(2)}, u32[]{:S(2)}) collective-permute-start(bf16[32,256]{1,0:T(8,128)(2,1)S(1)} %get-tuple-element.125), channel_id=1, source_target_pairs={{0,12},{4,8},{8,4},{12,0},{16,28},{20,24},{24,20},{28,16},{1,13},{... | collective-permute-start | bytes 49160 | tf_op jit(solution)/shard_map/ppermute | solution.py:180
  31.3 9.0 %collective-permute-start.14 = (bf16[128,256]{1,0:T(8,128)(2,1)S(1)}, bf16[128,256]{1,0:T(8,128)(2,1)S(1)}, u32[]{:S(2)}, u32[]{:S(2)}) collective-permute-start(bf16[128,256]{1,0:T(8,128)(2,1)S(1)} %get-tuple-element.138), channel_id=1, source_target_pairs={{0,4},{4,0},{8,12},{12,8},{16,20},{20,16},{24,28},{28,24},{1,5},{5... | collective-permute-start | bytes 196616 | tf_op jit(solution)/shard_map/ppermute | solution.py:289
  33.5 7.0 %collective-permute-start.15 = (bf16[128,256]{1,0:T(8,128)(2,1)S(1)}, bf16[128,256]{1,0:T(8,128)(2,1)S(1)}, u32[]{:S(2)}, u32[]{:S(2)}) collective-permute-start(bf16[128,256]{1,0:T(8,128)(2,1)S(1)} %get-tuple-element.139), channel_id=1, source_target_pairs={{0,28},{4,8},{8,4},{12,16},{16,12},{20,24},{24,20},{28,0},{1,29},{... | collective-permute-start | bytes 196616 | tf_op jit(solution)/shard_map/ppermute | solution.py:289
  36.0 4.9 %collective-permute-start.16 = (bf16[128,256]{1,0:T(8,128)(2,1)S(1)}, bf16[128,256]{1,0:T(8,128)(2,1)S(1)}, u32[]{:S(2)}, u32[]{:S(2)}) collective-permute-start(bf16[128,256]{1,0:T(8,128)(2,1)S(1)} %get-tuple-element.141), channel_id=1, source_target_pairs={{0,1},{1,0},{2,3},{3,2},{4,5},{5,4},{6,7},{7,6},{8,9},{9,8},{10,11... | collective-permute-start | bytes 196616 | tf_op jit(solution)/shard_map/ppermute | solution.py:289
  36.0 4.9 %collective-permute-start.17 = (bf16[128,256]{1,0:T(8,128)(2,1)S(1)}, bf16[128,256]{1,0:T(8,128)(2,1)S(1)}, u32[]{:S(2)}, u32[]{:S(2)}) collective-permute-start(bf16[128,256]{1,0:T(8,128)(2,1)S(1)} %get-tuple-element.142), channel_id=1, source_target_pairs={{0,3},{1,2},{2,1},{3,0},{4,7},{5,6},{6,5},{7,4},{8,11},{9,10},{10,... | collective-permute-start | bytes 196616 | tf_op jit(solution)/shard_map/ppermute | solution.py:289
  41.9 7.0 %collective-permute-start.19 = (bf16[128,256]{1,0:T(8,128)(2,1)S(1)}, bf16[128,256]{1,0:T(8,128)(2,1)S(1)}, u32[]{:S(2)}, u32[]{:S(2)}) collective-permute-start(bf16[128,256]{1,0:T(8,128)(2,1)S(1)} %get-tuple-element.148), channel_id=1, source_target_pairs={{0,28},{4,8},{8,4},{12,16},{16,12},{20,24},{24,20},{28,0},{1,29},{... | collective-permute-start | bytes 196616 | tf_op jit(solution)/shard_map/ppermute | solution.py:289
  44.5 5.6 %collective-permute-start.20 = (bf16[128,256]{1,0:T(8,128)(2,1)S(1)}, bf16[128,256]{1,0:T(8,128)(2,1)S(1)}, u32[]{:S(2)}, u32[]{:S(2)}) collective-permute-start(bf16[128,256]{1,0:T(8,128)(2,1)S(1)} %get-tuple-element.149), channel_id=1, source_target_pairs={{0,1},{1,0},{2,3},{3,2},{4,5},{5,4},{6,7},{7,6},{8,9},{9,8},{10,11... | collective-permute-start | bytes 196616 | tf_op jit(solution)/shard_map/ppermute | solution.py:289
  44.5 5.6 %collective-permute-start.21 = (bf16[128,256]{1,0:T(8,128)(2,1)S(1)}, bf16[128,256]{1,0:T(8,128)(2,1)S(1)}, u32[]{:S(2)}, u32[]{:S(2)}) collective-permute-start(bf16[128,256]{1,0:T(8,128)(2,1)S(1)} %get-tuple-element.150), channel_id=1, source_target_pairs={{0,3},{1,2},{2,1},{3,0},{4,7},{5,6},{6,5},{7,4},{8,11},{9,10},{10,... | collective-permute-start | bytes 196616 | tf_op jit(solution)/shard_map/ppermute | solution.py:289
  50.6 7.0 %collective-permute-start.23 = (bf16[128,256]{1,0:T(8,128)(2,1)S(1)}, bf16[128,256]{1,0:T(8,128)(2,1)S(1)}, u32[]{:S(2)}, u32[]{:S(2)}) collective-permute-start(bf16[128,256]{1,0:T(8,128)(2,1)S(1)} %get-tuple-element.152), channel_id=1, source_target_pairs={{0,28},{4,8},{8,4},{12,16},{16,12},{20,24},{24,20},{28,0},{1,29},{... | collective-permute-start | bytes 196616 | tf_op jit(solution)/shard_map/ppermute | solution.py:289
  53.1 4.8 %collective-permute-start.24 = (bf16[128,256]{1,0:T(8,128)(2,1)S(1)}, bf16[128,256]{1,0:T(8,128)(2,1)S(1)}, u32[]{:S(2)}, u32[]{:S(2)}) collective-permute-start(bf16[128,256]{1,0:T(8,128)(2,1)S(1)} %get-tuple-element.153), channel_id=1, source_target_pairs={{0,1},{1,0},{2,3},{3,2},{4,5},{5,4},{6,7},{7,6},{8,9},{9,8},{10,11... | collective-permute-start | bytes 196616 | tf_op jit(solution)/shard_map/ppermute | solution.py:289
  53.1 4.8 %collective-permute-start.25 = (bf16[128,256]{1,0:T(8,128)(2,1)S(1)}, bf16[128,256]{1,0:T(8,128)(2,1)S(1)}, u32[]{:S(2)}, u32[]{:S(2)}) collective-permute-start(bf16[128,256]{1,0:T(8,128)(2,1)S(1)} %get-tuple-element.154), channel_id=1, source_target_pairs={{0,3},{1,2},{2,1},{3,0},{4,7},{5,6},{6,5},{7,4},{8,11},{9,10},{10,... | collective-permute-start | bytes 196616 | tf_op jit(solution)/shard_map/ppermute | solution.py:289
  59.0 7.0 %collective-permute-start.27 = (bf16[128,256]{1,0:T(8,128)(2,1)S(1)}, bf16[128,256]{1,0:T(8,128)(2,1)S(1)}, u32[]{:S(2)}, u32[]{:S(2)}) collective-permute-start(bf16[128,256]{1,0:T(8,128)(2,1)S(1)} %get-tuple-element.157), channel_id=1, source_target_pairs={{0,28},{4,8},{8,4},{12,16},{16,12},{20,24},{24,20},{28,0},{1,29},{... | collective-permute-start | bytes 196616 | tf_op jit(solution)/shard_map/ppermute | solution.py:289
  61.5 5.7 %collective-permute-start.28 = (bf16[128,256]{1,0:T(8,128)(2,1)S(1)}, bf16[128,256]{1,0:T(8,128)(2,1)S(1)}, u32[]{:S(2)}, u32[]{:S(2)}) collective-permute-start(bf16[128,256]{1,0:T(8,128)(2,1)S(1)} %get-tuple-element.159), channel_id=1, source_target_pairs={{0,1},{1,0},{2,3},{3,2},{4,5},{5,4},{6,7},{7,6},{8,9},{9,8},{10,11... | collective-permute-start | bytes 196616 | tf_op jit(solution)/shard_map/ppermute | solution.py:289
  61.6 5.7 %collective-permute-start.29 = (bf16[128,256]{1,0:T(8,128)(2,1)S(1)}, bf16[128,256]{1,0:T(8,128)(2,1)S(1)}, u32[]{:S(2)}, u32[]{:S(2)}) collective-permute-start(bf16[128,256]{1,0:T(8,128)(2,1)S(1)} %get-tuple-element.160), channel_id=1, source_target_pairs={{0,3},{1,2},{2,1},{3,0},{4,7},{5,6},{6,5},{7,4},{8,11},{9,10},{10,... | collective-permute-start | bytes 196616 | tf_op jit(solution)/shard_map/ppermute | solution.py:289
  71.4 7.9 %collective-permute-start.33 = (bf16[32,256]{1,0:T(8,128)(2,1)S(1)}, bf16[32,256]{1,0:T(8,128)(2,1)S(1)}, u32[]{:S(2)}, u32[]{:S(2)}) collective-permute-start(bf16[32,256]{1,0:T(8,128)(2,1)S(1)} %get-tuple-element.163), channel_id=1, source_target_pairs={{0,28},{4,24},{8,20},{12,16},{16,12},{20,8},{24,4},{28,0},{1,29},{... | collective-permute-start | bytes 49160 | tf_op jit(solution)/shard_map/ppermute | solution.py:180
  74.0 6.7 %collective-permute-start.34 = (bf16[32,256]{1,0:T(8,128)(2,1)S(1)}, bf16[32,256]{1,0:T(8,128)(2,1)S(1)}, u32[]{:S(2)}, u32[]{:S(2)}) collective-permute-start(bf16[32,256]{1,0:T(8,128)(2,1)S(1)} %get-tuple-element.164), channel_id=1, source_target_pairs={{0,24},{4,28},{8,16},{12,20},{16,8},{20,12},{24,0},{28,4},{1,25},{... | collective-permute-start | bytes 49160 | tf_op jit(solution)/shard_map/ppermute | solution.py:180
  74.9 8.1 %collective-permute-start.35 = (bf16[32,256]{1,0:T(8,128)(2,1)S(1)}, bf16[32,256]{1,0:T(8,128)(2,1)S(1)}, u32[]{:S(2)}, u32[]{:S(2)}) collective-permute-start(bf16[32,256]{1,0:T(8,128)(2,1)S(1)} %get-tuple-element.165), channel_id=1, source_target_pairs={{0,20},{4,16},{8,28},{12,24},{16,4},{20,0},{24,12},{28,8},{1,21},{... | collective-permute-start | bytes 49160 | tf_op jit(solution)/shard_map/ppermute | solution.py:180
  74.9 8.1 %collective-permute-start.36 = (bf16[32,256]{1,0:T(8,128)(2,1)S(1)}, bf16[32,256]{1,0:T(8,128)(2,1)S(1)}, u32[]{:S(2)}, u32[]{:S(2)}) collective-permute-start(bf16[32,256]{1,0:T(8,128)(2,1)S(1)} %get-tuple-element.166), channel_id=1, source_target_pairs={{0,16},{4,20},{8,24},{12,28},{16,0},{20,4},{24,8},{28,12},{1,17},{... | collective-permute-start | bytes 49160 | tf_op jit(solution)/shard_map/ppermute | solution.py:180
  84.7 6.4 %collective-permute-start.40 = (bf16[128,256]{1,0:T(8,128)(2,1)S(1)}, bf16[128,256]{1,0:T(8,128)(2,1)S(1)}, u32[]{:S(2)}, u32[]{:S(2)}) collective-permute-start(bf16[128,256]{1,0:T(8,128)(2,1)S(1)} %get-tuple-element.173), channel_id=1, source_target_pairs={{0,4},{4,0},{8,12},{12,8},{16,20},{20,16},{24,28},{28,24},{1,5},{5... | collective-permute-start | bytes 196616 | tf_op jit(solution)/shard_map/ppermute | solution.py:289
  86.7 7.0 %collective-permute-start.41 = (bf16[128,256]{1,0:T(8,128)(2,1)S(1)}, bf16[128,256]{1,0:T(8,128)(2,1)S(1)}, u32[]{:S(2)}, u32[]{:S(2)}) collective-permute-start(bf16[128,256]{1,0:T(8,128)(2,1)S(1)} %get-tuple-element.174), channel_id=1, source_target_pairs={{0,28},{4,8},{8,4},{12,16},{16,12},{20,24},{24,20},{28,0},{1,29},{... | collective-permute-start | bytes 196616 | tf_op jit(solution)/shard_map/ppermute | solution.py:289
  89.2 4.9 %collective-permute-start.42 = (bf16[128,256]{1,0:T(8,128)(2,1)S(1)}, bf16[128,256]{1,0:T(8,128)(2,1)S(1)}, u32[]{:S(2)}, u32[]{:S(2)}) collective-permute-start(bf16[128,256]{1,0:T(8,128)(2,1)S(1)} %get-tuple-element.175), channel_id=1, source_target_pairs={{0,1},{1,0},{2,3},{3,2},{4,5},{5,4},{6,7},{7,6},{8,9},{9,8},{10,11... | collective-permute-start | bytes 196616 | tf_op jit(solution)/shard_map/ppermute | solution.py:289
  89.2 4.9 %collective-permute-start.43 = (bf16[128,256]{1,0:T(8,128)(2,1)S(1)}, bf16[128,256]{1,0:T(8,128)(2,1)S(1)}, u32[]{:S(2)}, u32[]{:S(2)}) collective-permute-start(bf16[128,256]{1,0:T(8,128)(2,1)S(1)} %get-tuple-element.176), channel_id=1, source_target_pairs={{0,3},{1,2},{2,1},{3,0},{4,7},{5,6},{6,5},{7,4},{8,11},{9,10},{10,... | collective-permute-start | bytes 196616 | tf_op jit(solution)/shard_map/ppermute | solution.py:289
  95.2 7.0 %collective-permute-start.45 = (bf16[128,256]{1,0:T(8,128)(2,1)S(1)}, bf16[128,256]{1,0:T(8,128)(2,1)S(1)}, u32[]{:S(2)}, u32[]{:S(2)}) collective-permute-start(bf16[128,256]{1,0:T(8,128)(2,1)S(1)} %get-tuple-element.180), channel_id=1, source_target_pairs={{0,28},{4,8},{8,4},{12,16},{16,12},{20,24},{24,20},{28,0},{1,29},{... | collective-permute-start | bytes 196616 | tf_op jit(solution)/shard_map/ppermute | solution.py:289
  97.9 5.6 %collective-permute-start.46 = (bf16[128,256]{1,0:T(8,128)(2,1)S(1)}, bf16[128,256]{1,0:T(8,128)(2,1)S(1)}, u32[]{:S(2)}, u32[]{:S(2)}) collective-permute-start(bf16[128,256]{1,0:T(8,128)(2,1)S(1)} %get-tuple-element.181), channel_id=1, source_target_pairs={{0,1},{1,0},{2,3},{3,2},{4,5},{5,4},{6,7},{7,6},{8,9},{9,8},{10,11... | collective-permute-start | bytes 196616 | tf_op jit(solution)/shard_map/ppermute | solution.py:289
  97.9 5.6 %collective-permute-start.47 = (bf16[128,256]{1,0:T(8,128)(2,1)S(1)}, bf16[128,256]{1,0:T(8,128)(2,1)S(1)}, u32[]{:S(2)}, u32[]{:S(2)}) collective-permute-start(bf16[128,256]{1,0:T(8,128)(2,1)S(1)} %get-tuple-element.182), channel_id=1, source_target_pairs={{0,3},{1,2},{2,1},{3,0},{4,7},{5,6},{6,5},{7,4},{8,11},{9,10},{10,... | collective-permute-start | bytes 196616 | tf_op jit(solution)/shard_map/ppermute | solution.py:289
  103.7 4.7 %collective-permute-start.48 = (bf16[128,256]{1,0:T(8,128)(2,1)S(1)}, bf16[128,256]{1,0:T(8,128)(2,1)S(1)}, u32[]{:S(2)}, u32[]{:S(2)}) collective-permute-start(bf16[128,256]{1,0:T(8,128)(2,1)S(1)} %get-tuple-element.183), channel_id=1, source_target_pairs={{0,4},{4,0},{8,12},{12,8},{16,20},{20,16},{24,28},{28,24},{1,5},{5... | collective-permute-start | bytes 196616 | tf_op jit(solution)/shard_map/ppermute | solution.py:289
  103.9 7.0 %collective-permute-start.49 = (bf16[128,256]{1,0:T(8,128)(2,1)S(1)}, bf16[128,256]{1,0:T(8,128)(2,1)S(1)}, u32[]{:S(2)}, u32[]{:S(2)}) collective-permute-start(bf16[128,256]{1,0:T(8,128)(2,1)S(1)} %get-tuple-element.184), channel_id=1, source_target_pairs={{0,28},{4,8},{8,4},{12,16},{16,12},{20,24},{24,20},{28,0},{1,29},{... | collective-permute-start | bytes 196616 | tf_op jit(solution)/shard_map/ppermute | solution.py:289
  106.5 4.9 %collective-permute-start.50 = (bf16[128,256]{1,0:T(8,128)(2,1)S(1)}, bf16[128,256]{1,0:T(8,128)(2,1)S(1)}, u32[]{:S(2)}, u32[]{:S(2)}) collective-permute-start(bf16[128,256]{1,0:T(8,128)(2,1)S(1)} %get-tuple-element.185), channel_id=1, source_target_pairs={{0,1},{1,0},{2,3},{3,2},{4,5},{5,4},{6,7},{7,6},{8,9},{9,8},{10,11... | collective-permute-start | bytes 196616 | tf_op jit(solution)/shard_map/ppermute | solution.py:289
  106.5 4.9 %collective-permute-start.51 = (bf16[128,256]{1,0:T(8,128)(2,1)S(1)}, bf16[128,256]{1,0:T(8,128)(2,1)S(1)}, u32[]{:S(2)}, u32[]{:S(2)}) collective-permute-start(bf16[128,256]{1,0:T(8,128)(2,1)S(1)} %get-tuple-element.186), channel_id=1, source_target_pairs={{0,3},{1,2},{2,1},{3,0},{4,7},{5,6},{6,5},{7,4},{8,11},{9,10},{10,... | collective-permute-start | bytes 196616 | tf_op jit(solution)/shard_map/ppermute | solution.py:289
  112.4 7.0 %collective-permute-start.53 = (bf16[128,256]{1,0:T(8,128)(2,1)S(1)}, bf16[128,256]{1,0:T(8,128)(2,1)S(1)}, u32[]{:S(2)}, u32[]{:S(2)}) collective-permute-start(bf16[128,256]{1,0:T(8,128)(2,1)S(1)} %get-tuple-element.189), channel_id=1, source_target_pairs={{0,28},{4,8},{8,4},{12,16},{16,12},{20,24},{24,20},{28,0},{1,29},{... | collective-permute-start | bytes 196616 | tf_op jit(solution)/shard_map/ppermute | solution.py:289
  114.9 5.7 %collective-permute-start.54 = (bf16[128,256]{1,0:T(8,128)(2,1)S(1)}, bf16[128,256]{1,0:T(8,128)(2,1)S(1)}, u32[]{:S(2)}, u32[]{:S(2)}) collective-permute-start(bf16[128,256]{1,0:T(8,128)(2,1)S(1)} %get-tuple-element.191), channel_id=1, source_target_pairs={{0,1},{1,0},{2,3},{3,2},{4,5},{5,4},{6,7},{7,6},{8,9},{9,8},{10,11... | collective-permute-start | bytes 196616 | tf_op jit(solution)/shard_map/ppermute | solution.py:289
  114.9 5.7 %collective-permute-start.55 = (bf16[128,256]{1,0:T(8,128)(2,1)S(1)}, bf16[128,256]{1,0:T(8,128)(2,1)S(1)}, u32[]{:S(2)}, u32[]{:S(2)}) collective-permute-start(bf16[128,256]{1,0:T(8,128)(2,1)S(1)} %get-tuple-element.192), channel_id=1, source_target_pairs={{0,3},{1,2},{2,1},{3,0},{4,7},{5,6},{6,5},{7,4},{8,11},{9,10},{10,... | collective-permute-start | bytes 196616 | tf_op jit(solution)/shard_map/ppermute | solution.py:289
  124.9 7.8 %collective-permute-start.59 = (bf16[32,256]{1,0:T(8,128)(2,1)S(1)}, bf16[32,256]{1,0:T(8,128)(2,1)S(1)}, u32[]{:S(2)}, u32[]{:S(2)}) collective-permute-start(bf16[32,256]{1,0:T(8,128)(2,1)S(1)} %get-tuple-element.195), channel_id=1, source_target_pairs={{0,28},{4,24},{8,20},{12,16},{16,12},{20,8},{24,4},{28,0},{1,29},{... | collective-permute-start | bytes 49160 | tf_op jit(solution)/shard_map/ppermute | solution.py:180
  127.4 6.7 %collective-permute-start.60 = (bf16[32,256]{1,0:T(8,128)(2,1)S(1)}, bf16[32,256]{1,0:T(8,128)(2,1)S(1)}, u32[]{:S(2)}, u32[]{:S(2)}) collective-permute-start(bf16[32,256]{1,0:T(8,128)(2,1)S(1)} %get-tuple-element.196), channel_id=1, source_target_pairs={{0,24},{4,28},{8,16},{12,20},{16,8},{20,12},{24,0},{28,4},{1,25},{... | collective-permute-start | bytes 49160 | tf_op jit(solution)/shard_map/ppermute | solution.py:180
  128.2 8.2 %collective-permute-start.61 = (bf16[32,256]{1,0:T(8,128)(2,1)S(1)}, bf16[32,256]{1,0:T(8,128)(2,1)S(1)}, u32[]{:S(2)}, u32[]{:S(2)}) collective-permute-start(bf16[32,256]{1,0:T(8,128)(2,1)S(1)} %get-tuple-element.197), channel_id=1, source_target_pairs={{0,20},{4,16},{8,28},{12,24},{16,4},{20,0},{24,12},{28,8},{1,21},{... | collective-permute-start | bytes 49160 | tf_op jit(solution)/shard_map/ppermute | solution.py:180
  128.2 8.3 %collective-permute-start.62 = (bf16[32,256]{1,0:T(8,128)(2,1)S(1)}, bf16[32,256]{1,0:T(8,128)(2,1)S(1)}, u32[]{:S(2)}, u32[]{:S(2)}) collective-permute-start(bf16[32,256]{1,0:T(8,128)(2,1)S(1)} %get-tuple-element.198), channel_id=1, source_target_pairs={{0,16},{4,20},{8,24},{12,28},{16,0},{20,4},{24,8},{28,12},{1,17},{... | collective-permute-start | bytes 49160 | tf_op jit(solution)/shard_map/ppermute | solution.py:180
  138.1 6.6 %collective-permute-start.66 = (bf16[128,256]{1,0:T(8,128)(2,1)S(1)}, bf16[128,256]{1,0:T(8,128)(2,1)S(1)}, u32[]{:S(2)}, u32[]{:S(2)}) collective-permute-start(bf16[128,256]{1,0:T(8,128)(2,1)S(1)} %get-tuple-element.205), channel_id=1, source_target_pairs={{0,4},{4,0},{8,12},{12,8},{16,20},{20,16},{24,28},{28,24},{1,5},{5... | collective-permute-start | bytes 196616 | tf_op jit(solution)/shard_map/ppermute | solution.py:289
  140.1 7.0 %collective-permute-start.67 = (bf16[128,256]{1,0:T(8,128)(2,1)S(1)}, bf16[128,256]{1,0:T(8,128)(2,1)S(1)}, u32[]{:S(2)}, u32[]{:S(2)}) collective-permute-start(bf16[128,256]{1,0:T(8,128)(2,1)S(1)} %get-tuple-element.206), channel_id=1, source_target_pairs={{0,28},{4,8},{8,4},{12,16},{16,12},{20,24},{24,20},{28,0},{1,29},{... | collective-permute-start | bytes 196616 | tf_op jit(solution)/shard_map/ppermute | solution.py:289
  142.6 5.0 %collective-permute-start.68 = (bf16[128,256]{1,0:T(8,128)(2,1)S(1)}, bf16[128,256]{1,0:T(8,128)(2,1)S(1)}, u32[]{:S(2)}, u32[]{:S(2)}) collective-permute-start(bf16[128,256]{1,0:T(8,128)(2,1)S(1)} %get-tuple-element.207), channel_id=1, source_target_pairs={{0,1},{1,0},{2,3},{3,2},{4,5},{5,4},{6,7},{7,6},{8,9},{9,8},{10,11... | collective-permute-start | bytes 196616 | tf_op jit(solution)/shard_map/ppermute | solution.py:289
  142.6 5.0 %collective-permute-start.69 = (bf16[128,256]{1,0:T(8,128)(2,1)S(1)}, bf16[128,256]{1,0:T(8,128)(2,1)S(1)}, u32[]{:S(2)}, u32[]{:S(2)}) collective-permute-start(bf16[128,256]{1,0:T(8,128)(2,1)S(1)} %get-tuple-element.208), channel_id=1, source_target_pairs={{0,3},{1,2},{2,1},{3,0},{4,7},{5,6},{6,5},{7,4},{8,11},{9,10},{10,... | collective-permute-start | bytes 196616 | tf_op jit(solution)/shard_map/ppermute | solution.py:289
  (23 other events, 89.7 us)

commit v10 on v9

--- a/solution.py
+++ b/solution.py
@@ -134,38 +134,31 @@
     return jnp.concatenate([part[...] for part in parts], axis=0)
 
 
-def load_kernel(far, owned, matrix, sems):
+def load_kernel(far, owned, matrix, out, sems):
     own = owned.shape[0]
     tile = (matrix.shape[0] - own) // 4
     for load in started(matrix_pieces(far, matrix, own, tile), sems):
         load.wait()
-
-
-def near_columns_kernel(matrix, owned, g0, g1, out):
+    out[...] = product(matrix[:, :own], owned[...])
+
+
+def own_columns_kernel(matrix, owned, out):
     own = owned.shape[0]
-    split = own + 2 * g0.shape[0]
-    out[...] = product(matrix[:, :own], owned[...]) + product(matrix[:, own:split], stacked(g0, g1))
-
-
-def near_solve_kernel(matrix, basis, owned, g0, g1, out, restricted):
+    out[...] = product(matrix[:, :own], owned[...])
+
+
+def restrict_kernel(basis, owned, g0, g1, g2, g3, out):
     own = owned.shape[0]
-    split = own + 2 * g0.shape[0]
-    ghosts = stacked(g0, g1)
-    out[...] = product(matrix[:, :own], owned[...]) + product(matrix[:, own:split], ghosts)
-    restricted[...] = product(basis[:, :own], owned[...]) + product(basis[:, own:split], ghosts)
-
-
-def restrict_kernel(basis, near, g2, g3, out):
-    split = basis.shape[1] - 2 * g2.shape[0]
-    out[...] = (near[...] + product(basis[:, split:], stacked(g2, g3))).astype(HALF)
-
-
-def solve_kernel(matrix, partial, g2, g3, rim, inner):
+    out[...] = (
+        product(basis[:, :own], owned[...]) + product(basis[:, own:], stacked(g0, g1, g2, g3))
+    ).astype(HALF)
+
+
+def solve_kernel(matrix, partial, g0, g1, g2, g3, rim, inner):
     own = inner.shape[0]
-    ghosts = stacked(g2, g3)
-    split = matrix.shape[1] - ghosts.shape[0]
-    rim[...] = partial[own:, :] + product(matrix[own:, split:], ghosts)
-    inner[...] = partial[:own, :] + product(matrix[:own, split:], ghosts)
+    ghosts = stacked(g0, g1, g2, g3)
+    rim[...] = partial[own:, :] + product(matrix[own:, own:], ghosts)
+    inner[...] = partial[:own, :] + product(matrix[:own, own:], ghosts)
 
 
 def met(place, turn, devices):
@@ -174,9 +167,11 @@
     return (turn + devices - place) % devices
 
 
-def meeting(shard, axis, turn):
+def meeting(shard, axis, turn, block=1):
     devices = lax.axis_size(axis)
-    pairs = [(i, met(i, turn, devices)) for i in range(devices)]
+    pairs = [
+        (i, met(i // block, turn, devices // block) * block + i % block) for i in range(devices)
+    ]
     return shard if all(i == j for i, j in pairs) else lax.ppermute(shard, axis, pairs)
 
 
@@ -187,92 +182,89 @@
         for turn, piece in enumerate(restricted):
             at = pl.multiple_of(met(lax.axis_index("col"), turn, across) * coarse, coarse)
             gathered[pl.ds(at, coarse), :] = piece[...]
+        pair = lax.axis_index("row") // 2
         for turn, part in enumerate(parts):
-            other = met(lax.axis_index("row"), turn, groups)
-            part[...] = product(inverse[other], gathered[...]).astype(HALF)
+            other = 2 * met(pair, turn, groups // 2)
+            for i in range(2):
+                part[i * coarse : (i + 1) * coarse, :] = product(
+                    inverse[other + i], gathered[...]
+                ).astype(HALF)
 
     return body
 
 
-def coarse_kernel(groups):
-    def body(*refs):
-        parts, (basis, rim, level, *tiles) = refs[:groups], refs[groups:]
-        tile = tiles[0].shape[0]
-        own = basis.shape[1] - 4 * tile
-        total = parts[0][...].astype(FULL)
-        for part in parts[1:]:
-            total += part[...].astype(FULL)
-        level[...] = total.astype(HALF)
-        for d in range(4):
-            here = slice(d * tile, (d + 1) * tile)
-            there = slice(own + d * tile, own + (d + 1) * tile)
-            tiles[d][...] = (
-                rim[here, :] + turned_product(basis[:, there], level[...])
-            ).astype(HALF)
-
-    return body
+def pair_kernel(*refs):
+    *parts, mine, others = refs
+    coarse = mine.shape[0]
+    total = parts[0][...].astype(FULL)
+    for part in parts[1:]:
+        total += part[...].astype(FULL)
+    odd = lax.rem(lax.axis_index("row"), 2) == 1
+    low, high = total[:coarse, :], total[coarse:, :]
+    mine[...] = jnp.where(odd, high, low)
+    others[...] = jnp.where(odd, low, high).astype(HALF)
+
+
+def coarse_kernel(mine, theirs, basis, rim, level, *tiles):
+    tile = tiles[0].shape[0]
+    own = basis.shape[1] - 4 * tile
+    level[...] = (mine[...] + theirs[...].astype(FULL)).astype(HALF)
+    for d in range(4):
+        here = slice(d * tile, (d + 1) * tile)
+        there = slice(own + d * tile, own + (d + 1) * tile)
+        tiles[d][...] = (rim[here, :] + turned_product(basis[:, there], level[...])).astype(HALF)
 
 
 def base_kernel(first):
     def body(*refs):
         refs = list(refs)
         before = None if first else refs.pop(0)
-        inner, level, basis, spread, r0, r1, out = refs
-        own, tile = out.shape[0], r0.shape[0]
-        update = (
-            inner[...]
-            + turned_product(basis[:, :own], level[...])
-            + product(spread[:, : 2 * tile], stacked(r0, r1))
-        )
+        inner, level, basis, out = refs
+        own = out.shape[0]
+        update = inner[...] + turned_product(basis[:, :own], level[...])
         out[...] = DAMPING * update if first else before[...] + DAMPING * update
 
     return body
 
 
-def update_kernel(base, pick, spread, r2, r3, after, half, *tiles):
-    tile = r2.shape[0]
-    after[...] = base[...] + DAMPING * product(spread[:, 2 * tile :], stacked(r2, r3))
+def update_kernel(base, pick, spread, r0, r1, r2, r3, after, half, *tiles):
+    after[...] = base[...] + DAMPING * product(spread[...], stacked(r0, r1, r2, r3))
     half[...] = after[...].astype(HALF)
     picked(pick, half, tiles)
 
 
-def last_update_kernel(base, spread, r2, r3, far, after, sems):
-    tile = r2.shape[0]
+def last_update_kernel(base, spread, r0, r1, r2, r3, far, after, sems):
     pieces = sems.shape[0]
     height = after.shape[0] // pieces
-    returned = stacked(r2, r3)
+    returned = stacked(r0, r1, r2, r3)
     stores = []
     for i in range(pieces):
         at = slice(i * height, (i + 1) * height)
-        after[at, :] = base[at, :] + DAMPING * product(spread[at, 2 * tile :], returned)
+        after[at, :] = base[at, :] + DAMPING * product(spread[at, :], returned)
         stores.append(pltpu.make_async_copy(after.at[at], far.at[at], sems.at[i]))
         stores[-1].start()
     for store in stores:
         store.wait()
 
 
-def rim_kernel(matrix, partial, g2, g3, *tiles):
-    tile = g2.shape[0]
+def rim_kernel(matrix, partial, g0, g1, g2, g3, *tiles):
+    tile = g0.shape[0]
     own = matrix.shape[1] - 4 * tile
-    ghosts = stacked(g2, g3)
+    ghosts = stacked(g0, g1, g2, g3)
     for d in range(4):
         at = slice(own + d * tile, own + (d + 1) * tile)
-        tiles[d][...] = (partial[at, :] + product(matrix[at, own + 2 * tile :], ghosts)).astype(HALF)
-
-
-def remainder_kernel(target, matrix, partial, g2, g3, spread, r0, r1, out):
-    own, tile = target.shape[0], g2.shape[0]
-    image = (
-        partial[:own, :]
-        + product(matrix[:own, own + 2 * tile :], stacked(g2, g3))
-        + product(spread[:, : 2 * tile], stacked(r0, r1))
+        tiles[d][...] = (partial[at, :] + product(matrix[at, own:], ghosts)).astype(HALF)
+
+
+def remainder_kernel(target, matrix, partial, g0, g1, g2, g3, out):
+    own = target.shape[0]
+    out[...] = target[...] - (
+        partial[:own, :] + product(matrix[:own, own:], stacked(g0, g1, g2, g3))
     )
-    out[...] = target[...] - image
-
-
-def residual_kernel(remainder, pick, spread, r2, r3, half, *tiles):
-    tile = r2.shape[0]
-    half[...] = (remainder[...] - product(spread[:, 2 * tile :], stacked(r2, r3))).astype(HALF)
+
+
+def residual_kernel(remainder, pick, spread, r0, r1, r2, r3, half, *tiles):
+    half[...] = (remainder[...] - product(spread[...], stacked(r0, r1, r2, r3))).astype(HALF)
     picked(pick, half, tiles)
 
 
@@ -340,16 +332,14 @@
     for sweep in range(ITERS):
         first, last = sweep == 0, sweep == ITERS - 1
         if sweep:
-            g0, g1, g2, g3 = traded(tiles)
+            ghosts = traded(tiles)
             (partial,) = call(
-                near_columns_kernel,
-                "operator_near",
+                own_columns_kernel,
+                "operator_own",
                 [local_full],
                 operator,
                 solution_half,
-                g0,
-                g1,
-                flops=2 * local * (own + 2 * tile) * columns,
+                flops=2 * local * own * columns,
             )
             tiles = call(
                 rim_kernel,
@@ -357,11 +347,10 @@
                 four_tiles,
                 operator,
                 partial,
-                g2,
-                g3,
-                flops=4 * margin * tile * columns,
-            )
-            r0, r1, r2, r3 = traded(tiles)
+                *ghosts,
+                flops=2 * margin * margin * columns,
+            )
+            returned = traded(tiles)
             (remainder,) = call(
                 remainder_kernel,
                 "remainder",
@@ -369,12 +358,8 @@
                 target,
                 operator,
                 partial,
-                g2,
-                g3,
-                spread,
-                r0,
-                r1,
-                flops=8 * own * tile * columns,
+                *ghosts,
+                flops=2 * own * margin * columns,
             )
             residual, *tiles = call(
                 residual_kernel,
@@ -383,42 +368,38 @@
                 remainder,
                 pick,
                 spread,
-                r2,
-                r3,
-                flops=(2 * margin + 4 * tile) * own * columns,
-            )
+                *returned,
+                flops=4 * margin * own * columns,
+            )
+        ghosts = traded(tiles)
         if first:
-            residual, tiles = lax.optimization_barrier((residual, tuple(tiles)))
-            (inverse,) = call(
+            inverse, partial = call(
                 load_kernel,
-                "load",
-                [(inverse.shape, HALF)],
+                "inverse_own",
+                [(inverse.shape, HALF), local_full],
                 inverse,
                 residual,
                 far=1,
                 scratch=(pltpu.SemaphoreType.DMA((MATRIX_PIECES,)),),
-            )
-        g0, g1, g2, g3 = traded(tiles)
-        partial, near = call(
-            near_solve_kernel,
-            "inverse_near",
-            [local_full, ((coarse, columns), FULL)],
-            inverse,
-            basis,
-            residual,
-            g0,
-            g1,
-            flops=2 * (local + coarse) * (own + 2 * tile) * columns,
-        )
+                flops=2 * local * own * columns,
+            )
+        else:
+            (partial,) = call(
+                own_columns_kernel,
+                "inverse_own",
+                [local_full],
+                inverse,
+                residual,
+                flops=2 * local * own * columns,
+            )
         (restricted,) = call(
             restrict_kernel,
             "restrict",
             [((coarse, columns), HALF)],
             basis,
-            near,
-            g2,
-            g3,
-            flops=4 * coarse * tile * columns,
+            residual,
+            *ghosts,
+            flops=2 * local * coarse * columns,
         )
         restricted = [meeting(restricted, "col", turn) for turn in reversed(range(across))][::-1]
         rim, inner = call(
@@ -427,25 +408,31 @@
             [((margin, columns), FULL), owned_full],
             inverse,
             partial,
-            g2,
-            g3,
-            flops=4 * local * tile * columns,
+            *ghosts,
+            flops=2 * local * margin * columns,
         )
         parts = call(
             parts_kernel(groups, across),
             "coarse_part",
-            [((coarse, columns), HALF)] * groups,
+            [((2 * coarse, columns), HALF)] * (groups // 2),
             coarse_inverse,
             *restricted,
             scratch=(pltpu.VMEM((across * coarse, columns), HALF),),
             flops=2 * coarse_inverse.size * columns,
         )
-        parts = [meeting(parts[turn], "row", turn) for turn in reversed(range(groups))]
+        parts = [meeting(parts[turn], "row", turn, 2) for turn in reversed(range(groups // 2))]
+        mine, others = call(
+            pair_kernel,
+            "coarse_pair",
+            [((coarse, columns), FULL), ((coarse, columns), HALF)],
+            *parts,
+        )
         level, *tiles = call(
-            coarse_kernel(groups),
+            coarse_kernel,
             "coarse",
             [((coarse, columns), HALF)] + four_tiles,
-            *parts,
+            mine,
+            swapped(others, "row", 0),
             basis,
             rim,
             flops=2 * coarse * margin * columns,
@@ -461,7 +448,7 @@
                 far=1,
                 scratch=(pltpu.SemaphoreType.DMA((MATRIX_PIECES,)),),
             )
-        r0, r1, r2, r3 = traded(tiles)
+        returned = traded(tiles)
         (base,) = call(
             base_kernel(first),
             "base",
@@ -470,10 +457,7 @@
             inner,
             level,
             basis,
-            spread,
-            r0,
-            r1,
-            flops=2 * (2 * tile + coarse) * own * columns,
+            flops=2 * coarse * own * columns,
         )
         if last:
             break
@@ -484,9 +468,8 @@
             base,
             pick,
             spread,
-            r2,
-            r3,
-            flops=(2 * margin + 4 * tile) * own * columns,
+            *returned,
+            flops=4 * margin * own * columns,
         )
     (solution,) = call(
         last_update_kernel,
@@ -494,11 +477,10 @@
         [owned_full],
         base,
         spread,
-        r2,
-        r3,
+        *returned,
         away=True,
         scratch=(pltpu.VMEM((own, columns), FULL), pltpu.SemaphoreType.DMA((4,))),
-        flops=4 * tile * own * columns,
+        flops=2 * margin * own * columns,
     )
     return solution[None, None]
 

time: 149 us -> 135 us (0.906)
  starting transfers between devices: 94.2 us -> 65.4 us
  waiting for transfers between devices: 30.7 us -> 44 us
    ppermute x30 -> x18, starting transfers between devices: 39.3 us -> 19.2 us  [meeting(): lax.ppermute(shard, axis, pairs)]
    ppermute x40 -> x43, waiting for transfers between devices: 20.5 us -> 34.5 us  [swapped(): lax.ppermute(shard, axis, [(i, j) for i, j in pairs if 0 <= j < devices])]
    ppermute x40 -> x43, starting transfers between devices: 54.9 us -> 46.1 us  [swapped(): lax.ppermute(shard, axis, [(i, j) for i, j in pairs if 0 <= j < devices])]
    pallas_call x32 -> x34, Pallas kernels: 23.5 us -> 24.6 us  [call(): pl.pallas_call(body, out_shape=tuple(((pltpu.HBM if away else pltpu.VMEM)...]
    ppermute x30 -> x18, waiting for transfers between devices: 10.1 us -> 9.54 us  [meeting(): lax.ppermute(shard, axis, pairs)]
  transfers between devices with their start and end apart: 70 -> 61, of which waited for: 21 -> 28; matrix products, arithmetic and copies ran while one was open for 0% -> 0% of each run, Pallas kernels for 10% -> 10%
where the time goes in v10:
time: 135 us
  starting transfers between devices  65.4 us (48%)
  waiting for transfers between devices  44 us (33%)
  Pallas kernels  24.6 us (18%)
    ppermute x43, starting transfers between devices, swapped(): lax.ppermute(shard, axis, [(i, j) for i, j in pairs if 0 <= j < devices])  46.1 us
    ppermute x43, waiting for transfers between devices, swapped(): lax.ppermute(shard, axis, [(i, j) for i, j in pairs if 0 <= j < devices])  34.5 us
    pallas_call x34, Pallas kernels, call(): pl.pallas_call(body, out_shape=tuple(((pltpu.HBM if away else pltpu.VMEM)...  24.6 us
    ppermute x18, starting transfers between devices, meeting(): lax.ppermute(shard, axis, pairs)  19.2 us
    ppermute x18, waiting for transfers between devices, meeting(): lax.ppermute(shard, axis, pairs)  9.54 us
  transfers between devices with their start and end apart: 61, of which 28 were waited for; matrix products, arithmetic and copies ran while one was open for 0% of the time, Pallas kernels for 10%

profile of v10, /device:TPU:0, one launch (start us, length us, event | category | flops | bytes accessed | tf_op | source)
XLA Modules:
  0.0 134.6 jit_solution(13693698069824969439)
XLA Ops:
  0.0 1.8 %select.1 = (f32[1024,256]{1,0:T(8,128)S(1)}, bf16[1024,256]{1,0:T(8,128)(2,1)S(1)}, bf16[512,1024]{1,0:T(8,128)(2,1)S(1)}, s32[4,128]{1,0:T(4,128)S(1)}, bf16[3...) custom-call(f32[1024,256]{1,0:T(8,128)} %bitcast.11, ...), custom_call_target="tpu_custom_call" | custom-call | flops 268435456 | bytes 1148944 | tf_op jit(solution)/shard_map/select/pallas_call | solution.py:28
  1.8 3.0 %collective-permute-start = (bf16[128,256]{1,0:T(8,128)(2,1)S(1)}, bf16[128,256]{1,0:T(8,128)(2,1)S(1)}, u32[]{:S(2)}, u32[]{:S(2)}) collective-permute-start(bf16[128,256]{1,0:T(8,128)(2,1)S(1)} %get-tuple-element.95), channel_id=1, source_target_pairs={{0,4},{4,0},{8,12},{12,8},{16,20},{20,16},{24,28},{28,24},{1,5},{5... | collective-permute-start | bytes 196616 | tf_op jit(solution)/shard_map/ppermute | solution.py:281
  4.9 3.6 %collective-permute-start.1 = (bf16[128,256]{1,0:T(8,128)(2,1)S(1)}, bf16[128,256]{1,0:T(8,128)(2,1)S(1)}, u32[]{:S(2)}, u32[]{:S(2)}) collective-permute-start(bf16[128,256]{1,0:T(8,128)(2,1)S(1)} %get-tuple-element.96), channel_id=1, source_target_pairs={{0,28},{4,8},{8,4},{12,16},{16,12},{20,24},{24,20},{28,0},{1,29},{... | collective-permute-start | bytes 196616 | tf_op jit(solution)/shard_map/ppermute | solution.py:281
  8.4 1.6 %collective-permute-start.3 = (bf16[128,256]{1,0:T(8,128)(2,1)S(1)}, bf16[128,256]{1,0:T(8,128)(2,1)S(1)}, u32[]{:S(2)}, u32[]{:S(2)}) collective-permute-start(bf16[128,256]{1,0:T(8,128)(2,1)S(1)} %get-tuple-element.98), channel_id=1, source_target_pairs={{0,3},{1,2},{2,1},{3,0},{4,7},{5,6},{6,5},{7,4},{8,11},{9,10},{10,... | collective-permute-start | bytes 196616 | tf_op jit(solution)/shard_map/ppermute | solution.py:281
  10.0 1.8 %collective-permute-done.1.g1 = bf16[128,256]{1,0:T(8,128)(2,1)S(1)} collective-permute-done((bf16[128,256]{1,0:T(8,128)(2,1)S(1)}, bf16[128,256]{1,0:T(8,128)(2,1)S(1)}, u32[]{:S(2)}, u32[]{:S(2)}) %collective-permute-start.1) | collective-permute-done | bytes 65568 | tf_op jit(solution)/shard_map/ppermute | solution.py:281
  12.4 1.6 %collective-permute-start.6 = (bf16[32,256]{1,0:T(8,128)(2,1)S(1)}, bf16[32,256]{1,0:T(8,128)(2,1)S(1)}, u32[]{:S(2)}, u32[]{:S(2)}) collective-permute-start(bf16[32,256]{1,0:T(8,128)(2,1)S(1)} %restrict.3.refs_0_), channel_id=1, source_target_pairs={{0,3},{1,2},{2,1},{3,0},{4,7},{5,6},{6,5},{7,4},{8,11},{9,10},{10,... | collective-permute-start | bytes 49160 | tf_op jit(solution)/shard_map/ppermute | solution.py:175
  15.6 2.1 %collective-permute-done.5.refs_2_ = bf16[32,256]{1,0:T(8,128)(2,1)S(1)} collective-permute-done((bf16[32,256]{1,0:T(8,128)(2,1)S(1)}, bf16[32,256]{1,0:T(8,128)(2,1)S(1)}, u32[]{:S(2)}, u32[]{:S(2)}) %collective-permute-start.5) | collective-permute-done | bytes 16416 | tf_op jit(solution)/shard_map/ppermute | solution.py:175
  18.7 3.7 %collective-permute-start.9 = (bf16[64,256]{1,0:T(8,128)(2,1)S(1)}, bf16[64,256]{1,0:T(8,128)(2,1)S(1)}, u32[]{:S(2)}, u32[]{:S(2)}) collective-permute-start(bf16[64,256]{1,0:T(8,128)(2,1)S(1)} %get-tuple-element.103), channel_id=1, source_target_pairs={{0,8},{4,12},{8,0},{12,4},{16,24},{20,28},{24,16},{28,20},{1,9},{5... | collective-permute-start | bytes 98312 | tf_op jit(solution)/shard_map/ppermute | solution.py:175
  22.4 3.5 %inverse_own.3 = (bf16[1536,1536]{1,0:T(8,128)(2,1)S(1)}, f32[1536,256]{1,0:T(8,128)S(1)}) custom-call(bf16[1536,1536]{1,0:T(8,128)(2,1)} %bitcast.9, bf16[1024,256]{1,0:T(8,128)(2,1)S(1)} %get-tuple-element.92.owned), custom_call_target="tpu_custom_call" | custom-call | flops 805306368 | bytes 5242880 | tf_op jit(solution)/shard_map/inverse_own/pallas_call | solution.py:28
  26.7 3.3 %collective-permute-done.10.theirs = bf16[32,256]{1,0:T(8,128)(2,1)S(1)} collective-permute-done((bf16[32,256]{1,0:T(8,128)(2,1)S(1)}, bf16[32,256]{1,0:T(8,128)(2,1)S(1)}, u32[]{:S(2)}, u32[]{:S(2)}) %collective-permute-start.10) | collective-permute-done | bytes 16416 | tf_op jit(solution)/shard_map/ppermute | solution.py:281
  30.3 2.0 %collective-permute-start.12 = (bf16[128,256]{1,0:T(8,128)(2,1)S(1)}, bf16[128,256]{1,0:T(8,128)(2,1)S(1)}, u32[]{:S(2)}, u32[]{:S(2)}) collective-permute-start(bf16[128,256]{1,0:T(8,128)(2,1)S(1)} %get-tuple-element.118), channel_id=1, source_target_pairs={{0,28},{4,8},{8,4},{12,16},{16,12},{20,24},{24,20},{28,0},{1,29},{... | collective-permute-start | bytes 196616 | tf_op jit(solution)/shard_map/ppermute | solution.py:281
  33.5 2.6 %spread.1 = (bf16[1024,512]{1,0:T(8,128)(2,1)S(1)}, bf16[1536,1536]{1,0:T(8,128)(2,1)S(1)}) custom-call(bf16[1536,1536]{1,0:T(8,128)(2,1)} %bitcast.10, s32[4,128]{1,0:T(4,128)S(1)} %get-tuple-element.115.masked), custom_call_target="tpu_custom_call" | custom-call | bytes 4720640 | tf_op jit(solution)/shard_map/spread/pallas_call | solution.py:28
  37.3 1.3 update.2
  38.8 1.9 %collective-permute-start.16 = (bf16[128,256]{1,0:T(8,128)(2,1)S(1)}, bf16[128,256]{1,0:T(8,128)(2,1)S(1)}, u32[]{:S(2)}, u32[]{:S(2)}) collective-permute-start(bf16[128,256]{1,0:T(8,128)(2,1)S(1)} %get-tuple-element.126), channel_id=1, source_target_pairs={{0,28},{4,8},{8,4},{12,16},{16,12},{20,24},{24,20},{28,0},{1,29},{... | collective-permute-start | bytes 196616 | tf_op jit(solution)/shard_map/ppermute | solution.py:281
  40.7 1.3 collective-permute-start.18
  43.0 2.8 %collective-permute-done.16.g1 = bf16[128,256]{1,0:T(8,128)(2,1)S(1)} collective-permute-done((bf16[128,256]{1,0:T(8,128)(2,1)S(1)}, bf16[128,256]{1,0:T(8,128)(2,1)S(1)}, u32[]{:S(2)}, u32[]{:S(2)}) %collective-permute-start.16) | collective-permute-done | bytes 65568 | tf_op jit(solution)/shard_map/ppermute | solution.py:281
  46.2 1.9 %collective-permute-start.20 = (bf16[128,256]{1,0:T(8,128)(2,1)S(1)}, bf16[128,256]{1,0:T(8,128)(2,1)S(1)}, u32[]{:S(2)}, u32[]{:S(2)}) collective-permute-start(bf16[128,256]{1,0:T(8,128)(2,1)S(1)} %get-tuple-element.130), channel_id=1, source_target_pairs={{0,28},{4,8},{8,4},{12,16},{16,12},{20,24},{24,20},{28,0},{1,29},{... | collective-permute-start | bytes 196616 | tf_op jit(solution)/shard_map/ppermute | solution.py:281
  50.4 2.8 %collective-permute-done.20.r1 = bf16[128,256]{1,0:T(8,128)(2,1)S(1)} collective-permute-done((bf16[128,256]{1,0:T(8,128)(2,1)S(1)}, bf16[128,256]{1,0:T(8,128)(2,1)S(1)}, u32[]{:S(2)}, u32[]{:S(2)}) %collective-permute-start.20) | collective-permute-done | bytes 65568 | tf_op jit(solution)/shard_map/ppermute | solution.py:281
  53.2 1.3 residual.2
  54.7 1.9 %collective-permute-start.24 = (bf16[128,256]{1,0:T(8,128)(2,1)S(1)}, bf16[128,256]{1,0:T(8,128)(2,1)S(1)}, u32[]{:S(2)}, u32[]{:S(2)}) collective-permute-start(bf16[128,256]{1,0:T(8,128)(2,1)S(1)} %get-tuple-element.135), channel_id=1, source_target_pairs={{0,28},{4,8},{8,4},{12,16},{16,12},{20,24},{24,20},{28,0},{1,29},{... | collective-permute-start | bytes 196616 | tf_op jit(solution)/shard_map/ppermute | solution.py:281
  56.6 1.3 collective-permute-start.26
  58.8 2.8 %collective-permute-done.24.g1 = bf16[128,256]{1,0:T(8,128)(2,1)S(1)} collective-permute-done((bf16[128,256]{1,0:T(8,128)(2,1)S(1)}, bf16[128,256]{1,0:T(8,128)(2,1)S(1)}, u32[]{:S(2)}, u32[]{:S(2)}) %collective-permute-start.24) | collective-permute-done | bytes 65568 | tf_op jit(solution)/shard_map/ppermute | solution.py:281
  63.8 1.3 collective-permute-done.29.refs_3_
  66.6 1.4 %collective-permute-start.31 = (bf16[64,256]{1,0:T(8,128)(2,1)S(1)}, bf16[64,256]{1,0:T(8,128)(2,1)S(1)}, u32[]{:S(2)}, u32[]{:S(2)}) collective-permute-start(bf16[64,256]{1,0:T(8,128)(2,1)S(1)} %get-tuple-element.140), channel_id=1, source_target_pairs={{0,16},{4,20},{8,24},{12,28},{16,0},{20,4},{24,8},{28,12},{1,17},{... | collective-permute-start | bytes 98312 | tf_op jit(solution)/shard_map/ppermute | solution.py:175
  68.0 2.4 %collective-permute-start.32 = (bf16[64,256]{1,0:T(8,128)(2,1)S(1)}, bf16[64,256]{1,0:T(8,128)(2,1)S(1)}, u32[]{:S(2)}, u32[]{:S(2)}) collective-permute-start(bf16[64,256]{1,0:T(8,128)(2,1)S(1)} %get-tuple-element.141), channel_id=1, source_target_pairs={{0,8},{4,12},{8,0},{12,4},{16,24},{20,28},{24,16},{28,20},{1,9},{5... | collective-permute-start | bytes 98312 | tf_op jit(solution)/shard_map/ppermute | solution.py:175
  72.3 1.5 %collective-permute-start.33 = (bf16[32,256]{1,0:T(8,128)(2,1)S(1)}, bf16[32,256]{1,0:T(8,128)(2,1)S(1)}, u32[]{:S(2)}, u32[]{:S(2)}) collective-permute-start(bf16[32,256]{1,0:T(8,128)(2,1)S(1)} %get-tuple-element.144), channel_id=1, source_target_pairs={{0,4},{4,0},{8,12},{12,8},{16,20},{20,16},{24,28},{28,24},{1,5},{5... | collective-permute-start | bytes 49160 | tf_op jit(solution)/shard_map/ppermute | solution.py:281
  74.3 1.8 %collective-permute-done.33.theirs = bf16[32,256]{1,0:T(8,128)(2,1)S(1)} collective-permute-done((bf16[32,256]{1,0:T(8,128)(2,1)S(1)}, bf16[32,256]{1,0:T(8,128)(2,1)S(1)}, u32[]{:S(2)}, u32[]{:S(2)}) %collective-permute-start.33) | collective-permute-done | bytes 16416 | tf_op jit(solution)/shard_map/ppermute | solution.py:281
  76.4 1.5 %collective-permute-start.34 = (bf16[128,256]{1,0:T(8,128)(2,1)S(1)}, bf16[128,256]{1,0:T(8,128)(2,1)S(1)}, u32[]{:S(2)}, u32[]{:S(2)}) collective-permute-start(bf16[128,256]{1,0:T(8,128)(2,1)S(1)} %get-tuple-element.147), channel_id=1, source_target_pairs={{0,4},{4,0},{8,12},{12,8},{16,20},{20,16},{24,28},{28,24},{1,5},{5... | collective-permute-start | bytes 196616 | tf_op jit(solution)/shard_map/ppermute | solution.py:281
  77.8 2.6 %collective-permute-start.35 = (bf16[128,256]{1,0:T(8,128)(2,1)S(1)}, bf16[128,256]{1,0:T(8,128)(2,1)S(1)}, u32[]{:S(2)}, u32[]{:S(2)}) collective-permute-start(bf16[128,256]{1,0:T(8,128)(2,1)S(1)} %get-tuple-element.148), channel_id=1, source_target_pairs={{0,28},{4,8},{8,4},{12,16},{16,12},{20,24},{24,20},{28,0},{1,29},{... | collective-permute-start | bytes 196616 | tf_op jit(solution)/shard_map/ppermute | solution.py:281
  81.7 3.0 %collective-permute-done.35.r1 = bf16[128,256]{1,0:T(8,128)(2,1)S(1)} collective-permute-done((bf16[128,256]{1,0:T(8,128)(2,1)S(1)}, bf16[128,256]{1,0:T(8,128)(2,1)S(1)}, u32[]{:S(2)}, u32[]{:S(2)}) %collective-permute-start.35) | collective-permute-done | bytes 65568 | tf_op jit(solution)/shard_map/ppermute | solution.py:281
  84.8 1.3 update.3
  86.1 2.7 %collective-permute-start.39 = (bf16[128,256]{1,0:T(8,128)(2,1)S(1)}, bf16[128,256]{1,0:T(8,128)(2,1)S(1)}, u32[]{:S(2)}, u32[]{:S(2)}) collective-permute-start(bf16[128,256]{1,0:T(8,128)(2,1)S(1)} %get-tuple-element.154), channel_id=1, source_target_pairs={{0,28},{4,8},{8,4},{12,16},{16,12},{20,24},{24,20},{28,0},{1,29},{... | collective-permute-start | bytes 196616 | tf_op jit(solution)/shard_map/ppermute | solution.py:281
  91.0 2.2 %collective-permute-done.39.g1 = bf16[128,256]{1,0:T(8,128)(2,1)S(1)} collective-permute-done((bf16[128,256]{1,0:T(8,128)(2,1)S(1)}, bf16[128,256]{1,0:T(8,128)(2,1)S(1)}, u32[]{:S(2)}, u32[]{:S(2)}) %collective-permute-start.39) | collective-permute-done | bytes 65568 | tf_op jit(solution)/shard_map/ppermute | solution.py:281
  93.7 2.6 %collective-permute-start.43 = (bf16[128,256]{1,0:T(8,128)(2,1)S(1)}, bf16[128,256]{1,0:T(8,128)(2,1)S(1)}, u32[]{:S(2)}, u32[]{:S(2)}) collective-permute-start(bf16[128,256]{1,0:T(8,128)(2,1)S(1)} %get-tuple-element.158), channel_id=1, source_target_pairs={{0,28},{4,8},{8,4},{12,16},{16,12},{20,24},{24,20},{28,0},{1,29},{... | collective-permute-start | bytes 196616 | tf_op jit(solution)/shard_map/ppermute | solution.py:281
  97.8 2.8 %collective-permute-done.43.r1 = bf16[128,256]{1,0:T(8,128)(2,1)S(1)} collective-permute-done((bf16[128,256]{1,0:T(8,128)(2,1)S(1)}, bf16[128,256]{1,0:T(8,128)(2,1)S(1)}, u32[]{:S(2)}, u32[]{:S(2)}) %collective-permute-start.43) | collective-permute-done | bytes 65568 | tf_op jit(solution)/shard_map/ppermute | solution.py:281
  100.7 1.3 residual.3
  102.1 2.6 %collective-permute-start.47 = (bf16[128,256]{1,0:T(8,128)(2,1)S(1)}, bf16[128,256]{1,0:T(8,128)(2,1)S(1)}, u32[]{:S(2)}, u32[]{:S(2)}) collective-permute-start(bf16[128,256]{1,0:T(8,128)(2,1)S(1)} %get-tuple-element.163), channel_id=1, source_target_pairs={{0,28},{4,8},{8,4},{12,16},{16,12},{20,24},{24,20},{28,0},{1,29},{... | collective-permute-start | bytes 196616 | tf_op jit(solution)/shard_map/ppermute | solution.py:281
  106.3 2.8 %collective-permute-done.47.g1 = bf16[128,256]{1,0:T(8,128)(2,1)S(1)} collective-permute-done((bf16[128,256]{1,0:T(8,128)(2,1)S(1)}, bf16[128,256]{1,0:T(8,128)(2,1)S(1)}, u32[]{:S(2)}, u32[]{:S(2)}) %collective-permute-start.47) | collective-permute-done | bytes 65568 | tf_op jit(solution)/shard_map/ppermute | solution.py:281
  111.2 1.3 collective-permute-done.52.refs_3_
  114.8 1.5 %collective-permute-start.54 = (bf16[64,256]{1,0:T(8,128)(2,1)S(1)}, bf16[64,256]{1,0:T(8,128)(2,1)S(1)}, u32[]{:S(2)}, u32[]{:S(2)}) collective-permute-start(bf16[64,256]{1,0:T(8,128)(2,1)S(1)} %get-tuple-element.168), channel_id=1, source_target_pairs={{0,16},{4,20},{8,24},{12,28},{16,0},{20,4},{24,8},{28,12},{1,17},{... | collective-permute-start | bytes 98312 | tf_op jit(solution)/shard_map/ppermute | solution.py:175
  116.3 2.0 %collective-permute-start.55 = (bf16[64,256]{1,0:T(8,128)(2,1)S(1)}, bf16[64,256]{1,0:T(8,128)(2,1)S(1)}, u32[]{:S(2)}, u32[]{:S(2)}) collective-permute-start(bf16[64,256]{1,0:T(8,128)(2,1)S(1)} %get-tuple-element.169), channel_id=1, source_target_pairs={{0,8},{4,12},{8,0},{12,4},{16,24},{20,28},{24,16},{28,20},{1,9},{5... | collective-permute-start | bytes 98312 | tf_op jit(solution)/shard_map/ppermute | solution.py:175
  120.3 1.6 %collective-permute-start.56 = (bf16[32,256]{1,0:T(8,128)(2,1)S(1)}, bf16[32,256]{1,0:T(8,128)(2,1)S(1)}, u32[]{:S(2)}, u32[]{:S(2)}) collective-permute-start(bf16[32,256]{1,0:T(8,128)(2,1)S(1)} %get-tuple-element.172), channel_id=1, source_target_pairs={{0,4},{4,0},{8,12},{12,8},{16,20},{20,16},{24,28},{28,24},{1,5},{5... | collective-permute-start | bytes 49160 | tf_op jit(solution)/shard_map/ppermute | solution.py:281
  122.5 1.7 %collective-permute-done.56.theirs = bf16[32,256]{1,0:T(8,128)(2,1)S(1)} collective-permute-done((bf16[32,256]{1,0:T(8,128)(2,1)S(1)}, bf16[32,256]{1,0:T(8,128)(2,1)S(1)}, u32[]{:S(2)}, u32[]{:S(2)}) %collective-permute-start.56) | collective-permute-done | bytes 16416 | tf_op jit(solution)/shard_map/ppermute | solution.py:281
  124.4 1.7 %collective-permute-start.57 = (bf16[128,256]{1,0:T(8,128)(2,1)S(1)}, bf16[128,256]{1,0:T(8,128)(2,1)S(1)}, u32[]{:S(2)}, u32[]{:S(2)}) collective-permute-start(bf16[128,256]{1,0:T(8,128)(2,1)S(1)} %get-tuple-element.175), channel_id=1, source_target_pairs={{0,4},{4,0},{8,12},{12,8},{16,20},{20,16},{24,28},{28,24},{1,5},{5... | collective-permute-start | bytes 196616 | tf_op jit(solution)/shard_map/ppermute | solution.py:281
  126.1 2.1 %collective-permute-start.58 = (bf16[128,256]{1,0:T(8,128)(2,1)S(1)}, bf16[128,256]{1,0:T(8,128)(2,1)S(1)}, u32[]{:S(2)}, u32[]{:S(2)}) collective-permute-start(bf16[128,256]{1,0:T(8,128)(2,1)S(1)} %get-tuple-element.176), channel_id=1, source_target_pairs={{0,28},{4,8},{8,4},{12,16},{16,12},{20,24},{24,20},{28,0},{1,29},{... | collective-permute-start | bytes 196616 | tf_op jit(solution)/shard_map/ppermute | solution.py:281
  128.3 1.3 collective-permute-start.60
  129.9 3.2 %collective-permute-done.58.r1 = bf16[128,256]{1,0:T(8,128)(2,1)S(1)} collective-permute-done((bf16[128,256]{1,0:T(8,128)(2,1)S(1)}, bf16[128,256]{1,0:T(8,128)(2,1)S(1)}, u32[]{:S(2)}, u32[]{:S(2)}) %collective-permute-start.58) | collective-permute-done | bytes 65568 | tf_op jit(solution)/shard_map/ppermute | solution.py:281
  133.1 1.3 last_update.1
  (110 shorter events, 32.9 us)
Async XLA Ops:
  1.8 8.2 %collective-permute-start = (bf16[128,256]{1,0:T(8,128)(2,1)S(1)}, bf16[128,256]{1,0:T(8,128)(2,1)S(1)}, u32[]{:S(2)}, u32[]{:S(2)}) collective-permute-start(bf16[128,256]{1,0:T(8,128)(2,1)S(1)} %get-tuple-element.95), channel_id=1, source_target_pairs={{0,4},{4,0},{8,12},{12,8},{16,20},{20,16},{24,28},{28,24},{1,5},{5... | collective-permute-start | bytes 196616 | tf_op jit(solution)/shard_map/ppermute | solution.py:281
  4.9 7.0 %collective-permute-start.1 = (bf16[128,256]{1,0:T(8,128)(2,1)S(1)}, bf16[128,256]{1,0:T(8,128)(2,1)S(1)}, u32[]{:S(2)}, u32[]{:S(2)}) collective-permute-start(bf16[128,256]{1,0:T(8,128)(2,1)S(1)} %get-tuple-element.96), channel_id=1, source_target_pairs={{0,28},{4,8},{8,4},{12,16},{16,12},{20,24},{24,20},{28,0},{1,29},{... | collective-permute-start | bytes 196616 | tf_op jit(solution)/shard_map/ppermute | solution.py:281
  17.9 8.0 %collective-permute-start.7 = (bf16[64,256]{1,0:T(8,128)(2,1)S(1)}, bf16[64,256]{1,0:T(8,128)(2,1)S(1)}, u32[]{:S(2)}, u32[]{:S(2)}) collective-permute-start(bf16[64,256]{1,0:T(8,128)(2,1)S(1)} %get-tuple-element.101), channel_id=1, source_target_pairs={{0,24},{4,28},{8,16},{12,20},{16,8},{20,12},{24,0},{28,4},{1,25},{... | collective-permute-start | bytes 98312 | tf_op jit(solution)/shard_map/ppermute | solution.py:175
  18.7 7.2 %collective-permute-start.8 = (bf16[64,256]{1,0:T(8,128)(2,1)S(1)}, bf16[64,256]{1,0:T(8,128)(2,1)S(1)}, u32[]{:S(2)}, u32[]{:S(2)}) collective-permute-start(bf16[64,256]{1,0:T(8,128)(2,1)S(1)} %get-tuple-element.102), channel_id=1, source_target_pairs={{0,16},{4,20},{8,24},{12,28},{16,0},{20,4},{24,8},{28,12},{1,17},{... | collective-permute-start | bytes 98312 | tf_op jit(solution)/shard_map/ppermute | solution.py:175
  18.7 7.2 %collective-permute-start.9 = (bf16[64,256]{1,0:T(8,128)(2,1)S(1)}, bf16[64,256]{1,0:T(8,128)(2,1)S(1)}, u32[]{:S(2)}, u32[]{:S(2)}) collective-permute-start(bf16[64,256]{1,0:T(8,128)(2,1)S(1)} %get-tuple-element.103), channel_id=1, source_target_pairs={{0,8},{4,12},{8,0},{12,4},{16,24},{20,28},{24,16},{28,20},{1,9},{5... | collective-permute-start | bytes 98312 | tf_op jit(solution)/shard_map/ppermute | solution.py:175
  26.0 4.0 %collective-permute-start.10 = (bf16[32,256]{1,0:T(8,128)(2,1)S(1)}, bf16[32,256]{1,0:T(8,128)(2,1)S(1)}, u32[]{:S(2)}, u32[]{:S(2)}) collective-permute-start(bf16[32,256]{1,0:T(8,128)(2,1)S(1)} %get-tuple-element.106), channel_id=1, source_target_pairs={{0,4},{4,0},{8,12},{12,8},{16,20},{20,16},{24,28},{28,24},{1,5},{5... | collective-permute-start | bytes 49160 | tf_op jit(solution)/shard_map/ppermute | solution.py:281
  30.2 6.2 %collective-permute-start.11 = (bf16[128,256]{1,0:T(8,128)(2,1)S(1)}, bf16[128,256]{1,0:T(8,128)(2,1)S(1)}, u32[]{:S(2)}, u32[]{:S(2)}) collective-permute-start(bf16[128,256]{1,0:T(8,128)(2,1)S(1)} %get-tuple-element.117), channel_id=1, source_target_pairs={{0,4},{4,0},{8,12},{12,8},{16,20},{20,16},{24,28},{28,24},{1,5},{5... | collective-permute-start | bytes 196616 | tf_op jit(solution)/shard_map/ppermute | solution.py:281
  30.3 7.0 %collective-permute-start.12 = (bf16[128,256]{1,0:T(8,128)(2,1)S(1)}, bf16[128,256]{1,0:T(8,128)(2,1)S(1)}, u32[]{:S(2)}, u32[]{:S(2)}) collective-permute-start(bf16[128,256]{1,0:T(8,128)(2,1)S(1)} %get-tuple-element.118), channel_id=1, source_target_pairs={{0,28},{4,8},{8,4},{12,16},{16,12},{20,24},{24,20},{28,0},{1,29},{... | collective-permute-start | bytes 196616 | tf_op jit(solution)/shard_map/ppermute | solution.py:281
  32.3 5.0 %collective-permute-start.13 = (bf16[128,256]{1,0:T(8,128)(2,1)S(1)}, bf16[128,256]{1,0:T(8,128)(2,1)S(1)}, u32[]{:S(2)}, u32[]{:S(2)}) collective-permute-start(bf16[128,256]{1,0:T(8,128)(2,1)S(1)} %get-tuple-element.119), channel_id=1, source_target_pairs={{0,1},{1,0},{2,3},{3,2},{4,5},{5,4},{6,7},{7,6},{8,9},{9,8},{10,11... | collective-permute-start | bytes 196616 | tf_op jit(solution)/shard_map/ppermute | solution.py:281
  32.3 5.0 %collective-permute-start.14 = (bf16[128,256]{1,0:T(8,128)(2,1)S(1)}, bf16[128,256]{1,0:T(8,128)(2,1)S(1)}, u32[]{:S(2)}, u32[]{:S(2)}) collective-permute-start(bf16[128,256]{1,0:T(8,128)(2,1)S(1)} %get-tuple-element.120), channel_id=1, source_target_pairs={{0,3},{1,2},{2,1},{3,0},{4,7},{5,6},{6,5},{7,4},{8,11},{9,10},{10,... | collective-permute-start | bytes 196616 | tf_op jit(solution)/shard_map/ppermute | solution.py:281
  38.6 4.4 %collective-permute-start.15 = (bf16[128,256]{1,0:T(8,128)(2,1)S(1)}, bf16[128,256]{1,0:T(8,128)(2,1)S(1)}, u32[]{:S(2)}, u32[]{:S(2)}) collective-permute-start(bf16[128,256]{1,0:T(8,128)(2,1)S(1)} %get-tuple-element.125), channel_id=1, source_target_pairs={{0,4},{4,0},{8,12},{12,8},{16,20},{20,16},{24,28},{28,24},{1,5},{5... | collective-permute-start | bytes 196616 | tf_op jit(solution)/shard_map/ppermute | solution.py:281
  38.8 7.0 %collective-permute-start.16 = (bf16[128,256]{1,0:T(8,128)(2,1)S(1)}, bf16[128,256]{1,0:T(8,128)(2,1)S(1)}, u32[]{:S(2)}, u32[]{:S(2)}) collective-permute-start(bf16[128,256]{1,0:T(8,128)(2,1)S(1)} %get-tuple-element.126), channel_id=1, source_target_pairs={{0,28},{4,8},{8,4},{12,16},{16,12},{20,24},{24,20},{28,0},{1,29},{... | collective-permute-start | bytes 196616 | tf_op jit(solution)/shard_map/ppermute | solution.py:281
  40.7 5.1 %collective-permute-start.17 = (bf16[128,256]{1,0:T(8,128)(2,1)S(1)}, bf16[128,256]{1,0:T(8,128)(2,1)S(1)}, u32[]{:S(2)}, u32[]{:S(2)}) collective-permute-start(bf16[128,256]{1,0:T(8,128)(2,1)S(1)} %get-tuple-element.127), channel_id=1, source_target_pairs={{0,1},{1,0},{2,3},{3,2},{4,5},{5,4},{6,7},{7,6},{8,9},{9,8},{10,11... | collective-permute-start | bytes 196616 | tf_op jit(solution)/shard_map/ppermute | solution.py:281
  40.7 5.1 %collective-permute-start.18 = (bf16[128,256]{1,0:T(8,128)(2,1)S(1)}, bf16[128,256]{1,0:T(8,128)(2,1)S(1)}, u32[]{:S(2)}, u32[]{:S(2)}) collective-permute-start(bf16[128,256]{1,0:T(8,128)(2,1)S(1)} %get-tuple-element.128), channel_id=1, source_target_pairs={{0,3},{1,2},{2,1},{3,0},{4,7},{5,6},{6,5},{7,4},{8,11},{9,10},{10,... | collective-permute-start | bytes 196616 | tf_op jit(solution)/shard_map/ppermute | solution.py:281
  46.1 4.3 %collective-permute-start.19 = (bf16[128,256]{1,0:T(8,128)(2,1)S(1)}, bf16[128,256]{1,0:T(8,128)(2,1)S(1)}, u32[]{:S(2)}, u32[]{:S(2)}) collective-permute-start(bf16[128,256]{1,0:T(8,128)(2,1)S(1)} %get-tuple-element.129), channel_id=1, source_target_pairs={{0,4},{4,0},{8,12},{12,8},{16,20},{20,16},{24,28},{28,24},{1,5},{5... | collective-permute-start | bytes 196616 | tf_op jit(solution)/shard_map/ppermute | solution.py:281
  46.2 7.0 %collective-permute-start.20 = (bf16[128,256]{1,0:T(8,128)(2,1)S(1)}, bf16[128,256]{1,0:T(8,128)(2,1)S(1)}, u32[]{:S(2)}, u32[]{:S(2)}) collective-permute-start(bf16[128,256]{1,0:T(8,128)(2,1)S(1)} %get-tuple-element.130), channel_id=1, source_target_pairs={{0,28},{4,8},{8,4},{12,16},{16,12},{20,24},{24,20},{28,0},{1,29},{... | collective-permute-start | bytes 196616 | tf_op jit(solution)/shard_map/ppermute | solution.py:281
  48.2 5.0 %collective-permute-start.21 = (bf16[128,256]{1,0:T(8,128)(2,1)S(1)}, bf16[128,256]{1,0:T(8,128)(2,1)S(1)}, u32[]{:S(2)}, u32[]{:S(2)}) collective-permute-start(bf16[128,256]{1,0:T(8,128)(2,1)S(1)} %get-tuple-element.131), channel_id=1, source_target_pairs={{0,1},{1,0},{2,3},{3,2},{4,5},{5,4},{6,7},{7,6},{8,9},{9,8},{10,11... | collective-permute-start | bytes 196616 | tf_op jit(solution)/shard_map/ppermute | solution.py:281
  48.2 5.0 %collective-permute-start.22 = (bf16[128,256]{1,0:T(8,128)(2,1)S(1)}, bf16[128,256]{1,0:T(8,128)(2,1)S(1)}, u32[]{:S(2)}, u32[]{:S(2)}) collective-permute-start(bf16[128,256]{1,0:T(8,128)(2,1)S(1)} %get-tuple-element.132), channel_id=1, source_target_pairs={{0,3},{1,2},{2,1},{3,0},{4,7},{5,6},{6,5},{7,4},{8,11},{9,10},{10,... | collective-permute-start | bytes 196616 | tf_op jit(solution)/shard_map/ppermute | solution.py:281
  54.5 4.3 %collective-permute-start.23 = (bf16[128,256]{1,0:T(8,128)(2,1)S(1)}, bf16[128,256]{1,0:T(8,128)(2,1)S(1)}, u32[]{:S(2)}, u32[]{:S(2)}) collective-permute-start(bf16[128,256]{1,0:T(8,128)(2,1)S(1)} %get-tuple-element.134), channel_id=1, source_target_pairs={{0,4},{4,0},{8,12},{12,8},{16,20},{20,16},{24,28},{28,24},{1,5},{5... | collective-permute-start | bytes 196616 | tf_op jit(solution)/shard_map/ppermute | solution.py:281
  54.7 7.0 %collective-permute-start.24 = (bf16[128,256]{1,0:T(8,128)(2,1)S(1)}, bf16[128,256]{1,0:T(8,128)(2,1)S(1)}, u32[]{:S(2)}, u32[]{:S(2)}) collective-permute-start(bf16[128,256]{1,0:T(8,128)(2,1)S(1)} %get-tuple-element.135), channel_id=1, source_target_pairs={{0,28},{4,8},{8,4},{12,16},{16,12},{20,24},{24,20},{28,0},{1,29},{... | collective-permute-start | bytes 196616 | tf_op jit(solution)/shard_map/ppermute | solution.py:281
  56.6 5.1 %collective-permute-start.25 = (bf16[128,256]{1,0:T(8,128)(2,1)S(1)}, bf16[128,256]{1,0:T(8,128)(2,1)S(1)}, u32[]{:S(2)}, u32[]{:S(2)}) collective-permute-start(bf16[128,256]{1,0:T(8,128)(2,1)S(1)} %get-tuple-element.136), channel_id=1, source_target_pairs={{0,1},{1,0},{2,3},{3,2},{4,5},{5,4},{6,7},{7,6},{8,9},{9,8},{10,11... | collective-permute-start | bytes 196616 | tf_op jit(solution)/shard_map/ppermute | solution.py:281
  56.6 5.1 %collective-permute-start.26 = (bf16[128,256]{1,0:T(8,128)(2,1)S(1)}, bf16[128,256]{1,0:T(8,128)(2,1)S(1)}, u32[]{:S(2)}, u32[]{:S(2)}) collective-permute-start(bf16[128,256]{1,0:T(8,128)(2,1)S(1)} %get-tuple-element.137), channel_id=1, source_target_pairs={{0,3},{1,2},{2,1},{3,0},{4,7},{5,6},{6,5},{7,4},{8,11},{9,10},{10,... | collective-permute-start | bytes 196616 | tf_op jit(solution)/shard_map/ppermute | solution.py:281
  65.9 5.8 %collective-permute-start.30 = (bf16[64,256]{1,0:T(8,128)(2,1)S(1)}, bf16[64,256]{1,0:T(8,128)(2,1)S(1)}, u32[]{:S(2)}, u32[]{:S(2)}) collective-permute-start(bf16[64,256]{1,0:T(8,128)(2,1)S(1)} %get-tuple-element.139), channel_id=1, source_target_pairs={{0,24},{4,28},{8,16},{12,20},{16,8},{20,12},{24,0},{28,4},{1,25},{... | collective-permute-start | bytes 98312 | tf_op jit(solution)/shard_map/ppermute | solution.py:175
  66.6 5.2 %collective-permute-start.31 = (bf16[64,256]{1,0:T(8,128)(2,1)S(1)}, bf16[64,256]{1,0:T(8,128)(2,1)S(1)}, u32[]{:S(2)}, u32[]{:S(2)}) collective-permute-start(bf16[64,256]{1,0:T(8,128)(2,1)S(1)} %get-tuple-element.140), channel_id=1, source_target_pairs={{0,16},{4,20},{8,24},{12,28},{16,0},{20,4},{24,8},{28,12},{1,17},{... | collective-permute-start | bytes 98312 | tf_op jit(solution)/shard_map/ppermute | solution.py:175
  68.0 4.3 %collective-permute-start.32 = (bf16[64,256]{1,0:T(8,128)(2,1)S(1)}, bf16[64,256]{1,0:T(8,128)(2,1)S(1)}, u32[]{:S(2)}, u32[]{:S(2)}) collective-permute-start(bf16[64,256]{1,0:T(8,128)(2,1)S(1)} %get-tuple-element.141), channel_id=1, source_target_pairs={{0,8},{4,12},{8,0},{12,4},{16,24},{20,28},{24,16},{28,20},{1,9},{5... | collective-permute-start | bytes 98312 | tf_op jit(solution)/shard_map/ppermute | solution.py:175
  76.4 5.4 %collective-permute-start.34 = (bf16[128,256]{1,0:T(8,128)(2,1)S(1)}, bf16[128,256]{1,0:T(8,128)(2,1)S(1)}, u32[]{:S(2)}, u32[]{:S(2)}) collective-permute-start(bf16[128,256]{1,0:T(8,128)(2,1)S(1)} %get-tuple-element.147), channel_id=1, source_target_pairs={{0,4},{4,0},{8,12},{12,8},{16,20},{20,16},{24,28},{28,24},{1,5},{5... | collective-permute-start | bytes 196616 | tf_op jit(solution)/shard_map/ppermute | solution.py:281
  77.8 7.0 %collective-permute-start.35 = (bf16[128,256]{1,0:T(8,128)(2,1)S(1)}, bf16[128,256]{1,0:T(8,128)(2,1)S(1)}, u32[]{:S(2)}, u32[]{:S(2)}) collective-permute-start(bf16[128,256]{1,0:T(8,128)(2,1)S(1)} %get-tuple-element.148), channel_id=1, source_target_pairs={{0,28},{4,8},{8,4},{12,16},{16,12},{20,24},{24,20},{28,0},{1,29},{... | collective-permute-start | bytes 196616 | tf_op jit(solution)/shard_map/ppermute | solution.py:281
  80.4 4.4 %collective-permute-start.36 = (bf16[128,256]{1,0:T(8,128)(2,1)S(1)}, bf16[128,256]{1,0:T(8,128)(2,1)S(1)}, u32[]{:S(2)}, u32[]{:S(2)}) collective-permute-start(bf16[128,256]{1,0:T(8,128)(2,1)S(1)} %get-tuple-element.149), channel_id=1, source_target_pairs={{0,1},{1,0},{2,3},{3,2},{4,5},{5,4},{6,7},{7,6},{8,9},{9,8},{10,11... | collective-permute-start | bytes 196616 | tf_op jit(solution)/shard_map/ppermute | solution.py:281
  80.4 4.4 %collective-permute-start.37 = (bf16[128,256]{1,0:T(8,128)(2,1)S(1)}, bf16[128,256]{1,0:T(8,128)(2,1)S(1)}, u32[]{:S(2)}, u32[]{:S(2)}) collective-permute-start(bf16[128,256]{1,0:T(8,128)(2,1)S(1)} %get-tuple-element.150), channel_id=1, source_target_pairs={{0,3},{1,2},{2,1},{3,0},{4,7},{5,6},{6,5},{7,4},{8,11},{9,10},{10,... | collective-permute-start | bytes 196616 | tf_op jit(solution)/shard_map/ppermute | solution.py:281
  86.1 4.9 %collective-permute-start.38 = (bf16[128,256]{1,0:T(8,128)(2,1)S(1)}, bf16[128,256]{1,0:T(8,128)(2,1)S(1)}, u32[]{:S(2)}, u32[]{:S(2)}) collective-permute-start(bf16[128,256]{1,0:T(8,128)(2,1)S(1)} %get-tuple-element.153), channel_id=1, source_target_pairs={{0,4},{4,0},{8,12},{12,8},{16,20},{20,16},{24,28},{28,24},{1,5},{5... | collective-permute-start | bytes 196616 | tf_op jit(solution)/shard_map/ppermute | solution.py:281
  86.1 7.0 %collective-permute-start.39 = (bf16[128,256]{1,0:T(8,128)(2,1)S(1)}, bf16[128,256]{1,0:T(8,128)(2,1)S(1)}, u32[]{:S(2)}, u32[]{:S(2)}) collective-permute-start(bf16[128,256]{1,0:T(8,128)(2,1)S(1)} %get-tuple-element.154), channel_id=1, source_target_pairs={{0,28},{4,8},{8,4},{12,16},{16,12},{20,24},{24,20},{28,0},{1,29},{... | collective-permute-start | bytes 196616 | tf_op jit(solution)/shard_map/ppermute | solution.py:281
  88.8 4.4 %collective-permute-start.40 = (bf16[128,256]{1,0:T(8,128)(2,1)S(1)}, bf16[128,256]{1,0:T(8,128)(2,1)S(1)}, u32[]{:S(2)}, u32[]{:S(2)}) collective-permute-start(bf16[128,256]{1,0:T(8,128)(2,1)S(1)} %get-tuple-element.155), channel_id=1, source_target_pairs={{0,1},{1,0},{2,3},{3,2},{4,5},{5,4},{6,7},{7,6},{8,9},{9,8},{10,11... | collective-permute-start | bytes 196616 | tf_op jit(solution)/shard_map/ppermute | solution.py:281
  88.8 4.4 %collective-permute-start.41 = (bf16[128,256]{1,0:T(8,128)(2,1)S(1)}, bf16[128,256]{1,0:T(8,128)(2,1)S(1)}, u32[]{:S(2)}, u32[]{:S(2)}) collective-permute-start(bf16[128,256]{1,0:T(8,128)(2,1)S(1)} %get-tuple-element.156), channel_id=1, source_target_pairs={{0,3},{1,2},{2,1},{3,0},{4,7},{5,6},{6,5},{7,4},{8,11},{9,10},{10,... | collective-permute-start | bytes 196616 | tf_op jit(solution)/shard_map/ppermute | solution.py:281
  93.5 4.3 %collective-permute-start.42 = (bf16[128,256]{1,0:T(8,128)(2,1)S(1)}, bf16[128,256]{1,0:T(8,128)(2,1)S(1)}, u32[]{:S(2)}, u32[]{:S(2)}) collective-permute-start(bf16[128,256]{1,0:T(8,128)(2,1)S(1)} %get-tuple-element.157), channel_id=1, source_target_pairs={{0,4},{4,0},{8,12},{12,8},{16,20},{20,16},{24,28},{28,24},{1,5},{5... | collective-permute-start | bytes 196616 | tf_op jit(solution)/shard_map/ppermute | solution.py:281
  93.7 7.0 %collective-permute-start.43 = (bf16[128,256]{1,0:T(8,128)(2,1)S(1)}, bf16[128,256]{1,0:T(8,128)(2,1)S(1)}, u32[]{:S(2)}, u32[]{:S(2)}) collective-permute-start(bf16[128,256]{1,0:T(8,128)(2,1)S(1)} %get-tuple-element.158), channel_id=1, source_target_pairs={{0,28},{4,8},{8,4},{12,16},{16,12},{20,24},{24,20},{28,0},{1,29},{... | collective-permute-start | bytes 196616 | tf_op jit(solution)/shard_map/ppermute | solution.py:281
  96.3 4.4 %collective-permute-start.44 = (bf16[128,256]{1,0:T(8,128)(2,1)S(1)}, bf16[128,256]{1,0:T(8,128)(2,1)S(1)}, u32[]{:S(2)}, u32[]{:S(2)}) collective-permute-start(bf16[128,256]{1,0:T(8,128)(2,1)S(1)} %get-tuple-element.159), channel_id=1, source_target_pairs={{0,1},{1,0},{2,3},{3,2},{4,5},{5,4},{6,7},{7,6},{8,9},{9,8},{10,11... | collective-permute-start | bytes 196616 | tf_op jit(solution)/shard_map/ppermute | solution.py:281
  96.3 4.4 %collective-permute-start.45 = (bf16[128,256]{1,0:T(8,128)(2,1)S(1)}, bf16[128,256]{1,0:T(8,128)(2,1)S(1)}, u32[]{:S(2)}, u32[]{:S(2)}) collective-permute-start(bf16[128,256]{1,0:T(8,128)(2,1)S(1)} %get-tuple-element.160), channel_id=1, source_target_pairs={{0,3},{1,2},{2,1},{3,0},{4,7},{5,6},{6,5},{7,4},{8,11},{9,10},{10,... | collective-permute-start | bytes 196616 | tf_op jit(solution)/shard_map/ppermute | solution.py:281
  101.9 4.3 %collective-permute-start.46 = (bf16[128,256]{1,0:T(8,128)(2,1)S(1)}, bf16[128,256]{1,0:T(8,128)(2,1)S(1)}, u32[]{:S(2)}, u32[]{:S(2)}) collective-permute-start(bf16[128,256]{1,0:T(8,128)(2,1)S(1)} %get-tuple-element.162), channel_id=1, source_target_pairs={{0,4},{4,0},{8,12},{12,8},{16,20},{20,16},{24,28},{28,24},{1,5},{5... | collective-permute-start | bytes 196616 | tf_op jit(solution)/shard_map/ppermute | solution.py:281
  102.1 7.0 %collective-permute-start.47 = (bf16[128,256]{1,0:T(8,128)(2,1)S(1)}, bf16[128,256]{1,0:T(8,128)(2,1)S(1)}, u32[]{:S(2)}, u32[]{:S(2)}) collective-permute-start(bf16[128,256]{1,0:T(8,128)(2,1)S(1)} %get-tuple-element.163), channel_id=1, source_target_pairs={{0,28},{4,8},{8,4},{12,16},{16,12},{20,24},{24,20},{28,0},{1,29},{... | collective-permute-start | bytes 196616 | tf_op jit(solution)/shard_map/ppermute | solution.py:281
  104.7 4.4 %collective-permute-start.48 = (bf16[128,256]{1,0:T(8,128)(2,1)S(1)}, bf16[128,256]{1,0:T(8,128)(2,1)S(1)}, u32[]{:S(2)}, u32[]{:S(2)}) collective-permute-start(bf16[128,256]{1,0:T(8,128)(2,1)S(1)} %get-tuple-element.164), channel_id=1, source_target_pairs={{0,1},{1,0},{2,3},{3,2},{4,5},{5,4},{6,7},{7,6},{8,9},{9,8},{10,11... | collective-permute-start | bytes 196616 | tf_op jit(solution)/shard_map/ppermute | solution.py:281
  104.7 4.4 %collective-permute-start.49 = (bf16[128,256]{1,0:T(8,128)(2,1)S(1)}, bf16[128,256]{1,0:T(8,128)(2,1)S(1)}, u32[]{:S(2)}, u32[]{:S(2)}) collective-permute-start(bf16[128,256]{1,0:T(8,128)(2,1)S(1)} %get-tuple-element.165), channel_id=1, source_target_pairs={{0,3},{1,2},{2,1},{3,0},{4,7},{5,6},{6,5},{7,4},{8,11},{9,10},{10,... | collective-permute-start | bytes 196616 | tf_op jit(solution)/shard_map/ppermute | solution.py:281
  113.9 6.1 %collective-permute-start.53 = (bf16[64,256]{1,0:T(8,128)(2,1)S(1)}, bf16[64,256]{1,0:T(8,128)(2,1)S(1)}, u32[]{:S(2)}, u32[]{:S(2)}) collective-permute-start(bf16[64,256]{1,0:T(8,128)(2,1)S(1)} %get-tuple-element.167), channel_id=1, source_target_pairs={{0,24},{4,28},{8,16},{12,20},{16,8},{20,12},{24,0},{28,4},{1,25},{... | collective-permute-start | bytes 98312 | tf_op jit(solution)/shard_map/ppermute | solution.py:175
  114.8 5.2 %collective-permute-start.54 = (bf16[64,256]{1,0:T(8,128)(2,1)S(1)}, bf16[64,256]{1,0:T(8,128)(2,1)S(1)}, u32[]{:S(2)}, u32[]{:S(2)}) collective-permute-start(bf16[64,256]{1,0:T(8,128)(2,1)S(1)} %get-tuple-element.168), channel_id=1, source_target_pairs={{0,16},{4,20},{8,24},{12,28},{16,0},{20,4},{24,8},{28,12},{1,17},{... | collective-permute-start | bytes 98312 | tf_op jit(solution)/shard_map/ppermute | solution.py:175
  116.3 4.0 %collective-permute-start.55 = (bf16[64,256]{1,0:T(8,128)(2,1)S(1)}, bf16[64,256]{1,0:T(8,128)(2,1)S(1)}, u32[]{:S(2)}, u32[]{:S(2)}) collective-permute-start(bf16[64,256]{1,0:T(8,128)(2,1)S(1)} %get-tuple-element.169), channel_id=1, source_target_pairs={{0,8},{4,12},{8,0},{12,4},{16,24},{20,28},{24,16},{28,20},{1,9},{5... | collective-permute-start | bytes 98312 | tf_op jit(solution)/shard_map/ppermute | solution.py:175
  124.4 5.5 %collective-permute-start.57 = (bf16[128,256]{1,0:T(8,128)(2,1)S(1)}, bf16[128,256]{1,0:T(8,128)(2,1)S(1)}, u32[]{:S(2)}, u32[]{:S(2)}) collective-permute-start(bf16[128,256]{1,0:T(8,128)(2,1)S(1)} %get-tuple-element.175), channel_id=1, source_target_pairs={{0,4},{4,0},{8,12},{12,8},{16,20},{20,16},{24,28},{28,24},{1,5},{5... | collective-permute-start | bytes 196616 | tf_op jit(solution)/shard_map/ppermute | solution.py:281
  126.1 7.0 %collective-permute-start.58 = (bf16[128,256]{1,0:T(8,128)(2,1)S(1)}, bf16[128,256]{1,0:T(8,128)(2,1)S(1)}, u32[]{:S(2)}, u32[]{:S(2)}) collective-permute-start(bf16[128,256]{1,0:T(8,128)(2,1)S(1)} %get-tuple-element.176), channel_id=1, source_target_pairs={{0,28},{4,8},{8,4},{12,16},{16,12},{20,24},{24,20},{28,0},{1,29},{... | collective-permute-start | bytes 196616 | tf_op jit(solution)/shard_map/ppermute | solution.py:281
  128.3 4.8 %collective-permute-start.59 = (bf16[128,256]{1,0:T(8,128)(2,1)S(1)}, bf16[128,256]{1,0:T(8,128)(2,1)S(1)}, u32[]{:S(2)}, u32[]{:S(2)}) collective-permute-start(bf16[128,256]{1,0:T(8,128)(2,1)S(1)} %get-tuple-element.177), channel_id=1, source_target_pairs={{0,1},{1,0},{2,3},{3,2},{4,5},{5,4},{6,7},{7,6},{8,9},{9,8},{10,11... | collective-permute-start | bytes 196616 | tf_op jit(solution)/shard_map/ppermute | solution.py:281
  128.3 4.8 %collective-permute-start.60 = (bf16[128,256]{1,0:T(8,128)(2,1)S(1)}, bf16[128,256]{1,0:T(8,128)(2,1)S(1)}, u32[]{:S(2)}, u32[]{:S(2)}) collective-permute-start(bf16[128,256]{1,0:T(8,128)(2,1)S(1)} %get-tuple-element.178), channel_id=1, source_target_pairs={{0,3},{1,2},{2,1},{3,0},{4,7},{5,6},{6,5},{7,4},{8,11},{9,10},{10,... | collective-permute-start | bytes 196616 | tf_op jit(solution)/shard_map/ppermute | solution.py:281
  (14 other events, 61.8 us)

commit v11 on v10

--- a/solution.py
+++ b/solution.py
@@ -219,28 +219,34 @@
     def body(*refs):
         refs = list(refs)
         before = None if first else refs.pop(0)
-        inner, level, basis, out = refs
-        own = out.shape[0]
-        update = inner[...] + turned_product(basis[:, :own], level[...])
+        inner, level, basis, spread, r0, r1, out = refs
+        own, tile = out.shape[0], r0.shape[0]
+        update = (
+            inner[...]
+            + turned_product(basis[:, :own], level[...])
+            + product(spread[:, : 2 * tile], stacked(r0, r1))
+        )
         out[...] = DAMPING * update if first else before[...] + DAMPING * update
 
     return body
 
 
-def update_kernel(base, pick, spread, r0, r1, r2, r3, after, half, *tiles):
-    after[...] = base[...] + DAMPING * product(spread[...], stacked(r0, r1, r2, r3))
+def update_kernel(base, pick, spread, r2, r3, after, half, *tiles):
+    tile = r2.shape[0]
+    after[...] = base[...] + DAMPING * product(spread[:, 2 * tile :], stacked(r2, r3))
     half[...] = after[...].astype(HALF)
     picked(pick, half, tiles)
 
 
-def last_update_kernel(base, spread, r0, r1, r2, r3, far, after, sems):
+def last_update_kernel(base, spread, r2, r3, far, after, sems):
+    tile = r2.shape[0]
     pieces = sems.shape[0]
     height = after.shape[0] // pieces
-    returned = stacked(r0, r1, r2, r3)
+    returned = stacked(r2, r3)
     stores = []
     for i in range(pieces):
         at = slice(i * height, (i + 1) * height)
-        after[at, :] = base[at, :] + DAMPING * product(spread[at, :], returned)
+        after[at, :] = base[at, :] + DAMPING * product(spread[at, 2 * tile :], returned)
         stores.append(pltpu.make_async_copy(after.at[at], far.at[at], sems.at[i]))
         stores[-1].start()
     for store in stores:
@@ -256,15 +262,19 @@
         tiles[d][...] = (partial[at, :] + product(matrix[at, own:], ghosts)).astype(HALF)
 
 
-def remainder_kernel(target, matrix, partial, g0, g1, g2, g3, out):
-    own = target.shape[0]
-    out[...] = target[...] - (
-        partial[:own, :] + product(matrix[:own, own:], stacked(g0, g1, g2, g3))
+def remainder_kernel(target, matrix, partial, g0, g1, g2, g3, spread, r0, r1, out):
+    own, tile = target.shape[0], r0.shape[0]
+    image = (
+        partial[:own, :]
+        + product(matrix[:own, own:], stacked(g0, g1, g2, g3))
+        + product(spread[:, : 2 * tile], stacked(r0, r1))
     )
-
-
-def residual_kernel(remainder, pick, spread, r0, r1, r2, r3, half, *tiles):
-    half[...] = (remainder[...] - product(spread[...], stacked(r0, r1, r2, r3))).astype(HALF)
+    out[...] = target[...] - image
+
+
+def residual_kernel(remainder, pick, spread, r2, r3, half, *tiles):
+    tile = r2.shape[0]
+    half[...] = (remainder[...] - product(spread[:, 2 * tile :], stacked(r2, r3))).astype(HALF)
     picked(pick, half, tiles)
 
 
@@ -274,11 +284,24 @@
 
 
 def swapped(shard, axis, exchange):
-    devices = lax.axis_size(axis)
-    pairs = [(i, partner(i, exchange)) for i in range(devices)]
-    if devices % 2 == 0:
-        pairs = [(i, j % devices) for i, j in pairs]
-    return lax.ppermute(shard, axis, [(i, j) for i, j in pairs if 0 <= j < devices])
+    rows, columns = lax.axis_size("row"), lax.axis_size("col")
+
+    def other(row, col):
+        if axis == "row":
+            there = partner(row, exchange), col
+            beside = row, partner(col, 0)
+        else:
+            there = row, partner(col, exchange)
+            beside = partner(row, 0), col
+        for at in (there, beside):
+            if 0 <= at[0] < rows and 0 <= at[1] < columns:
+                return at
+        return row, col
+
+    places = [(row, col) for row in range(rows) for col in range(columns)]
+    ends = [(at, other(*at)) for at in places]
+    pairs = [(i * columns + j, k * columns + l) for (i, j), (k, l) in ends]
+    return lax.ppermute(shard, ("row", "col"), pairs)
 
 
 def traded(tiles):
@@ -359,7 +382,9 @@
                 operator,
                 partial,
                 *ghosts,
-                flops=2 * own * margin * columns,
+                spread,
+                *returned[:2],
+                flops=2 * own * (margin + 2 * tile) * columns,
             )
             residual, *tiles = call(
                 residual_kernel,
@@ -368,8 +393,8 @@
                 remainder,
                 pick,
                 spread,
-                *returned,
-                flops=4 * margin * own * columns,
+                *returned[2:],
+                flops=2 * (margin + 2 * tile) * own * columns,
             )
         ghosts = traded(tiles)
         if first:
@@ -457,7 +482,9 @@
             inner,
             level,
             basis,
-            flops=2 * coarse * own * columns,
+            spread,
+            *returned[:2],
+            flops=2 * (coarse + 2 * tile) * own * columns,
         )
         if last:
             break
@@ -468,8 +495,8 @@
             base,
             pick,
             spread,
-            *returned,
-            flops=4 * margin * own * columns,
+            *returned[2:],
+            flops=2 * (margin + 2 * tile) * own * columns,
         )
     (solution,) = call(
         last_update_kernel,
@@ -477,7 +504,7 @@
         [owned_full],
         base,
         spread,
-        *returned,
+        *returned[2:],
         away=True,
         scratch=(pltpu.VMEM((own, columns), FULL), pltpu.SemaphoreType.DMA((4,))),
         flops=2 * margin * own * columns,

time: 135 us -> 126 us (0.933)
  waiting for transfers between devices: 44 us -> 35.5 us
    ppermute x43, waiting for transfers between devices: 34.5 us -> 23.4 us  [swapped(): return lax.ppermute(shard, ('row', 'col'), pairs)]
    ppermute x18, waiting for transfers between devices: 9.54 us -> 12.1 us  [meeting(): lax.ppermute(shard, axis, pairs)]
    ppermute x43, starting transfers between devices: 46.1 us -> 47.5 us  [swapped(): return lax.ppermute(shard, ('row', 'col'), pairs)]
  transfers between devices with their start and end apart: 61 -> 61, of which waited for: 28 -> 29; matrix products, arithmetic and copies ran while one was open for 0% -> 0% of each run, Pallas kernels for 10% -> 11%
where the time goes in v11:
time: 126 us
  starting transfers between devices  66.5 us (53%)
  waiting for transfers between devices  35.5 us (28%)
  Pallas kernels  23.7 us (19%)
    ppermute x43, starting transfers between devices, swapped(): return lax.ppermute(shard, ('row', 'col'), pairs)  47.5 us
    pallas_call x34, Pallas kernels, call(): pl.pallas_call(body, out_shape=tuple(((pltpu.HBM if away else pltpu.VMEM)...  23.7 us
    ppermute x43, waiting for transfers between devices, swapped(): return lax.ppermute(shard, ('row', 'col'), pairs)  23.4 us
    ppermute x18, starting transfers between devices, meeting(): lax.ppermute(shard, axis, pairs)  19 us
    ppermute x18, waiting for transfers between devices, meeting(): lax.ppermute(shard, axis, pairs)  12.1 us
  transfers between devices with their start and end apart: 61, of which 29 were waited for; matrix products, arithmetic and copies ran while one was open for 0% of the time, Pallas kernels for 11%

profile of v11, /device:TPU:0, one launch (start us, length us, event | category | flops | bytes accessed | tf_op | source)
XLA Modules:
  0.0 126.2 jit_solution(6620367779234673965)
XLA Ops:
  0.0 1.8 %select.1 = (f32[1024,256]{1,0:T(8,128)S(1)}, bf16[1024,256]{1,0:T(8,128)(2,1)S(1)}, bf16[512,1024]{1,0:T(8,128)(2,1)S(1)}, s32[4,128]{1,0:T(4,128)S(1)}, bf16[3...) custom-call(f32[1024,256]{1,0:T(8,128)} %bitcast.11, ...), custom_call_target="tpu_custom_call" | custom-call | flops 268435456 | bytes 1148944 | tf_op jit(solution)/shard_map/select/pallas_call | solution.py:28
  1.8 3.0 %collective-permute-start = (bf16[128,256]{1,0:T(8,128)(2,1)S(1)}, bf16[128,256]{1,0:T(8,128)(2,1)S(1)}, u32[]{:S(2)}, u32[]{:S(2)}) collective-permute-start(bf16[128,256]{1,0:T(8,128)(2,1)S(1)} %get-tuple-element.95), channel_id=1, source_target_pairs={{0,4},{1,5},{2,6},{3,7},{4,0},{5,1},{6,2},{7,3},{8,12},{9,13},{10,... | collective-permute-start | bytes 196616 | tf_op jit(solution)/shard_map/ppermute | solution.py:304
  5.4 2.5 %collective-permute-start.3 = (bf16[128,256]{1,0:T(8,128)(2,1)S(1)}, bf16[128,256]{1,0:T(8,128)(2,1)S(1)}, u32[]{:S(2)}, u32[]{:S(2)}) collective-permute-start(bf16[128,256]{1,0:T(8,128)(2,1)S(1)} %get-tuple-element.98), channel_id=1, source_target_pairs={{0,4},{1,2},{2,1},{3,7},{4,0},{5,6},{6,5},{7,3},{8,12},{9,10},{10,... | collective-permute-start | bytes 196616 | tf_op jit(solution)/shard_map/ppermute | solution.py:304
  8.0 2.2 %collective-permute-done.3.g3 = bf16[128,256]{1,0:T(8,128)(2,1)S(1)} collective-permute-done((bf16[128,256]{1,0:T(8,128)(2,1)S(1)}, bf16[128,256]{1,0:T(8,128)(2,1)S(1)}, u32[]{:S(2)}, u32[]{:S(2)}) %collective-permute-start.3) | collective-permute-done | bytes 65568 | tf_op jit(solution)/shard_map/ppermute | solution.py:304
  11.1 1.1 collective-permute-start.4
  12.3 1.3 %collective-permute-done.6.refs_3_ = bf16[32,256]{1,0:T(8,128)(2,1)S(1)} collective-permute-done((bf16[32,256]{1,0:T(8,128)(2,1)S(1)}, bf16[32,256]{1,0:T(8,128)(2,1)S(1)}, u32[]{:S(2)}, u32[]{:S(2)}) %collective-permute-start.6) | collective-permute-done | bytes 16416 | tf_op jit(solution)/shard_map/ppermute | solution.py:175
  13.6 1.3 %collective-permute-done.5.refs_2_ = bf16[32,256]{1,0:T(8,128)(2,1)S(1)} collective-permute-done((bf16[32,256]{1,0:T(8,128)(2,1)S(1)}, bf16[32,256]{1,0:T(8,128)(2,1)S(1)}, u32[]{:S(2)}, u32[]{:S(2)}) %collective-permute-start.5) | collective-permute-done | bytes 16416 | tf_op jit(solution)/shard_map/ppermute | solution.py:175
  15.1 3.1 %collective-permute-start.7 = (bf16[64,256]{1,0:T(8,128)(2,1)S(1)}, bf16[64,256]{1,0:T(8,128)(2,1)S(1)}, u32[]{:S(2)}, u32[]{:S(2)}) collective-permute-start(bf16[64,256]{1,0:T(8,128)(2,1)S(1)} %get-tuple-element.101), channel_id=1, source_target_pairs={{0,24},{4,28},{8,16},{12,20},{16,8},{20,12},{24,0},{28,4},{1,25},{... | collective-permute-start | bytes 98312 | tf_op jit(solution)/shard_map/ppermute | solution.py:175
  19.5 3.5 %inverse_own.3 = (bf16[1536,1536]{1,0:T(8,128)(2,1)S(1)}, f32[1536,256]{1,0:T(8,128)S(1)}) custom-call(bf16[1536,1536]{1,0:T(8,128)(2,1)} %bitcast.9, bf16[1024,256]{1,0:T(8,128)(2,1)S(1)} %get-tuple-element.92.owned), custom_call_target="tpu_custom_call" | custom-call | flops 805306368 | bytes 5242880 | tf_op jit(solution)/shard_map/inverse_own/pallas_call | solution.py:28
  23.2 2.0 %collective-permute-start.10 = (bf16[32,256]{1,0:T(8,128)(2,1)S(1)}, bf16[32,256]{1,0:T(8,128)(2,1)S(1)}, u32[]{:S(2)}, u32[]{:S(2)}) collective-permute-start(bf16[32,256]{1,0:T(8,128)(2,1)S(1)} %get-tuple-element.106), channel_id=1, source_target_pairs={{0,4},{1,5},{2,6},{3,7},{4,0},{5,1},{6,2},{7,3},{8,12},{9,13},{10,... | collective-permute-start | bytes 49160 | tf_op jit(solution)/shard_map/ppermute | solution.py:304
  25.7 1.3 %collective-permute-done.10.theirs = bf16[32,256]{1,0:T(8,128)(2,1)S(1)} collective-permute-done((bf16[32,256]{1,0:T(8,128)(2,1)S(1)}, bf16[32,256]{1,0:T(8,128)(2,1)S(1)}, u32[]{:S(2)}, u32[]{:S(2)}) %collective-permute-start.10) | collective-permute-done | bytes 16416 | tf_op jit(solution)/shard_map/ppermute | solution.py:304
  27.2 2.0 %collective-permute-start.11 = (bf16[128,256]{1,0:T(8,128)(2,1)S(1)}, bf16[128,256]{1,0:T(8,128)(2,1)S(1)}, u32[]{:S(2)}, u32[]{:S(2)}) collective-permute-start(bf16[128,256]{1,0:T(8,128)(2,1)S(1)} %get-tuple-element.116), channel_id=1, source_target_pairs={{0,4},{1,5},{2,6},{3,7},{4,0},{5,1},{6,2},{7,3},{8,12},{9,13},{10,... | collective-permute-start | bytes 196616 | tf_op jit(solution)/shard_map/ppermute | solution.py:304
  29.7 1.6 %collective-permute-start.14 = (bf16[128,256]{1,0:T(8,128)(2,1)S(1)}, bf16[128,256]{1,0:T(8,128)(2,1)S(1)}, u32[]{:S(2)}, u32[]{:S(2)}) collective-permute-start(bf16[128,256]{1,0:T(8,128)(2,1)S(1)} %get-tuple-element.120), channel_id=1, source_target_pairs={{0,4},{1,2},{2,1},{3,7},{4,0},{5,6},{6,5},{7,3},{8,12},{9,10},{10,... | collective-permute-start | bytes 196616 | tf_op jit(solution)/shard_map/ppermute | solution.py:304
  31.3 2.6 %spread.1 = (bf16[1024,512]{1,0:T(8,128)(2,1)S(1)}, bf16[1536,1536]{1,0:T(8,128)(2,1)S(1)}) custom-call(bf16[1536,1536]{1,0:T(8,128)(2,1)} %bitcast.10, s32[4,128]{1,0:T(4,128)S(1)} %get-tuple-element.114.masked), custom_call_target="tpu_custom_call" | custom-call | bytes 4720640 | tf_op jit(solution)/shard_map/spread/pallas_call | solution.py:28
  35.3 1.2 collective-permute-start.15
  37.0 2.5 %collective-permute-start.18 = (bf16[128,256]{1,0:T(8,128)(2,1)S(1)}, bf16[128,256]{1,0:T(8,128)(2,1)S(1)}, u32[]{:S(2)}, u32[]{:S(2)}) collective-permute-start(bf16[128,256]{1,0:T(8,128)(2,1)S(1)} %get-tuple-element.128), channel_id=1, source_target_pairs={{0,4},{1,2},{2,1},{3,7},{4,0},{5,6},{6,5},{7,3},{8,12},{9,10},{10,... | collective-permute-start | bytes 196616 | tf_op jit(solution)/shard_map/ppermute | solution.py:304
  40.6 1.2 collective-permute-done.18.g3
  42.1 2.1 %collective-permute-start.19 = (bf16[128,256]{1,0:T(8,128)(2,1)S(1)}, bf16[128,256]{1,0:T(8,128)(2,1)S(1)}, u32[]{:S(2)}, u32[]{:S(2)}) collective-permute-start(bf16[128,256]{1,0:T(8,128)(2,1)S(1)} %get-tuple-element.129), channel_id=1, source_target_pairs={{0,4},{1,5},{2,6},{3,7},{4,0},{5,1},{6,2},{7,3},{8,12},{9,13},{10,... | collective-permute-start | bytes 196616 | tf_op jit(solution)/shard_map/ppermute | solution.py:304
  44.7 1.9 %collective-permute-start.22 = (bf16[128,256]{1,0:T(8,128)(2,1)S(1)}, bf16[128,256]{1,0:T(8,128)(2,1)S(1)}, u32[]{:S(2)}, u32[]{:S(2)}) collective-permute-start(bf16[128,256]{1,0:T(8,128)(2,1)S(1)} %get-tuple-element.132), channel_id=1, source_target_pairs={{0,4},{1,2},{2,1},{3,7},{4,0},{5,6},{6,5},{7,3},{8,12},{9,10},{10,... | collective-permute-start | bytes 196616 | tf_op jit(solution)/shard_map/ppermute | solution.py:304
  49.8 2.0 %collective-permute-start.23 = (bf16[128,256]{1,0:T(8,128)(2,1)S(1)}, bf16[128,256]{1,0:T(8,128)(2,1)S(1)}, u32[]{:S(2)}, u32[]{:S(2)}) collective-permute-start(bf16[128,256]{1,0:T(8,128)(2,1)S(1)} %get-tuple-element.134), channel_id=1, source_target_pairs={{0,4},{1,5},{2,6},{3,7},{4,0},{5,1},{6,2},{7,3},{8,12},{9,13},{10,... | collective-permute-start | bytes 196616 | tf_op jit(solution)/shard_map/ppermute | solution.py:304
  52.4 2.2 %collective-permute-start.26 = (bf16[128,256]{1,0:T(8,128)(2,1)S(1)}, bf16[128,256]{1,0:T(8,128)(2,1)S(1)}, u32[]{:S(2)}, u32[]{:S(2)}) collective-permute-start(bf16[128,256]{1,0:T(8,128)(2,1)S(1)} %get-tuple-element.137), channel_id=1, source_target_pairs={{0,4},{1,2},{2,1},{3,7},{4,0},{5,6},{6,5},{7,3},{8,12},{9,10},{10,... | collective-permute-start | bytes 196616 | tf_op jit(solution)/shard_map/ppermute | solution.py:304
  55.1 1.7 %collective-permute-done.26.g3 = bf16[128,256]{1,0:T(8,128)(2,1)S(1)} collective-permute-done((bf16[128,256]{1,0:T(8,128)(2,1)S(1)}, bf16[128,256]{1,0:T(8,128)(2,1)S(1)}, u32[]{:S(2)}, u32[]{:S(2)}) %collective-permute-start.26) | collective-permute-done | bytes 65568 | tf_op jit(solution)/shard_map/ppermute | solution.py:304
  57.0 1.2 collective-permute-start.28
  58.9 1.3 %collective-permute-done.29.refs_3_ = bf16[32,256]{1,0:T(8,128)(2,1)S(1)} collective-permute-done((bf16[32,256]{1,0:T(8,128)(2,1)S(1)}, bf16[32,256]{1,0:T(8,128)(2,1)S(1)}, u32[]{:S(2)}, u32[]{:S(2)}) %collective-permute-start.29) | collective-permute-done | bytes 16416 | tf_op jit(solution)/shard_map/ppermute | solution.py:175
  61.0 3.1 %collective-permute-start.30 = (bf16[64,256]{1,0:T(8,128)(2,1)S(1)}, bf16[64,256]{1,0:T(8,128)(2,1)S(1)}, u32[]{:S(2)}, u32[]{:S(2)}) collective-permute-start(bf16[64,256]{1,0:T(8,128)(2,1)S(1)} %get-tuple-element.139), channel_id=1, source_target_pairs={{0,24},{4,28},{8,16},{12,20},{16,8},{20,12},{24,0},{28,4},{1,25},{... | collective-permute-start | bytes 98312 | tf_op jit(solution)/shard_map/ppermute | solution.py:175
  64.3 1.2 collective-permute-start.32
  67.2 1.9 %collective-permute-done.31.refs_1_ = bf16[64,256]{1,0:T(8,128)(2,1)S(1)} collective-permute-done((bf16[64,256]{1,0:T(8,128)(2,1)S(1)}, bf16[64,256]{1,0:T(8,128)(2,1)S(1)}, u32[]{:S(2)}, u32[]{:S(2)}) %collective-permute-start.31) | collective-permute-done | bytes 32800 | tf_op jit(solution)/shard_map/ppermute | solution.py:175
  70.6 2.4 %collective-permute-done.33.theirs = bf16[32,256]{1,0:T(8,128)(2,1)S(1)} collective-permute-done((bf16[32,256]{1,0:T(8,128)(2,1)S(1)}, bf16[32,256]{1,0:T(8,128)(2,1)S(1)}, u32[]{:S(2)}, u32[]{:S(2)}) %collective-permute-start.33) | collective-permute-done | bytes 16416 | tf_op jit(solution)/shard_map/ppermute | solution.py:304
  74.7 2.3 %collective-permute-start.37 = (bf16[128,256]{1,0:T(8,128)(2,1)S(1)}, bf16[128,256]{1,0:T(8,128)(2,1)S(1)}, u32[]{:S(2)}, u32[]{:S(2)}) collective-permute-start(bf16[128,256]{1,0:T(8,128)(2,1)S(1)} %get-tuple-element.150), channel_id=1, source_target_pairs={{0,4},{1,2},{2,1},{3,7},{4,0},{5,6},{6,5},{7,3},{8,12},{9,10},{10,... | collective-permute-start | bytes 196616 | tf_op jit(solution)/shard_map/ppermute | solution.py:304
  78.0 1.3 %collective-permute-done.37.r3 = bf16[128,256]{1,0:T(8,128)(2,1)S(1)} collective-permute-done((bf16[128,256]{1,0:T(8,128)(2,1)S(1)}, bf16[128,256]{1,0:T(8,128)(2,1)S(1)}, u32[]{:S(2)}, u32[]{:S(2)}) %collective-permute-start.37) | collective-permute-done | bytes 65568 | tf_op jit(solution)/shard_map/ppermute | solution.py:304
  80.1 2.1 %collective-permute-start.38 = (bf16[128,256]{1,0:T(8,128)(2,1)S(1)}, bf16[128,256]{1,0:T(8,128)(2,1)S(1)}, u32[]{:S(2)}, u32[]{:S(2)}) collective-permute-start(bf16[128,256]{1,0:T(8,128)(2,1)S(1)} %get-tuple-element.153), channel_id=1, source_target_pairs={{0,4},{1,5},{2,6},{3,7},{4,0},{5,1},{6,2},{7,3},{8,12},{9,13},{10,... | collective-permute-start | bytes 196616 | tf_op jit(solution)/shard_map/ppermute | solution.py:304
  82.7 1.2 collective-permute-start.41
  83.9 1.2 operator_own.3.partial
  85.5 1.5 %collective-permute-done.41.g3 = bf16[128,256]{1,0:T(8,128)(2,1)S(1)} collective-permute-done((bf16[128,256]{1,0:T(8,128)(2,1)S(1)}, bf16[128,256]{1,0:T(8,128)(2,1)S(1)}, u32[]{:S(2)}, u32[]{:S(2)}) %collective-permute-start.41) | collective-permute-done | bytes 65568 | tf_op jit(solution)/shard_map/ppermute | solution.py:304
  87.3 1.7 %collective-permute-start.42 = (bf16[128,256]{1,0:T(8,128)(2,1)S(1)}, bf16[128,256]{1,0:T(8,128)(2,1)S(1)}, u32[]{:S(2)}, u32[]{:S(2)}) collective-permute-start(bf16[128,256]{1,0:T(8,128)(2,1)S(1)} %get-tuple-element.157), channel_id=1, source_target_pairs={{0,4},{1,5},{2,6},{3,7},{4,0},{5,1},{6,2},{7,3},{8,12},{9,13},{10,... | collective-permute-start | bytes 196616 | tf_op jit(solution)/shard_map/ppermute | solution.py:304
  89.5 2.6 %collective-permute-start.45 = (bf16[128,256]{1,0:T(8,128)(2,1)S(1)}, bf16[128,256]{1,0:T(8,128)(2,1)S(1)}, u32[]{:S(2)}, u32[]{:S(2)}) collective-permute-start(bf16[128,256]{1,0:T(8,128)(2,1)S(1)} %get-tuple-element.160), channel_id=1, source_target_pairs={{0,4},{1,2},{2,1},{3,7},{4,0},{5,6},{6,5},{7,3},{8,12},{9,10},{10,... | collective-permute-start | bytes 196616 | tf_op jit(solution)/shard_map/ppermute | solution.py:304
  92.7 1.6 %collective-permute-done.45.r3 = bf16[128,256]{1,0:T(8,128)(2,1)S(1)} collective-permute-done((bf16[128,256]{1,0:T(8,128)(2,1)S(1)}, bf16[128,256]{1,0:T(8,128)(2,1)S(1)}, u32[]{:S(2)}, u32[]{:S(2)}) %collective-permute-start.45) | collective-permute-done | bytes 65568 | tf_op jit(solution)/shard_map/ppermute | solution.py:304
  95.2 2.1 %collective-permute-start.46 = (bf16[128,256]{1,0:T(8,128)(2,1)S(1)}, bf16[128,256]{1,0:T(8,128)(2,1)S(1)}, u32[]{:S(2)}, u32[]{:S(2)}) collective-permute-start(bf16[128,256]{1,0:T(8,128)(2,1)S(1)} %get-tuple-element.162), channel_id=1, source_target_pairs={{0,4},{1,5},{2,6},{3,7},{4,0},{5,1},{6,2},{7,3},{8,12},{9,13},{10,... | collective-permute-start | bytes 196616 | tf_op jit(solution)/shard_map/ppermute | solution.py:304
  97.8 1.6 %collective-permute-start.49 = (bf16[128,256]{1,0:T(8,128)(2,1)S(1)}, bf16[128,256]{1,0:T(8,128)(2,1)S(1)}, u32[]{:S(2)}, u32[]{:S(2)}) collective-permute-start(bf16[128,256]{1,0:T(8,128)(2,1)S(1)} %get-tuple-element.165), channel_id=1, source_target_pairs={{0,4},{1,2},{2,1},{3,7},{4,0},{5,6},{6,5},{7,3},{8,12},{9,10},{10,... | collective-permute-start | bytes 196616 | tf_op jit(solution)/shard_map/ppermute | solution.py:304
  99.4 1.1 collective-permute-done.46.g0
  100.5 1.5 %collective-permute-done.49.g3 = bf16[128,256]{1,0:T(8,128)(2,1)S(1)} collective-permute-done((bf16[128,256]{1,0:T(8,128)(2,1)S(1)}, bf16[128,256]{1,0:T(8,128)(2,1)S(1)}, u32[]{:S(2)}, u32[]{:S(2)}) %collective-permute-start.49) | collective-permute-done | bytes 65568 | tf_op jit(solution)/shard_map/ppermute | solution.py:304
  102.6 1.1 collective-permute-start.51
  104.2 1.4 %collective-permute-done.52.refs_3_ = bf16[32,256]{1,0:T(8,128)(2,1)S(1)} collective-permute-done((bf16[32,256]{1,0:T(8,128)(2,1)S(1)}, bf16[32,256]{1,0:T(8,128)(2,1)S(1)}, u32[]{:S(2)}, u32[]{:S(2)}) %collective-permute-start.52) | collective-permute-done | bytes 16416 | tf_op jit(solution)/shard_map/ppermute | solution.py:175
  106.5 3.0 %collective-permute-start.53 = (bf16[64,256]{1,0:T(8,128)(2,1)S(1)}, bf16[64,256]{1,0:T(8,128)(2,1)S(1)}, u32[]{:S(2)}, u32[]{:S(2)}) collective-permute-start(bf16[64,256]{1,0:T(8,128)(2,1)S(1)} %get-tuple-element.167), channel_id=1, source_target_pairs={{0,24},{4,28},{8,16},{12,20},{16,8},{20,12},{24,0},{28,4},{1,25},{... | collective-permute-start | bytes 98312 | tf_op jit(solution)/shard_map/ppermute | solution.py:175
  112.7 2.0 %collective-permute-done.54.refs_1_ = bf16[64,256]{1,0:T(8,128)(2,1)S(1)} collective-permute-done((bf16[64,256]{1,0:T(8,128)(2,1)S(1)}, bf16[64,256]{1,0:T(8,128)(2,1)S(1)}, u32[]{:S(2)}, u32[]{:S(2)}) %collective-permute-start.54) | collective-permute-done | bytes 32800 | tf_op jit(solution)/shard_map/ppermute | solution.py:175
  116.2 2.5 %collective-permute-done.56.theirs = bf16[32,256]{1,0:T(8,128)(2,1)S(1)} collective-permute-done((bf16[32,256]{1,0:T(8,128)(2,1)S(1)}, bf16[32,256]{1,0:T(8,128)(2,1)S(1)}, u32[]{:S(2)}, u32[]{:S(2)}) %collective-permute-start.56) | collective-permute-done | bytes 16416 | tf_op jit(solution)/shard_map/ppermute | solution.py:304
  120.3 2.3 %collective-permute-start.60 = (bf16[128,256]{1,0:T(8,128)(2,1)S(1)}, bf16[128,256]{1,0:T(8,128)(2,1)S(1)}, u32[]{:S(2)}, u32[]{:S(2)}) collective-permute-start(bf16[128,256]{1,0:T(8,128)(2,1)S(1)} %get-tuple-element.178), channel_id=1, source_target_pairs={{0,4},{1,2},{2,1},{3,7},{4,0},{5,6},{6,5},{7,3},{8,12},{9,10},{10,... | collective-permute-start | bytes 196616 | tf_op jit(solution)/shard_map/ppermute | solution.py:304
  124.8 1.2 last_update.1
  (110 shorter events, 34.9 us)
Async XLA Ops:
  1.8 6.1 %collective-permute-start = (bf16[128,256]{1,0:T(8,128)(2,1)S(1)}, bf16[128,256]{1,0:T(8,128)(2,1)S(1)}, u32[]{:S(2)}, u32[]{:S(2)}) collective-permute-start(bf16[128,256]{1,0:T(8,128)(2,1)S(1)} %get-tuple-element.95), channel_id=1, source_target_pairs={{0,4},{1,5},{2,6},{3,7},{4,0},{5,1},{6,2},{7,3},{8,12},{9,13},{10,... | collective-permute-start | bytes 196616 | tf_op jit(solution)/shard_map/ppermute | solution.py:304
  5.4 4.8 %collective-permute-start.3 = (bf16[128,256]{1,0:T(8,128)(2,1)S(1)}, bf16[128,256]{1,0:T(8,128)(2,1)S(1)}, u32[]{:S(2)}, u32[]{:S(2)}) collective-permute-start(bf16[128,256]{1,0:T(8,128)(2,1)S(1)} %get-tuple-element.98), channel_id=1, source_target_pairs={{0,4},{1,2},{2,1},{3,7},{4,0},{5,6},{6,5},{7,3},{8,12},{9,10},{10,... | collective-permute-start | bytes 196616 | tf_op jit(solution)/shard_map/ppermute | solution.py:304
  11.1 3.7 %collective-permute-start.5 = (bf16[32,256]{1,0:T(8,128)(2,1)S(1)}, bf16[32,256]{1,0:T(8,128)(2,1)S(1)}, u32[]{:S(2)}, u32[]{:S(2)}) collective-permute-start(bf16[32,256]{1,0:T(8,128)(2,1)S(1)} %restrict.3.refs_0_), channel_id=1, source_target_pairs={{0,2},{1,3},{2,0},{3,1},{4,6},{5,7},{6,4},{7,5},{8,10},{9,11},{10,... | collective-permute-start | bytes 49160 | tf_op jit(solution)/shard_map/ppermute | solution.py:175
  11.1 3.7 %collective-permute-start.4 = (bf16[32,256]{1,0:T(8,128)(2,1)S(1)}, bf16[32,256]{1,0:T(8,128)(2,1)S(1)}, u32[]{:S(2)}, u32[]{:S(2)}) collective-permute-start(bf16[32,256]{1,0:T(8,128)(2,1)S(1)} %restrict.3.refs_0_), channel_id=1, source_target_pairs={{0,1},{1,0},{2,3},{3,2},{4,5},{5,4},{6,7},{7,6},{8,9},{9,8},{10,11... | collective-permute-start | bytes 49160 | tf_op jit(solution)/shard_map/ppermute | solution.py:175
  15.1 8.0 %collective-permute-start.7 = (bf16[64,256]{1,0:T(8,128)(2,1)S(1)}, bf16[64,256]{1,0:T(8,128)(2,1)S(1)}, u32[]{:S(2)}, u32[]{:S(2)}) collective-permute-start(bf16[64,256]{1,0:T(8,128)(2,1)S(1)} %get-tuple-element.101), channel_id=1, source_target_pairs={{0,24},{4,28},{8,16},{12,20},{16,8},{20,12},{24,0},{28,4},{1,25},{... | collective-permute-start | bytes 98312 | tf_op jit(solution)/shard_map/ppermute | solution.py:175
  18.2 4.9 %collective-permute-start.8 = (bf16[64,256]{1,0:T(8,128)(2,1)S(1)}, bf16[64,256]{1,0:T(8,128)(2,1)S(1)}, u32[]{:S(2)}, u32[]{:S(2)}) collective-permute-start(bf16[64,256]{1,0:T(8,128)(2,1)S(1)} %get-tuple-element.102), channel_id=1, source_target_pairs={{0,16},{4,20},{8,24},{12,28},{16,0},{20,4},{24,8},{28,12},{1,17},{... | collective-permute-start | bytes 98312 | tf_op jit(solution)/shard_map/ppermute | solution.py:175
  18.9 4.3 %collective-permute-start.9 = (bf16[64,256]{1,0:T(8,128)(2,1)S(1)}, bf16[64,256]{1,0:T(8,128)(2,1)S(1)}, u32[]{:S(2)}, u32[]{:S(2)}) collective-permute-start(bf16[64,256]{1,0:T(8,128)(2,1)S(1)} %get-tuple-element.103), channel_id=1, source_target_pairs={{0,8},{4,12},{8,0},{12,4},{16,24},{20,28},{24,16},{28,20},{1,9},{5... | collective-permute-start | bytes 98312 | tf_op jit(solution)/shard_map/ppermute | solution.py:175
  23.2 3.8 %collective-permute-start.10 = (bf16[32,256]{1,0:T(8,128)(2,1)S(1)}, bf16[32,256]{1,0:T(8,128)(2,1)S(1)}, u32[]{:S(2)}, u32[]{:S(2)}) collective-permute-start(bf16[32,256]{1,0:T(8,128)(2,1)S(1)} %get-tuple-element.106), channel_id=1, source_target_pairs={{0,4},{1,5},{2,6},{3,7},{4,0},{5,1},{6,2},{7,3},{8,12},{9,13},{10,... | collective-permute-start | bytes 49160 | tf_op jit(solution)/shard_map/ppermute | solution.py:304
  27.2 6.7 %collective-permute-start.11 = (bf16[128,256]{1,0:T(8,128)(2,1)S(1)}, bf16[128,256]{1,0:T(8,128)(2,1)S(1)}, u32[]{:S(2)}, u32[]{:S(2)}) collective-permute-start(bf16[128,256]{1,0:T(8,128)(2,1)S(1)} %get-tuple-element.116), channel_id=1, source_target_pairs={{0,4},{1,5},{2,6},{3,7},{4,0},{5,1},{6,2},{7,3},{8,12},{9,13},{10,... | collective-permute-start | bytes 196616 | tf_op jit(solution)/shard_map/ppermute | solution.py:304
  29.2 4.7 %collective-permute-start.12 = (bf16[128,256]{1,0:T(8,128)(2,1)S(1)}, bf16[128,256]{1,0:T(8,128)(2,1)S(1)}, u32[]{:S(2)}, u32[]{:S(2)}) collective-permute-start(bf16[128,256]{1,0:T(8,128)(2,1)S(1)} %get-tuple-element.117), channel_id=1, source_target_pairs={{0,1},{1,0},{2,3},{3,2},{4,8},{5,9},{6,10},{7,11},{8,4},{9,5},{10,... | collective-permute-start | bytes 196616 | tf_op jit(solution)/shard_map/ppermute | solution.py:304
  29.2 5.2 %collective-permute-start.13 = (bf16[128,256]{1,0:T(8,128)(2,1)S(1)}, bf16[128,256]{1,0:T(8,128)(2,1)S(1)}, u32[]{:S(2)}, u32[]{:S(2)}) collective-permute-start(bf16[128,256]{1,0:T(8,128)(2,1)S(1)} %get-tuple-element.119), channel_id=1, source_target_pairs={{0,1},{1,0},{2,3},{3,2},{4,5},{5,4},{6,7},{7,6},{8,9},{9,8},{10,11... | collective-permute-start | bytes 196616 | tf_op jit(solution)/shard_map/ppermute | solution.py:304
  29.7 4.7 %collective-permute-start.14 = (bf16[128,256]{1,0:T(8,128)(2,1)S(1)}, bf16[128,256]{1,0:T(8,128)(2,1)S(1)}, u32[]{:S(2)}, u32[]{:S(2)}) collective-permute-start(bf16[128,256]{1,0:T(8,128)(2,1)S(1)} %get-tuple-element.120), channel_id=1, source_target_pairs={{0,4},{1,2},{2,1},{3,7},{4,0},{5,6},{6,5},{7,3},{8,12},{9,10},{10,... | collective-permute-start | bytes 196616 | tf_op jit(solution)/shard_map/ppermute | solution.py:304
  35.3 5.3 %collective-permute-start.15 = (bf16[128,256]{1,0:T(8,128)(2,1)S(1)}, bf16[128,256]{1,0:T(8,128)(2,1)S(1)}, u32[]{:S(2)}, u32[]{:S(2)}) collective-permute-start(bf16[128,256]{1,0:T(8,128)(2,1)S(1)} %get-tuple-element.125), channel_id=1, source_target_pairs={{0,4},{1,5},{2,6},{3,7},{4,0},{5,1},{6,2},{7,3},{8,12},{9,13},{10,... | collective-permute-start | bytes 196616 | tf_op jit(solution)/shard_map/ppermute | solution.py:304
  36.5 4.0 %collective-permute-start.16 = (bf16[128,256]{1,0:T(8,128)(2,1)S(1)}, bf16[128,256]{1,0:T(8,128)(2,1)S(1)}, u32[]{:S(2)}, u32[]{:S(2)}) collective-permute-start(bf16[128,256]{1,0:T(8,128)(2,1)S(1)} %get-tuple-element.126), channel_id=1, source_target_pairs={{0,1},{1,0},{2,3},{3,2},{4,8},{5,9},{6,10},{7,11},{8,4},{9,5},{10,... | collective-permute-start | bytes 196616 | tf_op jit(solution)/shard_map/ppermute | solution.py:304
  36.5 4.0 %collective-permute-start.17 = (bf16[128,256]{1,0:T(8,128)(2,1)S(1)}, bf16[128,256]{1,0:T(8,128)(2,1)S(1)}, u32[]{:S(2)}, u32[]{:S(2)}) collective-permute-start(bf16[128,256]{1,0:T(8,128)(2,1)S(1)} %get-tuple-element.127), channel_id=1, source_target_pairs={{0,1},{1,0},{2,3},{3,2},{4,5},{5,4},{6,7},{7,6},{8,9},{9,8},{10,11... | collective-permute-start | bytes 196616 | tf_op jit(solution)/shard_map/ppermute | solution.py:304
  37.0 4.8 %collective-permute-start.18 = (bf16[128,256]{1,0:T(8,128)(2,1)S(1)}, bf16[128,256]{1,0:T(8,128)(2,1)S(1)}, u32[]{:S(2)}, u32[]{:S(2)}) collective-permute-start(bf16[128,256]{1,0:T(8,128)(2,1)S(1)} %get-tuple-element.128), channel_id=1, source_target_pairs={{0,4},{1,2},{2,1},{3,7},{4,0},{5,6},{6,5},{7,3},{8,12},{9,10},{10,... | collective-permute-start | bytes 196616 | tf_op jit(solution)/shard_map/ppermute | solution.py:304
  42.1 5.3 %collective-permute-start.19 = (bf16[128,256]{1,0:T(8,128)(2,1)S(1)}, bf16[128,256]{1,0:T(8,128)(2,1)S(1)}, u32[]{:S(2)}, u32[]{:S(2)}) collective-permute-start(bf16[128,256]{1,0:T(8,128)(2,1)S(1)} %get-tuple-element.129), channel_id=1, source_target_pairs={{0,4},{1,5},{2,6},{3,7},{4,0},{5,1},{6,2},{7,3},{8,12},{9,13},{10,... | collective-permute-start | bytes 196616 | tf_op jit(solution)/shard_map/ppermute | solution.py:304
  44.2 3.2 %collective-permute-start.20 = (bf16[128,256]{1,0:T(8,128)(2,1)S(1)}, bf16[128,256]{1,0:T(8,128)(2,1)S(1)}, u32[]{:S(2)}, u32[]{:S(2)}) collective-permute-start(bf16[128,256]{1,0:T(8,128)(2,1)S(1)} %get-tuple-element.130), channel_id=1, source_target_pairs={{0,1},{1,0},{2,3},{3,2},{4,8},{5,9},{6,10},{7,11},{8,4},{9,5},{10,... | collective-permute-start | bytes 196616 | tf_op jit(solution)/shard_map/ppermute | solution.py:304
  44.2 3.8 %collective-permute-start.21 = (bf16[128,256]{1,0:T(8,128)(2,1)S(1)}, bf16[128,256]{1,0:T(8,128)(2,1)S(1)}, u32[]{:S(2)}, u32[]{:S(2)}) collective-permute-start(bf16[128,256]{1,0:T(8,128)(2,1)S(1)} %get-tuple-element.131), channel_id=1, source_target_pairs={{0,1},{1,0},{2,3},{3,2},{4,5},{5,4},{6,7},{7,6},{8,9},{9,8},{10,11... | collective-permute-start | bytes 196616 | tf_op jit(solution)/shard_map/ppermute | solution.py:304
  44.7 4.3 %collective-permute-start.22 = (bf16[128,256]{1,0:T(8,128)(2,1)S(1)}, bf16[128,256]{1,0:T(8,128)(2,1)S(1)}, u32[]{:S(2)}, u32[]{:S(2)}) collective-permute-start(bf16[128,256]{1,0:T(8,128)(2,1)S(1)} %get-tuple-element.132), channel_id=1, source_target_pairs={{0,4},{1,2},{2,1},{3,7},{4,0},{5,6},{6,5},{7,3},{8,12},{9,10},{10,... | collective-permute-start | bytes 196616 | tf_op jit(solution)/shard_map/ppermute | solution.py:304
  49.8 5.2 %collective-permute-start.23 = (bf16[128,256]{1,0:T(8,128)(2,1)S(1)}, bf16[128,256]{1,0:T(8,128)(2,1)S(1)}, u32[]{:S(2)}, u32[]{:S(2)}) collective-permute-start(bf16[128,256]{1,0:T(8,128)(2,1)S(1)} %get-tuple-element.134), channel_id=1, source_target_pairs={{0,4},{1,5},{2,6},{3,7},{4,0},{5,1},{6,2},{7,3},{8,12},{9,13},{10,... | collective-permute-start | bytes 196616 | tf_op jit(solution)/shard_map/ppermute | solution.py:304
  52.4 4.4 %collective-permute-start.26 = (bf16[128,256]{1,0:T(8,128)(2,1)S(1)}, bf16[128,256]{1,0:T(8,128)(2,1)S(1)}, u32[]{:S(2)}, u32[]{:S(2)}) collective-permute-start(bf16[128,256]{1,0:T(8,128)(2,1)S(1)} %get-tuple-element.137), channel_id=1, source_target_pairs={{0,4},{1,2},{2,1},{3,7},{4,0},{5,6},{6,5},{7,3},{8,12},{9,10},{10,... | collective-permute-start | bytes 196616 | tf_op jit(solution)/shard_map/ppermute | solution.py:304
  57.0 3.8 %collective-permute-start.28 = (bf16[32,256]{1,0:T(8,128)(2,1)S(1)}, bf16[32,256]{1,0:T(8,128)(2,1)S(1)}, u32[]{:S(2)}, u32[]{:S(2)}) collective-permute-start(bf16[32,256]{1,0:T(8,128)(2,1)S(1)} %restrict.4.refs_0_), channel_id=1, source_target_pairs={{0,2},{1,3},{2,0},{3,1},{4,6},{5,7},{6,4},{7,5},{8,10},{9,11},{10,... | collective-permute-start | bytes 49160 | tf_op jit(solution)/shard_map/ppermute | solution.py:175
  61.0 6.1 %collective-permute-start.30 = (bf16[64,256]{1,0:T(8,128)(2,1)S(1)}, bf16[64,256]{1,0:T(8,128)(2,1)S(1)}, u32[]{:S(2)}, u32[]{:S(2)}) collective-permute-start(bf16[64,256]{1,0:T(8,128)(2,1)S(1)} %get-tuple-element.139), channel_id=1, source_target_pairs={{0,24},{4,28},{8,16},{12,20},{16,8},{20,12},{24,0},{28,4},{1,25},{... | collective-permute-start | bytes 98312 | tf_op jit(solution)/shard_map/ppermute | solution.py:175
  64.2 4.9 %collective-permute-start.31 = (bf16[64,256]{1,0:T(8,128)(2,1)S(1)}, bf16[64,256]{1,0:T(8,128)(2,1)S(1)}, u32[]{:S(2)}, u32[]{:S(2)}) collective-permute-start(bf16[64,256]{1,0:T(8,128)(2,1)S(1)} %get-tuple-element.140), channel_id=1, source_target_pairs={{0,16},{4,20},{8,24},{12,28},{16,0},{20,4},{24,8},{28,12},{1,17},{... | collective-permute-start | bytes 98312 | tf_op jit(solution)/shard_map/ppermute | solution.py:175
  64.3 4.8 %collective-permute-start.32 = (bf16[64,256]{1,0:T(8,128)(2,1)S(1)}, bf16[64,256]{1,0:T(8,128)(2,1)S(1)}, u32[]{:S(2)}, u32[]{:S(2)}) collective-permute-start(bf16[64,256]{1,0:T(8,128)(2,1)S(1)} %get-tuple-element.141), channel_id=1, source_target_pairs={{0,8},{4,12},{8,0},{12,4},{16,24},{20,28},{24,16},{28,20},{1,9},{5... | collective-permute-start | bytes 98312 | tf_op jit(solution)/shard_map/ppermute | solution.py:175
  69.1 3.8 %collective-permute-start.33 = (bf16[32,256]{1,0:T(8,128)(2,1)S(1)}, bf16[32,256]{1,0:T(8,128)(2,1)S(1)}, u32[]{:S(2)}, u32[]{:S(2)}) collective-permute-start(bf16[32,256]{1,0:T(8,128)(2,1)S(1)} %get-tuple-element.144), channel_id=1, source_target_pairs={{0,4},{1,5},{2,6},{3,7},{4,0},{5,1},{6,2},{7,3},{8,12},{9,13},{10,... | collective-permute-start | bytes 49160 | tf_op jit(solution)/shard_map/ppermute | solution.py:304
  73.2 4.3 %collective-permute-start.34 = (bf16[128,256]{1,0:T(8,128)(2,1)S(1)}, bf16[128,256]{1,0:T(8,128)(2,1)S(1)}, u32[]{:S(2)}, u32[]{:S(2)}) collective-permute-start(bf16[128,256]{1,0:T(8,128)(2,1)S(1)} %get-tuple-element.147), channel_id=1, source_target_pairs={{0,4},{1,5},{2,6},{3,7},{4,0},{5,1},{6,2},{7,3},{8,12},{9,13},{10,... | collective-permute-start | bytes 196616 | tf_op jit(solution)/shard_map/ppermute | solution.py:304
  74.2 3.3 %collective-permute-start.35 = (bf16[128,256]{1,0:T(8,128)(2,1)S(1)}, bf16[128,256]{1,0:T(8,128)(2,1)S(1)}, u32[]{:S(2)}, u32[]{:S(2)}) collective-permute-start(bf16[128,256]{1,0:T(8,128)(2,1)S(1)} %get-tuple-element.148), channel_id=1, source_target_pairs={{0,1},{1,0},{2,3},{3,2},{4,8},{5,9},{6,10},{7,11},{8,4},{9,5},{10,... | collective-permute-start | bytes 196616 | tf_op jit(solution)/shard_map/ppermute | solution.py:304
  74.2 3.8 %collective-permute-start.36 = (bf16[128,256]{1,0:T(8,128)(2,1)S(1)}, bf16[128,256]{1,0:T(8,128)(2,1)S(1)}, u32[]{:S(2)}, u32[]{:S(2)}) collective-permute-start(bf16[128,256]{1,0:T(8,128)(2,1)S(1)} %get-tuple-element.149), channel_id=1, source_target_pairs={{0,1},{1,0},{2,3},{3,2},{4,5},{5,4},{6,7},{7,6},{8,9},{9,8},{10,11... | collective-permute-start | bytes 196616 | tf_op jit(solution)/shard_map/ppermute | solution.py:304
  74.7 4.6 %collective-permute-start.37 = (bf16[128,256]{1,0:T(8,128)(2,1)S(1)}, bf16[128,256]{1,0:T(8,128)(2,1)S(1)}, u32[]{:S(2)}, u32[]{:S(2)}) collective-permute-start(bf16[128,256]{1,0:T(8,128)(2,1)S(1)} %get-tuple-element.150), channel_id=1, source_target_pairs={{0,4},{1,2},{2,1},{3,7},{4,0},{5,6},{6,5},{7,3},{8,12},{9,10},{10,... | collective-permute-start | bytes 196616 | tf_op jit(solution)/shard_map/ppermute | solution.py:304
  80.1 5.3 %collective-permute-start.38 = (bf16[128,256]{1,0:T(8,128)(2,1)S(1)}, bf16[128,256]{1,0:T(8,128)(2,1)S(1)}, u32[]{:S(2)}, u32[]{:S(2)}) collective-permute-start(bf16[128,256]{1,0:T(8,128)(2,1)S(1)} %get-tuple-element.153), channel_id=1, source_target_pairs={{0,4},{1,5},{2,6},{3,7},{4,0},{5,1},{6,2},{7,3},{8,12},{9,13},{10,... | collective-permute-start | bytes 196616 | tf_op jit(solution)/shard_map/ppermute | solution.py:304
  82.7 4.3 %collective-permute-start.41 = (bf16[128,256]{1,0:T(8,128)(2,1)S(1)}, bf16[128,256]{1,0:T(8,128)(2,1)S(1)}, u32[]{:S(2)}, u32[]{:S(2)}) collective-permute-start(bf16[128,256]{1,0:T(8,128)(2,1)S(1)} %get-tuple-element.156), channel_id=1, source_target_pairs={{0,4},{1,2},{2,1},{3,7},{4,0},{5,6},{6,5},{7,3},{8,12},{9,10},{10,... | collective-permute-start | bytes 196616 | tf_op jit(solution)/shard_map/ppermute | solution.py:304
  87.3 4.8 %collective-permute-start.42 = (bf16[128,256]{1,0:T(8,128)(2,1)S(1)}, bf16[128,256]{1,0:T(8,128)(2,1)S(1)}, u32[]{:S(2)}, u32[]{:S(2)}) collective-permute-start(bf16[128,256]{1,0:T(8,128)(2,1)S(1)} %get-tuple-element.157), channel_id=1, source_target_pairs={{0,4},{1,5},{2,6},{3,7},{4,0},{5,1},{6,2},{7,3},{8,12},{9,13},{10,... | collective-permute-start | bytes 196616 | tf_op jit(solution)/shard_map/ppermute | solution.py:304
  89.0 3.7 %collective-permute-start.44 = (bf16[128,256]{1,0:T(8,128)(2,1)S(1)}, bf16[128,256]{1,0:T(8,128)(2,1)S(1)}, u32[]{:S(2)}, u32[]{:S(2)}) collective-permute-start(bf16[128,256]{1,0:T(8,128)(2,1)S(1)} %get-tuple-element.159), channel_id=1, source_target_pairs={{0,1},{1,0},{2,3},{3,2},{4,5},{5,4},{6,7},{7,6},{8,9},{9,8},{10,11... | collective-permute-start | bytes 196616 | tf_op jit(solution)/shard_map/ppermute | solution.py:304
  89.5 4.9 %collective-permute-start.45 = (bf16[128,256]{1,0:T(8,128)(2,1)S(1)}, bf16[128,256]{1,0:T(8,128)(2,1)S(1)}, u32[]{:S(2)}, u32[]{:S(2)}) collective-permute-start(bf16[128,256]{1,0:T(8,128)(2,1)S(1)} %get-tuple-element.160), channel_id=1, source_target_pairs={{0,4},{1,2},{2,1},{3,7},{4,0},{5,6},{6,5},{7,3},{8,12},{9,10},{10,... | collective-permute-start | bytes 196616 | tf_op jit(solution)/shard_map/ppermute | solution.py:304
  95.2 5.3 %collective-permute-start.46 = (bf16[128,256]{1,0:T(8,128)(2,1)S(1)}, bf16[128,256]{1,0:T(8,128)(2,1)S(1)}, u32[]{:S(2)}, u32[]{:S(2)}) collective-permute-start(bf16[128,256]{1,0:T(8,128)(2,1)S(1)} %get-tuple-element.162), channel_id=1, source_target_pairs={{0,4},{1,5},{2,6},{3,7},{4,0},{5,1},{6,2},{7,3},{8,12},{9,13},{10,... | collective-permute-start | bytes 196616 | tf_op jit(solution)/shard_map/ppermute | solution.py:304
  97.8 4.3 %collective-permute-start.49 = (bf16[128,256]{1,0:T(8,128)(2,1)S(1)}, bf16[128,256]{1,0:T(8,128)(2,1)S(1)}, u32[]{:S(2)}, u32[]{:S(2)}) collective-permute-start(bf16[128,256]{1,0:T(8,128)(2,1)S(1)} %get-tuple-element.165), channel_id=1, source_target_pairs={{0,4},{1,2},{2,1},{3,7},{4,0},{5,6},{6,5},{7,3},{8,12},{9,10},{10,... | collective-permute-start | bytes 196616 | tf_op jit(solution)/shard_map/ppermute | solution.py:304
  102.3 3.3 %collective-permute-start.52 = (bf16[32,256]{1,0:T(8,128)(2,1)S(1)}, bf16[32,256]{1,0:T(8,128)(2,1)S(1)}, u32[]{:S(2)}, u32[]{:S(2)}) collective-permute-start(bf16[32,256]{1,0:T(8,128)(2,1)S(1)} %restrict.5.refs_0_), channel_id=1, source_target_pairs={{0,3},{1,2},{2,1},{3,0},{4,7},{5,6},{6,5},{7,4},{8,11},{9,10},{10,... | collective-permute-start | bytes 49160 | tf_op jit(solution)/shard_map/ppermute | solution.py:175
  102.6 3.7 %collective-permute-start.51 = (bf16[32,256]{1,0:T(8,128)(2,1)S(1)}, bf16[32,256]{1,0:T(8,128)(2,1)S(1)}, u32[]{:S(2)}, u32[]{:S(2)}) collective-permute-start(bf16[32,256]{1,0:T(8,128)(2,1)S(1)} %restrict.5.refs_0_), channel_id=1, source_target_pairs={{0,2},{1,3},{2,0},{3,1},{4,6},{5,7},{6,4},{7,5},{8,10},{9,11},{10,... | collective-permute-start | bytes 49160 | tf_op jit(solution)/shard_map/ppermute | solution.py:175
  106.5 6.2 %collective-permute-start.53 = (bf16[64,256]{1,0:T(8,128)(2,1)S(1)}, bf16[64,256]{1,0:T(8,128)(2,1)S(1)}, u32[]{:S(2)}, u32[]{:S(2)}) collective-permute-start(bf16[64,256]{1,0:T(8,128)(2,1)S(1)} %get-tuple-element.167), channel_id=1, source_target_pairs={{0,24},{4,28},{8,16},{12,20},{16,8},{20,12},{24,0},{28,4},{1,25},{... | collective-permute-start | bytes 98312 | tf_op jit(solution)/shard_map/ppermute | solution.py:175
  109.6 5.2 %collective-permute-start.54 = (bf16[64,256]{1,0:T(8,128)(2,1)S(1)}, bf16[64,256]{1,0:T(8,128)(2,1)S(1)}, u32[]{:S(2)}, u32[]{:S(2)}) collective-permute-start(bf16[64,256]{1,0:T(8,128)(2,1)S(1)} %get-tuple-element.168), channel_id=1, source_target_pairs={{0,16},{4,20},{8,24},{12,28},{16,0},{20,4},{24,8},{28,12},{1,17},{... | collective-permute-start | bytes 98312 | tf_op jit(solution)/shard_map/ppermute | solution.py:175
  110.1 4.7 %collective-permute-start.55 = (bf16[64,256]{1,0:T(8,128)(2,1)S(1)}, bf16[64,256]{1,0:T(8,128)(2,1)S(1)}, u32[]{:S(2)}, u32[]{:S(2)}) collective-permute-start(bf16[64,256]{1,0:T(8,128)(2,1)S(1)} %get-tuple-element.169), channel_id=1, source_target_pairs={{0,8},{4,12},{8,0},{12,4},{16,24},{20,28},{24,16},{28,20},{1,9},{5... | collective-permute-start | bytes 98312 | tf_op jit(solution)/shard_map/ppermute | solution.py:175
  114.8 3.9 %collective-permute-start.56 = (bf16[32,256]{1,0:T(8,128)(2,1)S(1)}, bf16[32,256]{1,0:T(8,128)(2,1)S(1)}, u32[]{:S(2)}, u32[]{:S(2)}) collective-permute-start(bf16[32,256]{1,0:T(8,128)(2,1)S(1)} %get-tuple-element.172), channel_id=1, source_target_pairs={{0,4},{1,5},{2,6},{3,7},{4,0},{5,1},{6,2},{7,3},{8,12},{9,13},{10,... | collective-permute-start | bytes 49160 | tf_op jit(solution)/shard_map/ppermute | solution.py:304
  119.0 4.3 %collective-permute-start.57 = (bf16[128,256]{1,0:T(8,128)(2,1)S(1)}, bf16[128,256]{1,0:T(8,128)(2,1)S(1)}, u32[]{:S(2)}, u32[]{:S(2)}) collective-permute-start(bf16[128,256]{1,0:T(8,128)(2,1)S(1)} %get-tuple-element.175), channel_id=1, source_target_pairs={{0,4},{1,5},{2,6},{3,7},{4,0},{5,1},{6,2},{7,3},{8,12},{9,13},{10,... | collective-permute-start | bytes 196616 | tf_op jit(solution)/shard_map/ppermute | solution.py:304
  119.7 3.5 %collective-permute-start.58 = (bf16[128,256]{1,0:T(8,128)(2,1)S(1)}, bf16[128,256]{1,0:T(8,128)(2,1)S(1)}, u32[]{:S(2)}, u32[]{:S(2)}) collective-permute-start(bf16[128,256]{1,0:T(8,128)(2,1)S(1)} %get-tuple-element.176), channel_id=1, source_target_pairs={{0,1},{1,0},{2,3},{3,2},{4,8},{5,9},{6,10},{7,11},{8,4},{9,5},{10,... | collective-permute-start | bytes 196616 | tf_op jit(solution)/shard_map/ppermute | solution.py:304
  119.7 4.0 %collective-permute-start.59 = (bf16[128,256]{1,0:T(8,128)(2,1)S(1)}, bf16[128,256]{1,0:T(8,128)(2,1)S(1)}, u32[]{:S(2)}, u32[]{:S(2)}) collective-permute-start(bf16[128,256]{1,0:T(8,128)(2,1)S(1)} %get-tuple-element.177), channel_id=1, source_target_pairs={{0,1},{1,0},{2,3},{3,2},{4,5},{5,4},{6,7},{7,6},{8,9},{9,8},{10,11... | collective-permute-start | bytes 196616 | tf_op jit(solution)/shard_map/ppermute | solution.py:304
  120.3 4.5 %collective-permute-start.60 = (bf16[128,256]{1,0:T(8,128)(2,1)S(1)}, bf16[128,256]{1,0:T(8,128)(2,1)S(1)}, u32[]{:S(2)}, u32[]{:S(2)}) collective-permute-start(bf16[128,256]{1,0:T(8,128)(2,1)S(1)} %get-tuple-element.178), channel_id=1, source_target_pairs={{0,4},{1,2},{2,1},{3,7},{4,0},{5,6},{6,5},{7,3},{8,12},{9,10},{10,... | collective-permute-start | bytes 196616 | tf_op jit(solution)/shard_map/ppermute | solution.py:304
  (14 other events, 55.2 us)

commit v12 on v11

--- a/solution.py
+++ b/solution.py
@@ -305,7 +305,8 @@
 
 
 def traded(tiles):
-    return tuple(swapped(tiles[i], "row" if i < 2 else "col", i % 2) for i in range(4))
+    arrived = {i: swapped(tiles[i], "row" if i < 2 else "col", i % 2) for i in (1, 3, 0, 2)}
+    return [arrived[i] for i in range(4)]
 
 
 def per_device(

time: 126 us -> 126 us (level)
  no operation moved by 1% of the time
where the time goes in v12:
time: 126 us
  starting transfers between devices  66.5 us (53%)
  waiting for transfers between devices  35.5 us (28%)
  Pallas kernels  23.7 us (19%)
    ppermute x43, starting transfers between devices, swapped(): return lax.ppermute(shard, ('row', 'col'), pairs)  47.5 us
    pallas_call x34, Pallas kernels, call(): pl.pallas_call(body, out_shape=tuple(((pltpu.HBM if away else pltpu.VMEM)...  23.7 us
    ppermute x43, waiting for transfers between devices, swapped(): return lax.ppermute(shard, ('row', 'col'), pairs)  23.4 us
    ppermute x18, starting transfers between devices, meeting(): lax.ppermute(shard, axis, pairs)  19 us
    ppermute x18, waiting for transfers between devices, meeting(): lax.ppermute(shard, axis, pairs)  12.1 us
  transfers between devices with their start and end apart: 61, of which 29 were waited for; matrix products, arithmetic and copies ran while one was open for 0% of the time, Pallas kernels for 11%

profile of v12, /device:TPU:0, one launch (start us, length us, event | category | flops | bytes accessed | tf_op | source)
XLA Modules:
  0.0 126.2 jit_solution(6620367779234673965)
XLA Ops:
  0.0 1.8 %select.1 = (f32[1024,256]{1,0:T(8,128)S(1)}, bf16[1024,256]{1,0:T(8,128)(2,1)S(1)}, bf16[512,1024]{1,0:T(8,128)(2,1)S(1)}, s32[4,128]{1,0:T(4,128)S(1)}, bf16[3...) custom-call(f32[1024,256]{1,0:T(8,128)} %bitcast.11, ...), custom_call_target="tpu_custom_call" | custom-call | flops 268435456 | bytes 1148944 | tf_op jit(solution)/shard_map/select/pallas_call | solution.py:28
  1.8 3.0 %collective-permute-start = (bf16[128,256]{1,0:T(8,128)(2,1)S(1)}, bf16[128,256]{1,0:T(8,128)(2,1)S(1)}, u32[]{:S(2)}, u32[]{:S(2)}) collective-permute-start(bf16[128,256]{1,0:T(8,128)(2,1)S(1)} %get-tuple-element.95), channel_id=1, source_target_pairs={{0,4},{1,5},{2,6},{3,7},{4,0},{5,1},{6,2},{7,3},{8,12},{9,13},{10,... | collective-permute-start | bytes 196616 | tf_op jit(solution)/shard_map/ppermute | solution.py:304
  5.4 2.5 %collective-permute-start.3 = (bf16[128,256]{1,0:T(8,128)(2,1)S(1)}, bf16[128,256]{1,0:T(8,128)(2,1)S(1)}, u32[]{:S(2)}, u32[]{:S(2)}) collective-permute-start(bf16[128,256]{1,0:T(8,128)(2,1)S(1)} %get-tuple-element.98), channel_id=1, source_target_pairs={{0,4},{1,2},{2,1},{3,7},{4,0},{5,6},{6,5},{7,3},{8,12},{9,10},{10,... | collective-permute-start | bytes 196616 | tf_op jit(solution)/shard_map/ppermute | solution.py:304
  8.0 2.2 %collective-permute-done.3.g3 = bf16[128,256]{1,0:T(8,128)(2,1)S(1)} collective-permute-done((bf16[128,256]{1,0:T(8,128)(2,1)S(1)}, bf16[128,256]{1,0:T(8,128)(2,1)S(1)}, u32[]{:S(2)}, u32[]{:S(2)}) %collective-permute-start.3) | collective-permute-done | bytes 65568 | tf_op jit(solution)/shard_map/ppermute | solution.py:304
  11.1 1.1 collective-permute-start.4
  12.3 1.3 %collective-permute-done.6.refs_3_ = bf16[32,256]{1,0:T(8,128)(2,1)S(1)} collective-permute-done((bf16[32,256]{1,0:T(8,128)(2,1)S(1)}, bf16[32,256]{1,0:T(8,128)(2,1)S(1)}, u32[]{:S(2)}, u32[]{:S(2)}) %collective-permute-start.6) | collective-permute-done | bytes 16416 | tf_op jit(solution)/shard_map/ppermute | solution.py:175
  13.6 1.3 %collective-permute-done.5.refs_2_ = bf16[32,256]{1,0:T(8,128)(2,1)S(1)} collective-permute-done((bf16[32,256]{1,0:T(8,128)(2,1)S(1)}, bf16[32,256]{1,0:T(8,128)(2,1)S(1)}, u32[]{:S(2)}, u32[]{:S(2)}) %collective-permute-start.5) | collective-permute-done | bytes 16416 | tf_op jit(solution)/shard_map/ppermute | solution.py:175
  15.1 3.1 %collective-permute-start.7 = (bf16[64,256]{1,0:T(8,128)(2,1)S(1)}, bf16[64,256]{1,0:T(8,128)(2,1)S(1)}, u32[]{:S(2)}, u32[]{:S(2)}) collective-permute-start(bf16[64,256]{1,0:T(8,128)(2,1)S(1)} %get-tuple-element.101), channel_id=1, source_target_pairs={{0,24},{4,28},{8,16},{12,20},{16,8},{20,12},{24,0},{28,4},{1,25},{... | collective-permute-start | bytes 98312 | tf_op jit(solution)/shard_map/ppermute | solution.py:175
  19.5 3.5 %inverse_own.3 = (bf16[1536,1536]{1,0:T(8,128)(2,1)S(1)}, f32[1536,256]{1,0:T(8,128)S(1)}) custom-call(bf16[1536,1536]{1,0:T(8,128)(2,1)} %bitcast.9, bf16[1024,256]{1,0:T(8,128)(2,1)S(1)} %get-tuple-element.92.owned), custom_call_target="tpu_custom_call" | custom-call | flops 805306368 | bytes 5242880 | tf_op jit(solution)/shard_map/inverse_own/pallas_call | solution.py:28
  23.2 2.0 %collective-permute-start.10 = (bf16[32,256]{1,0:T(8,128)(2,1)S(1)}, bf16[32,256]{1,0:T(8,128)(2,1)S(1)}, u32[]{:S(2)}, u32[]{:S(2)}) collective-permute-start(bf16[32,256]{1,0:T(8,128)(2,1)S(1)} %get-tuple-element.106), channel_id=1, source_target_pairs={{0,4},{1,5},{2,6},{3,7},{4,0},{5,1},{6,2},{7,3},{8,12},{9,13},{10,... | collective-permute-start | bytes 49160 | tf_op jit(solution)/shard_map/ppermute | solution.py:304
  25.7 1.3 %collective-permute-done.10.theirs = bf16[32,256]{1,0:T(8,128)(2,1)S(1)} collective-permute-done((bf16[32,256]{1,0:T(8,128)(2,1)S(1)}, bf16[32,256]{1,0:T(8,128)(2,1)S(1)}, u32[]{:S(2)}, u32[]{:S(2)}) %collective-permute-start.10) | collective-permute-done | bytes 16416 | tf_op jit(solution)/shard_map/ppermute | solution.py:304
  27.2 2.0 %collective-permute-start.11 = (bf16[128,256]{1,0:T(8,128)(2,1)S(1)}, bf16[128,256]{1,0:T(8,128)(2,1)S(1)}, u32[]{:S(2)}, u32[]{:S(2)}) collective-permute-start(bf16[128,256]{1,0:T(8,128)(2,1)S(1)} %get-tuple-element.116), channel_id=1, source_target_pairs={{0,4},{1,5},{2,6},{3,7},{4,0},{5,1},{6,2},{7,3},{8,12},{9,13},{10,... | collective-permute-start | bytes 196616 | tf_op jit(solution)/shard_map/ppermute | solution.py:304
  29.7 1.6 %collective-permute-start.14 = (bf16[128,256]{1,0:T(8,128)(2,1)S(1)}, bf16[128,256]{1,0:T(8,128)(2,1)S(1)}, u32[]{:S(2)}, u32[]{:S(2)}) collective-permute-start(bf16[128,256]{1,0:T(8,128)(2,1)S(1)} %get-tuple-element.120), channel_id=1, source_target_pairs={{0,4},{1,2},{2,1},{3,7},{4,0},{5,6},{6,5},{7,3},{8,12},{9,10},{10,... | collective-permute-start | bytes 196616 | tf_op jit(solution)/shard_map/ppermute | solution.py:304
  31.3 2.6 %spread.1 = (bf16[1024,512]{1,0:T(8,128)(2,1)S(1)}, bf16[1536,1536]{1,0:T(8,128)(2,1)S(1)}) custom-call(bf16[1536,1536]{1,0:T(8,128)(2,1)} %bitcast.10, s32[4,128]{1,0:T(4,128)S(1)} %get-tuple-element.114.masked), custom_call_target="tpu_custom_call" | custom-call | bytes 4720640 | tf_op jit(solution)/shard_map/spread/pallas_call | solution.py:28
  35.3 1.2 collective-permute-start.15
  37.0 2.5 %collective-permute-start.18 = (bf16[128,256]{1,0:T(8,128)(2,1)S(1)}, bf16[128,256]{1,0:T(8,128)(2,1)S(1)}, u32[]{:S(2)}, u32[]{:S(2)}) collective-permute-start(bf16[128,256]{1,0:T(8,128)(2,1)S(1)} %get-tuple-element.128), channel_id=1, source_target_pairs={{0,4},{1,2},{2,1},{3,7},{4,0},{5,6},{6,5},{7,3},{8,12},{9,10},{10,... | collective-permute-start | bytes 196616 | tf_op jit(solution)/shard_map/ppermute | solution.py:304
  40.6 1.2 collective-permute-done.18.g3
  42.1 2.1 %collective-permute-start.19 = (bf16[128,256]{1,0:T(8,128)(2,1)S(1)}, bf16[128,256]{1,0:T(8,128)(2,1)S(1)}, u32[]{:S(2)}, u32[]{:S(2)}) collective-permute-start(bf16[128,256]{1,0:T(8,128)(2,1)S(1)} %get-tuple-element.129), channel_id=1, source_target_pairs={{0,4},{1,5},{2,6},{3,7},{4,0},{5,1},{6,2},{7,3},{8,12},{9,13},{10,... | collective-permute-start | bytes 196616 | tf_op jit(solution)/shard_map/ppermute | solution.py:304
  44.7 1.9 %collective-permute-start.22 = (bf16[128,256]{1,0:T(8,128)(2,1)S(1)}, bf16[128,256]{1,0:T(8,128)(2,1)S(1)}, u32[]{:S(2)}, u32[]{:S(2)}) collective-permute-start(bf16[128,256]{1,0:T(8,128)(2,1)S(1)} %get-tuple-element.132), channel_id=1, source_target_pairs={{0,4},{1,2},{2,1},{3,7},{4,0},{5,6},{6,5},{7,3},{8,12},{9,10},{10,... | collective-permute-start | bytes 196616 | tf_op jit(solution)/shard_map/ppermute | solution.py:304
  49.8 2.0 %collective-permute-start.23 = (bf16[128,256]{1,0:T(8,128)(2,1)S(1)}, bf16[128,256]{1,0:T(8,128)(2,1)S(1)}, u32[]{:S(2)}, u32[]{:S(2)}) collective-permute-start(bf16[128,256]{1,0:T(8,128)(2,1)S(1)} %get-tuple-element.134), channel_id=1, source_target_pairs={{0,4},{1,5},{2,6},{3,7},{4,0},{5,1},{6,2},{7,3},{8,12},{9,13},{10,... | collective-permute-start | bytes 196616 | tf_op jit(solution)/shard_map/ppermute | solution.py:304
  52.4 2.2 %collective-permute-start.26 = (bf16[128,256]{1,0:T(8,128)(2,1)S(1)}, bf16[128,256]{1,0:T(8,128)(2,1)S(1)}, u32[]{:S(2)}, u32[]{:S(2)}) collective-permute-start(bf16[128,256]{1,0:T(8,128)(2,1)S(1)} %get-tuple-element.137), channel_id=1, source_target_pairs={{0,4},{1,2},{2,1},{3,7},{4,0},{5,6},{6,5},{7,3},{8,12},{9,10},{10,... | collective-permute-start | bytes 196616 | tf_op jit(solution)/shard_map/ppermute | solution.py:304
  55.1 1.7 %collective-permute-done.26.g3 = bf16[128,256]{1,0:T(8,128)(2,1)S(1)} collective-permute-done((bf16[128,256]{1,0:T(8,128)(2,1)S(1)}, bf16[128,256]{1,0:T(8,128)(2,1)S(1)}, u32[]{:S(2)}, u32[]{:S(2)}) %collective-permute-start.26) | collective-permute-done | bytes 65568 | tf_op jit(solution)/shard_map/ppermute | solution.py:304
  57.0 1.2 collective-permute-start.28
  58.9 1.3 %collective-permute-done.29.refs_3_ = bf16[32,256]{1,0:T(8,128)(2,1)S(1)} collective-permute-done((bf16[32,256]{1,0:T(8,128)(2,1)S(1)}, bf16[32,256]{1,0:T(8,128)(2,1)S(1)}, u32[]{:S(2)}, u32[]{:S(2)}) %collective-permute-start.29) | collective-permute-done | bytes 16416 | tf_op jit(solution)/shard_map/ppermute | solution.py:175
  61.0 3.1 %collective-permute-start.30 = (bf16[64,256]{1,0:T(8,128)(2,1)S(1)}, bf16[64,256]{1,0:T(8,128)(2,1)S(1)}, u32[]{:S(2)}, u32[]{:S(2)}) collective-permute-start(bf16[64,256]{1,0:T(8,128)(2,1)S(1)} %get-tuple-element.139), channel_id=1, source_target_pairs={{0,24},{4,28},{8,16},{12,20},{16,8},{20,12},{24,0},{28,4},{1,25},{... | collective-permute-start | bytes 98312 | tf_op jit(solution)/shard_map/ppermute | solution.py:175
  64.3 1.2 collective-permute-start.32
  67.2 1.9 %collective-permute-done.31.refs_1_ = bf16[64,256]{1,0:T(8,128)(2,1)S(1)} collective-permute-done((bf16[64,256]{1,0:T(8,128)(2,1)S(1)}, bf16[64,256]{1,0:T(8,128)(2,1)S(1)}, u32[]{:S(2)}, u32[]{:S(2)}) %collective-permute-start.31) | collective-permute-done | bytes 32800 | tf_op jit(solution)/shard_map/ppermute | solution.py:175
  70.6 2.4 %collective-permute-done.33.theirs = bf16[32,256]{1,0:T(8,128)(2,1)S(1)} collective-permute-done((bf16[32,256]{1,0:T(8,128)(2,1)S(1)}, bf16[32,256]{1,0:T(8,128)(2,1)S(1)}, u32[]{:S(2)}, u32[]{:S(2)}) %collective-permute-start.33) | collective-permute-done | bytes 16416 | tf_op jit(solution)/shard_map/ppermute | solution.py:304
  74.7 2.3 %collective-permute-start.37 = (bf16[128,256]{1,0:T(8,128)(2,1)S(1)}, bf16[128,256]{1,0:T(8,128)(2,1)S(1)}, u32[]{:S(2)}, u32[]{:S(2)}) collective-permute-start(bf16[128,256]{1,0:T(8,128)(2,1)S(1)} %get-tuple-element.150), channel_id=1, source_target_pairs={{0,4},{1,2},{2,1},{3,7},{4,0},{5,6},{6,5},{7,3},{8,12},{9,10},{10,... | collective-permute-start | bytes 196616 | tf_op jit(solution)/shard_map/ppermute | solution.py:304
  78.0 1.3 %collective-permute-done.37.r3 = bf16[128,256]{1,0:T(8,128)(2,1)S(1)} collective-permute-done((bf16[128,256]{1,0:T(8,128)(2,1)S(1)}, bf16[128,256]{1,0:T(8,128)(2,1)S(1)}, u32[]{:S(2)}, u32[]{:S(2)}) %collective-permute-start.37) | collective-permute-done | bytes 65568 | tf_op jit(solution)/shard_map/ppermute | solution.py:304
  80.1 2.1 %collective-permute-start.38 = (bf16[128,256]{1,0:T(8,128)(2,1)S(1)}, bf16[128,256]{1,0:T(8,128)(2,1)S(1)}, u32[]{:S(2)}, u32[]{:S(2)}) collective-permute-start(bf16[128,256]{1,0:T(8,128)(2,1)S(1)} %get-tuple-element.153), channel_id=1, source_target_pairs={{0,4},{1,5},{2,6},{3,7},{4,0},{5,1},{6,2},{7,3},{8,12},{9,13},{10,... | collective-permute-start | bytes 196616 | tf_op jit(solution)/shard_map/ppermute | solution.py:304
  82.7 1.2 collective-permute-start.41
  83.9 1.2 operator_own.3.partial
  85.5 1.5 %collective-permute-done.41.g3 = bf16[128,256]{1,0:T(8,128)(2,1)S(1)} collective-permute-done((bf16[128,256]{1,0:T(8,128)(2,1)S(1)}, bf16[128,256]{1,0:T(8,128)(2,1)S(1)}, u32[]{:S(2)}, u32[]{:S(2)}) %collective-permute-start.41) | collective-permute-done | bytes 65568 | tf_op jit(solution)/shard_map/ppermute | solution.py:304
  87.3 1.7 %collective-permute-start.42 = (bf16[128,256]{1,0:T(8,128)(2,1)S(1)}, bf16[128,256]{1,0:T(8,128)(2,1)S(1)}, u32[]{:S(2)}, u32[]{:S(2)}) collective-permute-start(bf16[128,256]{1,0:T(8,128)(2,1)S(1)} %get-tuple-element.157), channel_id=1, source_target_pairs={{0,4},{1,5},{2,6},{3,7},{4,0},{5,1},{6,2},{7,3},{8,12},{9,13},{10,... | collective-permute-start | bytes 196616 | tf_op jit(solution)/shard_map/ppermute | solution.py:304
  89.5 2.6 %collective-permute-start.45 = (bf16[128,256]{1,0:T(8,128)(2,1)S(1)}, bf16[128,256]{1,0:T(8,128)(2,1)S(1)}, u32[]{:S(2)}, u32[]{:S(2)}) collective-permute-start(bf16[128,256]{1,0:T(8,128)(2,1)S(1)} %get-tuple-element.160), channel_id=1, source_target_pairs={{0,4},{1,2},{2,1},{3,7},{4,0},{5,6},{6,5},{7,3},{8,12},{9,10},{10,... | collective-permute-start | bytes 196616 | tf_op jit(solution)/shard_map/ppermute | solution.py:304
  92.7 1.6 %collective-permute-done.45.r3 = bf16[128,256]{1,0:T(8,128)(2,1)S(1)} collective-permute-done((bf16[128,256]{1,0:T(8,128)(2,1)S(1)}, bf16[128,256]{1,0:T(8,128)(2,1)S(1)}, u32[]{:S(2)}, u32[]{:S(2)}) %collective-permute-start.45) | collective-permute-done | bytes 65568 | tf_op jit(solution)/shard_map/ppermute | solution.py:304
  95.2 2.1 %collective-permute-start.46 = (bf16[128,256]{1,0:T(8,128)(2,1)S(1)}, bf16[128,256]{1,0:T(8,128)(2,1)S(1)}, u32[]{:S(2)}, u32[]{:S(2)}) collective-permute-start(bf16[128,256]{1,0:T(8,128)(2,1)S(1)} %get-tuple-element.162), channel_id=1, source_target_pairs={{0,4},{1,5},{2,6},{3,7},{4,0},{5,1},{6,2},{7,3},{8,12},{9,13},{10,... | collective-permute-start | bytes 196616 | tf_op jit(solution)/shard_map/ppermute | solution.py:304
  97.8 1.6 %collective-permute-start.49 = (bf16[128,256]{1,0:T(8,128)(2,1)S(1)}, bf16[128,256]{1,0:T(8,128)(2,1)S(1)}, u32[]{:S(2)}, u32[]{:S(2)}) collective-permute-start(bf16[128,256]{1,0:T(8,128)(2,1)S(1)} %get-tuple-element.165), channel_id=1, source_target_pairs={{0,4},{1,2},{2,1},{3,7},{4,0},{5,6},{6,5},{7,3},{8,12},{9,10},{10,... | collective-permute-start | bytes 196616 | tf_op jit(solution)/shard_map/ppermute | solution.py:304
  99.4 1.1 collective-permute-done.46.g0
  100.5 1.5 %collective-permute-done.49.g3 = bf16[128,256]{1,0:T(8,128)(2,1)S(1)} collective-permute-done((bf16[128,256]{1,0:T(8,128)(2,1)S(1)}, bf16[128,256]{1,0:T(8,128)(2,1)S(1)}, u32[]{:S(2)}, u32[]{:S(2)}) %collective-permute-start.49) | collective-permute-done | bytes 65568 | tf_op jit(solution)/shard_map/ppermute | solution.py:304
  102.6 1.1 collective-permute-start.51
  104.2 1.4 %collective-permute-done.52.refs_3_ = bf16[32,256]{1,0:T(8,128)(2,1)S(1)} collective-permute-done((bf16[32,256]{1,0:T(8,128)(2,1)S(1)}, bf16[32,256]{1,0:T(8,128)(2,1)S(1)}, u32[]{:S(2)}, u32[]{:S(2)}) %collective-permute-start.52) | collective-permute-done | bytes 16416 | tf_op jit(solution)/shard_map/ppermute | solution.py:175
  106.5 3.0 %collective-permute-start.53 = (bf16[64,256]{1,0:T(8,128)(2,1)S(1)}, bf16[64,256]{1,0:T(8,128)(2,1)S(1)}, u32[]{:S(2)}, u32[]{:S(2)}) collective-permute-start(bf16[64,256]{1,0:T(8,128)(2,1)S(1)} %get-tuple-element.167), channel_id=1, source_target_pairs={{0,24},{4,28},{8,16},{12,20},{16,8},{20,12},{24,0},{28,4},{1,25},{... | collective-permute-start | bytes 98312 | tf_op jit(solution)/shard_map/ppermute | solution.py:175
  112.7 2.0 %collective-permute-done.54.refs_1_ = bf16[64,256]{1,0:T(8,128)(2,1)S(1)} collective-permute-done((bf16[64,256]{1,0:T(8,128)(2,1)S(1)}, bf16[64,256]{1,0:T(8,128)(2,1)S(1)}, u32[]{:S(2)}, u32[]{:S(2)}) %collective-permute-start.54) | collective-permute-done | bytes 32800 | tf_op jit(solution)/shard_map/ppermute | solution.py:175
  116.2 2.5 %collective-permute-done.56.theirs = bf16[32,256]{1,0:T(8,128)(2,1)S(1)} collective-permute-done((bf16[32,256]{1,0:T(8,128)(2,1)S(1)}, bf16[32,256]{1,0:T(8,128)(2,1)S(1)}, u32[]{:S(2)}, u32[]{:S(2)}) %collective-permute-start.56) | collective-permute-done | bytes 16416 | tf_op jit(solution)/shard_map/ppermute | solution.py:304
  120.3 2.3 %collective-permute-start.60 = (bf16[128,256]{1,0:T(8,128)(2,1)S(1)}, bf16[128,256]{1,0:T(8,128)(2,1)S(1)}, u32[]{:S(2)}, u32[]{:S(2)}) collective-permute-start(bf16[128,256]{1,0:T(8,128)(2,1)S(1)} %get-tuple-element.178), channel_id=1, source_target_pairs={{0,4},{1,2},{2,1},{3,7},{4,0},{5,6},{6,5},{7,3},{8,12},{9,10},{10,... | collective-permute-start | bytes 196616 | tf_op jit(solution)/shard_map/ppermute | solution.py:304
  124.8 1.2 last_update.1
  (110 shorter events, 34.9 us)
Async XLA Ops:
  1.8 6.1 %collective-permute-start = (bf16[128,256]{1,0:T(8,128)(2,1)S(1)}, bf16[128,256]{1,0:T(8,128)(2,1)S(1)}, u32[]{:S(2)}, u32[]{:S(2)}) collective-permute-start(bf16[128,256]{1,0:T(8,128)(2,1)S(1)} %get-tuple-element.95), channel_id=1, source_target_pairs={{0,4},{1,5},{2,6},{3,7},{4,0},{5,1},{6,2},{7,3},{8,12},{9,13},{10,... | collective-permute-start | bytes 196616 | tf_op jit(solution)/shard_map/ppermute | solution.py:304
  5.4 4.8 %collective-permute-start.3 = (bf16[128,256]{1,0:T(8,128)(2,1)S(1)}, bf16[128,256]{1,0:T(8,128)(2,1)S(1)}, u32[]{:S(2)}, u32[]{:S(2)}) collective-permute-start(bf16[128,256]{1,0:T(8,128)(2,1)S(1)} %get-tuple-element.98), channel_id=1, source_target_pairs={{0,4},{1,2},{2,1},{3,7},{4,0},{5,6},{6,5},{7,3},{8,12},{9,10},{10,... | collective-permute-start | bytes 196616 | tf_op jit(solution)/shard_map/ppermute | solution.py:304
  11.1 3.7 %collective-permute-start.5 = (bf16[32,256]{1,0:T(8,128)(2,1)S(1)}, bf16[32,256]{1,0:T(8,128)(2,1)S(1)}, u32[]{:S(2)}, u32[]{:S(2)}) collective-permute-start(bf16[32,256]{1,0:T(8,128)(2,1)S(1)} %restrict.3.refs_0_), channel_id=1, source_target_pairs={{0,2},{1,3},{2,0},{3,1},{4,6},{5,7},{6,4},{7,5},{8,10},{9,11},{10,... | collective-permute-start | bytes 49160 | tf_op jit(solution)/shard_map/ppermute | solution.py:175
  11.1 3.7 %collective-permute-start.4 = (bf16[32,256]{1,0:T(8,128)(2,1)S(1)}, bf16[32,256]{1,0:T(8,128)(2,1)S(1)}, u32[]{:S(2)}, u32[]{:S(2)}) collective-permute-start(bf16[32,256]{1,0:T(8,128)(2,1)S(1)} %restrict.3.refs_0_), channel_id=1, source_target_pairs={{0,1},{1,0},{2,3},{3,2},{4,5},{5,4},{6,7},{7,6},{8,9},{9,8},{10,11... | collective-permute-start | bytes 49160 | tf_op jit(solution)/shard_map/ppermute | solution.py:175
  15.1 8.0 %collective-permute-start.7 = (bf16[64,256]{1,0:T(8,128)(2,1)S(1)}, bf16[64,256]{1,0:T(8,128)(2,1)S(1)}, u32[]{:S(2)}, u32[]{:S(2)}) collective-permute-start(bf16[64,256]{1,0:T(8,128)(2,1)S(1)} %get-tuple-element.101), channel_id=1, source_target_pairs={{0,24},{4,28},{8,16},{12,20},{16,8},{20,12},{24,0},{28,4},{1,25},{... | collective-permute-start | bytes 98312 | tf_op jit(solution)/shard_map/ppermute | solution.py:175
  18.2 4.9 %collective-permute-start.8 = (bf16[64,256]{1,0:T(8,128)(2,1)S(1)}, bf16[64,256]{1,0:T(8,128)(2,1)S(1)}, u32[]{:S(2)}, u32[]{:S(2)}) collective-permute-start(bf16[64,256]{1,0:T(8,128)(2,1)S(1)} %get-tuple-element.102), channel_id=1, source_target_pairs={{0,16},{4,20},{8,24},{12,28},{16,0},{20,4},{24,8},{28,12},{1,17},{... | collective-permute-start | bytes 98312 | tf_op jit(solution)/shard_map/ppermute | solution.py:175
  18.9 4.3 %collective-permute-start.9 = (bf16[64,256]{1,0:T(8,128)(2,1)S(1)}, bf16[64,256]{1,0:T(8,128)(2,1)S(1)}, u32[]{:S(2)}, u32[]{:S(2)}) collective-permute-start(bf16[64,256]{1,0:T(8,128)(2,1)S(1)} %get-tuple-element.103), channel_id=1, source_target_pairs={{0,8},{4,12},{8,0},{12,4},{16,24},{20,28},{24,16},{28,20},{1,9},{5... | collective-permute-start | bytes 98312 | tf_op jit(solution)/shard_map/ppermute | solution.py:175
  23.2 3.8 %collective-permute-start.10 = (bf16[32,256]{1,0:T(8,128)(2,1)S(1)}, bf16[32,256]{1,0:T(8,128)(2,1)S(1)}, u32[]{:S(2)}, u32[]{:S(2)}) collective-permute-start(bf16[32,256]{1,0:T(8,128)(2,1)S(1)} %get-tuple-element.106), channel_id=1, source_target_pairs={{0,4},{1,5},{2,6},{3,7},{4,0},{5,1},{6,2},{7,3},{8,12},{9,13},{10,... | collective-permute-start | bytes 49160 | tf_op jit(solution)/shard_map/ppermute | solution.py:304
  27.2 6.7 %collective-permute-start.11 = (bf16[128,256]{1,0:T(8,128)(2,1)S(1)}, bf16[128,256]{1,0:T(8,128)(2,1)S(1)}, u32[]{:S(2)}, u32[]{:S(2)}) collective-permute-start(bf16[128,256]{1,0:T(8,128)(2,1)S(1)} %get-tuple-element.116), channel_id=1, source_target_pairs={{0,4},{1,5},{2,6},{3,7},{4,0},{5,1},{6,2},{7,3},{8,12},{9,13},{10,... | collective-permute-start | bytes 196616 | tf_op jit(solution)/shard_map/ppermute | solution.py:304
  29.2 4.7 %collective-permute-start.12 = (bf16[128,256]{1,0:T(8,128)(2,1)S(1)}, bf16[128,256]{1,0:T(8,128)(2,1)S(1)}, u32[]{:S(2)}, u32[]{:S(2)}) collective-permute-start(bf16[128,256]{1,0:T(8,128)(2,1)S(1)} %get-tuple-element.117), channel_id=1, source_target_pairs={{0,1},{1,0},{2,3},{3,2},{4,8},{5,9},{6,10},{7,11},{8,4},{9,5},{10,... | collective-permute-start | bytes 196616 | tf_op jit(solution)/shard_map/ppermute | solution.py:304
  29.2 5.2 %collective-permute-start.13 = (bf16[128,256]{1,0:T(8,128)(2,1)S(1)}, bf16[128,256]{1,0:T(8,128)(2,1)S(1)}, u32[]{:S(2)}, u32[]{:S(2)}) collective-permute-start(bf16[128,256]{1,0:T(8,128)(2,1)S(1)} %get-tuple-element.119), channel_id=1, source_target_pairs={{0,1},{1,0},{2,3},{3,2},{4,5},{5,4},{6,7},{7,6},{8,9},{9,8},{10,11... | collective-permute-start | bytes 196616 | tf_op jit(solution)/shard_map/ppermute | solution.py:304
  29.7 4.7 %collective-permute-start.14 = (bf16[128,256]{1,0:T(8,128)(2,1)S(1)}, bf16[128,256]{1,0:T(8,128)(2,1)S(1)}, u32[]{:S(2)}, u32[]{:S(2)}) collective-permute-start(bf16[128,256]{1,0:T(8,128)(2,1)S(1)} %get-tuple-element.120), channel_id=1, source_target_pairs={{0,4},{1,2},{2,1},{3,7},{4,0},{5,6},{6,5},{7,3},{8,12},{9,10},{10,... | collective-permute-start | bytes 196616 | tf_op jit(solution)/shard_map/ppermute | solution.py:304
  35.3 5.3 %collective-permute-start.15 = (bf16[128,256]{1,0:T(8,128)(2,1)S(1)}, bf16[128,256]{1,0:T(8,128)(2,1)S(1)}, u32[]{:S(2)}, u32[]{:S(2)}) collective-permute-start(bf16[128,256]{1,0:T(8,128)(2,1)S(1)} %get-tuple-element.125), channel_id=1, source_target_pairs={{0,4},{1,5},{2,6},{3,7},{4,0},{5,1},{6,2},{7,3},{8,12},{9,13},{10,... | collective-permute-start | bytes 196616 | tf_op jit(solution)/shard_map/ppermute | solution.py:304
  36.5 4.0 %collective-permute-start.16 = (bf16[128,256]{1,0:T(8,128)(2,1)S(1)}, bf16[128,256]{1,0:T(8,128)(2,1)S(1)}, u32[]{:S(2)}, u32[]{:S(2)}) collective-permute-start(bf16[128,256]{1,0:T(8,128)(2,1)S(1)} %get-tuple-element.126), channel_id=1, source_target_pairs={{0,1},{1,0},{2,3},{3,2},{4,8},{5,9},{6,10},{7,11},{8,4},{9,5},{10,... | collective-permute-start | bytes 196616 | tf_op jit(solution)/shard_map/ppermute | solution.py:304
  36.5 4.0 %collective-permute-start.17 = (bf16[128,256]{1,0:T(8,128)(2,1)S(1)}, bf16[128,256]{1,0:T(8,128)(2,1)S(1)}, u32[]{:S(2)}, u32[]{:S(2)}) collective-permute-start(bf16[128,256]{1,0:T(8,128)(2,1)S(1)} %get-tuple-element.127), channel_id=1, source_target_pairs={{0,1},{1,0},{2,3},{3,2},{4,5},{5,4},{6,7},{7,6},{8,9},{9,8},{10,11... | collective-permute-start | bytes 196616 | tf_op jit(solution)/shard_map/ppermute | solution.py:304
  37.0 4.8 %collective-permute-start.18 = (bf16[128,256]{1,0:T(8,128)(2,1)S(1)}, bf16[128,256]{1,0:T(8,128)(2,1)S(1)}, u32[]{:S(2)}, u32[]{:S(2)}) collective-permute-start(bf16[128,256]{1,0:T(8,128)(2,1)S(1)} %get-tuple-element.128), channel_id=1, source_target_pairs={{0,4},{1,2},{2,1},{3,7},{4,0},{5,6},{6,5},{7,3},{8,12},{9,10},{10,... | collective-permute-start | bytes 196616 | tf_op jit(solution)/shard_map/ppermute | solution.py:304
  42.1 5.3 %collective-permute-start.19 = (bf16[128,256]{1,0:T(8,128)(2,1)S(1)}, bf16[128,256]{1,0:T(8,128)(2,1)S(1)}, u32[]{:S(2)}, u32[]{:S(2)}) collective-permute-start(bf16[128,256]{1,0:T(8,128)(2,1)S(1)} %get-tuple-element.129), channel_id=1, source_target_pairs={{0,4},{1,5},{2,6},{3,7},{4,0},{5,1},{6,2},{7,3},{8,12},{9,13},{10,... | collective-permute-start | bytes 196616 | tf_op jit(solution)/shard_map/ppermute | solution.py:304
  44.2 3.2 %collective-permute-start.20 = (bf16[128,256]{1,0:T(8,128)(2,1)S(1)}, bf16[128,256]{1,0:T(8,128)(2,1)S(1)}, u32[]{:S(2)}, u32[]{:S(2)}) collective-permute-start(bf16[128,256]{1,0:T(8,128)(2,1)S(1)} %get-tuple-element.130), channel_id=1, source_target_pairs={{0,1},{1,0},{2,3},{3,2},{4,8},{5,9},{6,10},{7,11},{8,4},{9,5},{10,... | collective-permute-start | bytes 196616 | tf_op jit(solution)/shard_map/ppermute | solution.py:304
  44.2 3.8 %collective-permute-start.21 = (bf16[128,256]{1,0:T(8,128)(2,1)S(1)}, bf16[128,256]{1,0:T(8,128)(2,1)S(1)}, u32[]{:S(2)}, u32[]{:S(2)}) collective-permute-start(bf16[128,256]{1,0:T(8,128)(2,1)S(1)} %get-tuple-element.131), channel_id=1, source_target_pairs={{0,1},{1,0},{2,3},{3,2},{4,5},{5,4},{6,7},{7,6},{8,9},{9,8},{10,11... | collective-permute-start | bytes 196616 | tf_op jit(solution)/shard_map/ppermute | solution.py:304
  44.7 4.3 %collective-permute-start.22 = (bf16[128,256]{1,0:T(8,128)(2,1)S(1)}, bf16[128,256]{1,0:T(8,128)(2,1)S(1)}, u32[]{:S(2)}, u32[]{:S(2)}) collective-permute-start(bf16[128,256]{1,0:T(8,128)(2,1)S(1)} %get-tuple-element.132), channel_id=1, source_target_pairs={{0,4},{1,2},{2,1},{3,7},{4,0},{5,6},{6,5},{7,3},{8,12},{9,10},{10,... | collective-permute-start | bytes 196616 | tf_op jit(solution)/shard_map/ppermute | solution.py:304
  49.8 5.2 %collective-permute-start.23 = (bf16[128,256]{1,0:T(8,128)(2,1)S(1)}, bf16[128,256]{1,0:T(8,128)(2,1)S(1)}, u32[]{:S(2)}, u32[]{:S(2)}) collective-permute-start(bf16[128,256]{1,0:T(8,128)(2,1)S(1)} %get-tuple-element.134), channel_id=1, source_target_pairs={{0,4},{1,5},{2,6},{3,7},{4,0},{5,1},{6,2},{7,3},{8,12},{9,13},{10,... | collective-permute-start | bytes 196616 | tf_op jit(solution)/shard_map/ppermute | solution.py:304
  52.4 4.4 %collective-permute-start.26 = (bf16[128,256]{1,0:T(8,128)(2,1)S(1)}, bf16[128,256]{1,0:T(8,128)(2,1)S(1)}, u32[]{:S(2)}, u32[]{:S(2)}) collective-permute-start(bf16[128,256]{1,0:T(8,128)(2,1)S(1)} %get-tuple-element.137), channel_id=1, source_target_pairs={{0,4},{1,2},{2,1},{3,7},{4,0},{5,6},{6,5},{7,3},{8,12},{9,10},{10,... | collective-permute-start | bytes 196616 | tf_op jit(solution)/shard_map/ppermute | solution.py:304
  57.0 3.8 %collective-permute-start.28 = (bf16[32,256]{1,0:T(8,128)(2,1)S(1)}, bf16[32,256]{1,0:T(8,128)(2,1)S(1)}, u32[]{:S(2)}, u32[]{:S(2)}) collective-permute-start(bf16[32,256]{1,0:T(8,128)(2,1)S(1)} %restrict.4.refs_0_), channel_id=1, source_target_pairs={{0,2},{1,3},{2,0},{3,1},{4,6},{5,7},{6,4},{7,5},{8,10},{9,11},{10,... | collective-permute-start | bytes 49160 | tf_op jit(solution)/shard_map/ppermute | solution.py:175
  61.0 6.1 %collective-permute-start.30 = (bf16[64,256]{1,0:T(8,128)(2,1)S(1)}, bf16[64,256]{1,0:T(8,128)(2,1)S(1)}, u32[]{:S(2)}, u32[]{:S(2)}) collective-permute-start(bf16[64,256]{1,0:T(8,128)(2,1)S(1)} %get-tuple-element.139), channel_id=1, source_target_pairs={{0,24},{4,28},{8,16},{12,20},{16,8},{20,12},{24,0},{28,4},{1,25},{... | collective-permute-start | bytes 98312 | tf_op jit(solution)/shard_map/ppermute | solution.py:175
  64.2 4.9 %collective-permute-start.31 = (bf16[64,256]{1,0:T(8,128)(2,1)S(1)}, bf16[64,256]{1,0:T(8,128)(2,1)S(1)}, u32[]{:S(2)}, u32[]{:S(2)}) collective-permute-start(bf16[64,256]{1,0:T(8,128)(2,1)S(1)} %get-tuple-element.140), channel_id=1, source_target_pairs={{0,16},{4,20},{8,24},{12,28},{16,0},{20,4},{24,8},{28,12},{1,17},{... | collective-permute-start | bytes 98312 | tf_op jit(solution)/shard_map/ppermute | solution.py:175
  64.3 4.8 %collective-permute-start.32 = (bf16[64,256]{1,0:T(8,128)(2,1)S(1)}, bf16[64,256]{1,0:T(8,128)(2,1)S(1)}, u32[]{:S(2)}, u32[]{:S(2)}) collective-permute-start(bf16[64,256]{1,0:T(8,128)(2,1)S(1)} %get-tuple-element.141), channel_id=1, source_target_pairs={{0,8},{4,12},{8,0},{12,4},{16,24},{20,28},{24,16},{28,20},{1,9},{5... | collective-permute-start | bytes 98312 | tf_op jit(solution)/shard_map/ppermute | solution.py:175
  69.1 3.8 %collective-permute-start.33 = (bf16[32,256]{1,0:T(8,128)(2,1)S(1)}, bf16[32,256]{1,0:T(8,128)(2,1)S(1)}, u32[]{:S(2)}, u32[]{:S(2)}) collective-permute-start(bf16[32,256]{1,0:T(8,128)(2,1)S(1)} %get-tuple-element.144), channel_id=1, source_target_pairs={{0,4},{1,5},{2,6},{3,7},{4,0},{5,1},{6,2},{7,3},{8,12},{9,13},{10,... | collective-permute-start | bytes 49160 | tf_op jit(solution)/shard_map/ppermute | solution.py:304
  73.2 4.3 %collective-permute-start.34 = (bf16[128,256]{1,0:T(8,128)(2,1)S(1)}, bf16[128,256]{1,0:T(8,128)(2,1)S(1)}, u32[]{:S(2)}, u32[]{:S(2)}) collective-permute-start(bf16[128,256]{1,0:T(8,128)(2,1)S(1)} %get-tuple-element.147), channel_id=1, source_target_pairs={{0,4},{1,5},{2,6},{3,7},{4,0},{5,1},{6,2},{7,3},{8,12},{9,13},{10,... | collective-permute-start | bytes 196616 | tf_op jit(solution)/shard_map/ppermute | solution.py:304
  74.2 3.3 %collective-permute-start.35 = (bf16[128,256]{1,0:T(8,128)(2,1)S(1)}, bf16[128,256]{1,0:T(8,128)(2,1)S(1)}, u32[]{:S(2)}, u32[]{:S(2)}) collective-permute-start(bf16[128,256]{1,0:T(8,128)(2,1)S(1)} %get-tuple-element.148), channel_id=1, source_target_pairs={{0,1},{1,0},{2,3},{3,2},{4,8},{5,9},{6,10},{7,11},{8,4},{9,5},{10,... | collective-permute-start | bytes 196616 | tf_op jit(solution)/shard_map/ppermute | solution.py:304
  74.2 3.8 %collective-permute-start.36 = (bf16[128,256]{1,0:T(8,128)(2,1)S(1)}, bf16[128,256]{1,0:T(8,128)(2,1)S(1)}, u32[]{:S(2)}, u32[]{:S(2)}) collective-permute-start(bf16[128,256]{1,0:T(8,128)(2,1)S(1)} %get-tuple-element.149), channel_id=1, source_target_pairs={{0,1},{1,0},{2,3},{3,2},{4,5},{5,4},{6,7},{7,6},{8,9},{9,8},{10,11... | collective-permute-start | bytes 196616 | tf_op jit(solution)/shard_map/ppermute | solution.py:304
  74.7 4.6 %collective-permute-start.37 = (bf16[128,256]{1,0:T(8,128)(2,1)S(1)}, bf16[128,256]{1,0:T(8,128)(2,1)S(1)}, u32[]{:S(2)}, u32[]{:S(2)}) collective-permute-start(bf16[128,256]{1,0:T(8,128)(2,1)S(1)} %get-tuple-element.150), channel_id=1, source_target_pairs={{0,4},{1,2},{2,1},{3,7},{4,0},{5,6},{6,5},{7,3},{8,12},{9,10},{10,... | collective-permute-start | bytes 196616 | tf_op jit(solution)/shard_map/ppermute | solution.py:304
  80.1 5.3 %collective-permute-start.38 = (bf16[128,256]{1,0:T(8,128)(2,1)S(1)}, bf16[128,256]{1,0:T(8,128)(2,1)S(1)}, u32[]{:S(2)}, u32[]{:S(2)}) collective-permute-start(bf16[128,256]{1,0:T(8,128)(2,1)S(1)} %get-tuple-element.153), channel_id=1, source_target_pairs={{0,4},{1,5},{2,6},{3,7},{4,0},{5,1},{6,2},{7,3},{8,12},{9,13},{10,... | collective-permute-start | bytes 196616 | tf_op jit(solution)/shard_map/ppermute | solution.py:304
  82.7 4.3 %collective-permute-start.41 = (bf16[128,256]{1,0:T(8,128)(2,1)S(1)}, bf16[128,256]{1,0:T(8,128)(2,1)S(1)}, u32[]{:S(2)}, u32[]{:S(2)}) collective-permute-start(bf16[128,256]{1,0:T(8,128)(2,1)S(1)} %get-tuple-element.156), channel_id=1, source_target_pairs={{0,4},{1,2},{2,1},{3,7},{4,0},{5,6},{6,5},{7,3},{8,12},{9,10},{10,... | collective-permute-start | bytes 196616 | tf_op jit(solution)/shard_map/ppermute | solution.py:304
  87.3 4.8 %collective-permute-start.42 = (bf16[128,256]{1,0:T(8,128)(2,1)S(1)}, bf16[128,256]{1,0:T(8,128)(2,1)S(1)}, u32[]{:S(2)}, u32[]{:S(2)}) collective-permute-start(bf16[128,256]{1,0:T(8,128)(2,1)S(1)} %get-tuple-element.157), channel_id=1, source_target_pairs={{0,4},{1,5},{2,6},{3,7},{4,0},{5,1},{6,2},{7,3},{8,12},{9,13},{10,... | collective-permute-start | bytes 196616 | tf_op jit(solution)/shard_map/ppermute | solution.py:304
  89.0 3.7 %collective-permute-start.44 = (bf16[128,256]{1,0:T(8,128)(2,1)S(1)}, bf16[128,256]{1,0:T(8,128)(2,1)S(1)}, u32[]{:S(2)}, u32[]{:S(2)}) collective-permute-start(bf16[128,256]{1,0:T(8,128)(2,1)S(1)} %get-tuple-element.159), channel_id=1, source_target_pairs={{0,1},{1,0},{2,3},{3,2},{4,5},{5,4},{6,7},{7,6},{8,9},{9,8},{10,11... | collective-permute-start | bytes 196616 | tf_op jit(solution)/shard_map/ppermute | solution.py:304
  89.5 4.9 %collective-permute-start.45 = (bf16[128,256]{1,0:T(8,128)(2,1)S(1)}, bf16[128,256]{1,0:T(8,128)(2,1)S(1)}, u32[]{:S(2)}, u32[]{:S(2)}) collective-permute-start(bf16[128,256]{1,0:T(8,128)(2,1)S(1)} %get-tuple-element.160), channel_id=1, source_target_pairs={{0,4},{1,2},{2,1},{3,7},{4,0},{5,6},{6,5},{7,3},{8,12},{9,10},{10,... | collective-permute-start | bytes 196616 | tf_op jit(solution)/shard_map/ppermute | solution.py:304
  95.2 5.3 %collective-permute-start.46 = (bf16[128,256]{1,0:T(8,128)(2,1)S(1)}, bf16[128,256]{1,0:T(8,128)(2,1)S(1)}, u32[]{:S(2)}, u32[]{:S(2)}) collective-permute-start(bf16[128,256]{1,0:T(8,128)(2,1)S(1)} %get-tuple-element.162), channel_id=1, source_target_pairs={{0,4},{1,5},{2,6},{3,7},{4,0},{5,1},{6,2},{7,3},{8,12},{9,13},{10,... | collective-permute-start | bytes 196616 | tf_op jit(solution)/shard_map/ppermute | solution.py:304
  97.8 4.3 %collective-permute-start.49 = (bf16[128,256]{1,0:T(8,128)(2,1)S(1)}, bf16[128,256]{1,0:T(8,128)(2,1)S(1)}, u32[]{:S(2)}, u32[]{:S(2)}) collective-permute-start(bf16[128,256]{1,0:T(8,128)(2,1)S(1)} %get-tuple-element.165), channel_id=1, source_target_pairs={{0,4},{1,2},{2,1},{3,7},{4,0},{5,6},{6,5},{7,3},{8,12},{9,10},{10,... | collective-permute-start | bytes 196616 | tf_op jit(solution)/shard_map/ppermute | solution.py:304
  102.3 3.3 %collective-permute-start.52 = (bf16[32,256]{1,0:T(8,128)(2,1)S(1)}, bf16[32,256]{1,0:T(8,128)(2,1)S(1)}, u32[]{:S(2)}, u32[]{:S(2)}) collective-permute-start(bf16[32,256]{1,0:T(8,128)(2,1)S(1)} %restrict.5.refs_0_), channel_id=1, source_target_pairs={{0,3},{1,2},{2,1},{3,0},{4,7},{5,6},{6,5},{7,4},{8,11},{9,10},{10,... | collective-permute-start | bytes 49160 | tf_op jit(solution)/shard_map/ppermute | solution.py:175
  102.6 3.7 %collective-permute-start.51 = (bf16[32,256]{1,0:T(8,128)(2,1)S(1)}, bf16[32,256]{1,0:T(8,128)(2,1)S(1)}, u32[]{:S(2)}, u32[]{:S(2)}) collective-permute-start(bf16[32,256]{1,0:T(8,128)(2,1)S(1)} %restrict.5.refs_0_), channel_id=1, source_target_pairs={{0,2},{1,3},{2,0},{3,1},{4,6},{5,7},{6,4},{7,5},{8,10},{9,11},{10,... | collective-permute-start | bytes 49160 | tf_op jit(solution)/shard_map/ppermute | solution.py:175
  106.5 6.2 %collective-permute-start.53 = (bf16[64,256]{1,0:T(8,128)(2,1)S(1)}, bf16[64,256]{1,0:T(8,128)(2,1)S(1)}, u32[]{:S(2)}, u32[]{:S(2)}) collective-permute-start(bf16[64,256]{1,0:T(8,128)(2,1)S(1)} %get-tuple-element.167), channel_id=1, source_target_pairs={{0,24},{4,28},{8,16},{12,20},{16,8},{20,12},{24,0},{28,4},{1,25},{... | collective-permute-start | bytes 98312 | tf_op jit(solution)/shard_map/ppermute | solution.py:175
  109.6 5.2 %collective-permute-start.54 = (bf16[64,256]{1,0:T(8,128)(2,1)S(1)}, bf16[64,256]{1,0:T(8,128)(2,1)S(1)}, u32[]{:S(2)}, u32[]{:S(2)}) collective-permute-start(bf16[64,256]{1,0:T(8,128)(2,1)S(1)} %get-tuple-element.168), channel_id=1, source_target_pairs={{0,16},{4,20},{8,24},{12,28},{16,0},{20,4},{24,8},{28,12},{1,17},{... | collective-permute-start | bytes 98312 | tf_op jit(solution)/shard_map/ppermute | solution.py:175
  110.1 4.7 %collective-permute-start.55 = (bf16[64,256]{1,0:T(8,128)(2,1)S(1)}, bf16[64,256]{1,0:T(8,128)(2,1)S(1)}, u32[]{:S(2)}, u32[]{:S(2)}) collective-permute-start(bf16[64,256]{1,0:T(8,128)(2,1)S(1)} %get-tuple-element.169), channel_id=1, source_target_pairs={{0,8},{4,12},{8,0},{12,4},{16,24},{20,28},{24,16},{28,20},{1,9},{5... | collective-permute-start | bytes 98312 | tf_op jit(solution)/shard_map/ppermute | solution.py:175
  114.8 3.9 %collective-permute-start.56 = (bf16[32,256]{1,0:T(8,128)(2,1)S(1)}, bf16[32,256]{1,0:T(8,128)(2,1)S(1)}, u32[]{:S(2)}, u32[]{:S(2)}) collective-permute-start(bf16[32,256]{1,0:T(8,128)(2,1)S(1)} %get-tuple-element.172), channel_id=1, source_target_pairs={{0,4},{1,5},{2,6},{3,7},{4,0},{5,1},{6,2},{7,3},{8,12},{9,13},{10,... | collective-permute-start | bytes 49160 | tf_op jit(solution)/shard_map/ppermute | solution.py:304
  119.0 4.3 %collective-permute-start.57 = (bf16[128,256]{1,0:T(8,128)(2,1)S(1)}, bf16[128,256]{1,0:T(8,128)(2,1)S(1)}, u32[]{:S(2)}, u32[]{:S(2)}) collective-permute-start(bf16[128,256]{1,0:T(8,128)(2,1)S(1)} %get-tuple-element.175), channel_id=1, source_target_pairs={{0,4},{1,5},{2,6},{3,7},{4,0},{5,1},{6,2},{7,3},{8,12},{9,13},{10,... | collective-permute-start | bytes 196616 | tf_op jit(solution)/shard_map/ppermute | solution.py:304
  119.7 3.5 %collective-permute-start.58 = (bf16[128,256]{1,0:T(8,128)(2,1)S(1)}, bf16[128,256]{1,0:T(8,128)(2,1)S(1)}, u32[]{:S(2)}, u32[]{:S(2)}) collective-permute-start(bf16[128,256]{1,0:T(8,128)(2,1)S(1)} %get-tuple-element.176), channel_id=1, source_target_pairs={{0,1},{1,0},{2,3},{3,2},{4,8},{5,9},{6,10},{7,11},{8,4},{9,5},{10,... | collective-permute-start | bytes 196616 | tf_op jit(solution)/shard_map/ppermute | solution.py:304
  119.7 4.0 %collective-permute-start.59 = (bf16[128,256]{1,0:T(8,128)(2,1)S(1)}, bf16[128,256]{1,0:T(8,128)(2,1)S(1)}, u32[]{:S(2)}, u32[]{:S(2)}) collective-permute-start(bf16[128,256]{1,0:T(8,128)(2,1)S(1)} %get-tuple-element.177), channel_id=1, source_target_pairs={{0,1},{1,0},{2,3},{3,2},{4,5},{5,4},{6,7},{7,6},{8,9},{9,8},{10,11... | collective-permute-start | bytes 196616 | tf_op jit(solution)/shard_map/ppermute | solution.py:304
  120.3 4.5 %collective-permute-start.60 = (bf16[128,256]{1,0:T(8,128)(2,1)S(1)}, bf16[128,256]{1,0:T(8,128)(2,1)S(1)}, u32[]{:S(2)}, u32[]{:S(2)}) collective-permute-start(bf16[128,256]{1,0:T(8,128)(2,1)S(1)} %get-tuple-element.178), channel_id=1, source_target_pairs={{0,4},{1,2},{2,1},{3,7},{4,0},{5,6},{6,5},{7,3},{8,12},{9,10},{10,... | collective-permute-start | bytes 196616 | tf_op jit(solution)/shard_map/ppermute | solution.py:304
  (14 other events, 55.2 us)

commit v13 on v11

--- a/solution.py
+++ b/solution.py
@@ -43,7 +43,7 @@
 
 def directions():
     row, col = parities()
-    return 1 - row, row, 3 - col, 2 + col
+    return row, 1 - row, 2 + col, 3 - col
 
 
 def margin_spans(own, tile):
@@ -93,10 +93,10 @@
     ]
     row, col = parities()
     ordered = (
+        jnp.where(row == 0, listed[0], listed[1]),
         jnp.where(row == 0, listed[1], listed[0]),
-        jnp.where(row == 0, listed[0], listed[1]),
+        jnp.where(col == 0, listed[2], listed[3]),
         jnp.where(col == 0, listed[3], listed[2]),
-        jnp.where(col == 0, listed[2], listed[3]),
     )
     for i, here in enumerate(ordered):
         masked[i : i + 1, :] = here
@@ -305,7 +305,7 @@
 
 
 def traded(tiles):
-    return tuple(swapped(tiles[i], "row" if i < 2 else "col", i % 2) for i in range(4))
+    return [swapped(tiles[i], "row" if i < 2 else "col", 1 - i % 2) for i in range(4)]
 
 
 def per_device(

time: 126 us -> 127 us (level)
  waiting for transfers between devices: 35.5 us -> 48.6 us
  starting transfers between devices: 66.5 us -> 54.2 us
    ppermute x43, waiting for transfers between devices: 23.4 us -> 39 us  [swapped(): return lax.ppermute(shard, ('row', 'col'), pairs)]
    ppermute x43, starting transfers between devices: 47.5 us -> 35.1 us  [swapped(): return lax.ppermute(shard, ('row', 'col'), pairs)]
    ppermute x18, waiting for transfers between devices: 12.1 us -> 9.62 us  [meeting(): lax.ppermute(shard, axis, pairs)]
  transfers between devices with their start and end apart: 61 -> 61, of which waited for: 29 -> 34; matrix products, arithmetic and copies ran while one was open for 0% -> 0% of each run, Pallas kernels for 11% -> 11%
where the time goes in v13:
time: 127 us
  starting transfers between devices  54.2 us (43%)
  waiting for transfers between devices  48.6 us (38%)
  Pallas kernels  23.7 us (19%)
    ppermute x43, waiting for transfers between devices, swapped(): return lax.ppermute(shard, ('row', 'col'), pairs)  39 us
    ppermute x43, starting transfers between devices, swapped(): return lax.ppermute(shard, ('row', 'col'), pairs)  35.1 us
    pallas_call x34, Pallas kernels, call(): pl.pallas_call(body, out_shape=tuple(((pltpu.HBM if away else pltpu.VMEM)...  23.7 us
    ppermute x18, starting transfers between devices, meeting(): lax.ppermute(shard, axis, pairs)  19.1 us
    ppermute x18, waiting for transfers between devices, meeting(): lax.ppermute(shard, axis, pairs)  9.62 us
  transfers between devices with their start and end apart: 61, of which 34 were waited for; matrix products, arithmetic and copies ran while one was open for 0% of the time, Pallas kernels for 11%

profile of v13, /device:TPU:0, one launch (start us, length us, event | category | flops | bytes accessed | tf_op | source)
XLA Modules:
  0.0 127.0 jit_solution(3975972441455708370)
XLA Ops:
  0.0 1.8 %select.1 = (f32[1024,256]{1,0:T(8,128)S(1)}, bf16[1024,256]{1,0:T(8,128)(2,1)S(1)}, bf16[512,1024]{1,0:T(8,128)(2,1)S(1)}, s32[4,128]{1,0:T(4,128)S(1)}, bf16[3...) custom-call(f32[1024,256]{1,0:T(8,128)} %bitcast.11, ...), custom_call_target="tpu_custom_call" | custom-call | flops 268435456 | bytes 1148944 | tf_op jit(solution)/shard_map/select/pallas_call | solution.py:28
  2.3 4.0 %collective-permute-start.1 = (bf16[128,256]{1,0:T(8,128)(2,1)S(1)}, bf16[128,256]{1,0:T(8,128)(2,1)S(1)}, u32[]{:S(2)}, u32[]{:S(2)}) collective-permute-start(bf16[128,256]{1,0:T(8,128)(2,1)S(1)} %get-tuple-element.96), channel_id=1, source_target_pairs={{0,4},{1,5},{2,6},{3,7},{4,0},{5,1},{6,2},{7,3},{8,12},{9,13},{10,... | collective-permute-start | bytes 196616 | tf_op jit(solution)/shard_map/ppermute | solution.py:304
  6.4 1.6 %collective-permute-start.3 = (bf16[128,256]{1,0:T(8,128)(2,1)S(1)}, bf16[128,256]{1,0:T(8,128)(2,1)S(1)}, u32[]{:S(2)}, u32[]{:S(2)}) collective-permute-start(bf16[128,256]{1,0:T(8,128)(2,1)S(1)} %get-tuple-element.98), channel_id=1, source_target_pairs={{0,1},{1,0},{2,3},{3,2},{4,5},{5,4},{6,7},{7,6},{8,9},{9,8},{10,11... | collective-permute-start | bytes 196616 | tf_op jit(solution)/shard_map/ppermute | solution.py:304
  8.6 2.0 %collective-permute-done.2.g2 = bf16[128,256]{1,0:T(8,128)(2,1)S(1)} collective-permute-done((bf16[128,256]{1,0:T(8,128)(2,1)S(1)}, bf16[128,256]{1,0:T(8,128)(2,1)S(1)}, u32[]{:S(2)}, u32[]{:S(2)}) %collective-permute-start.2) | collective-permute-done | bytes 65568 | tf_op jit(solution)/shard_map/ppermute | solution.py:304
  10.9 1.2 collective-permute-start.5
  12.8 1.3 %collective-permute-done.6.refs_3_ = bf16[32,256]{1,0:T(8,128)(2,1)S(1)} collective-permute-done((bf16[32,256]{1,0:T(8,128)(2,1)S(1)}, bf16[32,256]{1,0:T(8,128)(2,1)S(1)}, u32[]{:S(2)}, u32[]{:S(2)}) %collective-permute-start.6) | collective-permute-done | bytes 16416 | tf_op jit(solution)/shard_map/ppermute | solution.py:175
  15.1 4.0 %collective-permute-start.7 = (bf16[64,256]{1,0:T(8,128)(2,1)S(1)}, bf16[64,256]{1,0:T(8,128)(2,1)S(1)}, u32[]{:S(2)}, u32[]{:S(2)}) collective-permute-start(bf16[64,256]{1,0:T(8,128)(2,1)S(1)} %get-tuple-element.101), channel_id=1, source_target_pairs={{0,24},{4,28},{8,16},{12,20},{16,8},{20,12},{24,0},{28,4},{1,25},{... | collective-permute-start | bytes 98312 | tf_op jit(solution)/shard_map/ppermute | solution.py:175
  19.7 3.5 %inverse_own.3 = (bf16[1536,1536]{1,0:T(8,128)(2,1)S(1)}, f32[1536,256]{1,0:T(8,128)S(1)}) custom-call(bf16[1536,1536]{1,0:T(8,128)(2,1)} %bitcast.9, bf16[1024,256]{1,0:T(8,128)(2,1)S(1)} %get-tuple-element.92.owned), custom_call_target="tpu_custom_call" | custom-call | flops 805306368 | bytes 5242880 | tf_op jit(solution)/shard_map/inverse_own/pallas_call | solution.py:28
  23.9 1.1 collective-permute-start.10
  25.7 2.1 %collective-permute-done.10.theirs = bf16[32,256]{1,0:T(8,128)(2,1)S(1)} collective-permute-done((bf16[32,256]{1,0:T(8,128)(2,1)S(1)}, bf16[32,256]{1,0:T(8,128)(2,1)S(1)}, u32[]{:S(2)}, u32[]{:S(2)}) %collective-permute-start.10) | collective-permute-done | bytes 16416 | tf_op jit(solution)/shard_map/ppermute | solution.py:304
  28.1 2.3 %collective-permute-start.12 = (bf16[128,256]{1,0:T(8,128)(2,1)S(1)}, bf16[128,256]{1,0:T(8,128)(2,1)S(1)}, u32[]{:S(2)}, u32[]{:S(2)}) collective-permute-start(bf16[128,256]{1,0:T(8,128)(2,1)S(1)} %get-tuple-element.117), channel_id=1, source_target_pairs={{0,4},{1,5},{2,6},{3,7},{4,0},{5,1},{6,2},{7,3},{8,12},{9,13},{10,... | collective-permute-start | bytes 196616 | tf_op jit(solution)/shard_map/ppermute | solution.py:304
  30.8 2.6 %spread.1 = (bf16[1024,512]{1,0:T(8,128)(2,1)S(1)}, bf16[1536,1536]{1,0:T(8,128)(2,1)S(1)}) custom-call(bf16[1536,1536]{1,0:T(8,128)(2,1)} %bitcast.10, s32[4,128]{1,0:T(4,128)S(1)} %get-tuple-element.114.masked), custom_call_target="tpu_custom_call" | custom-call | bytes 4720640 | tf_op jit(solution)/shard_map/spread/pallas_call | solution.py:28
  35.5 3.2 %collective-permute-start.16 = (bf16[128,256]{1,0:T(8,128)(2,1)S(1)}, bf16[128,256]{1,0:T(8,128)(2,1)S(1)}, u32[]{:S(2)}, u32[]{:S(2)}) collective-permute-start(bf16[128,256]{1,0:T(8,128)(2,1)S(1)} %get-tuple-element.126), channel_id=1, source_target_pairs={{0,4},{1,5},{2,6},{3,7},{4,0},{5,1},{6,2},{7,3},{8,12},{9,13},{10,... | collective-permute-start | bytes 196616 | tf_op jit(solution)/shard_map/ppermute | solution.py:304
  39.8 1.2 collective-permute-done.16.g1
  41.0 2.0 %collective-permute-done.17.g2 = bf16[128,256]{1,0:T(8,128)(2,1)S(1)} collective-permute-done((bf16[128,256]{1,0:T(8,128)(2,1)S(1)}, bf16[128,256]{1,0:T(8,128)(2,1)S(1)}, u32[]{:S(2)}, u32[]{:S(2)}) %collective-permute-start.17) | collective-permute-done | bytes 65568 | tf_op jit(solution)/shard_map/ppermute | solution.py:304
  43.4 3.1 %collective-permute-start.20 = (bf16[128,256]{1,0:T(8,128)(2,1)S(1)}, bf16[128,256]{1,0:T(8,128)(2,1)S(1)}, u32[]{:S(2)}, u32[]{:S(2)}) collective-permute-start(bf16[128,256]{1,0:T(8,128)(2,1)S(1)} %get-tuple-element.130), channel_id=1, source_target_pairs={{0,4},{1,5},{2,6},{3,7},{4,0},{5,1},{6,2},{7,3},{8,12},{9,13},{10,... | collective-permute-start | bytes 196616 | tf_op jit(solution)/shard_map/ppermute | solution.py:304
  46.6 2.2 %collective-permute-done.20.r1 = bf16[128,256]{1,0:T(8,128)(2,1)S(1)} collective-permute-done((bf16[128,256]{1,0:T(8,128)(2,1)S(1)}, bf16[128,256]{1,0:T(8,128)(2,1)S(1)}, u32[]{:S(2)}, u32[]{:S(2)}) %collective-permute-start.20) | collective-permute-done | bytes 65568 | tf_op jit(solution)/shard_map/ppermute | solution.py:304
  49.4 1.4 %collective-permute-done.21.r2 = bf16[128,256]{1,0:T(8,128)(2,1)S(1)} collective-permute-done((bf16[128,256]{1,0:T(8,128)(2,1)S(1)}, bf16[128,256]{1,0:T(8,128)(2,1)S(1)}, u32[]{:S(2)}, u32[]{:S(2)}) %collective-permute-start.21) | collective-permute-done | bytes 65568 | tf_op jit(solution)/shard_map/ppermute | solution.py:304
  51.8 2.1 %collective-permute-start.24 = (bf16[128,256]{1,0:T(8,128)(2,1)S(1)}, bf16[128,256]{1,0:T(8,128)(2,1)S(1)}, u32[]{:S(2)}, u32[]{:S(2)}) collective-permute-start(bf16[128,256]{1,0:T(8,128)(2,1)S(1)} %get-tuple-element.135), channel_id=1, source_target_pairs={{0,4},{1,5},{2,6},{3,7},{4,0},{5,1},{6,2},{7,3},{8,12},{9,13},{10,... | collective-permute-start | bytes 196616 | tf_op jit(solution)/shard_map/ppermute | solution.py:304
  54.0 2.3 %collective-permute-done.24.g1 = bf16[128,256]{1,0:T(8,128)(2,1)S(1)} collective-permute-done((bf16[128,256]{1,0:T(8,128)(2,1)S(1)}, bf16[128,256]{1,0:T(8,128)(2,1)S(1)}, u32[]{:S(2)}, u32[]{:S(2)}) %collective-permute-start.24) | collective-permute-done | bytes 65568 | tf_op jit(solution)/shard_map/ppermute | solution.py:304
  56.3 1.9 %collective-permute-done.25.g2 = bf16[128,256]{1,0:T(8,128)(2,1)S(1)} collective-permute-done((bf16[128,256]{1,0:T(8,128)(2,1)S(1)}, bf16[128,256]{1,0:T(8,128)(2,1)S(1)}, u32[]{:S(2)}, u32[]{:S(2)}) %collective-permute-start.25) | collective-permute-done | bytes 65568 | tf_op jit(solution)/shard_map/ppermute | solution.py:304
  58.5 1.8 %collective-permute-start.27 = (bf16[32,256]{1,0:T(8,128)(2,1)S(1)}, bf16[32,256]{1,0:T(8,128)(2,1)S(1)}, u32[]{:S(2)}, u32[]{:S(2)}) collective-permute-start(bf16[32,256]{1,0:T(8,128)(2,1)S(1)} %restrict.4.refs_0_), channel_id=1, source_target_pairs={{0,1},{1,0},{2,3},{3,2},{4,5},{5,4},{6,7},{7,6},{8,9},{9,8},{10,11... | collective-permute-start | bytes 49160 | tf_op jit(solution)/shard_map/ppermute | solution.py:175
  60.3 1.3 %collective-permute-done.29.refs_3_ = bf16[32,256]{1,0:T(8,128)(2,1)S(1)} collective-permute-done((bf16[32,256]{1,0:T(8,128)(2,1)S(1)}, bf16[32,256]{1,0:T(8,128)(2,1)S(1)}, u32[]{:S(2)}, u32[]{:S(2)}) %collective-permute-start.29) | collective-permute-done | bytes 16416 | tf_op jit(solution)/shard_map/ppermute | solution.py:175
  62.4 2.0 %collective-permute-start.30 = (bf16[64,256]{1,0:T(8,128)(2,1)S(1)}, bf16[64,256]{1,0:T(8,128)(2,1)S(1)}, u32[]{:S(2)}, u32[]{:S(2)}) collective-permute-start(bf16[64,256]{1,0:T(8,128)(2,1)S(1)} %get-tuple-element.139), channel_id=1, source_target_pairs={{0,24},{4,28},{8,16},{12,20},{16,8},{20,12},{24,0},{28,4},{1,25},{... | collective-permute-start | bytes 98312 | tf_op jit(solution)/shard_map/ppermute | solution.py:175
  65.3 1.6 %collective-permute-start.32 = (bf16[64,256]{1,0:T(8,128)(2,1)S(1)}, bf16[64,256]{1,0:T(8,128)(2,1)S(1)}, u32[]{:S(2)}, u32[]{:S(2)}) collective-permute-start(bf16[64,256]{1,0:T(8,128)(2,1)S(1)} %get-tuple-element.141), channel_id=1, source_target_pairs={{0,8},{4,12},{8,0},{12,4},{16,24},{20,28},{24,16},{28,20},{1,9},{5... | collective-permute-start | bytes 98312 | tf_op jit(solution)/shard_map/ppermute | solution.py:175
  68.2 1.2 collective-permute-done.31.refs_1_
  71.2 2.2 %collective-permute-done.33.theirs = bf16[32,256]{1,0:T(8,128)(2,1)S(1)} collective-permute-done((bf16[32,256]{1,0:T(8,128)(2,1)S(1)}, bf16[32,256]{1,0:T(8,128)(2,1)S(1)}, u32[]{:S(2)}, u32[]{:S(2)}) %collective-permute-start.33) | collective-permute-done | bytes 16416 | tf_op jit(solution)/shard_map/ppermute | solution.py:304
  73.7 2.7 %collective-permute-start.35 = (bf16[128,256]{1,0:T(8,128)(2,1)S(1)}, bf16[128,256]{1,0:T(8,128)(2,1)S(1)}, u32[]{:S(2)}, u32[]{:S(2)}) collective-permute-start(bf16[128,256]{1,0:T(8,128)(2,1)S(1)} %get-tuple-element.148), channel_id=1, source_target_pairs={{0,4},{1,5},{2,6},{3,7},{4,0},{5,1},{6,2},{7,3},{8,12},{9,13},{10,... | collective-permute-start | bytes 196616 | tf_op jit(solution)/shard_map/ppermute | solution.py:304
  76.6 2.0 %collective-permute-done.35.refs_6_ = bf16[128,256]{1,0:T(8,128)(2,1)S(1)} collective-permute-done((bf16[128,256]{1,0:T(8,128)(2,1)S(1)}, bf16[128,256]{1,0:T(8,128)(2,1)S(1)}, u32[]{:S(2)}, u32[]{:S(2)}) %collective-permute-start.35) | collective-permute-done | bytes 65568 | tf_op jit(solution)/shard_map/ppermute | solution.py:304
  79.1 1.5 %collective-permute-done.36.r2 = bf16[128,256]{1,0:T(8,128)(2,1)S(1)} collective-permute-done((bf16[128,256]{1,0:T(8,128)(2,1)S(1)}, bf16[128,256]{1,0:T(8,128)(2,1)S(1)}, u32[]{:S(2)}, u32[]{:S(2)}) %collective-permute-start.36) | collective-permute-done | bytes 65568 | tf_op jit(solution)/shard_map/ppermute | solution.py:304
  81.6 2.5 %collective-permute-start.39 = (bf16[128,256]{1,0:T(8,128)(2,1)S(1)}, bf16[128,256]{1,0:T(8,128)(2,1)S(1)}, u32[]{:S(2)}, u32[]{:S(2)}) collective-permute-start(bf16[128,256]{1,0:T(8,128)(2,1)S(1)} %get-tuple-element.154), channel_id=1, source_target_pairs={{0,4},{1,5},{2,6},{3,7},{4,0},{5,1},{6,2},{7,3},{8,12},{9,13},{10,... | collective-permute-start | bytes 196616 | tf_op jit(solution)/shard_map/ppermute | solution.py:304
  84.1 1.2 operator_own.3.partial
  86.3 2.0 %collective-permute-done.40.g2 = bf16[128,256]{1,0:T(8,128)(2,1)S(1)} collective-permute-done((bf16[128,256]{1,0:T(8,128)(2,1)S(1)}, bf16[128,256]{1,0:T(8,128)(2,1)S(1)}, u32[]{:S(2)}, u32[]{:S(2)}) %collective-permute-start.40) | collective-permute-done | bytes 65568 | tf_op jit(solution)/shard_map/ppermute | solution.py:304
  88.7 2.3 %collective-permute-start.43 = (bf16[128,256]{1,0:T(8,128)(2,1)S(1)}, bf16[128,256]{1,0:T(8,128)(2,1)S(1)}, u32[]{:S(2)}, u32[]{:S(2)}) collective-permute-start(bf16[128,256]{1,0:T(8,128)(2,1)S(1)} %get-tuple-element.158), channel_id=1, source_target_pairs={{0,4},{1,5},{2,6},{3,7},{4,0},{5,1},{6,2},{7,3},{8,12},{9,13},{10,... | collective-permute-start | bytes 196616 | tf_op jit(solution)/shard_map/ppermute | solution.py:304
  91.0 2.2 %collective-permute-done.43.r1 = bf16[128,256]{1,0:T(8,128)(2,1)S(1)} collective-permute-done((bf16[128,256]{1,0:T(8,128)(2,1)S(1)}, bf16[128,256]{1,0:T(8,128)(2,1)S(1)}, u32[]{:S(2)}, u32[]{:S(2)}) %collective-permute-start.43) | collective-permute-done | bytes 65568 | tf_op jit(solution)/shard_map/ppermute | solution.py:304
  93.8 1.4 %collective-permute-done.44.r2 = bf16[128,256]{1,0:T(8,128)(2,1)S(1)} collective-permute-done((bf16[128,256]{1,0:T(8,128)(2,1)S(1)}, bf16[128,256]{1,0:T(8,128)(2,1)S(1)}, u32[]{:S(2)}, u32[]{:S(2)}) %collective-permute-start.44) | collective-permute-done | bytes 65568 | tf_op jit(solution)/shard_map/ppermute | solution.py:304
  96.2 2.6 %collective-permute-start.47 = (bf16[128,256]{1,0:T(8,128)(2,1)S(1)}, bf16[128,256]{1,0:T(8,128)(2,1)S(1)}, u32[]{:S(2)}, u32[]{:S(2)}) collective-permute-start(bf16[128,256]{1,0:T(8,128)(2,1)S(1)} %get-tuple-element.163), channel_id=1, source_target_pairs={{0,4},{1,5},{2,6},{3,7},{4,0},{5,1},{6,2},{7,3},{8,12},{9,13},{10,... | collective-permute-start | bytes 196616 | tf_op jit(solution)/shard_map/ppermute | solution.py:304
  98.9 2.2 %collective-permute-done.47.g1 = bf16[128,256]{1,0:T(8,128)(2,1)S(1)} collective-permute-done((bf16[128,256]{1,0:T(8,128)(2,1)S(1)}, bf16[128,256]{1,0:T(8,128)(2,1)S(1)}, u32[]{:S(2)}, u32[]{:S(2)}) %collective-permute-start.47) | collective-permute-done | bytes 65568 | tf_op jit(solution)/shard_map/ppermute | solution.py:304
  101.1 2.0 %collective-permute-done.48.g2 = bf16[128,256]{1,0:T(8,128)(2,1)S(1)} collective-permute-done((bf16[128,256]{1,0:T(8,128)(2,1)S(1)}, bf16[128,256]{1,0:T(8,128)(2,1)S(1)}, u32[]{:S(2)}, u32[]{:S(2)}) %collective-permute-start.48) | collective-permute-done | bytes 65568 | tf_op jit(solution)/shard_map/ppermute | solution.py:304
  103.4 1.8 %collective-permute-start.50 = (bf16[32,256]{1,0:T(8,128)(2,1)S(1)}, bf16[32,256]{1,0:T(8,128)(2,1)S(1)}, u32[]{:S(2)}, u32[]{:S(2)}) collective-permute-start(bf16[32,256]{1,0:T(8,128)(2,1)S(1)} %restrict.5.refs_0_), channel_id=1, source_target_pairs={{0,1},{1,0},{2,3},{3,2},{4,5},{5,4},{6,7},{7,6},{8,9},{9,8},{10,11... | collective-permute-start | bytes 49160 | tf_op jit(solution)/shard_map/ppermute | solution.py:175
  105.2 1.3 %collective-permute-done.52.refs_3_ = bf16[32,256]{1,0:T(8,128)(2,1)S(1)} collective-permute-done((bf16[32,256]{1,0:T(8,128)(2,1)S(1)}, bf16[32,256]{1,0:T(8,128)(2,1)S(1)}, u32[]{:S(2)}, u32[]{:S(2)}) %collective-permute-start.52) | collective-permute-done | bytes 16416 | tf_op jit(solution)/shard_map/ppermute | solution.py:175
  107.4 1.5 %collective-permute-start.53 = (bf16[64,256]{1,0:T(8,128)(2,1)S(1)}, bf16[64,256]{1,0:T(8,128)(2,1)S(1)}, u32[]{:S(2)}, u32[]{:S(2)}) collective-permute-start(bf16[64,256]{1,0:T(8,128)(2,1)S(1)} %get-tuple-element.167), channel_id=1, source_target_pairs={{0,24},{4,28},{8,16},{12,20},{16,8},{20,12},{24,0},{28,4},{1,25},{... | collective-permute-start | bytes 98312 | tf_op jit(solution)/shard_map/ppermute | solution.py:175
  109.7 2.1 %collective-permute-start.55 = (bf16[64,256]{1,0:T(8,128)(2,1)S(1)}, bf16[64,256]{1,0:T(8,128)(2,1)S(1)}, u32[]{:S(2)}, u32[]{:S(2)}) collective-permute-start(bf16[64,256]{1,0:T(8,128)(2,1)S(1)} %get-tuple-element.169), channel_id=1, source_target_pairs={{0,8},{4,12},{8,0},{12,4},{16,24},{20,28},{24,16},{28,20},{1,9},{5... | collective-permute-start | bytes 98312 | tf_op jit(solution)/shard_map/ppermute | solution.py:175
  115.7 2.2 %collective-permute-done.56.theirs = bf16[32,256]{1,0:T(8,128)(2,1)S(1)} collective-permute-done((bf16[32,256]{1,0:T(8,128)(2,1)S(1)}, bf16[32,256]{1,0:T(8,128)(2,1)S(1)}, u32[]{:S(2)}, u32[]{:S(2)}) %collective-permute-start.56) | collective-permute-done | bytes 16416 | tf_op jit(solution)/shard_map/ppermute | solution.py:304
  118.2 3.1 %collective-permute-start.58 = (bf16[128,256]{1,0:T(8,128)(2,1)S(1)}, bf16[128,256]{1,0:T(8,128)(2,1)S(1)}, u32[]{:S(2)}, u32[]{:S(2)}) collective-permute-start(bf16[128,256]{1,0:T(8,128)(2,1)S(1)} %get-tuple-element.176), channel_id=1, source_target_pairs={{0,4},{1,5},{2,6},{3,7},{4,0},{5,1},{6,2},{7,3},{8,12},{9,13},{10,... | collective-permute-start | bytes 196616 | tf_op jit(solution)/shard_map/ppermute | solution.py:304
  121.6 2.0 %collective-permute-done.58.refs_6_ = bf16[128,256]{1,0:T(8,128)(2,1)S(1)} collective-permute-done((bf16[128,256]{1,0:T(8,128)(2,1)S(1)}, bf16[128,256]{1,0:T(8,128)(2,1)S(1)}, u32[]{:S(2)}, u32[]{:S(2)}) %collective-permute-start.58) | collective-permute-done | bytes 65568 | tf_op jit(solution)/shard_map/ppermute | solution.py:304
  124.1 1.5 %collective-permute-done.59.r2 = bf16[128,256]{1,0:T(8,128)(2,1)S(1)} collective-permute-done((bf16[128,256]{1,0:T(8,128)(2,1)S(1)}, bf16[128,256]{1,0:T(8,128)(2,1)S(1)}, u32[]{:S(2)}, u32[]{:S(2)}) %collective-permute-start.59) | collective-permute-done | bytes 65568 | tf_op jit(solution)/shard_map/ppermute | solution.py:304
  125.6 1.2 last_update.1
  (110 shorter events, 28.0 us)
Async XLA Ops:
  1.8 6.2 %collective-permute-start = (bf16[128,256]{1,0:T(8,128)(2,1)S(1)}, bf16[128,256]{1,0:T(8,128)(2,1)S(1)}, u32[]{:S(2)}, u32[]{:S(2)}) collective-permute-start(bf16[128,256]{1,0:T(8,128)(2,1)S(1)} %get-tuple-element.95), channel_id=1, source_target_pairs={{0,1},{1,0},{2,3},{3,2},{4,8},{5,9},{6,10},{7,11},{8,4},{9,5},{10,... | collective-permute-start | bytes 196616 | tf_op jit(solution)/shard_map/ppermute | solution.py:304
  2.3 6.3 %collective-permute-start.1 = (bf16[128,256]{1,0:T(8,128)(2,1)S(1)}, bf16[128,256]{1,0:T(8,128)(2,1)S(1)}, u32[]{:S(2)}, u32[]{:S(2)}) collective-permute-start(bf16[128,256]{1,0:T(8,128)(2,1)S(1)} %get-tuple-element.96), channel_id=1, source_target_pairs={{0,4},{1,5},{2,6},{3,7},{4,0},{5,1},{6,2},{7,3},{8,12},{9,13},{10,... | collective-permute-start | bytes 196616 | tf_op jit(solution)/shard_map/ppermute | solution.py:304
  6.4 4.3 %collective-permute-start.2 = (bf16[128,256]{1,0:T(8,128)(2,1)S(1)}, bf16[128,256]{1,0:T(8,128)(2,1)S(1)}, u32[]{:S(2)}, u32[]{:S(2)}) collective-permute-start(bf16[128,256]{1,0:T(8,128)(2,1)S(1)} %get-tuple-element.97), channel_id=1, source_target_pairs={{0,4},{1,2},{2,1},{3,7},{4,0},{5,6},{6,5},{7,3},{8,12},{9,10},{10,... | collective-permute-start | bytes 196616 | tf_op jit(solution)/shard_map/ppermute | solution.py:304
  6.4 4.2 %collective-permute-start.3 = (bf16[128,256]{1,0:T(8,128)(2,1)S(1)}, bf16[128,256]{1,0:T(8,128)(2,1)S(1)}, u32[]{:S(2)}, u32[]{:S(2)}) collective-permute-start(bf16[128,256]{1,0:T(8,128)(2,1)S(1)} %get-tuple-element.98), channel_id=1, source_target_pairs={{0,1},{1,0},{2,3},{3,2},{4,5},{5,4},{6,7},{7,6},{8,9},{9,8},{10,11... | collective-permute-start | bytes 196616 | tf_op jit(solution)/shard_map/ppermute | solution.py:304
  10.9 4.0 %collective-permute-start.5 = (bf16[32,256]{1,0:T(8,128)(2,1)S(1)}, bf16[32,256]{1,0:T(8,128)(2,1)S(1)}, u32[]{:S(2)}, u32[]{:S(2)}) collective-permute-start(bf16[32,256]{1,0:T(8,128)(2,1)S(1)} %restrict.3.refs_0_), channel_id=1, source_target_pairs={{0,2},{1,3},{2,0},{3,1},{4,6},{5,7},{6,4},{7,5},{8,10},{9,11},{10,... | collective-permute-start | bytes 49160 | tf_op jit(solution)/shard_map/ppermute | solution.py:175
  15.1 8.2 %collective-permute-start.7 = (bf16[64,256]{1,0:T(8,128)(2,1)S(1)}, bf16[64,256]{1,0:T(8,128)(2,1)S(1)}, u32[]{:S(2)}, u32[]{:S(2)}) collective-permute-start(bf16[64,256]{1,0:T(8,128)(2,1)S(1)} %get-tuple-element.101), channel_id=1, source_target_pairs={{0,24},{4,28},{8,16},{12,20},{16,8},{20,12},{24,0},{28,4},{1,25},{... | collective-permute-start | bytes 98312 | tf_op jit(solution)/shard_map/ppermute | solution.py:175
  19.1 4.8 %collective-permute-start.8 = (bf16[64,256]{1,0:T(8,128)(2,1)S(1)}, bf16[64,256]{1,0:T(8,128)(2,1)S(1)}, u32[]{:S(2)}, u32[]{:S(2)}) collective-permute-start(bf16[64,256]{1,0:T(8,128)(2,1)S(1)} %get-tuple-element.102), channel_id=1, source_target_pairs={{0,16},{4,20},{8,24},{12,28},{16,0},{20,4},{24,8},{28,12},{1,17},{... | collective-permute-start | bytes 98312 | tf_op jit(solution)/shard_map/ppermute | solution.py:175
  19.1 4.8 %collective-permute-start.9 = (bf16[64,256]{1,0:T(8,128)(2,1)S(1)}, bf16[64,256]{1,0:T(8,128)(2,1)S(1)}, u32[]{:S(2)}, u32[]{:S(2)}) collective-permute-start(bf16[64,256]{1,0:T(8,128)(2,1)S(1)} %get-tuple-element.103), channel_id=1, source_target_pairs={{0,8},{4,12},{8,0},{12,4},{16,24},{20,28},{24,16},{28,20},{1,9},{5... | collective-permute-start | bytes 98312 | tf_op jit(solution)/shard_map/ppermute | solution.py:175
  23.9 3.8 %collective-permute-start.10 = (bf16[32,256]{1,0:T(8,128)(2,1)S(1)}, bf16[32,256]{1,0:T(8,128)(2,1)S(1)}, u32[]{:S(2)}, u32[]{:S(2)}) collective-permute-start(bf16[32,256]{1,0:T(8,128)(2,1)S(1)} %get-tuple-element.106), channel_id=1, source_target_pairs={{0,4},{1,5},{2,6},{3,7},{4,0},{5,1},{6,2},{7,3},{8,12},{9,13},{10,... | collective-permute-start | bytes 49160 | tf_op jit(solution)/shard_map/ppermute | solution.py:304
  28.0 5.4 %collective-permute-start.11 = (bf16[128,256]{1,0:T(8,128)(2,1)S(1)}, bf16[128,256]{1,0:T(8,128)(2,1)S(1)}, u32[]{:S(2)}, u32[]{:S(2)}) collective-permute-start(bf16[128,256]{1,0:T(8,128)(2,1)S(1)} %get-tuple-element.116), channel_id=1, source_target_pairs={{0,1},{1,0},{2,3},{3,2},{4,8},{5,9},{6,10},{7,11},{8,4},{9,5},{10,... | collective-permute-start | bytes 196616 | tf_op jit(solution)/shard_map/ppermute | solution.py:304
  28.1 5.3 %collective-permute-start.12 = (bf16[128,256]{1,0:T(8,128)(2,1)S(1)}, bf16[128,256]{1,0:T(8,128)(2,1)S(1)}, u32[]{:S(2)}, u32[]{:S(2)}) collective-permute-start(bf16[128,256]{1,0:T(8,128)(2,1)S(1)} %get-tuple-element.117), channel_id=1, source_target_pairs={{0,4},{1,5},{2,6},{3,7},{4,0},{5,1},{6,2},{7,3},{8,12},{9,13},{10,... | collective-permute-start | bytes 196616 | tf_op jit(solution)/shard_map/ppermute | solution.py:304
  30.3 4.3 %collective-permute-start.13 = (bf16[128,256]{1,0:T(8,128)(2,1)S(1)}, bf16[128,256]{1,0:T(8,128)(2,1)S(1)}, u32[]{:S(2)}, u32[]{:S(2)}) collective-permute-start(bf16[128,256]{1,0:T(8,128)(2,1)S(1)} %get-tuple-element.119), channel_id=1, source_target_pairs={{0,4},{1,2},{2,1},{3,7},{4,0},{5,6},{6,5},{7,3},{8,12},{9,10},{10,... | collective-permute-start | bytes 196616 | tf_op jit(solution)/shard_map/ppermute | solution.py:304
  30.4 4.2 %collective-permute-start.14 = (bf16[128,256]{1,0:T(8,128)(2,1)S(1)}, bf16[128,256]{1,0:T(8,128)(2,1)S(1)}, u32[]{:S(2)}, u32[]{:S(2)}) collective-permute-start(bf16[128,256]{1,0:T(8,128)(2,1)S(1)} %get-tuple-element.120), channel_id=1, source_target_pairs={{0,1},{1,0},{2,3},{3,2},{4,5},{5,4},{6,7},{7,6},{8,9},{9,8},{10,11... | collective-permute-start | bytes 196616 | tf_op jit(solution)/shard_map/ppermute | solution.py:304
  35.4 4.3 %collective-permute-start.15 = (bf16[128,256]{1,0:T(8,128)(2,1)S(1)}, bf16[128,256]{1,0:T(8,128)(2,1)S(1)}, u32[]{:S(2)}, u32[]{:S(2)}) collective-permute-start(bf16[128,256]{1,0:T(8,128)(2,1)S(1)} %get-tuple-element.125), channel_id=1, source_target_pairs={{0,1},{1,0},{2,3},{3,2},{4,8},{5,9},{6,10},{7,11},{8,4},{9,5},{10,... | collective-permute-start | bytes 196616 | tf_op jit(solution)/shard_map/ppermute | solution.py:304
  35.5 5.5 %collective-permute-start.16 = (bf16[128,256]{1,0:T(8,128)(2,1)S(1)}, bf16[128,256]{1,0:T(8,128)(2,1)S(1)}, u32[]{:S(2)}, u32[]{:S(2)}) collective-permute-start(bf16[128,256]{1,0:T(8,128)(2,1)S(1)} %get-tuple-element.126), channel_id=1, source_target_pairs={{0,4},{1,5},{2,6},{3,7},{4,0},{5,1},{6,2},{7,3},{8,12},{9,13},{10,... | collective-permute-start | bytes 196616 | tf_op jit(solution)/shard_map/ppermute | solution.py:304
  38.8 4.3 %collective-permute-start.17 = (bf16[128,256]{1,0:T(8,128)(2,1)S(1)}, bf16[128,256]{1,0:T(8,128)(2,1)S(1)}, u32[]{:S(2)}, u32[]{:S(2)}) collective-permute-start(bf16[128,256]{1,0:T(8,128)(2,1)S(1)} %get-tuple-element.127), channel_id=1, source_target_pairs={{0,4},{1,2},{2,1},{3,7},{4,0},{5,6},{6,5},{7,3},{8,12},{9,10},{10,... | collective-permute-start | bytes 196616 | tf_op jit(solution)/shard_map/ppermute | solution.py:304
  38.8 4.2 %collective-permute-start.18 = (bf16[128,256]{1,0:T(8,128)(2,1)S(1)}, bf16[128,256]{1,0:T(8,128)(2,1)S(1)}, u32[]{:S(2)}, u32[]{:S(2)}) collective-permute-start(bf16[128,256]{1,0:T(8,128)(2,1)S(1)} %get-tuple-element.128), channel_id=1, source_target_pairs={{0,1},{1,0},{2,3},{3,2},{4,5},{5,4},{6,7},{7,6},{8,9},{9,8},{10,11... | collective-permute-start | bytes 196616 | tf_op jit(solution)/shard_map/ppermute | solution.py:304
  43.4 5.4 %collective-permute-start.20 = (bf16[128,256]{1,0:T(8,128)(2,1)S(1)}, bf16[128,256]{1,0:T(8,128)(2,1)S(1)}, u32[]{:S(2)}, u32[]{:S(2)}) collective-permute-start(bf16[128,256]{1,0:T(8,128)(2,1)S(1)} %get-tuple-element.130), channel_id=1, source_target_pairs={{0,4},{1,5},{2,6},{3,7},{4,0},{5,1},{6,2},{7,3},{8,12},{9,13},{10,... | collective-permute-start | bytes 196616 | tf_op jit(solution)/shard_map/ppermute | solution.py:304
  46.6 4.3 %collective-permute-start.21 = (bf16[128,256]{1,0:T(8,128)(2,1)S(1)}, bf16[128,256]{1,0:T(8,128)(2,1)S(1)}, u32[]{:S(2)}, u32[]{:S(2)}) collective-permute-start(bf16[128,256]{1,0:T(8,128)(2,1)S(1)} %get-tuple-element.131), channel_id=1, source_target_pairs={{0,4},{1,2},{2,1},{3,7},{4,0},{5,6},{6,5},{7,3},{8,12},{9,10},{10,... | collective-permute-start | bytes 196616 | tf_op jit(solution)/shard_map/ppermute | solution.py:304
  46.6 4.2 %collective-permute-start.22 = (bf16[128,256]{1,0:T(8,128)(2,1)S(1)}, bf16[128,256]{1,0:T(8,128)(2,1)S(1)}, u32[]{:S(2)}, u32[]{:S(2)}) collective-permute-start(bf16[128,256]{1,0:T(8,128)(2,1)S(1)} %get-tuple-element.132), channel_id=1, source_target_pairs={{0,1},{1,0},{2,3},{3,2},{4,5},{5,4},{6,7},{7,6},{8,9},{9,8},{10,11... | collective-permute-start | bytes 196616 | tf_op jit(solution)/shard_map/ppermute | solution.py:304
  51.8 4.5 %collective-permute-start.24 = (bf16[128,256]{1,0:T(8,128)(2,1)S(1)}, bf16[128,256]{1,0:T(8,128)(2,1)S(1)}, u32[]{:S(2)}, u32[]{:S(2)}) collective-permute-start(bf16[128,256]{1,0:T(8,128)(2,1)S(1)} %get-tuple-element.135), channel_id=1, source_target_pairs={{0,4},{1,5},{2,6},{3,7},{4,0},{5,1},{6,2},{7,3},{8,12},{9,13},{10,... | collective-permute-start | bytes 196616 | tf_op jit(solution)/shard_map/ppermute | solution.py:304
  53.9 4.3 %collective-permute-start.25 = (bf16[128,256]{1,0:T(8,128)(2,1)S(1)}, bf16[128,256]{1,0:T(8,128)(2,1)S(1)}, u32[]{:S(2)}, u32[]{:S(2)}) collective-permute-start(bf16[128,256]{1,0:T(8,128)(2,1)S(1)} %get-tuple-element.136), channel_id=1, source_target_pairs={{0,4},{1,2},{2,1},{3,7},{4,0},{5,6},{6,5},{7,3},{8,12},{9,10},{10,... | collective-permute-start | bytes 196616 | tf_op jit(solution)/shard_map/ppermute | solution.py:304
  53.9 4.2 %collective-permute-start.26 = (bf16[128,256]{1,0:T(8,128)(2,1)S(1)}, bf16[128,256]{1,0:T(8,128)(2,1)S(1)}, u32[]{:S(2)}, u32[]{:S(2)}) collective-permute-start(bf16[128,256]{1,0:T(8,128)(2,1)S(1)} %get-tuple-element.137), channel_id=1, source_target_pairs={{0,1},{1,0},{2,3},{3,2},{4,5},{5,4},{6,7},{7,6},{8,9},{9,8},{10,11... | collective-permute-start | bytes 196616 | tf_op jit(solution)/shard_map/ppermute | solution.py:304
  58.4 3.8 %collective-permute-start.28 = (bf16[32,256]{1,0:T(8,128)(2,1)S(1)}, bf16[32,256]{1,0:T(8,128)(2,1)S(1)}, u32[]{:S(2)}, u32[]{:S(2)}) collective-permute-start(bf16[32,256]{1,0:T(8,128)(2,1)S(1)} %restrict.4.refs_0_), channel_id=1, source_target_pairs={{0,2},{1,3},{2,0},{3,1},{4,6},{5,7},{6,4},{7,5},{8,10},{9,11},{10,... | collective-permute-start | bytes 49160 | tf_op jit(solution)/shard_map/ppermute | solution.py:175
  62.4 5.8 %collective-permute-start.30 = (bf16[64,256]{1,0:T(8,128)(2,1)S(1)}, bf16[64,256]{1,0:T(8,128)(2,1)S(1)}, u32[]{:S(2)}, u32[]{:S(2)}) collective-permute-start(bf16[64,256]{1,0:T(8,128)(2,1)S(1)} %get-tuple-element.139), channel_id=1, source_target_pairs={{0,24},{4,28},{8,16},{12,20},{16,8},{20,12},{24,0},{28,4},{1,25},{... | collective-permute-start | bytes 98312 | tf_op jit(solution)/shard_map/ppermute | solution.py:175
  64.4 5.0 %collective-permute-start.31 = (bf16[64,256]{1,0:T(8,128)(2,1)S(1)}, bf16[64,256]{1,0:T(8,128)(2,1)S(1)}, u32[]{:S(2)}, u32[]{:S(2)}) collective-permute-start(bf16[64,256]{1,0:T(8,128)(2,1)S(1)} %get-tuple-element.140), channel_id=1, source_target_pairs={{0,16},{4,20},{8,24},{12,28},{16,0},{20,4},{24,8},{28,12},{1,17},{... | collective-permute-start | bytes 98312 | tf_op jit(solution)/shard_map/ppermute | solution.py:175
  65.3 4.3 %collective-permute-start.32 = (bf16[64,256]{1,0:T(8,128)(2,1)S(1)}, bf16[64,256]{1,0:T(8,128)(2,1)S(1)}, u32[]{:S(2)}, u32[]{:S(2)}) collective-permute-start(bf16[64,256]{1,0:T(8,128)(2,1)S(1)} %get-tuple-element.141), channel_id=1, source_target_pairs={{0,8},{4,12},{8,0},{12,4},{16,24},{20,28},{24,16},{28,20},{1,9},{5... | collective-permute-start | bytes 98312 | tf_op jit(solution)/shard_map/ppermute | solution.py:175
  69.6 3.8 %collective-permute-start.33 = (bf16[32,256]{1,0:T(8,128)(2,1)S(1)}, bf16[32,256]{1,0:T(8,128)(2,1)S(1)}, u32[]{:S(2)}, u32[]{:S(2)}) collective-permute-start(bf16[32,256]{1,0:T(8,128)(2,1)S(1)} %get-tuple-element.144), channel_id=1, source_target_pairs={{0,4},{1,5},{2,6},{3,7},{4,0},{5,1},{6,2},{7,3},{8,12},{9,13},{10,... | collective-permute-start | bytes 49160 | tf_op jit(solution)/shard_map/ppermute | solution.py:304
  73.7 4.9 %collective-permute-start.35 = (bf16[128,256]{1,0:T(8,128)(2,1)S(1)}, bf16[128,256]{1,0:T(8,128)(2,1)S(1)}, u32[]{:S(2)}, u32[]{:S(2)}) collective-permute-start(bf16[128,256]{1,0:T(8,128)(2,1)S(1)} %get-tuple-element.148), channel_id=1, source_target_pairs={{0,4},{1,5},{2,6},{3,7},{4,0},{5,1},{6,2},{7,3},{8,12},{9,13},{10,... | collective-permute-start | bytes 196616 | tf_op jit(solution)/shard_map/ppermute | solution.py:304
  76.4 4.3 %collective-permute-start.36 = (bf16[128,256]{1,0:T(8,128)(2,1)S(1)}, bf16[128,256]{1,0:T(8,128)(2,1)S(1)}, u32[]{:S(2)}, u32[]{:S(2)}) collective-permute-start(bf16[128,256]{1,0:T(8,128)(2,1)S(1)} %get-tuple-element.149), channel_id=1, source_target_pairs={{0,4},{1,2},{2,1},{3,7},{4,0},{5,6},{6,5},{7,3},{8,12},{9,10},{10,... | collective-permute-start | bytes 196616 | tf_op jit(solution)/shard_map/ppermute | solution.py:304
  76.4 4.2 %collective-permute-start.37 = (bf16[128,256]{1,0:T(8,128)(2,1)S(1)}, bf16[128,256]{1,0:T(8,128)(2,1)S(1)}, u32[]{:S(2)}, u32[]{:S(2)}) collective-permute-start(bf16[128,256]{1,0:T(8,128)(2,1)S(1)} %get-tuple-element.150), channel_id=1, source_target_pairs={{0,1},{1,0},{2,3},{3,2},{4,5},{5,4},{6,7},{7,6},{8,9},{9,8},{10,11... | collective-permute-start | bytes 196616 | tf_op jit(solution)/shard_map/ppermute | solution.py:304
  81.6 4.7 %collective-permute-start.39 = (bf16[128,256]{1,0:T(8,128)(2,1)S(1)}, bf16[128,256]{1,0:T(8,128)(2,1)S(1)}, u32[]{:S(2)}, u32[]{:S(2)}) collective-permute-start(bf16[128,256]{1,0:T(8,128)(2,1)S(1)} %get-tuple-element.154), channel_id=1, source_target_pairs={{0,4},{1,5},{2,6},{3,7},{4,0},{5,1},{6,2},{7,3},{8,12},{9,13},{10,... | collective-permute-start | bytes 196616 | tf_op jit(solution)/shard_map/ppermute | solution.py:304
  84.1 4.3 %collective-permute-start.40 = (bf16[128,256]{1,0:T(8,128)(2,1)S(1)}, bf16[128,256]{1,0:T(8,128)(2,1)S(1)}, u32[]{:S(2)}, u32[]{:S(2)}) collective-permute-start(bf16[128,256]{1,0:T(8,128)(2,1)S(1)} %get-tuple-element.155), channel_id=1, source_target_pairs={{0,4},{1,2},{2,1},{3,7},{4,0},{5,6},{6,5},{7,3},{8,12},{9,10},{10,... | collective-permute-start | bytes 196616 | tf_op jit(solution)/shard_map/ppermute | solution.py:304
  84.1 4.2 %collective-permute-start.41 = (bf16[128,256]{1,0:T(8,128)(2,1)S(1)}, bf16[128,256]{1,0:T(8,128)(2,1)S(1)}, u32[]{:S(2)}, u32[]{:S(2)}) collective-permute-start(bf16[128,256]{1,0:T(8,128)(2,1)S(1)} %get-tuple-element.156), channel_id=1, source_target_pairs={{0,1},{1,0},{2,3},{3,2},{4,5},{5,4},{6,7},{7,6},{8,9},{9,8},{10,11... | collective-permute-start | bytes 196616 | tf_op jit(solution)/shard_map/ppermute | solution.py:304
  88.7 4.5 %collective-permute-start.43 = (bf16[128,256]{1,0:T(8,128)(2,1)S(1)}, bf16[128,256]{1,0:T(8,128)(2,1)S(1)}, u32[]{:S(2)}, u32[]{:S(2)}) collective-permute-start(bf16[128,256]{1,0:T(8,128)(2,1)S(1)} %get-tuple-element.158), channel_id=1, source_target_pairs={{0,4},{1,5},{2,6},{3,7},{4,0},{5,1},{6,2},{7,3},{8,12},{9,13},{10,... | collective-permute-start | bytes 196616 | tf_op jit(solution)/shard_map/ppermute | solution.py:304
  91.0 4.3 %collective-permute-start.44 = (bf16[128,256]{1,0:T(8,128)(2,1)S(1)}, bf16[128,256]{1,0:T(8,128)(2,1)S(1)}, u32[]{:S(2)}, u32[]{:S(2)}) collective-permute-start(bf16[128,256]{1,0:T(8,128)(2,1)S(1)} %get-tuple-element.159), channel_id=1, source_target_pairs={{0,4},{1,2},{2,1},{3,7},{4,0},{5,6},{6,5},{7,3},{8,12},{9,10},{10,... | collective-permute-start | bytes 196616 | tf_op jit(solution)/shard_map/ppermute | solution.py:304
  91.0 4.2 %collective-permute-start.45 = (bf16[128,256]{1,0:T(8,128)(2,1)S(1)}, bf16[128,256]{1,0:T(8,128)(2,1)S(1)}, u32[]{:S(2)}, u32[]{:S(2)}) collective-permute-start(bf16[128,256]{1,0:T(8,128)(2,1)S(1)} %get-tuple-element.160), channel_id=1, source_target_pairs={{0,1},{1,0},{2,3},{3,2},{4,5},{5,4},{6,7},{7,6},{8,9},{9,8},{10,11... | collective-permute-start | bytes 196616 | tf_op jit(solution)/shard_map/ppermute | solution.py:304
  96.2 4.9 %collective-permute-start.47 = (bf16[128,256]{1,0:T(8,128)(2,1)S(1)}, bf16[128,256]{1,0:T(8,128)(2,1)S(1)}, u32[]{:S(2)}, u32[]{:S(2)}) collective-permute-start(bf16[128,256]{1,0:T(8,128)(2,1)S(1)} %get-tuple-element.163), channel_id=1, source_target_pairs={{0,4},{1,5},{2,6},{3,7},{4,0},{5,1},{6,2},{7,3},{8,12},{9,13},{10,... | collective-permute-start | bytes 196616 | tf_op jit(solution)/shard_map/ppermute | solution.py:304
  98.8 4.3 %collective-permute-start.48 = (bf16[128,256]{1,0:T(8,128)(2,1)S(1)}, bf16[128,256]{1,0:T(8,128)(2,1)S(1)}, u32[]{:S(2)}, u32[]{:S(2)}) collective-permute-start(bf16[128,256]{1,0:T(8,128)(2,1)S(1)} %get-tuple-element.164), channel_id=1, source_target_pairs={{0,4},{1,2},{2,1},{3,7},{4,0},{5,6},{6,5},{7,3},{8,12},{9,10},{10,... | collective-permute-start | bytes 196616 | tf_op jit(solution)/shard_map/ppermute | solution.py:304
  98.9 4.2 %collective-permute-start.49 = (bf16[128,256]{1,0:T(8,128)(2,1)S(1)}, bf16[128,256]{1,0:T(8,128)(2,1)S(1)}, u32[]{:S(2)}, u32[]{:S(2)}) collective-permute-start(bf16[128,256]{1,0:T(8,128)(2,1)S(1)} %get-tuple-element.165), channel_id=1, source_target_pairs={{0,1},{1,0},{2,3},{3,2},{4,5},{5,4},{6,7},{7,6},{8,9},{9,8},{10,11... | collective-permute-start | bytes 196616 | tf_op jit(solution)/shard_map/ppermute | solution.py:304
  103.4 3.8 %collective-permute-start.51 = (bf16[32,256]{1,0:T(8,128)(2,1)S(1)}, bf16[32,256]{1,0:T(8,128)(2,1)S(1)}, u32[]{:S(2)}, u32[]{:S(2)}) collective-permute-start(bf16[32,256]{1,0:T(8,128)(2,1)S(1)} %restrict.5.refs_0_), channel_id=1, source_target_pairs={{0,2},{1,3},{2,0},{3,1},{4,6},{5,7},{6,4},{7,5},{8,10},{9,11},{10,... | collective-permute-start | bytes 49160 | tf_op jit(solution)/shard_map/ppermute | solution.py:175
  107.4 6.0 %collective-permute-start.53 = (bf16[64,256]{1,0:T(8,128)(2,1)S(1)}, bf16[64,256]{1,0:T(8,128)(2,1)S(1)}, u32[]{:S(2)}, u32[]{:S(2)}) collective-permute-start(bf16[64,256]{1,0:T(8,128)(2,1)S(1)} %get-tuple-element.167), channel_id=1, source_target_pairs={{0,24},{4,28},{8,16},{12,20},{16,8},{20,12},{24,0},{28,4},{1,25},{... | collective-permute-start | bytes 98312 | tf_op jit(solution)/shard_map/ppermute | solution.py:175
  108.8 5.3 %collective-permute-start.54 = (bf16[64,256]{1,0:T(8,128)(2,1)S(1)}, bf16[64,256]{1,0:T(8,128)(2,1)S(1)}, u32[]{:S(2)}, u32[]{:S(2)}) collective-permute-start(bf16[64,256]{1,0:T(8,128)(2,1)S(1)} %get-tuple-element.168), channel_id=1, source_target_pairs={{0,16},{4,20},{8,24},{12,28},{16,0},{20,4},{24,8},{28,12},{1,17},{... | collective-permute-start | bytes 98312 | tf_op jit(solution)/shard_map/ppermute | solution.py:175
  109.7 4.4 %collective-permute-start.55 = (bf16[64,256]{1,0:T(8,128)(2,1)S(1)}, bf16[64,256]{1,0:T(8,128)(2,1)S(1)}, u32[]{:S(2)}, u32[]{:S(2)}) collective-permute-start(bf16[64,256]{1,0:T(8,128)(2,1)S(1)} %get-tuple-element.169), channel_id=1, source_target_pairs={{0,8},{4,12},{8,0},{12,4},{16,24},{20,28},{24,16},{28,20},{1,9},{5... | collective-permute-start | bytes 98312 | tf_op jit(solution)/shard_map/ppermute | solution.py:175
  114.1 3.8 %collective-permute-start.56 = (bf16[32,256]{1,0:T(8,128)(2,1)S(1)}, bf16[32,256]{1,0:T(8,128)(2,1)S(1)}, u32[]{:S(2)}, u32[]{:S(2)}) collective-permute-start(bf16[32,256]{1,0:T(8,128)(2,1)S(1)} %get-tuple-element.172), channel_id=1, source_target_pairs={{0,4},{1,5},{2,6},{3,7},{4,0},{5,1},{6,2},{7,3},{8,12},{9,13},{10,... | collective-permute-start | bytes 49160 | tf_op jit(solution)/shard_map/ppermute | solution.py:304
  118.2 5.3 %collective-permute-start.58 = (bf16[128,256]{1,0:T(8,128)(2,1)S(1)}, bf16[128,256]{1,0:T(8,128)(2,1)S(1)}, u32[]{:S(2)}, u32[]{:S(2)}) collective-permute-start(bf16[128,256]{1,0:T(8,128)(2,1)S(1)} %get-tuple-element.176), channel_id=1, source_target_pairs={{0,4},{1,5},{2,6},{3,7},{4,0},{5,1},{6,2},{7,3},{8,12},{9,13},{10,... | collective-permute-start | bytes 196616 | tf_op jit(solution)/shard_map/ppermute | solution.py:304
  121.3 4.3 %collective-permute-start.59 = (bf16[128,256]{1,0:T(8,128)(2,1)S(1)}, bf16[128,256]{1,0:T(8,128)(2,1)S(1)}, u32[]{:S(2)}, u32[]{:S(2)}) collective-permute-start(bf16[128,256]{1,0:T(8,128)(2,1)S(1)} %get-tuple-element.177), channel_id=1, source_target_pairs={{0,4},{1,2},{2,1},{3,7},{4,0},{5,6},{6,5},{7,3},{8,12},{9,10},{10,... | collective-permute-start | bytes 196616 | tf_op jit(solution)/shard_map/ppermute | solution.py:304
  121.4 4.2 %collective-permute-start.60 = (bf16[128,256]{1,0:T(8,128)(2,1)S(1)}, bf16[128,256]{1,0:T(8,128)(2,1)S(1)}, u32[]{:S(2)}, u32[]{:S(2)}) collective-permute-start(bf16[128,256]{1,0:T(8,128)(2,1)S(1)} %get-tuple-element.178), channel_id=1, source_target_pairs={{0,1},{1,0},{2,3},{3,2},{4,5},{5,4},{6,7},{7,6},{8,9},{9,8},{10,11... | collective-permute-start | bytes 196616 | tf_op jit(solution)/shard_map/ppermute | solution.py:304
  (14 other events, 55.5 us)

commit v14 on v13

--- a/solution.py
+++ b/solution.py
@@ -43,7 +43,7 @@
 
 def directions():
     row, col = parities()
-    return row, 1 - row, 2 + col, 3 - col
+    return 1 - row, row, 2 + col, 3 - col
 
 
 def margin_spans(own, tile):
@@ -93,8 +93,8 @@
     ]
     row, col = parities()
     ordered = (
+        jnp.where(row == 0, listed[1], listed[0]),
         jnp.where(row == 0, listed[0], listed[1]),
-        jnp.where(row == 0, listed[1], listed[0]),
         jnp.where(col == 0, listed[2], listed[3]),
         jnp.where(col == 0, listed[3], listed[2]),
     )
@@ -134,12 +134,11 @@
     return jnp.concatenate([part[...] for part in parts], axis=0)
 
 
-def load_kernel(far, owned, matrix, out, sems):
-    own = owned.shape[0]
+def load_kernel(far, own_like, matrix, sems):
+    own = own_like.shape[0]
     tile = (matrix.shape[0] - own) // 4
     for load in started(matrix_pieces(far, matrix, own, tile), sems):
         load.wait()
-    out[...] = product(matrix[:, :own], owned[...])
 
 
 def own_columns_kernel(matrix, owned, out):
@@ -147,7 +146,8 @@
     out[...] = product(matrix[:, :own], owned[...])
 
 
-def restrict_kernel(basis, owned, g0, g1, g2, g3, out):
+def restrict_kernel(basis, owned, g0, g1, g2, g3, *rest):
+    out = rest[-1]
     own = owned.shape[0]
     out[...] = (
         product(basis[:, :own], owned[...]) + product(basis[:, own:], stacked(g0, g1, g2, g3))
@@ -305,7 +305,8 @@
 
 
 def traded(tiles):
-    return [swapped(tiles[i], "row" if i < 2 else "col", 1 - i % 2) for i in range(4)]
+    ways = (("row", 0), ("row", 1), ("col", 1), ("col", 0))
+    return [swapped(tile, *way) for tile, way in zip(tiles, ways)]
 
 
 def per_device(
@@ -398,25 +399,23 @@
             )
         ghosts = traded(tiles)
         if first:
-            inverse, partial = call(
+            (inverse,) = call(
                 load_kernel,
-                "inverse_own",
-                [(inverse.shape, HALF), local_full],
+                "inverse_load",
+                [(inverse.shape, HALF)],
                 inverse,
                 residual,
                 far=1,
                 scratch=(pltpu.SemaphoreType.DMA((MATRIX_PIECES,)),),
-                flops=2 * local * own * columns,
             )
-        else:
-            (partial,) = call(
-                own_columns_kernel,
-                "inverse_own",
-                [local_full],
-                inverse,
-                residual,
-                flops=2 * local * own * columns,
-            )
+        (partial,) = call(
+            own_columns_kernel,
+            "inverse_own",
+            [local_full],
+            inverse,
+            residual,
+            flops=2 * local * own * columns,
+        )
         (restricted,) = call(
             restrict_kernel,
             "restrict",
@@ -424,6 +423,7 @@
             basis,
             residual,
             *ghosts,
+            *([inverse] if first else []),
             flops=2 * local * coarse * columns,
         )
         restricted = [meeting(restricted, "col", turn) for turn in reversed(range(across))][::-1]

time: 127 us -> 125 us (0.984)
  waiting for transfers between devices: 48.6 us -> 33.8 us
  starting transfers between devices: 54.2 us -> 66.6 us
    ppermute x43, waiting for transfers between devices: 39 us -> 20.5 us  [swapped(): return lax.ppermute(shard, ('row', 'col'), pairs)]
    ppermute x43, starting transfers between devices: 35.1 us -> 47.3 us  [swapped(): return lax.ppermute(shard, ('row', 'col'), pairs)]
    ppermute x18, waiting for transfers between devices: 9.62 us -> 13.3 us  [meeting(): lax.ppermute(shard, axis, pairs)]
    pallas_call x34 -> x35, Pallas kernels: 23.7 us -> 23.7 us  [call(): pl.pallas_call(body, out_shape=tuple(((pltpu.HBM if away else pltpu.VMEM)...]
  transfers between devices with their start and end apart: 61 -> 61, of which waited for: 34 -> 27; matrix products, arithmetic and copies ran while one was open for 0% -> 0% of each run, Pallas kernels for 11% -> 12%
where the time goes in v14:
time: 125 us
  starting transfers between devices  66.6 us (53%)
  waiting for transfers between devices  33.8 us (27%)
  Pallas kernels  23.7 us (19%)
    ppermute x43, starting transfers between devices, swapped(): return lax.ppermute(shard, ('row', 'col'), pairs)  47.3 us
    pallas_call x35, Pallas kernels, call(): pl.pallas_call(body, out_shape=tuple(((pltpu.HBM if away else pltpu.VMEM)...  23.7 us
    ppermute x43, waiting for transfers between devices, swapped(): return lax.ppermute(shard, ('row', 'col'), pairs)  20.5 us
    ppermute x18, starting transfers between devices, meeting(): lax.ppermute(shard, axis, pairs)  19.3 us
    ppermute x18, waiting for transfers between devices, meeting(): lax.ppermute(shard, axis, pairs)  13.3 us
  transfers between devices with their start and end apart: 61, of which 27 were waited for; matrix products, arithmetic and copies ran while one was open for 0% of the time, Pallas kernels for 12%

profile of v14, /device:TPU:0, one launch (start us, length us, event | category | flops | bytes accessed | tf_op | source)
XLA Modules:
  0.0 124.6 jit_solution(12164913426955007935)
XLA Ops:
  0.0 1.8 %select.1 = (f32[1024,256]{1,0:T(8,128)S(1)}, bf16[1024,256]{1,0:T(8,128)(2,1)S(1)}, bf16[512,1024]{1,0:T(8,128)(2,1)S(1)}, s32[4,128]{1,0:T(4,128)S(1)}, bf16[3...) custom-call(f32[1024,256]{1,0:T(8,128)} %bitcast.11, ...), custom_call_target="tpu_custom_call" | custom-call | flops 268435456 | bytes 1148944 | tf_op jit(solution)/shard_map/select/pallas_call | solution.py:28
  1.8 3.0 %collective-permute-start = (bf16[128,256]{1,0:T(8,128)(2,1)S(1)}, bf16[128,256]{1,0:T(8,128)(2,1)S(1)}, u32[]{:S(2)}, u32[]{:S(2)}) collective-permute-start(bf16[128,256]{1,0:T(8,128)(2,1)S(1)} %get-tuple-element.91), channel_id=1, source_target_pairs={{0,4},{1,5},{2,6},{3,7},{4,0},{5,1},{6,2},{7,3},{8,12},{9,13},{10,... | collective-permute-start | bytes 196616 | tf_op jit(solution)/shard_map/ppermute | solution.py:304
  4.8 3.0 %collective-permute-start.2 = (bf16[128,256]{1,0:T(8,128)(2,1)S(1)}, bf16[128,256]{1,0:T(8,128)(2,1)S(1)}, u32[]{:S(2)}, u32[]{:S(2)}) collective-permute-start(bf16[128,256]{1,0:T(8,128)(2,1)S(1)} %get-tuple-element.93), channel_id=1, source_target_pairs={{0,4},{1,2},{2,1},{3,7},{4,0},{5,6},{6,5},{7,3},{8,12},{9,10},{10,... | collective-permute-start | bytes 196616 | tf_op jit(solution)/shard_map/ppermute | solution.py:304
  7.9 2.6 %inverse_load.1.matrix.rest_0_ = bf16[1536,1536]{1,0:T(8,128)(2,1)S(1)} custom-call(bf16[1536,1536]{1,0:T(8,128)(2,1)} %bitcast.9, bf16[1024,256]{1,0:T(8,128)(2,1)S(1)} %get-tuple-element.90.own_like.owned), custom_call_target="tpu_custom_call" | custom-call | bytes 5242880 | tf_op jit(solution)/shard_map/inverse_load/pallas_call | solution.py:28
  10.8 2.1 %collective-permute-start.5 = (bf16[32,256]{1,0:T(8,128)(2,1)S(1)}, bf16[32,256]{1,0:T(8,128)(2,1)S(1)}, u32[]{:S(2)}, u32[]{:S(2)}) collective-permute-start(bf16[32,256]{1,0:T(8,128)(2,1)S(1)} %restrict.3.refs_0_), channel_id=1, source_target_pairs={{0,2},{1,3},{2,0},{3,1},{4,6},{5,7},{6,4},{7,5},{8,10},{9,11},{10,... | collective-permute-start | bytes 49160 | tf_op jit(solution)/shard_map/ppermute | solution.py:175
  15.0 3.1 %collective-permute-start.7 = (bf16[64,256]{1,0:T(8,128)(2,1)S(1)}, bf16[64,256]{1,0:T(8,128)(2,1)S(1)}, u32[]{:S(2)}, u32[]{:S(2)}) collective-permute-start(bf16[64,256]{1,0:T(8,128)(2,1)S(1)} %get-tuple-element.97), channel_id=1, source_target_pairs={{0,24},{4,28},{8,16},{12,20},{16,8},{20,12},{24,0},{28,4},{1,25},{... | collective-permute-start | bytes 98312 | tf_op jit(solution)/shard_map/ppermute | solution.py:175
  18.3 1.2 collective-permute-start.9
  20.8 2.2 %collective-permute-done.8.refs_1_ = bf16[64,256]{1,0:T(8,128)(2,1)S(1)} collective-permute-done((bf16[64,256]{1,0:T(8,128)(2,1)S(1)}, bf16[64,256]{1,0:T(8,128)(2,1)S(1)}, u32[]{:S(2)}, u32[]{:S(2)}) %collective-permute-start.8) | collective-permute-done | bytes 32800 | tf_op jit(solution)/shard_map/ppermute | solution.py:175
  24.6 2.2 %collective-permute-done.10.theirs = bf16[32,256]{1,0:T(8,128)(2,1)S(1)} collective-permute-done((bf16[32,256]{1,0:T(8,128)(2,1)S(1)}, bf16[32,256]{1,0:T(8,128)(2,1)S(1)}, u32[]{:S(2)}, u32[]{:S(2)}) %collective-permute-start.10) | collective-permute-done | bytes 16416 | tf_op jit(solution)/shard_map/ppermute | solution.py:304
  27.1 1.2 collective-permute-start.11
  28.3 2.4 %collective-permute-start.13 = (bf16[128,256]{1,0:T(8,128)(2,1)S(1)}, bf16[128,256]{1,0:T(8,128)(2,1)S(1)}, u32[]{:S(2)}, u32[]{:S(2)}) collective-permute-start(bf16[128,256]{1,0:T(8,128)(2,1)S(1)} %get-tuple-element.115), channel_id=1, source_target_pairs={{0,4},{1,2},{2,1},{3,7},{4,0},{5,6},{6,5},{7,3},{8,12},{9,10},{10,... | collective-permute-start | bytes 196616 | tf_op jit(solution)/shard_map/ppermute | solution.py:304
  30.7 2.6 %spread.1 = (bf16[1024,512]{1,0:T(8,128)(2,1)S(1)}, bf16[1536,1536]{1,0:T(8,128)(2,1)S(1)}) custom-call(bf16[1536,1536]{1,0:T(8,128)(2,1)} %bitcast.10, s32[4,128]{1,0:T(4,128)S(1)} %get-tuple-element.110.masked), custom_call_target="tpu_custom_call" | custom-call | bytes 4720640 | tf_op jit(solution)/shard_map/spread/pallas_call | solution.py:28
  34.6 1.6 %collective-permute-start.15 = (bf16[128,256]{1,0:T(8,128)(2,1)S(1)}, bf16[128,256]{1,0:T(8,128)(2,1)S(1)}, u32[]{:S(2)}, u32[]{:S(2)}) collective-permute-start(bf16[128,256]{1,0:T(8,128)(2,1)S(1)} %get-tuple-element.121), channel_id=1, source_target_pairs={{0,4},{1,5},{2,6},{3,7},{4,0},{5,1},{6,2},{7,3},{8,12},{9,13},{10,... | collective-permute-start | bytes 196616 | tf_op jit(solution)/shard_map/ppermute | solution.py:304
  36.2 2.3 %collective-permute-start.17 = (bf16[128,256]{1,0:T(8,128)(2,1)S(1)}, bf16[128,256]{1,0:T(8,128)(2,1)S(1)}, u32[]{:S(2)}, u32[]{:S(2)}) collective-permute-start(bf16[128,256]{1,0:T(8,128)(2,1)S(1)} %get-tuple-element.123), channel_id=1, source_target_pairs={{0,4},{1,2},{2,1},{3,7},{4,0},{5,6},{6,5},{7,3},{8,12},{9,10},{10,... | collective-permute-start | bytes 196616 | tf_op jit(solution)/shard_map/ppermute | solution.py:304
  39.5 1.2 collective-permute-done.17.g2
  41.1 2.1 %collective-permute-start.19 = (bf16[128,256]{1,0:T(8,128)(2,1)S(1)}, bf16[128,256]{1,0:T(8,128)(2,1)S(1)}, u32[]{:S(2)}, u32[]{:S(2)}) collective-permute-start(bf16[128,256]{1,0:T(8,128)(2,1)S(1)} %get-tuple-element.125), channel_id=1, source_target_pairs={{0,4},{1,5},{2,6},{3,7},{4,0},{5,1},{6,2},{7,3},{8,12},{9,13},{10,... | collective-permute-start | bytes 196616 | tf_op jit(solution)/shard_map/ppermute | solution.py:304
  43.2 3.0 %collective-permute-start.21 = (bf16[128,256]{1,0:T(8,128)(2,1)S(1)}, bf16[128,256]{1,0:T(8,128)(2,1)S(1)}, u32[]{:S(2)}, u32[]{:S(2)}) collective-permute-start(bf16[128,256]{1,0:T(8,128)(2,1)S(1)} %get-tuple-element.127), channel_id=1, source_target_pairs={{0,4},{1,2},{2,1},{3,7},{4,0},{5,6},{6,5},{7,3},{8,12},{9,10},{10,... | collective-permute-start | bytes 196616 | tf_op jit(solution)/shard_map/ppermute | solution.py:304
  46.8 1.6 %collective-permute-done.21.r2 = bf16[128,256]{1,0:T(8,128)(2,1)S(1)} collective-permute-done((bf16[128,256]{1,0:T(8,128)(2,1)S(1)}, bf16[128,256]{1,0:T(8,128)(2,1)S(1)}, u32[]{:S(2)}, u32[]{:S(2)}) %collective-permute-start.21) | collective-permute-done | bytes 65568 | tf_op jit(solution)/shard_map/ppermute | solution.py:304
  49.3 2.1 %collective-permute-start.23 = (bf16[128,256]{1,0:T(8,128)(2,1)S(1)}, bf16[128,256]{1,0:T(8,128)(2,1)S(1)}, u32[]{:S(2)}, u32[]{:S(2)}) collective-permute-start(bf16[128,256]{1,0:T(8,128)(2,1)S(1)} %get-tuple-element.130), channel_id=1, source_target_pairs={{0,4},{1,5},{2,6},{3,7},{4,0},{5,1},{6,2},{7,3},{8,12},{9,13},{10,... | collective-permute-start | bytes 196616 | tf_op jit(solution)/shard_map/ppermute | solution.py:304
  51.4 2.2 %collective-permute-start.25 = (bf16[128,256]{1,0:T(8,128)(2,1)S(1)}, bf16[128,256]{1,0:T(8,128)(2,1)S(1)}, u32[]{:S(2)}, u32[]{:S(2)}) collective-permute-start(bf16[128,256]{1,0:T(8,128)(2,1)S(1)} %get-tuple-element.132), channel_id=1, source_target_pairs={{0,4},{1,2},{2,1},{3,7},{4,0},{5,6},{6,5},{7,3},{8,12},{9,10},{10,... | collective-permute-start | bytes 196616 | tf_op jit(solution)/shard_map/ppermute | solution.py:304
  53.6 2.2 %collective-permute-done.25.g2 = bf16[128,256]{1,0:T(8,128)(2,1)S(1)} collective-permute-done((bf16[128,256]{1,0:T(8,128)(2,1)S(1)}, bf16[128,256]{1,0:T(8,128)(2,1)S(1)}, u32[]{:S(2)}, u32[]{:S(2)}) %collective-permute-start.25) | collective-permute-done | bytes 65568 | tf_op jit(solution)/shard_map/ppermute | solution.py:304
  56.1 1.6 %collective-permute-start.28 = (bf16[32,256]{1,0:T(8,128)(2,1)S(1)}, bf16[32,256]{1,0:T(8,128)(2,1)S(1)}, u32[]{:S(2)}, u32[]{:S(2)}) collective-permute-start(bf16[32,256]{1,0:T(8,128)(2,1)S(1)} %restrict.4.refs_0_), channel_id=1, source_target_pairs={{0,2},{1,3},{2,0},{3,1},{4,6},{5,7},{6,4},{7,5},{8,10},{9,11},{10,... | collective-permute-start | bytes 49160 | tf_op jit(solution)/shard_map/ppermute | solution.py:175
  58.0 1.3 %collective-permute-done.29.refs_3_ = bf16[32,256]{1,0:T(8,128)(2,1)S(1)} collective-permute-done((bf16[32,256]{1,0:T(8,128)(2,1)S(1)}, bf16[32,256]{1,0:T(8,128)(2,1)S(1)}, u32[]{:S(2)}, u32[]{:S(2)}) %collective-permute-start.29) | collective-permute-done | bytes 16416 | tf_op jit(solution)/shard_map/ppermute | solution.py:175
  60.1 3.0 %collective-permute-start.30 = (bf16[64,256]{1,0:T(8,128)(2,1)S(1)}, bf16[64,256]{1,0:T(8,128)(2,1)S(1)}, u32[]{:S(2)}, u32[]{:S(2)}) collective-permute-start(bf16[64,256]{1,0:T(8,128)(2,1)S(1)} %get-tuple-element.135), channel_id=1, source_target_pairs={{0,24},{4,28},{8,16},{12,20},{16,8},{20,12},{24,0},{28,4},{1,25},{... | collective-permute-start | bytes 98312 | tf_op jit(solution)/shard_map/ppermute | solution.py:175
  66.0 2.2 %collective-permute-done.31.refs_1_ = bf16[64,256]{1,0:T(8,128)(2,1)S(1)} collective-permute-done((bf16[64,256]{1,0:T(8,128)(2,1)S(1)}, bf16[64,256]{1,0:T(8,128)(2,1)S(1)}, u32[]{:S(2)}, u32[]{:S(2)}) %collective-permute-start.31) | collective-permute-done | bytes 32800 | tf_op jit(solution)/shard_map/ppermute | solution.py:175
  69.7 2.5 %collective-permute-done.33.theirs = bf16[32,256]{1,0:T(8,128)(2,1)S(1)} collective-permute-done((bf16[32,256]{1,0:T(8,128)(2,1)S(1)}, bf16[32,256]{1,0:T(8,128)(2,1)S(1)}, u32[]{:S(2)}, u32[]{:S(2)}) %collective-permute-start.33) | collective-permute-done | bytes 16416 | tf_op jit(solution)/shard_map/ppermute | solution.py:304
  73.3 3.0 %collective-permute-start.36 = (bf16[128,256]{1,0:T(8,128)(2,1)S(1)}, bf16[128,256]{1,0:T(8,128)(2,1)S(1)}, u32[]{:S(2)}, u32[]{:S(2)}) collective-permute-start(bf16[128,256]{1,0:T(8,128)(2,1)S(1)} %get-tuple-element.145), channel_id=1, source_target_pairs={{0,4},{1,2},{2,1},{3,7},{4,0},{5,6},{6,5},{7,3},{8,12},{9,10},{10,... | collective-permute-start | bytes 196616 | tf_op jit(solution)/shard_map/ppermute | solution.py:304
  77.2 1.3 %collective-permute-done.36.r2 = bf16[128,256]{1,0:T(8,128)(2,1)S(1)} collective-permute-done((bf16[128,256]{1,0:T(8,128)(2,1)S(1)}, bf16[128,256]{1,0:T(8,128)(2,1)S(1)}, u32[]{:S(2)}, u32[]{:S(2)}) %collective-permute-start.36) | collective-permute-done | bytes 65568 | tf_op jit(solution)/shard_map/ppermute | solution.py:304
  79.4 2.1 %collective-permute-start.38 = (bf16[128,256]{1,0:T(8,128)(2,1)S(1)}, bf16[128,256]{1,0:T(8,128)(2,1)S(1)}, u32[]{:S(2)}, u32[]{:S(2)}) collective-permute-start(bf16[128,256]{1,0:T(8,128)(2,1)S(1)} %get-tuple-element.149), channel_id=1, source_target_pairs={{0,4},{1,5},{2,6},{3,7},{4,0},{5,1},{6,2},{7,3},{8,12},{9,13},{10,... | collective-permute-start | bytes 196616 | tf_op jit(solution)/shard_map/ppermute | solution.py:304
  81.5 1.8 %collective-permute-start.40 = (bf16[128,256]{1,0:T(8,128)(2,1)S(1)}, bf16[128,256]{1,0:T(8,128)(2,1)S(1)}, u32[]{:S(2)}, u32[]{:S(2)}) collective-permute-start(bf16[128,256]{1,0:T(8,128)(2,1)S(1)} %get-tuple-element.151), channel_id=1, source_target_pairs={{0,4},{1,2},{2,1},{3,7},{4,0},{5,6},{6,5},{7,3},{8,12},{9,10},{10,... | collective-permute-start | bytes 196616 | tf_op jit(solution)/shard_map/ppermute | solution.py:304
  83.2 1.2 operator_own.3.partial
  84.4 1.3 %collective-permute-done.40.g2 = bf16[128,256]{1,0:T(8,128)(2,1)S(1)} collective-permute-done((bf16[128,256]{1,0:T(8,128)(2,1)S(1)}, bf16[128,256]{1,0:T(8,128)(2,1)S(1)}, u32[]{:S(2)}, u32[]{:S(2)}) %collective-permute-start.40) | collective-permute-done | bytes 65568 | tf_op jit(solution)/shard_map/ppermute | solution.py:304
  86.1 1.8 %collective-permute-start.42 = (bf16[128,256]{1,0:T(8,128)(2,1)S(1)}, bf16[128,256]{1,0:T(8,128)(2,1)S(1)}, u32[]{:S(2)}, u32[]{:S(2)}) collective-permute-start(bf16[128,256]{1,0:T(8,128)(2,1)S(1)} %get-tuple-element.153), channel_id=1, source_target_pairs={{0,4},{1,5},{2,6},{3,7},{4,0},{5,1},{6,2},{7,3},{8,12},{9,13},{10,... | collective-permute-start | bytes 196616 | tf_op jit(solution)/shard_map/ppermute | solution.py:304
  87.9 3.5 %collective-permute-start.44 = (bf16[128,256]{1,0:T(8,128)(2,1)S(1)}, bf16[128,256]{1,0:T(8,128)(2,1)S(1)}, u32[]{:S(2)}, u32[]{:S(2)}) collective-permute-start(bf16[128,256]{1,0:T(8,128)(2,1)S(1)} %get-tuple-element.155), channel_id=1, source_target_pairs={{0,4},{1,2},{2,1},{3,7},{4,0},{5,6},{6,5},{7,3},{8,12},{9,10},{10,... | collective-permute-start | bytes 196616 | tf_op jit(solution)/shard_map/ppermute | solution.py:304
  92.0 1.6 %collective-permute-done.44.r2 = bf16[128,256]{1,0:T(8,128)(2,1)S(1)} collective-permute-done((bf16[128,256]{1,0:T(8,128)(2,1)S(1)}, bf16[128,256]{1,0:T(8,128)(2,1)S(1)}, u32[]{:S(2)}, u32[]{:S(2)}) %collective-permute-start.44) | collective-permute-done | bytes 65568 | tf_op jit(solution)/shard_map/ppermute | solution.py:304
  94.5 2.1 %collective-permute-start.46 = (bf16[128,256]{1,0:T(8,128)(2,1)S(1)}, bf16[128,256]{1,0:T(8,128)(2,1)S(1)}, u32[]{:S(2)}, u32[]{:S(2)}) collective-permute-start(bf16[128,256]{1,0:T(8,128)(2,1)S(1)} %get-tuple-element.158), channel_id=1, source_target_pairs={{0,4},{1,5},{2,6},{3,7},{4,0},{5,1},{6,2},{7,3},{8,12},{9,13},{10,... | collective-permute-start | bytes 196616 | tf_op jit(solution)/shard_map/ppermute | solution.py:304
  96.5 1.8 %collective-permute-start.48 = (bf16[128,256]{1,0:T(8,128)(2,1)S(1)}, bf16[128,256]{1,0:T(8,128)(2,1)S(1)}, u32[]{:S(2)}, u32[]{:S(2)}) collective-permute-start(bf16[128,256]{1,0:T(8,128)(2,1)S(1)} %get-tuple-element.160), channel_id=1, source_target_pairs={{0,4},{1,2},{2,1},{3,7},{4,0},{5,6},{6,5},{7,3},{8,12},{9,10},{10,... | collective-permute-start | bytes 196616 | tf_op jit(solution)/shard_map/ppermute | solution.py:304
  98.8 2.0 %collective-permute-done.48.g2 = bf16[128,256]{1,0:T(8,128)(2,1)S(1)} collective-permute-done((bf16[128,256]{1,0:T(8,128)(2,1)S(1)}, bf16[128,256]{1,0:T(8,128)(2,1)S(1)}, u32[]{:S(2)}, u32[]{:S(2)}) %collective-permute-start.48) | collective-permute-done | bytes 65568 | tf_op jit(solution)/shard_map/ppermute | solution.py:304
  101.1 1.7 %collective-permute-start.51 = (bf16[32,256]{1,0:T(8,128)(2,1)S(1)}, bf16[32,256]{1,0:T(8,128)(2,1)S(1)}, u32[]{:S(2)}, u32[]{:S(2)}) collective-permute-start(bf16[32,256]{1,0:T(8,128)(2,1)S(1)} %restrict.5.refs_0_), channel_id=1, source_target_pairs={{0,2},{1,3},{2,0},{3,1},{4,6},{5,7},{6,4},{7,5},{8,10},{9,11},{10,... | collective-permute-start | bytes 49160 | tf_op jit(solution)/shard_map/ppermute | solution.py:175
  103.0 1.3 %collective-permute-done.52.refs_3_ = bf16[32,256]{1,0:T(8,128)(2,1)S(1)} collective-permute-done((bf16[32,256]{1,0:T(8,128)(2,1)S(1)}, bf16[32,256]{1,0:T(8,128)(2,1)S(1)}, u32[]{:S(2)}, u32[]{:S(2)}) %collective-permute-start.52) | collective-permute-done | bytes 16416 | tf_op jit(solution)/shard_map/ppermute | solution.py:175
  105.1 2.7 %collective-permute-start.53 = (bf16[64,256]{1,0:T(8,128)(2,1)S(1)}, bf16[64,256]{1,0:T(8,128)(2,1)S(1)}, u32[]{:S(2)}, u32[]{:S(2)}) collective-permute-start(bf16[64,256]{1,0:T(8,128)(2,1)S(1)} %get-tuple-element.163), channel_id=1, source_target_pairs={{0,24},{4,28},{8,16},{12,20},{16,8},{20,12},{24,0},{28,4},{1,25},{... | collective-permute-start | bytes 98312 | tf_op jit(solution)/shard_map/ppermute | solution.py:175
  111.0 1.6 %collective-permute-done.54.refs_1_ = bf16[64,256]{1,0:T(8,128)(2,1)S(1)} collective-permute-done((bf16[64,256]{1,0:T(8,128)(2,1)S(1)}, bf16[64,256]{1,0:T(8,128)(2,1)S(1)}, u32[]{:S(2)}, u32[]{:S(2)}) %collective-permute-start.54) | collective-permute-done | bytes 32800 | tf_op jit(solution)/shard_map/ppermute | solution.py:175
  112.8 1.5 %collective-permute-start.56 = (bf16[32,256]{1,0:T(8,128)(2,1)S(1)}, bf16[32,256]{1,0:T(8,128)(2,1)S(1)}, u32[]{:S(2)}, u32[]{:S(2)}) collective-permute-start(bf16[32,256]{1,0:T(8,128)(2,1)S(1)} %get-tuple-element.168), channel_id=1, source_target_pairs={{0,4},{1,5},{2,6},{3,7},{4,0},{5,1},{6,2},{7,3},{8,12},{9,13},{10,... | collective-permute-start | bytes 49160 | tf_op jit(solution)/shard_map/ppermute | solution.py:304
  114.9 1.7 %collective-permute-done.56.theirs = bf16[32,256]{1,0:T(8,128)(2,1)S(1)} collective-permute-done((bf16[32,256]{1,0:T(8,128)(2,1)S(1)}, bf16[32,256]{1,0:T(8,128)(2,1)S(1)}, u32[]{:S(2)}, u32[]{:S(2)}) %collective-permute-start.56) | collective-permute-done | bytes 16416 | tf_op jit(solution)/shard_map/ppermute | solution.py:304
  116.9 1.6 %collective-permute-start.57 = (bf16[128,256]{1,0:T(8,128)(2,1)S(1)}, bf16[128,256]{1,0:T(8,128)(2,1)S(1)}, u32[]{:S(2)}, u32[]{:S(2)}) collective-permute-start(bf16[128,256]{1,0:T(8,128)(2,1)S(1)} %get-tuple-element.171), channel_id=1, source_target_pairs={{0,4},{1,5},{2,6},{3,7},{4,0},{5,1},{6,2},{7,3},{8,12},{9,13},{10,... | collective-permute-start | bytes 196616 | tf_op jit(solution)/shard_map/ppermute | solution.py:304
  118.5 2.5 %collective-permute-start.59 = (bf16[128,256]{1,0:T(8,128)(2,1)S(1)}, bf16[128,256]{1,0:T(8,128)(2,1)S(1)}, u32[]{:S(2)}, u32[]{:S(2)}) collective-permute-start(bf16[128,256]{1,0:T(8,128)(2,1)S(1)} %get-tuple-element.173), channel_id=1, source_target_pairs={{0,4},{1,2},{2,1},{3,7},{4,0},{5,6},{6,5},{7,3},{8,12},{9,10},{10,... | collective-permute-start | bytes 196616 | tf_op jit(solution)/shard_map/ppermute | solution.py:304
  121.7 1.6 %collective-permute-done.59.r2 = bf16[128,256]{1,0:T(8,128)(2,1)S(1)} collective-permute-done((bf16[128,256]{1,0:T(8,128)(2,1)S(1)}, bf16[128,256]{1,0:T(8,128)(2,1)S(1)}, u32[]{:S(2)}, u32[]{:S(2)}) %collective-permute-start.59) | collective-permute-done | bytes 65568 | tf_op jit(solution)/shard_map/ppermute | solution.py:304
  123.2 1.2 last_update.1
  (111 shorter events, 26.8 us)
Async XLA Ops:
  1.8 8.7 %collective-permute-start = (bf16[128,256]{1,0:T(8,128)(2,1)S(1)}, bf16[128,256]{1,0:T(8,128)(2,1)S(1)}, u32[]{:S(2)}, u32[]{:S(2)}) collective-permute-start(bf16[128,256]{1,0:T(8,128)(2,1)S(1)} %get-tuple-element.91), channel_id=1, source_target_pairs={{0,4},{1,5},{2,6},{3,7},{4,0},{5,1},{6,2},{7,3},{8,12},{9,13},{10,... | collective-permute-start | bytes 196616 | tf_op jit(solution)/shard_map/ppermute | solution.py:304
  4.8 5.6 %collective-permute-start.1 = (bf16[128,256]{1,0:T(8,128)(2,1)S(1)}, bf16[128,256]{1,0:T(8,128)(2,1)S(1)}, u32[]{:S(2)}, u32[]{:S(2)}) collective-permute-start(bf16[128,256]{1,0:T(8,128)(2,1)S(1)} %get-tuple-element.92), channel_id=1, source_target_pairs={{0,1},{1,0},{2,3},{3,2},{4,8},{5,9},{6,10},{7,11},{8,4},{9,5},{10,... | collective-permute-start | bytes 196616 | tf_op jit(solution)/shard_map/ppermute | solution.py:304
  4.8 5.6 %collective-permute-start.2 = (bf16[128,256]{1,0:T(8,128)(2,1)S(1)}, bf16[128,256]{1,0:T(8,128)(2,1)S(1)}, u32[]{:S(2)}, u32[]{:S(2)}) collective-permute-start(bf16[128,256]{1,0:T(8,128)(2,1)S(1)} %get-tuple-element.93), channel_id=1, source_target_pairs={{0,4},{1,2},{2,1},{3,7},{4,0},{5,6},{6,5},{7,3},{8,12},{9,10},{10,... | collective-permute-start | bytes 196616 | tf_op jit(solution)/shard_map/ppermute | solution.py:304
  7.9 2.6 %collective-permute-start.3 = (bf16[128,256]{1,0:T(8,128)(2,1)S(1)}, bf16[128,256]{1,0:T(8,128)(2,1)S(1)}, u32[]{:S(2)}, u32[]{:S(2)}) collective-permute-start(bf16[128,256]{1,0:T(8,128)(2,1)S(1)} %get-tuple-element.94), channel_id=1, source_target_pairs={{0,1},{1,0},{2,3},{3,2},{4,5},{5,4},{6,7},{7,6},{8,9},{9,8},{10,11... | collective-permute-start | bytes 196616 | tf_op jit(solution)/shard_map/ppermute | solution.py:304
  10.7 3.2 %collective-permute-start.6 = (bf16[32,256]{1,0:T(8,128)(2,1)S(1)}, bf16[32,256]{1,0:T(8,128)(2,1)S(1)}, u32[]{:S(2)}, u32[]{:S(2)}) collective-permute-start(bf16[32,256]{1,0:T(8,128)(2,1)S(1)} %restrict.3.refs_0_), channel_id=1, source_target_pairs={{0,3},{1,2},{2,1},{3,0},{4,7},{5,6},{6,5},{7,4},{8,11},{9,10},{10,... | collective-permute-start | bytes 49160 | tf_op jit(solution)/shard_map/ppermute | solution.py:175
  10.8 4.0 %collective-permute-start.5 = (bf16[32,256]{1,0:T(8,128)(2,1)S(1)}, bf16[32,256]{1,0:T(8,128)(2,1)S(1)}, u32[]{:S(2)}, u32[]{:S(2)}) collective-permute-start(bf16[32,256]{1,0:T(8,128)(2,1)S(1)} %restrict.3.refs_0_), channel_id=1, source_target_pairs={{0,2},{1,3},{2,0},{3,1},{4,6},{5,7},{6,4},{7,5},{8,10},{9,11},{10,... | collective-permute-start | bytes 49160 | tf_op jit(solution)/shard_map/ppermute | solution.py:175
  15.0 5.8 %collective-permute-start.7 = (bf16[64,256]{1,0:T(8,128)(2,1)S(1)}, bf16[64,256]{1,0:T(8,128)(2,1)S(1)}, u32[]{:S(2)}, u32[]{:S(2)}) collective-permute-start(bf16[64,256]{1,0:T(8,128)(2,1)S(1)} %get-tuple-element.97), channel_id=1, source_target_pairs={{0,24},{4,28},{8,16},{12,20},{16,8},{20,12},{24,0},{28,4},{1,25},{... | collective-permute-start | bytes 98312 | tf_op jit(solution)/shard_map/ppermute | solution.py:175
  18.1 4.9 %collective-permute-start.8 = (bf16[64,256]{1,0:T(8,128)(2,1)S(1)}, bf16[64,256]{1,0:T(8,128)(2,1)S(1)}, u32[]{:S(2)}, u32[]{:S(2)}) collective-permute-start(bf16[64,256]{1,0:T(8,128)(2,1)S(1)} %get-tuple-element.98), channel_id=1, source_target_pairs={{0,16},{4,20},{8,24},{12,28},{16,0},{20,4},{24,8},{28,12},{1,17},{... | collective-permute-start | bytes 98312 | tf_op jit(solution)/shard_map/ppermute | solution.py:175
  18.3 4.7 %collective-permute-start.9 = (bf16[64,256]{1,0:T(8,128)(2,1)S(1)}, bf16[64,256]{1,0:T(8,128)(2,1)S(1)}, u32[]{:S(2)}, u32[]{:S(2)}) collective-permute-start(bf16[64,256]{1,0:T(8,128)(2,1)S(1)} %get-tuple-element.99), channel_id=1, source_target_pairs={{0,8},{4,12},{8,0},{12,4},{16,24},{20,28},{24,16},{28,20},{1,9},{5... | collective-permute-start | bytes 98312 | tf_op jit(solution)/shard_map/ppermute | solution.py:175
  23.0 3.8 %collective-permute-start.10 = (bf16[32,256]{1,0:T(8,128)(2,1)S(1)}, bf16[32,256]{1,0:T(8,128)(2,1)S(1)}, u32[]{:S(2)}, u32[]{:S(2)}) collective-permute-start(bf16[32,256]{1,0:T(8,128)(2,1)S(1)} %get-tuple-element.102), channel_id=1, source_target_pairs={{0,4},{1,5},{2,6},{3,7},{4,0},{5,1},{6,2},{7,3},{8,12},{9,13},{10,... | collective-permute-start | bytes 49160 | tf_op jit(solution)/shard_map/ppermute | solution.py:304
  27.1 6.2 %collective-permute-start.11 = (bf16[128,256]{1,0:T(8,128)(2,1)S(1)}, bf16[128,256]{1,0:T(8,128)(2,1)S(1)}, u32[]{:S(2)}, u32[]{:S(2)}) collective-permute-start(bf16[128,256]{1,0:T(8,128)(2,1)S(1)} %get-tuple-element.112), channel_id=1, source_target_pairs={{0,4},{1,5},{2,6},{3,7},{4,0},{5,1},{6,2},{7,3},{8,12},{9,13},{10,... | collective-permute-start | bytes 196616 | tf_op jit(solution)/shard_map/ppermute | solution.py:304
  28.2 5.0 %collective-permute-start.12 = (bf16[128,256]{1,0:T(8,128)(2,1)S(1)}, bf16[128,256]{1,0:T(8,128)(2,1)S(1)}, u32[]{:S(2)}, u32[]{:S(2)}) collective-permute-start(bf16[128,256]{1,0:T(8,128)(2,1)S(1)} %get-tuple-element.113), channel_id=1, source_target_pairs={{0,1},{1,0},{2,3},{3,2},{4,8},{5,9},{6,10},{7,11},{8,4},{9,5},{10,... | collective-permute-start | bytes 196616 | tf_op jit(solution)/shard_map/ppermute | solution.py:304
  28.3 5.5 %collective-permute-start.13 = (bf16[128,256]{1,0:T(8,128)(2,1)S(1)}, bf16[128,256]{1,0:T(8,128)(2,1)S(1)}, u32[]{:S(2)}, u32[]{:S(2)}) collective-permute-start(bf16[128,256]{1,0:T(8,128)(2,1)S(1)} %get-tuple-element.115), channel_id=1, source_target_pairs={{0,4},{1,2},{2,1},{3,7},{4,0},{5,6},{6,5},{7,3},{8,12},{9,10},{10,... | collective-permute-start | bytes 196616 | tf_op jit(solution)/shard_map/ppermute | solution.py:304
  30.7 3.1 %collective-permute-start.14 = (bf16[128,256]{1,0:T(8,128)(2,1)S(1)}, bf16[128,256]{1,0:T(8,128)(2,1)S(1)}, u32[]{:S(2)}, u32[]{:S(2)}) collective-permute-start(bf16[128,256]{1,0:T(8,128)(2,1)S(1)} %get-tuple-element.116), channel_id=1, source_target_pairs={{0,1},{1,0},{2,3},{3,2},{4,5},{5,4},{6,7},{7,6},{8,9},{9,8},{10,11... | collective-permute-start | bytes 196616 | tf_op jit(solution)/shard_map/ppermute | solution.py:304
  34.6 4.9 %collective-permute-start.15 = (bf16[128,256]{1,0:T(8,128)(2,1)S(1)}, bf16[128,256]{1,0:T(8,128)(2,1)S(1)}, u32[]{:S(2)}, u32[]{:S(2)}) collective-permute-start(bf16[128,256]{1,0:T(8,128)(2,1)S(1)} %get-tuple-element.121), channel_id=1, source_target_pairs={{0,4},{1,5},{2,6},{3,7},{4,0},{5,1},{6,2},{7,3},{8,12},{9,13},{10,... | collective-permute-start | bytes 196616 | tf_op jit(solution)/shard_map/ppermute | solution.py:304
  36.2 3.3 %collective-permute-start.16 = (bf16[128,256]{1,0:T(8,128)(2,1)S(1)}, bf16[128,256]{1,0:T(8,128)(2,1)S(1)}, u32[]{:S(2)}, u32[]{:S(2)}) collective-permute-start(bf16[128,256]{1,0:T(8,128)(2,1)S(1)} %get-tuple-element.122), channel_id=1, source_target_pairs={{0,1},{1,0},{2,3},{3,2},{4,8},{5,9},{6,10},{7,11},{8,4},{9,5},{10,... | collective-permute-start | bytes 196616 | tf_op jit(solution)/shard_map/ppermute | solution.py:304
  36.2 4.5 %collective-permute-start.17 = (bf16[128,256]{1,0:T(8,128)(2,1)S(1)}, bf16[128,256]{1,0:T(8,128)(2,1)S(1)}, u32[]{:S(2)}, u32[]{:S(2)}) collective-permute-start(bf16[128,256]{1,0:T(8,128)(2,1)S(1)} %get-tuple-element.123), channel_id=1, source_target_pairs={{0,4},{1,2},{2,1},{3,7},{4,0},{5,6},{6,5},{7,3},{8,12},{9,10},{10,... | collective-permute-start | bytes 196616 | tf_op jit(solution)/shard_map/ppermute | solution.py:304
  41.1 5.1 %collective-permute-start.19 = (bf16[128,256]{1,0:T(8,128)(2,1)S(1)}, bf16[128,256]{1,0:T(8,128)(2,1)S(1)}, u32[]{:S(2)}, u32[]{:S(2)}) collective-permute-start(bf16[128,256]{1,0:T(8,128)(2,1)S(1)} %get-tuple-element.125), channel_id=1, source_target_pairs={{0,4},{1,5},{2,6},{3,7},{4,0},{5,1},{6,2},{7,3},{8,12},{9,13},{10,... | collective-permute-start | bytes 196616 | tf_op jit(solution)/shard_map/ppermute | solution.py:304
  43.2 3.0 %collective-permute-start.20 = (bf16[128,256]{1,0:T(8,128)(2,1)S(1)}, bf16[128,256]{1,0:T(8,128)(2,1)S(1)}, u32[]{:S(2)}, u32[]{:S(2)}) collective-permute-start(bf16[128,256]{1,0:T(8,128)(2,1)S(1)} %get-tuple-element.126), channel_id=1, source_target_pairs={{0,1},{1,0},{2,3},{3,2},{4,8},{5,9},{6,10},{7,11},{8,4},{9,5},{10,... | collective-permute-start | bytes 196616 | tf_op jit(solution)/shard_map/ppermute | solution.py:304
  43.2 5.2 %collective-permute-start.21 = (bf16[128,256]{1,0:T(8,128)(2,1)S(1)}, bf16[128,256]{1,0:T(8,128)(2,1)S(1)}, u32[]{:S(2)}, u32[]{:S(2)}) collective-permute-start(bf16[128,256]{1,0:T(8,128)(2,1)S(1)} %get-tuple-element.127), channel_id=1, source_target_pairs={{0,4},{1,2},{2,1},{3,7},{4,0},{5,6},{6,5},{7,3},{8,12},{9,10},{10,... | collective-permute-start | bytes 196616 | tf_op jit(solution)/shard_map/ppermute | solution.py:304
  49.3 4.3 %collective-permute-start.23 = (bf16[128,256]{1,0:T(8,128)(2,1)S(1)}, bf16[128,256]{1,0:T(8,128)(2,1)S(1)}, u32[]{:S(2)}, u32[]{:S(2)}) collective-permute-start(bf16[128,256]{1,0:T(8,128)(2,1)S(1)} %get-tuple-element.130), channel_id=1, source_target_pairs={{0,4},{1,5},{2,6},{3,7},{4,0},{5,1},{6,2},{7,3},{8,12},{9,13},{10,... | collective-permute-start | bytes 196616 | tf_op jit(solution)/shard_map/ppermute | solution.py:304
  51.4 4.5 %collective-permute-start.25 = (bf16[128,256]{1,0:T(8,128)(2,1)S(1)}, bf16[128,256]{1,0:T(8,128)(2,1)S(1)}, u32[]{:S(2)}, u32[]{:S(2)}) collective-permute-start(bf16[128,256]{1,0:T(8,128)(2,1)S(1)} %get-tuple-element.132), channel_id=1, source_target_pairs={{0,4},{1,2},{2,1},{3,7},{4,0},{5,6},{6,5},{7,3},{8,12},{9,10},{10,... | collective-permute-start | bytes 196616 | tf_op jit(solution)/shard_map/ppermute | solution.py:304
  56.1 3.2 %collective-permute-start.29 = (bf16[32,256]{1,0:T(8,128)(2,1)S(1)}, bf16[32,256]{1,0:T(8,128)(2,1)S(1)}, u32[]{:S(2)}, u32[]{:S(2)}) collective-permute-start(bf16[32,256]{1,0:T(8,128)(2,1)S(1)} %restrict.4.refs_0_), channel_id=1, source_target_pairs={{0,3},{1,2},{2,1},{3,0},{4,7},{5,6},{6,5},{7,4},{8,11},{9,10},{10,... | collective-permute-start | bytes 49160 | tf_op jit(solution)/shard_map/ppermute | solution.py:175
  56.1 3.8 %collective-permute-start.28 = (bf16[32,256]{1,0:T(8,128)(2,1)S(1)}, bf16[32,256]{1,0:T(8,128)(2,1)S(1)}, u32[]{:S(2)}, u32[]{:S(2)}) collective-permute-start(bf16[32,256]{1,0:T(8,128)(2,1)S(1)} %restrict.4.refs_0_), channel_id=1, source_target_pairs={{0,2},{1,3},{2,0},{3,1},{4,6},{5,7},{6,4},{7,5},{8,10},{9,11},{10,... | collective-permute-start | bytes 49160 | tf_op jit(solution)/shard_map/ppermute | solution.py:175
  60.1 5.9 %collective-permute-start.30 = (bf16[64,256]{1,0:T(8,128)(2,1)S(1)}, bf16[64,256]{1,0:T(8,128)(2,1)S(1)}, u32[]{:S(2)}, u32[]{:S(2)}) collective-permute-start(bf16[64,256]{1,0:T(8,128)(2,1)S(1)} %get-tuple-element.135), channel_id=1, source_target_pairs={{0,24},{4,28},{8,16},{12,20},{16,8},{20,12},{24,0},{28,4},{1,25},{... | collective-permute-start | bytes 98312 | tf_op jit(solution)/shard_map/ppermute | solution.py:175
  63.1 5.2 %collective-permute-start.31 = (bf16[64,256]{1,0:T(8,128)(2,1)S(1)}, bf16[64,256]{1,0:T(8,128)(2,1)S(1)}, u32[]{:S(2)}, u32[]{:S(2)}) collective-permute-start(bf16[64,256]{1,0:T(8,128)(2,1)S(1)} %get-tuple-element.136), channel_id=1, source_target_pairs={{0,16},{4,20},{8,24},{12,28},{16,0},{20,4},{24,8},{28,12},{1,17},{... | collective-permute-start | bytes 98312 | tf_op jit(solution)/shard_map/ppermute | solution.py:175
  63.7 4.6 %collective-permute-start.32 = (bf16[64,256]{1,0:T(8,128)(2,1)S(1)}, bf16[64,256]{1,0:T(8,128)(2,1)S(1)}, u32[]{:S(2)}, u32[]{:S(2)}) collective-permute-start(bf16[64,256]{1,0:T(8,128)(2,1)S(1)} %get-tuple-element.137), channel_id=1, source_target_pairs={{0,8},{4,12},{8,0},{12,4},{16,24},{20,28},{24,16},{28,20},{1,9},{5... | collective-permute-start | bytes 98312 | tf_op jit(solution)/shard_map/ppermute | solution.py:175
  68.3 3.8 %collective-permute-start.33 = (bf16[32,256]{1,0:T(8,128)(2,1)S(1)}, bf16[32,256]{1,0:T(8,128)(2,1)S(1)}, u32[]{:S(2)}, u32[]{:S(2)}) collective-permute-start(bf16[32,256]{1,0:T(8,128)(2,1)S(1)} %get-tuple-element.140), channel_id=1, source_target_pairs={{0,4},{1,5},{2,6},{3,7},{4,0},{5,1},{6,2},{7,3},{8,12},{9,13},{10,... | collective-permute-start | bytes 49160 | tf_op jit(solution)/shard_map/ppermute | solution.py:304
  72.4 4.3 %collective-permute-start.34 = (bf16[128,256]{1,0:T(8,128)(2,1)S(1)}, bf16[128,256]{1,0:T(8,128)(2,1)S(1)}, u32[]{:S(2)}, u32[]{:S(2)}) collective-permute-start(bf16[128,256]{1,0:T(8,128)(2,1)S(1)} %get-tuple-element.143), channel_id=1, source_target_pairs={{0,4},{1,5},{2,6},{3,7},{4,0},{5,1},{6,2},{7,3},{8,12},{9,13},{10,... | collective-permute-start | bytes 196616 | tf_op jit(solution)/shard_map/ppermute | solution.py:304
  73.3 3.4 %collective-permute-start.35 = (bf16[128,256]{1,0:T(8,128)(2,1)S(1)}, bf16[128,256]{1,0:T(8,128)(2,1)S(1)}, u32[]{:S(2)}, u32[]{:S(2)}) collective-permute-start(bf16[128,256]{1,0:T(8,128)(2,1)S(1)} %get-tuple-element.144), channel_id=1, source_target_pairs={{0,1},{1,0},{2,3},{3,2},{4,8},{5,9},{6,10},{7,11},{8,4},{9,5},{10,... | collective-permute-start | bytes 196616 | tf_op jit(solution)/shard_map/ppermute | solution.py:304
  73.3 5.2 %collective-permute-start.36 = (bf16[128,256]{1,0:T(8,128)(2,1)S(1)}, bf16[128,256]{1,0:T(8,128)(2,1)S(1)}, u32[]{:S(2)}, u32[]{:S(2)}) collective-permute-start(bf16[128,256]{1,0:T(8,128)(2,1)S(1)} %get-tuple-element.145), channel_id=1, source_target_pairs={{0,4},{1,2},{2,1},{3,7},{4,0},{5,6},{6,5},{7,3},{8,12},{9,10},{10,... | collective-permute-start | bytes 196616 | tf_op jit(solution)/shard_map/ppermute | solution.py:304
  79.4 5.0 %collective-permute-start.38 = (bf16[128,256]{1,0:T(8,128)(2,1)S(1)}, bf16[128,256]{1,0:T(8,128)(2,1)S(1)}, u32[]{:S(2)}, u32[]{:S(2)}) collective-permute-start(bf16[128,256]{1,0:T(8,128)(2,1)S(1)} %get-tuple-element.149), channel_id=1, source_target_pairs={{0,4},{1,5},{2,6},{3,7},{4,0},{5,1},{6,2},{7,3},{8,12},{9,13},{10,... | collective-permute-start | bytes 196616 | tf_op jit(solution)/shard_map/ppermute | solution.py:304
  81.5 3.0 %collective-permute-start.39 = (bf16[128,256]{1,0:T(8,128)(2,1)S(1)}, bf16[128,256]{1,0:T(8,128)(2,1)S(1)}, u32[]{:S(2)}, u32[]{:S(2)}) collective-permute-start(bf16[128,256]{1,0:T(8,128)(2,1)S(1)} %get-tuple-element.150), channel_id=1, source_target_pairs={{0,1},{1,0},{2,3},{3,2},{4,8},{5,9},{6,10},{7,11},{8,4},{9,5},{10,... | collective-permute-start | bytes 196616 | tf_op jit(solution)/shard_map/ppermute | solution.py:304
  81.5 4.3 %collective-permute-start.40 = (bf16[128,256]{1,0:T(8,128)(2,1)S(1)}, bf16[128,256]{1,0:T(8,128)(2,1)S(1)}, u32[]{:S(2)}, u32[]{:S(2)}) collective-permute-start(bf16[128,256]{1,0:T(8,128)(2,1)S(1)} %get-tuple-element.151), channel_id=1, source_target_pairs={{0,4},{1,2},{2,1},{3,7},{4,0},{5,6},{6,5},{7,3},{8,12},{9,10},{10,... | collective-permute-start | bytes 196616 | tf_op jit(solution)/shard_map/ppermute | solution.py:304
  86.1 5.3 %collective-permute-start.42 = (bf16[128,256]{1,0:T(8,128)(2,1)S(1)}, bf16[128,256]{1,0:T(8,128)(2,1)S(1)}, u32[]{:S(2)}, u32[]{:S(2)}) collective-permute-start(bf16[128,256]{1,0:T(8,128)(2,1)S(1)} %get-tuple-element.153), channel_id=1, source_target_pairs={{0,4},{1,5},{2,6},{3,7},{4,0},{5,1},{6,2},{7,3},{8,12},{9,13},{10,... | collective-permute-start | bytes 196616 | tf_op jit(solution)/shard_map/ppermute | solution.py:304
  87.9 3.5 %collective-permute-start.43 = (bf16[128,256]{1,0:T(8,128)(2,1)S(1)}, bf16[128,256]{1,0:T(8,128)(2,1)S(1)}, u32[]{:S(2)}, u32[]{:S(2)}) collective-permute-start(bf16[128,256]{1,0:T(8,128)(2,1)S(1)} %get-tuple-element.154), channel_id=1, source_target_pairs={{0,1},{1,0},{2,3},{3,2},{4,8},{5,9},{6,10},{7,11},{8,4},{9,5},{10,... | collective-permute-start | bytes 196616 | tf_op jit(solution)/shard_map/ppermute | solution.py:304
  87.9 5.7 %collective-permute-start.44 = (bf16[128,256]{1,0:T(8,128)(2,1)S(1)}, bf16[128,256]{1,0:T(8,128)(2,1)S(1)}, u32[]{:S(2)}, u32[]{:S(2)}) collective-permute-start(bf16[128,256]{1,0:T(8,128)(2,1)S(1)} %get-tuple-element.155), channel_id=1, source_target_pairs={{0,4},{1,2},{2,1},{3,7},{4,0},{5,6},{6,5},{7,3},{8,12},{9,10},{10,... | collective-permute-start | bytes 196616 | tf_op jit(solution)/shard_map/ppermute | solution.py:304
  94.5 4.3 %collective-permute-start.46 = (bf16[128,256]{1,0:T(8,128)(2,1)S(1)}, bf16[128,256]{1,0:T(8,128)(2,1)S(1)}, u32[]{:S(2)}, u32[]{:S(2)}) collective-permute-start(bf16[128,256]{1,0:T(8,128)(2,1)S(1)} %get-tuple-element.158), channel_id=1, source_target_pairs={{0,4},{1,5},{2,6},{3,7},{4,0},{5,1},{6,2},{7,3},{8,12},{9,13},{10,... | collective-permute-start | bytes 196616 | tf_op jit(solution)/shard_map/ppermute | solution.py:304
  96.5 4.3 %collective-permute-start.48 = (bf16[128,256]{1,0:T(8,128)(2,1)S(1)}, bf16[128,256]{1,0:T(8,128)(2,1)S(1)}, u32[]{:S(2)}, u32[]{:S(2)}) collective-permute-start(bf16[128,256]{1,0:T(8,128)(2,1)S(1)} %get-tuple-element.160), channel_id=1, source_target_pairs={{0,4},{1,2},{2,1},{3,7},{4,0},{5,6},{6,5},{7,3},{8,12},{9,10},{10,... | collective-permute-start | bytes 196616 | tf_op jit(solution)/shard_map/ppermute | solution.py:304
  101.1 3.2 %collective-permute-start.52 = (bf16[32,256]{1,0:T(8,128)(2,1)S(1)}, bf16[32,256]{1,0:T(8,128)(2,1)S(1)}, u32[]{:S(2)}, u32[]{:S(2)}) collective-permute-start(bf16[32,256]{1,0:T(8,128)(2,1)S(1)} %restrict.5.refs_0_), channel_id=1, source_target_pairs={{0,3},{1,2},{2,1},{3,0},{4,7},{5,6},{6,5},{7,4},{8,11},{9,10},{10,... | collective-permute-start | bytes 49160 | tf_op jit(solution)/shard_map/ppermute | solution.py:175
  101.1 3.8 %collective-permute-start.51 = (bf16[32,256]{1,0:T(8,128)(2,1)S(1)}, bf16[32,256]{1,0:T(8,128)(2,1)S(1)}, u32[]{:S(2)}, u32[]{:S(2)}) collective-permute-start(bf16[32,256]{1,0:T(8,128)(2,1)S(1)} %restrict.5.refs_0_), channel_id=1, source_target_pairs={{0,2},{1,3},{2,0},{3,1},{4,6},{5,7},{6,4},{7,5},{8,10},{9,11},{10,... | collective-permute-start | bytes 49160 | tf_op jit(solution)/shard_map/ppermute | solution.py:175
  105.1 5.9 %collective-permute-start.53 = (bf16[64,256]{1,0:T(8,128)(2,1)S(1)}, bf16[64,256]{1,0:T(8,128)(2,1)S(1)}, u32[]{:S(2)}, u32[]{:S(2)}) collective-permute-start(bf16[64,256]{1,0:T(8,128)(2,1)S(1)} %get-tuple-element.163), channel_id=1, source_target_pairs={{0,24},{4,28},{8,16},{12,20},{16,8},{20,12},{24,0},{28,4},{1,25},{... | collective-permute-start | bytes 98312 | tf_op jit(solution)/shard_map/ppermute | solution.py:175
  107.7 4.9 %collective-permute-start.54 = (bf16[64,256]{1,0:T(8,128)(2,1)S(1)}, bf16[64,256]{1,0:T(8,128)(2,1)S(1)}, u32[]{:S(2)}, u32[]{:S(2)}) collective-permute-start(bf16[64,256]{1,0:T(8,128)(2,1)S(1)} %get-tuple-element.164), channel_id=1, source_target_pairs={{0,16},{4,20},{8,24},{12,28},{16,0},{20,4},{24,8},{28,12},{1,17},{... | collective-permute-start | bytes 98312 | tf_op jit(solution)/shard_map/ppermute | solution.py:175
  108.5 4.3 %collective-permute-start.55 = (bf16[64,256]{1,0:T(8,128)(2,1)S(1)}, bf16[64,256]{1,0:T(8,128)(2,1)S(1)}, u32[]{:S(2)}, u32[]{:S(2)}) collective-permute-start(bf16[64,256]{1,0:T(8,128)(2,1)S(1)} %get-tuple-element.165), channel_id=1, source_target_pairs={{0,8},{4,12},{8,0},{12,4},{16,24},{20,28},{24,16},{28,20},{1,9},{5... | collective-permute-start | bytes 98312 | tf_op jit(solution)/shard_map/ppermute | solution.py:175
  112.8 3.8 %collective-permute-start.56 = (bf16[32,256]{1,0:T(8,128)(2,1)S(1)}, bf16[32,256]{1,0:T(8,128)(2,1)S(1)}, u32[]{:S(2)}, u32[]{:S(2)}) collective-permute-start(bf16[32,256]{1,0:T(8,128)(2,1)S(1)} %get-tuple-element.168), channel_id=1, source_target_pairs={{0,4},{1,5},{2,6},{3,7},{4,0},{5,1},{6,2},{7,3},{8,12},{9,13},{10,... | collective-permute-start | bytes 49160 | tf_op jit(solution)/shard_map/ppermute | solution.py:304
  116.9 4.3 %collective-permute-start.57 = (bf16[128,256]{1,0:T(8,128)(2,1)S(1)}, bf16[128,256]{1,0:T(8,128)(2,1)S(1)}, u32[]{:S(2)}, u32[]{:S(2)}) collective-permute-start(bf16[128,256]{1,0:T(8,128)(2,1)S(1)} %get-tuple-element.171), channel_id=1, source_target_pairs={{0,4},{1,5},{2,6},{3,7},{4,0},{5,1},{6,2},{7,3},{8,12},{9,13},{10,... | collective-permute-start | bytes 196616 | tf_op jit(solution)/shard_map/ppermute | solution.py:304
  118.5 2.7 %collective-permute-start.58 = (bf16[128,256]{1,0:T(8,128)(2,1)S(1)}, bf16[128,256]{1,0:T(8,128)(2,1)S(1)}, u32[]{:S(2)}, u32[]{:S(2)}) collective-permute-start(bf16[128,256]{1,0:T(8,128)(2,1)S(1)} %get-tuple-element.172), channel_id=1, source_target_pairs={{0,1},{1,0},{2,3},{3,2},{4,8},{5,9},{6,10},{7,11},{8,4},{9,5},{10,... | collective-permute-start | bytes 196616 | tf_op jit(solution)/shard_map/ppermute | solution.py:304
  118.5 4.7 %collective-permute-start.59 = (bf16[128,256]{1,0:T(8,128)(2,1)S(1)}, bf16[128,256]{1,0:T(8,128)(2,1)S(1)}, u32[]{:S(2)}, u32[]{:S(2)}) collective-permute-start(bf16[128,256]{1,0:T(8,128)(2,1)S(1)} %get-tuple-element.173), channel_id=1, source_target_pairs={{0,4},{1,2},{2,1},{3,7},{4,0},{5,6},{6,5},{7,3},{8,12},{9,10},{10,... | collective-permute-start | bytes 196616 | tf_op jit(solution)/shard_map/ppermute | solution.py:304
  (14 other events, 33.5 us)

commit v15 on v14

--- a/solution.py
+++ b/solution.py
@@ -292,7 +292,7 @@
             beside = row, partner(col, 0)
         else:
             there = row, partner(col, exchange)
-            beside = partner(row, 0), col
+            beside = (row, there[1] % columns) if columns % 2 == 0 else (partner(row, 0), col)
         for at in (there, beside):
             if 0 <= at[0] < rows and 0 <= at[1] < columns:
                 return at

time: 125 us -> 123 us (0.984)
  starting transfers between devices: 66.6 us -> 58.4 us
  waiting for transfers between devices: 33.8 us -> 39.7 us
    ppermute x43, starting transfers between devices: 47.3 us -> 38.6 us  [swapped(): return lax.ppermute(shard, ('row', 'col'), pairs)]
    ppermute x43, waiting for transfers between devices: 20.5 us -> 23.8 us  [swapped(): return lax.ppermute(shard, ('row', 'col'), pairs)]
    ppermute x18, waiting for transfers between devices: 13.3 us -> 15.9 us  [meeting(): lax.ppermute(shard, axis, pairs)]
  transfers between devices with their start and end apart: 61 -> 61, of which waited for: 27 -> 30; matrix products, arithmetic and copies ran while one was open for 0% -> 0% of each run, Pallas kernels for 12% -> 12%
where the time goes in v15:
time: 123 us; the launch traced here: 122 us
  starting transfers between devices  58.4 us (47%)
  waiting for transfers between devices  39.7 us (32%)
  Pallas kernels  23.6 us (19%)
    ppermute x43, starting transfers between devices, swapped(): return lax.ppermute(shard, ('row', 'col'), pairs)  38.6 us
    ppermute x43, waiting for transfers between devices, swapped(): return lax.ppermute(shard, ('row', 'col'), pairs)  23.8 us
    pallas_call x35, Pallas kernels, call(): pl.pallas_call(body, out_shape=tuple(((pltpu.HBM if away else pltpu.VMEM)...  23.6 us
    ppermute x18, starting transfers between devices, meeting(): lax.ppermute(shard, axis, pairs)  19.7 us
    ppermute x18, waiting for transfers between devices, meeting(): lax.ppermute(shard, axis, pairs)  15.9 us
  transfers between devices with their start and end apart: 61, of which 30 were waited for; matrix products, arithmetic and copies ran while one was open for 0% of the time, Pallas kernels for 12%

profile of v15, /device:TPU:0, one launch (start us, length us, event | category | flops | bytes accessed | tf_op | source)
XLA Modules:
  0.0 122.2 jit_solution(15992546136444132681)
XLA Ops:
  0.0 1.8 %select.1 = (f32[1024,256]{1,0:T(8,128)S(1)}, bf16[1024,256]{1,0:T(8,128)(2,1)S(1)}, bf16[512,1024]{1,0:T(8,128)(2,1)S(1)}, s32[4,128]{1,0:T(4,128)S(1)}, bf16[3...) custom-call(f32[1024,256]{1,0:T(8,128)} %bitcast.11, ...), custom_call_target="tpu_custom_call" | custom-call | flops 268435456 | bytes 1148944 | tf_op jit(solution)/shard_map/select/pallas_call | solution.py:28
  1.8 3.0 %collective-permute-start = (bf16[128,256]{1,0:T(8,128)(2,1)S(1)}, bf16[128,256]{1,0:T(8,128)(2,1)S(1)}, u32[]{:S(2)}, u32[]{:S(2)}) collective-permute-start(bf16[128,256]{1,0:T(8,128)(2,1)S(1)} %get-tuple-element.91), channel_id=1, source_target_pairs={{0,4},{1,5},{2,6},{3,7},{4,0},{5,1},{6,2},{7,3},{8,12},{9,13},{10,... | collective-permute-start | bytes 196616 | tf_op jit(solution)/shard_map/ppermute | solution.py:304
  4.8 1.6 %collective-permute-start.2 = (bf16[128,256]{1,0:T(8,128)(2,1)S(1)}, bf16[128,256]{1,0:T(8,128)(2,1)S(1)}, u32[]{:S(2)}, u32[]{:S(2)}) collective-permute-start(bf16[128,256]{1,0:T(8,128)(2,1)S(1)} %get-tuple-element.93), channel_id=1, source_target_pairs={{0,3},{1,2},{2,1},{3,0},{4,7},{5,6},{6,5},{7,4},{8,11},{9,10},{10,... | collective-permute-start | bytes 196616 | tf_op jit(solution)/shard_map/ppermute | solution.py:304
  6.4 2.6 %inverse_load.1.matrix.rest_0_ = bf16[1536,1536]{1,0:T(8,128)(2,1)S(1)} custom-call(bf16[1536,1536]{1,0:T(8,128)(2,1)} %bitcast.9, bf16[1024,256]{1,0:T(8,128)(2,1)S(1)} %get-tuple-element.90.own_like.owned), custom_call_target="tpu_custom_call" | custom-call | bytes 5242880 | tf_op jit(solution)/shard_map/inverse_load/pallas_call | solution.py:28
  9.3 1.1 collective-permute-start.6
  12.5 1.7 %collective-permute-done.5.refs_2_ = bf16[32,256]{1,0:T(8,128)(2,1)S(1)} collective-permute-done((bf16[32,256]{1,0:T(8,128)(2,1)S(1)}, bf16[32,256]{1,0:T(8,128)(2,1)S(1)}, u32[]{:S(2)}, u32[]{:S(2)}) %collective-permute-start.5) | collective-permute-done | bytes 16416 | tf_op jit(solution)/shard_map/ppermute | solution.py:175
  14.3 3.6 %collective-permute-start.7 = (bf16[64,256]{1,0:T(8,128)(2,1)S(1)}, bf16[64,256]{1,0:T(8,128)(2,1)S(1)}, u32[]{:S(2)}, u32[]{:S(2)}) collective-permute-start(bf16[64,256]{1,0:T(8,128)(2,1)S(1)} %get-tuple-element.97), channel_id=1, source_target_pairs={{0,24},{4,28},{8,16},{12,20},{16,8},{20,12},{24,0},{28,4},{1,25},{... | collective-permute-start | bytes 98312 | tf_op jit(solution)/shard_map/ppermute | solution.py:175
  20.1 2.7 %collective-permute-done.8.refs_1_ = bf16[64,256]{1,0:T(8,128)(2,1)S(1)} collective-permute-done((bf16[64,256]{1,0:T(8,128)(2,1)S(1)}, bf16[64,256]{1,0:T(8,128)(2,1)S(1)}, u32[]{:S(2)}, u32[]{:S(2)}) %collective-permute-start.8) | collective-permute-done | bytes 32800 | tf_op jit(solution)/shard_map/ppermute | solution.py:175
  24.4 2.2 %collective-permute-done.10.theirs = bf16[32,256]{1,0:T(8,128)(2,1)S(1)} collective-permute-done((bf16[32,256]{1,0:T(8,128)(2,1)S(1)}, bf16[32,256]{1,0:T(8,128)(2,1)S(1)}, u32[]{:S(2)}, u32[]{:S(2)}) %collective-permute-start.10) | collective-permute-done | bytes 16416 | tf_op jit(solution)/shard_map/ppermute | solution.py:304
  27.9 1.7 %collective-permute-start.13 = (bf16[128,256]{1,0:T(8,128)(2,1)S(1)}, bf16[128,256]{1,0:T(8,128)(2,1)S(1)}, u32[]{:S(2)}, u32[]{:S(2)}) collective-permute-start(bf16[128,256]{1,0:T(8,128)(2,1)S(1)} %get-tuple-element.115), channel_id=1, source_target_pairs={{0,3},{1,2},{2,1},{3,0},{4,7},{5,6},{6,5},{7,4},{8,11},{9,10},{10,... | collective-permute-start | bytes 196616 | tf_op jit(solution)/shard_map/ppermute | solution.py:304
  29.6 2.6 %spread.1 = (bf16[1024,512]{1,0:T(8,128)(2,1)S(1)}, bf16[1536,1536]{1,0:T(8,128)(2,1)S(1)}) custom-call(bf16[1536,1536]{1,0:T(8,128)(2,1)} %bitcast.10, s32[4,128]{1,0:T(4,128)S(1)} %get-tuple-element.110.masked), custom_call_target="tpu_custom_call" | custom-call | bytes 4720640 | tf_op jit(solution)/shard_map/spread/pallas_call | solution.py:28
  33.5 2.9 %collective-permute-start.15 = (bf16[128,256]{1,0:T(8,128)(2,1)S(1)}, bf16[128,256]{1,0:T(8,128)(2,1)S(1)}, u32[]{:S(2)}, u32[]{:S(2)}) collective-permute-start(bf16[128,256]{1,0:T(8,128)(2,1)S(1)} %get-tuple-element.121), channel_id=1, source_target_pairs={{0,4},{1,5},{2,6},{3,7},{4,0},{5,1},{6,2},{7,3},{8,12},{9,13},{10,... | collective-permute-start | bytes 196616 | tf_op jit(solution)/shard_map/ppermute | solution.py:304
  38.3 1.3 %collective-permute-done.15.g0 = bf16[128,256]{1,0:T(8,128)(2,1)S(1)} collective-permute-done((bf16[128,256]{1,0:T(8,128)(2,1)S(1)}, bf16[128,256]{1,0:T(8,128)(2,1)S(1)}, u32[]{:S(2)}, u32[]{:S(2)}) %collective-permute-start.15) | collective-permute-done | bytes 65568 | tf_op jit(solution)/shard_map/ppermute | solution.py:304
  40.5 2.3 %collective-permute-start.19 = (bf16[128,256]{1,0:T(8,128)(2,1)S(1)}, bf16[128,256]{1,0:T(8,128)(2,1)S(1)}, u32[]{:S(2)}, u32[]{:S(2)}) collective-permute-start(bf16[128,256]{1,0:T(8,128)(2,1)S(1)} %get-tuple-element.125), channel_id=1, source_target_pairs={{0,4},{1,5},{2,6},{3,7},{4,0},{5,1},{6,2},{7,3},{8,12},{9,13},{10,... | collective-permute-start | bytes 196616 | tf_op jit(solution)/shard_map/ppermute | solution.py:304
  43.8 1.5 %collective-permute-done.19.r0 = bf16[128,256]{1,0:T(8,128)(2,1)S(1)} collective-permute-done((bf16[128,256]{1,0:T(8,128)(2,1)S(1)}, bf16[128,256]{1,0:T(8,128)(2,1)S(1)}, u32[]{:S(2)}, u32[]{:S(2)}) %collective-permute-start.19) | collective-permute-done | bytes 65568 | tf_op jit(solution)/shard_map/ppermute | solution.py:304
  47.3 3.5 %collective-permute-start.23 = (bf16[128,256]{1,0:T(8,128)(2,1)S(1)}, bf16[128,256]{1,0:T(8,128)(2,1)S(1)}, u32[]{:S(2)}, u32[]{:S(2)}) collective-permute-start(bf16[128,256]{1,0:T(8,128)(2,1)S(1)} %get-tuple-element.130), channel_id=1, source_target_pairs={{0,4},{1,5},{2,6},{3,7},{4,0},{5,1},{6,2},{7,3},{8,12},{9,13},{10,... | collective-permute-start | bytes 196616 | tf_op jit(solution)/shard_map/ppermute | solution.py:304
  50.9 1.2 collective-permute-start.25
  52.1 1.1 collective-permute-done.23.g0
  53.1 1.5 %collective-permute-done.25.g2 = bf16[128,256]{1,0:T(8,128)(2,1)S(1)} collective-permute-done((bf16[128,256]{1,0:T(8,128)(2,1)S(1)}, bf16[128,256]{1,0:T(8,128)(2,1)S(1)}, u32[]{:S(2)}, u32[]{:S(2)}) %collective-permute-start.25) | collective-permute-done | bytes 65568 | tf_op jit(solution)/shard_map/ppermute | solution.py:304
  54.8 1.2 collective-permute-start.29
  57.0 1.1 collective-permute-done.29.refs_3_
  58.0 1.7 %collective-permute-done.28.refs_2_ = bf16[32,256]{1,0:T(8,128)(2,1)S(1)} collective-permute-done((bf16[32,256]{1,0:T(8,128)(2,1)S(1)}, bf16[32,256]{1,0:T(8,128)(2,1)S(1)}, u32[]{:S(2)}, u32[]{:S(2)}) %collective-permute-start.28) | collective-permute-done | bytes 16416 | tf_op jit(solution)/shard_map/ppermute | solution.py:175
  60.0 3.0 %collective-permute-start.30 = (bf16[64,256]{1,0:T(8,128)(2,1)S(1)}, bf16[64,256]{1,0:T(8,128)(2,1)S(1)}, u32[]{:S(2)}, u32[]{:S(2)}) collective-permute-start(bf16[64,256]{1,0:T(8,128)(2,1)S(1)} %get-tuple-element.135), channel_id=1, source_target_pairs={{0,24},{4,28},{8,16},{12,20},{16,8},{20,12},{24,0},{28,4},{1,25},{... | collective-permute-start | bytes 98312 | tf_op jit(solution)/shard_map/ppermute | solution.py:175
  63.0 1.5 %collective-permute-start.32 = (bf16[64,256]{1,0:T(8,128)(2,1)S(1)}, bf16[64,256]{1,0:T(8,128)(2,1)S(1)}, u32[]{:S(2)}, u32[]{:S(2)}) collective-permute-start(bf16[64,256]{1,0:T(8,128)(2,1)S(1)} %get-tuple-element.137), channel_id=1, source_target_pairs={{0,8},{4,12},{8,0},{12,4},{16,24},{20,28},{24,16},{28,20},{1,9},{5... | collective-permute-start | bytes 98312 | tf_op jit(solution)/shard_map/ppermute | solution.py:175
  65.9 2.1 %collective-permute-done.31.refs_1_ = bf16[64,256]{1,0:T(8,128)(2,1)S(1)} collective-permute-done((bf16[64,256]{1,0:T(8,128)(2,1)S(1)}, bf16[64,256]{1,0:T(8,128)(2,1)S(1)}, u32[]{:S(2)}, u32[]{:S(2)}) %collective-permute-start.31) | collective-permute-done | bytes 32800 | tf_op jit(solution)/shard_map/ppermute | solution.py:175
  69.2 2.7 %collective-permute-done.33.theirs = bf16[32,256]{1,0:T(8,128)(2,1)S(1)} collective-permute-done((bf16[32,256]{1,0:T(8,128)(2,1)S(1)}, bf16[32,256]{1,0:T(8,128)(2,1)S(1)}, u32[]{:S(2)}, u32[]{:S(2)}) %collective-permute-start.33) | collective-permute-done | bytes 16416 | tf_op jit(solution)/shard_map/ppermute | solution.py:304
  72.6 1.2 %collective-permute-start.36 = (bf16[128,256]{1,0:T(8,128)(2,1)S(1)}, bf16[128,256]{1,0:T(8,128)(2,1)S(1)}, u32[]{:S(2)}, u32[]{:S(2)}) collective-permute-start(bf16[128,256]{1,0:T(8,128)(2,1)S(1)} %get-tuple-element.145), channel_id=1, source_target_pairs={{0,3},{1,2},{2,1},{3,0},{4,7},{5,6},{6,5},{7,4},{8,11},{9,10},{10,... | collective-permute-start | bytes 196616 | tf_op jit(solution)/shard_map/ppermute | solution.py:304
  73.9 2.6 %collective-permute-done.34.refs_5_ = bf16[128,256]{1,0:T(8,128)(2,1)S(1)} collective-permute-done((bf16[128,256]{1,0:T(8,128)(2,1)S(1)}, bf16[128,256]{1,0:T(8,128)(2,1)S(1)}, u32[]{:S(2)}, u32[]{:S(2)}) %collective-permute-start.34) | collective-permute-done | bytes 65568 | tf_op jit(solution)/shard_map/ppermute | solution.py:304
  77.8 3.0 %collective-permute-start.38 = (bf16[128,256]{1,0:T(8,128)(2,1)S(1)}, bf16[128,256]{1,0:T(8,128)(2,1)S(1)}, u32[]{:S(2)}, u32[]{:S(2)}) collective-permute-start(bf16[128,256]{1,0:T(8,128)(2,1)S(1)} %get-tuple-element.149), channel_id=1, source_target_pairs={{0,4},{1,5},{2,6},{3,7},{4,0},{5,1},{6,2},{7,3},{8,12},{9,13},{10,... | collective-permute-start | bytes 196616 | tf_op jit(solution)/shard_map/ppermute | solution.py:304
  81.8 1.2 operator_own.3.partial
  83.1 1.5 %collective-permute-done.40.g2 = bf16[128,256]{1,0:T(8,128)(2,1)S(1)} collective-permute-done((bf16[128,256]{1,0:T(8,128)(2,1)S(1)}, bf16[128,256]{1,0:T(8,128)(2,1)S(1)}, u32[]{:S(2)}, u32[]{:S(2)}) %collective-permute-start.40) | collective-permute-done | bytes 65568 | tf_op jit(solution)/shard_map/ppermute | solution.py:304
  84.9 1.9 %collective-permute-start.42 = (bf16[128,256]{1,0:T(8,128)(2,1)S(1)}, bf16[128,256]{1,0:T(8,128)(2,1)S(1)}, u32[]{:S(2)}, u32[]{:S(2)}) collective-permute-start(bf16[128,256]{1,0:T(8,128)(2,1)S(1)} %get-tuple-element.153), channel_id=1, source_target_pairs={{0,4},{1,5},{2,6},{3,7},{4,0},{5,1},{6,2},{7,3},{8,12},{9,13},{10,... | collective-permute-start | bytes 196616 | tf_op jit(solution)/shard_map/ppermute | solution.py:304
  86.8 1.2 collective-permute-start.44
  88.0 1.4 %collective-permute-done.42.r0 = bf16[128,256]{1,0:T(8,128)(2,1)S(1)} collective-permute-done((bf16[128,256]{1,0:T(8,128)(2,1)S(1)}, bf16[128,256]{1,0:T(8,128)(2,1)S(1)}, u32[]{:S(2)}, u32[]{:S(2)}) %collective-permute-start.42) | collective-permute-done | bytes 65568 | tf_op jit(solution)/shard_map/ppermute | solution.py:304
  91.4 3.5 %collective-permute-start.46 = (bf16[128,256]{1,0:T(8,128)(2,1)S(1)}, bf16[128,256]{1,0:T(8,128)(2,1)S(1)}, u32[]{:S(2)}, u32[]{:S(2)}) collective-permute-start(bf16[128,256]{1,0:T(8,128)(2,1)S(1)} %get-tuple-element.158), channel_id=1, source_target_pairs={{0,4},{1,5},{2,6},{3,7},{4,0},{5,1},{6,2},{7,3},{8,12},{9,13},{10,... | collective-permute-start | bytes 196616 | tf_op jit(solution)/shard_map/ppermute | solution.py:304
  94.9 1.3 %collective-permute-start.48 = (bf16[128,256]{1,0:T(8,128)(2,1)S(1)}, bf16[128,256]{1,0:T(8,128)(2,1)S(1)}, u32[]{:S(2)}, u32[]{:S(2)}) collective-permute-start(bf16[128,256]{1,0:T(8,128)(2,1)S(1)} %get-tuple-element.160), channel_id=1, source_target_pairs={{0,3},{1,2},{2,1},{3,0},{4,7},{5,6},{6,5},{7,4},{8,11},{9,10},{10,... | collective-permute-start | bytes 196616 | tf_op jit(solution)/shard_map/ppermute | solution.py:304
  97.1 1.5 %collective-permute-done.48.g2 = bf16[128,256]{1,0:T(8,128)(2,1)S(1)} collective-permute-done((bf16[128,256]{1,0:T(8,128)(2,1)S(1)}, bf16[128,256]{1,0:T(8,128)(2,1)S(1)}, u32[]{:S(2)}, u32[]{:S(2)}) %collective-permute-start.48) | collective-permute-done | bytes 65568 | tf_op jit(solution)/shard_map/ppermute | solution.py:304
  98.9 1.3 %collective-permute-start.52 = (bf16[32,256]{1,0:T(8,128)(2,1)S(1)}, bf16[32,256]{1,0:T(8,128)(2,1)S(1)}, u32[]{:S(2)}, u32[]{:S(2)}) collective-permute-start(bf16[32,256]{1,0:T(8,128)(2,1)S(1)} %restrict.5.refs_0_), channel_id=1, source_target_pairs={{0,3},{1,2},{2,1},{3,0},{4,7},{5,6},{6,5},{7,4},{8,11},{9,10},{10,... | collective-permute-start | bytes 49160 | tf_op jit(solution)/shard_map/ppermute | solution.py:175
  102.1 1.8 %collective-permute-done.51.refs_2_ = bf16[32,256]{1,0:T(8,128)(2,1)S(1)} collective-permute-done((bf16[32,256]{1,0:T(8,128)(2,1)S(1)}, bf16[32,256]{1,0:T(8,128)(2,1)S(1)}, u32[]{:S(2)}, u32[]{:S(2)}) %collective-permute-start.51) | collective-permute-done | bytes 16416 | tf_op jit(solution)/shard_map/ppermute | solution.py:175
  104.1 2.5 %collective-permute-start.53 = (bf16[64,256]{1,0:T(8,128)(2,1)S(1)}, bf16[64,256]{1,0:T(8,128)(2,1)S(1)}, u32[]{:S(2)}, u32[]{:S(2)}) collective-permute-start(bf16[64,256]{1,0:T(8,128)(2,1)S(1)} %get-tuple-element.163), channel_id=1, source_target_pairs={{0,24},{4,28},{8,16},{12,20},{16,8},{20,12},{24,0},{28,4},{1,25},{... | collective-permute-start | bytes 98312 | tf_op jit(solution)/shard_map/ppermute | solution.py:175
  107.1 1.4 %collective-permute-start.55 = (bf16[64,256]{1,0:T(8,128)(2,1)S(1)}, bf16[64,256]{1,0:T(8,128)(2,1)S(1)}, u32[]{:S(2)}, u32[]{:S(2)}) collective-permute-start(bf16[64,256]{1,0:T(8,128)(2,1)S(1)} %get-tuple-element.165), channel_id=1, source_target_pairs={{0,8},{4,12},{8,0},{12,4},{16,24},{20,28},{24,16},{28,20},{1,9},{5... | collective-permute-start | bytes 98312 | tf_op jit(solution)/shard_map/ppermute | solution.py:175
  110.1 1.3 %collective-permute-done.54.refs_1_ = bf16[64,256]{1,0:T(8,128)(2,1)S(1)} collective-permute-done((bf16[64,256]{1,0:T(8,128)(2,1)S(1)}, bf16[64,256]{1,0:T(8,128)(2,1)S(1)}, u32[]{:S(2)}, u32[]{:S(2)}) %collective-permute-start.54) | collective-permute-done | bytes 32800 | tf_op jit(solution)/shard_map/ppermute | solution.py:175
  111.4 1.6 %collective-permute-start.56 = (bf16[32,256]{1,0:T(8,128)(2,1)S(1)}, bf16[32,256]{1,0:T(8,128)(2,1)S(1)}, u32[]{:S(2)}, u32[]{:S(2)}) collective-permute-start(bf16[32,256]{1,0:T(8,128)(2,1)S(1)} %get-tuple-element.168), channel_id=1, source_target_pairs={{0,4},{1,5},{2,6},{3,7},{4,0},{5,1},{6,2},{7,3},{8,12},{9,13},{10,... | collective-permute-start | bytes 49160 | tf_op jit(solution)/shard_map/ppermute | solution.py:304
  113.6 1.7 %collective-permute-done.56.theirs = bf16[32,256]{1,0:T(8,128)(2,1)S(1)} collective-permute-done((bf16[32,256]{1,0:T(8,128)(2,1)S(1)}, bf16[32,256]{1,0:T(8,128)(2,1)S(1)}, u32[]{:S(2)}, u32[]{:S(2)}) %collective-permute-start.56) | collective-permute-done | bytes 16416 | tf_op jit(solution)/shard_map/ppermute | solution.py:304
  115.5 1.6 %collective-permute-start.57 = (bf16[128,256]{1,0:T(8,128)(2,1)S(1)}, bf16[128,256]{1,0:T(8,128)(2,1)S(1)}, u32[]{:S(2)}, u32[]{:S(2)}) collective-permute-start(bf16[128,256]{1,0:T(8,128)(2,1)S(1)} %get-tuple-element.171), channel_id=1, source_target_pairs={{0,4},{1,5},{2,6},{3,7},{4,0},{5,1},{6,2},{7,3},{8,12},{9,13},{10,... | collective-permute-start | bytes 196616 | tf_op jit(solution)/shard_map/ppermute | solution.py:304
  117.1 1.1 collective-permute-start.59
  118.2 1.6 %collective-permute-done.57.refs_5_ = bf16[128,256]{1,0:T(8,128)(2,1)S(1)} collective-permute-done((bf16[128,256]{1,0:T(8,128)(2,1)S(1)}, bf16[128,256]{1,0:T(8,128)(2,1)S(1)}, u32[]{:S(2)}, u32[]{:S(2)}) %collective-permute-start.57) | collective-permute-done | bytes 65568 | tf_op jit(solution)/shard_map/ppermute | solution.py:304
  120.9 1.2 %last_update.1 = f32[1024,256]{1,0:T(8,128)} custom-call(f32[1024,256]{1,0:T(8,128)S(1)} %base.5, bf16[1024,512]{1,0:T(8,128)(2,1)S(1)} %get-tuple-element.111.refs_3_.spread.refs_4_, bf16[128,256]{1,0:T(8,128)(2,1)S(1)} %collective-permute-done.59.r2, bf16[128,256]{1,0:T(8,128)(2,1)S(1)} %collective-permute-done.60.r3), custom_call_target="tpu_custom_call" | custom-call | flops 268435456 | bytes 2228224 | tf_op jit(solution)/shard_map/last_update/pallas_call | solution.py:28
  (111 shorter events, 31.5 us)
Async XLA Ops:
  1.8 7.2 %collective-permute-start = (bf16[128,256]{1,0:T(8,128)(2,1)S(1)}, bf16[128,256]{1,0:T(8,128)(2,1)S(1)}, u32[]{:S(2)}, u32[]{:S(2)}) collective-permute-start(bf16[128,256]{1,0:T(8,128)(2,1)S(1)} %get-tuple-element.91), channel_id=1, source_target_pairs={{0,4},{1,5},{2,6},{3,7},{4,0},{5,1},{6,2},{7,3},{8,12},{9,13},{10,... | collective-permute-start | bytes 196616 | tf_op jit(solution)/shard_map/ppermute | solution.py:304
  4.8 4.2 %collective-permute-start.1 = (bf16[128,256]{1,0:T(8,128)(2,1)S(1)}, bf16[128,256]{1,0:T(8,128)(2,1)S(1)}, u32[]{:S(2)}, u32[]{:S(2)}) collective-permute-start(bf16[128,256]{1,0:T(8,128)(2,1)S(1)} %get-tuple-element.92), channel_id=1, source_target_pairs={{0,1},{1,0},{2,3},{3,2},{4,8},{5,9},{6,10},{7,11},{8,4},{9,5},{10,... | collective-permute-start | bytes 196616 | tf_op jit(solution)/shard_map/ppermute | solution.py:304
  4.8 4.2 %collective-permute-start.2 = (bf16[128,256]{1,0:T(8,128)(2,1)S(1)}, bf16[128,256]{1,0:T(8,128)(2,1)S(1)}, u32[]{:S(2)}, u32[]{:S(2)}) collective-permute-start(bf16[128,256]{1,0:T(8,128)(2,1)S(1)} %get-tuple-element.93), channel_id=1, source_target_pairs={{0,3},{1,2},{2,1},{3,0},{4,7},{5,6},{6,5},{7,4},{8,11},{9,10},{10,... | collective-permute-start | bytes 196616 | tf_op jit(solution)/shard_map/ppermute | solution.py:304
  9.3 3.2 %collective-permute-start.6 = (bf16[32,256]{1,0:T(8,128)(2,1)S(1)}, bf16[32,256]{1,0:T(8,128)(2,1)S(1)}, u32[]{:S(2)}, u32[]{:S(2)}) collective-permute-start(bf16[32,256]{1,0:T(8,128)(2,1)S(1)} %restrict.3.refs_0_), channel_id=1, source_target_pairs={{0,3},{1,2},{2,1},{3,0},{4,7},{5,6},{6,5},{7,4},{8,11},{9,10},{10,... | collective-permute-start | bytes 49160 | tf_op jit(solution)/shard_map/ppermute | solution.py:175
  10.4 3.7 %collective-permute-start.5 = (bf16[32,256]{1,0:T(8,128)(2,1)S(1)}, bf16[32,256]{1,0:T(8,128)(2,1)S(1)}, u32[]{:S(2)}, u32[]{:S(2)}) collective-permute-start(bf16[32,256]{1,0:T(8,128)(2,1)S(1)} %restrict.3.refs_0_), channel_id=1, source_target_pairs={{0,2},{1,3},{2,0},{3,1},{4,6},{5,7},{6,4},{7,5},{8,10},{9,11},{10,... | collective-permute-start | bytes 49160 | tf_op jit(solution)/shard_map/ppermute | solution.py:175
  14.3 5.8 %collective-permute-start.7 = (bf16[64,256]{1,0:T(8,128)(2,1)S(1)}, bf16[64,256]{1,0:T(8,128)(2,1)S(1)}, u32[]{:S(2)}, u32[]{:S(2)}) collective-permute-start(bf16[64,256]{1,0:T(8,128)(2,1)S(1)} %get-tuple-element.97), channel_id=1, source_target_pairs={{0,24},{4,28},{8,16},{12,20},{16,8},{20,12},{24,0},{28,4},{1,25},{... | collective-permute-start | bytes 98312 | tf_op jit(solution)/shard_map/ppermute | solution.py:175
  18.0 4.8 %collective-permute-start.8 = (bf16[64,256]{1,0:T(8,128)(2,1)S(1)}, bf16[64,256]{1,0:T(8,128)(2,1)S(1)}, u32[]{:S(2)}, u32[]{:S(2)}) collective-permute-start(bf16[64,256]{1,0:T(8,128)(2,1)S(1)} %get-tuple-element.98), channel_id=1, source_target_pairs={{0,16},{4,20},{8,24},{12,28},{16,0},{20,4},{24,8},{28,12},{1,17},{... | collective-permute-start | bytes 98312 | tf_op jit(solution)/shard_map/ppermute | solution.py:175
  18.0 4.8 %collective-permute-start.9 = (bf16[64,256]{1,0:T(8,128)(2,1)S(1)}, bf16[64,256]{1,0:T(8,128)(2,1)S(1)}, u32[]{:S(2)}, u32[]{:S(2)}) collective-permute-start(bf16[64,256]{1,0:T(8,128)(2,1)S(1)} %get-tuple-element.99), channel_id=1, source_target_pairs={{0,8},{4,12},{8,0},{12,4},{16,24},{20,28},{24,16},{28,20},{1,9},{5... | collective-permute-start | bytes 98312 | tf_op jit(solution)/shard_map/ppermute | solution.py:175
  22.8 3.8 %collective-permute-start.10 = (bf16[32,256]{1,0:T(8,128)(2,1)S(1)}, bf16[32,256]{1,0:T(8,128)(2,1)S(1)}, u32[]{:S(2)}, u32[]{:S(2)}) collective-permute-start(bf16[32,256]{1,0:T(8,128)(2,1)S(1)} %get-tuple-element.102), channel_id=1, source_target_pairs={{0,4},{1,5},{2,6},{3,7},{4,0},{5,1},{6,2},{7,3},{8,12},{9,13},{10,... | collective-permute-start | bytes 49160 | tf_op jit(solution)/shard_map/ppermute | solution.py:304
  26.9 5.3 %collective-permute-start.11 = (bf16[128,256]{1,0:T(8,128)(2,1)S(1)}, bf16[128,256]{1,0:T(8,128)(2,1)S(1)}, u32[]{:S(2)}, u32[]{:S(2)}) collective-permute-start(bf16[128,256]{1,0:T(8,128)(2,1)S(1)} %get-tuple-element.112), channel_id=1, source_target_pairs={{0,4},{1,5},{2,6},{3,7},{4,0},{5,1},{6,2},{7,3},{8,12},{9,13},{10,... | collective-permute-start | bytes 196616 | tf_op jit(solution)/shard_map/ppermute | solution.py:304
  27.9 4.3 %collective-permute-start.12 = (bf16[128,256]{1,0:T(8,128)(2,1)S(1)}, bf16[128,256]{1,0:T(8,128)(2,1)S(1)}, u32[]{:S(2)}, u32[]{:S(2)}) collective-permute-start(bf16[128,256]{1,0:T(8,128)(2,1)S(1)} %get-tuple-element.113), channel_id=1, source_target_pairs={{0,1},{1,0},{2,3},{3,2},{4,8},{5,9},{6,10},{7,11},{8,4},{9,5},{10,... | collective-permute-start | bytes 196616 | tf_op jit(solution)/shard_map/ppermute | solution.py:304
  27.9 4.7 %collective-permute-start.13 = (bf16[128,256]{1,0:T(8,128)(2,1)S(1)}, bf16[128,256]{1,0:T(8,128)(2,1)S(1)}, u32[]{:S(2)}, u32[]{:S(2)}) collective-permute-start(bf16[128,256]{1,0:T(8,128)(2,1)S(1)} %get-tuple-element.115), channel_id=1, source_target_pairs={{0,3},{1,2},{2,1},{3,0},{4,7},{5,6},{6,5},{7,4},{8,11},{9,10},{10,... | collective-permute-start | bytes 196616 | tf_op jit(solution)/shard_map/ppermute | solution.py:304
  29.6 3.1 %collective-permute-start.14 = (bf16[128,256]{1,0:T(8,128)(2,1)S(1)}, bf16[128,256]{1,0:T(8,128)(2,1)S(1)}, u32[]{:S(2)}, u32[]{:S(2)}) collective-permute-start(bf16[128,256]{1,0:T(8,128)(2,1)S(1)} %get-tuple-element.116), channel_id=1, source_target_pairs={{0,1},{1,0},{2,3},{3,2},{4,5},{5,4},{6,7},{7,6},{8,9},{9,8},{10,11... | collective-permute-start | bytes 196616 | tf_op jit(solution)/shard_map/ppermute | solution.py:304
  33.5 6.1 %collective-permute-start.15 = (bf16[128,256]{1,0:T(8,128)(2,1)S(1)}, bf16[128,256]{1,0:T(8,128)(2,1)S(1)}, u32[]{:S(2)}, u32[]{:S(2)}) collective-permute-start(bf16[128,256]{1,0:T(8,128)(2,1)S(1)} %get-tuple-element.121), channel_id=1, source_target_pairs={{0,4},{1,5},{2,6},{3,7},{4,0},{5,1},{6,2},{7,3},{8,12},{9,13},{10,... | collective-permute-start | bytes 196616 | tf_op jit(solution)/shard_map/ppermute | solution.py:304
  36.4 3.2 %collective-permute-start.16 = (bf16[128,256]{1,0:T(8,128)(2,1)S(1)}, bf16[128,256]{1,0:T(8,128)(2,1)S(1)}, u32[]{:S(2)}, u32[]{:S(2)}) collective-permute-start(bf16[128,256]{1,0:T(8,128)(2,1)S(1)} %get-tuple-element.122), channel_id=1, source_target_pairs={{0,1},{1,0},{2,3},{3,2},{4,8},{5,9},{6,10},{7,11},{8,4},{9,5},{10,... | collective-permute-start | bytes 196616 | tf_op jit(solution)/shard_map/ppermute | solution.py:304
  36.4 3.7 %collective-permute-start.17 = (bf16[128,256]{1,0:T(8,128)(2,1)S(1)}, bf16[128,256]{1,0:T(8,128)(2,1)S(1)}, u32[]{:S(2)}, u32[]{:S(2)}) collective-permute-start(bf16[128,256]{1,0:T(8,128)(2,1)S(1)} %get-tuple-element.123), channel_id=1, source_target_pairs={{0,3},{1,2},{2,1},{3,0},{4,7},{5,6},{6,5},{7,4},{8,11},{9,10},{10,... | collective-permute-start | bytes 196616 | tf_op jit(solution)/shard_map/ppermute | solution.py:304
  37.3 2.8 %collective-permute-start.18 = (bf16[128,256]{1,0:T(8,128)(2,1)S(1)}, bf16[128,256]{1,0:T(8,128)(2,1)S(1)}, u32[]{:S(2)}, u32[]{:S(2)}) collective-permute-start(bf16[128,256]{1,0:T(8,128)(2,1)S(1)} %get-tuple-element.124), channel_id=1, source_target_pairs={{0,1},{1,0},{2,3},{3,2},{4,5},{5,4},{6,7},{7,6},{8,9},{9,8},{10,11... | collective-permute-start | bytes 196616 | tf_op jit(solution)/shard_map/ppermute | solution.py:304
  40.5 4.8 %collective-permute-start.19 = (bf16[128,256]{1,0:T(8,128)(2,1)S(1)}, bf16[128,256]{1,0:T(8,128)(2,1)S(1)}, u32[]{:S(2)}, u32[]{:S(2)}) collective-permute-start(bf16[128,256]{1,0:T(8,128)(2,1)S(1)} %get-tuple-element.125), channel_id=1, source_target_pairs={{0,4},{1,5},{2,6},{3,7},{4,0},{5,1},{6,2},{7,3},{8,12},{9,13},{10,... | collective-permute-start | bytes 196616 | tf_op jit(solution)/shard_map/ppermute | solution.py:304
  42.7 3.7 %collective-permute-start.21 = (bf16[128,256]{1,0:T(8,128)(2,1)S(1)}, bf16[128,256]{1,0:T(8,128)(2,1)S(1)}, u32[]{:S(2)}, u32[]{:S(2)}) collective-permute-start(bf16[128,256]{1,0:T(8,128)(2,1)S(1)} %get-tuple-element.127), channel_id=1, source_target_pairs={{0,3},{1,2},{2,1},{3,0},{4,7},{5,6},{6,5},{7,4},{8,11},{9,10},{10,... | collective-permute-start | bytes 196616 | tf_op jit(solution)/shard_map/ppermute | solution.py:304
  47.3 5.8 %collective-permute-start.23 = (bf16[128,256]{1,0:T(8,128)(2,1)S(1)}, bf16[128,256]{1,0:T(8,128)(2,1)S(1)}, u32[]{:S(2)}, u32[]{:S(2)}) collective-permute-start(bf16[128,256]{1,0:T(8,128)(2,1)S(1)} %get-tuple-element.130), channel_id=1, source_target_pairs={{0,4},{1,5},{2,6},{3,7},{4,0},{5,1},{6,2},{7,3},{8,12},{9,13},{10,... | collective-permute-start | bytes 196616 | tf_op jit(solution)/shard_map/ppermute | solution.py:304
  50.9 3.7 %collective-permute-start.25 = (bf16[128,256]{1,0:T(8,128)(2,1)S(1)}, bf16[128,256]{1,0:T(8,128)(2,1)S(1)}, u32[]{:S(2)}, u32[]{:S(2)}) collective-permute-start(bf16[128,256]{1,0:T(8,128)(2,1)S(1)} %get-tuple-element.132), channel_id=1, source_target_pairs={{0,3},{1,2},{2,1},{3,0},{4,7},{5,6},{6,5},{7,4},{8,11},{9,10},{10,... | collective-permute-start | bytes 196616 | tf_op jit(solution)/shard_map/ppermute | solution.py:304
  54.8 3.2 %collective-permute-start.29 = (bf16[32,256]{1,0:T(8,128)(2,1)S(1)}, bf16[32,256]{1,0:T(8,128)(2,1)S(1)}, u32[]{:S(2)}, u32[]{:S(2)}) collective-permute-start(bf16[32,256]{1,0:T(8,128)(2,1)S(1)} %restrict.4.refs_0_), channel_id=1, source_target_pairs={{0,3},{1,2},{2,1},{3,0},{4,7},{5,6},{6,5},{7,4},{8,11},{9,10},{10,... | collective-permute-start | bytes 49160 | tf_op jit(solution)/shard_map/ppermute | solution.py:175
  56.0 3.7 %collective-permute-start.28 = (bf16[32,256]{1,0:T(8,128)(2,1)S(1)}, bf16[32,256]{1,0:T(8,128)(2,1)S(1)}, u32[]{:S(2)}, u32[]{:S(2)}) collective-permute-start(bf16[32,256]{1,0:T(8,128)(2,1)S(1)} %restrict.4.refs_0_), channel_id=1, source_target_pairs={{0,2},{1,3},{2,0},{3,1},{4,6},{5,7},{6,4},{7,5},{8,10},{9,11},{10,... | collective-permute-start | bytes 49160 | tf_op jit(solution)/shard_map/ppermute | solution.py:175
  57.0 2.8 %collective-permute-start.27 = (bf16[32,256]{1,0:T(8,128)(2,1)S(1)}, bf16[32,256]{1,0:T(8,128)(2,1)S(1)}, u32[]{:S(2)}, u32[]{:S(2)}) collective-permute-start(bf16[32,256]{1,0:T(8,128)(2,1)S(1)} %restrict.4.refs_0_), channel_id=1, source_target_pairs={{0,1},{1,0},{2,3},{3,2},{4,5},{5,4},{6,7},{7,6},{8,9},{9,8},{10,11... | collective-permute-start | bytes 49160 | tf_op jit(solution)/shard_map/ppermute | solution.py:175
  60.0 5.9 %collective-permute-start.30 = (bf16[64,256]{1,0:T(8,128)(2,1)S(1)}, bf16[64,256]{1,0:T(8,128)(2,1)S(1)}, u32[]{:S(2)}, u32[]{:S(2)}) collective-permute-start(bf16[64,256]{1,0:T(8,128)(2,1)S(1)} %get-tuple-element.135), channel_id=1, source_target_pairs={{0,24},{4,28},{8,16},{12,20},{16,8},{20,12},{24,0},{28,4},{1,25},{... | collective-permute-start | bytes 98312 | tf_op jit(solution)/shard_map/ppermute | solution.py:175
  62.9 5.1 %collective-permute-start.31 = (bf16[64,256]{1,0:T(8,128)(2,1)S(1)}, bf16[64,256]{1,0:T(8,128)(2,1)S(1)}, u32[]{:S(2)}, u32[]{:S(2)}) collective-permute-start(bf16[64,256]{1,0:T(8,128)(2,1)S(1)} %get-tuple-element.136), channel_id=1, source_target_pairs={{0,16},{4,20},{8,24},{12,28},{16,0},{20,4},{24,8},{28,12},{1,17},{... | collective-permute-start | bytes 98312 | tf_op jit(solution)/shard_map/ppermute | solution.py:175
  63.0 5.1 %collective-permute-start.32 = (bf16[64,256]{1,0:T(8,128)(2,1)S(1)}, bf16[64,256]{1,0:T(8,128)(2,1)S(1)}, u32[]{:S(2)}, u32[]{:S(2)}) collective-permute-start(bf16[64,256]{1,0:T(8,128)(2,1)S(1)} %get-tuple-element.137), channel_id=1, source_target_pairs={{0,8},{4,12},{8,0},{12,4},{16,24},{20,28},{24,16},{28,20},{1,9},{5... | collective-permute-start | bytes 98312 | tf_op jit(solution)/shard_map/ppermute | solution.py:175
  68.1 3.8 %collective-permute-start.33 = (bf16[32,256]{1,0:T(8,128)(2,1)S(1)}, bf16[32,256]{1,0:T(8,128)(2,1)S(1)}, u32[]{:S(2)}, u32[]{:S(2)}) collective-permute-start(bf16[32,256]{1,0:T(8,128)(2,1)S(1)} %get-tuple-element.140), channel_id=1, source_target_pairs={{0,4},{1,5},{2,6},{3,7},{4,0},{5,1},{6,2},{7,3},{8,12},{9,13},{10,... | collective-permute-start | bytes 49160 | tf_op jit(solution)/shard_map/ppermute | solution.py:304
  72.1 4.3 %collective-permute-start.34 = (bf16[128,256]{1,0:T(8,128)(2,1)S(1)}, bf16[128,256]{1,0:T(8,128)(2,1)S(1)}, u32[]{:S(2)}, u32[]{:S(2)}) collective-permute-start(bf16[128,256]{1,0:T(8,128)(2,1)S(1)} %get-tuple-element.143), channel_id=1, source_target_pairs={{0,4},{1,5},{2,6},{3,7},{4,0},{5,1},{6,2},{7,3},{8,12},{9,13},{10,... | collective-permute-start | bytes 196616 | tf_op jit(solution)/shard_map/ppermute | solution.py:304
  72.6 3.8 %collective-permute-start.35 = (bf16[128,256]{1,0:T(8,128)(2,1)S(1)}, bf16[128,256]{1,0:T(8,128)(2,1)S(1)}, u32[]{:S(2)}, u32[]{:S(2)}) collective-permute-start(bf16[128,256]{1,0:T(8,128)(2,1)S(1)} %get-tuple-element.144), channel_id=1, source_target_pairs={{0,1},{1,0},{2,3},{3,2},{4,8},{5,9},{6,10},{7,11},{8,4},{9,5},{10,... | collective-permute-start | bytes 196616 | tf_op jit(solution)/shard_map/ppermute | solution.py:304
  72.6 4.3 %collective-permute-start.36 = (bf16[128,256]{1,0:T(8,128)(2,1)S(1)}, bf16[128,256]{1,0:T(8,128)(2,1)S(1)}, u32[]{:S(2)}, u32[]{:S(2)}) collective-permute-start(bf16[128,256]{1,0:T(8,128)(2,1)S(1)} %get-tuple-element.145), channel_id=1, source_target_pairs={{0,3},{1,2},{2,1},{3,0},{4,7},{5,6},{6,5},{7,4},{8,11},{9,10},{10,... | collective-permute-start | bytes 196616 | tf_op jit(solution)/shard_map/ppermute | solution.py:304
  73.9 3.1 %collective-permute-start.37 = (bf16[128,256]{1,0:T(8,128)(2,1)S(1)}, bf16[128,256]{1,0:T(8,128)(2,1)S(1)}, u32[]{:S(2)}, u32[]{:S(2)}) collective-permute-start(bf16[128,256]{1,0:T(8,128)(2,1)S(1)} %get-tuple-element.146), channel_id=1, source_target_pairs={{0,1},{1,0},{2,3},{3,2},{4,5},{5,4},{6,7},{7,6},{8,9},{9,8},{10,11... | collective-permute-start | bytes 196616 | tf_op jit(solution)/shard_map/ppermute | solution.py:304
  77.8 5.2 %collective-permute-start.38 = (bf16[128,256]{1,0:T(8,128)(2,1)S(1)}, bf16[128,256]{1,0:T(8,128)(2,1)S(1)}, u32[]{:S(2)}, u32[]{:S(2)}) collective-permute-start(bf16[128,256]{1,0:T(8,128)(2,1)S(1)} %get-tuple-element.149), channel_id=1, source_target_pairs={{0,4},{1,5},{2,6},{3,7},{4,0},{5,1},{6,2},{7,3},{8,12},{9,13},{10,... | collective-permute-start | bytes 196616 | tf_op jit(solution)/shard_map/ppermute | solution.py:304
  80.8 3.7 %collective-permute-start.40 = (bf16[128,256]{1,0:T(8,128)(2,1)S(1)}, bf16[128,256]{1,0:T(8,128)(2,1)S(1)}, u32[]{:S(2)}, u32[]{:S(2)}) collective-permute-start(bf16[128,256]{1,0:T(8,128)(2,1)S(1)} %get-tuple-element.151), channel_id=1, source_target_pairs={{0,3},{1,2},{2,1},{3,0},{4,7},{5,6},{6,5},{7,4},{8,11},{9,10},{10,... | collective-permute-start | bytes 196616 | tf_op jit(solution)/shard_map/ppermute | solution.py:304
  81.8 2.8 %collective-permute-start.41 = (bf16[128,256]{1,0:T(8,128)(2,1)S(1)}, bf16[128,256]{1,0:T(8,128)(2,1)S(1)}, u32[]{:S(2)}, u32[]{:S(2)}) collective-permute-start(bf16[128,256]{1,0:T(8,128)(2,1)S(1)} %get-tuple-element.152), channel_id=1, source_target_pairs={{0,1},{1,0},{2,3},{3,2},{4,5},{5,4},{6,7},{7,6},{8,9},{9,8},{10,11... | collective-permute-start | bytes 196616 | tf_op jit(solution)/shard_map/ppermute | solution.py:304
  84.9 4.5 %collective-permute-start.42 = (bf16[128,256]{1,0:T(8,128)(2,1)S(1)}, bf16[128,256]{1,0:T(8,128)(2,1)S(1)}, u32[]{:S(2)}, u32[]{:S(2)}) collective-permute-start(bf16[128,256]{1,0:T(8,128)(2,1)S(1)} %get-tuple-element.153), channel_id=1, source_target_pairs={{0,4},{1,5},{2,6},{3,7},{4,0},{5,1},{6,2},{7,3},{8,12},{9,13},{10,... | collective-permute-start | bytes 196616 | tf_op jit(solution)/shard_map/ppermute | solution.py:304
  86.8 3.7 %collective-permute-start.44 = (bf16[128,256]{1,0:T(8,128)(2,1)S(1)}, bf16[128,256]{1,0:T(8,128)(2,1)S(1)}, u32[]{:S(2)}, u32[]{:S(2)}) collective-permute-start(bf16[128,256]{1,0:T(8,128)(2,1)S(1)} %get-tuple-element.155), channel_id=1, source_target_pairs={{0,3},{1,2},{2,1},{3,0},{4,7},{5,6},{6,5},{7,4},{8,11},{9,10},{10,... | collective-permute-start | bytes 196616 | tf_op jit(solution)/shard_map/ppermute | solution.py:304
  91.4 5.7 %collective-permute-start.46 = (bf16[128,256]{1,0:T(8,128)(2,1)S(1)}, bf16[128,256]{1,0:T(8,128)(2,1)S(1)}, u32[]{:S(2)}, u32[]{:S(2)}) collective-permute-start(bf16[128,256]{1,0:T(8,128)(2,1)S(1)} %get-tuple-element.158), channel_id=1, source_target_pairs={{0,4},{1,5},{2,6},{3,7},{4,0},{5,1},{6,2},{7,3},{8,12},{9,13},{10,... | collective-permute-start | bytes 196616 | tf_op jit(solution)/shard_map/ppermute | solution.py:304
  94.9 3.7 %collective-permute-start.48 = (bf16[128,256]{1,0:T(8,128)(2,1)S(1)}, bf16[128,256]{1,0:T(8,128)(2,1)S(1)}, u32[]{:S(2)}, u32[]{:S(2)}) collective-permute-start(bf16[128,256]{1,0:T(8,128)(2,1)S(1)} %get-tuple-element.160), channel_id=1, source_target_pairs={{0,3},{1,2},{2,1},{3,0},{4,7},{5,6},{6,5},{7,4},{8,11},{9,10},{10,... | collective-permute-start | bytes 196616 | tf_op jit(solution)/shard_map/ppermute | solution.py:304
  98.9 3.2 %collective-permute-start.52 = (bf16[32,256]{1,0:T(8,128)(2,1)S(1)}, bf16[32,256]{1,0:T(8,128)(2,1)S(1)}, u32[]{:S(2)}, u32[]{:S(2)}) collective-permute-start(bf16[32,256]{1,0:T(8,128)(2,1)S(1)} %restrict.5.refs_0_), channel_id=1, source_target_pairs={{0,3},{1,2},{2,1},{3,0},{4,7},{5,6},{6,5},{7,4},{8,11},{9,10},{10,... | collective-permute-start | bytes 49160 | tf_op jit(solution)/shard_map/ppermute | solution.py:175
  100.1 3.7 %collective-permute-start.51 = (bf16[32,256]{1,0:T(8,128)(2,1)S(1)}, bf16[32,256]{1,0:T(8,128)(2,1)S(1)}, u32[]{:S(2)}, u32[]{:S(2)}) collective-permute-start(bf16[32,256]{1,0:T(8,128)(2,1)S(1)} %restrict.5.refs_0_), channel_id=1, source_target_pairs={{0,2},{1,3},{2,0},{3,1},{4,6},{5,7},{6,4},{7,5},{8,10},{9,11},{10,... | collective-permute-start | bytes 49160 | tf_op jit(solution)/shard_map/ppermute | solution.py:175
  101.0 2.9 %collective-permute-start.50 = (bf16[32,256]{1,0:T(8,128)(2,1)S(1)}, bf16[32,256]{1,0:T(8,128)(2,1)S(1)}, u32[]{:S(2)}, u32[]{:S(2)}) collective-permute-start(bf16[32,256]{1,0:T(8,128)(2,1)S(1)} %restrict.5.refs_0_), channel_id=1, source_target_pairs={{0,1},{1,0},{2,3},{3,2},{4,5},{5,4},{6,7},{7,6},{8,9},{9,8},{10,11... | collective-permute-start | bytes 49160 | tf_op jit(solution)/shard_map/ppermute | solution.py:175
  104.1 6.0 %collective-permute-start.53 = (bf16[64,256]{1,0:T(8,128)(2,1)S(1)}, bf16[64,256]{1,0:T(8,128)(2,1)S(1)}, u32[]{:S(2)}, u32[]{:S(2)}) collective-permute-start(bf16[64,256]{1,0:T(8,128)(2,1)S(1)} %get-tuple-element.163), channel_id=1, source_target_pairs={{0,24},{4,28},{8,16},{12,20},{16,8},{20,12},{24,0},{28,4},{1,25},{... | collective-permute-start | bytes 98312 | tf_op jit(solution)/shard_map/ppermute | solution.py:175
  106.6 4.8 %collective-permute-start.54 = (bf16[64,256]{1,0:T(8,128)(2,1)S(1)}, bf16[64,256]{1,0:T(8,128)(2,1)S(1)}, u32[]{:S(2)}, u32[]{:S(2)}) collective-permute-start(bf16[64,256]{1,0:T(8,128)(2,1)S(1)} %get-tuple-element.164), channel_id=1, source_target_pairs={{0,16},{4,20},{8,24},{12,28},{16,0},{20,4},{24,8},{28,12},{1,17},{... | collective-permute-start | bytes 98312 | tf_op jit(solution)/shard_map/ppermute | solution.py:175
  107.1 4.3 %collective-permute-start.55 = (bf16[64,256]{1,0:T(8,128)(2,1)S(1)}, bf16[64,256]{1,0:T(8,128)(2,1)S(1)}, u32[]{:S(2)}, u32[]{:S(2)}) collective-permute-start(bf16[64,256]{1,0:T(8,128)(2,1)S(1)} %get-tuple-element.165), channel_id=1, source_target_pairs={{0,8},{4,12},{8,0},{12,4},{16,24},{20,28},{24,16},{28,20},{1,9},{5... | collective-permute-start | bytes 98312 | tf_op jit(solution)/shard_map/ppermute | solution.py:175
  111.4 3.8 %collective-permute-start.56 = (bf16[32,256]{1,0:T(8,128)(2,1)S(1)}, bf16[32,256]{1,0:T(8,128)(2,1)S(1)}, u32[]{:S(2)}, u32[]{:S(2)}) collective-permute-start(bf16[32,256]{1,0:T(8,128)(2,1)S(1)} %get-tuple-element.168), channel_id=1, source_target_pairs={{0,4},{1,5},{2,6},{3,7},{4,0},{5,1},{6,2},{7,3},{8,12},{9,13},{10,... | collective-permute-start | bytes 49160 | tf_op jit(solution)/shard_map/ppermute | solution.py:304
  115.5 4.3 %collective-permute-start.57 = (bf16[128,256]{1,0:T(8,128)(2,1)S(1)}, bf16[128,256]{1,0:T(8,128)(2,1)S(1)}, u32[]{:S(2)}, u32[]{:S(2)}) collective-permute-start(bf16[128,256]{1,0:T(8,128)(2,1)S(1)} %get-tuple-element.171), channel_id=1, source_target_pairs={{0,4},{1,5},{2,6},{3,7},{4,0},{5,1},{6,2},{7,3},{8,12},{9,13},{10,... | collective-permute-start | bytes 196616 | tf_op jit(solution)/shard_map/ppermute | solution.py:304
  117.1 3.7 %collective-permute-start.59 = (bf16[128,256]{1,0:T(8,128)(2,1)S(1)}, bf16[128,256]{1,0:T(8,128)(2,1)S(1)}, u32[]{:S(2)}, u32[]{:S(2)}) collective-permute-start(bf16[128,256]{1,0:T(8,128)(2,1)S(1)} %get-tuple-element.173), channel_id=1, source_target_pairs={{0,3},{1,2},{2,1},{3,0},{4,7},{5,6},{6,5},{7,4},{8,11},{9,10},{10,... | collective-permute-start | bytes 196616 | tf_op jit(solution)/shard_map/ppermute | solution.py:304
  (14 other events, 37.9 us)

commit v16 on v15

--- a/solution.py
+++ b/solution.py
@@ -177,42 +177,45 @@
 
 def parts_kernel(groups, across):
     def body(inverse, *refs):
-        restricted, parts, gathered = refs[:across], refs[across:-1], refs[-1]
+        restricted, (mine, others, gathered) = refs[:across], refs[across:]
         coarse = inverse.shape[1]
         for turn, piece in enumerate(restricted):
             at = pl.multiple_of(met(lax.axis_index("col"), turn, across) * coarse, coarse)
             gathered[pl.ds(at, coarse), :] = piece[...]
-        pair = lax.axis_index("row") // 2
-        for turn, part in enumerate(parts):
-            other = 2 * met(pair, turn, groups // 2)
-            for i in range(2):
-                part[i * coarse : (i + 1) * coarse, :] = product(
-                    inverse[other + i], gathered[...]
-                ).astype(HALF)
+        pair, odd = lax.axis_index("row") // 2, lax.rem(lax.axis_index("row"), 2)
+        for turn in range(groups // 2):
+            low = 2 * met(pair, turn, groups // 2)
+            at = slice(turn * coarse, (turn + 1) * coarse)
+            mine[at, :] = product(inverse[low + odd], gathered[...])
+            others[at, :] = product(inverse[low + 1 - odd], gathered[...]).astype(HALF)
 
     return body
 
 
-def pair_kernel(*refs):
-    *parts, mine, others = refs
-    coarse = mine.shape[0]
-    total = parts[0][...].astype(FULL)
-    for part in parts[1:]:
-        total += part[...].astype(FULL)
-    odd = lax.rem(lax.axis_index("row"), 2) == 1
-    low, high = total[:coarse, :], total[coarse:, :]
-    mine[...] = jnp.where(odd, high, low)
-    others[...] = jnp.where(odd, low, high).astype(HALF)
-
-
-def coarse_kernel(mine, theirs, basis, rim, level, *tiles):
-    tile = tiles[0].shape[0]
-    own = basis.shape[1] - 4 * tile
-    level[...] = (mine[...] + theirs[...].astype(FULL)).astype(HALF)
-    for d in range(4):
-        here = slice(d * tile, (d + 1) * tile)
-        there = slice(own + d * tile, own + (d + 1) * tile)
-        tiles[d][...] = (rim[here, :] + turned_product(basis[:, there], level[...])).astype(HALF)
+def pair_kernel(mine, theirs, *parts):
+    coarse = parts[0].shape[0]
+    for turn, part in enumerate(parts):
+        at = slice(turn * coarse, (turn + 1) * coarse)
+        part[...] = (mine[at, :] + theirs[at, :].astype(FULL)).astype(part.dtype)
+
+
+def coarse_kernel(turns):
+    def body(*refs):
+        parts, (basis, rim, level, *tiles) = refs[:turns], refs[turns:]
+        tile = tiles[0].shape[0]
+        own = basis.shape[1] - 4 * tile
+        total = parts[0][...].astype(FULL)
+        for part in parts[1:]:
+            total += part[...].astype(FULL)
+        level[...] = total.astype(HALF)
+        for d in range(4):
+            here = slice(d * tile, (d + 1) * tile)
+            there = slice(own + d * tile, own + (d + 1) * tile)
+            tiles[d][...] = (
+                rim[here, :] + turned_product(basis[:, there], level[...])
+            ).astype(HALF)
+
+    return body
 
 
 def base_kernel(first):
@@ -436,28 +439,30 @@
             *ghosts,
             flops=2 * local * margin * columns,
         )
-        parts = call(
+        turns = groups // 2
+        stack = (turns * coarse, columns)
+        mine, others = call(
             parts_kernel(groups, across),
             "coarse_part",
-            [((2 * coarse, columns), HALF)] * (groups // 2),
+            [(stack, FULL), (stack, HALF)],
             coarse_inverse,
             *restricted,
             scratch=(pltpu.VMEM((across * coarse, columns), HALF),),
             flops=2 * coarse_inverse.size * columns,
         )
-        parts = [meeting(parts[turn], "row", turn, 2) for turn in reversed(range(groups // 2))]
-        mine, others = call(
+        parts = call(
             pair_kernel,
             "coarse_pair",
-            [((coarse, columns), FULL), ((coarse, columns), HALF)],
-            *parts,
-        )
+            [((coarse, columns), FULL)] + [((coarse, columns), HALF)] * (turns - 1),
+            mine,
+            swapped(others, "row", 0),
+        )
+        parts = [meeting(parts[turn], "row", turn, 2) for turn in reversed(range(turns))]
         level, *tiles = call(
-            coarse_kernel,
+            coarse_kernel(turns),
             "coarse",
             [((coarse, columns), HALF)] + four_tiles,
-            mine,
-            swapped(others, "row", 0),
+            *parts,
             basis,
             rim,
             flops=2 * coarse * margin * columns,

time: 123 us -> 123 us (level)
  starting transfers between devices: 58.4 us -> 61 us
  waiting for transfers between devices: 39.7 us -> 37.8 us
    ppermute x43, starting transfers between devices: 38.6 us -> 41.2 us  [swapped(): return lax.ppermute(shard, ('row', 'col'), pairs)]
    ppermute x43, waiting for transfers between devices: 23.8 us -> 21.9 us  [swapped(): return lax.ppermute(shard, ('row', 'col'), pairs)]
  transfers between devices with their start and end apart: 61 -> 61, of which waited for: 30 -> 29; matrix products, arithmetic and copies ran while one was open for 0% -> 0% of each run, Pallas kernels for 12% -> 12%
where the time goes in v16:
time: 123 us
  starting transfers between devices  61 us (50%)
  waiting for transfers between devices  37.8 us (31%)
  Pallas kernels  23.6 us (19%)
    ppermute x43, starting transfers between devices, swapped(): return lax.ppermute(shard, ('row', 'col'), pairs)  41.2 us
    pallas_call x35, Pallas kernels, call(): pl.pallas_call(body, out_shape=tuple(((pltpu.HBM if away else pltpu.VMEM)...  23.6 us
    ppermute x43, waiting for transfers between devices, swapped(): return lax.ppermute(shard, ('row', 'col'), pairs)  21.9 us
    ppermute x18, starting transfers between devices, meeting(): lax.ppermute(shard, axis, pairs)  19.7 us
    ppermute x18, waiting for transfers between devices, meeting(): lax.ppermute(shard, axis, pairs)  15.9 us
  transfers between devices with their start and end apart: 61, of which 29 were waited for; matrix products, arithmetic and copies ran while one was open for 0% of the time, Pallas kernels for 12%

profile of v16, /device:TPU:0, one launch (start us, length us, event | category | flops | bytes accessed | tf_op | source)
XLA Modules:
  0.0 123.0 jit_solution(968890452574458226)
XLA Ops:
  0.0 1.8 %select.1 = (f32[1024,256]{1,0:T(8,128)S(1)}, bf16[1024,256]{1,0:T(8,128)(2,1)S(1)}, bf16[512,1024]{1,0:T(8,128)(2,1)S(1)}, s32[4,128]{1,0:T(4,128)S(1)}, bf16[3...) custom-call(f32[1024,256]{1,0:T(8,128)} %bitcast.11, ...), custom_call_target="tpu_custom_call" | custom-call | flops 268435456 | bytes 1148944 | tf_op jit(solution)/shard_map/select/pallas_call | solution.py:28
  1.8 3.0 %collective-permute-start = (bf16[128,256]{1,0:T(8,128)(2,1)S(1)}, bf16[128,256]{1,0:T(8,128)(2,1)S(1)}, u32[]{:S(2)}, u32[]{:S(2)}) collective-permute-start(bf16[128,256]{1,0:T(8,128)(2,1)S(1)} %get-tuple-element.91), channel_id=1, source_target_pairs={{0,4},{1,5},{2,6},{3,7},{4,0},{5,1},{6,2},{7,3},{8,12},{9,13},{10,... | collective-permute-start | bytes 196616 | tf_op jit(solution)/shard_map/ppermute | solution.py:307
  4.8 1.6 %collective-permute-start.2 = (bf16[128,256]{1,0:T(8,128)(2,1)S(1)}, bf16[128,256]{1,0:T(8,128)(2,1)S(1)}, u32[]{:S(2)}, u32[]{:S(2)}) collective-permute-start(bf16[128,256]{1,0:T(8,128)(2,1)S(1)} %get-tuple-element.93), channel_id=1, source_target_pairs={{0,3},{1,2},{2,1},{3,0},{4,7},{5,6},{6,5},{7,4},{8,11},{9,10},{10,... | collective-permute-start | bytes 196616 | tf_op jit(solution)/shard_map/ppermute | solution.py:307
  6.4 2.6 %inverse_load.1.matrix.rest_0_ = bf16[1536,1536]{1,0:T(8,128)(2,1)S(1)} custom-call(bf16[1536,1536]{1,0:T(8,128)(2,1)} %bitcast.9, bf16[1024,256]{1,0:T(8,128)(2,1)S(1)} %get-tuple-element.90.own_like.owned), custom_call_target="tpu_custom_call" | custom-call | bytes 5242880 | tf_op jit(solution)/shard_map/inverse_load/pallas_call | solution.py:28
  9.3 1.1 collective-permute-start.6
  12.5 1.7 %collective-permute-done.5.refs_2_ = bf16[32,256]{1,0:T(8,128)(2,1)S(1)} collective-permute-done((bf16[32,256]{1,0:T(8,128)(2,1)S(1)}, bf16[32,256]{1,0:T(8,128)(2,1)S(1)}, u32[]{:S(2)}, u32[]{:S(2)}) %collective-permute-start.5) | collective-permute-done | bytes 16416 | tf_op jit(solution)/shard_map/ppermute | solution.py:175
  14.3 2.5 %collective-permute-start.7 = (bf16[128,256]{1,0:T(8,128)(2,1)S(1)}, bf16[128,256]{1,0:T(8,128)(2,1)S(1)}, u32[]{:S(2)}, u32[]{:S(2)}) collective-permute-start(bf16[128,256]{1,0:T(8,128)(2,1)S(1)} %get-tuple-element.98), channel_id=1, source_target_pairs={{0,4},{1,5},{2,6},{3,7},{4,0},{5,1},{6,2},{7,3},{8,12},{9,13},{10,... | collective-permute-start | bytes 196616 | tf_op jit(solution)/shard_map/ppermute | solution.py:307
  17.8 1.3 %collective-permute-done.7.theirs = bf16[128,256]{1,0:T(8,128)(2,1)S(1)} collective-permute-done((bf16[128,256]{1,0:T(8,128)(2,1)S(1)}, bf16[128,256]{1,0:T(8,128)(2,1)S(1)}, u32[]{:S(2)}, u32[]{:S(2)}) %collective-permute-start.7) | collective-permute-done | bytes 65568 | tf_op jit(solution)/shard_map/ppermute | solution.py:307
  19.1 3.3 %collective-permute-start.8 = (bf16[32,256]{1,0:T(8,128)(2,1)S(1)}, bf16[32,256]{1,0:T(8,128)(2,1)S(1)}, u32[]{:S(2)}, u32[]{:S(2)}) collective-permute-start(bf16[32,256]{1,0:T(8,128)(2,1)S(1)} %get-tuple-element.99), channel_id=1, source_target_pairs={{0,24},{4,28},{8,16},{12,20},{16,8},{20,12},{24,0},{28,4},{1,25},{... | collective-permute-start | bytes 49160 | tf_op jit(solution)/shard_map/ppermute | solution.py:175
  22.4 1.1 collective-permute-start.10
  24.8 2.2 %collective-permute-done.9.refs_1_ = bf16[32,256]{1,0:T(8,128)(2,1)S(1)} collective-permute-done((bf16[32,256]{1,0:T(8,128)(2,1)S(1)}, bf16[32,256]{1,0:T(8,128)(2,1)S(1)}, u32[]{:S(2)}, u32[]{:S(2)}) %collective-permute-start.9) | collective-permute-done | bytes 16416 | tf_op jit(solution)/shard_map/ppermute | solution.py:175
  28.2 1.6 %collective-permute-start.13 = (bf16[128,256]{1,0:T(8,128)(2,1)S(1)}, bf16[128,256]{1,0:T(8,128)(2,1)S(1)}, u32[]{:S(2)}, u32[]{:S(2)}) collective-permute-start(bf16[128,256]{1,0:T(8,128)(2,1)S(1)} %get-tuple-element.115), channel_id=1, source_target_pairs={{0,3},{1,2},{2,1},{3,0},{4,7},{5,6},{6,5},{7,4},{8,11},{9,10},{10,... | collective-permute-start | bytes 196616 | tf_op jit(solution)/shard_map/ppermute | solution.py:307
  29.8 2.6 %spread.1 = (bf16[1024,512]{1,0:T(8,128)(2,1)S(1)}, bf16[1536,1536]{1,0:T(8,128)(2,1)S(1)}) custom-call(bf16[1536,1536]{1,0:T(8,128)(2,1)} %bitcast.10, s32[4,128]{1,0:T(4,128)S(1)} %get-tuple-element.110.masked), custom_call_target="tpu_custom_call" | custom-call | bytes 4720640 | tf_op jit(solution)/shard_map/spread/pallas_call | solution.py:28
  33.8 2.9 %collective-permute-start.15 = (bf16[128,256]{1,0:T(8,128)(2,1)S(1)}, bf16[128,256]{1,0:T(8,128)(2,1)S(1)}, u32[]{:S(2)}, u32[]{:S(2)}) collective-permute-start(bf16[128,256]{1,0:T(8,128)(2,1)S(1)} %get-tuple-element.121), channel_id=1, source_target_pairs={{0,4},{1,5},{2,6},{3,7},{4,0},{5,1},{6,2},{7,3},{8,12},{9,13},{10,... | collective-permute-start | bytes 196616 | tf_op jit(solution)/shard_map/ppermute | solution.py:307
  38.5 1.4 %collective-permute-done.15.g0 = bf16[128,256]{1,0:T(8,128)(2,1)S(1)} collective-permute-done((bf16[128,256]{1,0:T(8,128)(2,1)S(1)}, bf16[128,256]{1,0:T(8,128)(2,1)S(1)}, u32[]{:S(2)}, u32[]{:S(2)}) %collective-permute-start.15) | collective-permute-done | bytes 65568 | tf_op jit(solution)/shard_map/ppermute | solution.py:307
  40.7 2.2 %collective-permute-start.19 = (bf16[128,256]{1,0:T(8,128)(2,1)S(1)}, bf16[128,256]{1,0:T(8,128)(2,1)S(1)}, u32[]{:S(2)}, u32[]{:S(2)}) collective-permute-start(bf16[128,256]{1,0:T(8,128)(2,1)S(1)} %get-tuple-element.125), channel_id=1, source_target_pairs={{0,4},{1,5},{2,6},{3,7},{4,0},{5,1},{6,2},{7,3},{8,12},{9,13},{10,... | collective-permute-start | bytes 196616 | tf_op jit(solution)/shard_map/ppermute | solution.py:307
  44.0 1.4 %collective-permute-done.19.r0 = bf16[128,256]{1,0:T(8,128)(2,1)S(1)} collective-permute-done((bf16[128,256]{1,0:T(8,128)(2,1)S(1)}, bf16[128,256]{1,0:T(8,128)(2,1)S(1)}, u32[]{:S(2)}, u32[]{:S(2)}) %collective-permute-start.19) | collective-permute-done | bytes 65568 | tf_op jit(solution)/shard_map/ppermute | solution.py:307
  47.5 3.5 %collective-permute-start.23 = (bf16[128,256]{1,0:T(8,128)(2,1)S(1)}, bf16[128,256]{1,0:T(8,128)(2,1)S(1)}, u32[]{:S(2)}, u32[]{:S(2)}) collective-permute-start(bf16[128,256]{1,0:T(8,128)(2,1)S(1)} %get-tuple-element.130), channel_id=1, source_target_pairs={{0,4},{1,5},{2,6},{3,7},{4,0},{5,1},{6,2},{7,3},{8,12},{9,13},{10,... | collective-permute-start | bytes 196616 | tf_op jit(solution)/shard_map/ppermute | solution.py:307
  51.0 1.2 collective-permute-start.25
  53.3 1.5 %collective-permute-done.25.g2 = bf16[128,256]{1,0:T(8,128)(2,1)S(1)} collective-permute-done((bf16[128,256]{1,0:T(8,128)(2,1)S(1)}, bf16[128,256]{1,0:T(8,128)(2,1)S(1)}, u32[]{:S(2)}, u32[]{:S(2)}) %collective-permute-start.25) | collective-permute-done | bytes 65568 | tf_op jit(solution)/shard_map/ppermute | solution.py:307
  55.0 1.2 collective-permute-start.29
  58.2 1.7 %collective-permute-done.28.refs_2_ = bf16[32,256]{1,0:T(8,128)(2,1)S(1)} collective-permute-done((bf16[32,256]{1,0:T(8,128)(2,1)S(1)}, bf16[32,256]{1,0:T(8,128)(2,1)S(1)}, u32[]{:S(2)}, u32[]{:S(2)}) %collective-permute-start.28) | collective-permute-done | bytes 16416 | tf_op jit(solution)/shard_map/ppermute | solution.py:175
  60.1 1.8 %collective-permute-start.30 = (bf16[128,256]{1,0:T(8,128)(2,1)S(1)}, bf16[128,256]{1,0:T(8,128)(2,1)S(1)}, u32[]{:S(2)}, u32[]{:S(2)}) collective-permute-start(bf16[128,256]{1,0:T(8,128)(2,1)S(1)} %get-tuple-element.136), channel_id=1, source_target_pairs={{0,4},{1,5},{2,6},{3,7},{4,0},{5,1},{6,2},{7,3},{8,12},{9,13},{10,... | collective-permute-start | bytes 196616 | tf_op jit(solution)/shard_map/ppermute | solution.py:307
  62.9 1.5 %collective-permute-done.30.theirs = bf16[128,256]{1,0:T(8,128)(2,1)S(1)} collective-permute-done((bf16[128,256]{1,0:T(8,128)(2,1)S(1)}, bf16[128,256]{1,0:T(8,128)(2,1)S(1)}, u32[]{:S(2)}, u32[]{:S(2)}) %collective-permute-start.30) | collective-permute-done | bytes 65568 | tf_op jit(solution)/shard_map/ppermute | solution.py:307
  64.5 3.0 %collective-permute-start.31 = (bf16[32,256]{1,0:T(8,128)(2,1)S(1)}, bf16[32,256]{1,0:T(8,128)(2,1)S(1)}, u32[]{:S(2)}, u32[]{:S(2)}) collective-permute-start(bf16[32,256]{1,0:T(8,128)(2,1)S(1)} %get-tuple-element.137), channel_id=1, source_target_pairs={{0,24},{4,28},{8,16},{12,20},{16,8},{20,12},{24,0},{28,4},{1,25},{... | collective-permute-start | bytes 49160 | tf_op jit(solution)/shard_map/ppermute | solution.py:175
  67.5 1.5 %collective-permute-start.33 = (bf16[32,256]{1,0:T(8,128)(2,1)S(1)}, bf16[32,256]{1,0:T(8,128)(2,1)S(1)}, u32[]{:S(2)}, u32[]{:S(2)}) collective-permute-start(bf16[32,256]{1,0:T(8,128)(2,1)S(1)} %get-tuple-element.139), channel_id=1, source_target_pairs={{0,8},{4,12},{8,0},{12,4},{16,24},{20,28},{24,16},{28,20},{1,9},{5... | collective-permute-start | bytes 49160 | tf_op jit(solution)/shard_map/ppermute | solution.py:175
  70.1 2.1 %collective-permute-done.32.refs_1_ = bf16[32,256]{1,0:T(8,128)(2,1)S(1)} collective-permute-done((bf16[32,256]{1,0:T(8,128)(2,1)S(1)}, bf16[32,256]{1,0:T(8,128)(2,1)S(1)}, u32[]{:S(2)}, u32[]{:S(2)}) %collective-permute-start.32) | collective-permute-done | bytes 16416 | tf_op jit(solution)/shard_map/ppermute | solution.py:175
  73.0 1.3 %collective-permute-start.36 = (bf16[128,256]{1,0:T(8,128)(2,1)S(1)}, bf16[128,256]{1,0:T(8,128)(2,1)S(1)}, u32[]{:S(2)}, u32[]{:S(2)}) collective-permute-start(bf16[128,256]{1,0:T(8,128)(2,1)S(1)} %get-tuple-element.145), channel_id=1, source_target_pairs={{0,3},{1,2},{2,1},{3,0},{4,7},{5,6},{6,5},{7,4},{8,11},{9,10},{10,... | collective-permute-start | bytes 196616 | tf_op jit(solution)/shard_map/ppermute | solution.py:307
  74.3 2.5 %collective-permute-done.34.refs_5_ = bf16[128,256]{1,0:T(8,128)(2,1)S(1)} collective-permute-done((bf16[128,256]{1,0:T(8,128)(2,1)S(1)}, bf16[128,256]{1,0:T(8,128)(2,1)S(1)}, u32[]{:S(2)}, u32[]{:S(2)}) %collective-permute-start.34) | collective-permute-done | bytes 65568 | tf_op jit(solution)/shard_map/ppermute | solution.py:307
  78.2 3.0 %collective-permute-start.38 = (bf16[128,256]{1,0:T(8,128)(2,1)S(1)}, bf16[128,256]{1,0:T(8,128)(2,1)S(1)}, u32[]{:S(2)}, u32[]{:S(2)}) collective-permute-start(bf16[128,256]{1,0:T(8,128)(2,1)S(1)} %get-tuple-element.149), channel_id=1, source_target_pairs={{0,4},{1,5},{2,6},{3,7},{4,0},{5,1},{6,2},{7,3},{8,12},{9,13},{10,... | collective-permute-start | bytes 196616 | tf_op jit(solution)/shard_map/ppermute | solution.py:307
  82.2 1.2 operator_own.3.partial
  83.4 1.5 %collective-permute-done.40.g2 = bf16[128,256]{1,0:T(8,128)(2,1)S(1)} collective-permute-done((bf16[128,256]{1,0:T(8,128)(2,1)S(1)}, bf16[128,256]{1,0:T(8,128)(2,1)S(1)}, u32[]{:S(2)}, u32[]{:S(2)}) %collective-permute-start.40) | collective-permute-done | bytes 65568 | tf_op jit(solution)/shard_map/ppermute | solution.py:307
  85.2 2.1 %collective-permute-start.42 = (bf16[128,256]{1,0:T(8,128)(2,1)S(1)}, bf16[128,256]{1,0:T(8,128)(2,1)S(1)}, u32[]{:S(2)}, u32[]{:S(2)}) collective-permute-start(bf16[128,256]{1,0:T(8,128)(2,1)S(1)} %get-tuple-element.153), channel_id=1, source_target_pairs={{0,4},{1,5},{2,6},{3,7},{4,0},{5,1},{6,2},{7,3},{8,12},{9,13},{10,... | collective-permute-start | bytes 196616 | tf_op jit(solution)/shard_map/ppermute | solution.py:307
  87.3 1.2 collective-permute-start.44
  88.5 1.3 %collective-permute-done.42.r0 = bf16[128,256]{1,0:T(8,128)(2,1)S(1)} collective-permute-done((bf16[128,256]{1,0:T(8,128)(2,1)S(1)}, bf16[128,256]{1,0:T(8,128)(2,1)S(1)}, u32[]{:S(2)}, u32[]{:S(2)}) %collective-permute-start.42) | collective-permute-done | bytes 65568 | tf_op jit(solution)/shard_map/ppermute | solution.py:307
  91.9 3.5 %collective-permute-start.46 = (bf16[128,256]{1,0:T(8,128)(2,1)S(1)}, bf16[128,256]{1,0:T(8,128)(2,1)S(1)}, u32[]{:S(2)}, u32[]{:S(2)}) collective-permute-start(bf16[128,256]{1,0:T(8,128)(2,1)S(1)} %get-tuple-element.158), channel_id=1, source_target_pairs={{0,4},{1,5},{2,6},{3,7},{4,0},{5,1},{6,2},{7,3},{8,12},{9,13},{10,... | collective-permute-start | bytes 196616 | tf_op jit(solution)/shard_map/ppermute | solution.py:307
  95.5 1.3 %collective-permute-start.48 = (bf16[128,256]{1,0:T(8,128)(2,1)S(1)}, bf16[128,256]{1,0:T(8,128)(2,1)S(1)}, u32[]{:S(2)}, u32[]{:S(2)}) collective-permute-start(bf16[128,256]{1,0:T(8,128)(2,1)S(1)} %get-tuple-element.160), channel_id=1, source_target_pairs={{0,3},{1,2},{2,1},{3,0},{4,7},{5,6},{6,5},{7,4},{8,11},{9,10},{10,... | collective-permute-start | bytes 196616 | tf_op jit(solution)/shard_map/ppermute | solution.py:307
  97.8 1.5 %collective-permute-done.48.g2 = bf16[128,256]{1,0:T(8,128)(2,1)S(1)} collective-permute-done((bf16[128,256]{1,0:T(8,128)(2,1)S(1)}, bf16[128,256]{1,0:T(8,128)(2,1)S(1)}, u32[]{:S(2)}, u32[]{:S(2)}) %collective-permute-start.48) | collective-permute-done | bytes 65568 | tf_op jit(solution)/shard_map/ppermute | solution.py:307
  99.5 1.3 %collective-permute-start.52 = (bf16[32,256]{1,0:T(8,128)(2,1)S(1)}, bf16[32,256]{1,0:T(8,128)(2,1)S(1)}, u32[]{:S(2)}, u32[]{:S(2)}) collective-permute-start(bf16[32,256]{1,0:T(8,128)(2,1)S(1)} %restrict.5.refs_0_), channel_id=1, source_target_pairs={{0,3},{1,2},{2,1},{3,0},{4,7},{5,6},{6,5},{7,4},{8,11},{9,10},{10,... | collective-permute-start | bytes 49160 | tf_op jit(solution)/shard_map/ppermute | solution.py:175
  102.6 1.8 %collective-permute-done.51.refs_2_ = bf16[32,256]{1,0:T(8,128)(2,1)S(1)} collective-permute-done((bf16[32,256]{1,0:T(8,128)(2,1)S(1)}, bf16[32,256]{1,0:T(8,128)(2,1)S(1)}, u32[]{:S(2)}, u32[]{:S(2)}) %collective-permute-start.51) | collective-permute-done | bytes 16416 | tf_op jit(solution)/shard_map/ppermute | solution.py:175
  104.7 1.4 %collective-permute-start.53 = (bf16[128,256]{1,0:T(8,128)(2,1)S(1)}, bf16[128,256]{1,0:T(8,128)(2,1)S(1)}, u32[]{:S(2)}, u32[]{:S(2)}) collective-permute-start(bf16[128,256]{1,0:T(8,128)(2,1)S(1)} %get-tuple-element.164), channel_id=1, source_target_pairs={{0,4},{1,5},{2,6},{3,7},{4,0},{5,1},{6,2},{7,3},{8,12},{9,13},{10,... | collective-permute-start | bytes 196616 | tf_op jit(solution)/shard_map/ppermute | solution.py:307
  107.1 1.9 %collective-permute-done.53.theirs = bf16[128,256]{1,0:T(8,128)(2,1)S(1)} collective-permute-done((bf16[128,256]{1,0:T(8,128)(2,1)S(1)}, bf16[128,256]{1,0:T(8,128)(2,1)S(1)}, u32[]{:S(2)}, u32[]{:S(2)}) %collective-permute-start.53) | collective-permute-done | bytes 65568 | tf_op jit(solution)/shard_map/ppermute | solution.py:307
  109.0 2.3 %collective-permute-start.54 = (bf16[32,256]{1,0:T(8,128)(2,1)S(1)}, bf16[32,256]{1,0:T(8,128)(2,1)S(1)}, u32[]{:S(2)}, u32[]{:S(2)}) collective-permute-start(bf16[32,256]{1,0:T(8,128)(2,1)S(1)} %get-tuple-element.165), channel_id=1, source_target_pairs={{0,24},{4,28},{8,16},{12,20},{16,8},{20,12},{24,0},{28,4},{1,25},{... | collective-permute-start | bytes 49160 | tf_op jit(solution)/shard_map/ppermute | solution.py:175
  111.9 1.6 %collective-permute-start.56 = (bf16[32,256]{1,0:T(8,128)(2,1)S(1)}, bf16[32,256]{1,0:T(8,128)(2,1)S(1)}, u32[]{:S(2)}, u32[]{:S(2)}) collective-permute-start(bf16[32,256]{1,0:T(8,128)(2,1)S(1)} %get-tuple-element.167), channel_id=1, source_target_pairs={{0,8},{4,12},{8,0},{12,4},{16,24},{20,28},{24,16},{28,20},{1,9},{5... | collective-permute-start | bytes 49160 | tf_op jit(solution)/shard_map/ppermute | solution.py:175
  114.7 1.3 %collective-permute-done.55.refs_1_ = bf16[32,256]{1,0:T(8,128)(2,1)S(1)} collective-permute-done((bf16[32,256]{1,0:T(8,128)(2,1)S(1)}, bf16[32,256]{1,0:T(8,128)(2,1)S(1)}, u32[]{:S(2)}, u32[]{:S(2)}) %collective-permute-start.55) | collective-permute-done | bytes 16416 | tf_op jit(solution)/shard_map/ppermute | solution.py:175
  116.3 1.6 %collective-permute-start.57 = (bf16[128,256]{1,0:T(8,128)(2,1)S(1)}, bf16[128,256]{1,0:T(8,128)(2,1)S(1)}, u32[]{:S(2)}, u32[]{:S(2)}) collective-permute-start(bf16[128,256]{1,0:T(8,128)(2,1)S(1)} %get-tuple-element.171), channel_id=1, source_target_pairs={{0,4},{1,5},{2,6},{3,7},{4,0},{5,1},{6,2},{7,3},{8,12},{9,13},{10,... | collective-permute-start | bytes 196616 | tf_op jit(solution)/shard_map/ppermute | solution.py:307
  118.9 1.7 %collective-permute-done.57.refs_5_ = bf16[128,256]{1,0:T(8,128)(2,1)S(1)} collective-permute-done((bf16[128,256]{1,0:T(8,128)(2,1)S(1)}, bf16[128,256]{1,0:T(8,128)(2,1)S(1)}, u32[]{:S(2)}, u32[]{:S(2)}) %collective-permute-start.57) | collective-permute-done | bytes 65568 | tf_op jit(solution)/shard_map/ppermute | solution.py:307
  121.6 1.2 %last_update.1 = f32[1024,256]{1,0:T(8,128)} custom-call(f32[1024,256]{1,0:T(8,128)S(1)} %base.5, bf16[1024,512]{1,0:T(8,128)(2,1)S(1)} %get-tuple-element.111.refs_3_.spread.refs_4_, bf16[128,256]{1,0:T(8,128)(2,1)S(1)} %collective-permute-done.59.r2, bf16[128,256]{1,0:T(8,128)(2,1)S(1)} %collective-permute-done.60.r3), custom_call_target="tpu_custom_call" | custom-call | flops 268435456 | bytes 2228224 | tf_op jit(solution)/shard_map/last_update/pallas_call | solution.py:28
  (111 shorter events, 32.9 us)
Async XLA Ops:
  1.8 7.2 %collective-permute-start = (bf16[128,256]{1,0:T(8,128)(2,1)S(1)}, bf16[128,256]{1,0:T(8,128)(2,1)S(1)}, u32[]{:S(2)}, u32[]{:S(2)}) collective-permute-start(bf16[128,256]{1,0:T(8,128)(2,1)S(1)} %get-tuple-element.91), channel_id=1, source_target_pairs={{0,4},{1,5},{2,6},{3,7},{4,0},{5,1},{6,2},{7,3},{8,12},{9,13},{10,... | collective-permute-start | bytes 196616 | tf_op jit(solution)/shard_map/ppermute | solution.py:307
  4.8 4.2 %collective-permute-start.1 = (bf16[128,256]{1,0:T(8,128)(2,1)S(1)}, bf16[128,256]{1,0:T(8,128)(2,1)S(1)}, u32[]{:S(2)}, u32[]{:S(2)}) collective-permute-start(bf16[128,256]{1,0:T(8,128)(2,1)S(1)} %get-tuple-element.92), channel_id=1, source_target_pairs={{0,1},{1,0},{2,3},{3,2},{4,8},{5,9},{6,10},{7,11},{8,4},{9,5},{10,... | collective-permute-start | bytes 196616 | tf_op jit(solution)/shard_map/ppermute | solution.py:307
  4.8 4.2 %collective-permute-start.2 = (bf16[128,256]{1,0:T(8,128)(2,1)S(1)}, bf16[128,256]{1,0:T(8,128)(2,1)S(1)}, u32[]{:S(2)}, u32[]{:S(2)}) collective-permute-start(bf16[128,256]{1,0:T(8,128)(2,1)S(1)} %get-tuple-element.93), channel_id=1, source_target_pairs={{0,3},{1,2},{2,1},{3,0},{4,7},{5,6},{6,5},{7,4},{8,11},{9,10},{10,... | collective-permute-start | bytes 196616 | tf_op jit(solution)/shard_map/ppermute | solution.py:307
  9.3 3.2 %collective-permute-start.6 = (bf16[32,256]{1,0:T(8,128)(2,1)S(1)}, bf16[32,256]{1,0:T(8,128)(2,1)S(1)}, u32[]{:S(2)}, u32[]{:S(2)}) collective-permute-start(bf16[32,256]{1,0:T(8,128)(2,1)S(1)} %restrict.3.refs_0_), channel_id=1, source_target_pairs={{0,3},{1,2},{2,1},{3,0},{4,7},{5,6},{6,5},{7,4},{8,11},{9,10},{10,... | collective-permute-start | bytes 49160 | tf_op jit(solution)/shard_map/ppermute | solution.py:175
  10.4 3.7 %collective-permute-start.5 = (bf16[32,256]{1,0:T(8,128)(2,1)S(1)}, bf16[32,256]{1,0:T(8,128)(2,1)S(1)}, u32[]{:S(2)}, u32[]{:S(2)}) collective-permute-start(bf16[32,256]{1,0:T(8,128)(2,1)S(1)} %restrict.3.refs_0_), channel_id=1, source_target_pairs={{0,2},{1,3},{2,0},{3,1},{4,6},{5,7},{6,4},{7,5},{8,10},{9,11},{10,... | collective-permute-start | bytes 49160 | tf_op jit(solution)/shard_map/ppermute | solution.py:175
  14.3 4.7 %collective-permute-start.7 = (bf16[128,256]{1,0:T(8,128)(2,1)S(1)}, bf16[128,256]{1,0:T(8,128)(2,1)S(1)}, u32[]{:S(2)}, u32[]{:S(2)}) collective-permute-start(bf16[128,256]{1,0:T(8,128)(2,1)S(1)} %get-tuple-element.98), channel_id=1, source_target_pairs={{0,4},{1,5},{2,6},{3,7},{4,0},{5,1},{6,2},{7,3},{8,12},{9,13},{10,... | collective-permute-start | bytes 196616 | tf_op jit(solution)/shard_map/ppermute | solution.py:307
  19.1 5.7 %collective-permute-start.8 = (bf16[32,256]{1,0:T(8,128)(2,1)S(1)}, bf16[32,256]{1,0:T(8,128)(2,1)S(1)}, u32[]{:S(2)}, u32[]{:S(2)}) collective-permute-start(bf16[32,256]{1,0:T(8,128)(2,1)S(1)} %get-tuple-element.99), channel_id=1, source_target_pairs={{0,24},{4,28},{8,16},{12,20},{16,8},{20,12},{24,0},{28,4},{1,25},{... | collective-permute-start | bytes 49160 | tf_op jit(solution)/shard_map/ppermute | solution.py:175
  22.4 4.6 %collective-permute-start.9 = (bf16[32,256]{1,0:T(8,128)(2,1)S(1)}, bf16[32,256]{1,0:T(8,128)(2,1)S(1)}, u32[]{:S(2)}, u32[]{:S(2)}) collective-permute-start(bf16[32,256]{1,0:T(8,128)(2,1)S(1)} %get-tuple-element.100), channel_id=1, source_target_pairs={{0,16},{4,20},{8,24},{12,28},{16,0},{20,4},{24,8},{28,12},{1,17},{... | collective-permute-start | bytes 49160 | tf_op jit(solution)/shard_map/ppermute | solution.py:175
  22.4 4.6 %collective-permute-start.10 = (bf16[32,256]{1,0:T(8,128)(2,1)S(1)}, bf16[32,256]{1,0:T(8,128)(2,1)S(1)}, u32[]{:S(2)}, u32[]{:S(2)}) collective-permute-start(bf16[32,256]{1,0:T(8,128)(2,1)S(1)} %get-tuple-element.101), channel_id=1, source_target_pairs={{0,8},{4,12},{8,0},{12,4},{16,24},{20,28},{24,16},{28,20},{1,9},{5... | collective-permute-start | bytes 49160 | tf_op jit(solution)/shard_map/ppermute | solution.py:175
  27.3 5.1 %collective-permute-start.11 = (bf16[128,256]{1,0:T(8,128)(2,1)S(1)}, bf16[128,256]{1,0:T(8,128)(2,1)S(1)}, u32[]{:S(2)}, u32[]{:S(2)}) collective-permute-start(bf16[128,256]{1,0:T(8,128)(2,1)S(1)} %get-tuple-element.112), channel_id=1, source_target_pairs={{0,4},{1,5},{2,6},{3,7},{4,0},{5,1},{6,2},{7,3},{8,12},{9,13},{10,... | collective-permute-start | bytes 196616 | tf_op jit(solution)/shard_map/ppermute | solution.py:307
  28.2 4.1 %collective-permute-start.12 = (bf16[128,256]{1,0:T(8,128)(2,1)S(1)}, bf16[128,256]{1,0:T(8,128)(2,1)S(1)}, u32[]{:S(2)}, u32[]{:S(2)}) collective-permute-start(bf16[128,256]{1,0:T(8,128)(2,1)S(1)} %get-tuple-element.113), channel_id=1, source_target_pairs={{0,1},{1,0},{2,3},{3,2},{4,8},{5,9},{6,10},{7,11},{8,4},{9,5},{10,... | collective-permute-start | bytes 196616 | tf_op jit(solution)/shard_map/ppermute | solution.py:307
  28.2 4.6 %collective-permute-start.13 = (bf16[128,256]{1,0:T(8,128)(2,1)S(1)}, bf16[128,256]{1,0:T(8,128)(2,1)S(1)}, u32[]{:S(2)}, u32[]{:S(2)}) collective-permute-start(bf16[128,256]{1,0:T(8,128)(2,1)S(1)} %get-tuple-element.115), channel_id=1, source_target_pairs={{0,3},{1,2},{2,1},{3,0},{4,7},{5,6},{6,5},{7,4},{8,11},{9,10},{10,... | collective-permute-start | bytes 196616 | tf_op jit(solution)/shard_map/ppermute | solution.py:307
  29.8 3.1 %collective-permute-start.14 = (bf16[128,256]{1,0:T(8,128)(2,1)S(1)}, bf16[128,256]{1,0:T(8,128)(2,1)S(1)}, u32[]{:S(2)}, u32[]{:S(2)}) collective-permute-start(bf16[128,256]{1,0:T(8,128)(2,1)S(1)} %get-tuple-element.116), channel_id=1, source_target_pairs={{0,1},{1,0},{2,3},{3,2},{4,5},{5,4},{6,7},{7,6},{8,9},{9,8},{10,11... | collective-permute-start | bytes 196616 | tf_op jit(solution)/shard_map/ppermute | solution.py:307
  33.8 6.1 %collective-permute-start.15 = (bf16[128,256]{1,0:T(8,128)(2,1)S(1)}, bf16[128,256]{1,0:T(8,128)(2,1)S(1)}, u32[]{:S(2)}, u32[]{:S(2)}) collective-permute-start(bf16[128,256]{1,0:T(8,128)(2,1)S(1)} %get-tuple-element.121), channel_id=1, source_target_pairs={{0,4},{1,5},{2,6},{3,7},{4,0},{5,1},{6,2},{7,3},{8,12},{9,13},{10,... | collective-permute-start | bytes 196616 | tf_op jit(solution)/shard_map/ppermute | solution.py:307
  36.6 3.2 %collective-permute-start.16 = (bf16[128,256]{1,0:T(8,128)(2,1)S(1)}, bf16[128,256]{1,0:T(8,128)(2,1)S(1)}, u32[]{:S(2)}, u32[]{:S(2)}) collective-permute-start(bf16[128,256]{1,0:T(8,128)(2,1)S(1)} %get-tuple-element.122), channel_id=1, source_target_pairs={{0,1},{1,0},{2,3},{3,2},{4,8},{5,9},{6,10},{7,11},{8,4},{9,5},{10,... | collective-permute-start | bytes 196616 | tf_op jit(solution)/shard_map/ppermute | solution.py:307
  36.6 3.7 %collective-permute-start.17 = (bf16[128,256]{1,0:T(8,128)(2,1)S(1)}, bf16[128,256]{1,0:T(8,128)(2,1)S(1)}, u32[]{:S(2)}, u32[]{:S(2)}) collective-permute-start(bf16[128,256]{1,0:T(8,128)(2,1)S(1)} %get-tuple-element.123), channel_id=1, source_target_pairs={{0,3},{1,2},{2,1},{3,0},{4,7},{5,6},{6,5},{7,4},{8,11},{9,10},{10,... | collective-permute-start | bytes 196616 | tf_op jit(solution)/shard_map/ppermute | solution.py:307
  37.5 2.9 %collective-permute-start.18 = (bf16[128,256]{1,0:T(8,128)(2,1)S(1)}, bf16[128,256]{1,0:T(8,128)(2,1)S(1)}, u32[]{:S(2)}, u32[]{:S(2)}) collective-permute-start(bf16[128,256]{1,0:T(8,128)(2,1)S(1)} %get-tuple-element.124), channel_id=1, source_target_pairs={{0,1},{1,0},{2,3},{3,2},{4,5},{5,4},{6,7},{7,6},{8,9},{9,8},{10,11... | collective-permute-start | bytes 196616 | tf_op jit(solution)/shard_map/ppermute | solution.py:307
  40.7 4.8 %collective-permute-start.19 = (bf16[128,256]{1,0:T(8,128)(2,1)S(1)}, bf16[128,256]{1,0:T(8,128)(2,1)S(1)}, u32[]{:S(2)}, u32[]{:S(2)}) collective-permute-start(bf16[128,256]{1,0:T(8,128)(2,1)S(1)} %get-tuple-element.125), channel_id=1, source_target_pairs={{0,4},{1,5},{2,6},{3,7},{4,0},{5,1},{6,2},{7,3},{8,12},{9,13},{10,... | collective-permute-start | bytes 196616 | tf_op jit(solution)/shard_map/ppermute | solution.py:307
  42.9 3.7 %collective-permute-start.21 = (bf16[128,256]{1,0:T(8,128)(2,1)S(1)}, bf16[128,256]{1,0:T(8,128)(2,1)S(1)}, u32[]{:S(2)}, u32[]{:S(2)}) collective-permute-start(bf16[128,256]{1,0:T(8,128)(2,1)S(1)} %get-tuple-element.127), channel_id=1, source_target_pairs={{0,3},{1,2},{2,1},{3,0},{4,7},{5,6},{6,5},{7,4},{8,11},{9,10},{10,... | collective-permute-start | bytes 196616 | tf_op jit(solution)/shard_map/ppermute | solution.py:307
  47.5 5.8 %collective-permute-start.23 = (bf16[128,256]{1,0:T(8,128)(2,1)S(1)}, bf16[128,256]{1,0:T(8,128)(2,1)S(1)}, u32[]{:S(2)}, u32[]{:S(2)}) collective-permute-start(bf16[128,256]{1,0:T(8,128)(2,1)S(1)} %get-tuple-element.130), channel_id=1, source_target_pairs={{0,4},{1,5},{2,6},{3,7},{4,0},{5,1},{6,2},{7,3},{8,12},{9,13},{10,... | collective-permute-start | bytes 196616 | tf_op jit(solution)/shard_map/ppermute | solution.py:307
  51.0 3.7 %collective-permute-start.25 = (bf16[128,256]{1,0:T(8,128)(2,1)S(1)}, bf16[128,256]{1,0:T(8,128)(2,1)S(1)}, u32[]{:S(2)}, u32[]{:S(2)}) collective-permute-start(bf16[128,256]{1,0:T(8,128)(2,1)S(1)} %get-tuple-element.132), channel_id=1, source_target_pairs={{0,3},{1,2},{2,1},{3,0},{4,7},{5,6},{6,5},{7,4},{8,11},{9,10},{10,... | collective-permute-start | bytes 196616 | tf_op jit(solution)/shard_map/ppermute | solution.py:307
  55.0 3.2 %collective-permute-start.29 = (bf16[32,256]{1,0:T(8,128)(2,1)S(1)}, bf16[32,256]{1,0:T(8,128)(2,1)S(1)}, u32[]{:S(2)}, u32[]{:S(2)}) collective-permute-start(bf16[32,256]{1,0:T(8,128)(2,1)S(1)} %restrict.4.refs_0_), channel_id=1, source_target_pairs={{0,3},{1,2},{2,1},{3,0},{4,7},{5,6},{6,5},{7,4},{8,11},{9,10},{10,... | collective-permute-start | bytes 49160 | tf_op jit(solution)/shard_map/ppermute | solution.py:175
  56.2 3.7 %collective-permute-start.28 = (bf16[32,256]{1,0:T(8,128)(2,1)S(1)}, bf16[32,256]{1,0:T(8,128)(2,1)S(1)}, u32[]{:S(2)}, u32[]{:S(2)}) collective-permute-start(bf16[32,256]{1,0:T(8,128)(2,1)S(1)} %restrict.4.refs_0_), channel_id=1, source_target_pairs={{0,2},{1,3},{2,0},{3,1},{4,6},{5,7},{6,4},{7,5},{8,10},{9,11},{10,... | collective-permute-start | bytes 49160 | tf_op jit(solution)/shard_map/ppermute | solution.py:175
  57.1 2.8 %collective-permute-start.27 = (bf16[32,256]{1,0:T(8,128)(2,1)S(1)}, bf16[32,256]{1,0:T(8,128)(2,1)S(1)}, u32[]{:S(2)}, u32[]{:S(2)}) collective-permute-start(bf16[32,256]{1,0:T(8,128)(2,1)S(1)} %restrict.4.refs_0_), channel_id=1, source_target_pairs={{0,1},{1,0},{2,3},{3,2},{4,5},{5,4},{6,7},{7,6},{8,9},{9,8},{10,11... | collective-permute-start | bytes 49160 | tf_op jit(solution)/shard_map/ppermute | solution.py:175
  60.1 4.3 %collective-permute-start.30 = (bf16[128,256]{1,0:T(8,128)(2,1)S(1)}, bf16[128,256]{1,0:T(8,128)(2,1)S(1)}, u32[]{:S(2)}, u32[]{:S(2)}) collective-permute-start(bf16[128,256]{1,0:T(8,128)(2,1)S(1)} %get-tuple-element.136), channel_id=1, source_target_pairs={{0,4},{1,5},{2,6},{3,7},{4,0},{5,1},{6,2},{7,3},{8,12},{9,13},{10,... | collective-permute-start | bytes 196616 | tf_op jit(solution)/shard_map/ppermute | solution.py:307
  64.5 5.7 %collective-permute-start.31 = (bf16[32,256]{1,0:T(8,128)(2,1)S(1)}, bf16[32,256]{1,0:T(8,128)(2,1)S(1)}, u32[]{:S(2)}, u32[]{:S(2)}) collective-permute-start(bf16[32,256]{1,0:T(8,128)(2,1)S(1)} %get-tuple-element.137), channel_id=1, source_target_pairs={{0,24},{4,28},{8,16},{12,20},{16,8},{20,12},{24,0},{28,4},{1,25},{... | collective-permute-start | bytes 49160 | tf_op jit(solution)/shard_map/ppermute | solution.py:175
  67.5 4.8 %collective-permute-start.32 = (bf16[32,256]{1,0:T(8,128)(2,1)S(1)}, bf16[32,256]{1,0:T(8,128)(2,1)S(1)}, u32[]{:S(2)}, u32[]{:S(2)}) collective-permute-start(bf16[32,256]{1,0:T(8,128)(2,1)S(1)} %get-tuple-element.138), channel_id=1, source_target_pairs={{0,16},{4,20},{8,24},{12,28},{16,0},{20,4},{24,8},{28,12},{1,17},{... | collective-permute-start | bytes 49160 | tf_op jit(solution)/shard_map/ppermute | solution.py:175
  67.5 4.7 %collective-permute-start.33 = (bf16[32,256]{1,0:T(8,128)(2,1)S(1)}, bf16[32,256]{1,0:T(8,128)(2,1)S(1)}, u32[]{:S(2)}, u32[]{:S(2)}) collective-permute-start(bf16[32,256]{1,0:T(8,128)(2,1)S(1)} %get-tuple-element.139), channel_id=1, source_target_pairs={{0,8},{4,12},{8,0},{12,4},{16,24},{20,28},{24,16},{28,20},{1,9},{5... | collective-permute-start | bytes 49160 | tf_op jit(solution)/shard_map/ppermute | solution.py:175
  72.5 4.3 %collective-permute-start.34 = (bf16[128,256]{1,0:T(8,128)(2,1)S(1)}, bf16[128,256]{1,0:T(8,128)(2,1)S(1)}, u32[]{:S(2)}, u32[]{:S(2)}) collective-permute-start(bf16[128,256]{1,0:T(8,128)(2,1)S(1)} %get-tuple-element.143), channel_id=1, source_target_pairs={{0,4},{1,5},{2,6},{3,7},{4,0},{5,1},{6,2},{7,3},{8,12},{9,13},{10,... | collective-permute-start | bytes 196616 | tf_op jit(solution)/shard_map/ppermute | solution.py:307
  73.0 3.8 %collective-permute-start.35 = (bf16[128,256]{1,0:T(8,128)(2,1)S(1)}, bf16[128,256]{1,0:T(8,128)(2,1)S(1)}, u32[]{:S(2)}, u32[]{:S(2)}) collective-permute-start(bf16[128,256]{1,0:T(8,128)(2,1)S(1)} %get-tuple-element.144), channel_id=1, source_target_pairs={{0,1},{1,0},{2,3},{3,2},{4,8},{5,9},{6,10},{7,11},{8,4},{9,5},{10,... | collective-permute-start | bytes 196616 | tf_op jit(solution)/shard_map/ppermute | solution.py:307
  73.0 4.2 %collective-permute-start.36 = (bf16[128,256]{1,0:T(8,128)(2,1)S(1)}, bf16[128,256]{1,0:T(8,128)(2,1)S(1)}, u32[]{:S(2)}, u32[]{:S(2)}) collective-permute-start(bf16[128,256]{1,0:T(8,128)(2,1)S(1)} %get-tuple-element.145), channel_id=1, source_target_pairs={{0,3},{1,2},{2,1},{3,0},{4,7},{5,6},{6,5},{7,4},{8,11},{9,10},{10,... | collective-permute-start | bytes 196616 | tf_op jit(solution)/shard_map/ppermute | solution.py:307
  74.3 3.0 %collective-permute-start.37 = (bf16[128,256]{1,0:T(8,128)(2,1)S(1)}, bf16[128,256]{1,0:T(8,128)(2,1)S(1)}, u32[]{:S(2)}, u32[]{:S(2)}) collective-permute-start(bf16[128,256]{1,0:T(8,128)(2,1)S(1)} %get-tuple-element.146), channel_id=1, source_target_pairs={{0,1},{1,0},{2,3},{3,2},{4,5},{5,4},{6,7},{7,6},{8,9},{9,8},{10,11... | collective-permute-start | bytes 196616 | tf_op jit(solution)/shard_map/ppermute | solution.py:307
  78.2 5.2 %collective-permute-start.38 = (bf16[128,256]{1,0:T(8,128)(2,1)S(1)}, bf16[128,256]{1,0:T(8,128)(2,1)S(1)}, u32[]{:S(2)}, u32[]{:S(2)}) collective-permute-start(bf16[128,256]{1,0:T(8,128)(2,1)S(1)} %get-tuple-element.149), channel_id=1, source_target_pairs={{0,4},{1,5},{2,6},{3,7},{4,0},{5,1},{6,2},{7,3},{8,12},{9,13},{10,... | collective-permute-start | bytes 196616 | tf_op jit(solution)/shard_map/ppermute | solution.py:307
  81.2 3.7 %collective-permute-start.40 = (bf16[128,256]{1,0:T(8,128)(2,1)S(1)}, bf16[128,256]{1,0:T(8,128)(2,1)S(1)}, u32[]{:S(2)}, u32[]{:S(2)}) collective-permute-start(bf16[128,256]{1,0:T(8,128)(2,1)S(1)} %get-tuple-element.151), channel_id=1, source_target_pairs={{0,3},{1,2},{2,1},{3,0},{4,7},{5,6},{6,5},{7,4},{8,11},{9,10},{10,... | collective-permute-start | bytes 196616 | tf_op jit(solution)/shard_map/ppermute | solution.py:307
  85.2 4.6 %collective-permute-start.42 = (bf16[128,256]{1,0:T(8,128)(2,1)S(1)}, bf16[128,256]{1,0:T(8,128)(2,1)S(1)}, u32[]{:S(2)}, u32[]{:S(2)}) collective-permute-start(bf16[128,256]{1,0:T(8,128)(2,1)S(1)} %get-tuple-element.153), channel_id=1, source_target_pairs={{0,4},{1,5},{2,6},{3,7},{4,0},{5,1},{6,2},{7,3},{8,12},{9,13},{10,... | collective-permute-start | bytes 196616 | tf_op jit(solution)/shard_map/ppermute | solution.py:307
  87.3 3.7 %collective-permute-start.44 = (bf16[128,256]{1,0:T(8,128)(2,1)S(1)}, bf16[128,256]{1,0:T(8,128)(2,1)S(1)}, u32[]{:S(2)}, u32[]{:S(2)}) collective-permute-start(bf16[128,256]{1,0:T(8,128)(2,1)S(1)} %get-tuple-element.155), channel_id=1, source_target_pairs={{0,3},{1,2},{2,1},{3,0},{4,7},{5,6},{6,5},{7,4},{8,11},{9,10},{10,... | collective-permute-start | bytes 196616 | tf_op jit(solution)/shard_map/ppermute | solution.py:307
  91.9 5.8 %collective-permute-start.46 = (bf16[128,256]{1,0:T(8,128)(2,1)S(1)}, bf16[128,256]{1,0:T(8,128)(2,1)S(1)}, u32[]{:S(2)}, u32[]{:S(2)}) collective-permute-start(bf16[128,256]{1,0:T(8,128)(2,1)S(1)} %get-tuple-element.158), channel_id=1, source_target_pairs={{0,4},{1,5},{2,6},{3,7},{4,0},{5,1},{6,2},{7,3},{8,12},{9,13},{10,... | collective-permute-start | bytes 196616 | tf_op jit(solution)/shard_map/ppermute | solution.py:307
  95.5 3.7 %collective-permute-start.48 = (bf16[128,256]{1,0:T(8,128)(2,1)S(1)}, bf16[128,256]{1,0:T(8,128)(2,1)S(1)}, u32[]{:S(2)}, u32[]{:S(2)}) collective-permute-start(bf16[128,256]{1,0:T(8,128)(2,1)S(1)} %get-tuple-element.160), channel_id=1, source_target_pairs={{0,3},{1,2},{2,1},{3,0},{4,7},{5,6},{6,5},{7,4},{8,11},{9,10},{10,... | collective-permute-start | bytes 196616 | tf_op jit(solution)/shard_map/ppermute | solution.py:307
  99.5 3.2 %collective-permute-start.52 = (bf16[32,256]{1,0:T(8,128)(2,1)S(1)}, bf16[32,256]{1,0:T(8,128)(2,1)S(1)}, u32[]{:S(2)}, u32[]{:S(2)}) collective-permute-start(bf16[32,256]{1,0:T(8,128)(2,1)S(1)} %restrict.5.refs_0_), channel_id=1, source_target_pairs={{0,3},{1,2},{2,1},{3,0},{4,7},{5,6},{6,5},{7,4},{8,11},{9,10},{10,... | collective-permute-start | bytes 49160 | tf_op jit(solution)/shard_map/ppermute | solution.py:175
  100.7 3.7 %collective-permute-start.51 = (bf16[32,256]{1,0:T(8,128)(2,1)S(1)}, bf16[32,256]{1,0:T(8,128)(2,1)S(1)}, u32[]{:S(2)}, u32[]{:S(2)}) collective-permute-start(bf16[32,256]{1,0:T(8,128)(2,1)S(1)} %restrict.5.refs_0_), channel_id=1, source_target_pairs={{0,2},{1,3},{2,0},{3,1},{4,6},{5,7},{6,4},{7,5},{8,10},{9,11},{10,... | collective-permute-start | bytes 49160 | tf_op jit(solution)/shard_map/ppermute | solution.py:175
  101.6 2.9 %collective-permute-start.50 = (bf16[32,256]{1,0:T(8,128)(2,1)S(1)}, bf16[32,256]{1,0:T(8,128)(2,1)S(1)}, u32[]{:S(2)}, u32[]{:S(2)}) collective-permute-start(bf16[32,256]{1,0:T(8,128)(2,1)S(1)} %restrict.5.refs_0_), channel_id=1, source_target_pairs={{0,1},{1,0},{2,3},{3,2},{4,5},{5,4},{6,7},{7,6},{8,9},{9,8},{10,11... | collective-permute-start | bytes 49160 | tf_op jit(solution)/shard_map/ppermute | solution.py:175
  104.7 4.3 %collective-permute-start.53 = (bf16[128,256]{1,0:T(8,128)(2,1)S(1)}, bf16[128,256]{1,0:T(8,128)(2,1)S(1)}, u32[]{:S(2)}, u32[]{:S(2)}) collective-permute-start(bf16[128,256]{1,0:T(8,128)(2,1)S(1)} %get-tuple-element.164), channel_id=1, source_target_pairs={{0,4},{1,5},{2,6},{3,7},{4,0},{5,1},{6,2},{7,3},{8,12},{9,13},{10,... | collective-permute-start | bytes 196616 | tf_op jit(solution)/shard_map/ppermute | solution.py:307
  109.0 5.7 %collective-permute-start.54 = (bf16[32,256]{1,0:T(8,128)(2,1)S(1)}, bf16[32,256]{1,0:T(8,128)(2,1)S(1)}, u32[]{:S(2)}, u32[]{:S(2)}) collective-permute-start(bf16[32,256]{1,0:T(8,128)(2,1)S(1)} %get-tuple-element.165), channel_id=1, source_target_pairs={{0,24},{4,28},{8,16},{12,20},{16,8},{20,12},{24,0},{28,4},{1,25},{... | collective-permute-start | bytes 49160 | tf_op jit(solution)/shard_map/ppermute | solution.py:175
  111.4 4.6 %collective-permute-start.55 = (bf16[32,256]{1,0:T(8,128)(2,1)S(1)}, bf16[32,256]{1,0:T(8,128)(2,1)S(1)}, u32[]{:S(2)}, u32[]{:S(2)}) collective-permute-start(bf16[32,256]{1,0:T(8,128)(2,1)S(1)} %get-tuple-element.166), channel_id=1, source_target_pairs={{0,16},{4,20},{8,24},{12,28},{16,0},{20,4},{24,8},{28,12},{1,17},{... | collective-permute-start | bytes 49160 | tf_op jit(solution)/shard_map/ppermute | solution.py:175
  111.9 4.1 %collective-permute-start.56 = (bf16[32,256]{1,0:T(8,128)(2,1)S(1)}, bf16[32,256]{1,0:T(8,128)(2,1)S(1)}, u32[]{:S(2)}, u32[]{:S(2)}) collective-permute-start(bf16[32,256]{1,0:T(8,128)(2,1)S(1)} %get-tuple-element.167), channel_id=1, source_target_pairs={{0,8},{4,12},{8,0},{12,4},{16,24},{20,28},{24,16},{28,20},{1,9},{5... | collective-permute-start | bytes 49160 | tf_op jit(solution)/shard_map/ppermute | solution.py:175
  116.3 4.3 %collective-permute-start.57 = (bf16[128,256]{1,0:T(8,128)(2,1)S(1)}, bf16[128,256]{1,0:T(8,128)(2,1)S(1)}, u32[]{:S(2)}, u32[]{:S(2)}) collective-permute-start(bf16[128,256]{1,0:T(8,128)(2,1)S(1)} %get-tuple-element.171), channel_id=1, source_target_pairs={{0,4},{1,5},{2,6},{3,7},{4,0},{5,1},{6,2},{7,3},{8,12},{9,13},{10,... | collective-permute-start | bytes 196616 | tf_op jit(solution)/shard_map/ppermute | solution.py:307
  117.8 2.8 %collective-permute-start.58 = (bf16[128,256]{1,0:T(8,128)(2,1)S(1)}, bf16[128,256]{1,0:T(8,128)(2,1)S(1)}, u32[]{:S(2)}, u32[]{:S(2)}) collective-permute-start(bf16[128,256]{1,0:T(8,128)(2,1)S(1)} %get-tuple-element.172), channel_id=1, source_target_pairs={{0,1},{1,0},{2,3},{3,2},{4,8},{5,9},{6,10},{7,11},{8,4},{9,5},{10,... | collective-permute-start | bytes 196616 | tf_op jit(solution)/shard_map/ppermute | solution.py:307
  117.8 3.7 %collective-permute-start.59 = (bf16[128,256]{1,0:T(8,128)(2,1)S(1)}, bf16[128,256]{1,0:T(8,128)(2,1)S(1)}, u32[]{:S(2)}, u32[]{:S(2)}) collective-permute-start(bf16[128,256]{1,0:T(8,128)(2,1)S(1)} %get-tuple-element.173), channel_id=1, source_target_pairs={{0,3},{1,2},{2,1},{3,0},{4,7},{5,6},{6,5},{7,4},{8,11},{9,10},{10,... | collective-permute-start | bytes 196616 | tf_op jit(solution)/shard_map/ppermute | solution.py:307
  (14 other events, 37.8 us)
